TPU v7x, 32 devices: a whole 2x2x4 slice. The times are simulated.
32 devices in a mesh: space: 16 (over z, y, core), ens: 2 (over x).
Axes of the slice: x: 2, y: 2, z: 4, core: 2. Of those that a mesh axis runs over, the one named last changes fastest.
Arguments:
- members: bfloat16 [2, 2048, 1024], P('ens', 'space'), may hold values from -6 to 6
- w_attn: bfloat16 [1024, 3072], P(('space', 'ens'))
- w_mix: bfloat16 [1024, 1024], P(('space', 'ens')), may hold values from -0.1875 to 0.1875
- readout_matrix: bfloat16 [1024, 100], P(('space', 'ens')), may hold values from -0.1875 to 0.1875
- observed_truth: float32 [100, 2048], P(None, 'space'), may hold values from -6 to 6
- cell_surface_factor: float32 [2048], P('space'), may hold values from 0.3 to 3
- neighbours: int32 [32, 4], P('space'), may hold values from -1 to 31, as said below
Outputs:
- prediction: float32 [2, 100, 2048], P('ens', None, 'space')
- grad_kv: float32 [1024, 2048], P(('space', 'ens'))
Inputs may be any that keep to these rules, and one draw needn't show every extreme that they name: `neighbours`: row t holds t itself in slot 0 and 3 distinct other tiles of t - 2 to t + 2; a slot whose tile lies outside the grid holds -1.
All inputs are finite; a program needn't handle non-finite values.
Results may differ from a plain program's by a relative error of at most 0.013.
Values may be sent and summed in bfloat16 or wider, within the bound.
No kernel may reach another device: no remote copies, remote signals or barrier semaphores. Data moves between devices by JAX's collectives and lax.ppermute only.
A program may use at most 64 MiB of HBM per device.

v0:
```python
import jax
import jax.numpy as jnp
from jax import lax
from jax.sharding import PartitionSpec as P

LATENT_DIM = 1024
HEADS = 16
HEAD = 64
FIELD_NUM = 100
TILE = 64
RADIUS = 2
K_NB = 4


NORM_EPS = 1e-06
SOFT_WIDTH = 0.0625
MASKED = -1e30


def with_halo(block, sides, width):
    for axis, dim in sides:
        count = lax.axis_size(axis)
        forward = [(i, i + 1) for i in range(count - 1)]
        backward = [(target, source) for source, target in forward]
        low = lax.ppermute(
            lax.slice_in_dim(block, block.shape[dim] - width, None, axis=dim), axis, forward
        )
        high = lax.ppermute(lax.slice_in_dim(block, 0, width, axis=dim), axis, backward)
        block = jnp.concatenate([low, block, high], axis=dim)
    return block


def rms_rows(matrix):
    return matrix * lax.rsqrt(jnp.mean(matrix * matrix, axis=-1, keepdims=True) + NORM_EPS)


def rms_back(matrix, upstream):
    inverse = lax.rsqrt(jnp.mean(matrix * matrix, axis=-1, keepdims=True) + NORM_EPS)
    return inverse * upstream - matrix * inverse**3 * jnp.mean(
        upstream * matrix, axis=-1, keepdims=True
    )


def softened_derivative(spread):
    return spread * lax.rsqrt(spread * spread + SOFT_WIDTH)


def attend(queries, key_rows, values, usable):
    factor = HEAD ** (-0.5)
    scores = (
        jnp.einsum("bihc,bjhc->bhij", queries, key_rows, preferred_element_type=jnp.float32)
        * factor
    )
    scores = jnp.where(usable[:, None, None, :], scores, MASKED)
    peak_score = jnp.max(scores, axis=-1, keepdims=True)
    raised = jnp.exp(scores - peak_score)
    attn_probs = raised / jnp.sum(raised, axis=-1, keepdims=True)
    outcome = jnp.einsum(
        "bhij,bjhc->bihc",
        attn_probs.astype(jnp.bfloat16),
        values,
        preferred_element_type=jnp.float32,
    )
    return (attn_probs, outcome.astype(jnp.bfloat16))


def attend_back(attn_probs, queries, values, grad_out):
    factor = HEAD ** (-0.5)
    grad_probs = jnp.einsum("bihc,bjhc->bhij", grad_out, values, preferred_element_type=jnp.float32)
    row_delta = jnp.sum(attn_probs * grad_probs, axis=-1, keepdims=True)
    grad_scores = (attn_probs * (grad_probs - row_delta) * factor).astype(jnp.bfloat16)
    key_grad = jnp.einsum(
        "bhij,bihc->bjhc", grad_scores, queries, preferred_element_type=jnp.float32
    ).astype(jnp.bfloat16)
    value_grad = jnp.einsum(
        "bhij,bihc->bjhc",
        attn_probs.astype(jnp.bfloat16),
        grad_out,
        preferred_element_type=jnp.float32,
    ).astype(jnp.bfloat16)
    return (key_grad, value_grad)


def body(members, w_attn, w_mix, readout_matrix, observed_truth, cell_surface_factor, neighbours):
    node_rows = members.shape[1]
    local_tiles = neighbours.shape[0]
    rim_rows = RADIUS * TILE
    ext_tiles = local_tiles + 2 * RADIUS
    key_count = K_NB * TILE
    realization_number = lax.axis_size("ens")
    attn_full, mix_full, dec_full = (
        lax.all_gather(w_attn, ("space", "ens"), axis=0, tiled=True),
        lax.all_gather(w_mix, ("space", "ens"), axis=0, tiled=True),
        lax.all_gather(readout_matrix, ("space", "ens"), axis=0, tiled=True),
    )
    source = members[0].astype(jnp.float32)
    normed = rms_rows(source).astype(jnp.bfloat16)
    projected = jnp.dot(normed, attn_full, preferred_element_type=jnp.float32).astype(jnp.bfloat16)
    queries = projected[:, :LATENT_DIM]
    kv_ext = with_halo(projected[:, LATENT_DIM:], (("space", 0),), rim_rows)
    first_tile = lax.axis_index("space") * local_tiles
    usable_slot = neighbours >= 0
    tile_ids = jnp.clip(neighbours - first_tile + RADIUS, 0, ext_tiles - 1)
    slot_table = (
        (tile_ids.reshape(-1)[:, None] == jnp.arange(ext_tiles, dtype=jnp.int32)[None, :])
        & usable_slot.reshape(-1)[:, None]
    ).astype(jnp.bfloat16)
    kv_flat = kv_ext.reshape(ext_tiles, TILE * 2 * LATENT_DIM)
    kv_tiles = jnp.dot(slot_table, kv_flat, preferred_element_type=jnp.float32).astype(jnp.bfloat16)
    kv_tiles = kv_tiles.reshape(local_tiles, key_count, 2 * LATENT_DIM)
    key_rows = kv_tiles[:, :, :LATENT_DIM].reshape(local_tiles, key_count, HEADS, HEAD)
    value_rows = kv_tiles[:, :, LATENT_DIM:].reshape(local_tiles, key_count, HEADS, HEAD)
    usable = jnp.repeat(usable_slot, TILE, axis=1)
    query_tiles = queries.reshape(local_tiles, TILE, HEADS, HEAD)
    attn_probs, outcome = attend(query_tiles, key_rows, value_rows, usable)
    attn_out = outcome.reshape(node_rows, LATENT_DIM)
    hidden = source + jnp.dot(attn_out, mix_full, preferred_element_type=jnp.float32)
    predicted_fields = rms_rows(hidden).astype(jnp.bfloat16)
    prediction = lax.dot_general(
        dec_full, predicted_fields, (((0,), (1,)), ((), ())), preferred_element_type=jnp.float32
    )[None]
    spread_pair_values = jnp.sum(
        softened_derivative(prediction - lax.all_gather(prediction, "ens", axis=0, tiled=True)),
        axis=0,
        keepdims=True,
    )
    derivative_sum_all = (
        cell_surface_factor[None, None, :]
        / FIELD_NUM
        * (
            softened_derivative(prediction - observed_truth[None])
            - spread_pair_values / (realization_number - 1)
        )
    )
    grad_fore = derivative_sum_all[0].astype(jnp.bfloat16)
    grad_decoded = lax.dot_general(
        grad_fore, dec_full, (((0,), (1,)), ((), ())), preferred_element_type=jnp.float32
    )
    grad_hidden = rms_back(hidden, grad_decoded).astype(jnp.bfloat16)
    grad_attn_out = lax.dot_general(
        grad_hidden, mix_full, (((1,), (1,)), ((), ())), preferred_element_type=jnp.float32
    ).astype(jnp.bfloat16)
    key_grad, value_grad = attend_back(
        attn_probs, query_tiles, value_rows, grad_attn_out.reshape(local_tiles, TILE, HEADS, HEAD)
    )
    contrib = jnp.concatenate(
        [
            key_grad.reshape(local_tiles, K_NB, TILE, LATENT_DIM),
            value_grad.reshape(local_tiles, K_NB, TILE, LATENT_DIM),
        ],
        axis=3,
    )
    contrib_flat = contrib.reshape(local_tiles * K_NB, TILE * 2 * LATENT_DIM)
    kv_grads = lax.dot_general(
        slot_table, contrib_flat, (((0,), (0,)), ((), ())), preferred_element_type=jnp.float32
    ).reshape(-1, 2 * LATENT_DIM)
    own_grads = kv_grads[rim_rows : rim_rows + node_rows]
    rim_grads = jnp.concatenate([kv_grads[:rim_rows], kv_grads[rim_rows + node_rows :]], axis=0)
    arrived = with_halo(rim_grads.astype(jnp.bfloat16), (("space", 0),), rim_rows).astype(
        rim_grads.dtype
    )
    own_grads = own_grads.at[:rim_rows].add(arrived[:rim_rows])
    own_grads = own_grads.at[node_rows - rim_rows :].add(arrived[3 * rim_rows :])
    kv_high = own_grads.astype(jnp.bfloat16)
    kv_low = (own_grads - kv_high.astype(jnp.float32)).astype(jnp.bfloat16)
    over_rows = (((0,), (0,)), ((), ()))
    accumulated_values = lax.psum_scatter(
        lax.dot_general(normed, kv_high, over_rows, preferred_element_type=jnp.float32)
        + lax.dot_general(normed, kv_low, over_rows, preferred_element_type=jnp.float32),
        ("space", "ens"),
        scatter_dimension=0,
        tiled=True,
    )
    return (prediction, accumulated_values)


def solution(mesh):
    in_specs = (
        P("ens", "space", None),
        P(("space", "ens"), None),
        P(("space", "ens"), None),
        P(("space", "ens"), None),
        P(None, "space"),
        P("space"),
        P("space", None),
    )
    out_specs = (P("ens", None, "space"), P(("space", "ens"), None))
    return jax.shard_map(body, mesh=mesh, in_specs=in_specs, out_specs=out_specs, check_vma=False)
```

profile of v0, /device:TPU:1, one launch (start us, length us, event | category | flops | bytes accessed | tf_op | source)
XLA Modules:
  0.0 431.9 jit_solution(10409057455613475555)
XLA Ops:
  7.2 0.7 all-gather.5.cloned.1.call-update
  7.9 0.7 all-gather.7.cloned.1.call-update
  8.7 0.7 broadcast_compare_fusion
  9.6 1.1 fusion.24
  10.8 72.2 %all-gather.5.cloned.1.call-done = bf16[1024,3072]{1,0:T(8,128)(2,1)} async-done(((bf16[32,3072]{1,0:T(8,128)(2,1)}), bf16[1024,3072]{1,0:T(8,128)(2,1)}) %all-gather.5.cloned.1.call-update) | async-done | bytes 6291472 | tf_op jit(solution)/shard_map/all_gather | solution.py:92
  82.9 3.9 convolution_convert_fusion.1
  86.9 2.2 collective-permute-start.1
  89.1 3.4 collective-permute-start
  92.6 62.5 %all_gather.14 = bf16[1024,100]{1,0:T(8,128)(2,1)S(1)} all-gather(bf16[32,100]{1,0:T(8,128)(2,1)S(1)} %copy-done.6), channel_id=1, replica_groups=mesh['space'=16,'ens'=2] {'space','ens'}, dimensions={0}, use_global_device_ids=true | all-gather | bytes 211200 | tf_op jit(solution)/shard_map/all_gather | solution.py:94
  155.1 0.3 reshape.154
  155.5 1.3 copy.31
  156.7 1.3 pad_maximum_fusion.1
  158.0 3.9 reshape.151
  161.8 2.1 convolution_convert_fusion
  164.0 2.5 reshape.152
  166.5 1.2 fusion.64
  167.7 2.3 copy.27
  170.0 0.5 copy.26
  170.6 3.3 fusion.65
  173.9 2.1 fusion.16
  176.1 0.4 copy.29
  176.9 2.1 multiply_reduce_fusion.2
  179.3 4.0 all-gather.1
  183.4 0.3 multiply_reduce_fusion.1
  183.7 0.9 convolution_convert_fusion.4
  184.9 1.3 copy.33
  186.2 1.7 fusion.67
  188.1 1.5 fusion.15
  189.6 14.4 %fusion.12 = bf16[2,256,16,64]{1,3,2,0:T(8,128)(2,1)} fusion(bf16[2,64,16,64]{1,3,2,0:T(8,128)(2,1)S(1)} %copy-done.4, f32[2,16,64,256]{3,2,1,0:T(8,128)S(1)} %fusion.67, f32[2,16,64,256]{3,2,1,0:T(8,128)} %get-tuple-element.55, f32[2,16,64]{2,1,0:T(8,128)S(1)} %get-tuple-element.54), kind=kOutput, calls=%fused_computation.16 | convolution fusion | flops 71305472 | bytes 5513216 | tf_op jit(solution)/shard_map/bhij,bihc->bjhc/dot_general | solution.py:72
  204.1 3.3 reshape.167
  207.4 1.3 copy.37
  208.6 3.3 reshape.166
  212.0 2.4 copy.36
  214.3 1.4 pad_maximum_fusion
  215.7 1.2 copy.38
  216.9 2.5 fusion.66
  219.4 0.7 fusion.63
  220.2 0.5 slice.75
  220.6 0.5 slice.77
  221.1 6.4 %collective-permute-start.3 = (bf16[128,2048]{1,0:T(8,128)(2,1)S(1)}, bf16[128,2048]{1,0:T(8,128)(2,1)}, u32[]{:S(2)}, u32[]{:S(2)}) collective-permute-start(bf16[128,2048]{1,0:T(8,128)(2,1)S(1)} %slice.77), channel_id=1, source_target_pairs={{2,0},{4,2},{6,4},{8,6},{10,8},{12,10},{14,12},{16,14},{18,16},{20... | collective-permute-start | bytes 1572872 | tf_op jit(solution)/shard_map/ppermute | solution.py:28
  227.5 2.1 collective-permute-start.2
  229.7 2.7 slice.84
  232.4 0.9 slice.73
  233.3 2.2 collective-permute-done.2
  235.6 2.6 fusion.33
  238.1 5.8 %convolution_add_fusion = f32[1024,2048]{1,0:T(8,128)} fusion(f32[1024,2048]{1,0:T(8,128)S(1)} %fusion.33, bf16[1,128,1024]{2,1,0:T(8,128)(2,1)S(1)} %copy-done, f32[128]{0:T(128)S(1)} %add_rsqrt_fusion.1, f32[128,2048]{1,0:T(8,128)S(1)} %slice.73, bf16[128,2048]{1,0:T(8,128)(2,1)} %collective-permute-done.3, bf16[128,2048]{1,0:T(8,128)(2,1)S(1)} %slice.75, ...), kind=kOutput, calls=%fused_computation.3 | convolution fusion | flops 545128448 | bytes 20185600 | tf_op jit(solution)/shard_map/dot_general | solution.py:169
  244.0 0.7 copy.35
  244.6 180.8 %reduce-scatter.2.cloned.1.call-done = f32[32,2048]{1,0:T(8,128)} async-done(((f32[1024,2048]{1,0:T(8,128)}), f32[32,2048]{1,0:T(8,128)}) %reduce-scatter.2.cloned.1.call-update) | async-done | bytes 262160 | tf_op jit(solution)/shard_map/reduce_scatter | solution.py:167
  (43 shorter events, 1.8 us)
Async XLA Ops:
  7.2 75.8 %all-gather.5.cloned.1.call-start = ((), (), s32[]{:S(2)}) async-start(), calls=%async_computation.1 | async-start | bytes 6488064 | tf_op jit(solution)/shard_map/all_gather | solution.py:92
  7.9 169.0 %all-gather.7.cloned.1.call-start = ((), (), s32[]{:S(2)}) async-start(), calls=%async_computation.2 | async-start | bytes 2162688 | tf_op jit(solution)/shard_map/all_gather | solution.py:93
  8.6 416.8 %reduce-scatter.2.cloned.1.call-start = ((), (), s32[]{:S(2)}) async-start(), calls=%async_computation.3 | async-start | bytes 8650752 | tf_op jit(solution)/shard_map/reduce_scatter | solution.py:167
  10.7 81.8 %copy-start.7 = (s32[2,4]{1,0:T(2,128)S(1)}, s32[2,4]{1,0:T(2,128)}, u32[]{:S(2)}) copy-start(s32[2,4]{1,0:T(2,128)} %param.21) | copy-start | bytes 100
  10.7 81.9 %copy-start.6 = (bf16[32,100]{1,0:T(8,128)(2,1)S(1)}, bf16[32,100]{1,0:T(8,128)(2,1)}, u32[]{:S(2)}) copy-start(bf16[32,100]{1,0:T(8,128)(2,1)} %param.18) | copy-start | bytes 19204
  10.7 144.3 %copy-start.8 = (f32[128]{0:T(128)S(1)}, f32[128]{0:T(128)}, u32[]{:S(2)}) copy-start(f32[128]{0:T(128)} %param.20) | copy-start | bytes 1540
  86.9 69.8 %collective-permute-start.1 = (bf16[128,2048]{1,0:T(8,128)(2,1)S(1)}, bf16[128,2048]{1,0:T(8,128)(2,1)S(1)}, u32[]{:S(2)}, u32[]{:S(2)}) collective-permute-start(bf16[128,2048]{1,0:T(8,128)(2,1)S(1)} %slice.80), channel_id=1, source_target_pairs={{2,0},{4,2},{6,4},{8,6},{10,8},{12,10},{14,12},{16,14},{18,16},{20... | collective-permute-start | bytes 1572872 | tf_op jit(solution)/shard_map/ppermute | solution.py:28
  89.1 67.7 %collective-permute-start = (bf16[128,2048]{1,0:T(8,128)(2,1)S(1)}, bf16[128,2048]{1,0:T(8,128)(2,1)S(1)}, u32[]{:S(2)}, u32[]{:S(2)}) collective-permute-start(bf16[128,2048]{1,0:T(8,128)(2,1)S(1)} %slice.80), channel_id=1, source_target_pairs={{0,2},{2,4},{4,6},{6,8},{8,10},{10,12},{12,14},{14,16},{16,18},{18... | collective-permute-start | bytes 1572872 | tf_op jit(solution)/shard_map/ppermute | solution.py:25
  167.7 2.9 copy-start.3
  173.9 3.0 copy-start
  176.8 6.5 %copy-start.5 = (f32[100,128]{1,0:T(8,128)S(1)}, f32[100,128]{1,0:T(8,128)}, u32[]{:S(2)}) copy-start(f32[100,128]{1,0:T(8,128)} %param.19) | copy-start | bytes 153604
  179.0 4.7 %copy-start.1 = (bf16[1024,1024]{1,0:T(8,128)(2,1)S(1)}, bf16[1024,1024]{1,0:T(8,128)(2,1)}, u32[]{:S(2)}) copy-start(bf16[1024,1024]{1,0:T(8,128)(2,1)} %all-gather.7.cloned.1.call-done) | copy-start | bytes 6291460
  186.2 1.7 copy-start.2
  186.2 1.9 copy-start.9
  188.1 1.5 copy-start.4
  221.1 12.2 %collective-permute-start.3 = (bf16[128,2048]{1,0:T(8,128)(2,1)S(1)}, bf16[128,2048]{1,0:T(8,128)(2,1)}, u32[]{:S(2)}, u32[]{:S(2)}) collective-permute-start(bf16[128,2048]{1,0:T(8,128)(2,1)S(1)} %slice.77), channel_id=1, source_target_pairs={{2,0},{4,2},{6,4},{8,6},{10,8},{12,10},{14,12},{16,14},{18,16},{20... | collective-permute-start | bytes 1572872 | tf_op jit(solution)/shard_map/ppermute | solution.py:28
  227.5 8.0 %collective-permute-start.2 = (bf16[128,2048]{1,0:T(8,128)(2,1)S(1)}, bf16[128,2048]{1,0:T(8,128)(2,1)}, u32[]{:S(2)}, u32[]{:S(2)}) collective-permute-start(bf16[128,2048]{1,0:T(8,128)(2,1)S(1)} %slice.75), channel_id=1, source_target_pairs={{0,2},{2,4},{4,6},{6,8},{8,10},{10,12},{12,14},{14,16},{16,18},{18... | collective-permute-start | bytes 1572872 | tf_op jit(solution)/shard_map/ppermute | solution.py:25
Sparse Core Ops, SparseCore 0:
  10.9 71.9 all-gather.4
  85.9 59.4 all-gather.6
  244.1 181.2 reduce-scatter.1
where the time goes:
time: 434 us; the launch traced here: 432 us
  waiting for transfers between devices  257 us (59%)
  blocking collectives  66.5 us (15%)
  matrix products  43.6 us (10%)
  local copies, waits for them, and re-layouts  32.4 us (7%)
  starting transfers between devices  14.2 us (3%)
  between operations  14.1 us (3%)
  other arithmetic  4.49 us (1%)
    reduce_scatter x1, waiting for transfers between devices, body(): lax.psum_scatter(lax.dot_general(normed, kv_high, over_rows, preferred_el...  181 us
    all_gather x1, waiting for transfers between devices, body(): lax.all_gather(w_attn, ('space', 'ens'), axis=0, tiled=True)  72.2 us
    all_gather x1, blocking collectives, body(): lax.all_gather(readout_matrix, ('space', 'ens'), axis=0, tiled=True)  62.5 us
    dot_general x1, matrix products, attend_back(): jnp.einsum('bhij,bihc->bjhc', grad_scores, queries, preferred_element_typ...  14.4 us
  transfers between devices with their start and end apart: 7, of which 3 were waited for; matrix products, arithmetic and copies ran while one was open for 7% of the time, Pallas kernels for 0%

commit v1 on v0

v1 whole, which is shorter than its diff:
```python
import functools

import jax
import jax.numpy as jnp
from jax import lax
from jax.experimental import pallas as pl
from jax.experimental.pallas import tpu as pltpu
from jax.sharding import Mesh
from jax.sharding import PartitionSpec as P

LATENT_DIM = 1024
HEADS = 16
HEAD = 64
FIELD_NUM = 100
TILE = 64
RADIUS = 2
K_NB = 4
GROUP = 8
COLS = LATENT_DIM // GROUP
RIM = RADIUS * TILE
FIELD_PAD = 128

NORM_EPS = 1e-06
SOFT_WIDTH = 0.0625
MASKED = -1e30

F32 = jnp.float32
BF16 = jnp.bfloat16


def rms_rows(matrix):
    return matrix * lax.rsqrt(jnp.mean(matrix * matrix, axis=-1, keepdims=True) + NORM_EPS)


def rms_back(matrix, upstream):
    inverse = lax.rsqrt(jnp.mean(matrix * matrix, axis=-1, keepdims=True) + NORM_EPS)
    return inverse * upstream - matrix * inverse**3 * jnp.mean(
        upstream * matrix, axis=-1, keepdims=True
    )


def softened_derivative(spread):
    return spread * lax.rsqrt(spread * spread + SOFT_WIDTH)


def by_head(rows):
    lane = lax.broadcasted_iota(jnp.int32, rows.shape, 1)
    zero = jnp.zeros_like(rows)
    return jnp.concatenate(
        [jnp.where(lane < HEAD, rows, zero), jnp.where(lane < HEAD, zero, rows)], axis=0
    )


def tile_keys(slots_ref, tile, last_tile, kv):
    lane = lax.broadcasted_iota(jnp.int32, (1, K_NB * TILE), 1)
    usable = jnp.zeros((1, K_NB * TILE), jnp.int32)
    places, keys, values = [], [], []
    for slot in range(K_NB):
        at = slots_ref[tile, slot]
        usable = jnp.where(lane // TILE == slot, (at >= 0).astype(jnp.int32), usable)
        place = pl.multiple_of(jnp.clip(at, 0, last_tile) * TILE, TILE)
        places.append(place)
        keys.append(kv[pl.ds(place, TILE), :COLS])
        values.append(kv[pl.ds(place, TILE), COLS:])
    return places, usable > 0, jnp.concatenate(keys, axis=0), jnp.concatenate(values, axis=0)


def probabilities(queries, keys, usable):
    scores = lax.dot_general(
        queries, keys, (((1,), (1,)), ((), ())), preferred_element_type=F32
    ) * (HEAD**-0.5)
    scores = jnp.where(usable, scores, MASKED)
    raised = jnp.exp(scores - jnp.max(scores, axis=-1, keepdims=True))
    return raised * (1.0 / jnp.sum(raised, axis=-1, keepdims=True))


def fill(kv, low_ref, own_ref, high_ref):
    rows = own_ref.shape[0]
    kv[0:RIM, :] = low_ref[...]
    kv[RIM : RIM + rows, :] = own_ref[...]
    kv[RIM + rows : 2 * RIM + rows, :] = high_ref[...]


def forward_kernel(slots_ref, q_ref, low_ref, own_ref, high_ref, out_ref, kv):
    tiles = q_ref.shape[0] // TILE
    last_tile = tiles + 2 * RADIUS - 1
    fill(kv, low_ref, own_ref, high_ref)

    def step(tile, carry):
        rows = pl.ds(pl.multiple_of(tile * TILE, TILE), TILE)
        _, usable, keys, values = tile_keys(slots_ref, tile, last_tile, kv)
        probs = probabilities(by_head(q_ref[rows, :]), keys, usable)
        both = jnp.dot(probs.astype(BF16), values, preferred_element_type=F32)
        lane = lax.broadcasted_iota(jnp.int32, (TILE, COLS), 1)
        out_ref[rows, :] = jnp.where(lane < HEAD, both[:TILE], both[TILE:]).astype(BF16)
        return carry

    lax.fori_loop(0, tiles, step, 0, unroll=4)


def backward_kernel(slots_ref, q_ref, low_ref, own_ref, high_ref, g_ref, out_ref, kv, total):
    tiles = q_ref.shape[0] // TILE
    last_tile = tiles + 2 * RADIUS - 1
    fill(kv, low_ref, own_ref, high_ref)
    total[...] = jnp.zeros_like(total)
    over_rows = (((0,), (0,)), ((), ()))

    def step(tile, carry):
        rows = pl.ds(pl.multiple_of(tile * TILE, TILE), TILE)
        places, usable, keys, values = tile_keys(slots_ref, tile, last_tile, kv)
        queries = by_head(q_ref[rows, :])
        grads = by_head(g_ref[rows, :])
        probs = probabilities(queries, keys, usable)
        grad_probs = lax.dot_general(
            grads, values, (((1,), (1,)), ((), ())), preferred_element_type=F32
        )
        row_delta = jnp.sum(probs * grad_probs, axis=-1, keepdims=True)
        grad_scores = (probs * (grad_probs - row_delta) * (HEAD**-0.5)).astype(BF16)
        key_grad = lax.dot_general(grad_scores, queries, over_rows, preferred_element_type=F32)
        value_grad = lax.dot_general(
            probs.astype(BF16), grads, over_rows, preferred_element_type=F32
        )
        key_grad = key_grad.astype(BF16).astype(F32)
        value_grad = value_grad.astype(BF16).astype(F32)
        for slot in range(K_NB):
            part = slice(slot * TILE, (slot + 1) * TILE)
            total[pl.ds(places[slot], TILE), :COLS] += key_grad[part]
            total[pl.ds(places[slot], TILE), COLS:] += value_grad[part]
        return carry

    lax.fori_loop(0, tiles, step, 0, unroll=2)
    high = total[...].astype(BF16)
    out_ref[:, : 2 * COLS] = high
    out_ref[:, 2 * COLS :] = (total[...] - high.astype(F32)).astype(BF16)


VMEM = pl.BlockSpec(memory_space=pltpu.VMEM)
SMEM = pl.BlockSpec(memory_space=pltpu.SMEM)


def attention_forward(slots, queries, low, own, high):
    rows = queries.shape[0]
    return pl.pallas_call(
        forward_kernel,
        out_shape=jax.ShapeDtypeStruct((rows, COLS), BF16),
        in_specs=[SMEM] + [VMEM] * 4,
        out_specs=VMEM,
        scratch_shapes=[pltpu.VMEM((rows + 2 * RIM, 2 * COLS), BF16)],
        compiler_params=pltpu.CompilerParams(vmem_limit_bytes=24 * 2**20),
        cost_estimate=pl.CostEstimate(
            flops=rows * COLS * 4 * 512, bytes_accessed=rows * COLS * 8, transcendentals=rows * 512
        ),
        name="attention_forward",
    )(slots, queries, low, own, high)


def attention_backward(slots, queries, low, own, high, grads):
    rows = queries.shape[0]
    ext = rows + 2 * RIM
    return pl.pallas_call(
        backward_kernel,
        out_shape=jax.ShapeDtypeStruct((ext, 4 * COLS), BF16),
        in_specs=[SMEM] + [VMEM] * 5,
        out_specs=VMEM,
        scratch_shapes=[pltpu.VMEM((ext, 2 * COLS), BF16), pltpu.VMEM((ext, 2 * COLS), F32)],
        compiler_params=pltpu.CompilerParams(vmem_limit_bytes=24 * 2**20),
        cost_estimate=pl.CostEstimate(
            flops=rows * COLS * 10 * 512, bytes_accessed=rows * COLS * 16, transcendentals=rows * 512
        ),
        name="attention_backward",
    )(slots, queries, low, own, high, grads)


def body(members, w_attn, w_mix, readout_matrix, observed_truth, cell_surface_factor, neighbours):
    halves, group, members_num = (lax.axis_size(axis) for axis in ("half", "group", "ens"))
    shard = w_attn.shape[0]
    node_rows = members.shape[1]
    up = [(i, i + 1) for i in range(halves - 1)]
    down = [(target, source) for source, target in up]

    source = members[0].astype(F32)
    normed = rms_rows(source).astype(BF16)
    normed_all = lax.all_gather(normed, "group", axis=0, tiled=True)
    slots = lax.all_gather(neighbours, "group", axis=0, tiled=True)
    tiles = slots.shape[0]
    slots = jnp.where(slots >= 0, slots - lax.axis_index("half") * tiles + RADIUS, -1)

    columns = w_attn.reshape(shard, 3, group, COLS).transpose(2, 0, 1, 3).reshape(group, shard, 3 * COLS)
    columns = lax.all_to_all(columns, "group", 0, 0)
    columns = lax.all_gather(columns, ("half", "ens"), axis=0)
    columns = columns.reshape(halves, members_num, group, shard, 3 * COLS)
    columns = columns.transpose(0, 2, 1, 3, 4).reshape(LATENT_DIM, 3 * COLS)

    packed = jnp.concatenate(
        [w_mix, jnp.pad(readout_matrix, ((0, 0), (0, FIELD_PAD - FIELD_NUM)))], axis=1
    )
    width = packed.shape[1]
    packed = lax.all_gather(packed, "ens", axis=0, tiled=True)
    packed = lax.all_gather(packed, "half", axis=0)
    packed = lax.all_gather(packed, "group", axis=0)
    packed = packed.transpose(1, 0, 2, 3).reshape(LATENT_DIM, width)
    mix_full = packed[:, :LATENT_DIM]
    dec_full = packed[:, LATENT_DIM : LATENT_DIM + FIELD_NUM]

    projected = jnp.dot(normed_all, columns, preferred_element_type=F32).astype(BF16)
    queries, own = projected[:, :COLS], projected[:, COLS:]
    low = lax.ppermute(own[-RIM:], "half", up)
    high = lax.ppermute(own[:RIM], "half", down)
    normed_low = lax.ppermute(normed_all[-RIM:], "half", up)
    normed_high = lax.ppermute(normed_all[:RIM], "half", down)

    outcome = attention_forward(slots, queries, low, own, high)
    attn_out = lax.all_to_all(outcome.reshape(group, node_rows, COLS), "group", 0, 0)
    attn_out = attn_out.transpose(1, 0, 2).reshape(node_rows, LATENT_DIM)
    hidden = source + jnp.dot(attn_out, mix_full, preferred_element_type=F32)
    predicted_fields = rms_rows(hidden).astype(BF16)
    prediction = lax.dot_general(
        dec_full, predicted_fields, (((0,), (1,)), ((), ())), preferred_element_type=F32
    )[None]
    spread_pair_values = jnp.sum(
        softened_derivative(prediction - lax.all_gather(prediction, "ens", axis=0, tiled=True)),
        axis=0,
        keepdims=True,
    )
    derivative_sum_all = (
        cell_surface_factor[None, None, :]
        / FIELD_NUM
        * (
            softened_derivative(prediction - observed_truth[None])
            - spread_pair_values / (members_num - 1)
        )
    )
    grad_fore = derivative_sum_all[0].astype(BF16)
    grad_decoded = lax.dot_general(
        grad_fore, dec_full, (((0,), (1,)), ((), ())), preferred_element_type=F32
    )
    grad_hidden = rms_back(hidden, grad_decoded).astype(BF16)
    grad_attn_out = lax.dot_general(
        grad_hidden, mix_full, (((1,), (1,)), ((), ())), preferred_element_type=F32
    ).astype(BF16)
    grads = grad_attn_out.reshape(node_rows, group, COLS).transpose(1, 0, 2)
    grads = lax.all_to_all(grads, "group", 0, 0).reshape(group * node_rows, COLS)

    kv_grads = attention_backward(slots, queries, low, own, high, grads)
    normed_ext = jnp.concatenate([normed_low, normed_all, normed_high], axis=0)
    over_rows = (((0,), (0,)), ((), ()))
    term = lax.dot_general(normed_ext, kv_grads[:, : 2 * COLS], over_rows, preferred_element_type=F32)
    term = term + lax.dot_general(
        normed_ext, kv_grads[:, 2 * COLS :], over_rows, preferred_element_type=F32
    )
    term = term.astype(BF16).reshape(halves, group, members_num, shard, 2 * COLS)
    term = term.transpose(0, 2, 1, 3, 4).reshape(halves * members_num, group, shard, 2 * COLS)
    term = lax.all_to_all(term, ("half", "ens"), 0, 0)
    term = jnp.sum(term.astype(F32), axis=0)
    term = lax.all_to_all(term, "group", 0, 0)
    grad_kv = term.reshape(group, shard, 2, COLS).transpose(1, 2, 0, 3).reshape(shard, 2 * LATENT_DIM)
    return (prediction, grad_kv)


def solution(mesh):
    space, ens = mesh.shape["space"], mesh.shape["ens"]
    split = Mesh(mesh.devices.reshape(space // GROUP, GROUP, ens), ("half", "group", "ens"))
    nodes, rows = ("half", "group"), ("half", "group", "ens")
    in_specs = (
        P("ens", nodes, None),
        P(rows, None),
        P(rows, None),
        P(rows, None),
        P(None, nodes),
        P(nodes),
        P(nodes, None),
    )
    out_specs = (P("ens", None, nodes), P(rows, None))
    return jax.shard_map(body, mesh=split, in_specs=in_specs, out_specs=out_specs, check_vma=False)
```

time: 434 us -> 171 us (0.39)
  waiting for transfers between devices: 257 us -> 16.4 us
  matrix products: 43.6 us -> 11.2 us
  starting transfers between devices: 14.2 us -> 35.1 us
  local copies, waits for them, and re-layouts: 32.4 us -> 14.8 us
  Pallas kernels: 0 us -> 14.2 us
  blocking collectives: 66.5 us -> 58.6 us
    reduce_scatter x1 -> x0, waiting for transfers between devices: 181 us -> none  [body(): lax.psum_scatter(lax.dot_general(normed, kv_high, over_rows, preferred_el...]
    all_gather x2, waiting for transfers between devices: 72.2 us -> 0.02 us  [the longest x1 0.02 us: body(): normed_all = lax.all_gather(normed, 'group', axis=0, tiled=True)]
    dot_general x10 -> x4, matrix products: 38.8 us -> 9.69 us  [the longest x1 2.88 us: body(): jnp.dot(normed_all, columns, preferred_element_type=F32).astype(BF16)]
    all_to_all x0 -> x4, starting transfers between devices: none -> 21.9 us  [the longest x1 6.18 us: body(): lax.all_to_all(outcome.reshape(group, node_rows, COLS), 'group', 0, 0)]
    all_gather x1 -> x4, blocking collectives: 62.5 us -> 43 us  [the longest x1 18.9 us: body(): columns = lax.all_gather(columns, ('half', 'ens'), axis=0)]
    reshape x11 -> x6, local copies, waits for them, and re-layouts: 20.2 us -> 2.72 us  [the longest x2 0.94 us: body(): w_attn.reshape(shard, 3, group, COLS).transpose(2, 0, 1, 3)]
    pallas_call x0 -> x2, Pallas kernels: none -> 14.2 us  [the longest x1 9.91 us: attention_backward(): pl.pallas_call(backward_kernel, out_shape=jax.ShapeDtypeStruct((ext, 4 *...]
    all_to_all x0 -> x1, blocking collectives: none -> 11.9 us  [body(): term = lax.all_to_all(term, ('half', 'ens'), 0, 0)]
  transfers between devices with their start and end apart: 7 -> 10, of which waited for: 3 -> 3; matrix products, arithmetic and copies ran while one was open for 7% -> 12% of each run, Pallas kernels for 0% -> 3%
where the time goes in v1:
time: 171 us; the launch traced here: 169 us
  blocking collectives  58.6 us (34%)
  starting transfers between devices  35.1 us (21%)
  waiting for transfers between devices  16.4 us (10%)
  local copies, waits for them, and re-layouts  14.8 us (9%)
  between operations  14.3 us (8%)
  Pallas kernels  14.2 us (8%)
  matrix products  11.2 us (7%)
  other arithmetic  4.57 us (3%)
    all_gather x1, blocking collectives, body(): columns = lax.all_gather(columns, ('half', 'ens'), axis=0)  18.9 us
    all_to_all x1, blocking collectives, body(): term = lax.all_to_all(term, ('half', 'ens'), 0, 0)  11.9 us
    ppermute x1, waiting for transfers between devices, body(): normed_high = lax.ppermute(normed_all[:RIM], 'half', down)  10.5 us
    all_gather x1, blocking collectives, body(): slots = lax.all_gather(neighbours, 'group', axis=0, tiled=True)  10.2 us
    pallas_call x1, Pallas kernels, attention_backward(): pl.pallas_call(backward_kernel, out_shape=jax.ShapeDtypeStruct((ext, 4 *...  9.91 us
    all_gather x1, blocking collectives, body(): packed = lax.all_gather(packed, 'half', axis=0)  9.5 us
    unnamed x13, local copies, waits for them, and re-layouts  7.21 us
    all_to_all x1, starting transfers between devices, body(): lax.all_to_all(outcome.reshape(group, node_rows, COLS), 'group', 0, 0)  6.18 us
  transfers between devices with their start and end apart: 10, of which 3 were waited for; matrix products, arithmetic and copies ran while one was open for 12% of the time, Pallas kernels for 3%

profile of v1, /device:TPU:1, one launch (start us, length us, event | category | flops | bytes accessed | tf_op | source)
XLA Modules:
  0.0 169.2 jit_solution(17260138195616024484)
XLA Ops:
  7.2 0.0 all-gather.9.cloned.1.call-start
  7.2 1.1 fusion.17
  8.3 1.8 %fusion.18 = bf16[128,1024]{1,0:T(8,128)(2,1)} fusion(bf16[1,128,1024]{2,1,0:T(8,128)(2,1)} %param.7, f32[128]{0:T(128)S(1)} %add_rsqrt_fusion.1), kind=kLoop, calls=%fused_computation.17 | loop fusion | flops 393216 | bytes 524800 | tf_op jit(solution)/shard_map/convert_element_type | solution.py:182
  10.1 0.0 all-gather.11.cloned.1.call-start
  10.2 0.9 fusion.28
  11.0 4.4 %all_gather.30 = bf16[64,1152]{1,0:T(8,128)(2,1)S(1)} all-gather(bf16[32,1152]{1,0:T(8,128)(2,1)S(1)} %fusion.28), channel_id=1, replica_groups=mesh['half'=2,'group'=8,'ens'=2] {'ens'}, dimensions={0}, use_global_device_ids=true | all-gather | bytes 221184 | tf_op jit(solution)/shard_map/all_gather | solution.py:198
  15.4 9.5 %all-gather = bf16[128,1152]{1,0:T(8,128)(2,1)} all-gather(bf16[64,1152]{1,0:T(8,128)(2,1)S(1)} %all_gather.30), channel_id=2, replica_groups=mesh['half'=2,'group'=8,'ens'=2] {'half'}, dimensions={0}, use_global_device_ids=true | all-gather | bytes 442368 | tf_op jit(solution)/shard_map/all_gather | solution.py:199
  25.0 1.0 copy.41
  25.9 0.1 copy.48
  26.0 0.8 reshape.86
  26.9 5.2 %all-to-all-start = ((bf16[8,32,384]{2,1,0:T(8,128)(2,1)}), bf16[8,32,384]{2,1,0:T(8,128)(2,1)S(1)}, u32[]{:S(2)}, u32[]{:S(2)}) async-start(bf16[8,32,384]{2,1,0:T(8,128)(2,1)} %reshape.86), calls=%async_computation | async-start | bytes 393216 | tf_op jit(solution)/shard_map/all_to_all | solution.py:189
  32.1 10.2 %all-gather.4 = s32[8,2,4]{2,1,0:T(2,128)S(1)} all-gather(s32[1,2,4]{2,1,0:T(2,128)S(1)} %bitcast.73), channel_id=1, replica_groups=mesh['half'=2,'group'=8,'ens'=2] {'group'}, dimensions={0}, use_global_device_ids=true | all-gather | bytes 288 | tf_op jit(solution)/shard_map/all_gather | solution.py:184
  42.3 18.9 %all-gather.2 = bf16[32,32,384]{2,1,0:T(8,128)(2,1)S(1)} all-gather(bf16[8,32,384]{2,1,0:T(8,128)(2,1)S(1)} %all-to-all-done), channel_id=4, replica_groups=mesh['half'=2,'group'=8,'ens'=2] {'half','ens'}, dimensions={0}, use_global_device_ids=true | all-gather | bytes 983040 | tf_op jit(solution)/shard_map/all_gather | solution.py:190
  61.2 0.1 copy.34
  61.3 0.0 all-gather.9.cloned.1.call-done
  61.3 2.9 %convolution_convert_fusion = bf16[1024,384]{1,0:T(8,128)(2,1)S(1)} fusion(bf16[1024,1024]{1,0:T(8,128)(2,1)} %all-gather.9.cloned.1.call-done, bf16[1024,384]{1,0:T(8,128)(2,1)S(1)} %bitcast.69), kind=kOutput, calls=%fused_computation.4 | convolution fusion | flops 805699584 | bytes 3670016 | tf_op jit(solution)/shard_map/dot_general | solution.py:205
  64.2 1.3 collective-permute-start.1
  65.5 4.9 %collective-permute-start = (bf16[128,256]{1,0:T(8,128)(2,1)S(1)}, bf16[128,256]{1,0:T(8,128)(2,1)S(1)}, u32[]{:S(2)}, u32[]{:S(2)}) collective-permute-start(bf16[128,256]{1,0:T(8,128)(2,1)S(1)} %get-tuple-element.15), channel_id=1, source_target_pairs={{0,16},{1,17},{2,18},{3,19},{4,20},{5,21},{6,22},{7,23},{8,24},{9,... | collective-permute-start | bytes 196616 | tf_op jit(solution)/shard_map/ppermute | solution.py:207
  70.5 1.2 collective-permute-done.low_ref
  71.7 4.3 %attention_forward.1 = bf16[1024,128]{1,0:T(8,128)(2,1)S(1)} custom-call(s32[16,4]{1,0:T(8,128)S(1)} %bitcast.53, bf16[1024,128]{1,0:T(8,128)(2,1)S(1)} %slice.43.q_ref, bf16[128,256]{1,0:T(8,128)(2,1)S(1)} %collective-permute-done.low_ref, bf16[1024,256]{1,0:T(8,128)(2,1)S(1)} %slice.45.own_ref, bf16[128,256]{1,0:T(8,128)(2,1)S(1)} %collective-permute-done.1.high_ref), custom_call_target="tpu_custom_call" | custom-call | flops 268435456 | bytes 1048576 | tf_op jit(solution)/shard_map/attention_forward/pallas_call | solution.py:143
  76.1 0.9 copy.35
  76.9 6.2 %all-to-all-start.1 = ((bf16[8,128,128]{1,2,0:T(8,128)(2,1)}), bf16[8,128,128]{1,2,0:T(8,128)(2,1)}, u32[]{:S(2)}, u32[]{:S(2)}) async-start(bf16[8,128,128]{1,2,0:T(8,128)(2,1)} %copy.35), calls=%async_computation.1 | async-start | bytes 524288 | tf_op jit(solution)/shard_map/all_to_all | solution.py:213
  83.1 1.9 %fusion.32 = (bf16[128,1024]{1,0:T(8,128)(2,1)}, bf16[128,1024]{1,0:T(8,128)(2,1)}) fusion(bf16[1024,1024]{1,0:T(8,128)(2,1)} %all-gather.9.cloned.1.call-done), kind=kLoop, calls=%fused_computation.50 | loop fusion | bytes 1048576 | tf_op jit(solution)/shard_map/slice | solution.py:210
  85.0 5.7 %collective-permute-start.2 = (bf16[128,1024]{1,0:T(8,128)(2,1)}, bf16[128,1024]{1,0:T(8,128)(2,1)}, u32[]{:S(2)}, u32[]{:S(2)}) collective-permute-start(bf16[128,1024]{1,0:T(8,128)(2,1)} %get-tuple-element.13), channel_id=1, source_target_pairs={{0,16},{1,17},{2,18},{3,19},{4,20},{5,21},{6,22},{7,23},{8,24},{9,... | collective-permute-start | bytes 786440 | tf_op jit(solution)/shard_map/ppermute | solution.py:209
  90.7 1.9 %copy.32 = bf16[2,8,64,1152]{3,2,1,0:T(8,128)(2,1)S(1)} copy(bf16[2,8,64,1152]{3,2,0,1:T(8,128)(2,1)} %bitcast.60) | data formatting | bytes 4718592 | tf_op jit(solution)/shard_map/transpose | solution.py:201
  92.6 1.5 multiply_reduce_fusion.1
  94.1 0.3 fusion.19
  94.4 3.7 %all-gather.5 = f32[2,100,128]{2,1,0:T(8,128)S(1)} all-gather(f32[1,100,128]{2,1,0:T(8,128)S(1)} %bitcast.62), channel_id=5, replica_groups=mesh['half'=2,'group'=8,'ens'=2] {'ens'}, dimensions={0}, use_global_device_ids=true | all-gather | bytes 153600 | tf_op jit(solution)/shard_map/all_gather | solution.py:221
  98.2 0.3 multiply_reduce_fusion
  98.5 0.8 fusion.11
  99.4 0.8 copy.47
  100.1 5.7 %all-to-all-start.2 = ((bf16[8,128,128]{2,1,0:T(8,128)(2,1)}), bf16[8,128,128]{2,1,0:T(8,128)(2,1)S(1)}, u32[]{:S(2)}, u32[]{:S(2)}) async-start(bf16[8,128,128]{2,1,0:T(8,128)(2,1)} %bitcast.49), calls=%async_computation.2 | async-start | bytes 524288 | tf_op jit(solution)/shard_map/all_to_all | solution.py:242
  105.8 1.3 collective-permute-start.3
  107.1 1.7 constant_dynamic-update-slice_fusion.2
  108.7 3.1 %constant_dynamic-update-slice_fusion.1 = bf16[1280,1024]{1,0:T(8,128)(2,1)} fusion(bf16[1280,1024]{1,0:T(8,128)(2,1)} %constant_dynamic-update-slice_fusion.2, bf16[1024,1024]{1,0:T(8,128)(2,1)} %all-gather.9.cloned.1.call-done), kind=kLoop, calls=%fused_computation.42 | loop fusion | bytes 4194304
  111.9 10.5 %collective-permute-done.3 = bf16[128,1024]{1,0:T(8,128)(2,1)S(1)} collective-permute-done((bf16[128,1024]{1,0:T(8,128)(2,1)}, bf16[128,1024]{1,0:T(8,128)(2,1)S(1)}, u32[]{:S(2)}, u32[]{:S(2)}) %collective-permute-start.3) | collective-permute-done | bytes 262176 | tf_op jit(solution)/shard_map/ppermute | solution.py:210
  122.3 0.7 constant_dynamic-update-slice_fusion
  123.0 9.9 %attention_backward.1 = bf16[1280,512]{1,0:T(8,128)(2,1)S(1)} custom-call(s32[16,4]{1,0:T(8,128)S(1)} %bitcast.54, bf16[1024,128]{1,0:T(8,128)(2,1)S(1)} %slice.43.q_ref, bf16[128,256]{1,0:T(8,128)(2,1)S(1)} %collective-permute-done.low_ref, bf16[1024,256]{1,0:T(8,128)(2,1)S(1)} %slice.45.own_ref, bf16[128,256]{1,0:T(8,128)(2,1)S(1)} %collective-permute-done.1.high_ref, ...), custom_call_target="tpu_custom_call" | custom-call | flops 671088640 | bytes 2097152 | tf_op jit(solution)/shard_map/attention_backward/pallas_call | solution.py:160
  133.0 2.6 %fusion.14 = f32[1024,256]{1,0:T(8,128)S(1)} fusion(bf16[1280,1024]{1,0:T(8,128)(2,1)} %constant_dynamic-update-slice_fusion, bf16[1280,512]{1,0:T(8,128)(2,1)S(1)} %attention_backward.1), kind=kOutput, calls=%fused_computation.13 | convolution fusion | flops 671088640 | bytes 4325376 | tf_op jit(solution)/shard_map/dot_general | solution.py:248
  135.6 2.7 %fusion.4 = bf16[1024,256]{1,0:T(8,128)(2,1)S(1)} fusion(f32[1024,256]{1,0:T(8,128)S(1)} %fusion.14, bf16[1280,1024]{1,0:T(8,128)(2,1)} %constant_dynamic-update-slice_fusion, bf16[1280,512]{1,0:T(8,128)(2,1)S(1)} %attention_backward.1), kind=kOutput, calls=%fused_computation.6 | convolution fusion | flops 671612928 | bytes 4849664 | tf_op jit(solution)/shard_map/dot_general | solution.py:247
  138.3 11.9 %all_to_all.25 = bf16[4,8,32,256]{3,2,1,0:T(8,128)(2,1)S(1)} all-to-all(bf16[4,8,32,256]{3,2,1,0:T(8,128)(2,1)S(1)} %bitcast.61), channel_id=1, replica_groups=mesh['half'=2,'group'=8,'ens'=2] {'half','ens'}, dimensions={0} | all-to-all | bytes 1048576 | tf_op jit(solution)/shard_map/all_to_all | solution.py:253
  150.3 0.8 convert_reduce_fusion
  151.0 4.9 %all-to-all-start.4 = ((f32[8,32,256]{2,1,0:T(8,128)}), f32[8,32,256]{2,1,0:T(8,128)S(1)}, u32[]{:S(2)}, u32[]{:S(2)}) async-start(f32[8,32,256]{2,1,0:T(8,128)} %convert_reduce_fusion), calls=%async_computation.4 | async-start | bytes 524288 | tf_op jit(solution)/shard_map/all_to_all | solution.py:255
  155.9 0.7 copy.39
  156.6 4.6 %all-to-all-done.4 = f32[8,32,256]{2,1,0:T(8,128)S(1)} async-done(((f32[8,32,256]{2,1,0:T(8,128)}), f32[8,32,256]{2,1,0:T(8,128)S(1)}, u32[]{:S(2)}, u32[]{:S(2)}) %all-to-all-start.4) | async-done | bytes 262176 | tf_op jit(solution)/shard_map/all_to_all | solution.py:255
  161.3 0.1 reshape.95
  161.4 0.2 copy.38
  161.6 0.8 copy.46
  (26 shorter events, 0.2 us)
Async XLA Ops:
  7.2 24.9 %copy-start.2 = (s32[2,4]{1,0:T(2,128)S(1)}, s32[2,4]{1,0:T(2,128)}, u32[]{:S(2)}) copy-start(s32[2,4]{1,0:T(2,128)} %param.13) | copy-start | bytes 100
  7.2 54.1 %all-gather.9.cloned.1.call-start = ((), (), s32[]{:S(2)}) async-start(), calls=%async_computation.5 | async-start | bytes 2359296 | tf_op jit(solution)/shard_map/all_gather | solution.py:183
  10.1 80.6 %all-gather.11.cloned.1.call-start = ((), (), s32[]{:S(2)}) async-start(), calls=%async_computation.6 | async-start | bytes 2654208 | tf_op jit(solution)/shard_map/all_gather | solution.py:200
  26.9 15.4 %all-to-all-start = ((bf16[8,32,384]{2,1,0:T(8,128)(2,1)}), bf16[8,32,384]{2,1,0:T(8,128)(2,1)S(1)}, u32[]{:S(2)}, u32[]{:S(2)}) async-start(bf16[8,32,384]{2,1,0:T(8,128)(2,1)} %reshape.86), calls=%async_computation | async-start | bytes 393216 | tf_op jit(solution)/shard_map/all_to_all | solution.py:189
  64.2 18.9 %copy-start.3 = (f32[128]{0:T(128)S(1)}, f32[128]{0:T(128)}, u32[]{:S(2)}) copy-start(f32[128]{0:T(128)} %param.12) | copy-start | bytes 1540
  64.2 6.3 %collective-permute-start.1 = (bf16[128,256]{1,0:T(8,128)(2,1)S(1)}, bf16[128,256]{1,0:T(8,128)(2,1)S(1)}, u32[]{:S(2)}, u32[]{:S(2)}) collective-permute-start(bf16[128,256]{1,0:T(8,128)(2,1)S(1)} %get-tuple-element.14), channel_id=1, source_target_pairs={{16,0},{17,1},{18,2},{19,3},{20,4},{21,5},{22,6},{23,7},{24,8},{25... | collective-permute-start | bytes 196616 | tf_op jit(solution)/shard_map/ppermute | solution.py:208
  65.5 6.2 %collective-permute-start = (bf16[128,256]{1,0:T(8,128)(2,1)S(1)}, bf16[128,256]{1,0:T(8,128)(2,1)S(1)}, u32[]{:S(2)}, u32[]{:S(2)}) collective-permute-start(bf16[128,256]{1,0:T(8,128)(2,1)S(1)} %get-tuple-element.15), channel_id=1, source_target_pairs={{0,16},{1,17},{2,18},{3,19},{4,20},{5,21},{6,22},{7,23},{8,24},{9,... | collective-permute-start | bytes 196616 | tf_op jit(solution)/shard_map/ppermute | solution.py:207
  76.9 15.7 %all-to-all-start.1 = ((bf16[8,128,128]{1,2,0:T(8,128)(2,1)}), bf16[8,128,128]{1,2,0:T(8,128)(2,1)}, u32[]{:S(2)}, u32[]{:S(2)}) async-start(bf16[8,128,128]{1,2,0:T(8,128)(2,1)} %copy.35), calls=%async_computation.1 | async-start | bytes 524288 | tf_op jit(solution)/shard_map/all_to_all | solution.py:213
  85.0 22.1 %collective-permute-start.2 = (bf16[128,1024]{1,0:T(8,128)(2,1)}, bf16[128,1024]{1,0:T(8,128)(2,1)}, u32[]{:S(2)}, u32[]{:S(2)}) collective-permute-start(bf16[128,1024]{1,0:T(8,128)(2,1)} %get-tuple-element.13), channel_id=1, source_target_pairs={{0,16},{1,17},{2,18},{3,19},{4,20},{5,21},{6,22},{7,23},{8,24},{9,... | collective-permute-start | bytes 786440 | tf_op jit(solution)/shard_map/ppermute | solution.py:209
  90.7 1.9 %copy-start = (bf16[1,128,1024]{2,1,0:T(8,128)(2,1)S(1)}, bf16[1,128,1024]{2,1,0:T(8,128)(2,1)}, u32[]{:S(2)}) copy-start(bf16[1,128,1024]{2,1,0:T(8,128)(2,1)} %param.7) | copy-start | bytes 786436
  92.6 5.6 %copy-start.1 = (f32[100,128]{1,0:T(8,128)S(1)}, f32[100,128]{1,0:T(8,128)}, u32[]{:S(2)}) copy-start(f32[100,128]{1,0:T(8,128)} %param.11) | copy-start | bytes 153604
  100.1 22.9 %all-to-all-start.2 = ((bf16[8,128,128]{2,1,0:T(8,128)(2,1)}), bf16[8,128,128]{2,1,0:T(8,128)(2,1)S(1)}, u32[]{:S(2)}, u32[]{:S(2)}) async-start(bf16[8,128,128]{2,1,0:T(8,128)(2,1)} %bitcast.49), calls=%async_computation.2 | async-start | bytes 524288 | tf_op jit(solution)/shard_map/all_to_all | solution.py:242
  105.8 16.5 %collective-permute-start.3 = (bf16[128,1024]{1,0:T(8,128)(2,1)}, bf16[128,1024]{1,0:T(8,128)(2,1)S(1)}, u32[]{:S(2)}, u32[]{:S(2)}) collective-permute-start(bf16[128,1024]{1,0:T(8,128)(2,1)} %get-tuple-element.12), channel_id=1, source_target_pairs={{16,0},{17,1},{18,2},{19,3},{20,4},{21,5},{22,6},{23,7},{24,8},{25... | collective-permute-start | bytes 786440 | tf_op jit(solution)/shard_map/ppermute | solution.py:210
  151.0 10.2 %all-to-all-start.4 = ((f32[8,32,256]{2,1,0:T(8,128)}), f32[8,32,256]{2,1,0:T(8,128)S(1)}, u32[]{:S(2)}, u32[]{:S(2)}) async-start(f32[8,32,256]{2,1,0:T(8,128)} %convert_reduce_fusion), calls=%async_computation.4 | async-start | bytes 524288 | tf_op jit(solution)/shard_map/all_to_all | solution.py:255
Sparse Core Ops, SparseCore 0:
  10.2 25.7 all-gather.8
  37.6 29.5 all-gather.10

commit v2 on v1

v2 whole, which is shorter than its diff:
```python
import functools

import jax
import jax.numpy as jnp
from jax import lax
from jax.experimental import pallas as pl
from jax.experimental.pallas import tpu as pltpu
from jax.sharding import Mesh
from jax.sharding import PartitionSpec as P

LATENT_DIM = 1024
HEADS = 16
HEAD = 64
FIELD_NUM = 100
TILE = 64
RADIUS = 2
K_NB = 4
QUAD = 4
CORES = 2
GROUP = QUAD * CORES
COLS = LATENT_DIM // GROUP
RIM = RADIUS * TILE
FIELD_PAD = 128

NORM_EPS = 1e-06
SOFT_WIDTH = 0.0625
MASKED = -1e30

F32 = jnp.float32
BF16 = jnp.bfloat16

VMEM = pl.BlockSpec(memory_space=pltpu.VMEM)
SMEM = pl.BlockSpec(memory_space=pltpu.SMEM)
OVER_ROWS = (((0,), (0,)), ((), ()))
OVER_COLUMNS = (((1,), (1,)), ((), ()))


def call(kernel, name, outs, ins, scratch=(), flops=0, moved=0, exps=0):
    return pl.pallas_call(
        kernel,
        out_shape=[jax.ShapeDtypeStruct(shape, kind) for shape, kind in outs],
        in_specs=[SMEM if space == "s" else VMEM for space in ins],
        out_specs=[VMEM] * len(outs),
        scratch_shapes=[pltpu.VMEM(shape, kind) for shape, kind in scratch],
        compiler_params=pltpu.CompilerParams(vmem_limit_bytes=32 * 2**20),
        cost_estimate=pl.CostEstimate(flops=flops, bytes_accessed=moved, transcendentals=exps),
        name=name,
    )


def norm_kernel(source_ref, out_ref):
    source = source_ref[...].astype(F32)
    inverse = lax.rsqrt(jnp.mean(source * source, axis=-1, keepdims=True) + NORM_EPS)
    normed = (source * inverse).astype(BF16)
    for copy in range(out_ref.shape[0]):
        out_ref[copy] = normed


def project_kernel(core_ref, mine_ref, other_ref, w_ref, q_ref, kv_ref, rims_ref, normed_rims_ref):
    core = core_ref[0]
    block = mine_ref.shape[1]
    for rows_ref, owner in ((mine_ref, core), (other_ref, 1 - core)):
        for quad in range(QUAD):
            rows = rows_ref[quad]
            projected = jnp.dot(rows, w_ref[...], preferred_element_type=F32).astype(BF16)
            at = pl.ds(pl.multiple_of((quad * CORES + owner) * block, block), block)
            q_ref[at, :] = projected[:, :COLS]
            kv_ref[at, :] = projected[:, COLS:]
            if quad == 0:

                @pl.when(owner == 0)
                def _():
                    rims_ref[0] = projected[:RIM, COLS:]
                    normed_rims_ref[0] = rows[:RIM]

            if quad == QUAD - 1:

                @pl.when(owner == CORES - 1)
                def _():
                    rims_ref[1] = projected[block - RIM :, COLS:]
                    normed_rims_ref[1] = rows[block - RIM :]


def by_head(rows):
    lane = lax.broadcasted_iota(jnp.int32, rows.shape, 1)
    zero = jnp.zeros_like(rows)
    return jnp.concatenate(
        [jnp.where(lane < HEAD, rows, zero), jnp.where(lane < HEAD, zero, rows)], axis=0
    )


def tile_keys(slots_ref, first, tile, last_tile, kv):
    lane = lax.broadcasted_iota(jnp.int32, (1, K_NB * TILE), 1)
    usable = jnp.zeros((1, K_NB * TILE), jnp.int32)
    places, keys, values = [], [], []
    for slot in range(K_NB):
        at = slots_ref[tile, slot]
        usable = jnp.where(lane // TILE == slot, (at >= 0).astype(jnp.int32), usable)
        place = jnp.clip(at - first + RADIUS, 0, last_tile) * TILE
        place = pl.multiple_of(place, TILE)
        places.append(place)
        keys.append(kv[pl.ds(place, TILE), :COLS])
        values.append(kv[pl.ds(place, TILE), COLS:])
    return places, usable > 0, jnp.concatenate(keys, axis=0), jnp.concatenate(values, axis=0)


def probabilities(queries, keys, usable):
    scores = lax.dot_general(queries, keys, OVER_COLUMNS, preferred_element_type=F32) * (HEAD**-0.5)
    scores = jnp.where(usable, scores, MASKED)
    raised = jnp.exp(scores - jnp.max(scores, axis=-1, keepdims=True))
    return raised * (1.0 / jnp.sum(raised, axis=-1, keepdims=True))


def fill(kv, low_ref, own_ref, high_ref):
    rows = own_ref.shape[0]
    kv[0:RIM, :] = low_ref[...]
    kv[RIM : RIM + rows, :] = own_ref[...]
    kv[RIM + rows : 2 * RIM + rows, :] = high_ref[...]


def forward_kernel(where_ref, slots_ref, q_ref, low_ref, own_ref, high_ref, out_ref, kv):
    tiles = q_ref.shape[0] // TILE
    last_tile = tiles + 2 * RADIUS - 1
    fill(kv, low_ref, own_ref, high_ref)

    def step(tile, carry):
        rows = pl.ds(pl.multiple_of(tile * TILE, TILE), TILE)
        _, usable, keys, values = tile_keys(slots_ref, where_ref[1], tile, last_tile, kv)
        probs = probabilities(by_head(q_ref[rows, :]), keys, usable)
        both = jnp.dot(probs.astype(BF16), values, preferred_element_type=F32)
        lane = lax.broadcasted_iota(jnp.int32, (TILE, COLS), 1)
        out_ref[rows, :] = jnp.where(lane < HEAD, both[:TILE], both[TILE:]).astype(BF16)
        return carry

    lax.fori_loop(0, tiles, step, 0, unroll=4)


def backward_kernel(
    where_ref, slots_ref, q_ref, low_ref, own_ref, high_ref, g_ref, out_ref, kv, total
):
    tiles = q_ref.shape[0] // TILE
    last_tile = tiles + 2 * RADIUS - 1
    fill(kv, low_ref, own_ref, high_ref)
    total[...] = jnp.zeros_like(total)

    def step(tile, carry):
        rows = pl.ds(pl.multiple_of(tile * TILE, TILE), TILE)
        places, usable, keys, values = tile_keys(slots_ref, where_ref[1], tile, last_tile, kv)
        queries = by_head(q_ref[rows, :])
        grads = by_head(g_ref[rows, :])
        probs = probabilities(queries, keys, usable)
        grad_probs = lax.dot_general(grads, values, OVER_COLUMNS, preferred_element_type=F32)
        row_delta = jnp.sum(probs * grad_probs, axis=-1, keepdims=True)
        grad_scores = (probs * (grad_probs - row_delta) * (HEAD**-0.5)).astype(BF16)
        key_grad = lax.dot_general(grad_scores, queries, OVER_ROWS, preferred_element_type=F32)
        value_grad = lax.dot_general(
            probs.astype(BF16), grads, OVER_ROWS, preferred_element_type=F32
        )
        key_grad = key_grad.astype(BF16).astype(F32)
        value_grad = value_grad.astype(BF16).astype(F32)
        for slot in range(K_NB):
            part = slice(slot * TILE, (slot + 1) * TILE)
            total[pl.ds(places[slot], TILE), :COLS] += key_grad[part]
            total[pl.ds(places[slot], TILE), COLS:] += value_grad[part]
        return carry

    lax.fori_loop(0, tiles, step, 0, unroll=2)

    core = where_ref[0]
    rows = q_ref.shape[0]
    block = rows // GROUP

    def split(to, place, count):
        both = total[pl.ds(place, count), :]
        high = both.astype(BF16)
        out_ref[to : to + count, : 2 * COLS] = high
        out_ref[to : to + count, 2 * COLS :] = (both - high.astype(F32)).astype(BF16)

    for at, owner in ((0, core), (QUAD, 1 - core)):
        for quad in range(QUAD):
            place = pl.multiple_of((quad * CORES + owner) * block + RIM, RIM)
            split((at + quad) * block, place, block)
    split(rows, 0, RIM)
    split(rows + RIM, rows + RIM, RIM)


def slope(spread):
    return spread * lax.rsqrt(spread * spread + SOFT_WIDTH)


def mix_kernel(att_ref, source_ref, packed_ref, truth_ref, factor_ref, pred_ref, grad_ref, w, a):
    group, halves, block, _ = packed_ref.shape
    members_num, part, _ = source_ref.shape
    for g in range(group):
        for half in range(halves):
            at = (half * group + g) * block
            w[at : at + block, :] = packed_ref[g, half]
        for m in range(members_num):
            a[m * part : (m + 1) * part, g * COLS : (g + 1) * COLS] = att_ref[g * members_num + m]
    mix, readout = w[:, :LATENT_DIM], w[:, LATENT_DIM:]
    rows = members_num * part
    source = source_ref[...].reshape(rows, LATENT_DIM).astype(F32)
    hidden = source + jnp.dot(a[...], mix, preferred_element_type=F32)
    inverse = lax.rsqrt(jnp.mean(hidden * hidden, axis=-1, keepdims=True) + NORM_EPS)
    decoded = (hidden * inverse).astype(BF16)
    prediction = lax.dot_general(
        readout, decoded, (((0,), (1,)), ((), ())), preferred_element_type=F32
    )
    pred_ref[...] = prediction[:FIELD_NUM]
    spread = jnp.zeros_like(prediction)
    for other in range(1, members_num):
        spread = spread + slope(prediction - pltpu.roll(prediction, other * part, 1))
    derivative = factor_ref[...] / FIELD_NUM * (
        slope(prediction - truth_ref[...]) - spread / (members_num - 1)
    )
    grad_decoded = lax.dot_general(
        derivative.astype(BF16), readout, (((0,), (1,)), ((), ())), preferred_element_type=F32
    )
    grad_hidden = inverse * grad_decoded - hidden * inverse**3 * jnp.mean(
        grad_decoded * hidden, axis=-1, keepdims=True
    )
    grads = lax.dot_general(
        grad_hidden.astype(BF16), mix, OVER_COLUMNS, preferred_element_type=F32
    ).astype(BF16)
    for g in range(group):
        for m in range(members_num):
            grad_ref[g * members_num + m] = grads[
                m * part : (m + 1) * part, g * COLS : (g + 1) * COLS
            ]


def product_kernel(mine_ref, other_ref, rims_ref, kv_ref, out_ref):
    def term(rows, at):
        both = lax.dot_general(
            rows, kv_ref[at : at + rows.shape[0], :], OVER_ROWS, preferred_element_type=F32
        )
        return both[:, : 2 * COLS] + both[:, 2 * COLS :]

    count = mine_ref.shape[0] * mine_ref.shape[1]
    total = term(mine_ref[...].reshape(count, LATENT_DIM), 0)
    total += term(other_ref[...].reshape(count, LATENT_DIM), count)
    total += term(rims_ref[...].reshape(2 * RIM, LATENT_DIM), 2 * count)
    out_ref[...] = total.astype(BF16)


def exchange(chunks, axes):
    return lax.all_to_all(chunks, axes, 0, 0)


def body(members, w_attn, w_mix, readout_matrix, observed_truth, cell_surface_factor, neighbours):
    halves, members_num = lax.axis_size("half"), lax.axis_size("ens")
    everyone = ("half", "quad", "core", "ens")
    shard = w_attn.shape[0]
    node_rows = members.shape[1]
    rows = GROUP * node_rows
    part = node_rows // members_num
    tiles = rows // TILE
    up = [(i, i + 1) for i in range(halves - 1)]
    down = [(target, source) for source, target in up]
    core, ens = lax.axis_index("core"), lax.axis_index("ens")
    where = jnp.stack([core, lax.axis_index("half") * tiles]).astype(jnp.int32)

    (normed,) = call(
        norm_kernel, "norm", [((QUAD, node_rows, LATENT_DIM), BF16)], "v", flops=10, moved=2**20
    )(members.reshape(node_rows, LATENT_DIM))
    mine = exchange(normed, "quad")
    other = lax.ppermute(mine, "core", [(i, (i + 1) % CORES) for i in range(CORES)])

    columns = w_attn.reshape(shard, 3, GROUP, COLS).transpose(2, 0, 1, 3)
    columns = columns.reshape(1, GROUP, 1, shard, 3 * COLS)
    columns = jnp.broadcast_to(columns, (halves, GROUP, members_num, shard, 3 * COLS))
    columns = exchange(columns.reshape(-1, shard, 3 * COLS), everyone)
    columns = columns.reshape(LATENT_DIM, 3 * COLS)

    packed = jnp.concatenate(
        [w_mix, jnp.pad(readout_matrix, ((0, 0), (0, FIELD_PAD - FIELD_NUM)))], axis=1
    )
    width = packed.shape[1]
    packed = jnp.broadcast_to(packed, (halves * members_num, shard, width))
    packed = exchange(packed, ("half", "ens"))
    packed = lax.all_gather(packed, ("quad", "core"), axis=0)
    packed = packed.reshape(GROUP, halves, members_num * shard, width)

    slots = exchange(jnp.broadcast_to(neighbours, (GROUP,) + neighbours.shape), ("quad", "core"))
    slots = slots.reshape(tiles, K_NB)
    sources = exchange(members.reshape(members_num, part, LATENT_DIM), "ens")
    truth = lax.dynamic_slice_in_dim(observed_truth, ens * part, part, 1)
    truth = jnp.tile(jnp.pad(truth, ((0, FIELD_PAD - FIELD_NUM), (0, 0))), (1, members_num))
    factor = lax.dynamic_slice_in_dim(cell_surface_factor, ens * part, part, 0)
    factor = jnp.tile(factor[None], (1, members_num))

    queries, own, rims, normed_rims = call(
        project_kernel,
        "project",
        [
            ((rows, COLS), BF16),
            ((rows, 2 * COLS), BF16),
            ((2, RIM, 2 * COLS), BF16),
            ((2, RIM, LATENT_DIM), BF16),
        ],
        "svvv",
        flops=rows * LATENT_DIM * 6 * COLS,
        moved=4 * 2**20,
    )(where, mine, other, columns)
    low = lax.ppermute(rims[1], "half", up)
    high = lax.ppermute(rims[0], "half", down)
    normed_low = lax.ppermute(normed_rims[1], "half", up)
    normed_high = lax.ppermute(normed_rims[0], "half", down)

    (outcome,) = call(
        forward_kernel,
        "attention_forward",
        [((rows, COLS), BF16)],
        "ssvvvv",
        [((rows + 2 * RIM, 2 * COLS), BF16)],
        flops=rows * COLS * 2048,
        moved=2**21,
        exps=rows * 512,
    )(where, slots, queries, low, own, high)
    attended = exchange(outcome.reshape(GROUP * members_num, part, COLS), ("quad", "core", "ens"))

    prediction, grads = call(
        mix_kernel,
        "mix_loss_backward",
        [((FIELD_NUM, node_rows), F32), ((GROUP * members_num, part, COLS), BF16)],
        "vvvvv",
        [((LATENT_DIM, width), BF16), ((node_rows, LATENT_DIM), BF16)],
        flops=node_rows * LATENT_DIM * 4 * width,
        moved=2**22,
    )(attended, sources, packed, truth, factor)
    grads = exchange(grads, ("quad", "core", "ens")).reshape(rows, COLS)

    normed_low, normed_high, grads = lax.optimization_barrier((normed_low, normed_high, grads))
    (kv_grads,) = call(
        backward_kernel,
        "attention_backward",
        [((rows + 2 * RIM, 4 * COLS), BF16)],
        "ssvvvvv",
        [((rows + 2 * RIM, 2 * COLS), BF16), ((rows + 2 * RIM, 2 * COLS), F32)],
        flops=rows * COLS * 5120,
        moved=2**22,
        exps=rows * 512,
    )(where, slots, queries, low, own, high, grads)
    (term,) = call(
        product_kernel,
        "product",
        [((LATENT_DIM, 2 * COLS), BF16)],
        "vvvv",
        flops=(rows + 2 * RIM) * LATENT_DIM * 8 * COLS,
        moved=2**22,
    )(mine, other, jnp.stack([normed_low, normed_high]), kv_grads)
    term = exchange(term.reshape(-1, shard, 2 * COLS), everyone)
    term = term.reshape(halves, GROUP, members_num, shard, 2, COLS).astype(F32)
    grad_kv = jnp.sum(term, axis=(0, 2)).transpose(1, 2, 0, 3).reshape(shard, 2 * LATENT_DIM)

    prediction = prediction.reshape(FIELD_NUM, members_num, part).transpose(1, 0, 2)
    prediction = exchange(prediction, "ens").transpose(1, 0, 2).reshape(1, FIELD_NUM, node_rows)
    return (prediction, grad_kv)


def solution(mesh):
    space, ens = mesh.shape["space"], mesh.shape["ens"]
    split = Mesh(
        mesh.devices.reshape(space // GROUP, QUAD, CORES, ens), ("half", "quad", "core", "ens")
    )
    nodes = ("half", "quad", "core")
    shards = nodes + ("ens",)
    in_specs = (
        P("ens", nodes, None),
        P(shards, None),
        P(shards, None),
        P(shards, None),
        P(None, nodes),
        P(nodes),
        P(nodes, None),
    )
    out_specs = (P("ens", None, nodes), P(shards, None))
    return jax.shard_map(body, mesh=split, in_specs=in_specs, out_specs=out_specs, check_vma=False)
```

time: 171 us -> 188 us (1.099)
  waiting for transfers between devices: 16.4 us -> 75.5 us
  blocking collectives: 58.6 us -> 15.1 us
  matrix products: 11.2 us -> 0 us
  Pallas kernels: 14.2 us -> 24.5 us
  starting transfers between devices: 35.1 us -> 43.6 us
  local copies, waits for them, and re-layouts: 14.8 us -> 11.8 us
  other arithmetic: 4.57 us -> 1.74 us
    all_to_all x4 -> x8, waiting for transfers between devices: 4.65 us -> 63.3 us  [exchange(): return lax.all_to_all(chunks, axes, 0, 0)]
    all_gather x5 -> x0, blocking collectives: 46.7 us -> none  [the longest x1 18.9 us: body(): columns = lax.all_gather(columns, ('half', 'ens'), axis=0)]
    all_to_all x4 -> x8, starting transfers between devices: 21.9 us -> 36 us  [exchange(): return lax.all_to_all(chunks, axes, 0, 0)]
    dot_general x7 -> x0, matrix products: 11.2 us -> none  [the longest x1 2.88 us: body(): jnp.dot(normed_all, columns, preferred_element_type=F32).astype(BF16)]
    pallas_call x2 -> x6, Pallas kernels: 14.2 us -> 24.5 us  [the longest x1 9.87 us: body(): call(backward_kernel, 'attention_backward', [((rows + 2 * RIM, 4 * COLS),...]
    ppermute x4 -> x5, starting transfers between devices: 13.2 us -> 7.63 us  [the longest x1 3.43 us: body(): low = lax.ppermute(rims[1], 'half', up)]
    all_to_all x1, blocking collectives: 11.9 us -> 15.1 us  [exchange(): return lax.all_to_all(chunks, axes, 0, 0)]
    reshape x6 -> x1, local copies, waits for them, and re-layouts: 2.72 us -> 0.1 us  [body(): columns = w_attn.reshape(shard, 3, GROUP, COLS).transpose(2, 0, 1, 3)]
  transfers between devices with their start and end apart: 10 -> 14, of which waited for: 3 -> 7; matrix products, arithmetic and copies ran while one was open for 12% -> 2% of each run, Pallas kernels for 3% -> 12%
where the time goes in v2:
time: 188 us; the launch traced here: 187 us
  waiting for transfers between devices  75.5 us (40%)
  starting transfers between devices  43.6 us (23%)
  Pallas kernels  24.5 us (13%)
  blocking collectives  15.1 us (8%)
  between operations  14.3 us (8%)
  local copies, waits for them, and re-layouts  11.8 us (6%)
    all_to_all x8, waiting for transfers between devices, exchange(): return lax.all_to_all(chunks, axes, 0, 0)  63.3 us
    all_to_all x8, starting transfers between devices, exchange(): return lax.all_to_all(chunks, axes, 0, 0)  36 us
    all_to_all x1, blocking collectives, exchange(): return lax.all_to_all(chunks, axes, 0, 0)  15.1 us
    pallas_call x1, Pallas kernels, body(): call(backward_kernel, 'attention_backward', [((rows + 2 * RIM, 4 * COLS),...  9.87 us
    ppermute x1, waiting for transfers between devices, body(): normed_high = lax.ppermute(normed_rims[0], 'half', down)  7.62 us
    unnamed x24, local copies, waits for them, and re-layouts  7.49 us
    pallas_call x1, Pallas kernels, body(): call(forward_kernel, 'attention_forward', [((rows, COLS), BF16)], 'ssvvvv...  5.01 us
    ppermute x1, waiting for transfers between devices, body(): high = lax.ppermute(rims[0], 'half', down)  4.6 us
  transfers between devices with their start and end apart: 14, of which 7 were waited for; matrix products, arithmetic and copies ran while one was open for 2% of the time, Pallas kernels for 12%

profile of v2, /device:TPU:1, one launch (start us, length us, event | category | flops | bytes accessed | tf_op | source)
XLA Modules:
  0.0 186.6 jit_solution(5959801139002946960)
XLA Ops:
  7.2 0.9 fusion.1
  8.1 15.1 %all_to_all.45 = bf16[4,32,1152]{2,1,0:T(8,128)(2,1)} all-to-all(bf16[4,32,1152]{2,1,0:T(8,128)(2,1)S(1)} %broadcast_in_dim.16), channel_id=1, replica_groups=mesh['half'=2,'quad'=4,'core'=2,'ens'=2] {'half','ens'}, dimensions={0} | all-to-all | bytes 589824 | tf_op jit(solution)/shard_map/all_to_all | solution.py:247
  23.2 2.1 %norm.1 = bf16[4,128,1024]{2,1,0:T(8,128)(2,1)} custom-call(bf16[128,1024]{1,0:T(8,128)(2,1)} %bitcast.3.source_ref), custom_call_target="tpu_custom_call" | custom-call | flops 10 | bytes 1048576 | tf_op jit(solution)/shard_map/norm/pallas_call | solution.py:263
  25.3 3.5 %all-to-all-start.1 = ((bf16[4,128,1024]{2,1,0:T(8,128)(2,1)}), bf16[4,128,1024]{2,1,0:T(8,128)(2,1)S(1)}, u32[]{:S(2)}, u32[]{:S(2)}) async-start(bf16[4,128,1024]{2,1,0:T(8,128)(2,1)} %norm.1), calls=%async_computation.1 | async-start | bytes 2097152 | tf_op jit(solution)/shard_map/all_to_all | solution.py:247
  28.9 0.1 copy.31
  29.0 0.2 broadcast_in_dim.14
  29.2 18.4 %all-to-all-done.1.mine_ref = bf16[4,128,1024]{2,1,0:T(8,128)(2,1)S(1)} async-done(((bf16[4,128,1024]{2,1,0:T(8,128)(2,1)}), bf16[4,128,1024]{2,1,0:T(8,128)(2,1)S(1)}, u32[]{:S(2)}, u32[]{:S(2)}) %all-to-all-start.1) | async-done | bytes 1048608 | tf_op jit(solution)/shard_map/all_to_all | solution.py:247
  47.5 1.0 broadcast_in_dim.15
  48.5 7.4 %all-to-all-start.2 = ((bf16[32,32,384]{2,1,0:T(8,128)(2,1)}), bf16[32,32,384]{2,1,0:T(8,128)(2,1)S(1)}, u32[]{:S(2)}, u32[]{:S(2)}) async-start(bf16[32,32,384]{2,1,0:T(8,128)(2,1)} %bitcast.5), calls=%async_computation.2 | async-start | bytes 1572864 | tf_op jit(solution)/shard_map/all_to_all | solution.py:247
  56.0 0.3 collective-permute-start
  56.4 20.5 %all-to-all-done.2 = bf16[32,32,384]{2,1,0:T(8,128)(2,1)S(1)} async-done(((bf16[32,32,384]{2,1,0:T(8,128)(2,1)}), bf16[32,32,384]{2,1,0:T(8,128)(2,1)S(1)}, u32[]{:S(2)}, u32[]{:S(2)}) %all-to-all-start.2) | async-done | bytes 786464 | tf_op jit(solution)/shard_map/all_to_all | solution.py:247
  76.9 0.6 broadcast_in_dim.13
  77.5 3.3 %all-to-all-start = ((s32[8,2,4]{2,1,0:T(2,128)}), s32[8,2,4]{2,1,0:T(2,128)S(1)}, u32[]{:S(2)}, u32[]{:S(2)}) async-start(s32[8,2,4]{2,1,0:T(2,128)} %broadcast_in_dim.13), calls=%async_computation | async-start | bytes 16384 | tf_op jit(solution)/shard_map/all_to_all | solution.py:247
  80.8 0.9 copy-done.4
  81.8 1.2 copy-done.5
  83.0 2.4 %project.1 = (bf16[1024,128]{1,0:T(8,128)(2,1)S(1)}, bf16[1024,256]{1,0:T(8,128)(2,1)S(1)}, bf16[2,128,256]{2,1,0:T(8,128)(2,1)S(1)}, bf16[2,128,1024]{2,1,0:T(8,128)(2,1)S(1)}) custom-call(s32[2]{0:T(128)S(1)} %pad_add_fusion.core_ref.where_ref, bf16[4,128,1024]{2,1,0:T(8,128)(2,1)S(1)} %all-to-all-done.1.mine_ref, bf16[4,128,1024]{2,1,0:T(8,128)(2,1)S(1)} %copy-done.5, ...), custom_call_target="tpu_custom_call" | custom-call | flops 805306368 | bytes 4194304 | tf_op jit(solution)/shard_map/project/pallas_call | solution.py:292
  85.3 0.8 copy-done.2
  86.1 3.4 %all-to-all-start.4 = ((bf16[2,64,1024]{2,1,0:T(8,128)(2,1)}), bf16[2,64,1024]{2,1,0:T(8,128)(2,1)S(1)}, u32[]{:S(2)}, u32[]{:S(2)}) async-start(bf16[2,64,1024]{2,1,0:T(8,128)(2,1)} %bitcast.10), calls=%async_computation.4 | async-start | bytes 524288 | tf_op jit(solution)/shard_map/all_to_all | solution.py:247
  89.6 3.4 %collective-permute-start.1 = (bf16[128,256]{1,0:T(8,128)(2,1)S(1)}, bf16[128,256]{1,0:T(8,128)(2,1)S(1)}, u32[]{:S(2)}, u32[]{:S(2)}) collective-permute-start(bf16[128,256]{1,0:T(8,128)(2,1)S(1)} %get-tuple-element.29), channel_id=1, source_target_pairs={{0,16},{1,17},{2,18},{3,19},{4,20},{5,21},{6,22},{7,23},{8,24},{9,... | collective-permute-start | bytes 196616 | tf_op jit(solution)/shard_map/ppermute | solution.py:305
  93.1 1.3 collective-permute-start.2
  94.4 4.6 %collective-permute-done.2.high_ref = bf16[128,256]{1,0:T(8,128)(2,1)S(1)} collective-permute-done((bf16[128,256]{1,0:T(8,128)(2,1)S(1)}, bf16[128,256]{1,0:T(8,128)(2,1)S(1)}, u32[]{:S(2)}, u32[]{:S(2)}) %collective-permute-start.2) | collective-permute-done | bytes 65568 | tf_op jit(solution)/shard_map/ppermute | solution.py:306
  99.0 5.0 %attention_forward.1 = bf16[1024,128]{1,0:T(8,128)(2,1)} custom-call(s32[2]{0:T(128)S(1)} %pad_add_fusion.core_ref.where_ref, s32[16,4]{1,0:T(8,128)S(1)} %bitcast.43, bf16[1024,128]{1,0:T(8,128)(2,1)S(1)} %get-tuple-element.11.q_ref, bf16[128,256]{1,0:T(8,128)(2,1)S(1)} %collective-permute-done.1.low_ref, bf16[1024,256]{1,0:T(8,128)(2,1)S(1)} %get-tuple-element.13.own_ref, ...), custom_call_target="tpu_custom_call" | custom-call | flops 268435456 | bytes 2097152 | tf_op jit(solution)/shard_map/attention_forward/pallas_call | solution.py:310
  104.0 7.3 %all-to-all-start.3 = ((bf16[16,64,128]{2,1,0:T(8,128)(2,1)}), bf16[16,64,128]{2,1,0:T(8,128)(2,1)S(1)}, u32[]{:S(2)}, u32[]{:S(2)}) async-start(bf16[16,64,128]{2,1,0:T(8,128)(2,1)} %bitcast.9), calls=%async_computation.3 | async-start | bytes 524288 | tf_op jit(solution)/shard_map/all_to_all | solution.py:247
  111.2 0.1 constant_dynamic-slice_fusion
  111.4 0.1 copy.21.truth_ref
  111.5 0.1 dynamic_slice.7
  111.6 0.1 tile.20.factor_ref
  111.7 6.4 %all-to-all-done.3.att_ref = bf16[16,64,128]{2,1,0:T(8,128)(2,1)S(1)} async-done(((bf16[16,64,128]{2,1,0:T(8,128)(2,1)}), bf16[16,64,128]{2,1,0:T(8,128)(2,1)S(1)}, u32[]{:S(2)}, u32[]{:S(2)}) %all-to-all-start.3) | async-done | bytes 262176 | tf_op jit(solution)/shard_map/all_to_all | solution.py:247
  118.1 1.7 copy-done.1
  119.8 2.7 %mix_loss_backward.1 = (f32[100,128]{1,0:T(8,128)S(1)}, bf16[16,64,128]{2,1,0:T(8,128)(2,1)}) custom-call(bf16[16,64,128]{2,1,0:T(8,128)(2,1)S(1)} %all-to-all-done.3.att_ref, bf16[2,64,1024]{2,1,0:T(8,128)(2,1)S(1)} %all-to-all-done.4.source_ref, bf16[8,2,64,1152]{3,2,1,0:T(8,128)(2,1)S(1)} %bitcast.40, f32[128,128]{1,0:T(8,128)S(1)} %copy.21.truth_ref, ...), custom_call_target="tpu_custom_call" | custom-call | flops 603979776 | bytes 4194304 | tf_op jit(solution)/shard_map/mix_loss_backward/pallas_call | solution.py:322
  122.5 3.7 %all-to-all-start.7 = ((bf16[16,64,128]{2,1,0:T(8,128)(2,1)}), bf16[16,64,128]{2,1,0:T(8,128)(2,1)S(1)}, u32[]{:S(2)}, u32[]{:S(2)}) async-start(bf16[16,64,128]{2,1,0:T(8,128)(2,1)} %get-tuple-element.16), calls=%async_computation.7 | async-start | bytes 524288 | tf_op jit(solution)/shard_map/all_to_all | solution.py:247
  126.2 0.7 slice_bitcast_fusion
  127.0 1.3 collective-permute-start.3
  128.3 1.3 collective-permute-start.4
  129.6 0.7 copy.22
  130.3 2.9 %all-to-all-done.7 = bf16[16,64,128]{2,1,0:T(8,128)(2,1)S(1)} async-done(((bf16[16,64,128]{2,1,0:T(8,128)(2,1)}), bf16[16,64,128]{2,1,0:T(8,128)(2,1)S(1)}, u32[]{:S(2)}, u32[]{:S(2)}) %all-to-all-start.7) | async-done | bytes 262176 | tf_op jit(solution)/shard_map/all_to_all | solution.py:247
  133.2 3.3 %all-to-all-start.6 = ((f32[2,100,64]{1,2,0:T(8,128)}), f32[2,100,64]{1,2,0:T(8,128)S(1)}, u32[]{:S(2)}, u32[]{:S(2)}) async-start(f32[2,100,64]{1,2,0:T(8,128)} %bitcast.14), calls=%async_computation.6 | async-start | bytes 131072 | tf_op jit(solution)/shard_map/all_to_all | solution.py:247
  136.5 7.6 %collective-permute-done.4 = bf16[128,1024]{1,0:T(8,128)(2,1)S(1)} collective-permute-done((bf16[128,1024]{1,0:T(8,128)(2,1)S(1)}, bf16[128,1024]{1,0:T(8,128)(2,1)S(1)}, u32[]{:S(2)}, u32[]{:S(2)}) %collective-permute-start.4) | collective-permute-done | bytes 262176 | tf_op jit(solution)/shard_map/ppermute | solution.py:308
  144.1 9.9 %attention_backward.1.kv_ref = bf16[1280,512]{1,0:T(8,128)(2,1)S(1)} custom-call(s32[2]{0:T(128)S(1)} %pad_add_fusion.core_ref.where_ref, s32[16,4]{1,0:T(8,128)S(1)} %bitcast.44, bf16[1024,128]{1,0:T(8,128)(2,1)S(1)} %get-tuple-element.11.q_ref, bf16[128,256]{1,0:T(8,128)(2,1)S(1)} %collective-permute-done.1.low_ref, ...), custom_call_target="tpu_custom_call" | custom-call | flops 671088640 | bytes 4194304 | tf_op jit(solution)/shard_map/attention_backward/pallas_call | solution.py:334
  154.0 1.2 copy-done.6
  155.3 2.4 %product.1 = bf16[1024,256]{1,0:T(8,128)(2,1)} custom-call(bf16[4,128,1024]{2,1,0:T(8,128)(2,1)S(1)} %all-to-all-done.1.mine_ref, bf16[4,128,1024]{2,1,0:T(8,128)(2,1)S(1)} %copy-done.6, bf16[2,128,1024]{2,1,0:T(8,128)(2,1)S(1)} %pad_maximum_fusion.rims_ref, bf16[1280,512]{1,0:T(8,128)(2,1)S(1)} %attention_backward.1.kv_ref), custom_call_target="tpu_custom_call" | custom-call | flops 1342177280 | bytes 4194304 | tf_op jit(solution)/shard_map/product/pallas_call | solution.py:344
  157.7 4.0 %all-to-all-start.8 = ((bf16[32,32,256]{2,1,0:T(8,128)(2,1)}), bf16[32,32,256]{2,1,0:T(8,128)(2,1)S(1)}, u32[]{:S(2)}, u32[]{:S(2)}) async-start(bf16[32,32,256]{2,1,0:T(8,128)(2,1)} %bitcast.22), calls=%async_computation.8 | async-start | bytes 1048576 | tf_op jit(solution)/shard_map/all_to_all | solution.py:247
  161.7 0.7 copy.24
  162.4 15.1 %all-to-all-done.8 = bf16[32,32,256]{2,1,0:T(8,128)(2,1)S(1)} async-done(((bf16[32,32,256]{2,1,0:T(8,128)(2,1)}), bf16[32,32,256]{2,1,0:T(8,128)(2,1)S(1)}, u32[]{:S(2)}, u32[]{:S(2)}) %all-to-all-start.8) | async-done | bytes 524320 | tf_op jit(solution)/shard_map/all_to_all | solution.py:247
  177.5 0.5 reshape.71
  178.0 0.8 reduce_sum.9
  178.8 0.2 copy.23
  178.9 0.8 copy.30
  (33 shorter events, 0.4 us)
Async XLA Ops:
  7.2 104.1 %copy-start = (f32[100,128]{1,0:T(8,128)S(1)}, f32[100,128]{1,0:T(8,128)}, u32[]{:S(2)}) copy-start(f32[100,128]{1,0:T(8,128)} %param.11) | copy-start | bytes 153604
  7.2 110.9 %all-gather.3.cloned.1.call-start = ((), (), s32[]{:S(2)}) async-start(), calls=%async_computation.9 | async-start | bytes 2654208 | tf_op jit(solution)/shard_map/all_gather | solution.py:281
  8.1 20.7 %copy-start.7 = (bf16[32,3072]{1,0:T(8,128)(2,1)S(1)}, bf16[32,3072]{1,0:T(8,128)(2,1)}, u32[]{:S(2)}) copy-start(bf16[32,3072]{1,0:T(8,128)(2,1)} %param.8) | copy-start | bytes 589828
  25.3 22.3 %all-to-all-start.1 = ((bf16[4,128,1024]{2,1,0:T(8,128)(2,1)}), bf16[4,128,1024]{2,1,0:T(8,128)(2,1)S(1)}, u32[]{:S(2)}, u32[]{:S(2)}) async-start(bf16[4,128,1024]{2,1,0:T(8,128)(2,1)} %norm.1), calls=%async_computation.1 | async-start | bytes 2097152 | tf_op jit(solution)/shard_map/all_to_all | solution.py:247
  28.8 48.1 %copy-start.8 = (s32[2,4]{1,0:T(2,128)S(1)}, s32[2,4]{1,0:T(2,128)}, u32[]{:S(2)}) copy-start(s32[2,4]{1,0:T(2,128)} %param.13) | copy-start | bytes 100
  48.5 28.4 %all-to-all-start.2 = ((bf16[32,32,384]{2,1,0:T(8,128)(2,1)}), bf16[32,32,384]{2,1,0:T(8,128)(2,1)S(1)}, u32[]{:S(2)}, u32[]{:S(2)}) async-start(bf16[32,32,384]{2,1,0:T(8,128)(2,1)} %bitcast.5), calls=%async_computation.2 | async-start | bytes 1572864 | tf_op jit(solution)/shard_map/all_to_all | solution.py:247
  56.0 24.8 %collective-permute-start = (bf16[4,128,1024]{2,1,0:T(8,128)(2,1)S(1)}, bf16[4,128,1024]{2,1,0:T(8,128)(2,1)S(1)}, u32[]{:S(2)}, u32[]{:S(2)}) collective-permute-start(bf16[4,128,1024]{2,1,0:T(8,128)(2,1)S(1)} %all-to-all-done.1.mine_ref), channel_id=1, source_target_pairs={{0,2},{2,0},{1,3},{3,1},{4,6},{6,4},{5,7},{7,5},{8,10},{10,8},{9,1... | collective-permute-start | bytes 3145736 | tf_op jit(solution)/shard_map/ppermute | solution.py:267
  77.5 8.7 %all-to-all-start = ((s32[8,2,4]{2,1,0:T(2,128)}), s32[8,2,4]{2,1,0:T(2,128)S(1)}, u32[]{:S(2)}, u32[]{:S(2)}) async-start(s32[8,2,4]{2,1,0:T(2,128)} %broadcast_in_dim.13), calls=%async_computation | async-start | bytes 16384 | tf_op jit(solution)/shard_map/all_to_all | solution.py:247
  80.8 1.0 copy-start.4
  81.8 1.2 copy-start.5
  83.0 28.6 %copy-start.9 = (f32[128]{0:T(128)S(1)}, f32[128]{0:T(128)}, u32[]{:S(2)}) copy-start(f32[128]{0:T(128)} %param.12) | copy-start | bytes 1540
  85.3 0.8 copy-start.2
  86.1 17.8 %all-to-all-start.4 = ((bf16[2,64,1024]{2,1,0:T(8,128)(2,1)}), bf16[2,64,1024]{2,1,0:T(8,128)(2,1)S(1)}, u32[]{:S(2)}, u32[]{:S(2)}) async-start(bf16[2,64,1024]{2,1,0:T(8,128)(2,1)} %bitcast.10), calls=%async_computation.4 | async-start | bytes 524288 | tf_op jit(solution)/shard_map/all_to_all | solution.py:247
  89.6 4.8 %collective-permute-start.1 = (bf16[128,256]{1,0:T(8,128)(2,1)S(1)}, bf16[128,256]{1,0:T(8,128)(2,1)S(1)}, u32[]{:S(2)}, u32[]{:S(2)}) collective-permute-start(bf16[128,256]{1,0:T(8,128)(2,1)S(1)} %get-tuple-element.29), channel_id=1, source_target_pairs={{0,16},{1,17},{2,18},{3,19},{4,20},{5,21},{6,22},{7,23},{8,24},{9,... | collective-permute-start | bytes 196616 | tf_op jit(solution)/shard_map/ppermute | solution.py:305
  93.1 5.9 %collective-permute-start.2 = (bf16[128,256]{1,0:T(8,128)(2,1)S(1)}, bf16[128,256]{1,0:T(8,128)(2,1)S(1)}, u32[]{:S(2)}, u32[]{:S(2)}) collective-permute-start(bf16[128,256]{1,0:T(8,128)(2,1)S(1)} %get-tuple-element.28), channel_id=1, source_target_pairs={{16,0},{17,1},{18,2},{19,3},{20,4},{21,5},{22,6},{23,7},{24,8},{25... | collective-permute-start | bytes 196616 | tf_op jit(solution)/shard_map/ppermute | solution.py:306
  104.0 22.3 %copy-start.3 = (bf16[2,128,1024]{2,1,0:T(8,128)(2,1)S(1)}, bf16[2,128,1024]{2,1,0:T(8,128)(2,1)}, u32[]{:S(2)}) copy-start(bf16[2,128,1024]{2,1,0:T(8,128)(2,1)} %copy-done.2) | copy-start | bytes 1572868
  104.0 14.1 %all-to-all-start.3 = ((bf16[16,64,128]{2,1,0:T(8,128)(2,1)}), bf16[16,64,128]{2,1,0:T(8,128)(2,1)S(1)}, u32[]{:S(2)}, u32[]{:S(2)}) async-start(bf16[16,64,128]{2,1,0:T(8,128)(2,1)} %bitcast.9), calls=%async_computation.3 | async-start | bytes 524288 | tf_op jit(solution)/shard_map/all_to_all | solution.py:247
  118.1 1.7 copy-start.1
  122.5 10.7 %all-to-all-start.7 = ((bf16[16,64,128]{2,1,0:T(8,128)(2,1)}), bf16[16,64,128]{2,1,0:T(8,128)(2,1)S(1)}, u32[]{:S(2)}, u32[]{:S(2)}) async-start(bf16[16,64,128]{2,1,0:T(8,128)(2,1)} %get-tuple-element.16), calls=%async_computation.7 | async-start | bytes 524288 | tf_op jit(solution)/shard_map/all_to_all | solution.py:247
  127.0 9.5 %collective-permute-start.3 = (bf16[128,1024]{1,0:T(8,128)(2,1)}, bf16[128,1024]{1,0:T(8,128)(2,1)S(1)}, u32[]{:S(2)}, u32[]{:S(2)}) collective-permute-start(bf16[128,1024]{1,0:T(8,128)(2,1)} %get-tuple-element.27), channel_id=1, source_target_pairs={{0,16},{1,17},{2,18},{3,19},{4,20},{5,21},{6,22},{7,23},{8,24},{9,... | collective-permute-start | bytes 786440 | tf_op jit(solution)/shard_map/ppermute | solution.py:307
  128.3 15.8 %collective-permute-start.4 = (bf16[128,1024]{1,0:T(8,128)(2,1)S(1)}, bf16[128,1024]{1,0:T(8,128)(2,1)S(1)}, u32[]{:S(2)}, u32[]{:S(2)}) collective-permute-start(bf16[128,1024]{1,0:T(8,128)(2,1)S(1)} %get-tuple-element.26), channel_id=1, source_target_pairs={{16,0},{17,1},{18,2},{19,3},{20,4},{21,5},{22,6},{23,7},{24,8},{25... | collective-permute-start | bytes 786440 | tf_op jit(solution)/shard_map/ppermute | solution.py:308
  133.2 24.5 %all-to-all-start.6 = ((f32[2,100,64]{1,2,0:T(8,128)}), f32[2,100,64]{1,2,0:T(8,128)S(1)}, u32[]{:S(2)}, u32[]{:S(2)}) async-start(f32[2,100,64]{1,2,0:T(8,128)} %bitcast.14), calls=%async_computation.6 | async-start | bytes 131072 | tf_op jit(solution)/shard_map/all_to_all | solution.py:247
  154.0 1.2 copy-start.6
  157.7 19.8 %all-to-all-start.8 = ((bf16[32,32,256]{2,1,0:T(8,128)(2,1)}), bf16[32,32,256]{2,1,0:T(8,128)(2,1)S(1)}, u32[]{:S(2)}, u32[]{:S(2)}) async-start(bf16[32,32,256]{2,1,0:T(8,128)(2,1)} %bitcast.22), calls=%async_computation.8 | async-start | bytes 1048576 | tf_op jit(solution)/shard_map/all_to_all | solution.py:247
Sparse Core Ops, SparseCore 0:
  23.3 31.3 all-gather.2

commit v3 on v2

v3 whole, which is shorter than its diff:
```python
import functools

import jax
import jax.numpy as jnp
from jax import lax
from jax.experimental import pallas as pl
from jax.experimental.pallas import tpu as pltpu
from jax.sharding import Mesh
from jax.sharding import PartitionSpec as P

LATENT_DIM = 1024
HEADS = 16
HEAD = 64
FIELD_NUM = 100
TILE = 64
RADIUS = 2
K_NB = 4
QUAD = 4
CORES = 2
GROUP = QUAD * CORES
COLS = LATENT_DIM // GROUP
RIM = RADIUS * TILE
FIELD_PAD = 128
PAIR = 2
WINDOW = (PAIR + 2 * RADIUS) * TILE
NOWHERE = 100

NORM_EPS = 1e-06
SOFT_WIDTH = 0.0625
MASKED = -1e30

F32 = jnp.float32
BF16 = jnp.bfloat16

VMEM = pl.BlockSpec(memory_space=pltpu.VMEM)
SMEM = pl.BlockSpec(memory_space=pltpu.SMEM)
OVER_ROWS = (((0,), (0,)), ((), ()))
OVER_COLUMNS = (((1,), (1,)), ((), ()))


def call(kernel, name, outs, ins, scratch=(), flops=0, moved=0, exps=0):
    return pl.pallas_call(
        kernel,
        out_shape=[jax.ShapeDtypeStruct(shape, kind) for shape, kind in outs],
        in_specs=[SMEM if space == "s" else VMEM for space in ins],
        out_specs=[VMEM] * len(outs),
        scratch_shapes=[pltpu.VMEM(shape, kind) for shape, kind in scratch],
        compiler_params=pltpu.CompilerParams(vmem_limit_bytes=32 * 2**20),
        cost_estimate=pl.CostEstimate(flops=flops, bytes_accessed=moved, transcendentals=exps),
        name=name,
    )


def norm_kernel(source_ref, out_ref):
    source = source_ref[...].astype(F32)
    inverse = lax.rsqrt(jnp.mean(source * source, axis=-1, keepdims=True) + NORM_EPS)
    out_ref[...] = (source * inverse).astype(BF16)


def owners(where_ref):
    core, quad = where_ref[0], where_ref[1]
    return [(quad ^ step) * CORES + (core ^ flip) for flip in range(CORES) for step in range(QUAD)]


def project_kernel(where_ref, *refs):
    blocks, (w_ref, q_ref, kv_ref, rims_ref, normed_rims_ref) = refs[:GROUP], refs[GROUP:]
    block = blocks[0].shape[0]
    for rows_ref, owner in zip(blocks, owners(where_ref)):
        projected = jnp.dot(rows_ref[...], w_ref[...], preferred_element_type=F32).astype(BF16)
        at = pl.ds(pl.multiple_of(owner * block, block), block)
        q_ref[at, :] = projected[:, :COLS]
        kv_ref[at, :] = projected[:, COLS:]

        @pl.when(owner == 0)
        def _():
            rims_ref[0] = projected[:RIM, COLS:]
            normed_rims_ref[0] = rows_ref[:RIM, :]

        @pl.when(owner == GROUP - 1)
        def _():
            rims_ref[1] = projected[block - RIM :, COLS:]
            normed_rims_ref[1] = rows_ref[block - RIM :, :]


def by_head(rows):
    lane = lax.broadcasted_iota(jnp.int32, rows.shape, 1)
    zero = jnp.zeros_like(rows)
    return jnp.concatenate(
        [jnp.where(lane < HEAD, rows, zero), jnp.where(lane < HEAD, zero, rows)], axis=0
    )


def usable_keys(steps_ref, pair):
    lane = lax.broadcasted_iota(jnp.int32, (1, WINDOW), 1) // TILE - RADIUS
    masks = []
    for query_tile in range(PAIR):
        found = jnp.zeros((1, WINDOW), jnp.int32)
        for slot in range(K_NB):
            step = steps_ref[pair, query_tile : query_tile + 1, slot : slot + 1]
            found = jnp.where(lane - query_tile == step, 1, found)
        masks.append(found)
    row = lax.broadcasted_iota(jnp.int32, (2 * PAIR * TILE, 1), 0) // TILE % PAIR
    return jnp.where(row == 0, masks[0], masks[1]) > 0


def probabilities(queries, keys, usable):
    scores = lax.dot_general(queries, keys, OVER_COLUMNS, preferred_element_type=F32) * (HEAD**-0.5)
    scores = jnp.where(usable, scores, MASKED)
    raised = jnp.exp(scores - jnp.max(scores, axis=-1, keepdims=True))
    return raised * (1.0 / jnp.sum(raised, axis=-1, keepdims=True))


def attend(steps_ref, pair, queries, keys, values):
    probs = probabilities(by_head(queries), keys, usable_keys(steps_ref, pair))
    both = jnp.dot(probs.astype(BF16), values, preferred_element_type=F32)
    lane = lax.broadcasted_iota(jnp.int32, queries.shape, 1)
    half = PAIR * TILE
    return jnp.where(lane < HEAD, both[:half], both[half:]).astype(BF16)


def interior_kernel(steps_ref, q_ref, kv_ref, out_ref):
    step = PAIR * TILE
    pairs = q_ref.shape[0] // step
    for pair in range(1, pairs - 1):
        window = slice((pair - 1) * step, (pair + 2) * step)
        rows = slice(pair * step, (pair + 1) * step)
        out_ref[rows, :] = attend(
            steps_ref, pair, q_ref[rows, :], kv_ref[window, :COLS], kv_ref[window, COLS:]
        )


def edge_kernel(steps_ref, q_ref, kv_ref, low_ref, high_ref, done_ref, out_ref):
    step = PAIR * TILE
    count = q_ref.shape[0]
    pairs = count // step
    out_ref[step : count - step, :] = done_ref[step : count - step, :]
    first = jnp.concatenate([low_ref[...], kv_ref[: 2 * step, :]], axis=0)
    last = jnp.concatenate([kv_ref[count - 2 * step :, :], high_ref[...]], axis=0)
    for pair, window in ((0, first), (pairs - 1, last)):
        rows = slice(pair * step, (pair + 1) * step)
        out_ref[rows, :] = attend(
            steps_ref, pair, q_ref[rows, :], window[:, :COLS], window[:, COLS:]
        )


def backward_kernel(steps_ref, q_ref, low_ref, own_ref, high_ref, g_ref, out_ref, kv, total):
    count = q_ref.shape[0]
    step = PAIR * TILE
    kv[0:RIM, :] = low_ref[...]
    kv[RIM : RIM + count, :] = own_ref[...]
    kv[RIM + count : 2 * RIM + count, :] = high_ref[...]
    total[...] = jnp.zeros_like(total)
    for pair in range(count // step):
        rows = slice(pair * step, (pair + 1) * step)
        window = slice(pair * step, pair * step + WINDOW)
        keys, values = kv[window, :COLS], kv[window, COLS:]
        queries, grads = by_head(q_ref[rows, :]), by_head(g_ref[rows, :])
        probs = probabilities(queries, keys, usable_keys(steps_ref, pair))
        grad_probs = lax.dot_general(grads, values, OVER_COLUMNS, preferred_element_type=F32)
        row_delta = jnp.sum(probs * grad_probs, axis=-1, keepdims=True)
        grad_scores = (probs * (grad_probs - row_delta) * (HEAD**-0.5)).astype(BF16)
        total[window, :COLS] += lax.dot_general(
            grad_scores, queries, OVER_ROWS, preferred_element_type=F32
        )
        total[window, COLS:] += lax.dot_general(
            probs.astype(BF16), grads, OVER_ROWS, preferred_element_type=F32
        )
    both = total[...]
    high = both.astype(BF16)
    out_ref[:, : 2 * COLS] = high
    out_ref[:, 2 * COLS :] = (both - high.astype(F32)).astype(BF16)


def slope(spread):
    return spread * lax.rsqrt(spread * spread + SOFT_WIDTH)


def mix_kernel(where_ref, att_ref, source_ref, *refs):
    pieces = refs[:GROUP]
    truth_ref, factor_ref, pred_ref, grad_ref, w, a = refs[GROUP:]
    halves, block, _ = pieces[0].shape
    members_num, part, _ = source_ref.shape
    for piece, owner in zip(pieces, owners(where_ref)):
        for half in range(halves):
            at = pl.multiple_of((half * GROUP + owner) * block, block)
            w[pl.ds(at, block), :] = piece[half]
    for g in range(GROUP):
        for m in range(members_num):
            a[m * part : (m + 1) * part, g * COLS : (g + 1) * COLS] = att_ref[g * members_num + m]
    mix, readout = w[:, :LATENT_DIM], w[:, LATENT_DIM:]
    rows = members_num * part
    source = source_ref[...].reshape(rows, LATENT_DIM).astype(F32)
    hidden = source + jnp.dot(a[...], mix, preferred_element_type=F32)
    inverse = lax.rsqrt(jnp.mean(hidden * hidden, axis=-1, keepdims=True) + NORM_EPS)
    decoded = (hidden * inverse).astype(BF16)
    prediction = lax.dot_general(
        readout, decoded, (((0,), (1,)), ((), ())), preferred_element_type=F32
    )
    pred_ref[...] = prediction[:FIELD_NUM]
    spread = jnp.zeros_like(prediction)
    for other in range(1, members_num):
        spread = spread + slope(prediction - pltpu.roll(prediction, other * part, 1))
    derivative = factor_ref[...] / FIELD_NUM * (
        slope(prediction - truth_ref[...]) - spread / (members_num - 1)
    )
    grad_decoded = lax.dot_general(
        derivative.astype(BF16), readout, (((0,), (1,)), ((), ())), preferred_element_type=F32
    )
    grad_hidden = inverse * grad_decoded - hidden * inverse**3 * jnp.mean(
        grad_decoded * hidden, axis=-1, keepdims=True
    )
    grads = lax.dot_general(
        grad_hidden.astype(BF16), mix, OVER_COLUMNS, preferred_element_type=F32
    ).astype(BF16)
    for g in range(GROUP):
        for m in range(members_num):
            grad_ref[g * members_num + m] = grads[
                m * part : (m + 1) * part, g * COLS : (g + 1) * COLS
            ]


def product_kernel(where_ref, *refs):
    blocks, (low_ref, high_ref, kv_ref, out_ref) = refs[:GROUP], refs[GROUP:]
    places = [(owner + 1) * RIM for owner in owners(where_ref)]
    places += [0, (GROUP + 1) * RIM]
    blocks = list(blocks) + [low_ref, high_ref]
    total = None
    for at in range(0, len(blocks), 2):
        rows = jnp.concatenate([blocks[at][...], blocks[at + 1][...]], axis=0)
        kv = jnp.concatenate(
            [kv_ref[pl.ds(pl.multiple_of(place, RIM), RIM), :] for place in places[at : at + 2]], axis=0
        )
        both = lax.dot_general(rows, kv, OVER_ROWS, preferred_element_type=F32)
        term = both[:, : 2 * COLS] + both[:, 2 * COLS :]
        total = term if total is None else total + term
    out_ref[...] = total.astype(BF16)


def exchange(chunks, axes):
    return lax.all_to_all(chunks, axes, 0, 0)


def swap(value, axis, step):
    return lax.ppermute(value, axis, [(i, i ^ step) for i in range(lax.axis_size(axis))])


def in_order(mine, axis, at):
    if lax.axis_size(axis) != 2:
        return lax.all_gather(mine, axis, axis=at)
    other = swap(mine, axis, 1)
    first = lax.axis_index(axis) == 0
    return jnp.stack([jnp.where(first, mine, other), jnp.where(first, other, mine)], axis=at)


def group_pieces(mine):
    near = [mine] + [swap(mine, "quad", step) for step in range(1, QUAD)]
    return near, [swap(piece, "core", 1) for piece in near]


def body(members, w_attn, w_mix, readout_matrix, observed_truth, cell_surface_factor, neighbours):
    halves, members_num = lax.axis_size("half"), lax.axis_size("ens")
    everyone = ("half", "quad", "core", "ens")
    shard = w_attn.shape[0]
    node_rows = members.shape[1]
    rows = GROUP * node_rows
    part = node_rows // members_num
    up = [(i, i + 1) for i in range(halves - 1)]
    down = [(target, source) for source, target in up]
    core, quad, ens = (lax.axis_index(axis) for axis in ("core", "quad", "ens"))
    where = jnp.stack([core, quad]).astype(jnp.int32)

    (normed,) = call(
        norm_kernel, "norm", [((node_rows, LATENT_DIM), BF16)], "v", flops=10, moved=2**20
    )(members.reshape(node_rows, LATENT_DIM))
    near, far = group_pieces(normed)
    blocks = near + far

    columns = w_attn.reshape(shard, 3, GROUP, COLS).transpose(2, 0, 1, 3)
    columns = columns.reshape(1, GROUP, 1, shard, 3 * COLS)
    columns = jnp.broadcast_to(columns, (halves, GROUP, members_num, shard, 3 * COLS))
    columns = exchange(columns.reshape(-1, shard, 3 * COLS), everyone)
    columns = columns.reshape(LATENT_DIM, 3 * COLS)

    local_tiles = neighbours.shape[0]
    first_tile = lax.axis_index(("half", "quad", "core")) * local_tiles
    steps = neighbours - first_tile - jnp.arange(local_tiles, dtype=jnp.int32)[:, None]
    steps = jnp.where(neighbours >= 0, steps, NOWHERE)
    steps = jnp.pad(steps, ((0, 8 - local_tiles), (0, 128 - K_NB)))
    steps = lax.all_gather(steps, ("quad", "core"), axis=0)

    packed = jnp.concatenate(
        [w_mix, jnp.pad(readout_matrix, ((0, 0), (0, FIELD_PAD - FIELD_NUM)))], axis=1
    )
    width = packed.shape[1]
    packed = in_order(packed, "half", 0)
    packed = in_order(packed, "ens", 1).reshape(halves, members_num * shard, width)
    packed, near[3] = lax.optimization_barrier((packed, near[3]))
    mix_near, mix_far = group_pieces(packed)

    sources = members.reshape(members_num, part, LATENT_DIM)
    if members_num == 2:
        kept = lax.dynamic_index_in_dim(sources, ens, 0, keepdims=False)
        sent = swap(lax.dynamic_index_in_dim(sources, 1 - ens, 0, keepdims=False), "ens", 1)
        sources = jnp.stack([jnp.where(ens == 0, kept, sent), jnp.where(ens == 0, sent, kept)])
    else:
        sources = exchange(sources, "ens")
    truth = lax.dynamic_slice_in_dim(observed_truth, ens * part, part, 1)
    truth = jnp.tile(jnp.pad(truth, ((0, FIELD_PAD - FIELD_NUM), (0, 0))), (1, members_num))
    factor = lax.dynamic_slice_in_dim(cell_surface_factor, ens * part, part, 0)
    factor = jnp.tile(factor[None], (1, members_num))

    queries, own, rims, normed_rims = call(
        project_kernel,
        "project",
        [
            ((rows, COLS), BF16),
            ((rows, 2 * COLS), BF16),
            ((2, RIM, 2 * COLS), BF16),
            ((2, RIM, LATENT_DIM), BF16),
        ],
        "s" + "v" * (GROUP + 1),
        flops=rows * LATENT_DIM * 6 * COLS,
        moved=4 * 2**20,
    )(where, *blocks, columns)
    low = lax.ppermute(rims[1], "half", up)
    high = lax.ppermute(rims[0], "half", down)

    (outcome,) = call(
        interior_kernel,
        "attention_interior",
        [((rows, COLS), BF16)],
        "vvv",
        flops=rows * COLS * 2048,
        moved=2**21,
        exps=rows * 512,
    )(steps, queries, own)
    (outcome,) = call(
        edge_kernel,
        "attention_edges",
        [((rows, COLS), BF16)],
        "vvvvvv",
        flops=rows * COLS * 512,
        moved=2**20,
        exps=rows * 128,
    )(steps, queries, own, low, high, outcome)
    attended = exchange(outcome.reshape(GROUP * members_num, part, COLS), ("quad", "core", "ens"))
    normed_rims, attended = lax.optimization_barrier((normed_rims, attended))
    normed_low = lax.ppermute(normed_rims[1], "half", up)
    normed_high = lax.ppermute(normed_rims[0], "half", down)

    prediction, grads = call(
        mix_kernel,
        "mix_loss_backward",
        [((FIELD_NUM, node_rows), F32), ((GROUP * members_num, part, COLS), BF16)],
        "s" + "v" * (GROUP + 4),
        [((LATENT_DIM, width), BF16), ((node_rows, LATENT_DIM), BF16)],
        flops=node_rows * LATENT_DIM * 4 * width,
        moved=2**22,
    )(where, attended, sources, *mix_near, *mix_far, truth, factor)
    grads = exchange(grads, ("quad", "core", "ens")).reshape(rows, COLS)

    (kv_grads,) = call(
        backward_kernel,
        "attention_backward",
        [((rows + 2 * RIM, 4 * COLS), BF16)],
        "vvvvvv",
        [((rows + 2 * RIM, 2 * COLS), BF16), ((rows + 2 * RIM, 2 * COLS), F32)],
        flops=rows * COLS * 5120,
        moved=2**22,
        exps=rows * 512,
    )(steps, queries, low, own, high, grads)
    (term,) = call(
        product_kernel,
        "product",
        [((LATENT_DIM, 2 * COLS), BF16)],
        "s" + "v" * (GROUP + 3),
        flops=(rows + 2 * RIM) * LATENT_DIM * 8 * COLS,
        moved=2**22,
    )(where, *blocks, normed_low, normed_high, kv_grads)
    term, prediction = lax.optimization_barrier((term, prediction))
    term = exchange(term.reshape(-1, shard, 2 * COLS), everyone)
    term = term.reshape(halves, GROUP, members_num, shard, 2, COLS).astype(F32)
    grad_kv = jnp.sum(term, axis=(0, 2)).transpose(1, 2, 0, 3).reshape(shard, 2 * LATENT_DIM)

    if members_num == 2:
        got = jnp.roll(swap(prediction, "ens", 1), part, axis=1)
        lane = lax.broadcasted_iota(jnp.int32, prediction.shape, 1)
        prediction = jnp.where(lane // part == ens, prediction, got)
    else:
        prediction = prediction.reshape(FIELD_NUM, members_num, part).transpose(1, 0, 2)
        prediction = exchange(prediction, "ens").transpose(1, 0, 2)
    return (prediction.reshape(1, FIELD_NUM, node_rows), grad_kv)


def solution(mesh):
    space, ens = mesh.shape["space"], mesh.shape["ens"]
    split = Mesh(
        mesh.devices.reshape(space // GROUP, QUAD, CORES, ens), ("half", "quad", "core", "ens")
    )
    nodes = ("half", "quad", "core")
    shards = nodes + ("ens",)
    in_specs = (
        P("ens", nodes, None),
        P(shards, None),
        P(shards, None),
        P(shards, None),
        P(None, nodes),
        P(nodes),
        P(nodes, None),
    )
    out_specs = (P("ens", None, nodes), P(shards, None))
    return jax.shard_map(body, mesh=split, in_specs=in_specs, out_specs=out_specs, check_vma=False)
```

time: 188 us -> 141 us (0.75)
  waiting for transfers between devices: 75.5 us -> 34.1 us
  between operations: 14.3 us -> 1.15 us
  local copies, waits for them, and re-layouts: 11.8 us -> 19.5 us
  starting transfers between devices: 43.6 us -> 48.9 us
  Pallas kernels: 24.5 us -> 19.5 us
    all_to_all x8 -> x4, waiting for transfers between devices: 63.3 us -> 13.7 us  [exchange(): return lax.all_to_all(chunks, axes, 0, 0)]
    ppermute x1 -> x18, starting transfers between devices: 0.32 us -> 20.9 us  [swap(): lax.ppermute(value, axis, [(i, i ^ step) for i in range(lax.axis_size(axi...]
    all_to_all x8 -> x4, starting transfers between devices: 36 us -> 17.3 us  [exchange(): return lax.all_to_all(chunks, axes, 0, 0)]
    all_to_all x1 -> x0, blocking collectives: 15.1 us -> none  [exchange(): return lax.all_to_all(chunks, axes, 0, 0)]
    all_gather x0 -> x1, blocking collectives: none -> 14.2 us  [body(): steps = lax.all_gather(steps, ('quad', 'core'), axis=0)]
    ppermute x1 -> x18, waiting for transfers between devices: 0.01 us -> 10.8 us  [swap(): lax.ppermute(value, axis, [(i, i ^ step) for i in range(lax.axis_size(axi...]
    unnamed x24 -> x68, local copies, waits for them, and re-layouts: 7.49 us -> 15.6 us
    pallas_call x1, Pallas kernels: 9.87 us -> 5.18 us  [body(): call(backward_kernel, 'attention_backward', [((rows + 2 * RIM, 4 * COLS),...]
  transfers between devices with their start and end apart: 14 -> 26, of which waited for: 7 -> 7; matrix products, arithmetic and copies ran while one was open for 2% -> 4% of each run, Pallas kernels for 12% -> 9%
where the time goes in v3:
time: 141 us; the launch traced here: 140 us
  starting transfers between devices  48.9 us (35%)
  waiting for transfers between devices  34.1 us (24%)
  local copies, waits for them, and re-layouts  19.5 us (14%)
  Pallas kernels  19.5 us (14%)
  blocking collectives  14.2 us (10%)
  other arithmetic  2.88 us (2%)
    ppermute x18, starting transfers between devices, swap(): lax.ppermute(value, axis, [(i, i ^ step) for i in range(lax.axis_size(axi...  20.9 us
    all_to_all x4, starting transfers between devices, exchange(): return lax.all_to_all(chunks, axes, 0, 0)  17.3 us
    unnamed x68, local copies, waits for them, and re-layouts  15.6 us
    all_gather x1, blocking collectives, body(): steps = lax.all_gather(steps, ('quad', 'core'), axis=0)  14.2 us
    all_to_all x4, waiting for transfers between devices, exchange(): return lax.all_to_all(chunks, axes, 0, 0)  13.7 us
    ppermute x18, waiting for transfers between devices, swap(): lax.ppermute(value, axis, [(i, i ^ step) for i in range(lax.axis_size(axi...  10.8 us
    ppermute x1, waiting for transfers between devices, body(): normed_high = lax.ppermute(normed_rims[0], 'half', down)  9.57 us
    ppermute x1, starting transfers between devices, body(): normed_low = lax.ppermute(normed_rims[1], 'half', up)  5.9 us
  transfers between devices with their start and end apart: 26, of which 7 were waited for; matrix products, arithmetic and copies ran while one was open for 4% of the time, Pallas kernels for 9%

profile of v3, /device:TPU:1, one launch (start us, length us, event | category | flops | bytes accessed | tf_op | source)
XLA Modules:
  0.0 140.3 jit_solution(1743969053903958947)
XLA Ops:
  0.6 0.9 fusion.3
  1.5 3.1 %collective-permute-start.12 = (bf16[32,1152]{1,0:T(8,128)(2,1)S(1)}, bf16[32,1152]{1,0:T(8,128)(2,1)S(1)}, u32[]{:S(2)}, u32[]{:S(2)}) collective-permute-start(bf16[32,1152]{1,0:T(8,128)(2,1)S(1)} %fusion.3), channel_id=1, source_target_pairs={{0,16},{16,0},{1,17},{17,1},{2,18},{18,2},{3,19},{19,3},{4,20},{20... | collective-permute-start | bytes 221192 | tf_op jit(solution)/shard_map/ppermute | solution.py:244
  4.7 0.9 copy-done.1
  5.8 1.3 collective-permute-start
  7.1 1.3 collective-permute-start.1
  8.5 1.0 copy.28
  9.8 1.0 broadcast_in_dim.13
  10.8 5.4 %all-to-all-start = ((bf16[32,32,384]{2,1,0:T(8,128)(2,1)}), bf16[32,32,384]{2,1,0:T(8,128)(2,1)S(1)}, u32[]{:S(2)}, u32[]{:S(2)}) async-start(bf16[32,32,384]{2,1,0:T(8,128)(2,1)} %bitcast.4), calls=%async_computation | async-start | bytes 1572864 | tf_op jit(solution)/shard_map/all_to_all | solution.py:240
  16.2 1.5 %collective-permute-start.13 = (bf16[2,32,1152]{2,1,0:T(8,128)(2,1)S(1)}, bf16[2,32,1152]{2,1,0:T(8,128)(2,1)S(1)}, u32[]{:S(2)}, u32[]{:S(2)}) collective-permute-start(bf16[2,32,1152]{2,1,0:T(8,128)(2,1)S(1)} %pad_maximum_fusion.2), channel_id=1, source_target_pairs={{0,1},{1,0},{2,3},{3,2},{4,5},{5,4},{6,7},{7,6},{8,9},{9,8},{10,11... | collective-permute-start | bytes 442376 | tf_op jit(solution)/shard_map/ppermute | solution.py:244
  18.9 0.8 collective-permute-done.2.refs_3_
  19.7 5.4 %collective-permute-start.6 = (bf16[128,1024]{1,0:T(8,128)(2,1)S(1)}, bf16[128,1024]{1,0:T(8,128)(2,1)S(1)}, u32[]{:S(2)}, u32[]{:S(2)}) collective-permute-start(bf16[128,1024]{1,0:T(8,128)(2,1)S(1)} %collective-permute-done.2.refs_3_), channel_id=1, source_target_pairs={{0,2},{2,0},{1,3},{3,1},{4,6},{6,4},{5,7},{7,5},{8,10},{10,8},{9,1... | collective-permute-start | bytes 786440 | tf_op jit(solution)/shard_map/ppermute | solution.py:244
  25.1 1.1 collective-permute-done.13
  26.4 0.9 collective-permute-start.14
  28.0 1.0 collective-permute-start.15
  29.7 1.2 collective-permute-start.16
  32.3 4.8 %all-to-all-done = bf16[32,32,384]{2,1,0:T(8,128)(2,1)S(1)} async-done(((bf16[32,32,384]{2,1,0:T(8,128)(2,1)}), bf16[32,32,384]{2,1,0:T(8,128)(2,1)S(1)}, u32[]{:S(2)}, u32[]{:S(2)}) %all-to-all-start) | async-done | bytes 786464 | tf_op jit(solution)/shard_map/all_to_all | solution.py:240
  37.1 0.9 copy-done.4
  38.0 0.9 copy-done.8
  39.0 0.9 copy-done.11
  39.9 0.9 copy-done.14
  40.9 0.9 copy-done.17
  41.8 0.9 copy-done.20
  42.8 0.9 copy-done.23
  43.7 0.9 copy-done.26
  44.7 3.0 %project.1 = (bf16[1024,128]{1,0:T(8,128)(2,1)S(1)}, bf16[1024,256]{1,0:T(8,128)(2,1)S(1)}, bf16[2,128,256]{2,1,0:T(8,128)(2,1)S(1)}, bf16[2,128,1024]{2,1,0:T(8,128)(2,1)S(1)}) custom-call(s32[2]{0:T(128)S(1)} %pad_add_fusion.where_ref, bf16[128,1024]{1,0:T(8,128)(2,1)S(1)} %copy-done.4, bf16[128,1024]{1,0:T(8,128)(2,1)S(1)} %copy-done.8, ...), custom_call_target="tpu_custom_call" | custom-call | flops 805306368 | bytes 4194304 | tf_op jit(solution)/shard_map/project/pallas_call | solution.py:312
  47.7 2.0 %collective-permute-start.7 = (bf16[128,256]{1,0:T(8,128)(2,1)S(1)}, bf16[128,256]{1,0:T(8,128)(2,1)S(1)}, u32[]{:S(2)}, u32[]{:S(2)}) collective-permute-start(bf16[128,256]{1,0:T(8,128)(2,1)S(1)} %get-tuple-element.41), channel_id=1, source_target_pairs={{0,16},{1,17},{2,18},{3,19},{4,20},{5,21},{6,22},{7,23},{8,24},{9,... | collective-permute-start | bytes 196616 | tf_op jit(solution)/shard_map/ppermute | solution.py:325
  49.7 1.3 collective-permute-start.8
  51.0 14.2 %all-gather = s32[64,128]{1,0:T(8,128)S(1)} all-gather(s32[8,128]{1,0:T(8,128)S(1)} %pad.12), channel_id=2, replica_groups=mesh['half'=2,'quad'=4,'core'=2,'ens'=2] {'quad','core'}, dimensions={0}, use_global_device_ids=true | all-gather | bytes 36864 | tf_op jit(solution)/shard_map/all_gather | solution.py:289
  65.2 2.6 %attention_interior.1.done_ref = bf16[1024,128]{1,0:T(8,128)(2,1)S(1)} custom-call(s32[8,8,128]{2,1,0:T(8,128)S(1)} %bitcast.65, bf16[1024,128]{1,0:T(8,128)(2,1)S(1)} %get-tuple-element.14.q_ref, bf16[1024,256]{1,0:T(8,128)(2,1)S(1)} %get-tuple-element.15.kv_ref.own_ref), custom_call_target="tpu_custom_call" | custom-call | flops 268435456 | bytes 2097152 | tf_op jit(solution)/shard_map/attention_interior/pallas_call | solution.py:328
  67.9 1.7 %attention_edges.1 = bf16[1024,128]{1,0:T(8,128)(2,1)} custom-call(s32[8,8,128]{2,1,0:T(8,128)S(1)} %bitcast.66, bf16[1024,128]{1,0:T(8,128)(2,1)S(1)} %get-tuple-element.14.q_ref, bf16[1024,256]{1,0:T(8,128)(2,1)S(1)} %get-tuple-element.15.kv_ref.own_ref, bf16[128,256]{1,0:T(8,128)(2,1)S(1)} %collective-permute-done.7.low_ref, ...), custom_call_target="tpu_custom_call" | custom-call | flops 67108864 | bytes 1048576 | tf_op jit(solution)/shard_map/attention_edges/pallas_call | solution.py:337
  69.5 3.5 %all-to-all-start.1 = ((bf16[16,64,128]{2,1,0:T(8,128)(2,1)}), bf16[16,64,128]{2,1,0:T(8,128)(2,1)S(1)}, u32[]{:S(2)}, u32[]{:S(2)}) async-start(bf16[16,64,128]{2,1,0:T(8,128)(2,1)} %bitcast.9), calls=%async_computation.1 | async-start | bytes 524288 | tf_op jit(solution)/shard_map/all_to_all | solution.py:240
  73.7 1.4 collective-permute-start.11
  76.8 4.3 %collective-permute-done.11 = bf16[64,1024]{1,0:T(8,128)(2,1)} collective-permute-done((bf16[64,1024]{1,0:T(8,128)(2,1)}, bf16[64,1024]{1,0:T(8,128)(2,1)}, u32[]{:S(2)}, u32[]{:S(2)}) %collective-permute-start.11) | collective-permute-done | bytes 131104 | tf_op jit(solution)/shard_map/ppermute | solution.py:244
  81.1 0.9 fusion.1
  82.2 3.4 %mix_loss_backward.1 = (f32[100,128]{1,0:T(8,128)S(1)}, bf16[16,64,128]{2,1,0:T(8,128)(2,1)S(1)}) custom-call(s32[2]{0:T(128)S(1)} %pad_add_fusion.where_ref, bf16[16,64,128]{2,1,0:T(8,128)(2,1)S(1)} %all-to-all-done.1.att_ref, bf16[2,64,1024]{2,1,0:T(8,128)(2,1)S(1)} %pad_maximum_fusion.1.source_ref, bf16[2,64,1152]{2,1,0:T(8,128)(2,1)S(1)} %bitcast.59, ...), custom_call_target="tpu_custom_call" | custom-call | flops 603979776 | bytes 4194304 | tf_op jit(solution)/shard_map/mix_loss_backward/pallas_call | solution.py:351
  86.3 4.6 %all-to-all-start.2 = ((bf16[16,64,128]{2,1,0:T(8,128)(2,1)}), bf16[16,64,128]{2,1,0:T(8,128)(2,1)S(1)}, u32[]{:S(2)}, u32[]{:S(2)}) async-start(bf16[16,64,128]{2,1,0:T(8,128)(2,1)} %copy-done.6), calls=%async_computation.2 | async-start | bytes 524288 | tf_op jit(solution)/shard_map/all_to_all | solution.py:240
  90.9 0.8 slice_bitcast_fusion
  91.8 5.9 %collective-permute-start.9 = (bf16[128,1024]{1,0:T(8,128)(2,1)}, bf16[128,1024]{1,0:T(8,128)(2,1)}, u32[]{:S(2)}, u32[]{:S(2)}) collective-permute-start(bf16[128,1024]{1,0:T(8,128)(2,1)} %get-tuple-element.33), channel_id=1, source_target_pairs={{0,16},{1,17},{2,18},{3,19},{4,20},{5,21},{6,22},{7,23},{8,24},{9,... | collective-permute-start | bytes 786440 | tf_op jit(solution)/shard_map/ppermute | solution.py:348
  97.7 1.5 %collective-permute-start.10 = (bf16[128,1024]{1,0:T(8,128)(2,1)}, bf16[128,1024]{1,0:T(8,128)(2,1)}, u32[]{:S(2)}, u32[]{:S(2)}) collective-permute-start(bf16[128,1024]{1,0:T(8,128)(2,1)} %get-tuple-element.32), channel_id=1, source_target_pairs={{16,0},{17,1},{18,2},{19,3},{20,4},{21,5},{22,6},{23,7},{24,8},{25... | collective-permute-start | bytes 786440 | tf_op jit(solution)/shard_map/ppermute | solution.py:349
  99.1 5.2 %attention_backward.1.refs_10_ = bf16[1280,512]{1,0:T(8,128)(2,1)S(1)} custom-call(s32[8,8,128]{2,1,0:T(8,128)S(1)} %bitcast.67, bf16[1024,128]{1,0:T(8,128)(2,1)S(1)} %get-tuple-element.14.q_ref, bf16[128,256]{1,0:T(8,128)(2,1)S(1)} %collective-permute-done.7.low_ref, bf16[1024,256]{1,0:T(8,128)(2,1)S(1)} %get-tuple-element.15.kv_ref.own_ref, ...), custom_call_target="tpu_custom_call" | custom-call | flops 671088640 | bytes 4194304 | tf_op jit(solution)/shard_map/attention_backward/pallas_call | solution.py:362
  104.3 9.6 %collective-permute-done.10.refs_9_ = bf16[128,1024]{1,0:T(8,128)(2,1)} collective-permute-done((bf16[128,1024]{1,0:T(8,128)(2,1)}, bf16[128,1024]{1,0:T(8,128)(2,1)}, u32[]{:S(2)}, u32[]{:S(2)}) %collective-permute-start.10) | collective-permute-done | bytes 262176 | tf_op jit(solution)/shard_map/ppermute | solution.py:349
  114.0 0.9 copy-done.27
  114.9 3.5 %product.1 = bf16[1024,256]{1,0:T(8,128)(2,1)} custom-call(s32[2]{0:T(128)S(1)} %pad_add_fusion.where_ref, bf16[128,1024]{1,0:T(8,128)(2,1)S(1)} %copy-done.5, bf16[128,1024]{1,0:T(8,128)(2,1)S(1)} %copy-done.9, bf16[128,1024]{1,0:T(8,128)(2,1)S(1)} %copy-done.12, bf16[128,1024]{1,0:T(8,128)(2,1)S(1)} %copy-done.15, bf16[128,1024]{1,0:T(8,128)(2,1)S(1)} %copy-done.18, ...), custom_call_target="tpu_custom_call" | custom-call | flops 1342177280 | bytes 4194304 | tf_op jit(solution)/shard_map/product/pallas_call | solution.py:372
  118.4 3.8 %all-to-all-start.3 = ((bf16[32,32,256]{2,1,0:T(8,128)(2,1)}), bf16[32,32,256]{2,1,0:T(8,128)(2,1)S(1)}, u32[]{:S(2)}, u32[]{:S(2)}) async-start(bf16[32,32,256]{2,1,0:T(8,128)(2,1)} %bitcast.25), calls=%async_computation.3 | async-start | bytes 1048576 | tf_op jit(solution)/shard_map/all_to_all | solution.py:240
  122.2 1.5 %collective-permute-start.21 = (f32[100,128]{1,0:T(8,128)S(1)}, f32[100,128]{1,0:T(8,128)S(1)}, u32[]{:S(2)}, u32[]{:S(2)}) collective-permute-start(f32[100,128]{1,0:T(8,128)S(1)} %get-tuple-element.22), channel_id=1, source_target_pairs={{0,1},{1,0},{2,3},{3,2},{4,5},{5,4},{6,7},{7,6},{8,9},{9,8},{10,11... | collective-permute-start | bytes 153608 | tf_op jit(solution)/shard_map/ppermute | solution.py:244
  123.7 4.5 %collective-permute-done.21 = f32[100,128]{1,0:T(8,128)S(1)} collective-permute-done((f32[100,128]{1,0:T(8,128)S(1)}, f32[100,128]{1,0:T(8,128)S(1)}, u32[]{:S(2)}, u32[]{:S(2)}) %collective-permute-start.21) | collective-permute-done | bytes 51232 | tf_op jit(solution)/shard_map/ppermute | solution.py:244
  129.1 9.0 %all-to-all-done.3 = bf16[32,32,256]{2,1,0:T(8,128)(2,1)S(1)} async-done(((bf16[32,32,256]{2,1,0:T(8,128)(2,1)}), bf16[32,32,256]{2,1,0:T(8,128)(2,1)S(1)}, u32[]{:S(2)}, u32[]{:S(2)}) %all-to-all-start.3) | async-done | bytes 524320 | tf_op jit(solution)/shard_map/all_to_all | solution.py:240
  139.5 0.8 copy.32
  (111 shorter events, 10.2 us)
Async XLA Ops:
  0.6 74.5 %copy-start = (f32[100,128]{1,0:T(8,128)S(1)}, f32[100,128]{1,0:T(8,128)}, u32[]{:S(2)}) copy-start(f32[100,128]{1,0:T(8,128)} %param.11) | copy-start | bytes 153604
  1.5 14.6 %collective-permute-start.12 = (bf16[32,1152]{1,0:T(8,128)(2,1)S(1)}, bf16[32,1152]{1,0:T(8,128)(2,1)S(1)}, u32[]{:S(2)}, u32[]{:S(2)}) collective-permute-start(bf16[32,1152]{1,0:T(8,128)(2,1)S(1)} %fusion.3), channel_id=1, source_target_pairs={{0,16},{16,0},{1,17},{17,1},{2,18},{18,2},{3,19},{19,3},{4,20},{20... | collective-permute-start | bytes 221192 | tf_op jit(solution)/shard_map/ppermute | solution.py:244
  4.7 0.9 copy-start.1
  5.8 11.9 %copy-start.3 = (bf16[128,1024]{1,0:T(8,128)(2,1)}, bf16[128,1024]{1,0:T(8,128)(2,1)S(1)}, u32[]{:S(2)}) copy-start(bf16[128,1024]{1,0:T(8,128)(2,1)S(1)} %norm.1.refs_0_) | copy-start | bytes 786436
  5.8 12.6 %collective-permute-start = (bf16[128,1024]{1,0:T(8,128)(2,1)S(1)}, bf16[128,1024]{1,0:T(8,128)(2,1)S(1)}, u32[]{:S(2)}, u32[]{:S(2)}) collective-permute-start(bf16[128,1024]{1,0:T(8,128)(2,1)S(1)} %norm.1.refs_0_), channel_id=1, source_target_pairs={{0,4},{4,0},{8,12},{12,8},{1,5},{5,1},{9,13},{13,9},{2,6},{6,2},{1... | collective-permute-start | bytes 786440 | tf_op jit(solution)/shard_map/ppermute | solution.py:244
  7.1 11.4 %collective-permute-start.1 = (bf16[128,1024]{1,0:T(8,128)(2,1)S(1)}, bf16[128,1024]{1,0:T(8,128)(2,1)S(1)}, u32[]{:S(2)}, u32[]{:S(2)}) collective-permute-start(bf16[128,1024]{1,0:T(8,128)(2,1)S(1)} %norm.1.refs_0_), channel_id=1, source_target_pairs={{0,8},{4,12},{8,0},{12,4},{1,9},{5,13},{9,1},{13,5},{2,10},{6,14},... | collective-permute-start | bytes 786440 | tf_op jit(solution)/shard_map/ppermute | solution.py:244
  8.4 11.3 %collective-permute-start.2 = (bf16[128,1024]{1,0:T(8,128)(2,1)S(1)}, bf16[128,1024]{1,0:T(8,128)(2,1)S(1)}, u32[]{:S(2)}, u32[]{:S(2)}) collective-permute-start(bf16[128,1024]{1,0:T(8,128)(2,1)S(1)} %norm.1.refs_0_), channel_id=1, source_target_pairs={{0,12},{4,8},{8,4},{12,0},{1,13},{5,9},{9,5},{13,1},{2,14},{6,10},... | collective-permute-start | bytes 786440 | tf_op jit(solution)/shard_map/ppermute | solution.py:244
  9.7 6.4 %copy-start.28 = (bf16[32,1024]{1,0:T(8,128)(2,1)S(1)}, bf16[32,1024]{1,0:T(8,128)(2,1)}, u32[]{:S(2)}) copy-start(bf16[32,1024]{1,0:T(8,128)(2,1)} %param.9) | copy-start | bytes 196612
  9.7 6.4 %copy-start.29 = (bf16[32,100]{1,0:T(8,128)(2,1)S(1)}, bf16[32,100]{1,0:T(8,128)(2,1)}, u32[]{:S(2)}) copy-start(bf16[32,100]{1,0:T(8,128)(2,1)} %param.10) | copy-start | bytes 19204
  10.8 26.3 %all-to-all-start = ((bf16[32,32,384]{2,1,0:T(8,128)(2,1)}), bf16[32,32,384]{2,1,0:T(8,128)(2,1)S(1)}, u32[]{:S(2)}, u32[]{:S(2)}) async-start(bf16[32,32,384]{2,1,0:T(8,128)(2,1)} %bitcast.4), calls=%async_computation | async-start | bytes 1572864 | tf_op jit(solution)/shard_map/all_to_all | solution.py:240
  16.2 10.0 %collective-permute-start.13 = (bf16[2,32,1152]{2,1,0:T(8,128)(2,1)S(1)}, bf16[2,32,1152]{2,1,0:T(8,128)(2,1)S(1)}, u32[]{:S(2)}, u32[]{:S(2)}) collective-permute-start(bf16[2,32,1152]{2,1,0:T(8,128)(2,1)S(1)} %pad_maximum_fusion.2), channel_id=1, source_target_pairs={{0,1},{1,0},{2,3},{3,2},{4,5},{5,4},{6,7},{7,6},{8,9},{9,8},{10,11... | collective-permute-start | bytes 442376 | tf_op jit(solution)/shard_map/ppermute | solution.py:244
  17.7 9.5 %collective-permute-start.3 = (bf16[128,1024]{1,0:T(8,128)(2,1)S(1)}, bf16[128,1024]{1,0:T(8,128)(2,1)S(1)}, u32[]{:S(2)}, u32[]{:S(2)}) collective-permute-start(bf16[128,1024]{1,0:T(8,128)(2,1)S(1)} %norm.1.refs_0_), channel_id=1, source_target_pairs={{0,2},{2,0},{1,3},{3,1},{4,6},{6,4},{5,7},{7,5},{8,10},{10,8},{9,1... | collective-permute-start | bytes 786440 | tf_op jit(solution)/shard_map/ppermute | solution.py:244
  18.4 18.6 %copy-start.7 = (bf16[128,1024]{1,0:T(8,128)(2,1)}, bf16[128,1024]{1,0:T(8,128)(2,1)S(1)}, u32[]{:S(2)}) copy-start(bf16[128,1024]{1,0:T(8,128)(2,1)S(1)} %collective-permute-done.refs_1_) | copy-start | bytes 786436
  18.4 10.6 %collective-permute-start.4 = (bf16[128,1024]{1,0:T(8,128)(2,1)S(1)}, bf16[128,1024]{1,0:T(8,128)(2,1)S(1)}, u32[]{:S(2)}, u32[]{:S(2)}) collective-permute-start(bf16[128,1024]{1,0:T(8,128)(2,1)S(1)} %collective-permute-done.refs_1_), channel_id=1, source_target_pairs={{0,2},{2,0},{1,3},{3,1},{4,6},{6,4},{5,7},{7,5},{8,10},{10,8},{9,1... | collective-permute-start | bytes 786440 | tf_op jit(solution)/shard_map/ppermute | solution.py:244
  18.4 18.6 %copy-start.10 = (bf16[128,1024]{1,0:T(8,128)(2,1)}, bf16[128,1024]{1,0:T(8,128)(2,1)S(1)}, u32[]{:S(2)}) copy-start(bf16[128,1024]{1,0:T(8,128)(2,1)S(1)} %collective-permute-done.1.refs_2_) | copy-start | bytes 786436
  18.4 12.4 %collective-permute-start.5 = (bf16[128,1024]{1,0:T(8,128)(2,1)S(1)}, bf16[128,1024]{1,0:T(8,128)(2,1)S(1)}, u32[]{:S(2)}, u32[]{:S(2)}) collective-permute-start(bf16[128,1024]{1,0:T(8,128)(2,1)S(1)} %collective-permute-done.1.refs_2_), channel_id=1, source_target_pairs={{0,2},{2,0},{1,3},{3,1},{4,6},{6,4},{5,7},{7,5},{8,10},{10,8},{9,1... | collective-permute-start | bytes 786440 | tf_op jit(solution)/shard_map/ppermute | solution.py:244
  19.7 17.3 %copy-start.13 = (bf16[128,1024]{1,0:T(8,128)(2,1)}, bf16[128,1024]{1,0:T(8,128)(2,1)S(1)}, u32[]{:S(2)}) copy-start(bf16[128,1024]{1,0:T(8,128)(2,1)S(1)} %collective-permute-done.2.refs_3_) | copy-start | bytes 786436
  19.7 11.8 %collective-permute-start.6 = (bf16[128,1024]{1,0:T(8,128)(2,1)S(1)}, bf16[128,1024]{1,0:T(8,128)(2,1)S(1)}, u32[]{:S(2)}, u32[]{:S(2)}) collective-permute-start(bf16[128,1024]{1,0:T(8,128)(2,1)S(1)} %collective-permute-done.2.refs_3_), channel_id=1, source_target_pairs={{0,2},{2,0},{1,3},{3,1},{4,6},{6,4},{5,7},{7,5},{8,10},{10,8},{9,1... | collective-permute-start | bytes 786440 | tf_op jit(solution)/shard_map/ppermute | solution.py:244
  26.4 49.9 %collective-permute-start.14 = (bf16[2,64,1152]{2,1,0:T(8,128)(2,1)S(1)}, bf16[2,64,1152]{2,1,0:T(8,128)(2,1)S(1)}, u32[]{:S(2)}, u32[]{:S(2)}) collective-permute-start(bf16[2,64,1152]{2,1,0:T(8,128)(2,1)S(1)} %bitcast.55), channel_id=1, source_target_pairs={{0,4},{4,0},{8,12},{12,8},{1,5},{5,1},{9,13},{13,9},{2,6},{6,2},{1... | collective-permute-start | bytes 884744 | tf_op jit(solution)/shard_map/ppermute | solution.py:244
  28.0 48.3 %collective-permute-start.15 = (bf16[2,64,1152]{2,1,0:T(8,128)(2,1)S(1)}, bf16[2,64,1152]{2,1,0:T(8,128)(2,1)S(1)}, u32[]{:S(2)}, u32[]{:S(2)}) collective-permute-start(bf16[2,64,1152]{2,1,0:T(8,128)(2,1)S(1)} %bitcast.56), channel_id=1, source_target_pairs={{0,8},{4,12},{8,0},{12,4},{1,9},{5,13},{9,1},{13,5},{2,10},{6,14},... | collective-permute-start | bytes 884744 | tf_op jit(solution)/shard_map/ppermute | solution.py:244
  29.7 47.1 %collective-permute-start.16 = (bf16[2,64,1152]{2,1,0:T(8,128)(2,1)S(1)}, bf16[2,64,1152]{2,1,0:T(8,128)(2,1)S(1)}, u32[]{:S(2)}, u32[]{:S(2)}) collective-permute-start(bf16[2,64,1152]{2,1,0:T(8,128)(2,1)S(1)} %bitcast.57), channel_id=1, source_target_pairs={{0,12},{4,8},{8,4},{12,0},{1,13},{5,9},{9,5},{13,1},{2,14},{6,10},... | collective-permute-start | bytes 884744 | tf_op jit(solution)/shard_map/ppermute | solution.py:244
  37.0 1.0 copy-start.4
  38.0 0.9 copy-start.8
  39.0 0.9 copy-start.11
  44.7 6.4 %copy-start.30 = (s32[2,4]{1,0:T(2,128)S(1)}, s32[2,4]{1,0:T(2,128)}, u32[]{:S(2)}) copy-start(s32[2,4]{1,0:T(2,128)} %param.13) | copy-start | bytes 100
  47.7 20.2 %collective-permute-start.7 = (bf16[128,256]{1,0:T(8,128)(2,1)S(1)}, bf16[128,256]{1,0:T(8,128)(2,1)S(1)}, u32[]{:S(2)}, u32[]{:S(2)}) collective-permute-start(bf16[128,256]{1,0:T(8,128)(2,1)S(1)} %get-tuple-element.41), channel_id=1, source_target_pairs={{0,16},{1,17},{2,18},{3,19},{4,20},{5,21},{6,22},{7,23},{8,24},{9,... | collective-permute-start | bytes 196616 | tf_op jit(solution)/shard_map/ppermute | solution.py:325
  49.7 18.2 %collective-permute-start.8 = (bf16[128,256]{1,0:T(8,128)(2,1)S(1)}, bf16[128,256]{1,0:T(8,128)(2,1)S(1)}, u32[]{:S(2)}, u32[]{:S(2)}) collective-permute-start(bf16[128,256]{1,0:T(8,128)(2,1)S(1)} %get-tuple-element.40), channel_id=1, source_target_pairs={{16,0},{17,1},{18,2},{19,3},{20,4},{21,5},{22,6},{23,7},{24,8},{25... | collective-permute-start | bytes 196616 | tf_op jit(solution)/shard_map/ppermute | solution.py:326
  65.2 7.8 %copy-start.2 = (bf16[1,128,1024]{2,1,0:T(8,128)(2,1)S(1)}, bf16[1,128,1024]{2,1,0:T(8,128)(2,1)}, u32[]{:S(2)}) copy-start(bf16[1,128,1024]{2,1,0:T(8,128)(2,1)} %param.7) | copy-start | bytes 786436
  67.8 7.6 %copy-start.31 = (f32[128]{0:T(128)S(1)}, f32[128]{0:T(128)}, u32[]{:S(2)}) copy-start(f32[128]{0:T(128)} %param.12) | copy-start | bytes 1540
  69.5 12.6 %all-to-all-start.1 = ((bf16[16,64,128]{2,1,0:T(8,128)(2,1)}), bf16[16,64,128]{2,1,0:T(8,128)(2,1)S(1)}, u32[]{:S(2)}, u32[]{:S(2)}) async-start(bf16[16,64,128]{2,1,0:T(8,128)(2,1)} %bitcast.9), calls=%async_computation.1 | async-start | bytes 524288 | tf_op jit(solution)/shard_map/all_to_all | solution.py:240
  73.7 7.4 %collective-permute-start.11 = (bf16[64,1024]{1,0:T(8,128)(2,1)}, bf16[64,1024]{1,0:T(8,128)(2,1)}, u32[]{:S(2)}, u32[]{:S(2)}) collective-permute-start(bf16[64,1024]{1,0:T(8,128)(2,1)} %dynamic-slice_bitcast_fusion), channel_id=1, source_target_pairs={{0,1},{1,0},{2,3},{3,2},{4,5},{5,4},{6,7},{7,6},{8,9},{9,8},{10,11... | collective-permute-start | bytes 393224 | tf_op jit(solution)/shard_map/ppermute | solution.py:244
  75.6 6.5 %collective-permute-start.17 = (bf16[2,64,1152]{2,1,0:T(8,128)(2,1)S(1)}, bf16[2,64,1152]{2,1,0:T(8,128)(2,1)}, u32[]{:S(2)}, u32[]{:S(2)}) collective-permute-start(bf16[2,64,1152]{2,1,0:T(8,128)(2,1)S(1)} %bitcast.58), channel_id=1, source_target_pairs={{0,2},{2,0},{1,3},{3,1},{4,6},{6,4},{5,7},{7,5},{8,10},{10,8},{9,1... | collective-permute-start | bytes 884744 | tf_op jit(solution)/shard_map/ppermute | solution.py:244
  76.2 5.9 %collective-permute-start.18 = (bf16[2,64,1152]{2,1,0:T(8,128)(2,1)S(1)}, bf16[2,64,1152]{2,1,0:T(8,128)(2,1)}, u32[]{:S(2)}, u32[]{:S(2)}) collective-permute-start(bf16[2,64,1152]{2,1,0:T(8,128)(2,1)S(1)} %collective-permute-done.14.refs_1_), channel_id=1, source_target_pairs={{0,2},{2,0},{1,3},{3,1},{4,6},{6,4},{5,7},{7,5},{8,10},{10,8},{9,1... | collective-permute-start | bytes 884744 | tf_op jit(solution)/shard_map/ppermute | solution.py:244
  76.3 5.8 %collective-permute-start.19 = (bf16[2,64,1152]{2,1,0:T(8,128)(2,1)S(1)}, bf16[2,64,1152]{2,1,0:T(8,128)(2,1)}, u32[]{:S(2)}, u32[]{:S(2)}) collective-permute-start(bf16[2,64,1152]{2,1,0:T(8,128)(2,1)S(1)} %collective-permute-done.15.refs_2_), channel_id=1, source_target_pairs={{0,2},{2,0},{1,3},{3,1},{4,6},{6,4},{5,7},{7,5},{8,10},{10,8},{9,1... | collective-permute-start | bytes 884744 | tf_op jit(solution)/shard_map/ppermute | solution.py:244
  76.8 5.4 %collective-permute-start.20 = (bf16[2,64,1152]{2,1,0:T(8,128)(2,1)S(1)}, bf16[2,64,1152]{2,1,0:T(8,128)(2,1)}, u32[]{:S(2)}, u32[]{:S(2)}) collective-permute-start(bf16[2,64,1152]{2,1,0:T(8,128)(2,1)S(1)} %collective-permute-done.16.refs_3_), channel_id=1, source_target_pairs={{0,2},{2,0},{1,3},{3,1},{4,6},{6,4},{5,7},{7,5},{8,10},{10,8},{9,1... | collective-permute-start | bytes 884744 | tf_op jit(solution)/shard_map/ppermute | solution.py:244
  86.3 12.9 %all-to-all-start.2 = ((bf16[16,64,128]{2,1,0:T(8,128)(2,1)}), bf16[16,64,128]{2,1,0:T(8,128)(2,1)S(1)}, u32[]{:S(2)}, u32[]{:S(2)}) async-start(bf16[16,64,128]{2,1,0:T(8,128)(2,1)} %copy-done.6), calls=%async_computation.2 | async-start | bytes 524288 | tf_op jit(solution)/shard_map/all_to_all | solution.py:240
  91.7 22.2 %copy-start.5 = (bf16[128,1024]{1,0:T(8,128)(2,1)S(1)}, bf16[128,1024]{1,0:T(8,128)(2,1)}, u32[]{:S(2)}) copy-start(bf16[128,1024]{1,0:T(8,128)(2,1)} %copy-done.3) | copy-start | bytes 786436
  91.7 22.2 %copy-start.9 = (bf16[128,1024]{1,0:T(8,128)(2,1)S(1)}, bf16[128,1024]{1,0:T(8,128)(2,1)}, u32[]{:S(2)}) copy-start(bf16[128,1024]{1,0:T(8,128)(2,1)} %copy-done.7) | copy-start | bytes 786436
  91.7 22.2 %copy-start.12 = (bf16[128,1024]{1,0:T(8,128)(2,1)S(1)}, bf16[128,1024]{1,0:T(8,128)(2,1)}, u32[]{:S(2)}) copy-start(bf16[128,1024]{1,0:T(8,128)(2,1)} %copy-done.10) | copy-start | bytes 786436
  91.7 22.2 %copy-start.15 = (bf16[128,1024]{1,0:T(8,128)(2,1)S(1)}, bf16[128,1024]{1,0:T(8,128)(2,1)}, u32[]{:S(2)}) copy-start(bf16[128,1024]{1,0:T(8,128)(2,1)} %copy-done.13) | copy-start | bytes 786436
  91.7 22.2 %copy-start.18 = (bf16[128,1024]{1,0:T(8,128)(2,1)S(1)}, bf16[128,1024]{1,0:T(8,128)(2,1)}, u32[]{:S(2)}) copy-start(bf16[128,1024]{1,0:T(8,128)(2,1)} %copy-done.16) | copy-start | bytes 786436
  91.7 22.2 %copy-start.21 = (bf16[128,1024]{1,0:T(8,128)(2,1)S(1)}, bf16[128,1024]{1,0:T(8,128)(2,1)}, u32[]{:S(2)}) copy-start(bf16[128,1024]{1,0:T(8,128)(2,1)} %copy-done.19) | copy-start | bytes 786436
  91.7 22.2 %copy-start.24 = (bf16[128,1024]{1,0:T(8,128)(2,1)S(1)}, bf16[128,1024]{1,0:T(8,128)(2,1)}, u32[]{:S(2)}) copy-start(bf16[128,1024]{1,0:T(8,128)(2,1)} %copy-done.22) | copy-start | bytes 786436
  91.8 12.6 %collective-permute-start.9 = (bf16[128,1024]{1,0:T(8,128)(2,1)}, bf16[128,1024]{1,0:T(8,128)(2,1)}, u32[]{:S(2)}, u32[]{:S(2)}) collective-permute-start(bf16[128,1024]{1,0:T(8,128)(2,1)} %get-tuple-element.33), channel_id=1, source_target_pairs={{0,16},{1,17},{2,18},{3,19},{4,20},{5,21},{6,22},{7,23},{8,24},{9,... | collective-permute-start | bytes 786440 | tf_op jit(solution)/shard_map/ppermute | solution.py:348
  97.7 16.2 %collective-permute-start.10 = (bf16[128,1024]{1,0:T(8,128)(2,1)}, bf16[128,1024]{1,0:T(8,128)(2,1)}, u32[]{:S(2)}, u32[]{:S(2)}) collective-permute-start(bf16[128,1024]{1,0:T(8,128)(2,1)} %get-tuple-element.32), channel_id=1, source_target_pairs={{16,0},{17,1},{18,2},{19,3},{20,4},{21,5},{22,6},{23,7},{24,8},{25... | collective-permute-start | bytes 786440 | tf_op jit(solution)/shard_map/ppermute | solution.py:349
  114.0 1.0 copy-start.27
  118.4 19.7 %all-to-all-start.3 = ((bf16[32,32,256]{2,1,0:T(8,128)(2,1)}), bf16[32,32,256]{2,1,0:T(8,128)(2,1)S(1)}, u32[]{:S(2)}, u32[]{:S(2)}) async-start(bf16[32,32,256]{2,1,0:T(8,128)(2,1)} %bitcast.25), calls=%async_computation.3 | async-start | bytes 1048576 | tf_op jit(solution)/shard_map/all_to_all | solution.py:240
  122.2 6.0 %collective-permute-start.21 = (f32[100,128]{1,0:T(8,128)S(1)}, f32[100,128]{1,0:T(8,128)S(1)}, u32[]{:S(2)}, u32[]{:S(2)}) collective-permute-start(f32[100,128]{1,0:T(8,128)S(1)} %get-tuple-element.22), channel_id=1, source_target_pairs={{0,1},{1,0},{2,3},{3,2},{4,5},{5,4},{6,7},{7,6},{8,9},{9,8},{10,11... | collective-permute-start | bytes 153608 | tf_op jit(solution)/shard_map/ppermute | solution.py:244
  (10 other events, 8.3 us)

commit v4 on v3

--- a/solution.py
+++ b/solution.py
@@ -24,6 +24,7 @@
 PAIR = 2
 WINDOW = (PAIR + 2 * RADIUS) * TILE
 NOWHERE = 100
+NOTE_ROWS = 16
 
 NORM_EPS = 1e-06
 SOFT_WIDTH = 0.0625
@@ -38,23 +39,48 @@
 OVER_COLUMNS = (((1,), (1,)), ((), ()))
 
 
-def call(kernel, name, outs, ins, scratch=(), flops=0, moved=0, exps=0):
+def call(kernel, name, outs, ins, scratch=(), flops=0, moved=0, exps=0, room=8):
     return pl.pallas_call(
         kernel,
         out_shape=[jax.ShapeDtypeStruct(shape, kind) for shape, kind in outs],
         in_specs=[SMEM if space == "s" else VMEM for space in ins],
         out_specs=[VMEM] * len(outs),
         scratch_shapes=[pltpu.VMEM(shape, kind) for shape, kind in scratch],
-        compiler_params=pltpu.CompilerParams(vmem_limit_bytes=32 * 2**20),
+        compiler_params=pltpu.CompilerParams(vmem_limit_bytes=room * 2**20),
         cost_estimate=pl.CostEstimate(flops=flops, bytes_accessed=moved, transcendentals=exps),
         name=name,
     )
 
 
-def norm_kernel(source_ref, out_ref):
+def prepare_kernel(
+    where_ref, source_ref, w_ref, mix_ref, readout_ref, near_ref, normed_ref, columns_ref, packed_ref
+):
+    halves, _, members_num = columns_ref.shape[:3]
+    for g in range(GROUP):
+        chunk = jnp.concatenate(
+            [w_ref[:, (part * GROUP + g) * COLS : (part * GROUP + g + 1) * COLS] for part in range(3)],
+            axis=1,
+        )
+        for half in range(halves):
+            for m in range(members_num):
+                columns_ref[half, g, m] = chunk
+    rows = source_ref.shape[0]
     source = source_ref[...].astype(F32)
     inverse = lax.rsqrt(jnp.mean(source * source, axis=-1, keepdims=True) + NORM_EPS)
-    out_ref[...] = (source * inverse).astype(BF16)
+    normed_ref[:rows, :] = (source * inverse).astype(BF16)
+    normed_ref[rows:, :] = jnp.zeros((NOTE_ROWS, LATENT_DIM), BF16)
+    row = lax.broadcasted_iota(jnp.int32, (NOTE_ROWS, 128), 0)
+    lane = lax.broadcasted_iota(jnp.int32, (NOTE_ROWS, 128), 1)
+    note = jnp.zeros((NOTE_ROWS, 128), F32)
+    for tile in range(near_ref.shape[0]):
+        for slot in range(K_NB):
+            at = near_ref[tile, slot]
+            step = jnp.where(at >= 0, at - where_ref[2] - tile, NOWHERE).astype(F32)
+            note = jnp.where((row == tile) & (lane == slot), step, note)
+    normed_ref[rows:, :128] = note.astype(BF16)
+    packed_ref[:, :LATENT_DIM] = mix_ref[...]
+    packed_ref[:, LATENT_DIM:] = jnp.zeros((packed_ref.shape[0], FIELD_PAD), BF16)
+    packed_ref[:, LATENT_DIM : LATENT_DIM + FIELD_NUM] = readout_ref[...]
 
 
 def owners(where_ref):
@@ -63,23 +89,18 @@
 
 
 def project_kernel(where_ref, *refs):
-    blocks, (w_ref, q_ref, kv_ref, rims_ref, normed_rims_ref) = refs[:GROUP], refs[GROUP:]
-    block = blocks[0].shape[0]
+    blocks = refs[:GROUP]
+    w_ref, normed_ref, q_ref, kv_ref, steps_ref, first_ref, last_ref = refs[GROUP:]
+    block = blocks[0].shape[0] - NOTE_ROWS
     for rows_ref, owner in zip(blocks, owners(where_ref)):
-        projected = jnp.dot(rows_ref[...], w_ref[...], preferred_element_type=F32).astype(BF16)
         at = pl.ds(pl.multiple_of(owner * block, block), block)
-        q_ref[at, :] = projected[:, :COLS]
-        kv_ref[at, :] = projected[:, COLS:]
-
-        @pl.when(owner == 0)
-        def _():
-            rims_ref[0] = projected[:RIM, COLS:]
-            normed_rims_ref[0] = rows_ref[:RIM, :]
-
-        @pl.when(owner == GROUP - 1)
-        def _():
-            rims_ref[1] = projected[block - RIM :, COLS:]
-            normed_rims_ref[1] = rows_ref[block - RIM :, :]
+        normed_ref[at, :] = rows_ref[:block, :]
+        steps_ref[owner] = rows_ref[block:, :128].astype(F32)
+    projected = jnp.dot(normed_ref[...], w_ref[...], preferred_element_type=F32).astype(BF16)
+    q_ref[...] = projected[:, :COLS]
+    kv_ref[...] = projected[:, COLS:]
+    first_ref[...] = projected[:RIM, COLS:]
+    last_ref[...] = projected[GROUP * block - RIM :, COLS:]
 
 
 def by_head(rows):
@@ -91,13 +112,13 @@
 
 
 def usable_keys(steps_ref, pair):
-    lane = lax.broadcasted_iota(jnp.int32, (1, WINDOW), 1) // TILE - RADIUS
+    lane = (lax.broadcasted_iota(jnp.int32, (1, WINDOW), 1) // TILE - RADIUS).astype(F32)
     masks = []
     for query_tile in range(PAIR):
-        found = jnp.zeros((1, WINDOW), jnp.int32)
+        found = jnp.zeros((1, WINDOW), F32)
         for slot in range(K_NB):
             step = steps_ref[pair, query_tile : query_tile + 1, slot : slot + 1]
-            found = jnp.where(lane - query_tile == step, 1, found)
+            found = jnp.where(lane - query_tile == step, 1.0, found)
         masks.append(found)
     row = lax.broadcasted_iota(jnp.int32, (2 * PAIR * TILE, 1), 0) // TILE % PAIR
     return jnp.where(row == 0, masks[0], masks[1]) > 0
@@ -219,21 +240,27 @@
             ]
 
 
-def product_kernel(where_ref, *refs):
-    blocks, (low_ref, high_ref, kv_ref, out_ref) = refs[:GROUP], refs[GROUP:]
-    places = [(owner + 1) * RIM for owner in owners(where_ref)]
-    places += [0, (GROUP + 1) * RIM]
-    blocks = list(blocks) + [low_ref, high_ref]
-    total = None
-    for at in range(0, len(blocks), 2):
-        rows = jnp.concatenate([blocks[at][...], blocks[at + 1][...]], axis=0)
-        kv = jnp.concatenate(
-            [kv_ref[pl.ds(pl.multiple_of(place, RIM), RIM), :] for place in places[at : at + 2]], axis=0
-        )
-        both = lax.dot_general(rows, kv, OVER_ROWS, preferred_element_type=F32)
-        term = both[:, : 2 * COLS] + both[:, 2 * COLS :]
-        total = term if total is None else total + term
+def product_kernel(normed_ref, low_ref, high_ref, kv_ref, out_ref):
+    def term(rows_ref, at):
+        kv = kv_ref[at : at + rows_ref.shape[0], :]
+        both = lax.dot_general(rows_ref[...], kv, OVER_ROWS, preferred_element_type=F32)
+        return both[:, : 2 * COLS] + both[:, 2 * COLS :]
+
+    count = normed_ref.shape[0]
+    total = term(normed_ref, RIM) + term(low_ref, 0) + term(high_ref, RIM + count)
     out_ref[...] = total.astype(BF16)
+
+
+def gather_kernel(parts_ref, out_ref):
+    halves, _, members_num = parts_ref.shape[:3]
+    for g in range(GROUP):
+        total = None
+        for half in range(halves):
+            for m in range(members_num):
+                part = parts_ref[half, g, m].astype(F32)
+                total = part if total is None else total + part
+        out_ref[:, g * COLS : (g + 1) * COLS] = total[:, :COLS]
+        out_ref[:, LATENT_DIM + g * COLS : LATENT_DIM + (g + 1) * COLS] = total[:, COLS:]
 
 
 def exchange(chunks, axes):
@@ -267,31 +294,35 @@
     up = [(i, i + 1) for i in range(halves - 1)]
     down = [(target, source) for source, target in up]
     core, quad, ens = (lax.axis_index(axis) for axis in ("core", "quad", "ens"))
-    where = jnp.stack([core, quad]).astype(jnp.int32)
-
-    (normed,) = call(
-        norm_kernel, "norm", [((node_rows, LATENT_DIM), BF16)], "v", flops=10, moved=2**20
-    )(members.reshape(node_rows, LATENT_DIM))
+    first_tile = lax.axis_index(("half", "quad", "core")) * neighbours.shape[0]
+    where = jnp.stack([core, quad, first_tile]).astype(jnp.int32)
+    width = LATENT_DIM + FIELD_PAD
+
+    normed, columns, packed = call(
+        prepare_kernel,
+        "prepare",
+        [
+            ((node_rows + NOTE_ROWS, LATENT_DIM), BF16),
+            ((halves, GROUP, members_num, shard, 3 * COLS), BF16),
+            ((shard, width), BF16),
+        ],
+        "svvvvs",
+        flops=2**20,
+        moved=2**20,
+        room=10,
+    )(
+        where,
+        members.reshape(node_rows, LATENT_DIM),
+        w_attn,
+        w_mix,
+        readout_matrix,
+        neighbours,
+    )
+    columns = exchange(columns.reshape(-1, shard, 3 * COLS), everyone)
+    columns = columns.reshape(LATENT_DIM, 3 * COLS)
     near, far = group_pieces(normed)
     blocks = near + far
 
-    columns = w_attn.reshape(shard, 3, GROUP, COLS).transpose(2, 0, 1, 3)
-    columns = columns.reshape(1, GROUP, 1, shard, 3 * COLS)
-    columns = jnp.broadcast_to(columns, (halves, GROUP, members_num, shard, 3 * COLS))
-    columns = exchange(columns.reshape(-1, shard, 3 * COLS), everyone)
-    columns = columns.reshape(LATENT_DIM, 3 * COLS)
-
-    local_tiles = neighbours.shape[0]
-    first_tile = lax.axis_index(("half", "quad", "core")) * local_tiles
-    steps = neighbours - first_tile - jnp.arange(local_tiles, dtype=jnp.int32)[:, None]
-    steps = jnp.where(neighbours >= 0, steps, NOWHERE)
-    steps = jnp.pad(steps, ((0, 8 - local_tiles), (0, 128 - K_NB)))
-    steps = lax.all_gather(steps, ("quad", "core"), axis=0)
-
-    packed = jnp.concatenate(
-        [w_mix, jnp.pad(readout_matrix, ((0, 0), (0, FIELD_PAD - FIELD_NUM)))], axis=1
-    )
-    width = packed.shape[1]
     packed = in_order(packed, "half", 0)
     packed = in_order(packed, "ens", 1).reshape(halves, members_num * shard, width)
     packed, near[3] = lax.optimization_barrier((packed, near[3]))
@@ -309,21 +340,24 @@
     factor = lax.dynamic_slice_in_dim(cell_surface_factor, ens * part, part, 0)
     factor = jnp.tile(factor[None], (1, members_num))
 
-    queries, own, rims, normed_rims = call(
+    normed, queries, own, steps, first, last = call(
         project_kernel,
         "project",
         [
+            ((rows, LATENT_DIM), BF16),
             ((rows, COLS), BF16),
             ((rows, 2 * COLS), BF16),
-            ((2, RIM, 2 * COLS), BF16),
-            ((2, RIM, LATENT_DIM), BF16),
+            ((GROUP, NOTE_ROWS, 128), F32),
+            ((RIM, 2 * COLS), BF16),
+            ((RIM, 2 * COLS), BF16),
         ],
         "s" + "v" * (GROUP + 1),
         flops=rows * LATENT_DIM * 6 * COLS,
         moved=4 * 2**20,
+        room=14,
     )(where, *blocks, columns)
-    low = lax.ppermute(rims[1], "half", up)
-    high = lax.ppermute(rims[0], "half", down)
+    low = lax.ppermute(last, "half", up)
+    high = lax.ppermute(first, "half", down)
 
     (outcome,) = call(
         interior_kernel,
@@ -343,10 +377,10 @@
         moved=2**20,
         exps=rows * 128,
     )(steps, queries, own, low, high, outcome)
+    normed, outcome = lax.optimization_barrier((normed, outcome))
+    normed_low = lax.ppermute(normed[rows - RIM :], "half", up)
+    normed_high = lax.ppermute(normed[:RIM], "half", down)
     attended = exchange(outcome.reshape(GROUP * members_num, part, COLS), ("quad", "core", "ens"))
-    normed_rims, attended = lax.optimization_barrier((normed_rims, attended))
-    normed_low = lax.ppermute(normed_rims[1], "half", up)
-    normed_high = lax.ppermute(normed_rims[0], "half", down)
 
     prediction, grads = call(
         mix_kernel,
@@ -356,6 +390,7 @@
         [((LATENT_DIM, width), BF16), ((node_rows, LATENT_DIM), BF16)],
         flops=node_rows * LATENT_DIM * 4 * width,
         moved=2**22,
+        room=14,
     )(where, attended, sources, *mix_near, *mix_far, truth, factor)
     grads = exchange(grads, ("quad", "core", "ens")).reshape(rows, COLS)
 
@@ -368,19 +403,22 @@
         flops=rows * COLS * 5120,
         moved=2**22,
         exps=rows * 512,
+        room=14,
     )(steps, queries, low, own, high, grads)
     (term,) = call(
         product_kernel,
         "product",
         [((LATENT_DIM, 2 * COLS), BF16)],
-        "s" + "v" * (GROUP + 3),
+        "vvvv",
         flops=(rows + 2 * RIM) * LATENT_DIM * 8 * COLS,
         moved=2**22,
-    )(where, *blocks, normed_low, normed_high, kv_grads)
+        room=16,
+    )(normed, normed_low, normed_high, kv_grads)
     term, prediction = lax.optimization_barrier((term, prediction))
     term = exchange(term.reshape(-1, shard, 2 * COLS), everyone)
-    term = term.reshape(halves, GROUP, members_num, shard, 2, COLS).astype(F32)
-    grad_kv = jnp.sum(term, axis=(0, 2)).transpose(1, 2, 0, 3).reshape(shard, 2 * LATENT_DIM)
+    (grad_kv,) = call(
+        gather_kernel, "gather_sums", [((shard, 2 * LATENT_DIM), F32)], "v", flops=2**17, moved=2**20
+    )(term.reshape(halves, GROUP, members_num, shard, 2 * COLS))
 
     if members_num == 2:
         got = jnp.roll(swap(prediction, "ens", 1), part, axis=1)

time: 141 us -> 140 us (level)
  blocking collectives: 14.2 us -> 0 us
  waiting for transfers between devices: 34.1 us -> 47.9 us
    ppermute x18, waiting for transfers between devices: 10.8 us -> 27.9 us  [swap(): lax.ppermute(value, axis, [(i, i ^ step) for i in range(lax.axis_size(axi...]
    all_gather x1 -> x0, blocking collectives: 14.2 us -> none  [body(): steps = lax.all_gather(steps, ('quad', 'core'), axis=0)]
    all_to_all x4, waiting for transfers between devices: 13.7 us -> 8.96 us  [exchange(): return lax.all_to_all(chunks, axes, 0, 0)]
    ppermute x18, starting transfers between devices: 20.9 us -> 17.9 us  [swap(): lax.ppermute(value, axis, [(i, i ^ step) for i in range(lax.axis_size(axi...]
    all_to_all x4, starting transfers between devices: 17.3 us -> 20.2 us  [exchange(): return lax.all_to_all(chunks, axes, 0, 0)]
    slice x0 -> x1, local copies, waits for them, and re-layouts: none -> 1.85 us  [body(): normed_high = lax.ppermute(normed[:RIM], 'half', down)]
    ppermute x4, waiting for transfers between devices: 9.58 us -> 11 us  [the longest x1 9.57 us: body(): normed_high = lax.ppermute(normed[:RIM], 'half', down)]
    pallas_call x3 -> x4, Pallas kernels: 6.6 us -> 8 us  [the longest x1 3.74 us: body(): call(product_kernel, 'product', [((LATENT_DIM, 2 * COLS), BF16)], 'vvvv',...]
  transfers between devices with their start and end apart: 26 -> 26, of which waited for: 7 -> 7; matrix products, arithmetic and copies ran while one was open for 4% -> 4% of each run, Pallas kernels for 9% -> 7%
where the time goes in v4:
time: 140 us; the launch traced here: 139 us
  starting transfers between devices  50 us (36%)
  waiting for transfers between devices  47.9 us (34%)
  Pallas kernels  20.2 us (14%)
  local copies, waits for them, and re-layouts  18.3 us (13%)
  other arithmetic  1.96 us (1%)
    ppermute x18, waiting for transfers between devices, swap(): lax.ppermute(value, axis, [(i, i ^ step) for i in range(lax.axis_size(axi...  27.9 us
    all_to_all x4, starting transfers between devices, exchange(): return lax.all_to_all(chunks, axes, 0, 0)  20.2 us
    ppermute x18, starting transfers between devices, swap(): lax.ppermute(value, axis, [(i, i ^ step) for i in range(lax.axis_size(axi...  17.9 us
    unnamed x48, local copies, waits for them, and re-layouts  15.4 us
    ppermute x1, waiting for transfers between devices, body(): normed_high = lax.ppermute(normed[:RIM], 'half', down)  9.57 us
    all_to_all x4, waiting for transfers between devices, exchange(): return lax.all_to_all(chunks, axes, 0, 0)  8.96 us
    pallas_call x1, Pallas kernels, body(): call(backward_kernel, 'attention_backward', [((rows + 2 * RIM, 4 * COLS),...  5.18 us
    ppermute x1, starting transfers between devices, body(): normed_low = lax.ppermute(normed[rows - RIM:], 'half', up)  5.03 us
  transfers between devices with their start and end apart: 26, of which 7 were waited for; matrix products, arithmetic and copies ran while one was open for 4% of the time, Pallas kernels for 7%

profile of v4, /device:TPU:1, one launch (start us, length us, event | category | flops | bytes accessed | tf_op | source)
XLA Modules:
  0.0 139.3 jit_solution(7453363026125310950)
XLA Ops:
  0.7 0.9 copy-done.1
  1.7 0.9 copy-done.14
  2.6 0.8 copy-done.17
  4.8 1.6 %prepare.1 = (bf16[144,1024]{1,0:T(8,128)(2,1)S(1)}, bf16[2,8,2,32,384]{4,3,2,1,0:T(8,128)(2,1)}, bf16[32,1152]{1,0:T(8,128)(2,1)S(1)}) custom-call(s32[3]{0:T(128)S(1)} %pad_add_fusion.where_ref, bf16[128,1024]{1,0:T(8,128)(2,1)S(1)} %bitcast.44, bf16[32,3072]{1,0:T(8,128)(2,1)S(1)} %copy-done.14, bf16[32,1024]{1,0:T(8,128)(2,1)S(1)} %copy-done.17, ...), custom_call_target="tpu_custom_call" | custom-call | flops 1048576 | bytes 1048576 | tf_op jit(solution)/shard_map/prepare/pallas_call | solution.py:301
  6.4 7.1 %all-to-all-start = ((bf16[32,32,384]{2,1,0:T(8,128)(2,1)}), bf16[32,32,384]{2,1,0:T(8,128)(2,1)S(1)}, u32[]{:S(2)}, u32[]{:S(2)}) async-start(bf16[32,32,384]{2,1,0:T(8,128)(2,1)} %bitcast.4), calls=%async_computation | async-start | bytes 1572864 | tf_op jit(solution)/shard_map/all_to_all | solution.py:267
  13.5 2.4 %collective-permute-start.12 = (bf16[32,1152]{1,0:T(8,128)(2,1)S(1)}, bf16[32,1152]{1,0:T(8,128)(2,1)S(1)}, u32[]{:S(2)}, u32[]{:S(2)}) collective-permute-start(bf16[32,1152]{1,0:T(8,128)(2,1)S(1)} %get-tuple-element.28), channel_id=1, source_target_pairs={{0,16},{16,0},{1,17},{17,1},{2,18},{18,2},{3,19},{19,3},{4,20},{20... | collective-permute-start | bytes 221192 | tf_op jit(solution)/shard_map/ppermute | solution.py:271
  15.9 1.2 collective-permute-start
  17.1 1.2 collective-permute-start.1
  18.5 18.2 %collective-permute-done.12 = bf16[32,1152]{1,0:T(8,128)(2,1)S(1)} collective-permute-done((bf16[32,1152]{1,0:T(8,128)(2,1)S(1)}, bf16[32,1152]{1,0:T(8,128)(2,1)S(1)}, u32[]{:S(2)}, u32[]{:S(2)}) %collective-permute-start.12) | collective-permute-done | bytes 73760 | tf_op jit(solution)/shard_map/ppermute | solution.py:271
  36.7 1.2 collective-permute-start.13
  38.0 1.2 collective-permute-start.3
  39.7 3.9 %collective-permute-done.2.refs_3_ = bf16[144,1024]{1,0:T(8,128)(2,1)S(1)} collective-permute-done((bf16[144,1024]{1,0:T(8,128)(2,1)S(1)}, bf16[144,1024]{1,0:T(8,128)(2,1)S(1)}, u32[]{:S(2)}, u32[]{:S(2)}) %collective-permute-start.2) | collective-permute-done | bytes 294944 | tf_op jit(solution)/shard_map/ppermute | solution.py:271
  43.5 0.9 collective-permute-start.6
  44.4 0.8 select_bitcast_fusion.1
  45.2 0.7 copy-done.3
  45.9 0.7 copy-done.7
  47.4 1.0 copy-done.4
  48.3 1.0 copy-done.8
  49.3 1.0 copy-done.12
  50.3 1.9 %project.1 = (bf16[1024,1024]{1,0:T(8,128)(2,1)S(1)}, bf16[1024,128]{1,0:T(8,128)(2,1)S(1)}, bf16[1024,256]{1,0:T(8,128)(2,1)S(1)}, f32[8,16,128]{2,1,0:T(8,128)...) custom-call(s32[3]{0:T(128)S(1)} %pad_add_fusion.where_ref, ...), custom_call_target="tpu_custom_call" | custom-call | flops 805306368 | bytes 4194304 | tf_op jit(solution)/shard_map/project/pallas_call | solution.py:343
  52.2 1.4 copy-done.15
  53.5 4.1 %collective-permute-start.7 = (bf16[128,256]{1,0:T(8,128)(2,1)S(1)}, bf16[128,256]{1,0:T(8,128)(2,1)S(1)}, u32[]{:S(2)}, u32[]{:S(2)}) collective-permute-start(bf16[128,256]{1,0:T(8,128)(2,1)S(1)} %get-tuple-element.24), channel_id=1, source_target_pairs={{0,16},{1,17},{2,18},{3,19},{4,20},{5,21},{6,22},{7,23},{8,24},{9,... | collective-permute-start | bytes 196616 | tf_op jit(solution)/shard_map/ppermute | solution.py:359
  57.6 1.3 collective-permute-start.8
  59.4 2.4 %collective-permute-start.16 = (bf16[2,64,1152]{2,1,0:T(8,128)(2,1)S(1)}, bf16[2,64,1152]{2,1,0:T(8,128)(2,1)S(1)}, u32[]{:S(2)}, u32[]{:S(2)}) collective-permute-start(bf16[2,64,1152]{2,1,0:T(8,128)(2,1)S(1)} %bitcast.40), channel_id=1, source_target_pairs={{0,12},{4,8},{8,4},{12,0},{1,13},{5,9},{9,5},{13,1},{2,14},{6,10},... | collective-permute-start | bytes 884744 | tf_op jit(solution)/shard_map/ppermute | solution.py:271
  61.7 2.6 %attention_interior.1.done_ref = bf16[1024,128]{1,0:T(8,128)(2,1)S(1)} custom-call(f32[8,16,128]{2,1,0:T(8,128)S(1)} %get-tuple-element.21.steps_ref, bf16[1024,128]{1,0:T(8,128)(2,1)S(1)} %get-tuple-element.22.q_ref, bf16[1024,256]{1,0:T(8,128)(2,1)S(1)} %get-tuple-element.23.kv_ref.own_ref), custom_call_target="tpu_custom_call" | custom-call | flops 268435456 | bytes 2097152 | tf_op jit(solution)/shard_map/attention_interior/pallas_call | solution.py:362
  64.3 1.5 %collective-permute-done.8.high_ref = bf16[128,256]{1,0:T(8,128)(2,1)S(1)} collective-permute-done((bf16[128,256]{1,0:T(8,128)(2,1)S(1)}, bf16[128,256]{1,0:T(8,128)(2,1)S(1)}, u32[]{:S(2)}, u32[]{:S(2)}) %collective-permute-start.8) | collective-permute-done | bytes 65568 | tf_op jit(solution)/shard_map/ppermute | solution.py:360
  65.8 1.7 %attention_edges.1 = bf16[1024,128]{1,0:T(8,128)(2,1)} custom-call(f32[8,16,128]{2,1,0:T(8,128)S(1)} %get-tuple-element.21.steps_ref, bf16[1024,128]{1,0:T(8,128)(2,1)S(1)} %get-tuple-element.22.q_ref, bf16[1024,256]{1,0:T(8,128)(2,1)S(1)} %get-tuple-element.23.kv_ref.own_ref, bf16[128,256]{1,0:T(8,128)(2,1)S(1)} %collective-permute-done.7.low_ref, ...), custom_call_target="tpu_custom_call" | custom-call | flops 67108864 | bytes 1048576 | tf_op jit(solution)/shard_map/attention_edges/pallas_call | solution.py:371
  67.5 3.9 %all-to-all-start.1 = ((bf16[16,64,128]{2,1,0:T(8,128)(2,1)}), bf16[16,64,128]{2,1,0:T(8,128)(2,1)S(1)}, u32[]{:S(2)}, u32[]{:S(2)}) async-start(bf16[16,64,128]{2,1,0:T(8,128)(2,1)} %bitcast.6), calls=%async_computation.1 | async-start | bytes 524288 | tf_op jit(solution)/shard_map/all_to_all | solution.py:267
  72.0 1.4 collective-permute-start.11
  75.0 1.3 collective-permute-done.16.refs_3_
  76.3 2.4 %collective-permute-start.20 = (bf16[2,64,1152]{2,1,0:T(8,128)(2,1)S(1)}, bf16[2,64,1152]{2,1,0:T(8,128)(2,1)S(1)}, u32[]{:S(2)}, u32[]{:S(2)}) collective-permute-start(bf16[2,64,1152]{2,1,0:T(8,128)(2,1)S(1)} %collective-permute-done.16.refs_3_), channel_id=1, source_target_pairs={{0,2},{2,0},{1,3},{3,1},{4,6},{6,4},{5,7},{7,5},{8,10},{10,8},{9,1... | collective-permute-start | bytes 884744 | tf_op jit(solution)/shard_map/ppermute | solution.py:271
  78.7 0.9 fusion
  79.8 0.7 copy-done.5
  81.2 1.0 copy-done.6
  82.2 1.0 copy-done.10
  83.1 2.7 %mix_loss_backward.1 = (f32[100,128]{1,0:T(8,128)S(1)}, bf16[16,64,128]{2,1,0:T(8,128)(2,1)S(1)}) custom-call(s32[3]{0:T(128)S(1)} %pad_add_fusion.where_ref, bf16[16,64,128]{2,1,0:T(8,128)(2,1)S(1)} %all-to-all-done.1.att_ref, bf16[2,64,1024]{2,1,0:T(8,128)(2,1)S(1)} %pad_maximum_fusion.1.source_ref, bf16[2,64,1152]{2,1,0:T(8,128)(2,1)S(1)} %bitcast.42, ...), custom_call_target="tpu_custom_call" | custom-call | flops 603979776 | bytes 4194304 | tf_op jit(solution)/shard_map/mix_loss_backward/pallas_call | solution.py:385
  86.6 5.5 %all-to-all-start.2 = ((bf16[16,64,128]{2,1,0:T(8,128)(2,1)}), bf16[16,64,128]{2,1,0:T(8,128)(2,1)S(1)}, u32[]{:S(2)}, u32[]{:S(2)}) async-start(bf16[16,64,128]{2,1,0:T(8,128)(2,1)} %copy-done.13), calls=%async_computation.2 | async-start | bytes 524288 | tf_op jit(solution)/shard_map/all_to_all | solution.py:267
  92.0 1.9 %fusion.3 = (bf16[128,1024]{1,0:T(8,128)(2,1)}, bf16[128,1024]{1,0:T(8,128)(2,1)}) fusion(bf16[1024,1024]{1,0:T(8,128)(2,1)} %copy-done.15), kind=kLoop, calls=%fused_computation.22 | loop fusion | bytes 1048576 | tf_op jit(solution)/shard_map/slice | solution.py:382
  93.9 5.0 %collective-permute-start.9 = (bf16[128,1024]{1,0:T(8,128)(2,1)}, bf16[128,1024]{1,0:T(8,128)(2,1)}, u32[]{:S(2)}, u32[]{:S(2)}) collective-permute-start(bf16[128,1024]{1,0:T(8,128)(2,1)} %get-tuple-element.39), channel_id=1, source_target_pairs={{0,16},{1,17},{2,18},{3,19},{4,20},{5,21},{6,22},{7,23},{8,24},{9,... | collective-permute-start | bytes 786440 | tf_op jit(solution)/shard_map/ppermute | solution.py:381
  98.9 1.5 %collective-permute-start.10 = (bf16[128,1024]{1,0:T(8,128)(2,1)}, bf16[128,1024]{1,0:T(8,128)(2,1)}, u32[]{:S(2)}, u32[]{:S(2)}) collective-permute-start(bf16[128,1024]{1,0:T(8,128)(2,1)} %get-tuple-element.38), channel_id=1, source_target_pairs={{16,0},{17,1},{18,2},{19,3},{20,4},{21,5},{22,6},{23,7},{24,8},{25... | collective-permute-start | bytes 786440 | tf_op jit(solution)/shard_map/ppermute | solution.py:382
  100.4 5.2 %attention_backward.1.kv_ref = bf16[1280,512]{1,0:T(8,128)(2,1)S(1)} custom-call(f32[8,16,128]{2,1,0:T(8,128)S(1)} %get-tuple-element.21.steps_ref, bf16[1024,128]{1,0:T(8,128)(2,1)S(1)} %get-tuple-element.22.q_ref, bf16[128,256]{1,0:T(8,128)(2,1)S(1)} %collective-permute-done.7.low_ref, bf16[1024,256]{1,0:T(8,128)(2,1)S(1)} %get-tuple-element.23.kv_ref.own_ref, ...), custom_call_target="tpu_custom_call" | custom-call | flops 671088640 | bytes 4194304 | tf_op jit(solution)/shard_map/attention_backward/pallas_call | solution.py:397
  105.6 9.6 %collective-permute-done.10.high_ref = bf16[128,1024]{1,0:T(8,128)(2,1)} collective-permute-done((bf16[128,1024]{1,0:T(8,128)(2,1)}, bf16[128,1024]{1,0:T(8,128)(2,1)}, u32[]{:S(2)}, u32[]{:S(2)}) %collective-permute-start.10) | collective-permute-done | bytes 262176 | tf_op jit(solution)/shard_map/ppermute | solution.py:382
  115.2 3.7 %product.1 = bf16[1024,256]{1,0:T(8,128)(2,1)} custom-call(bf16[1024,1024]{1,0:T(8,128)(2,1)S(1)} %copy-done.16, bf16[128,1024]{1,0:T(8,128)(2,1)} %collective-permute-done.9.low_ref, bf16[128,1024]{1,0:T(8,128)(2,1)} %collective-permute-done.10.high_ref, bf16[1280,512]{1,0:T(8,128)(2,1)S(1)} %attention_backward.1.kv_ref), custom_call_target="tpu_custom_call" | custom-call | flops 1342177280 | bytes 4194304 | tf_op jit(solution)/shard_map/product/pallas_call | solution.py:408
  118.9 3.8 %all-to-all-start.3 = ((bf16[32,32,256]{2,1,0:T(8,128)(2,1)}), bf16[32,32,256]{2,1,0:T(8,128)(2,1)S(1)}, u32[]{:S(2)}, u32[]{:S(2)}) async-start(bf16[32,32,256]{2,1,0:T(8,128)(2,1)} %bitcast.20), calls=%async_computation.3 | async-start | bytes 1048576 | tf_op jit(solution)/shard_map/all_to_all | solution.py:267
  122.8 1.5 %collective-permute-start.21 = (f32[100,128]{1,0:T(8,128)S(1)}, f32[100,128]{1,0:T(8,128)S(1)}, u32[]{:S(2)}, u32[]{:S(2)}) collective-permute-start(f32[100,128]{1,0:T(8,128)S(1)} %get-tuple-element.32), channel_id=1, source_target_pairs={{0,1},{1,0},{2,3},{3,2},{4,5},{5,4},{6,7},{7,6},{8,9},{9,8},{10,11... | collective-permute-start | bytes 153608 | tf_op jit(solution)/shard_map/ppermute | solution.py:271
  124.2 4.5 %collective-permute-done.21 = f32[100,128]{1,0:T(8,128)S(1)} collective-permute-done((f32[100,128]{1,0:T(8,128)S(1)}, f32[100,128]{1,0:T(8,128)S(1)}, u32[]{:S(2)}, u32[]{:S(2)}) %collective-permute-start.21) | collective-permute-done | bytes 51232 | tf_op jit(solution)/shard_map/ppermute | solution.py:271
  129.6 9.0 %all-to-all-done.3 = bf16[32,32,256]{2,1,0:T(8,128)(2,1)S(1)} async-done(((bf16[32,32,256]{2,1,0:T(8,128)(2,1)}), bf16[32,32,256]{2,1,0:T(8,128)(2,1)S(1)}, u32[]{:S(2)}, u32[]{:S(2)}) %all-to-all-start.3) | async-done | bytes 524320 | tf_op jit(solution)/shard_map/all_to_all | solution.py:267
  138.6 0.8 gather_sums.1
  (81 shorter events, 8.0 us)
Async XLA Ops:
  0.6 72.8 %copy-start = (f32[100,128]{1,0:T(8,128)S(1)}, f32[100,128]{1,0:T(8,128)}, u32[]{:S(2)}) copy-start(f32[100,128]{1,0:T(8,128)} %param.11) | copy-start | bytes 153604
  0.7 1.0 copy-start.1
  1.7 0.9 copy-start.14
  2.6 0.8 copy-start.17
  3.5 0.7 copy-start.18
  6.4 40.9 %all-to-all-start = ((bf16[32,32,384]{2,1,0:T(8,128)(2,1)}), bf16[32,32,384]{2,1,0:T(8,128)(2,1)S(1)}, u32[]{:S(2)}, u32[]{:S(2)}) async-start(bf16[32,32,384]{2,1,0:T(8,128)(2,1)} %bitcast.4), calls=%async_computation | async-start | bytes 1572864 | tf_op jit(solution)/shard_map/all_to_all | solution.py:267
  13.5 23.2 %collective-permute-start.12 = (bf16[32,1152]{1,0:T(8,128)(2,1)S(1)}, bf16[32,1152]{1,0:T(8,128)(2,1)S(1)}, u32[]{:S(2)}, u32[]{:S(2)}) collective-permute-start(bf16[32,1152]{1,0:T(8,128)(2,1)S(1)} %get-tuple-element.28), channel_id=1, source_target_pairs={{0,16},{16,0},{1,17},{17,1},{2,18},{18,2},{3,19},{19,3},{4,20},{20... | collective-permute-start | bytes 221192 | tf_op jit(solution)/shard_map/ppermute | solution.py:271
  15.9 23.3 %collective-permute-start = (bf16[144,1024]{1,0:T(8,128)(2,1)S(1)}, bf16[144,1024]{1,0:T(8,128)(2,1)S(1)}, u32[]{:S(2)}, u32[]{:S(2)}) collective-permute-start(bf16[144,1024]{1,0:T(8,128)(2,1)S(1)} %get-tuple-element.18.refs_0_), channel_id=1, source_target_pairs={{0,4},{4,0},{8,12},{12,8},{1,5},{5,1},{9,13},{13,9},{2,6},{6,2},{1... | collective-permute-start | bytes 884744 | tf_op jit(solution)/shard_map/ppermute | solution.py:271
  17.1 22.1 %collective-permute-start.1 = (bf16[144,1024]{1,0:T(8,128)(2,1)S(1)}, bf16[144,1024]{1,0:T(8,128)(2,1)S(1)}, u32[]{:S(2)}, u32[]{:S(2)}) collective-permute-start(bf16[144,1024]{1,0:T(8,128)(2,1)S(1)} %get-tuple-element.18.refs_0_), channel_id=1, source_target_pairs={{0,8},{4,12},{8,0},{12,4},{1,9},{5,13},{9,1},{13,5},{2,10},{6,14},... | collective-permute-start | bytes 884744 | tf_op jit(solution)/shard_map/ppermute | solution.py:271
  18.3 25.2 %collective-permute-start.2 = (bf16[144,1024]{1,0:T(8,128)(2,1)S(1)}, bf16[144,1024]{1,0:T(8,128)(2,1)S(1)}, u32[]{:S(2)}, u32[]{:S(2)}) collective-permute-start(bf16[144,1024]{1,0:T(8,128)(2,1)S(1)} %get-tuple-element.18.refs_0_), channel_id=1, source_target_pairs={{0,12},{4,8},{8,4},{12,0},{1,13},{5,9},{9,5},{13,1},{2,14},{6,10},... | collective-permute-start | bytes 884744 | tf_op jit(solution)/shard_map/ppermute | solution.py:271
  36.7 7.7 %collective-permute-start.13 = (bf16[2,32,1152]{2,1,0:T(8,128)(2,1)S(1)}, bf16[2,32,1152]{2,1,0:T(8,128)(2,1)S(1)}, u32[]{:S(2)}, u32[]{:S(2)}) collective-permute-start(bf16[2,32,1152]{2,1,0:T(8,128)(2,1)S(1)} %pad_maximum_fusion.2), channel_id=1, source_target_pairs={{0,1},{1,0},{2,3},{3,2},{4,5},{5,4},{6,7},{7,6},{8,9},{9,8},{10,11... | collective-permute-start | bytes 442376 | tf_op jit(solution)/shard_map/ppermute | solution.py:271
  38.0 7.2 %collective-permute-start.3 = (bf16[144,1024]{1,0:T(8,128)(2,1)S(1)}, bf16[144,1024]{1,0:T(8,128)(2,1)S(1)}, u32[]{:S(2)}, u32[]{:S(2)}) collective-permute-start(bf16[144,1024]{1,0:T(8,128)(2,1)S(1)} %get-tuple-element.18.refs_0_), channel_id=1, source_target_pairs={{0,2},{2,0},{1,3},{3,1},{4,6},{6,4},{5,7},{7,5},{8,10},{10,8},{9,1... | collective-permute-start | bytes 884744 | tf_op jit(solution)/shard_map/ppermute | solution.py:271
  39.1 6.0 %collective-permute-start.4 = (bf16[144,1024]{1,0:T(8,128)(2,1)S(1)}, bf16[144,1024]{1,0:T(8,128)(2,1)S(1)}, u32[]{:S(2)}, u32[]{:S(2)}) collective-permute-start(bf16[144,1024]{1,0:T(8,128)(2,1)S(1)} %collective-permute-done.refs_1_), channel_id=1, source_target_pairs={{0,2},{2,0},{1,3},{3,1},{4,6},{6,4},{5,7},{7,5},{8,10},{10,8},{9,1... | collective-permute-start | bytes 884744 | tf_op jit(solution)/shard_map/ppermute | solution.py:271
  39.2 6.7 %collective-permute-start.5 = (bf16[144,1024]{1,0:T(8,128)(2,1)S(1)}, bf16[144,1024]{1,0:T(8,128)(2,1)S(1)}, u32[]{:S(2)}, u32[]{:S(2)}) collective-permute-start(bf16[144,1024]{1,0:T(8,128)(2,1)S(1)} %collective-permute-done.1.refs_2_), channel_id=1, source_target_pairs={{0,2},{2,0},{1,3},{3,1},{4,6},{6,4},{5,7},{7,5},{8,10},{10,8},{9,1... | collective-permute-start | bytes 884744 | tf_op jit(solution)/shard_map/ppermute | solution.py:271
  43.5 3.1 %collective-permute-start.6 = (bf16[144,1024]{1,0:T(8,128)(2,1)S(1)}, bf16[144,1024]{1,0:T(8,128)(2,1)S(1)}, u32[]{:S(2)}, u32[]{:S(2)}) collective-permute-start(bf16[144,1024]{1,0:T(8,128)(2,1)S(1)} %collective-permute-done.2.refs_3_), channel_id=1, source_target_pairs={{0,2},{2,0},{1,3},{3,1},{4,6},{6,4},{5,7},{7,5},{8,10},{10,8},{9,1... | collective-permute-start | bytes 884744 | tf_op jit(solution)/shard_map/ppermute | solution.py:271
  45.2 0.7 copy-start.3
  45.9 0.7 copy-start.7
  46.6 0.7 copy-start.11
  47.4 1.0 copy-start.4
  48.3 1.0 copy-start.8
  49.3 1.0 copy-start.12
  50.2 8.6 %copy-start.20 = (bf16[2,1,32,1152]{3,2,0,1:T(8,128)(2,1)S(1)}, bf16[2,1,32,1152]{3,2,0,1:T(8,128)(2,1)}, u32[]{:S(2)}) copy-start(bf16[2,1,32,1152]{3,2,0,1:T(8,128)(2,1)} %get-tuple-element.42) | copy-start | bytes 442372
  50.2 8.7 %copy-start.21 = (bf16[2,1,32,1152]{3,2,0,1:T(8,128)(2,1)S(1)}, bf16[2,1,32,1152]{3,2,0,1:T(8,128)(2,1)}, u32[]{:S(2)}) copy-start(bf16[2,1,32,1152]{3,2,0,1:T(8,128)(2,1)} %get-tuple-element.43) | copy-start | bytes 442372
  52.2 1.4 copy-start.15
  53.5 10.8 %collective-permute-start.7 = (bf16[128,256]{1,0:T(8,128)(2,1)S(1)}, bf16[128,256]{1,0:T(8,128)(2,1)S(1)}, u32[]{:S(2)}, u32[]{:S(2)}) collective-permute-start(bf16[128,256]{1,0:T(8,128)(2,1)S(1)} %get-tuple-element.24), channel_id=1, source_target_pairs={{0,16},{1,17},{2,18},{3,19},{4,20},{5,21},{6,22},{7,23},{8,24},{9,... | collective-permute-start | bytes 196616 | tf_op jit(solution)/shard_map/ppermute | solution.py:359
  57.6 8.2 %collective-permute-start.8 = (bf16[128,256]{1,0:T(8,128)(2,1)S(1)}, bf16[128,256]{1,0:T(8,128)(2,1)S(1)}, u32[]{:S(2)}, u32[]{:S(2)}) collective-permute-start(bf16[128,256]{1,0:T(8,128)(2,1)S(1)} %get-tuple-element.25), channel_id=1, source_target_pairs={{16,0},{17,1},{18,2},{19,3},{20,4},{21,5},{22,6},{23,7},{24,8},{25... | collective-permute-start | bytes 196616 | tf_op jit(solution)/shard_map/ppermute | solution.py:360
  58.9 12.4 %copy-start.2 = (bf16[1,128,1024]{2,1,0:T(8,128)(2,1)S(1)}, bf16[1,128,1024]{2,1,0:T(8,128)(2,1)}, u32[]{:S(2)}) copy-start(bf16[1,128,1024]{2,1,0:T(8,128)(2,1)} %param.7) | copy-start | bytes 786436
  59.0 14.7 %copy-start.22 = (f32[128]{0:T(128)S(1)}, f32[128]{0:T(128)}, u32[]{:S(2)}) copy-start(f32[128]{0:T(128)} %param.12) | copy-start | bytes 1540
  59.0 15.5 %collective-permute-start.14 = (bf16[2,64,1152]{2,1,0:T(8,128)(2,1)S(1)}, bf16[2,64,1152]{2,1,0:T(8,128)(2,1)S(1)}, u32[]{:S(2)}, u32[]{:S(2)}) collective-permute-start(bf16[2,64,1152]{2,1,0:T(8,128)(2,1)S(1)} %bitcast.38), channel_id=1, source_target_pairs={{0,4},{4,0},{8,12},{12,8},{1,5},{5,1},{9,13},{13,9},{2,6},{6,2},{1... | collective-permute-start | bytes 884744 | tf_op jit(solution)/shard_map/ppermute | solution.py:271
  59.3 15.2 %collective-permute-start.15 = (bf16[2,64,1152]{2,1,0:T(8,128)(2,1)S(1)}, bf16[2,64,1152]{2,1,0:T(8,128)(2,1)S(1)}, u32[]{:S(2)}, u32[]{:S(2)}) collective-permute-start(bf16[2,64,1152]{2,1,0:T(8,128)(2,1)S(1)} %bitcast.39), channel_id=1, source_target_pairs={{0,8},{4,12},{8,0},{12,4},{1,9},{5,13},{9,1},{13,5},{2,10},{6,14},... | collective-permute-start | bytes 884744 | tf_op jit(solution)/shard_map/ppermute | solution.py:271
  59.4 17.0 %collective-permute-start.16 = (bf16[2,64,1152]{2,1,0:T(8,128)(2,1)S(1)}, bf16[2,64,1152]{2,1,0:T(8,128)(2,1)S(1)}, u32[]{:S(2)}, u32[]{:S(2)}) collective-permute-start(bf16[2,64,1152]{2,1,0:T(8,128)(2,1)S(1)} %bitcast.40), channel_id=1, source_target_pairs={{0,12},{4,8},{8,4},{12,0},{1,13},{5,9},{9,5},{13,1},{2,14},{6,10},... | collective-permute-start | bytes 884744 | tf_op jit(solution)/shard_map/ppermute | solution.py:271
  67.5 13.7 %all-to-all-start.1 = ((bf16[16,64,128]{2,1,0:T(8,128)(2,1)}), bf16[16,64,128]{2,1,0:T(8,128)(2,1)S(1)}, u32[]{:S(2)}, u32[]{:S(2)}) async-start(bf16[16,64,128]{2,1,0:T(8,128)(2,1)} %bitcast.6), calls=%async_computation.1 | async-start | bytes 524288 | tf_op jit(solution)/shard_map/all_to_all | solution.py:267
  72.0 6.7 %collective-permute-start.11 = (bf16[64,1024]{1,0:T(8,128)(2,1)}, bf16[64,1024]{1,0:T(8,128)(2,1)}, u32[]{:S(2)}, u32[]{:S(2)}) collective-permute-start(bf16[64,1024]{1,0:T(8,128)(2,1)} %dynamic-slice_bitcast_fusion), channel_id=1, source_target_pairs={{0,1},{1,0},{2,3},{3,2},{4,5},{5,4},{6,7},{7,6},{8,9},{9,8},{10,11... | collective-permute-start | bytes 393224 | tf_op jit(solution)/shard_map/ppermute | solution.py:271
  73.9 5.9 %collective-permute-start.17 = (bf16[2,64,1152]{2,1,0:T(8,128)(2,1)S(1)}, bf16[2,64,1152]{2,1,0:T(8,128)(2,1)S(1)}, u32[]{:S(2)}, u32[]{:S(2)}) collective-permute-start(bf16[2,64,1152]{2,1,0:T(8,128)(2,1)S(1)} %bitcast.41), channel_id=1, source_target_pairs={{0,2},{2,0},{1,3},{3,1},{4,6},{6,4},{5,7},{7,5},{8,10},{10,8},{9,1... | collective-permute-start | bytes 884744 | tf_op jit(solution)/shard_map/ppermute | solution.py:271
  74.5 5.2 %collective-permute-start.18 = (bf16[2,64,1152]{2,1,0:T(8,128)(2,1)S(1)}, bf16[2,64,1152]{2,1,0:T(8,128)(2,1)S(1)}, u32[]{:S(2)}, u32[]{:S(2)}) collective-permute-start(bf16[2,64,1152]{2,1,0:T(8,128)(2,1)S(1)} %collective-permute-done.14.refs_1_), channel_id=1, source_target_pairs={{0,2},{2,0},{1,3},{3,1},{4,6},{6,4},{5,7},{7,5},{8,10},{10,8},{9,1... | collective-permute-start | bytes 884744 | tf_op jit(solution)/shard_map/ppermute | solution.py:271
  74.6 5.2 %collective-permute-start.19 = (bf16[2,64,1152]{2,1,0:T(8,128)(2,1)S(1)}, bf16[2,64,1152]{2,1,0:T(8,128)(2,1)S(1)}, u32[]{:S(2)}, u32[]{:S(2)}) collective-permute-start(bf16[2,64,1152]{2,1,0:T(8,128)(2,1)S(1)} %collective-permute-done.15.refs_2_), channel_id=1, source_target_pairs={{0,2},{2,0},{1,3},{3,1},{4,6},{6,4},{5,7},{7,5},{8,10},{10,8},{9,1... | collective-permute-start | bytes 884744 | tf_op jit(solution)/shard_map/ppermute | solution.py:271
  76.3 4.1 %collective-permute-start.20 = (bf16[2,64,1152]{2,1,0:T(8,128)(2,1)S(1)}, bf16[2,64,1152]{2,1,0:T(8,128)(2,1)S(1)}, u32[]{:S(2)}, u32[]{:S(2)}) collective-permute-start(bf16[2,64,1152]{2,1,0:T(8,128)(2,1)S(1)} %collective-permute-done.16.refs_3_), channel_id=1, source_target_pairs={{0,2},{2,0},{1,3},{3,1},{4,6},{6,4},{5,7},{7,5},{8,10},{10,8},{9,1... | collective-permute-start | bytes 884744 | tf_op jit(solution)/shard_map/ppermute | solution.py:271
  79.7 0.7 copy-start.5
  80.5 0.7 copy-start.9
  81.2 1.0 copy-start.6
  82.2 1.0 copy-start.10
  85.8 0.7 copy-start.13
  86.6 28.6 %copy-start.16 = (bf16[1024,1024]{1,0:T(8,128)(2,1)S(1)}, bf16[1024,1024]{1,0:T(8,128)(2,1)}, u32[]{:S(2)}) copy-start(bf16[1024,1024]{1,0:T(8,128)(2,1)} %copy-done.15) | copy-start | bytes 6291460
  86.6 13.8 %all-to-all-start.2 = ((bf16[16,64,128]{2,1,0:T(8,128)(2,1)}), bf16[16,64,128]{2,1,0:T(8,128)(2,1)S(1)}, u32[]{:S(2)}, u32[]{:S(2)}) async-start(bf16[16,64,128]{2,1,0:T(8,128)(2,1)} %copy-done.13), calls=%async_computation.2 | async-start | bytes 524288 | tf_op jit(solution)/shard_map/all_to_all | solution.py:267
  93.9 11.7 %collective-permute-start.9 = (bf16[128,1024]{1,0:T(8,128)(2,1)}, bf16[128,1024]{1,0:T(8,128)(2,1)}, u32[]{:S(2)}, u32[]{:S(2)}) collective-permute-start(bf16[128,1024]{1,0:T(8,128)(2,1)} %get-tuple-element.39), channel_id=1, source_target_pairs={{0,16},{1,17},{2,18},{3,19},{4,20},{5,21},{6,22},{7,23},{8,24},{9,... | collective-permute-start | bytes 786440 | tf_op jit(solution)/shard_map/ppermute | solution.py:381
  98.9 16.2 %collective-permute-start.10 = (bf16[128,1024]{1,0:T(8,128)(2,1)}, bf16[128,1024]{1,0:T(8,128)(2,1)}, u32[]{:S(2)}, u32[]{:S(2)}) collective-permute-start(bf16[128,1024]{1,0:T(8,128)(2,1)} %get-tuple-element.38), channel_id=1, source_target_pairs={{16,0},{17,1},{18,2},{19,3},{20,4},{21,5},{22,6},{23,7},{24,8},{25... | collective-permute-start | bytes 786440 | tf_op jit(solution)/shard_map/ppermute | solution.py:382
  118.9 19.7 %all-to-all-start.3 = ((bf16[32,32,256]{2,1,0:T(8,128)(2,1)}), bf16[32,32,256]{2,1,0:T(8,128)(2,1)S(1)}, u32[]{:S(2)}, u32[]{:S(2)}) async-start(bf16[32,32,256]{2,1,0:T(8,128)(2,1)} %bitcast.20), calls=%async_computation.3 | async-start | bytes 1048576 | tf_op jit(solution)/shard_map/all_to_all | solution.py:267
  122.8 6.0 %collective-permute-start.21 = (f32[100,128]{1,0:T(8,128)S(1)}, f32[100,128]{1,0:T(8,128)S(1)}, u32[]{:S(2)}, u32[]{:S(2)}) collective-permute-start(f32[100,128]{1,0:T(8,128)S(1)} %get-tuple-element.32), channel_id=1, source_target_pairs={{0,1},{1,0},{2,3},{3,2},{4,5},{5,4},{6,7},{7,6},{8,9},{9,8},{10,11... | collective-permute-start | bytes 153608 | tf_op jit(solution)/shard_map/ppermute | solution.py:271
  (1 other events, 0.7 us)

commit v5 on v4

--- a/solution.py
+++ b/solution.py
@@ -35,35 +35,59 @@
 
 VMEM = pl.BlockSpec(memory_space=pltpu.VMEM)
 SMEM = pl.BlockSpec(memory_space=pltpu.SMEM)
+ANYWHERE = pl.BlockSpec(memory_space=pl.ANY)
 OVER_ROWS = (((0,), (0,)), ((), ()))
 OVER_COLUMNS = (((1,), (1,)), ((), ()))
 
 
-def call(kernel, name, outs, ins, scratch=(), flops=0, moved=0, exps=0, room=8):
+def call(kernel, name, outs, ins, scratch=(), flops=0, moved=0, exps=0, room=8, results=None):
+    spaces = {"s": SMEM, "v": VMEM, "a": ANYWHERE}
     return pl.pallas_call(
         kernel,
         out_shape=[jax.ShapeDtypeStruct(shape, kind) for shape, kind in outs],
-        in_specs=[SMEM if space == "s" else VMEM for space in ins],
-        out_specs=[VMEM] * len(outs),
-        scratch_shapes=[pltpu.VMEM(shape, kind) for shape, kind in scratch],
+        in_specs=[spaces[space] for space in ins],
+        out_specs=[spaces[space] for space in results or "v" * len(outs)],
+        scratch_shapes=list(scratch),
         compiler_params=pltpu.CompilerParams(vmem_limit_bytes=room * 2**20),
         cost_estimate=pl.CostEstimate(flops=flops, bytes_accessed=moved, transcendentals=exps),
         name=name,
     )
 
 
+def fetch(pairs, sems):
+    copies = [
+        pltpu.make_async_copy(source, target, sems.at[at]) for at, (source, target) in enumerate(pairs)
+    ]
+    for copy in copies:
+        copy.start()
+    return copies
+
+
 def prepare_kernel(
-    where_ref, source_ref, w_ref, mix_ref, readout_ref, near_ref, normed_ref, columns_ref, packed_ref
+    where_ref,
+    near_ref,
+    source_any,
+    w_any,
+    mix_any,
+    readout_any,
+    normed_ref,
+    columns_ref,
+    packed_ref,
+    source_ref,
+    w_ref,
+    readout_ref,
+    sems,
 ):
-    halves, _, members_num = columns_ref.shape[:3]
-    for g in range(GROUP):
-        chunk = jnp.concatenate(
-            [w_ref[:, (part * GROUP + g) * COLS : (part * GROUP + g + 1) * COLS] for part in range(3)],
-            axis=1,
-        )
-        for half in range(halves):
-            for m in range(members_num):
-                columns_ref[half, g, m] = chunk
+    copies = fetch(
+        [
+            (w_any, w_ref),
+            (source_any, source_ref),
+            (readout_any, readout_ref),
+            (mix_any, packed_ref.at[:, :LATENT_DIM]),
+        ],
+        sems,
+    )
+    copies[1].wait()
     rows = source_ref.shape[0]
     source = source_ref[...].astype(F32)
     inverse = lax.rsqrt(jnp.mean(source * source, axis=-1, keepdims=True) + NORM_EPS)
@@ -75,12 +99,23 @@
     for tile in range(near_ref.shape[0]):
         for slot in range(K_NB):
             at = near_ref[tile, slot]
-            step = jnp.where(at >= 0, at - where_ref[2] - tile, NOWHERE).astype(F32)
+            step = jnp.where(at >= 0, at - where_ref[3] - tile, NOWHERE).astype(F32)
             note = jnp.where((row == tile) & (lane == slot), step, note)
     normed_ref[rows:, :128] = note.astype(BF16)
-    packed_ref[:, :LATENT_DIM] = mix_ref[...]
+    copies[0].wait()
+    halves, _, members_num = columns_ref.shape[:3]
+    for g in range(GROUP):
+        chunk = jnp.concatenate(
+            [w_ref[:, (part * GROUP + g) * COLS : (part * GROUP + g + 1) * COLS] for part in range(3)],
+            axis=1,
+        )
+        for half in range(halves):
+            for m in range(members_num):
+                columns_ref[half, g, m] = chunk
+    copies[2].wait()
     packed_ref[:, LATENT_DIM:] = jnp.zeros((packed_ref.shape[0], FIELD_PAD), BF16)
     packed_ref[:, LATENT_DIM : LATENT_DIM + FIELD_NUM] = readout_ref[...]
+    copies[3].wait()
 
 
 def owners(where_ref):
@@ -89,18 +124,62 @@
 
 
 def project_kernel(where_ref, *refs):
-    blocks = refs[:GROUP]
-    w_ref, normed_ref, q_ref, kv_ref, steps_ref, first_ref, last_ref = refs[GROUP:]
+    blocks, refs = refs[:GROUP], refs[GROUP:]
+    columns, refs = refs[:-12], refs[-12:]
+    q_ref, kv_ref, steps_ref, first_ref, last_ref, first_n_ref, last_n_ref, normed_any = refs[:8]
+    notes, normed, w, sems = refs[8:]
     block = blocks[0].shape[0] - NOTE_ROWS
-    for rows_ref, owner in zip(blocks, owners(where_ref)):
-        at = pl.ds(pl.multiple_of(owner * block, block), block)
-        normed_ref[at, :] = rows_ref[:block, :]
-        steps_ref[owner] = rows_ref[block:, :128].astype(F32)
-    projected = jnp.dot(normed_ref[...], w_ref[...], preferred_element_type=F32).astype(BF16)
+    pairs = []
+    for at, (rows_ref, owner) in enumerate(zip(blocks, owners(where_ref))):
+        place = pl.ds(pl.multiple_of(owner * block, block), block)
+        pairs.append((rows_ref.at[:block], normed.at[place]))
+        pairs.append((rows_ref.at[block:, :128], notes.at[owner]))
+    if len(columns) == 1:
+        pairs.append((columns[0], w))
+    else:
+        for step, part in enumerate(columns):
+            count, shard, _ = part.shape
+            for at in range(count):
+                place = pl.multiple_of((at * 2 + (where_ref[2] ^ step)) * shard, shard)
+                pairs.append((part.at[at], w.at[pl.ds(place, shard)]))
+    copies = fetch(pairs, sems)
+    for copy in copies:
+        copy.wait()
+    keep = pltpu.make_async_copy(normed, normed_any, sems.at[0])
+    keep.start()
+    projected = jnp.dot(normed[...], w[...], preferred_element_type=F32).astype(BF16)
     q_ref[...] = projected[:, :COLS]
     kv_ref[...] = projected[:, COLS:]
+    last = GROUP * block - RIM
     first_ref[...] = projected[:RIM, COLS:]
-    last_ref[...] = projected[GROUP * block - RIM :, COLS:]
+    last_ref[...] = projected[last:, COLS:]
+    first_n_ref[...] = normed[:RIM, :]
+    last_n_ref[...] = normed[last:, :]
+    steps_ref[...] = notes[...].astype(F32)
+    keep.wait()
+
+
+def weights_kernel(where_ref, *refs):
+    pieces, (w_ref, sems) = refs[:-2], refs[-2:]
+    pairs = []
+    for piece, (first, stride, count, shift) in zip(pieces, placements(where_ref, pieces)):
+        halves, block = piece.shape[-3], piece.shape[-2]
+        for at in range(count):
+            for half in range(halves):
+                owner = (where_ref[1] ^ (first + at)) * CORES + (where_ref[0] ^ shift[0])
+                place = (half * GROUP + owner) * stride + shift[1]
+                source = piece.at[at, half] if len(piece.shape) == 4 else piece.at[half]
+                pairs.append((source, w_ref.at[pl.ds(pl.multiple_of(place, block), block)]))
+    for copy in fetch(pairs, sems):
+        copy.wait()
+
+
+def placements(where_ref, pieces):
+    block = pieces[0].shape[-2]
+    if len(pieces[0].shape) == 3:
+        return [(at % QUAD, block, 1, (at // QUAD, 0)) for at in range(len(pieces))]
+    ens = where_ref[2]
+    return [(0, 2 * block, QUAD, (at // 2, (ens ^ (at % 2)) * block)) for at in range(len(pieces))]
 
 
 def by_head(rows):
@@ -196,15 +275,8 @@
     return spread * lax.rsqrt(spread * spread + SOFT_WIDTH)
 
 
-def mix_kernel(where_ref, att_ref, source_ref, *refs):
-    pieces = refs[:GROUP]
-    truth_ref, factor_ref, pred_ref, grad_ref, w, a = refs[GROUP:]
-    halves, block, _ = pieces[0].shape
+def mix_kernel(att_ref, source_ref, w, truth_ref, factor_ref, pred_ref, grad_ref, a):
     members_num, part, _ = source_ref.shape
-    for piece, owner in zip(pieces, owners(where_ref)):
-        for half in range(halves):
-            at = pl.multiple_of((half * GROUP + owner) * block, block)
-            w[pl.ds(at, block), :] = piece[half]
     for g in range(GROUP):
         for m in range(members_num):
             a[m * part : (m + 1) * part, g * COLS : (g + 1) * COLS] = att_ref[g * members_num + m]
@@ -279,14 +351,10 @@
     return jnp.stack([jnp.where(first, mine, other), jnp.where(first, other, mine)], axis=at)
 
 
-def group_pieces(mine):
-    near = [mine] + [swap(mine, "quad", step) for step in range(1, QUAD)]
-    return near, [swap(piece, "core", 1) for piece in near]
-
-
 def body(members, w_attn, w_mix, readout_matrix, observed_truth, cell_surface_factor, neighbours):
     halves, members_num = lax.axis_size("half"), lax.axis_size("ens")
-    everyone = ("half", "quad", "core", "ens")
+    nodes = ("half", "quad", "core")
+    everyone = nodes + ("ens",)
     shard = w_attn.shape[0]
     node_rows = members.shape[1]
     rows = GROUP * node_rows
@@ -295,69 +363,93 @@
     down = [(target, source) for source, target in up]
     core, quad, ens = (lax.axis_index(axis) for axis in ("core", "quad", "ens"))
     first_tile = lax.axis_index(("half", "quad", "core")) * neighbours.shape[0]
-    where = jnp.stack([core, quad, first_tile]).astype(jnp.int32)
+    where = jnp.stack([core, quad, ens, first_tile]).astype(jnp.int32)
     width = LATENT_DIM + FIELD_PAD
+    paired = members_num == 2
+    copies = 1 if paired else members_num
 
     normed, columns, packed = call(
         prepare_kernel,
         "prepare",
         [
             ((node_rows + NOTE_ROWS, LATENT_DIM), BF16),
-            ((halves, GROUP, members_num, shard, 3 * COLS), BF16),
+            ((halves, GROUP, copies, shard, 3 * COLS), BF16),
             ((shard, width), BF16),
         ],
-        "svvvvs",
+        "ssaaaa",
+        [
+            pltpu.VMEM((node_rows, LATENT_DIM), BF16),
+            pltpu.VMEM(w_attn.shape, BF16),
+            pltpu.VMEM(readout_matrix.shape, BF16),
+            pltpu.SemaphoreType.DMA((4,)),
+        ],
         flops=2**20,
         moved=2**20,
-        room=10,
-    )(
-        where,
-        members.reshape(node_rows, LATENT_DIM),
-        w_attn,
-        w_mix,
-        readout_matrix,
-        neighbours,
-    )
-    columns = exchange(columns.reshape(-1, shard, 3 * COLS), everyone)
-    columns = columns.reshape(LATENT_DIM, 3 * COLS)
-    near, far = group_pieces(normed)
-    blocks = near + far
+    )(where, neighbours, members.reshape(node_rows, LATENT_DIM), w_attn, w_mix, readout_matrix)
 
     packed = in_order(packed, "half", 0)
-    packed = in_order(packed, "ens", 1).reshape(halves, members_num * shard, width)
-    packed, near[3] = lax.optimization_barrier((packed, near[3]))
-    mix_near, mix_far = group_pieces(packed)
+    near = [normed] + [swap(normed, "quad", step) for step in range(1, QUAD)]
+    if paired:
+        columns = exchange(columns.reshape(-1, shard, 3 * COLS), nodes)
+        columns = [columns, swap(columns, "ens", 1)]
+    else:
+        columns = [exchange(columns.reshape(-1, shard, 3 * COLS), everyone)]
+        columns = [columns[0].reshape(LATENT_DIM, 3 * COLS)]
+    far = [swap(piece, "core", 1) for piece in near]
 
     sources = members.reshape(members_num, part, LATENT_DIM)
-    if members_num == 2:
+    if paired:
         kept = lax.dynamic_index_in_dim(sources, ens, 0, keepdims=False)
         sent = swap(lax.dynamic_index_in_dim(sources, 1 - ens, 0, keepdims=False), "ens", 1)
         sources = jnp.stack([jnp.where(ens == 0, kept, sent), jnp.where(ens == 0, sent, kept)])
     else:
         sources = exchange(sources, "ens")
+
+    packed, near[3] = lax.optimization_barrier((packed, near[3]))
+    if paired:
+        pieces = jnp.stack([packed] + [swap(packed, "quad", step) for step in range(1, QUAD)])
+        pieces, columns[1] = lax.optimization_barrier((pieces, columns[1]))
+        pieces = [pieces, swap(pieces, "ens", 1)]
+    else:
+        packed = in_order(packed, "ens", 1).reshape(halves, members_num * shard, width)
+        pieces = [packed] + [swap(packed, "quad", step) for step in range(1, QUAD)]
+    pieces = pieces + [swap(piece, "core", 1) for piece in pieces]
+    columns[-1], sources = lax.optimization_barrier((columns[-1], sources))
+
     truth = lax.dynamic_slice_in_dim(observed_truth, ens * part, part, 1)
     truth = jnp.tile(jnp.pad(truth, ((0, FIELD_PAD - FIELD_NUM), (0, 0))), (1, members_num))
     factor = lax.dynamic_slice_in_dim(cell_surface_factor, ens * part, part, 0)
     factor = jnp.tile(factor[None], (1, members_num))
 
-    normed, queries, own, steps, first, last = call(
+    queries, own, steps, first, last, first_normed, last_normed, normed = call(
         project_kernel,
         "project",
         [
-            ((rows, LATENT_DIM), BF16),
             ((rows, COLS), BF16),
             ((rows, 2 * COLS), BF16),
             ((GROUP, NOTE_ROWS, 128), F32),
             ((RIM, 2 * COLS), BF16),
             ((RIM, 2 * COLS), BF16),
+            ((RIM, LATENT_DIM), BF16),
+            ((RIM, LATENT_DIM), BF16),
+            ((rows, LATENT_DIM), BF16),
         ],
-        "s" + "v" * (GROUP + 1),
+        "s" + "a" * (GROUP + len(columns)),
+        [
+            pltpu.VMEM((GROUP, NOTE_ROWS, 128), BF16),
+            pltpu.VMEM((rows, LATENT_DIM), BF16),
+            pltpu.VMEM((LATENT_DIM, 3 * COLS), BF16),
+            pltpu.SemaphoreType.DMA((2 * GROUP + (2 * GROUP * halves if paired else 1),)),
+        ],
         flops=rows * LATENT_DIM * 6 * COLS,
         moved=4 * 2**20,
         room=14,
-    )(where, *blocks, columns)
+        results="vvvvvvva",
+    )(where, *near, *far, *columns)
     low = lax.ppermute(last, "half", up)
     high = lax.ppermute(first, "half", down)
+    normed_low = lax.ppermute(last_normed, "half", up)
+    normed_high = lax.ppermute(first_normed, "half", down)
 
     (outcome,) = call(
         interior_kernel,
@@ -377,21 +469,27 @@
         moved=2**20,
         exps=rows * 128,
     )(steps, queries, own, low, high, outcome)
-    normed, outcome = lax.optimization_barrier((normed, outcome))
-    normed_low = lax.ppermute(normed[rows - RIM :], "half", up)
-    normed_high = lax.ppermute(normed[:RIM], "half", down)
     attended = exchange(outcome.reshape(GROUP * members_num, part, COLS), ("quad", "core", "ens"))
+    (weights,) = call(
+        weights_kernel,
+        "weights",
+        [((LATENT_DIM, width), BF16)],
+        "s" + "a" * len(pieces),
+        [pltpu.SemaphoreType.DMA((2 * GROUP * halves,))],
+        moved=4 * 2**20,
+    )(where, *pieces)
+    attended, normed_low, normed_high = lax.optimization_barrier((attended, normed_low, normed_high))
 
     prediction, grads = call(
         mix_kernel,
         "mix_loss_backward",
         [((FIELD_NUM, node_rows), F32), ((GROUP * members_num, part, COLS), BF16)],
-        "s" + "v" * (GROUP + 4),
-        [((LATENT_DIM, width), BF16), ((node_rows, LATENT_DIM), BF16)],
+        "vvvvv",
+        [pltpu.VMEM((node_rows, LATENT_DIM), BF16)],
         flops=node_rows * LATENT_DIM * 4 * width,
         moved=2**22,
         room=14,
-    )(where, attended, sources, *mix_near, *mix_far, truth, factor)
+    )(attended, sources, weights, truth, factor)
     grads = exchange(grads, ("quad", "core", "ens")).reshape(rows, COLS)
 
     (kv_grads,) = call(
@@ -399,7 +497,10 @@
         "attention_backward",
         [((rows + 2 * RIM, 4 * COLS), BF16)],
         "vvvvvv",
-        [((rows + 2 * RIM, 2 * COLS), BF16), ((rows + 2 * RIM, 2 * COLS), F32)],
+        [
+            pltpu.VMEM((rows + 2 * RIM, 2 * COLS), BF16),
+            pltpu.VMEM((rows + 2 * RIM, 2 * COLS), F32),
+        ],
         flops=rows * COLS * 5120,
         moved=2**22,
         exps=rows * 512,

time: 140 us -> 154 us (1.10)
  waiting for transfers between devices: 47.9 us -> 63 us
  blocking collectives: 0 us -> 11.9 us
  local copies, waits for them, and re-layouts: 18.3 us -> 8.96 us
  starting transfers between devices: 50 us -> 41.7 us
  Pallas kernels: 20.2 us -> 26.3 us
  other arithmetic: 1.96 us -> 0.36 us
    all_to_all x0 -> x1, blocking collectives: none -> 11.9 us  [exchange(): return lax.all_to_all(chunks, axes, 0, 0)]
    all_to_all x4 -> x3, starting transfers between devices: 20.2 us -> 11.5 us  [exchange(): return lax.all_to_all(chunks, axes, 0, 0)]
    ppermute x18 -> x17, waiting for transfers between devices: 27.9 us -> 35.6 us  [swap(): lax.ppermute(value, axis, [(i, i ^ step) for i in range(lax.axis_size(axi...]
    unnamed x48 -> x38, local copies, waits for them, and re-layouts: 15.4 us -> 8.52 us
    pallas_call x1 -> x2, Pallas kernels: 1.9 us -> 8.54 us  [the longest x1 4.65 us: body(): call(weights_kernel, 'weights', [((LATENT_DIM, width), BF16)], 's' + 'a'...]
    ppermute x2, waiting for transfers between devices: 9.58 us -> 14.4 us  [the longest x1 9.19 us: body(): normed_high = lax.ppermute(first_normed, 'half', down)]
    ppermute x18 -> x17, starting transfers between devices: 17.9 us -> 21.1 us  [swap(): lax.ppermute(value, axis, [(i, i ^ step) for i in range(lax.axis_size(axi...]
    ppermute x2, starting transfers between devices: 6.49 us -> 3.25 us  [the longest x1 1.97 us: body(): normed_low = lax.ppermute(last_normed, 'half', up)]
  transfers between devices with their start and end apart: 26 -> 24, of which waited for: 7 -> 12; matrix products, arithmetic and copies ran while one was open for 4% -> 1% of each run, Pallas kernels for 7% -> 5%
where the time goes in v5:
time: 154 us; the launch traced here: 153 us
  waiting for transfers between devices  63 us (41%)
  starting transfers between devices  41.7 us (27%)
  Pallas kernels  26.3 us (17%)
  blocking collectives  11.9 us (8%)
  local copies, waits for them, and re-layouts  8.96 us (6%)
    ppermute x17, waiting for transfers between devices, swap(): lax.ppermute(value, axis, [(i, i ^ step) for i in range(lax.axis_size(axi...  35.6 us
    ppermute x17, starting transfers between devices, swap(): lax.ppermute(value, axis, [(i, i ^ step) for i in range(lax.axis_size(axi...  21.1 us
    all_to_all x1, blocking collectives, exchange(): return lax.all_to_all(chunks, axes, 0, 0)  11.9 us
    all_to_all x3, starting transfers between devices, exchange(): return lax.all_to_all(chunks, axes, 0, 0)  11.5 us
    ppermute x1, waiting for transfers between devices, body(): normed_high = lax.ppermute(first_normed, 'half', down)  9.19 us
    all_to_all x3, waiting for transfers between devices, exchange(): return lax.all_to_all(chunks, axes, 0, 0)  9.09 us
    unnamed x38, local copies, waits for them, and re-layouts  8.52 us
    ppermute x1, waiting for transfers between devices, body(): normed_low = lax.ppermute(last_normed, 'half', up)  5.25 us
  transfers between devices with their start and end apart: 24, of which 12 were waited for; matrix products, arithmetic and copies ran while one was open for 1% of the time, Pallas kernels for 5%

profile of v5, /device:TPU:1, one launch (start us, length us, event | category | flops | bytes accessed | tf_op | source)
XLA Modules:
  0.0 153.2 jit_solution(590188543105567847)
XLA Ops:
  0.7 0.9 copy-done.1
  1.7 0.9 copy-done.9
  2.6 0.8 copy-done.10
  3.5 0.7 copy-done.11
  4.2 0.7 copy-done.12
  4.8 1.8 %prepare.1 = (bf16[144,1024]{1,0:T(8,128)(2,1)S(1)}, bf16[2,8,1,32,384]{4,3,2,1,0:T(8,128)(2,1)}, bf16[32,1152]{1,0:T(8,128)(2,1)S(1)}) custom-call(s32[4]{0:T(128)S(1)} %pad_add_fusion.where_ref, s32[2,4]{1,0:T(2,128)S(1)} %copy-done.12, bf16[128,1024]{1,0:T(8,128)(2,1)S(1)} %bitcast.37, bf16[32,3072]{1,0:T(8,128)(2,1)S(1)} %copy-done.9, ...), custom_call_target="tpu_custom_call" | custom-call | flops 1048576 | bytes 1048576 | tf_op jit(solution)/shard_map/prepare/pallas_call | solution.py:371
  6.7 3.2 %collective-permute-start.2 = (bf16[32,1152]{1,0:T(8,128)(2,1)S(1)}, bf16[32,1152]{1,0:T(8,128)(2,1)S(1)}, u32[]{:S(2)}, u32[]{:S(2)}) collective-permute-start(bf16[32,1152]{1,0:T(8,128)(2,1)S(1)} %get-tuple-element.27), channel_id=1, source_target_pairs={{0,16},{16,0},{1,17},{17,1},{2,18},{18,2},{3,19},{19,3},{4,20},{20... | collective-permute-start | bytes 221192 | tf_op jit(solution)/shard_map/ppermute | solution.py:343
  9.9 4.8 %all-to-all-start = ((bf16[16,32,384]{2,1,0:T(8,128)(2,1)}), bf16[16,32,384]{2,1,0:T(8,128)(2,1)S(1)}, u32[]{:S(2)}, u32[]{:S(2)}) async-start(bf16[16,32,384]{2,1,0:T(8,128)(2,1)} %bitcast.7), calls=%async_computation | async-start | bytes 786432 | tf_op jit(solution)/shard_map/all_to_all | solution.py:339
  14.6 2.3 %collective-permute-start.3 = (bf16[144,1024]{1,0:T(8,128)(2,1)S(1)}, bf16[144,1024]{1,0:T(8,128)(2,1)}, u32[]{:S(2)}, u32[]{:S(2)}) collective-permute-start(bf16[144,1024]{1,0:T(8,128)(2,1)S(1)} %get-tuple-element.26.refs_0_), channel_id=1, source_target_pairs={{0,12},{4,8},{8,4},{12,0},{1,13},{5,9},{9,5},{13,1},{2,14},{6,10},... | collective-permute-start | bytes 884744 | tf_op jit(solution)/shard_map/ppermute | solution.py:343
  17.0 13.7 %collective-permute-done.3.refs_3_ = bf16[144,1024]{1,0:T(8,128)(2,1)} collective-permute-done((bf16[144,1024]{1,0:T(8,128)(2,1)S(1)}, bf16[144,1024]{1,0:T(8,128)(2,1)}, u32[]{:S(2)}, u32[]{:S(2)}) %collective-permute-start.3) | collective-permute-done | bytes 294944 | tf_op jit(solution)/shard_map/ppermute | solution.py:343
  30.6 1.6 %collective-permute-start.10 = (bf16[2,32,1152]{2,1,0:T(8,128)(2,1)S(1)}, bf16[2,32,1152]{2,1,0:T(8,128)(2,1)S(1)}, u32[]{:S(2)}, u32[]{:S(2)}) collective-permute-start(bf16[2,32,1152]{2,1,0:T(8,128)(2,1)S(1)} %pad_maximum_fusion.2), channel_id=1, source_target_pairs={{0,12},{4,8},{8,4},{12,0},{1,13},{5,9},{9,5},{13,1},{2,14},{6,10},... | collective-permute-start | bytes 442376 | tf_op jit(solution)/shard_map/ppermute | solution.py:343
  32.2 1.1 collective-permute-start.8
  33.3 1.2 collective-permute-start.11
  34.9 1.1 collective-permute-done.10
  36.0 0.9 collective-permute-start.1
  36.9 1.4 collective-permute-done.9
  38.3 1.9 %collective-permute-done.8 = bf16[2,32,1152]{2,1,0:T(8,128)(2,1)S(1)} collective-permute-done((bf16[2,32,1152]{2,1,0:T(8,128)(2,1)S(1)}, bf16[2,32,1152]{2,1,0:T(8,128)(2,1)S(1)}, u32[]{:S(2)}, u32[]{:S(2)}) %collective-permute-start.8) | collective-permute-done | bytes 147488 | tf_op jit(solution)/shard_map/ppermute | solution.py:343
  40.3 2.0 %collective-permute-done.11.refs_9_ = bf16[16,32,384]{2,1,0:T(8,128)(2,1)S(1)} collective-permute-done((bf16[16,32,384]{2,1,0:T(8,128)(2,1)S(1)}, bf16[16,32,384]{2,1,0:T(8,128)(2,1)S(1)}, u32[]{:S(2)}, u32[]{:S(2)}) %collective-permute-start.11) | collective-permute-done | bytes 393248 | tf_op jit(solution)/shard_map/ppermute | solution.py:343
  42.3 1.2 collective-permute-start.17
  43.9 3.1 %collective-permute-start.4 = (bf16[144,1024]{1,0:T(8,128)(2,1)S(1)}, bf16[144,1024]{1,0:T(8,128)(2,1)S(1)}, u32[]{:S(2)}, u32[]{:S(2)}) collective-permute-start(bf16[144,1024]{1,0:T(8,128)(2,1)S(1)} %get-tuple-element.26.refs_0_), channel_id=1, source_target_pairs={{0,2},{2,0},{1,3},{3,1},{4,6},{6,4},{5,7},{7,5},{8,10},{10,8},{9,1... | collective-permute-start | bytes 884744 | tf_op jit(solution)/shard_map/ppermute | solution.py:343
  46.9 10.5 %collective-permute-done.12 = bf16[64,1024]{1,0:T(8,128)(2,1)S(1)} collective-permute-done((bf16[64,1024]{1,0:T(8,128)(2,1)S(1)}, bf16[64,1024]{1,0:T(8,128)(2,1)S(1)}, u32[]{:S(2)}, u32[]{:S(2)}) %collective-permute-start.12) | collective-permute-done | bytes 131104 | tf_op jit(solution)/shard_map/ppermute | solution.py:343
  57.4 3.5 %collective-permute-start.7 = (bf16[144,1024]{1,0:T(8,128)(2,1)}, bf16[144,1024]{1,0:T(8,128)(2,1)S(1)}, u32[]{:S(2)}, u32[]{:S(2)}) collective-permute-start(bf16[144,1024]{1,0:T(8,128)(2,1)} %collective-permute-done.3.refs_3_), channel_id=1, source_target_pairs={{0,2},{2,0},{1,3},{3,1},{4,6},{6,4},{5,7},{7,5},{8,10},{10,8},{9,1... | collective-permute-start | bytes 884744 | tf_op jit(solution)/shard_map/ppermute | solution.py:343
  61.5 0.7 copy-done.7
  63.1 1.0 copy-done.4
  64.1 1.0 copy-done.6
  65.1 1.0 copy-done.8
  66.1 3.9 %project.1 = (bf16[1024,128]{1,0:T(8,128)(2,1)S(1)}, bf16[1024,256]{1,0:T(8,128)(2,1)S(1)}, f32[8,16,128]{2,1,0:T(8,128)S(1)}, bf16[128,256]{1,0:T(8,128)(2,1)S(...) custom-call(s32[4]{0:T(128)S(1)} %pad_add_fusion.where_ref, ...), custom_call_target="tpu_custom_call" | custom-call | flops 805306368 | bytes 4194304 | tf_op jit(solution)/shard_map/project/pallas_call | solution.py:424
  70.0 4.5 %collective-permute-start.13 = (bf16[128,256]{1,0:T(8,128)(2,1)S(1)}, bf16[128,256]{1,0:T(8,128)(2,1)S(1)}, u32[]{:S(2)}, u32[]{:S(2)}) collective-permute-start(bf16[128,256]{1,0:T(8,128)(2,1)S(1)} %get-tuple-element.37), channel_id=1, source_target_pairs={{0,16},{1,17},{2,18},{3,19},{4,20},{5,21},{6,22},{7,23},{8,24},{9,... | collective-permute-start | bytes 196616 | tf_op jit(solution)/shard_map/ppermute | solution.py:449
  74.5 1.3 collective-permute-start.14
  75.8 2.6 %attention_interior.1.done_ref = bf16[1024,128]{1,0:T(8,128)(2,1)S(1)} custom-call(f32[8,16,128]{2,1,0:T(8,128)S(1)} %get-tuple-element.34.steps_ref, bf16[1024,128]{1,0:T(8,128)(2,1)S(1)} %get-tuple-element.35.q_ref, bf16[1024,256]{1,0:T(8,128)(2,1)S(1)} %get-tuple-element.36.kv_ref.own_ref), custom_call_target="tpu_custom_call" | custom-call | flops 268435456 | bytes 2097152 | tf_op jit(solution)/shard_map/attention_interior/pallas_call | solution.py:454
  78.4 3.9 %collective-permute-done.14.high_ref = bf16[128,256]{1,0:T(8,128)(2,1)S(1)} collective-permute-done((bf16[128,256]{1,0:T(8,128)(2,1)S(1)}, bf16[128,256]{1,0:T(8,128)(2,1)S(1)}, u32[]{:S(2)}, u32[]{:S(2)}) %collective-permute-start.14) | collective-permute-done | bytes 65568 | tf_op jit(solution)/shard_map/ppermute | solution.py:450
  82.4 1.7 %attention_edges.1 = bf16[1024,128]{1,0:T(8,128)(2,1)} custom-call(f32[8,16,128]{2,1,0:T(8,128)S(1)} %get-tuple-element.34.steps_ref, bf16[1024,128]{1,0:T(8,128)(2,1)S(1)} %get-tuple-element.35.q_ref, bf16[1024,256]{1,0:T(8,128)(2,1)S(1)} %get-tuple-element.36.kv_ref.own_ref, bf16[128,256]{1,0:T(8,128)(2,1)S(1)} %collective-permute-done.13.low_ref, ...), custom_call_target="tpu_custom_call" | custom-call | flops 67108864 | bytes 1048576 | tf_op jit(solution)/shard_map/attention_edges/pallas_call | solution.py:463
  84.0 4.2 %all-to-all-start.1 = ((bf16[16,64,128]{2,1,0:T(8,128)(2,1)}), bf16[16,64,128]{2,1,0:T(8,128)(2,1)S(1)}, u32[]{:S(2)}, u32[]{:S(2)}) async-start(bf16[16,64,128]{2,1,0:T(8,128)(2,1)} %bitcast.17), calls=%async_computation.1 | async-start | bytes 524288 | tf_op jit(solution)/shard_map/all_to_all | solution.py:339
  88.2 2.0 %collective-permute-start.15 = (bf16[128,1024]{1,0:T(8,128)(2,1)}, bf16[128,1024]{1,0:T(8,128)(2,1)}, u32[]{:S(2)}, u32[]{:S(2)}) collective-permute-start(bf16[128,1024]{1,0:T(8,128)(2,1)} %copy-done.16), channel_id=1, source_target_pairs={{0,16},{1,17},{2,18},{3,19},{4,20},{5,21},{6,22},{7,23},{8,24},{9,... | collective-permute-start | bytes 786440 | tf_op jit(solution)/shard_map/ppermute | solution.py:451
  90.2 1.3 collective-permute-start.16
  91.9 5.2 %collective-permute-done.15.low_ref = bf16[128,1024]{1,0:T(8,128)(2,1)} collective-permute-done((bf16[128,1024]{1,0:T(8,128)(2,1)}, bf16[128,1024]{1,0:T(8,128)(2,1)}, u32[]{:S(2)}, u32[]{:S(2)}) %collective-permute-start.15) | collective-permute-done | bytes 262176 | tf_op jit(solution)/shard_map/ppermute | solution.py:451
  97.2 9.2 %collective-permute-done.16.high_ref = bf16[128,1024]{1,0:T(8,128)(2,1)} collective-permute-done((bf16[128,1024]{1,0:T(8,128)(2,1)}, bf16[128,1024]{1,0:T(8,128)(2,1)}, u32[]{:S(2)}, u32[]{:S(2)}) %collective-permute-start.16) | collective-permute-done | bytes 262176 | tf_op jit(solution)/shard_map/ppermute | solution.py:452
  106.4 4.6 %weights.1.w = bf16[1024,1152]{1,0:T(8,128)(2,1)S(1)} custom-call(s32[4]{0:T(128)S(1)} %pad_add_fusion.where_ref, bf16[4,2,32,1152]{3,2,1,0:T(8,128)(2,1)S(1)} %pad_maximum_fusion.refs_0_, bf16[4,2,32,1152]{3,2,1,0:T(8,128)(2,1)S(1)} %collective-permute-done.17.refs_1_, bf16[4,2,32,1152]{3,2,1,0:T(8,128)(2,1)S(1)} %collective-permute-done.18.refs_2_, ...), custom_call_target="tpu_custom_call" | custom-call | bytes 4194304 | tf_op jit(solution)/shard_map/weights/pallas_call | solution.py:473
  111.0 2.0 %mix_loss_backward.1 = (f32[100,128]{1,0:T(8,128)S(1)}, bf16[16,64,128]{2,1,0:T(8,128)(2,1)S(1)}) custom-call(bf16[16,64,128]{2,1,0:T(8,128)(2,1)S(1)} %all-to-all-done.1.att_ref, bf16[2,64,1024]{2,1,0:T(8,128)(2,1)S(1)} %pad_maximum_fusion.1.source_ref, bf16[1024,1152]{1,0:T(8,128)(2,1)S(1)} %weights.1.w, f32[128,128]{1,0:T(8,128)S(1)} %copy.11.truth_ref, ...), custom_call_target="tpu_custom_call" | custom-call | flops 603979776 | bytes 4194304 | tf_op jit(solution)/shard_map/mix_loss_backward/pallas_call | solution.py:483
  113.1 11.9 %all_to_all.20 = bf16[16,64,128]{2,1,0:T(8,128)(2,1)S(1)} all-to-all(bf16[16,64,128]{2,1,0:T(8,128)(2,1)S(1)} %get-tuple-element.46), channel_id=1, replica_groups=mesh['half'=2,'quad'=4,'core'=2,'ens'=2] {'quad','core','ens'}, dimensions={0} | all-to-all | bytes 524288 | tf_op jit(solution)/shard_map/all_to_all | solution.py:339
  125.0 5.2 %attention_backward.1.kv_ref = bf16[1280,512]{1,0:T(8,128)(2,1)S(1)} custom-call(f32[8,16,128]{2,1,0:T(8,128)S(1)} %get-tuple-element.34.steps_ref, bf16[1024,128]{1,0:T(8,128)(2,1)S(1)} %get-tuple-element.35.q_ref, bf16[128,256]{1,0:T(8,128)(2,1)S(1)} %collective-permute-done.13.low_ref, bf16[1024,256]{1,0:T(8,128)(2,1)S(1)} %get-tuple-element.36.kv_ref.own_ref, ...), custom_call_target="tpu_custom_call" | custom-call | flops 671088640 | bytes 4194304 | tf_op jit(solution)/shard_map/attention_backward/pallas_call | solution.py:495
  130.2 3.7 %product.1 = bf16[1024,256]{1,0:T(8,128)(2,1)} custom-call(bf16[1024,1024]{1,0:T(8,128)(2,1)S(1)} %copy-done.14, bf16[128,1024]{1,0:T(8,128)(2,1)} %collective-permute-done.15.low_ref, bf16[128,1024]{1,0:T(8,128)(2,1)} %collective-permute-done.16.high_ref, bf16[1280,512]{1,0:T(8,128)(2,1)S(1)} %attention_backward.1.kv_ref), custom_call_target="tpu_custom_call" | custom-call | flops 1342177280 | bytes 4194304 | tf_op jit(solution)/shard_map/product/pallas_call | solution.py:509
  133.9 2.6 %all-to-all-start.3 = ((bf16[32,32,256]{2,1,0:T(8,128)(2,1)}), bf16[32,32,256]{2,1,0:T(8,128)(2,1)S(1)}, u32[]{:S(2)}, u32[]{:S(2)}) async-start(bf16[32,32,256]{2,1,0:T(8,128)(2,1)} %bitcast.21), calls=%async_computation.3 | async-start | bytes 1048576 | tf_op jit(solution)/shard_map/all_to_all | solution.py:339
  136.5 1.5 collective-permute-start.20
  138.0 4.5 %collective-permute-done.20 = f32[100,128]{1,0:T(8,128)S(1)} collective-permute-done((f32[100,128]{1,0:T(8,128)S(1)}, f32[100,128]{1,0:T(8,128)S(1)}, u32[]{:S(2)}, u32[]{:S(2)}) %collective-permute-start.20) | collective-permute-done | bytes 51232 | tf_op jit(solution)/shard_map/ppermute | solution.py:343
  142.7 0.7 copy.12
  143.4 9.1 %all-to-all-done.3 = bf16[32,32,256]{2,1,0:T(8,128)(2,1)S(1)} async-done(((bf16[32,32,256]{2,1,0:T(8,128)(2,1)}), bf16[32,32,256]{2,1,0:T(8,128)(2,1)S(1)}, u32[]{:S(2)}, u32[]{:S(2)}) %all-to-all-start.3) | async-done | bytes 524320 | tf_op jit(solution)/shard_map/all_to_all | solution.py:339
  152.4 0.8 gather_sums.1
  (66 shorter events, 3.1 us)
Async XLA Ops:
  0.6 90.8 %copy-start = (f32[100,128]{1,0:T(8,128)S(1)}, f32[100,128]{1,0:T(8,128)}, u32[]{:S(2)}) copy-start(f32[100,128]{1,0:T(8,128)} %param.11) | copy-start | bytes 153604
  0.7 1.0 copy-start.1
  1.7 0.9 copy-start.9
  2.6 0.8 copy-start.10
  3.5 0.7 copy-start.11
  4.2 0.7 copy-start.12
  4.8 38.7 %copy-start.2 = (bf16[1,128,1024]{2,1,0:T(8,128)(2,1)S(1)}, bf16[1,128,1024]{2,1,0:T(8,128)(2,1)}, u32[]{:S(2)}) copy-start(bf16[1,128,1024]{2,1,0:T(8,128)(2,1)} %param.7) | copy-start | bytes 786436
  6.7 54.8 %copy-start.5 = (bf16[144,1024]{1,0:T(8,128)(2,1)}, bf16[144,1024]{1,0:T(8,128)(2,1)S(1)}, u32[]{:S(2)}) copy-start(bf16[144,1024]{1,0:T(8,128)(2,1)S(1)} %get-tuple-element.26.refs_0_) | copy-start | bytes 884740
  6.7 10.3 %collective-permute-start.2 = (bf16[32,1152]{1,0:T(8,128)(2,1)S(1)}, bf16[32,1152]{1,0:T(8,128)(2,1)S(1)}, u32[]{:S(2)}, u32[]{:S(2)}) collective-permute-start(bf16[32,1152]{1,0:T(8,128)(2,1)S(1)} %get-tuple-element.27), channel_id=1, source_target_pairs={{0,16},{16,0},{1,17},{17,1},{2,18},{18,2},{3,19},{19,3},{4,20},{20... | collective-permute-start | bytes 221192 | tf_op jit(solution)/shard_map/ppermute | solution.py:343
  9.9 23.4 %all-to-all-start = ((bf16[16,32,384]{2,1,0:T(8,128)(2,1)}), bf16[16,32,384]{2,1,0:T(8,128)(2,1)S(1)}, u32[]{:S(2)}, u32[]{:S(2)}) async-start(bf16[16,32,384]{2,1,0:T(8,128)(2,1)} %bitcast.7), calls=%async_computation | async-start | bytes 786432 | tf_op jit(solution)/shard_map/all_to_all | solution.py:339
  14.6 16.0 %collective-permute-start.3 = (bf16[144,1024]{1,0:T(8,128)(2,1)S(1)}, bf16[144,1024]{1,0:T(8,128)(2,1)}, u32[]{:S(2)}, u32[]{:S(2)}) collective-permute-start(bf16[144,1024]{1,0:T(8,128)(2,1)S(1)} %get-tuple-element.26.refs_0_), channel_id=1, source_target_pairs={{0,12},{4,8},{8,4},{12,0},{1,13},{5,9},{9,5},{13,1},{2,14},{6,10},... | collective-permute-start | bytes 884744 | tf_op jit(solution)/shard_map/ppermute | solution.py:343
  30.6 5.4 %collective-permute-start.10 = (bf16[2,32,1152]{2,1,0:T(8,128)(2,1)S(1)}, bf16[2,32,1152]{2,1,0:T(8,128)(2,1)S(1)}, u32[]{:S(2)}, u32[]{:S(2)}) collective-permute-start(bf16[2,32,1152]{2,1,0:T(8,128)(2,1)S(1)} %pad_maximum_fusion.2), channel_id=1, source_target_pairs={{0,12},{4,8},{8,4},{12,0},{1,13},{5,9},{9,5},{13,1},{2,14},{6,10},... | collective-permute-start | bytes 442376 | tf_op jit(solution)/shard_map/ppermute | solution.py:343
  32.2 6.1 %collective-permute-start.9 = (bf16[2,32,1152]{2,1,0:T(8,128)(2,1)S(1)}, bf16[2,32,1152]{2,1,0:T(8,128)(2,1)S(1)}, u32[]{:S(2)}, u32[]{:S(2)}) collective-permute-start(bf16[2,32,1152]{2,1,0:T(8,128)(2,1)S(1)} %pad_maximum_fusion.2), channel_id=1, source_target_pairs={{0,8},{4,12},{8,0},{12,4},{1,9},{5,13},{9,1},{13,5},{2,10},{6,14},... | collective-permute-start | bytes 442376 | tf_op jit(solution)/shard_map/ppermute | solution.py:343
  32.2 8.0 %collective-permute-start.8 = (bf16[2,32,1152]{2,1,0:T(8,128)(2,1)S(1)}, bf16[2,32,1152]{2,1,0:T(8,128)(2,1)S(1)}, u32[]{:S(2)}, u32[]{:S(2)}) collective-permute-start(bf16[2,32,1152]{2,1,0:T(8,128)(2,1)S(1)} %pad_maximum_fusion.2), channel_id=1, source_target_pairs={{0,4},{4,0},{8,12},{12,8},{1,5},{5,1},{9,13},{13,9},{2,6},{6,2},{1... | collective-permute-start | bytes 442376 | tf_op jit(solution)/shard_map/ppermute | solution.py:343
  33.3 9.0 %collective-permute-start.11 = (bf16[16,32,384]{2,1,0:T(8,128)(2,1)S(1)}, bf16[16,32,384]{2,1,0:T(8,128)(2,1)S(1)}, u32[]{:S(2)}, u32[]{:S(2)}) collective-permute-start(bf16[16,32,384]{2,1,0:T(8,128)(2,1)S(1)} %all-to-all-done.refs_8_), channel_id=1, source_target_pairs={{0,1},{1,0},{2,3},{3,2},{4,5},{5,4},{6,7},{7,6},{8,9},{9,8},{10,11... | collective-permute-start | bytes 1179656 | tf_op jit(solution)/shard_map/ppermute | solution.py:343
  34.5 26.3 %collective-permute-start = (bf16[144,1024]{1,0:T(8,128)(2,1)S(1)}, bf16[144,1024]{1,0:T(8,128)(2,1)}, u32[]{:S(2)}, u32[]{:S(2)}) collective-permute-start(bf16[144,1024]{1,0:T(8,128)(2,1)S(1)} %get-tuple-element.26.refs_0_), channel_id=1, source_target_pairs={{0,4},{4,0},{8,12},{12,8},{1,5},{5,1},{9,13},{13,9},{2,6},{6,2},{1... | collective-permute-start | bytes 884744 | tf_op jit(solution)/shard_map/ppermute | solution.py:343
  36.0 24.8 %collective-permute-start.1 = (bf16[144,1024]{1,0:T(8,128)(2,1)S(1)}, bf16[144,1024]{1,0:T(8,128)(2,1)}, u32[]{:S(2)}, u32[]{:S(2)}) collective-permute-start(bf16[144,1024]{1,0:T(8,128)(2,1)S(1)} %get-tuple-element.26.refs_0_), channel_id=1, source_target_pairs={{0,8},{4,12},{8,0},{12,4},{1,9},{5,13},{9,1},{13,5},{2,10},{6,14},... | collective-permute-start | bytes 884744 | tf_op jit(solution)/shard_map/ppermute | solution.py:343
  42.3 20.8 %copy-start.3 = (bf16[16,32,384]{2,1,0:T(8,128)(2,1)}, bf16[16,32,384]{2,1,0:T(8,128)(2,1)S(1)}, u32[]{:S(2)}) copy-start(bf16[16,32,384]{2,1,0:T(8,128)(2,1)S(1)} %collective-permute-done.11.refs_9_) | copy-start | bytes 1179652
  42.3 19.9 %collective-permute-start.17 = (bf16[4,2,32,1152]{3,2,1,0:T(8,128)(2,1)S(1)}, bf16[4,2,32,1152]{3,2,1,0:T(8,128)(2,1)S(1)}, u32[]{:S(2)}, u32[]{:S(2)}) collective-permute-start(bf16[4,2,32,1152]{3,2,1,0:T(8,128)(2,1)S(1)} %pad_maximum_fusion.refs_0_), channel_id=1, source_target_pairs={{0,1},{1,0},{2,3},{3,2},{4,5},{5,4},{6,7},{7,6},{8,9},{9,8},{10,11... | collective-permute-start | bytes 1769480 | tf_op jit(solution)/shard_map/ppermute | solution.py:343
  43.5 13.9 %collective-permute-start.12 = (bf16[64,1024]{1,0:T(8,128)(2,1)S(1)}, bf16[64,1024]{1,0:T(8,128)(2,1)S(1)}, u32[]{:S(2)}, u32[]{:S(2)}) collective-permute-start(bf16[64,1024]{1,0:T(8,128)(2,1)S(1)} %dynamic-slice_bitcast_fusion), channel_id=1, source_target_pairs={{0,1},{1,0},{2,3},{3,2},{4,5},{5,4},{6,7},{7,6},{8,9},{9,8},{10,11... | collective-permute-start | bytes 393224 | tf_op jit(solution)/shard_map/ppermute | solution.py:343
  43.9 17.6 %collective-permute-start.4 = (bf16[144,1024]{1,0:T(8,128)(2,1)S(1)}, bf16[144,1024]{1,0:T(8,128)(2,1)S(1)}, u32[]{:S(2)}, u32[]{:S(2)}) collective-permute-start(bf16[144,1024]{1,0:T(8,128)(2,1)S(1)} %get-tuple-element.26.refs_0_), channel_id=1, source_target_pairs={{0,2},{2,0},{1,3},{3,1},{4,6},{6,4},{5,7},{7,5},{8,10},{10,8},{9,1... | collective-permute-start | bytes 884744 | tf_op jit(solution)/shard_map/ppermute | solution.py:343
  57.4 5.7 %collective-permute-start.7 = (bf16[144,1024]{1,0:T(8,128)(2,1)}, bf16[144,1024]{1,0:T(8,128)(2,1)S(1)}, u32[]{:S(2)}, u32[]{:S(2)}) collective-permute-start(bf16[144,1024]{1,0:T(8,128)(2,1)} %collective-permute-done.3.refs_3_), channel_id=1, source_target_pairs={{0,2},{2,0},{1,3},{3,1},{4,6},{6,4},{5,7},{7,5},{8,10},{10,8},{9,1... | collective-permute-start | bytes 884744 | tf_op jit(solution)/shard_map/ppermute | solution.py:343
  60.9 1.8 %collective-permute-start.5 = (bf16[144,1024]{1,0:T(8,128)(2,1)}, bf16[144,1024]{1,0:T(8,128)(2,1)S(1)}, u32[]{:S(2)}, u32[]{:S(2)}) collective-permute-start(bf16[144,1024]{1,0:T(8,128)(2,1)} %collective-permute-done.refs_1_), channel_id=1, source_target_pairs={{0,2},{2,0},{1,3},{3,1},{4,6},{6,4},{5,7},{7,5},{8,10},{10,8},{9,1... | collective-permute-start | bytes 884744 | tf_op jit(solution)/shard_map/ppermute | solution.py:343
  60.9 2.3 %collective-permute-start.6 = (bf16[144,1024]{1,0:T(8,128)(2,1)}, bf16[144,1024]{1,0:T(8,128)(2,1)S(1)}, u32[]{:S(2)}, u32[]{:S(2)}) collective-permute-start(bf16[144,1024]{1,0:T(8,128)(2,1)} %collective-permute-done.1.refs_2_), channel_id=1, source_target_pairs={{0,2},{2,0},{1,3},{3,1},{4,6},{6,4},{5,7},{7,5},{8,10},{10,8},{9,1... | collective-permute-start | bytes 884744 | tf_op jit(solution)/shard_map/ppermute | solution.py:343
  61.5 0.7 copy-start.7
  62.2 44.2 %collective-permute-start.18 = (bf16[4,2,32,1152]{3,2,1,0:T(8,128)(2,1)S(1)}, bf16[4,2,32,1152]{3,2,1,0:T(8,128)(2,1)S(1)}, u32[]{:S(2)}, u32[]{:S(2)}) collective-permute-start(bf16[4,2,32,1152]{3,2,1,0:T(8,128)(2,1)S(1)} %pad_maximum_fusion.refs_0_), channel_id=1, source_target_pairs={{0,2},{2,0},{1,3},{3,1},{4,6},{6,4},{5,7},{7,5},{8,10},{10,8},{9,1... | collective-permute-start | bytes 1769480 | tf_op jit(solution)/shard_map/ppermute | solution.py:343
  62.3 44.1 %collective-permute-start.19 = (bf16[4,2,32,1152]{3,2,1,0:T(8,128)(2,1)S(1)}, bf16[4,2,32,1152]{3,2,1,0:T(8,128)(2,1)}, u32[]{:S(2)}, u32[]{:S(2)}) collective-permute-start(bf16[4,2,32,1152]{3,2,1,0:T(8,128)(2,1)S(1)} %collective-permute-done.17.refs_1_), channel_id=1, source_target_pairs={{0,2},{2,0},{1,3},{3,1},{4,6},{6,4},{5,7},{7,5},{8,10},{10,8},{9,1... | collective-permute-start | bytes 1769480 | tf_op jit(solution)/shard_map/ppermute | solution.py:343
  63.1 1.0 copy-start.4
  64.1 1.0 copy-start.6
  65.1 1.0 copy-start.8
  70.0 14.1 %copy-start.13 = (bf16[1024,1024]{1,0:T(8,128)(2,1)}, bf16[1024,1024]{1,0:T(8,128)(2,1)S(1)}, u32[]{:S(2)}) copy-start(bf16[1024,1024]{1,0:T(8,128)(2,1)S(1)} %get-tuple-element.33.normed_ref) | copy-start | bytes 6291460
  70.0 14.1 %copy-start.15 = (bf16[128,1024]{1,0:T(8,128)(2,1)}, bf16[128,1024]{1,0:T(8,128)(2,1)S(1)}, u32[]{:S(2)}) copy-start(bf16[128,1024]{1,0:T(8,128)(2,1)S(1)} %get-tuple-element.40) | copy-start | bytes 786436
  70.0 14.1 %copy-start.16 = (bf16[128,1024]{1,0:T(8,128)(2,1)}, bf16[128,1024]{1,0:T(8,128)(2,1)S(1)}, u32[]{:S(2)}) copy-start(bf16[128,1024]{1,0:T(8,128)(2,1)S(1)} %get-tuple-element.39) | copy-start | bytes 786436
  70.0 21.8 %copy-start.17 = (f32[128]{0:T(128)S(1)}, f32[128]{0:T(128)}, u32[]{:S(2)}) copy-start(f32[128]{0:T(128)} %param.12) | copy-start | bytes 1540
  70.0 8.4 %collective-permute-start.13 = (bf16[128,256]{1,0:T(8,128)(2,1)S(1)}, bf16[128,256]{1,0:T(8,128)(2,1)S(1)}, u32[]{:S(2)}, u32[]{:S(2)}) collective-permute-start(bf16[128,256]{1,0:T(8,128)(2,1)S(1)} %get-tuple-element.37), channel_id=1, source_target_pairs={{0,16},{1,17},{2,18},{3,19},{4,20},{5,21},{6,22},{7,23},{8,24},{9,... | collective-permute-start | bytes 196616 | tf_op jit(solution)/shard_map/ppermute | solution.py:449
  74.5 7.8 %collective-permute-start.14 = (bf16[128,256]{1,0:T(8,128)(2,1)S(1)}, bf16[128,256]{1,0:T(8,128)(2,1)S(1)}, u32[]{:S(2)}, u32[]{:S(2)}) collective-permute-start(bf16[128,256]{1,0:T(8,128)(2,1)S(1)} %get-tuple-element.38), channel_id=1, source_target_pairs={{16,0},{17,1},{18,2},{19,3},{20,4},{21,5},{22,6},{23,7},{24,8},{25... | collective-permute-start | bytes 196616 | tf_op jit(solution)/shard_map/ppermute | solution.py:450
  84.0 22.3 %all-to-all-start.1 = ((bf16[16,64,128]{2,1,0:T(8,128)(2,1)}), bf16[16,64,128]{2,1,0:T(8,128)(2,1)S(1)}, u32[]{:S(2)}, u32[]{:S(2)}) async-start(bf16[16,64,128]{2,1,0:T(8,128)(2,1)} %bitcast.17), calls=%async_computation.1 | async-start | bytes 524288 | tf_op jit(solution)/shard_map/all_to_all | solution.py:339
  88.2 9.0 %collective-permute-start.15 = (bf16[128,1024]{1,0:T(8,128)(2,1)}, bf16[128,1024]{1,0:T(8,128)(2,1)}, u32[]{:S(2)}, u32[]{:S(2)}) collective-permute-start(bf16[128,1024]{1,0:T(8,128)(2,1)} %copy-done.16), channel_id=1, source_target_pairs={{0,16},{1,17},{2,18},{3,19},{4,20},{5,21},{6,22},{7,23},{8,24},{9,... | collective-permute-start | bytes 786440 | tf_op jit(solution)/shard_map/ppermute | solution.py:451
  90.2 16.2 %collective-permute-start.16 = (bf16[128,1024]{1,0:T(8,128)(2,1)}, bf16[128,1024]{1,0:T(8,128)(2,1)}, u32[]{:S(2)}, u32[]{:S(2)}) collective-permute-start(bf16[128,1024]{1,0:T(8,128)(2,1)} %copy-done.15), channel_id=1, source_target_pairs={{16,0},{17,1},{18,2},{19,3},{20,4},{21,5},{22,6},{23,7},{24,8},{25... | collective-permute-start | bytes 786440 | tf_op jit(solution)/shard_map/ppermute | solution.py:452
  113.1 17.1 %copy-start.14 = (bf16[1024,1024]{1,0:T(8,128)(2,1)S(1)}, bf16[1024,1024]{1,0:T(8,128)(2,1)}, u32[]{:S(2)}) copy-start(bf16[1024,1024]{1,0:T(8,128)(2,1)} %copy-done.13) | copy-start | bytes 6291460
  133.9 18.6 %all-to-all-start.3 = ((bf16[32,32,256]{2,1,0:T(8,128)(2,1)}), bf16[32,32,256]{2,1,0:T(8,128)(2,1)S(1)}, u32[]{:S(2)}, u32[]{:S(2)}) async-start(bf16[32,32,256]{2,1,0:T(8,128)(2,1)} %bitcast.21), calls=%async_computation.3 | async-start | bytes 1048576 | tf_op jit(solution)/shard_map/all_to_all | solution.py:339
  136.5 6.0 %collective-permute-start.20 = (f32[100,128]{1,0:T(8,128)S(1)}, f32[100,128]{1,0:T(8,128)S(1)}, u32[]{:S(2)}, u32[]{:S(2)}) collective-permute-start(f32[100,128]{1,0:T(8,128)S(1)} %get-tuple-element.48), channel_id=1, source_target_pairs={{0,1},{1,0},{2,3},{3,2},{4,5},{5,4},{6,7},{7,6},{8,9},{9,8},{10,11... | collective-permute-start | bytes 153608 | tf_op jit(solution)/shard_map/ppermute | solution.py:343

commit v6 on v5

--- a/solution.py
+++ b/solution.py
@@ -35,7 +35,7 @@
 
 VMEM = pl.BlockSpec(memory_space=pltpu.VMEM)
 SMEM = pl.BlockSpec(memory_space=pltpu.SMEM)
-ANYWHERE = pl.BlockSpec(memory_space=pl.ANY)
+ANYWHERE = pl.BlockSpec(memory_space=pltpu.HBM)
 OVER_ROWS = (((0,), (0,)), ((), ()))
 OVER_COLUMNS = (((1,), (1,)), ((), ()))
 
@@ -73,11 +73,9 @@
     normed_ref,
     columns_ref,
     packed_ref,
-    source_ref,
-    w_ref,
-    readout_ref,
-    sems,
+    *refs,
 ):
+    parts, (source_ref, w_ref, readout_ref, sems) = refs[:-4], refs[-4:]
     copies = fetch(
         [
             (w_any, w_ref),
@@ -92,6 +90,13 @@
     source = source_ref[...].astype(F32)
     inverse = lax.rsqrt(jnp.mean(source * source, axis=-1, keepdims=True) + NORM_EPS)
     normed_ref[:rows, :] = (source * inverse).astype(BF16)
+    if len(parts) == 1:
+        parts[0][...] = source_ref[...].reshape(parts[0].shape)
+    else:
+        for step, part_ref in enumerate(parts):
+            part = part_ref.shape[1]
+            place = pl.multiple_of((where_ref[2] ^ step) * part, part)
+            part_ref[0] = source_ref[pl.ds(place, part), :]
     normed_ref[rows:, :] = jnp.zeros((NOTE_ROWS, LATENT_DIM), BF16)
     row = lax.broadcasted_iota(jnp.int32, (NOTE_ROWS, 128), 0)
     lane = lax.broadcasted_iota(jnp.int32, (NOTE_ROWS, 128), 1)
@@ -125,9 +130,9 @@
 
 def project_kernel(where_ref, *refs):
     blocks, refs = refs[:GROUP], refs[GROUP:]
-    columns, refs = refs[:-12], refs[-12:]
-    q_ref, kv_ref, steps_ref, first_ref, last_ref, first_n_ref, last_n_ref, normed_any = refs[:8]
-    notes, normed, w, sems = refs[8:]
+    columns, refs = refs[:-10], refs[-10:]
+    q_ref, kv_ref, steps_ref, first_ref, last_ref, normed_any = refs[:6]
+    notes, normed, w, sems = refs[6:]
     block = blocks[0].shape[0] - NOTE_ROWS
     pairs = []
     for at, (rows_ref, owner) in enumerate(zip(blocks, owners(where_ref))):
@@ -138,48 +143,38 @@
         pairs.append((columns[0], w))
     else:
         for step, part in enumerate(columns):
-            count, shard, _ = part.shape
-            for at in range(count):
-                place = pl.multiple_of((at * 2 + (where_ref[2] ^ step)) * shard, shard)
-                pairs.append((part.at[at], w.at[pl.ds(place, shard)]))
+            pairs.append((part, w.at[:, where_ref[2] ^ step]))
     copies = fetch(pairs, sems)
     for copy in copies:
         copy.wait()
     keep = pltpu.make_async_copy(normed, normed_any, sems.at[0])
     keep.start()
-    projected = jnp.dot(normed[...], w[...], preferred_element_type=F32).astype(BF16)
+    weights = w[...].reshape(LATENT_DIM, 3 * COLS)
+    projected = jnp.dot(normed[...], weights, preferred_element_type=F32).astype(BF16)
     q_ref[...] = projected[:, :COLS]
     kv_ref[...] = projected[:, COLS:]
     last = GROUP * block - RIM
     first_ref[...] = projected[:RIM, COLS:]
     last_ref[...] = projected[last:, COLS:]
-    first_n_ref[...] = normed[:RIM, :]
-    last_n_ref[...] = normed[last:, :]
     steps_ref[...] = notes[...].astype(F32)
     keep.wait()
 
 
 def weights_kernel(where_ref, *refs):
     pieces, (w_ref, sems) = refs[:-2], refs[-2:]
+    core, quad, ens = where_ref[0], where_ref[1], where_ref[2]
     pairs = []
-    for piece, (first, stride, count, shift) in zip(pieces, placements(where_ref, pieces)):
-        halves, block = piece.shape[-3], piece.shape[-2]
-        for at in range(count):
-            for half in range(halves):
-                owner = (where_ref[1] ^ (first + at)) * CORES + (where_ref[0] ^ shift[0])
-                place = (half * GROUP + owner) * stride + shift[1]
-                source = piece.at[at, half] if len(piece.shape) == 4 else piece.at[half]
-                pairs.append((source, w_ref.at[pl.ds(pl.multiple_of(place, block), block)]))
+    if len(pieces) == GROUP:
+        for at, piece in enumerate(pieces):
+            place = (quad ^ (at % QUAD), core ^ (at // QUAD))
+            pairs.append((piece, w_ref.at[:, place[0], place[1], 0]))
+    else:
+        for at, piece in enumerate(pieces):
+            for step in range(QUAD):
+                place = (quad ^ step, core ^ (at // 2), ens ^ (at % 2))
+                pairs.append((piece.at[step], w_ref.at[:, place[0], place[1], place[2]]))
     for copy in fetch(pairs, sems):
         copy.wait()
-
-
-def placements(where_ref, pieces):
-    block = pieces[0].shape[-2]
-    if len(pieces[0].shape) == 3:
-        return [(at % QUAD, block, 1, (at // QUAD, 0)) for at in range(len(pieces))]
-    ens = where_ref[2]
-    return [(0, 2 * block, QUAD, (at // 2, (ens ^ (at % 2)) * block)) for at in range(len(pieces))]
 
 
 def by_head(rows):
@@ -243,47 +238,102 @@
         )
 
 
-def backward_kernel(steps_ref, q_ref, low_ref, own_ref, high_ref, g_ref, out_ref, kv, total):
+def attend_back(steps_ref, pair, queries, grads, keys, values):
+    queries, grads = by_head(queries), by_head(grads)
+    probs = probabilities(queries, keys, usable_keys(steps_ref, pair))
+    grad_probs = lax.dot_general(grads, values, OVER_COLUMNS, preferred_element_type=F32)
+    row_delta = jnp.sum(probs * grad_probs, axis=-1, keepdims=True)
+    grad_scores = (probs * (grad_probs - row_delta) * (HEAD**-0.5)).astype(BF16)
+    key_grad = lax.dot_general(grad_scores, queries, OVER_ROWS, preferred_element_type=F32)
+    value_grad = lax.dot_general(probs.astype(BF16), grads, OVER_ROWS, preferred_element_type=F32)
+    return key_grad, value_grad
+
+
+def edge_back_kernel(
+    steps_ref, q_ref, kv_ref, low_ref, high_ref, g_ref, rim_low_ref, rim_high_ref, part_ref
+):
+    step = PAIR * TILE
     count = q_ref.shape[0]
+    first = jnp.concatenate([low_ref[...], kv_ref[: 2 * step, :]], axis=0)
+    last = jnp.concatenate([kv_ref[count - 2 * step :, :], high_ref[...]], axis=0)
+    pairs = count // step
+    for edge, pair, window, rim_ref in ((0, 0, first, rim_low_ref), (1, pairs - 1, last, rim_high_ref)):
+        rows = slice(pair * step, (pair + 1) * step)
+        grads = attend_back(
+            steps_ref, pair, q_ref[rows, :], g_ref[rows, :], window[:, :COLS], window[:, COLS:]
+        )
+        rim = slice(0, RIM) if edge == 0 else slice(WINDOW - RIM, WINDOW)
+        own = slice(RIM, WINDOW) if edge == 0 else slice(0, WINDOW - RIM)
+        for at, grad in enumerate(grads):
+            columns = slice(at * COLS, (at + 1) * COLS)
+            rim_ref[:, columns] = grad[rim].astype(BF16)
+            part_ref[edge, :, columns] = grad[own]
+
+
+def interior_back_kernel(steps_ref, q_ref, kv_ref, g_ref, part_ref, out_ref):
     step = PAIR * TILE
-    kv[0:RIM, :] = low_ref[...]
-    kv[RIM : RIM + count, :] = own_ref[...]
-    kv[RIM + count : 2 * RIM + count, :] = high_ref[...]
-    total[...] = jnp.zeros_like(total)
-    for pair in range(count // step):
+    count = q_ref.shape[0]
+    pairs = count // step
+    reach = 2 * step
+    out_ref[:reach, :] = part_ref[0]
+    out_ref[reach : count - reach, :] = jnp.zeros((count - 2 * reach, 2 * COLS), F32)
+    out_ref[count - reach :, :] = part_ref[1]
+    for pair in range(1, pairs - 1):
+        window = slice((pair - 1) * step, (pair + 2) * step)
         rows = slice(pair * step, (pair + 1) * step)
-        window = slice(pair * step, pair * step + WINDOW)
-        keys, values = kv[window, :COLS], kv[window, COLS:]
-        queries, grads = by_head(q_ref[rows, :]), by_head(g_ref[rows, :])
-        probs = probabilities(queries, keys, usable_keys(steps_ref, pair))
-        grad_probs = lax.dot_general(grads, values, OVER_COLUMNS, preferred_element_type=F32)
-        row_delta = jnp.sum(probs * grad_probs, axis=-1, keepdims=True)
-        grad_scores = (probs * (grad_probs - row_delta) * (HEAD**-0.5)).astype(BF16)
-        total[window, :COLS] += lax.dot_general(
-            grad_scores, queries, OVER_ROWS, preferred_element_type=F32
+        key_grad, value_grad = attend_back(
+            steps_ref,
+            pair,
+            q_ref[rows, :],
+            g_ref[rows, :],
+            kv_ref[window, :COLS],
+            kv_ref[window, COLS:],
         )
-        total[window, COLS:] += lax.dot_general(
-            probs.astype(BF16), grads, OVER_ROWS, preferred_element_type=F32
-        )
-    both = total[...]
-    high = both.astype(BF16)
-    out_ref[:, : 2 * COLS] = high
-    out_ref[:, 2 * COLS :] = (both - high.astype(F32)).astype(BF16)
+        out_ref[window, :COLS] += key_grad
+        out_ref[window, COLS:] += value_grad
 
 
 def slope(spread):
     return spread * lax.rsqrt(spread * spread + SOFT_WIDTH)
 
 
-def mix_kernel(att_ref, source_ref, w, truth_ref, factor_ref, pred_ref, grad_ref, a):
-    members_num, part, _ = source_ref.shape
+def mix_kernel(
+    where_ref,
+    att_ref,
+    kept_ref,
+    sent_ref,
+    w,
+    truth_ref,
+    factor_ref,
+    pred_ref,
+    grad_ref,
+    a,
+    source,
+    truth,
+):
+    part = kept_ref.shape[1]
+    members_num = a.shape[0] // part
+    if members_num == 2:
+        for step, rows_ref in enumerate((kept_ref, sent_ref)):
+            place = pl.multiple_of((where_ref[2] ^ step) * part, part)
+            source[pl.ds(place, part), :] = rows_ref[0]
+    else:
+        source[...] = sent_ref[...].reshape(source.shape)
     for g in range(GROUP):
         for m in range(members_num):
             a[m * part : (m + 1) * part, g * COLS : (g + 1) * COLS] = att_ref[g * members_num + m]
-    mix, readout = w[:, :LATENT_DIM], w[:, LATENT_DIM:]
-    rows = members_num * part
-    source = source_ref[...].reshape(rows, LATENT_DIM).astype(F32)
-    hidden = source + jnp.dot(a[...], mix, preferred_element_type=F32)
+    lane_part = lax.broadcasted_iota(jnp.int32, (1, a.shape[0]), 1) // part
+    own_truth, own_factor = truth_ref[...], factor_ref[...]
+    for turn in range(1, members_num):
+        at = lane_part - turn
+        here = jnp.where(at < 0, at + members_num, at) == where_ref[2]
+        own_truth = jnp.where(here, pltpu.roll(truth_ref[...], turn * part, 1), own_truth)
+        own_factor = jnp.where(here, pltpu.roll(factor_ref[...], turn * part, 1), own_factor)
+    truth[...] = jnp.zeros_like(truth)
+    truth[:FIELD_NUM, :] = own_truth
+    both = w[...].reshape(LATENT_DIM, LATENT_DIM + FIELD_PAD)
+    mix, readout = both[:, :LATENT_DIM], both[:, LATENT_DIM:]
+    hidden = source[...].astype(F32) + jnp.dot(a[...], mix, preferred_element_type=F32)
     inverse = lax.rsqrt(jnp.mean(hidden * hidden, axis=-1, keepdims=True) + NORM_EPS)
     decoded = (hidden * inverse).astype(BF16)
     prediction = lax.dot_general(
@@ -293,8 +343,8 @@
     spread = jnp.zeros_like(prediction)
     for other in range(1, members_num):
         spread = spread + slope(prediction - pltpu.roll(prediction, other * part, 1))
-    derivative = factor_ref[...] / FIELD_NUM * (
-        slope(prediction - truth_ref[...]) - spread / (members_num - 1)
+    derivative = own_factor / FIELD_NUM * (
+        slope(prediction - truth[...]) - spread / (members_num - 1)
     )
     grad_decoded = lax.dot_general(
         derivative.astype(BF16), readout, (((0,), (1,)), ((), ())), preferred_element_type=F32
@@ -312,15 +362,23 @@
             ]
 
 
-def product_kernel(normed_ref, low_ref, high_ref, kv_ref, out_ref):
-    def term(rows_ref, at):
-        kv = kv_ref[at : at + rows_ref.shape[0], :]
-        both = lax.dot_general(rows_ref[...], kv, OVER_ROWS, preferred_element_type=F32)
-        return both[:, : 2 * COLS] + both[:, 2 * COLS :]
-
+def product_kernel(normed_ref, from_low_ref, from_high_ref, grads_ref, out_ref):
     count = normed_ref.shape[0]
-    total = term(normed_ref, RIM) + term(low_ref, 0) + term(high_ref, RIM + count)
-    out_ref[...] = total.astype(BF16)
+    grads = grads_ref[...]
+    grads = jnp.concatenate(
+        [
+            grads[:RIM] + from_low_ref[...].astype(F32),
+            grads[RIM : count - RIM],
+            grads[count - RIM :] + from_high_ref[...].astype(F32),
+        ],
+        axis=0,
+    )
+    high = grads.astype(BF16)
+    low = (grads - high.astype(F32)).astype(BF16)
+    both = lax.dot_general(
+        normed_ref[...], jnp.concatenate([high, low], axis=1), OVER_ROWS, preferred_element_type=F32
+    )
+    out_ref[...] = (both[:, : 2 * COLS] + both[:, 2 * COLS :]).astype(BF16)
 
 
 def gather_kernel(parts_ref, out_ref):
@@ -368,14 +426,15 @@
     paired = members_num == 2
     copies = 1 if paired else members_num
 
-    normed, columns, packed = call(
+    normed, columns, packed, *sources = call(
         prepare_kernel,
         "prepare",
         [
             ((node_rows + NOTE_ROWS, LATENT_DIM), BF16),
             ((halves, GROUP, copies, shard, 3 * COLS), BF16),
             ((shard, width), BF16),
-        ],
+        ]
+        + [((1 if paired else members_num, part, LATENT_DIM), BF16)] * (2 if paired else 1),
         "ssaaaa",
         [
             pltpu.VMEM((node_rows, LATENT_DIM), BF16),
@@ -385,6 +444,7 @@
         ],
         flops=2**20,
         moved=2**20,
+        room=56,
     )(where, neighbours, members.reshape(node_rows, LATENT_DIM), w_attn, w_mix, readout_matrix)
 
     packed = in_order(packed, "half", 0)
@@ -397,31 +457,16 @@
         columns = [columns[0].reshape(LATENT_DIM, 3 * COLS)]
     far = [swap(piece, "core", 1) for piece in near]
 
-    sources = members.reshape(members_num, part, LATENT_DIM)
     if paired:
-        kept = lax.dynamic_index_in_dim(sources, ens, 0, keepdims=False)
-        sent = swap(lax.dynamic_index_in_dim(sources, 1 - ens, 0, keepdims=False), "ens", 1)
-        sources = jnp.stack([jnp.where(ens == 0, kept, sent), jnp.where(ens == 0, sent, kept)])
+        kept, sent = sources[0], swap(sources[1], "ens", 1)
+        packed, columns[0] = lax.optimization_barrier((packed, columns[0]))
+        pieces = [packed] + [swap(packed, "quad", step) for step in range(1, QUAD)]
     else:
-        sources = exchange(sources, "ens")
-
-    packed, near[3] = lax.optimization_barrier((packed, near[3]))
-    if paired:
-        pieces = jnp.stack([packed] + [swap(packed, "quad", step) for step in range(1, QUAD)])
-        pieces, columns[1] = lax.optimization_barrier((pieces, columns[1]))
-        pieces = [pieces, swap(pieces, "ens", 1)]
-    else:
+        kept = sent = exchange(sources[0], "ens")
         packed = in_order(packed, "ens", 1).reshape(halves, members_num * shard, width)
         pieces = [packed] + [swap(packed, "quad", step) for step in range(1, QUAD)]
-    pieces = pieces + [swap(piece, "core", 1) for piece in pieces]
-    columns[-1], sources = lax.optimization_barrier((columns[-1], sources))
-
-    truth = lax.dynamic_slice_in_dim(observed_truth, ens * part, part, 1)
-    truth = jnp.tile(jnp.pad(truth, ((0, FIELD_PAD - FIELD_NUM), (0, 0))), (1, members_num))
-    factor = lax.dynamic_slice_in_dim(cell_surface_factor, ens * part, part, 0)
-    factor = jnp.tile(factor[None], (1, members_num))
-
-    queries, own, steps, first, last, first_normed, last_normed, normed = call(
+
+    queries, own, steps, first, last, normed = call(
         project_kernel,
         "project",
         [
@@ -430,26 +475,28 @@
             ((GROUP, NOTE_ROWS, 128), F32),
             ((RIM, 2 * COLS), BF16),
             ((RIM, 2 * COLS), BF16),
-            ((RIM, LATENT_DIM), BF16),
-            ((RIM, LATENT_DIM), BF16),
             ((rows, LATENT_DIM), BF16),
         ],
         "s" + "a" * (GROUP + len(columns)),
         [
             pltpu.VMEM((GROUP, NOTE_ROWS, 128), BF16),
             pltpu.VMEM((rows, LATENT_DIM), BF16),
-            pltpu.VMEM((LATENT_DIM, 3 * COLS), BF16),
-            pltpu.SemaphoreType.DMA((2 * GROUP + (2 * GROUP * halves if paired else 1),)),
+            pltpu.VMEM(
+                (GROUP * halves, 2, shard, 3 * COLS) if paired else (LATENT_DIM, 3 * COLS), BF16
+            ),
+            pltpu.SemaphoreType.DMA((2 * GROUP + 2,)),
         ],
         flops=rows * LATENT_DIM * 6 * COLS,
         moved=4 * 2**20,
         room=14,
-        results="vvvvvvva",
+        results="vvvvva",
     )(where, *near, *far, *columns)
     low = lax.ppermute(last, "half", up)
     high = lax.ppermute(first, "half", down)
-    normed_low = lax.ppermute(last_normed, "half", up)
-    normed_high = lax.ppermute(first_normed, "half", down)
+    if paired:
+        pieces = jnp.stack(pieces)
+        pieces, own = lax.optimization_barrier((pieces, own))
+        pieces = [pieces, swap(pieces, "ens", 1)]
 
     (outcome,) = call(
         interior_kernel,
@@ -469,52 +516,69 @@
         moved=2**20,
         exps=rows * 128,
     )(steps, queries, own, low, high, outcome)
+    *pieces, outcome = lax.optimization_barrier((*pieces, outcome))
     attended = exchange(outcome.reshape(GROUP * members_num, part, COLS), ("quad", "core", "ens"))
+    pieces = pieces + [swap(piece, "core", 1) for piece in pieces]
+    block = (halves, QUAD, CORES) + ((2, shard) if paired else (1, members_num * shard)) + (width,)
     (weights,) = call(
         weights_kernel,
         "weights",
-        [((LATENT_DIM, width), BF16)],
+        [(block, BF16)],
         "s" + "a" * len(pieces),
-        [pltpu.SemaphoreType.DMA((2 * GROUP * halves,))],
+        [pltpu.SemaphoreType.DMA((4 * QUAD,))],
         moved=4 * 2**20,
     )(where, *pieces)
-    attended, normed_low, normed_high = lax.optimization_barrier((attended, normed_low, normed_high))
 
     prediction, grads = call(
         mix_kernel,
         "mix_loss_backward",
         [((FIELD_NUM, node_rows), F32), ((GROUP * members_num, part, COLS), BF16)],
-        "vvvvv",
-        [pltpu.VMEM((node_rows, LATENT_DIM), BF16)],
+        "svvvvvv",
+        [
+            pltpu.VMEM((node_rows, LATENT_DIM), BF16),
+            pltpu.VMEM((node_rows, LATENT_DIM), BF16),
+            pltpu.VMEM((FIELD_PAD, node_rows), F32),
+        ],
         flops=node_rows * LATENT_DIM * 4 * width,
         moved=2**22,
         room=14,
-    )(attended, sources, weights, truth, factor)
+    )(where, attended, kept, sent, weights, observed_truth, cell_surface_factor[None])
     grads = exchange(grads, ("quad", "core", "ens")).reshape(rows, COLS)
 
+    rim_low, rim_high, edges = call(
+        edge_back_kernel,
+        "attention_edges_back",
+        [
+            ((RIM, 2 * COLS), BF16),
+            ((RIM, 2 * COLS), BF16),
+            ((2, WINDOW - RIM, 2 * COLS), F32),
+        ],
+        "vvvvvv",
+        flops=rows * COLS * 1280,
+        moved=2**20,
+        exps=rows * 128,
+    )(steps, queries, own, low, high, grads)
+    from_low = lax.ppermute(rim_high, "half", up)
+    from_high = lax.ppermute(rim_low, "half", down)
     (kv_grads,) = call(
-        backward_kernel,
-        "attention_backward",
-        [((rows + 2 * RIM, 4 * COLS), BF16)],
-        "vvvvvv",
-        [
-            pltpu.VMEM((rows + 2 * RIM, 2 * COLS), BF16),
-            pltpu.VMEM((rows + 2 * RIM, 2 * COLS), F32),
-        ],
-        flops=rows * COLS * 5120,
+        interior_back_kernel,
+        "attention_interior_back",
+        [((rows, 2 * COLS), F32)],
+        "vvvvv",
+        flops=rows * COLS * 4096,
         moved=2**22,
         exps=rows * 512,
-        room=14,
-    )(steps, queries, low, own, high, grads)
+        room=10,
+    )(steps, queries, own, grads, edges)
     (term,) = call(
         product_kernel,
         "product",
         [((LATENT_DIM, 2 * COLS), BF16)],
         "vvvv",
-        flops=(rows + 2 * RIM) * LATENT_DIM * 8 * COLS,
+        flops=rows * LATENT_DIM * 8 * COLS,
         moved=2**22,
         room=16,
-    )(normed, normed_low, normed_high, kv_grads)
+    )(normed, from_low, from_high, kv_grads)
     term, prediction = lax.optimization_barrier((term, prediction))
     term = exchange(term.reshape(-1, shard, 2 * COLS), everyone)
     (grad_kv,) = call(

time: 154 us -> 128 us (0.83)
  waiting for transfers between devices: 63 us -> 38.6 us
  Pallas kernels: 26.3 us -> 22.5 us
  local copies, waits for them, and re-layouts: 8.96 us -> 10.8 us
    ppermute x17, waiting for transfers between devices: 35.6 us -> 16.5 us  [swap(): lax.ppermute(value, axis, [(i, i ^ step) for i in range(lax.axis_size(axi...]
    ppermute x2, waiting for transfers between devices: 14.4 us -> 2.49 us  [the longest x1 2.49 us: body(): from_high = lax.ppermute(rim_low, 'half', down)]
    all_to_all x3, waiting for transfers between devices: 9.09 us -> 16.9 us  [exchange(): return lax.all_to_all(chunks, axes, 0, 0)]
    pallas_call x2 -> x3, Pallas kernels: 9.83 us -> 7.53 us  [the longest x1 3.86 us: body(): call(interior_back_kernel, 'attention_interior_back', [((rows, 2 * COLS),...]
    ppermute x2, starting transfers between devices: 3.25 us -> 5.51 us  [the longest x1 4.04 us: body(): from_low = lax.ppermute(rim_high, 'half', up)]
    unnamed x38 -> x43, local copies, waits for them, and re-layouts: 8.52 us -> 10.7 us
    ppermute x17, starting transfers between devices: 21.1 us -> 19.4 us  [swap(): lax.ppermute(value, axis, [(i, i ^ step) for i in range(lax.axis_size(axi...]
    pallas_call x1, Pallas kernels: 3.72 us -> 2.09 us  [body(): call(product_kernel, 'product', [((LATENT_DIM, 2 * COLS), BF16)], 'vvvv',...]
  transfers between devices with their start and end apart: 24 -> 24, of which waited for: 12 -> 12; matrix products, arithmetic and copies ran while one was open for 1% -> 1% of each run, Pallas kernels for 5% -> 8%
where the time goes in v6:
time: 128 us; the launch traced here: 127 us
  starting transfers between devices  41.8 us (33%)
  waiting for transfers between devices  38.6 us (30%)
  Pallas kernels  22.5 us (18%)
  blocking collectives  11.1 us (9%)
  local copies, waits for them, and re-layouts  10.8 us (8%)
  other arithmetic  1.72 us (1%)
    ppermute x17, starting transfers between devices, swap(): lax.ppermute(value, axis, [(i, i ^ step) for i in range(lax.axis_size(axi...  19.4 us
    all_to_all x3, waiting for transfers between devices, exchange(): return lax.all_to_all(chunks, axes, 0, 0)  16.9 us
    ppermute x17, waiting for transfers between devices, swap(): lax.ppermute(value, axis, [(i, i ^ step) for i in range(lax.axis_size(axi...  16.5 us
    all_to_all x3, starting transfers between devices, exchange(): return lax.all_to_all(chunks, axes, 0, 0)  11.8 us
    all_to_all x1, blocking collectives, exchange(): return lax.all_to_all(chunks, axes, 0, 0)  11.1 us
    unnamed x43, local copies, waits for them, and re-layouts  10.7 us
    ppermute x1, starting transfers between devices, body(): from_low = lax.ppermute(rim_high, 'half', up)  4.04 us
    pallas_call x1, Pallas kernels, body(): call(interior_back_kernel, 'attention_interior_back', [((rows, 2 * COLS),...  3.86 us
  transfers between devices with their start and end apart: 24, of which 12 were waited for; matrix products, arithmetic and copies ran while one was open for 1% of the time, Pallas kernels for 8%

profile of v6, /device:TPU:1, one launch (start us, length us, event | category | flops | bytes accessed | tf_op | source)
XLA Modules:
  0.0 127.4 jit_solution(2170086380073508242)
XLA Ops:
  1.2 3.0 %prepare.1 = (bf16[144,1024]{1,0:T(8,128)(2,1)}, bf16[2,8,1,32,384]{4,3,2,1,0:T(8,128)(2,1)}, bf16[32,1152]{1,0:T(8,128)(2,1)}, bf16[1,64,1024]{2,1,0:T(8,128)(2,1)}, bf16[1,64,1024]{2,1,0:T(8,128)(2,1)}) custom-call(s32[4]{0:T(128)} %pad_add_fusion.where_ref, s32[2,4]{1,0:T(2,128)} %near_ref.1, bf16[128,1024]{1,0:T(8,128)(2,1)} %bitcast.27, ...), custom_call_target="tpu_custom_call" | custom-call | flops 1048576 | bytes 1048576 | tf_op jit(solution)/shard_map/prepare/pallas_call | solution.py:429
  4.2 3.2 %collective-permute-start.7 = (bf16[32,1152]{1,0:T(8,128)(2,1)}, bf16[32,1152]{1,0:T(8,128)(2,1)S(1)}, u32[]{:S(2)}, u32[]{:S(2)}) collective-permute-start(bf16[32,1152]{1,0:T(8,128)(2,1)} %get-tuple-element.28), channel_id=1, source_target_pairs={{0,16},{16,0},{1,17},{17,1},{2,18},{18,2},{3,19},{19,3},{4,20},{20... | collective-permute-start | bytes 221192 | tf_op jit(solution)/shard_map/ppermute | solution.py:401
  7.4 4.8 %all-to-all-start = ((bf16[16,32,384]{2,1,0:T(8,128)(2,1)}), bf16[16,32,384]{2,1,0:T(8,128)(2,1)S(1)}, u32[]{:S(2)}, u32[]{:S(2)}) async-start(bf16[16,32,384]{2,1,0:T(8,128)(2,1)} %bitcast.26), calls=%async_computation | async-start | bytes 786432 | tf_op jit(solution)/shard_map/all_to_all | solution.py:397
  12.2 1.4 %collective-permute-start = (bf16[144,1024]{1,0:T(8,128)(2,1)}, bf16[144,1024]{1,0:T(8,128)(2,1)S(1)}, u32[]{:S(2)}, u32[]{:S(2)}) collective-permute-start(bf16[144,1024]{1,0:T(8,128)(2,1)} %get-tuple-element.27.refs_0_), channel_id=1, source_target_pairs={{0,4},{4,0},{8,12},{12,8},{1,5},{5,1},{9,13},{13,9},{2,6},{6,2},{1... | collective-permute-start | bytes 884744 | tf_op jit(solution)/shard_map/ppermute | solution.py:401
  13.6 1.2 collective-permute-start.1
  14.9 0.9 select_bitcast_fusion.1
  15.8 7.8 %all-to-all-done.refs_8_ = bf16[16,32,384]{2,1,0:T(8,128)(2,1)S(1)} async-done(((bf16[16,32,384]{2,1,0:T(8,128)(2,1)}), bf16[16,32,384]{2,1,0:T(8,128)(2,1)S(1)}, u32[]{:S(2)}, u32[]{:S(2)}) %all-to-all-start) | async-done | bytes 393248 | tf_op jit(solution)/shard_map/all_to_all | solution.py:397
  23.6 1.9 %collective-permute-start.11 = (bf16[2,32,1152]{2,1,0:T(8,128)(2,1)S(1)}, bf16[2,32,1152]{2,1,0:T(8,128)(2,1)S(1)}, u32[]{:S(2)}, u32[]{:S(2)}) collective-permute-start(bf16[2,32,1152]{2,1,0:T(8,128)(2,1)S(1)} %pad_maximum_fusion.1), channel_id=1, source_target_pairs={{0,12},{4,8},{8,4},{12,0},{1,13},{5,9},{9,5},{13,1},{2,14},{6,10},... | collective-permute-start | bytes 442376 | tf_op jit(solution)/shard_map/ppermute | solution.py:401
  26.3 0.9 collective-permute-done.1.refs_2_
  27.2 1.2 collective-permute-start.8
  28.4 6.1 %collective-permute-done.2.refs_3_ = bf16[144,1024]{1,0:T(8,128)(2,1)S(1)} collective-permute-done((bf16[144,1024]{1,0:T(8,128)(2,1)}, bf16[144,1024]{1,0:T(8,128)(2,1)S(1)}, u32[]{:S(2)}, u32[]{:S(2)}) %collective-permute-start.2) | collective-permute-done | bytes 294944 | tf_op jit(solution)/shard_map/ppermute | solution.py:401
  34.5 1.4 %collective-permute-start.3 = (bf16[144,1024]{1,0:T(8,128)(2,1)}, bf16[144,1024]{1,0:T(8,128)(2,1)S(1)}, u32[]{:S(2)}, u32[]{:S(2)}) collective-permute-start(bf16[144,1024]{1,0:T(8,128)(2,1)} %get-tuple-element.27.refs_0_), channel_id=1, source_target_pairs={{0,2},{2,0},{1,3},{3,1},{4,6},{6,4},{5,7},{7,5},{8,10},{10,8},{9,1... | collective-permute-start | bytes 884744 | tf_op jit(solution)/shard_map/ppermute | solution.py:401
  35.9 1.8 %collective-permute-done.11 = bf16[2,32,1152]{2,1,0:T(8,128)(2,1)S(1)} collective-permute-done((bf16[2,32,1152]{2,1,0:T(8,128)(2,1)S(1)}, bf16[2,32,1152]{2,1,0:T(8,128)(2,1)S(1)}, u32[]{:S(2)}, u32[]{:S(2)}) %collective-permute-start.11) | collective-permute-done | bytes 147488 | tf_op jit(solution)/shard_map/ppermute | solution.py:401
  37.6 1.3 %collective-permute-start.4 = (bf16[144,1024]{1,0:T(8,128)(2,1)S(1)}, bf16[144,1024]{1,0:T(8,128)(2,1)S(1)}, u32[]{:S(2)}, u32[]{:S(2)}) collective-permute-start(bf16[144,1024]{1,0:T(8,128)(2,1)S(1)} %collective-permute-done.refs_1_), channel_id=1, source_target_pairs={{0,2},{2,0},{1,3},{3,1},{4,6},{6,4},{5,7},{7,5},{8,10},{10,8},{9,1... | collective-permute-start | bytes 884744 | tf_op jit(solution)/shard_map/ppermute | solution.py:401
  39.0 0.9 collective-permute-done.10
  39.9 0.9 collective-permute-start.5
  42.6 2.4 %project.1 = (bf16[1024,128]{1,0:T(8,128)(2,1)S(1)}, bf16[1024,256]{1,0:T(8,128)(2,1)S(1)}, f32[8,16,128]{2,1,0:T(8,128)S(1)}, bf16[128,256]{1,0:T(8,128)(2,1)S(...) custom-call(s32[4]{0:T(128)S(1)} %copy-done.17, bf16[144,1024]{1,0:T(8,128)(2,1)S(1)} %copy-done.8, ...), custom_call_target="tpu_custom_call" | custom-call | flops 805306368 | bytes 4194304 | tf_op jit(solution)/shard_map/project/pallas_call | solution.py:469
  45.0 1.3 %collective-permute-start.14 = (bf16[4,2,32,1152]{3,2,1,0:T(8,128)(2,1)S(1)}, bf16[4,2,32,1152]{3,2,1,0:T(8,128)(2,1)S(1)}, u32[]{:S(2)}, u32[]{:S(2)}) collective-permute-start(bf16[4,2,32,1152]{3,2,1,0:T(8,128)(2,1)S(1)} %pad_maximum_fusion.refs_0_), channel_id=1, source_target_pairs={{0,1},{1,0},{2,3},{3,2},{4,5},{5,4},{6,7},{7,6},{8,9},{9,8},{10,11... | collective-permute-start | bytes 1769480 | tf_op jit(solution)/shard_map/ppermute | solution.py:401
  46.3 3.8 %collective-permute-start.12 = (bf16[128,256]{1,0:T(8,128)(2,1)S(1)}, bf16[128,256]{1,0:T(8,128)(2,1)S(1)}, u32[]{:S(2)}, u32[]{:S(2)}) collective-permute-start(bf16[128,256]{1,0:T(8,128)(2,1)S(1)} %get-tuple-element.37), channel_id=1, source_target_pairs={{0,16},{1,17},{2,18},{3,19},{4,20},{5,21},{6,22},{7,23},{8,24},{9,... | collective-permute-start | bytes 196616 | tf_op jit(solution)/shard_map/ppermute | solution.py:494
  50.1 1.3 %collective-permute-start.13 = (bf16[128,256]{1,0:T(8,128)(2,1)S(1)}, bf16[128,256]{1,0:T(8,128)(2,1)S(1)}, u32[]{:S(2)}, u32[]{:S(2)}) collective-permute-start(bf16[128,256]{1,0:T(8,128)(2,1)S(1)} %get-tuple-element.38), channel_id=1, source_target_pairs={{16,0},{17,1},{18,2},{19,3},{20,4},{21,5},{22,6},{23,7},{24,8},{25... | collective-permute-start | bytes 196616 | tf_op jit(solution)/shard_map/ppermute | solution.py:495
  51.4 2.6 %attention_interior.1.done_ref = bf16[1024,128]{1,0:T(8,128)(2,1)S(1)} custom-call(f32[8,16,128]{2,1,0:T(8,128)S(1)} %get-tuple-element.32.steps_ref, bf16[1024,128]{1,0:T(8,128)(2,1)S(1)} %get-tuple-element.33.q_ref, bf16[1024,256]{1,0:T(8,128)(2,1)S(1)} %get-tuple-element.36.kv_ref), custom_call_target="tpu_custom_call" | custom-call | flops 268435456 | bytes 2097152 | tf_op jit(solution)/shard_map/attention_interior/pallas_call | solution.py:501
  54.0 2.7 %collective-permute-done.13.high_ref = bf16[128,256]{1,0:T(8,128)(2,1)S(1)} collective-permute-done((bf16[128,256]{1,0:T(8,128)(2,1)S(1)}, bf16[128,256]{1,0:T(8,128)(2,1)S(1)}, u32[]{:S(2)}, u32[]{:S(2)}) %collective-permute-start.13) | collective-permute-done | bytes 65568 | tf_op jit(solution)/shard_map/ppermute | solution.py:495
  56.7 1.7 %attention_edges.1 = bf16[1024,128]{1,0:T(8,128)(2,1)} custom-call(f32[8,16,128]{2,1,0:T(8,128)S(1)} %get-tuple-element.32.steps_ref, bf16[1024,128]{1,0:T(8,128)(2,1)S(1)} %get-tuple-element.33.q_ref, bf16[1024,256]{1,0:T(8,128)(2,1)S(1)} %get-tuple-element.36.kv_ref, bf16[128,256]{1,0:T(8,128)(2,1)S(1)} %collective-permute-done.12.low_ref, ...), custom_call_target="tpu_custom_call" | custom-call | flops 67108864 | bytes 1048576 | tf_op jit(solution)/shard_map/attention_edges/pallas_call | solution.py:510
  58.4 1.2 collective-permute-done.14.refs_1_
  59.6 1.2 collective-permute-start.16
  60.8 0.8 copy-done.2
  61.7 4.0 %all-to-all-start.1 = ((bf16[16,64,128]{2,1,0:T(8,128)(2,1)}), bf16[16,64,128]{2,1,0:T(8,128)(2,1)S(1)}, u32[]{:S(2)}, u32[]{:S(2)}) async-start(bf16[16,64,128]{2,1,0:T(8,128)(2,1)} %bitcast.12), calls=%async_computation.1 | async-start | bytes 524288 | tf_op jit(solution)/shard_map/all_to_all | solution.py:397
  65.7 1.4 %collective-permute-start.15 = (bf16[1,64,1024]{2,1,0:T(8,128)(2,1)}, bf16[1,64,1024]{2,1,0:T(8,128)(2,1)S(1)}, u32[]{:S(2)}, u32[]{:S(2)}) collective-permute-start(bf16[1,64,1024]{2,1,0:T(8,128)(2,1)} %get-tuple-element.42), channel_id=1, source_target_pairs={{0,1},{1,0},{2,3},{3,2},{4,5},{5,4},{6,7},{7,6},{8,9},{9,8},{10,11... | collective-permute-start | bytes 393224 | tf_op jit(solution)/shard_map/ppermute | solution.py:401
  67.9 0.8 copy-done.6
  68.7 1.1 copy-done.1
  69.8 1.1 copy-done.3
  70.9 1.1 copy-done.5
  71.9 1.1 copy-done.7
  73.0 2.3 %weights.1.w = bf16[2,4,2,2,32,1152]{5,4,3,2,1,0:T(8,128)(2,1)S(1)} custom-call(s32[4]{0:T(128)S(1)} %copy-done.17, bf16[4,2,32,1152]{3,2,1,0:T(8,128)(2,1)S(1)} %copy-done.1, bf16[4,2,32,1152]{3,2,1,0:T(8,128)(2,1)S(1)} %copy-done.3, bf16[4,2,32,1152]{3,2,1,0:T(8,128)(2,1)S(1)} %copy-done.5, bf16[4,2,32,1152]{3,2,1,0:T(8,128)(2,1)S(1)} %copy-done.7), custom_call_target="tpu_custom_call" | custom-call | bytes 4194304 | tf_op jit(solution)/shard_map/weights/pallas_call | solution.py:523
  75.9 0.9 copy-done.11
  76.9 0.9 copy-done.13
  78.6 2.5 %mix_loss_backward.1 = (f32[100,128]{1,0:T(8,128)S(1)}, bf16[16,64,128]{2,1,0:T(8,128)(2,1)S(1)}) custom-call(s32[4]{0:T(128)S(1)} %copy-done.17, bf16[16,64,128]{2,1,0:T(8,128)(2,1)S(1)} %all-to-all-done.1.att_ref, bf16[1,64,1024]{2,1,0:T(8,128)(2,1)S(1)} %copy-done.11, bf16[1,64,1024]{2,1,0:T(8,128)(2,1)S(1)} %copy-done.13, ...), custom_call_target="tpu_custom_call" | custom-call | flops 603979776 | bytes 4194304 | tf_op jit(solution)/shard_map/mix_loss_backward/pallas_call | solution.py:532
  81.1 11.1 %all_to_all.20 = bf16[16,64,128]{2,1,0:T(8,128)(2,1)S(1)} all-to-all(bf16[16,64,128]{2,1,0:T(8,128)(2,1)S(1)} %get-tuple-element.45), channel_id=1, replica_groups=mesh['half'=2,'quad'=4,'core'=2,'ens'=2] {'quad','core','ens'}, dimensions={0} | all-to-all | bytes 524288 | tf_op jit(solution)/shard_map/all_to_all | solution.py:397
  92.2 1.4 %attention_edges_back.1 = (bf16[128,256]{1,0:T(8,128)(2,1)S(1)}, bf16[128,256]{1,0:T(8,128)(2,1)S(1)}, f32[2,256,256]{2,1,0:T(8,128)S(1)}) custom-call(f32[8,16,128]{2,1,0:T(8,128)S(1)} %get-tuple-element.32.steps_ref, bf16[1024,128]{1,0:T(8,128)(2,1)S(1)} %get-tuple-element.33.q_ref, bf16[1024,256]{1,0:T(8,128)(2,1)S(1)} %get-tuple-element.36.kv_ref, ...), custom_call_target="tpu_custom_call" | custom-call | flops 167772160 | bytes 1048576 | tf_op jit(solution)/shard_map/attention_edges_back/pallas_call | solution.py:548
  93.6 4.0 %collective-permute-start.18 = (bf16[128,256]{1,0:T(8,128)(2,1)S(1)}, bf16[128,256]{1,0:T(8,128)(2,1)S(1)}, u32[]{:S(2)}, u32[]{:S(2)}) collective-permute-start(bf16[128,256]{1,0:T(8,128)(2,1)S(1)} %get-tuple-element.46), channel_id=1, source_target_pairs={{0,16},{1,17},{2,18},{3,19},{4,20},{5,21},{6,22},{7,23},{8,24},{9,... | collective-permute-start | bytes 196616 | tf_op jit(solution)/shard_map/ppermute | solution.py:561
  97.7 1.5 %collective-permute-start.19 = (bf16[128,256]{1,0:T(8,128)(2,1)S(1)}, bf16[128,256]{1,0:T(8,128)(2,1)S(1)}, u32[]{:S(2)}, u32[]{:S(2)}) collective-permute-start(bf16[128,256]{1,0:T(8,128)(2,1)S(1)} %get-tuple-element.47), channel_id=1, source_target_pairs={{16,0},{17,1},{18,2},{19,3},{20,4},{21,5},{22,6},{23,7},{24,8},{25... | collective-permute-start | bytes 196616 | tf_op jit(solution)/shard_map/ppermute | solution.py:562
  99.2 3.9 %attention_interior_back.1.grads_ref = f32[1024,256]{1,0:T(8,128)S(1)} custom-call(f32[8,16,128]{2,1,0:T(8,128)S(1)} %get-tuple-element.32.steps_ref, bf16[1024,128]{1,0:T(8,128)(2,1)S(1)} %get-tuple-element.33.q_ref, bf16[1024,256]{1,0:T(8,128)(2,1)S(1)} %get-tuple-element.36.kv_ref, bf16[1024,128]{1,0:T(8,128)(2,1)S(1)} %bitcast.22, ...), custom_call_target="tpu_custom_call" | custom-call | flops 536870912 | bytes 4194304 | tf_op jit(solution)/shard_map/attention_interior_back/pallas_call | solution.py:563
  103.1 2.5 %collective-permute-done.19.from_high_ref = bf16[128,256]{1,0:T(8,128)(2,1)S(1)} collective-permute-done((bf16[128,256]{1,0:T(8,128)(2,1)S(1)}, bf16[128,256]{1,0:T(8,128)(2,1)S(1)}, u32[]{:S(2)}, u32[]{:S(2)}) %collective-permute-start.19) | collective-permute-done | bytes 65568 | tf_op jit(solution)/shard_map/ppermute | solution.py:562
  105.6 2.1 %product.1 = bf16[1024,256]{1,0:T(8,128)(2,1)} custom-call(bf16[1024,1024]{1,0:T(8,128)(2,1)S(1)} %copy-done.20, bf16[128,256]{1,0:T(8,128)(2,1)S(1)} %collective-permute-done.18.from_low_ref, bf16[128,256]{1,0:T(8,128)(2,1)S(1)} %collective-permute-done.19.from_high_ref, f32[1024,256]{1,0:T(8,128)S(1)} %attention_interior_back.1.grads_ref), custom_call_target="tpu_custom_call" | custom-call | flops 1073741824 | bytes 4194304 | tf_op jit(solution)/shard_map/product/pallas_call | solution.py:573
  107.6 3.0 %all-to-all-start.3 = ((bf16[32,32,256]{2,1,0:T(8,128)(2,1)}), bf16[32,32,256]{2,1,0:T(8,128)(2,1)S(1)}, u32[]{:S(2)}, u32[]{:S(2)}) async-start(bf16[32,32,256]{2,1,0:T(8,128)(2,1)} %bitcast.16), calls=%async_computation.3 | async-start | bytes 1048576 | tf_op jit(solution)/shard_map/all_to_all | solution.py:397
  110.7 1.5 %collective-permute-start.20 = (f32[100,128]{1,0:T(8,128)S(1)}, f32[100,128]{1,0:T(8,128)S(1)}, u32[]{:S(2)}, u32[]{:S(2)}) collective-permute-start(f32[100,128]{1,0:T(8,128)S(1)} %copy-done.15), channel_id=1, source_target_pairs={{0,1},{1,0},{2,3},{3,2},{4,5},{5,4},{6,7},{7,6},{8,9},{9,8},{10,11... | collective-permute-start | bytes 153608 | tf_op jit(solution)/shard_map/ppermute | solution.py:401
  112.2 4.5 %collective-permute-done.20 = f32[100,128]{1,0:T(8,128)S(1)} collective-permute-done((f32[100,128]{1,0:T(8,128)S(1)}, f32[100,128]{1,0:T(8,128)S(1)}, u32[]{:S(2)}, u32[]{:S(2)}) %collective-permute-start.20) | collective-permute-done | bytes 51232 | tf_op jit(solution)/shard_map/ppermute | solution.py:401
  117.6 9.1 %all-to-all-done.3 = bf16[32,32,256]{2,1,0:T(8,128)(2,1)S(1)} async-done(((bf16[32,32,256]{2,1,0:T(8,128)(2,1)}), bf16[32,32,256]{2,1,0:T(8,128)(2,1)S(1)}, u32[]{:S(2)}, u32[]{:S(2)}) %all-to-all-start.3) | async-done | bytes 524320 | tf_op jit(solution)/shard_map/all_to_all | solution.py:397
  (62 shorter events, 7.2 us)
Async XLA Ops:
  1.2 41.4 %copy-start.17 = (s32[4]{0:T(128)S(1)}, s32[4]{0:T(128)}, u32[]{:S(2)}) copy-start(s32[4]{0:T(128)} %pad_add_fusion.where_ref) | copy-start | bytes 52
  4.2 38.4 %copy-start.8 = (bf16[144,1024]{1,0:T(8,128)(2,1)S(1)}, bf16[144,1024]{1,0:T(8,128)(2,1)}, u32[]{:S(2)}) copy-start(bf16[144,1024]{1,0:T(8,128)(2,1)} %get-tuple-element.27.refs_0_) | copy-start | bytes 884740
  4.2 10.6 %collective-permute-start.7 = (bf16[32,1152]{1,0:T(8,128)(2,1)}, bf16[32,1152]{1,0:T(8,128)(2,1)S(1)}, u32[]{:S(2)}, u32[]{:S(2)}) collective-permute-start(bf16[32,1152]{1,0:T(8,128)(2,1)} %get-tuple-element.28), channel_id=1, source_target_pairs={{0,16},{16,0},{1,17},{17,1},{2,18},{18,2},{3,19},{19,3},{4,20},{20... | collective-permute-start | bytes 221192 | tf_op jit(solution)/shard_map/ppermute | solution.py:401
  7.4 16.2 %all-to-all-start = ((bf16[16,32,384]{2,1,0:T(8,128)(2,1)}), bf16[16,32,384]{2,1,0:T(8,128)(2,1)S(1)}, u32[]{:S(2)}, u32[]{:S(2)}) async-start(bf16[16,32,384]{2,1,0:T(8,128)(2,1)} %bitcast.26), calls=%async_computation | async-start | bytes 786432 | tf_op jit(solution)/shard_map/all_to_all | solution.py:397
  12.2 13.7 %collective-permute-start = (bf16[144,1024]{1,0:T(8,128)(2,1)}, bf16[144,1024]{1,0:T(8,128)(2,1)S(1)}, u32[]{:S(2)}, u32[]{:S(2)}) collective-permute-start(bf16[144,1024]{1,0:T(8,128)(2,1)} %get-tuple-element.27.refs_0_), channel_id=1, source_target_pairs={{0,4},{4,0},{8,12},{12,8},{1,5},{5,1},{9,13},{13,9},{2,6},{6,2},{1... | collective-permute-start | bytes 884744 | tf_op jit(solution)/shard_map/ppermute | solution.py:401
  13.6 13.6 %collective-permute-start.1 = (bf16[144,1024]{1,0:T(8,128)(2,1)}, bf16[144,1024]{1,0:T(8,128)(2,1)S(1)}, u32[]{:S(2)}, u32[]{:S(2)}) collective-permute-start(bf16[144,1024]{1,0:T(8,128)(2,1)} %get-tuple-element.27.refs_0_), channel_id=1, source_target_pairs={{0,8},{4,12},{8,0},{12,4},{1,9},{5,13},{9,1},{13,5},{2,10},{6,14},... | collective-permute-start | bytes 884744 | tf_op jit(solution)/shard_map/ppermute | solution.py:401
  14.8 19.7 %collective-permute-start.2 = (bf16[144,1024]{1,0:T(8,128)(2,1)}, bf16[144,1024]{1,0:T(8,128)(2,1)S(1)}, u32[]{:S(2)}, u32[]{:S(2)}) collective-permute-start(bf16[144,1024]{1,0:T(8,128)(2,1)} %get-tuple-element.27.refs_0_), channel_id=1, source_target_pairs={{0,12},{4,8},{8,4},{12,0},{1,13},{5,9},{9,5},{13,1},{2,14},{6,10},... | collective-permute-start | bytes 884744 | tf_op jit(solution)/shard_map/ppermute | solution.py:401
  23.6 14.0 %collective-permute-start.11 = (bf16[2,32,1152]{2,1,0:T(8,128)(2,1)S(1)}, bf16[2,32,1152]{2,1,0:T(8,128)(2,1)S(1)}, u32[]{:S(2)}, u32[]{:S(2)}) collective-permute-start(bf16[2,32,1152]{2,1,0:T(8,128)(2,1)S(1)} %pad_maximum_fusion.1), channel_id=1, source_target_pairs={{0,12},{4,8},{8,4},{12,0},{1,13},{5,9},{9,5},{13,1},{2,14},{6,10},... | collective-permute-start | bytes 442376 | tf_op jit(solution)/shard_map/ppermute | solution.py:401
  25.6 14.3 %collective-permute-start.10 = (bf16[2,32,1152]{2,1,0:T(8,128)(2,1)S(1)}, bf16[2,32,1152]{2,1,0:T(8,128)(2,1)S(1)}, u32[]{:S(2)}, u32[]{:S(2)}) collective-permute-start(bf16[2,32,1152]{2,1,0:T(8,128)(2,1)S(1)} %pad_maximum_fusion.1), channel_id=1, source_target_pairs={{0,8},{4,12},{8,0},{12,4},{1,9},{5,13},{9,1},{13,5},{2,10},{6,14},... | collective-permute-start | bytes 442376 | tf_op jit(solution)/shard_map/ppermute | solution.py:401
  25.9 14.9 %collective-permute-start.9 = (bf16[2,32,1152]{2,1,0:T(8,128)(2,1)S(1)}, bf16[2,32,1152]{2,1,0:T(8,128)(2,1)S(1)}, u32[]{:S(2)}, u32[]{:S(2)}) collective-permute-start(bf16[2,32,1152]{2,1,0:T(8,128)(2,1)S(1)} %pad_maximum_fusion.1), channel_id=1, source_target_pairs={{0,4},{4,0},{8,12},{12,8},{1,5},{5,1},{9,13},{13,9},{2,6},{6,2},{1... | collective-permute-start | bytes 442376 | tf_op jit(solution)/shard_map/ppermute | solution.py:401
  27.2 15.4 %collective-permute-start.8 = (bf16[16,32,384]{2,1,0:T(8,128)(2,1)S(1)}, bf16[16,32,384]{2,1,0:T(8,128)(2,1)S(1)}, u32[]{:S(2)}, u32[]{:S(2)}) collective-permute-start(bf16[16,32,384]{2,1,0:T(8,128)(2,1)S(1)} %all-to-all-done.refs_8_), channel_id=1, source_target_pairs={{0,1},{1,0},{2,3},{3,2},{4,5},{5,4},{6,7},{7,6},{8,9},{9,8},{10,11... | collective-permute-start | bytes 1179656 | tf_op jit(solution)/shard_map/ppermute | solution.py:401
  34.5 7.0 %collective-permute-start.3 = (bf16[144,1024]{1,0:T(8,128)(2,1)}, bf16[144,1024]{1,0:T(8,128)(2,1)S(1)}, u32[]{:S(2)}, u32[]{:S(2)}) collective-permute-start(bf16[144,1024]{1,0:T(8,128)(2,1)} %get-tuple-element.27.refs_0_), channel_id=1, source_target_pairs={{0,2},{2,0},{1,3},{3,1},{4,6},{6,4},{5,7},{7,5},{8,10},{10,8},{9,1... | collective-permute-start | bytes 884744 | tf_op jit(solution)/shard_map/ppermute | solution.py:401
  37.6 3.9 %collective-permute-start.4 = (bf16[144,1024]{1,0:T(8,128)(2,1)S(1)}, bf16[144,1024]{1,0:T(8,128)(2,1)S(1)}, u32[]{:S(2)}, u32[]{:S(2)}) collective-permute-start(bf16[144,1024]{1,0:T(8,128)(2,1)S(1)} %collective-permute-done.refs_1_), channel_id=1, source_target_pairs={{0,2},{2,0},{1,3},{3,1},{4,6},{6,4},{5,7},{7,5},{8,10},{10,8},{9,1... | collective-permute-start | bytes 884744 | tf_op jit(solution)/shard_map/ppermute | solution.py:401
  39.9 2.1 %collective-permute-start.5 = (bf16[144,1024]{1,0:T(8,128)(2,1)S(1)}, bf16[144,1024]{1,0:T(8,128)(2,1)S(1)}, u32[]{:S(2)}, u32[]{:S(2)}) collective-permute-start(bf16[144,1024]{1,0:T(8,128)(2,1)S(1)} %collective-permute-done.1.refs_2_), channel_id=1, source_target_pairs={{0,2},{2,0},{1,3},{3,1},{4,6},{6,4},{5,7},{7,5},{8,10},{10,8},{9,1... | collective-permute-start | bytes 884744 | tf_op jit(solution)/shard_map/ppermute | solution.py:401
  40.8 1.8 %collective-permute-start.6 = (bf16[144,1024]{1,0:T(8,128)(2,1)S(1)}, bf16[144,1024]{1,0:T(8,128)(2,1)S(1)}, u32[]{:S(2)}, u32[]{:S(2)}) collective-permute-start(bf16[144,1024]{1,0:T(8,128)(2,1)S(1)} %collective-permute-done.2.refs_3_), channel_id=1, source_target_pairs={{0,2},{2,0},{1,3},{3,1},{4,6},{6,4},{5,7},{7,5},{8,10},{10,8},{9,1... | collective-permute-start | bytes 884744 | tf_op jit(solution)/shard_map/ppermute | solution.py:401
  41.5 18.1 %copy-start = (bf16[4,2,32,1152]{3,2,1,0:T(8,128)(2,1)}, bf16[4,2,32,1152]{3,2,1,0:T(8,128)(2,1)S(1)}, u32[]{:S(2)}) copy-start(bf16[4,2,32,1152]{3,2,1,0:T(8,128)(2,1)S(1)} %pad_maximum_fusion.refs_0_) | copy-start | bytes 1769476
  45.0 15.8 %copy-start.19 = (bf16[1024,1024]{1,0:T(8,128)(2,1)}, bf16[1024,1024]{1,0:T(8,128)(2,1)S(1)}, u32[]{:S(2)}) copy-start(bf16[1024,1024]{1,0:T(8,128)(2,1)S(1)} %get-tuple-element.31.normed_ref) | copy-start | bytes 6291460
  45.0 14.6 %collective-permute-start.14 = (bf16[4,2,32,1152]{3,2,1,0:T(8,128)(2,1)S(1)}, bf16[4,2,32,1152]{3,2,1,0:T(8,128)(2,1)S(1)}, u32[]{:S(2)}, u32[]{:S(2)}) collective-permute-start(bf16[4,2,32,1152]{3,2,1,0:T(8,128)(2,1)S(1)} %pad_maximum_fusion.refs_0_), channel_id=1, source_target_pairs={{0,1},{1,0},{2,3},{3,2},{4,5},{5,4},{6,7},{7,6},{8,9},{9,8},{10,11... | collective-permute-start | bytes 1769480 | tf_op jit(solution)/shard_map/ppermute | solution.py:401
  46.3 7.7 %collective-permute-start.12 = (bf16[128,256]{1,0:T(8,128)(2,1)S(1)}, bf16[128,256]{1,0:T(8,128)(2,1)S(1)}, u32[]{:S(2)}, u32[]{:S(2)}) collective-permute-start(bf16[128,256]{1,0:T(8,128)(2,1)S(1)} %get-tuple-element.37), channel_id=1, source_target_pairs={{0,16},{1,17},{2,18},{3,19},{4,20},{5,21},{6,22},{7,23},{8,24},{9,... | collective-permute-start | bytes 196616 | tf_op jit(solution)/shard_map/ppermute | solution.py:494
  50.1 6.6 %collective-permute-start.13 = (bf16[128,256]{1,0:T(8,128)(2,1)S(1)}, bf16[128,256]{1,0:T(8,128)(2,1)S(1)}, u32[]{:S(2)}, u32[]{:S(2)}) collective-permute-start(bf16[128,256]{1,0:T(8,128)(2,1)S(1)} %get-tuple-element.38), channel_id=1, source_target_pairs={{16,0},{17,1},{18,2},{19,3},{20,4},{21,5},{22,6},{23,7},{24,8},{25... | collective-permute-start | bytes 196616 | tf_op jit(solution)/shard_map/ppermute | solution.py:495
  56.7 4.1 %copy-start.9 = (bf16[128,256]{1,0:T(8,128)(2,1)}, bf16[128,256]{1,0:T(8,128)(2,1)S(1)}, u32[]{:S(2)}) copy-start(bf16[128,256]{1,0:T(8,128)(2,1)S(1)} %collective-permute-done.13.high_ref) | copy-start | bytes 196612
  59.6 7.5 %collective-permute-start.16 = (bf16[4,2,32,1152]{3,2,1,0:T(8,128)(2,1)S(1)}, bf16[4,2,32,1152]{3,2,1,0:T(8,128)(2,1)S(1)}, u32[]{:S(2)}, u32[]{:S(2)}) collective-permute-start(bf16[4,2,32,1152]{3,2,1,0:T(8,128)(2,1)S(1)} %pad_maximum_fusion.refs_0_), channel_id=1, source_target_pairs={{0,2},{2,0},{1,3},{3,1},{4,6},{6,4},{5,7},{7,5},{8,10},{10,8},{9,1... | collective-permute-start | bytes 1769480 | tf_op jit(solution)/shard_map/ppermute | solution.py:401
  60.8 7.1 %collective-permute-start.17 = (bf16[4,2,32,1152]{3,2,1,0:T(8,128)(2,1)S(1)}, bf16[4,2,32,1152]{3,2,1,0:T(8,128)(2,1)S(1)}, u32[]{:S(2)}, u32[]{:S(2)}) collective-permute-start(bf16[4,2,32,1152]{3,2,1,0:T(8,128)(2,1)S(1)} %collective-permute-done.14.refs_1_), channel_id=1, source_target_pairs={{0,2},{2,0},{1,3},{3,1},{4,6},{6,4},{5,7},{7,5},{8,10},{10,8},{9,1... | collective-permute-start | bytes 1769480 | tf_op jit(solution)/shard_map/ppermute | solution.py:401
  60.8 0.8 copy-start.2
  61.7 14.3 %all-to-all-start.1 = ((bf16[16,64,128]{2,1,0:T(8,128)(2,1)}), bf16[16,64,128]{2,1,0:T(8,128)(2,1)S(1)}, u32[]{:S(2)}, u32[]{:S(2)}) async-start(bf16[16,64,128]{2,1,0:T(8,128)(2,1)} %bitcast.12), calls=%async_computation.1 | async-start | bytes 524288 | tf_op jit(solution)/shard_map/all_to_all | solution.py:397
  65.6 10.3 %copy-start.18 = (f32[128]{0:T(128)S(1)}, f32[128]{0:T(128)}, u32[]{:S(2)}) copy-start(f32[128]{0:T(128)} %param.12) | copy-start | bytes 1540
  65.7 9.6 %collective-permute-start.15 = (bf16[1,64,1024]{2,1,0:T(8,128)(2,1)}, bf16[1,64,1024]{2,1,0:T(8,128)(2,1)S(1)}, u32[]{:S(2)}, u32[]{:S(2)}) collective-permute-start(bf16[1,64,1024]{2,1,0:T(8,128)(2,1)} %get-tuple-element.42), channel_id=1, source_target_pairs={{0,1},{1,0},{2,3},{3,2},{4,5},{5,4},{6,7},{7,6},{8,9},{9,8},{10,11... | collective-permute-start | bytes 393224 | tf_op jit(solution)/shard_map/ppermute | solution.py:401
  67.1 0.8 copy-start.4
  67.9 0.8 copy-start.6
  68.7 1.1 copy-start.1
  69.8 1.1 copy-start.3
  70.9 1.1 copy-start.5
  71.9 1.1 copy-start.7
  75.3 0.7 copy-start.12
  75.9 16.3 %copy-start.10 = (bf16[128,256]{1,0:T(8,128)(2,1)S(1)}, bf16[128,256]{1,0:T(8,128)(2,1)}, u32[]{:S(2)}) copy-start(bf16[128,256]{1,0:T(8,128)(2,1)} %copy-done.9) | copy-start | bytes 196612
  75.9 0.9 copy-start.11
  76.9 0.9 copy-start.13
  77.8 0.8 copy-start.16
  81.1 21.9 %copy-start.14 = (f32[100,128]{1,0:T(8,128)}, f32[100,128]{1,0:T(8,128)S(1)}, u32[]{:S(2)}) copy-start(f32[100,128]{1,0:T(8,128)S(1)} %get-tuple-element.50) | copy-start | bytes 153604
  81.1 24.4 %copy-start.20 = (bf16[1024,1024]{1,0:T(8,128)(2,1)S(1)}, bf16[1024,1024]{1,0:T(8,128)(2,1)}, u32[]{:S(2)}) copy-start(bf16[1024,1024]{1,0:T(8,128)(2,1)} %copy-done.19) | copy-start | bytes 6291460
  93.6 9.4 %collective-permute-start.18 = (bf16[128,256]{1,0:T(8,128)(2,1)S(1)}, bf16[128,256]{1,0:T(8,128)(2,1)S(1)}, u32[]{:S(2)}, u32[]{:S(2)}) collective-permute-start(bf16[128,256]{1,0:T(8,128)(2,1)S(1)} %get-tuple-element.46), channel_id=1, source_target_pairs={{0,16},{1,17},{2,18},{3,19},{4,20},{5,21},{6,22},{7,23},{8,24},{9,... | collective-permute-start | bytes 196616 | tf_op jit(solution)/shard_map/ppermute | solution.py:561
  97.7 7.9 %collective-permute-start.19 = (bf16[128,256]{1,0:T(8,128)(2,1)S(1)}, bf16[128,256]{1,0:T(8,128)(2,1)S(1)}, u32[]{:S(2)}, u32[]{:S(2)}) collective-permute-start(bf16[128,256]{1,0:T(8,128)(2,1)S(1)} %get-tuple-element.47), channel_id=1, source_target_pairs={{16,0},{17,1},{18,2},{19,3},{20,4},{21,5},{22,6},{23,7},{24,8},{25... | collective-permute-start | bytes 196616 | tf_op jit(solution)/shard_map/ppermute | solution.py:562
  105.5 5.2 %copy-start.15 = (f32[100,128]{1,0:T(8,128)S(1)}, f32[100,128]{1,0:T(8,128)}, u32[]{:S(2)}) copy-start(f32[100,128]{1,0:T(8,128)} %copy-done.14) | copy-start | bytes 153604
  107.6 19.0 %all-to-all-start.3 = ((bf16[32,32,256]{2,1,0:T(8,128)(2,1)}), bf16[32,32,256]{2,1,0:T(8,128)(2,1)S(1)}, u32[]{:S(2)}, u32[]{:S(2)}) async-start(bf16[32,32,256]{2,1,0:T(8,128)(2,1)} %bitcast.16), calls=%async_computation.3 | async-start | bytes 1048576 | tf_op jit(solution)/shard_map/all_to_all | solution.py:397
  110.7 6.0 %collective-permute-start.20 = (f32[100,128]{1,0:T(8,128)S(1)}, f32[100,128]{1,0:T(8,128)S(1)}, u32[]{:S(2)}, u32[]{:S(2)}) collective-permute-start(f32[100,128]{1,0:T(8,128)S(1)} %copy-done.15), channel_id=1, source_target_pairs={{0,1},{1,0},{2,3},{3,2},{4,5},{5,4},{6,7},{7,6},{8,9},{9,8},{10,11... | collective-permute-start | bytes 153608 | tf_op jit(solution)/shard_map/ppermute | solution.py:401

commit v7 on v6

--- a/solution.py
+++ b/solution.py
@@ -128,11 +128,18 @@
     return [(quad ^ step) * CORES + (core ^ flip) for flip in range(CORES) for step in range(QUAD)]
 
 
-def project_kernel(where_ref, *refs):
+def put_rims(where_ref, rims, first, last):
+    if len(rims) == 1:
+        rims[0][...] = jnp.where(where_ref[4] == 0, last, first)
+    else:
+        rims[0][...], rims[1][...] = first, last
+
+
+def project_kernel(parts, where_ref, *refs):
     blocks, refs = refs[:GROUP], refs[GROUP:]
-    columns, refs = refs[:-10], refs[-10:]
-    q_ref, kv_ref, steps_ref, first_ref, last_ref, normed_any = refs[:6]
-    notes, normed, w, sems = refs[6:]
+    columns, refs = refs[:parts], refs[parts:]
+    q_ref, kv_ref, steps_ref, normed_any, *rims = refs[:-4]
+    notes, normed, w, sems = refs[-4:]
     block = blocks[0].shape[0] - NOTE_ROWS
     pairs = []
     for at, (rows_ref, owner) in enumerate(zip(blocks, owners(where_ref))):
@@ -154,25 +161,23 @@
     q_ref[...] = projected[:, :COLS]
     kv_ref[...] = projected[:, COLS:]
     last = GROUP * block - RIM
-    first_ref[...] = projected[:RIM, COLS:]
-    last_ref[...] = projected[last:, COLS:]
+    put_rims(where_ref, rims, projected[:RIM, COLS:], projected[last:, COLS:])
     steps_ref[...] = notes[...].astype(F32)
     keep.wait()
 
 
-def weights_kernel(where_ref, *refs):
-    pieces, (w_ref, sems) = refs[:-2], refs[-2:]
+def assemble_kernel(where_ref, *refs):
+    pieces, refs = refs[:GROUP], refs[GROUP:]
+    sources, (truth_any, w_ref, source_ref, truth_ref, sems) = refs[:-5], refs[-5:]
     core, quad, ens = where_ref[0], where_ref[1], where_ref[2]
-    pairs = []
-    if len(pieces) == GROUP:
-        for at, piece in enumerate(pieces):
-            place = (quad ^ (at % QUAD), core ^ (at // QUAD))
-            pairs.append((piece, w_ref.at[:, place[0], place[1], 0]))
+    pairs = [(truth_any, truth_ref)]
+    if len(sources) == 1:
+        pairs.append((sources[0], source_ref))
     else:
-        for at, piece in enumerate(pieces):
-            for step in range(QUAD):
-                place = (quad ^ step, core ^ (at // 2), ens ^ (at % 2))
-                pairs.append((piece.at[step], w_ref.at[:, place[0], place[1], place[2]]))
+        for step, part in enumerate(sources):
+            pairs.append((part.at[0], source_ref.at[ens ^ step]))
+    for at, piece in enumerate(pieces):
+        pairs.append((piece, w_ref.at[:, quad ^ (at % QUAD), core ^ (at // QUAD)]))
     for copy in fetch(pairs, sems):
         copy.wait()
 
@@ -250,14 +255,15 @@
 
 
 def edge_back_kernel(
-    steps_ref, q_ref, kv_ref, low_ref, high_ref, g_ref, rim_low_ref, rim_high_ref, part_ref
+    where_ref, steps_ref, q_ref, kv_ref, low_ref, high_ref, g_ref, part_ref, *rims
 ):
+    outer = []
     step = PAIR * TILE
     count = q_ref.shape[0]
     first = jnp.concatenate([low_ref[...], kv_ref[: 2 * step, :]], axis=0)
     last = jnp.concatenate([kv_ref[count - 2 * step :, :], high_ref[...]], axis=0)
     pairs = count // step
-    for edge, pair, window, rim_ref in ((0, 0, first, rim_low_ref), (1, pairs - 1, last, rim_high_ref)):
+    for edge, pair, window in ((0, 0, first), (1, pairs - 1, last)):
         rows = slice(pair * step, (pair + 1) * step)
         grads = attend_back(
             steps_ref, pair, q_ref[rows, :], g_ref[rows, :], window[:, :COLS], window[:, COLS:]
@@ -266,8 +272,9 @@
         own = slice(RIM, WINDOW) if edge == 0 else slice(0, WINDOW - RIM)
         for at, grad in enumerate(grads):
             columns = slice(at * COLS, (at + 1) * COLS)
-            rim_ref[:, columns] = grad[rim].astype(BF16)
             part_ref[edge, :, columns] = grad[own]
+        outer.append(jnp.concatenate([grad[rim].astype(BF16) for grad in grads], axis=1))
+    put_rims(where_ref, rims, *outer)
 
 
 def interior_back_kernel(steps_ref, q_ref, kv_ref, g_ref, part_ref, out_ref):
@@ -298,27 +305,9 @@
 
 
 def mix_kernel(
-    where_ref,
-    att_ref,
-    kept_ref,
-    sent_ref,
-    w,
-    truth_ref,
-    factor_ref,
-    pred_ref,
-    grad_ref,
-    a,
-    source,
-    truth,
+    where_ref, att_ref, source_ref, w, truth_ref, factor_ref, pred_ref, grad_ref, a, truth
 ):
-    part = kept_ref.shape[1]
-    members_num = a.shape[0] // part
-    if members_num == 2:
-        for step, rows_ref in enumerate((kept_ref, sent_ref)):
-            place = pl.multiple_of((where_ref[2] ^ step) * part, part)
-            source[pl.ds(place, part), :] = rows_ref[0]
-    else:
-        source[...] = sent_ref[...].reshape(source.shape)
+    members_num, part, _ = source_ref.shape
     for g in range(GROUP):
         for m in range(members_num):
             a[m * part : (m + 1) * part, g * COLS : (g + 1) * COLS] = att_ref[g * members_num + m]
@@ -333,7 +322,8 @@
     truth[:FIELD_NUM, :] = own_truth
     both = w[...].reshape(LATENT_DIM, LATENT_DIM + FIELD_PAD)
     mix, readout = both[:, :LATENT_DIM], both[:, LATENT_DIM:]
-    hidden = source[...].astype(F32) + jnp.dot(a[...], mix, preferred_element_type=F32)
+    source = source_ref[...].reshape(a.shape).astype(F32)
+    hidden = source + jnp.dot(a[...], mix, preferred_element_type=F32)
     inverse = lax.rsqrt(jnp.mean(hidden * hidden, axis=-1, keepdims=True) + NORM_EPS)
     decoded = (hidden * inverse).astype(BF16)
     prediction = lax.dot_general(
@@ -362,14 +352,16 @@
             ]
 
 
-def product_kernel(normed_ref, from_low_ref, from_high_ref, grads_ref, out_ref):
+def product_kernel(where_ref, normed_ref, from_low_ref, from_high_ref, grads_ref, out_ref):
     count = normed_ref.shape[0]
+    from_low = jnp.where(where_ref[4] > 0, from_low_ref[...].astype(F32), 0.0)
+    from_high = jnp.where(where_ref[4] < where_ref[5], from_high_ref[...].astype(F32), 0.0)
     grads = grads_ref[...]
     grads = jnp.concatenate(
         [
-            grads[:RIM] + from_low_ref[...].astype(F32),
+            grads[:RIM] + from_low,
             grads[RIM : count - RIM],
-            grads[count - RIM :] + from_high_ref[...].astype(F32),
+            grads[count - RIM :] + from_high,
         ],
         axis=0,
     )
@@ -421,7 +413,8 @@
     down = [(target, source) for source, target in up]
     core, quad, ens = (lax.axis_index(axis) for axis in ("core", "quad", "ens"))
     first_tile = lax.axis_index(("half", "quad", "core")) * neighbours.shape[0]
-    where = jnp.stack([core, quad, ens, first_tile]).astype(jnp.int32)
+    half = lax.axis_index("half")
+    where = jnp.stack([core, quad, ens, first_tile, half, halves - 1]).astype(jnp.int32)
     width = LATENT_DIM + FIELD_PAD
     paired = members_num == 2
     copies = 1 if paired else members_num
@@ -457,26 +450,25 @@
         columns = [columns[0].reshape(LATENT_DIM, 3 * COLS)]
     far = [swap(piece, "core", 1) for piece in near]
 
+    packed = in_order(packed, "ens", 1).reshape(halves, members_num * shard, width)
     if paired:
-        kept, sent = sources[0], swap(sources[1], "ens", 1)
-        packed, columns[0] = lax.optimization_barrier((packed, columns[0]))
-        pieces = [packed] + [swap(packed, "quad", step) for step in range(1, QUAD)]
+        sources = [sources[0], swap(sources[1], "ens", 1)]
+        columns[1], sources[1] = lax.optimization_barrier((columns[1], sources[1]))
     else:
-        kept = sent = exchange(sources[0], "ens")
-        packed = in_order(packed, "ens", 1).reshape(halves, members_num * shard, width)
-        pieces = [packed] + [swap(packed, "quad", step) for step in range(1, QUAD)]
-
-    queries, own, steps, first, last, normed = call(
-        project_kernel,
+        sources = [exchange(sources[0], "ens")]
+
+    rim = ((RIM, 2 * COLS), BF16)
+    rims = [rim] if halves == 2 else [rim, rim]
+    queries, own, steps, normed, *inner = call(
+        functools.partial(project_kernel, len(columns)),
         "project",
         [
             ((rows, COLS), BF16),
             ((rows, 2 * COLS), BF16),
             ((GROUP, NOTE_ROWS, 128), F32),
-            ((RIM, 2 * COLS), BF16),
-            ((RIM, 2 * COLS), BF16),
             ((rows, LATENT_DIM), BF16),
-        ],
+        ]
+        + rims,
         "s" + "a" * (GROUP + len(columns)),
         [
             pltpu.VMEM((GROUP, NOTE_ROWS, 128), BF16),
@@ -489,14 +481,16 @@
         flops=rows * LATENT_DIM * 6 * COLS,
         moved=4 * 2**20,
         room=14,
-        results="vvvvva",
+        results="vvvavv"[: 4 + len(rims)],
     )(where, *near, *far, *columns)
-    low = lax.ppermute(last, "half", up)
-    high = lax.ppermute(first, "half", down)
-    if paired:
-        pieces = jnp.stack(pieces)
-        pieces, own = lax.optimization_barrier((pieces, own))
-        pieces = [pieces, swap(pieces, "ens", 1)]
+
+    def across(inner):
+        if halves == 2:
+            got = swap(inner[0], "half", 1)
+            return got, got
+        return lax.ppermute(inner[1], "half", up), lax.ppermute(inner[0], "half", down)
+
+    low, high = across(inner)
 
     (outcome,) = call(
         interior_kernel,
@@ -516,50 +510,49 @@
         moved=2**20,
         exps=rows * 128,
     )(steps, queries, own, low, high, outcome)
-    *pieces, outcome = lax.optimization_barrier((*pieces, outcome))
+    packed, own = lax.optimization_barrier((packed, own))
+    pieces = [packed] + [swap(packed, "quad", step) for step in range(1, QUAD)]
+    pieces = pieces + [swap(piece, "core", 1) for piece in pieces]
     attended = exchange(outcome.reshape(GROUP * members_num, part, COLS), ("quad", "core", "ens"))
-    pieces = pieces + [swap(piece, "core", 1) for piece in pieces]
-    block = (halves, QUAD, CORES) + ((2, shard) if paired else (1, members_num * shard)) + (width,)
-    (weights,) = call(
-        weights_kernel,
-        "weights",
-        [(block, BF16)],
-        "s" + "a" * len(pieces),
-        [pltpu.SemaphoreType.DMA((4 * QUAD,))],
+    weights, sources, truth = call(
+        assemble_kernel,
+        "assemble",
+        [
+            ((halves, QUAD, CORES, members_num * shard, width), BF16),
+            ((members_num, part, LATENT_DIM), BF16),
+            (observed_truth.shape, F32),
+        ],
+        "s" + "a" * (len(pieces) + len(sources) + 1),
+        [pltpu.SemaphoreType.DMA((GROUP + len(sources) + 1,))],
         moved=4 * 2**20,
-    )(where, *pieces)
+        room=48,
+    )(where, *pieces, *sources, observed_truth)
 
     prediction, grads = call(
         mix_kernel,
         "mix_loss_backward",
         [((FIELD_NUM, node_rows), F32), ((GROUP * members_num, part, COLS), BF16)],
-        "svvvvvv",
-        [
-            pltpu.VMEM((node_rows, LATENT_DIM), BF16),
+        "svvvvv",
+        [
             pltpu.VMEM((node_rows, LATENT_DIM), BF16),
             pltpu.VMEM((FIELD_PAD, node_rows), F32),
         ],
         flops=node_rows * LATENT_DIM * 4 * width,
         moved=2**22,
         room=14,
-    )(where, attended, kept, sent, weights, observed_truth, cell_surface_factor[None])
+    )(where, attended, sources, weights, truth, cell_surface_factor[None])
     grads = exchange(grads, ("quad", "core", "ens")).reshape(rows, COLS)
 
-    rim_low, rim_high, edges = call(
+    edges, *inner = call(
         edge_back_kernel,
         "attention_edges_back",
-        [
-            ((RIM, 2 * COLS), BF16),
-            ((RIM, 2 * COLS), BF16),
-            ((2, WINDOW - RIM, 2 * COLS), F32),
-        ],
-        "vvvvvv",
+        [((2, WINDOW - RIM, 2 * COLS), F32)] + rims,
+        "svvvvvv",
         flops=rows * COLS * 1280,
         moved=2**20,
         exps=rows * 128,
-    )(steps, queries, own, low, high, grads)
-    from_low = lax.ppermute(rim_high, "half", up)
-    from_high = lax.ppermute(rim_low, "half", down)
+    )(where, steps, queries, own, low, high, grads)
+    from_low, from_high = across(inner)
     (kv_grads,) = call(
         interior_back_kernel,
         "attention_interior_back",
@@ -574,11 +567,11 @@
         product_kernel,
         "product",
         [((LATENT_DIM, 2 * COLS), BF16)],
-        "vvvv",
+        "svvvv",
         flops=rows * LATENT_DIM * 8 * COLS,
         moved=2**22,
         room=16,
-    )(normed, from_low, from_high, kv_grads)
+    )(where, normed, from_low, from_high, kv_grads)
     term, prediction = lax.optimization_barrier((term, prediction))
     term = exchange(term.reshape(-1, shard, 2 * COLS), everyone)
     (grad_kv,) = call(

time: 128 us -> 132 us (1.031)
  local copies, waits for them, and re-layouts: 10.8 us -> 16.2 us
  starting transfers between devices: 41.8 us -> 38.6 us
    ppermute x17 -> x21, waiting for transfers between devices: 16.5 us -> 28.8 us  [swap(): lax.ppermute(value, axis, [(i, i ^ step) for i in range(lax.axis_size(axi...]
    ppermute x4 -> x0, starting transfers between devices: 10.6 us -> none  [the longest x1 4.04 us: body(): from_low = lax.ppermute(rim_high, 'half', up)]
    all_to_all x3, waiting for transfers between devices: 16.9 us -> 10.1 us  [exchange(): return lax.all_to_all(chunks, axes, 0, 0)]
    ppermute x4 -> x0, waiting for transfers between devices: 5.21 us -> none  [the longest x1 2.72 us: body(): high = lax.ppermute(first, 'half', down)]
    unnamed x43 -> x51, local copies, waits for them, and re-layouts: 10.7 us -> 15.5 us
    all_to_all x3, starting transfers between devices: 11.8 us -> 16.2 us  [exchange(): return lax.all_to_all(chunks, axes, 0, 0)]
    ppermute x17 -> x21, starting transfers between devices: 19.4 us -> 22.4 us  [swap(): lax.ppermute(value, axis, [(i, i ^ step) for i in range(lax.axis_size(axi...]
  transfers between devices with their start and end apart: 24 -> 24, of which waited for: 12 -> 8; matrix products, arithmetic and copies ran while one was open for 1% -> 1% of each run, Pallas kernels for 8% -> 7%
where the time goes in v7:
time: 132 us; the launch traced here: 131 us
  waiting for transfers between devices  39 us (30%)
  starting transfers between devices  38.6 us (29%)
  Pallas kernels  23.1 us (18%)
  local copies, waits for them, and re-layouts  16.2 us (12%)
  blocking collectives  11.9 us (9%)
    ppermute x21, waiting for transfers between devices, swap(): lax.ppermute(value, axis, [(i, i ^ step) for i in range(lax.axis_size(axi...  28.8 us
    ppermute x21, starting transfers between devices, swap(): lax.ppermute(value, axis, [(i, i ^ step) for i in range(lax.axis_size(axi...  22.4 us
    all_to_all x3, starting transfers between devices, exchange(): return lax.all_to_all(chunks, axes, 0, 0)  16.2 us
    unnamed x51, local copies, waits for them, and re-layouts  15.5 us
    all_to_all x1, blocking collectives, exchange(): return lax.all_to_all(chunks, axes, 0, 0)  11.9 us
    all_to_all x3, waiting for transfers between devices, exchange(): return lax.all_to_all(chunks, axes, 0, 0)  10.1 us
    pallas_call x1, Pallas kernels, body(): call(interior_back_kernel, 'attention_interior_back', [((rows, 2 * COLS),...  3.87 us
    pallas_call x1, Pallas kernels, body(): call(prepare_kernel, 'prepare', [((node_rows + NOTE_ROWS, LATENT_DIM), BF...  2.97 us
  transfers between devices with their start and end apart: 24, of which 8 were waited for; matrix products, arithmetic and copies ran while one was open for 1% of the time, Pallas kernels for 7%

profile of v7, /device:TPU:1, one launch (start us, length us, event | category | flops | bytes accessed | tf_op | source)
XLA Modules:
  0.0 130.7 jit_solution(15554106274712017073)
XLA Ops:
  1.3 3.0 %prepare.1 = (bf16[144,1024]{1,0:T(8,128)(2,1)}, bf16[2,8,1,32,384]{4,3,2,1,0:T(8,128)(2,1)}, bf16[32,1152]{1,0:T(8,128)(2,1)}, bf16[1,64,1024]{2,1,0:T(8,128)(2,1)}, bf16[1,64,1024]{2,1,0:T(8,128)(2,1)}) custom-call(s32[6]{0:T(128)} %stack.41.where_ref, s32[2,4]{1,0:T(2,128)} %near_ref.1, bf16[128,1024]{1,0:T(8,128)(2,1)} %bitcast.33, ...), custom_call_target="tpu_custom_call" | custom-call | flops 1048576 | bytes 1048576 | tf_op jit(solution)/shard_map/prepare/pallas_call | solution.py:422
  4.2 3.2 %collective-permute-start.9 = (bf16[32,1152]{1,0:T(8,128)(2,1)}, bf16[32,1152]{1,0:T(8,128)(2,1)S(1)}, u32[]{:S(2)}, u32[]{:S(2)}) collective-permute-start(bf16[32,1152]{1,0:T(8,128)(2,1)} %get-tuple-element.32), channel_id=1, source_target_pairs={{0,16},{16,0},{1,17},{17,1},{2,18},{18,2},{3,19},{19,3},{4,20},{20... | collective-permute-start | bytes 221192 | tf_op jit(solution)/shard_map/ppermute | solution.py:393
  7.4 1.2 collective-permute-start
  8.7 1.3 collective-permute-start.1
  10.1 5.6 %all-to-all-start = ((bf16[16,32,384]{2,1,0:T(8,128)(2,1)}), bf16[16,32,384]{2,1,0:T(8,128)(2,1)S(1)}, u32[]{:S(2)}, u32[]{:S(2)}) async-start(bf16[16,32,384]{2,1,0:T(8,128)(2,1)} %bitcast.32), calls=%async_computation | async-start | bytes 786432 | tf_op jit(solution)/shard_map/all_to_all | solution.py:389
  15.7 0.9 select_bitcast_fusion.3
  16.7 1.3 collective-permute-start.10
  18.2 6.7 %collective-permute-done.8.refs_9_ = bf16[1,64,1024]{2,1,0:T(8,128)(2,1)S(1)} collective-permute-done((bf16[1,64,1024]{2,1,0:T(8,128)(2,1)}, bf16[1,64,1024]{2,1,0:T(8,128)(2,1)S(1)}, u32[]{:S(2)}, u32[]{:S(2)}) %collective-permute-start.8) | collective-permute-done | bytes 131104 | tf_op jit(solution)/shard_map/ppermute | solution.py:393
  25.6 0.9 collective-permute-start.3
  27.0 2.6 %collective-permute-start.6 = (bf16[144,1024]{1,0:T(8,128)(2,1)S(1)}, bf16[144,1024]{1,0:T(8,128)(2,1)S(1)}, u32[]{:S(2)}, u32[]{:S(2)}) collective-permute-start(bf16[144,1024]{1,0:T(8,128)(2,1)S(1)} %collective-permute-done.2.refs_3_), channel_id=1, source_target_pairs={{0,2},{2,0},{1,3},{3,1},{4,6},{6,4},{5,7},{7,5},{8,10},{10,8},{9,1... | collective-permute-start | bytes 884744 | tf_op jit(solution)/shard_map/ppermute | solution.py:393
  29.5 1.0 all-to-all-done.refs_8_
  30.6 1.2 collective-permute-start.7
  31.9 7.4 %collective-permute-done.7.refs_9_ = bf16[16,32,384]{2,1,0:T(8,128)(2,1)S(1)} collective-permute-done((bf16[16,32,384]{2,1,0:T(8,128)(2,1)S(1)}, bf16[16,32,384]{2,1,0:T(8,128)(2,1)S(1)}, u32[]{:S(2)}, u32[]{:S(2)}) %collective-permute-start.7) | collective-permute-done | bytes 393248 | tf_op jit(solution)/shard_map/ppermute | solution.py:393
  39.4 0.7 copy-done.9
  40.8 1.0 copy-done.10
  41.8 1.0 copy-done.12
  42.7 2.4 %project.1 = (bf16[1024,128]{1,0:T(8,128)(2,1)S(1)}, bf16[1024,256]{1,0:T(8,128)(2,1)S(1)}, f32[8,16,128]{2,1,0:T(8,128)S(1)}, bf16[1024,1024]{1,0:T(8,128)(2,1)S(1)}, bf16[128,256]{1,0:T(8,128)(2,1)S(1)}) custom-call(s32[6]{0:T(128)S(1)} %copy-done.21, bf16[144,1024]{1,0:T(8,128)(2,1)S(1)} %copy-done.8, bf16[144,1024]{1,0:T(8,128)(2,1)S(1)} %collective-permute-done.refs_1_, ...), custom_call_target="tpu_custom_call" | custom-call | flops 805306368 | bytes 4194304 | tf_op jit(solution)/shard_map/project/pallas_call | solution.py:462
  45.1 3.3 %collective-permute-start.12 = (bf16[2,64,1152]{2,1,0:T(8,128)(2,1)S(1)}, bf16[2,64,1152]{2,1,0:T(8,128)(2,1)S(1)}, u32[]{:S(2)}, u32[]{:S(2)}) collective-permute-start(bf16[2,64,1152]{2,1,0:T(8,128)(2,1)S(1)} %bitcast.26), channel_id=1, source_target_pairs={{0,4},{4,0},{8,12},{12,8},{1,5},{5,1},{9,13},{13,9},{2,6},{6,2},{1... | collective-permute-start | bytes 884744 | tf_op jit(solution)/shard_map/ppermute | solution.py:393
  48.6 1.1 collective-permute-start.14
  49.7 2.1 %collective-permute-start.11 = (bf16[128,256]{1,0:T(8,128)(2,1)S(1)}, bf16[128,256]{1,0:T(8,128)(2,1)S(1)}, u32[]{:S(2)}, u32[]{:S(2)}) collective-permute-start(bf16[128,256]{1,0:T(8,128)(2,1)S(1)} %get-tuple-element.35), channel_id=1, source_target_pairs={{0,16},{16,0},{1,17},{17,1},{2,18},{18,2},{3,19},{19,3},{4,20},{20... | collective-permute-start | bytes 196616 | tf_op jit(solution)/shard_map/ppermute | solution.py:393
  51.8 2.6 %attention_interior.1.done_ref = bf16[1024,128]{1,0:T(8,128)(2,1)S(1)} custom-call(f32[8,16,128]{2,1,0:T(8,128)S(1)} %get-tuple-element.30.steps_ref, bf16[1024,128]{1,0:T(8,128)(2,1)S(1)} %get-tuple-element.31.q_ref, bf16[1024,256]{1,0:T(8,128)(2,1)S(1)} %get-tuple-element.34.kv_ref), custom_call_target="tpu_custom_call" | custom-call | flops 268435456 | bytes 2097152 | tf_op jit(solution)/shard_map/attention_interior/pallas_call | solution.py:495
  54.4 7.8 %collective-permute-done.11.low_ref.high_ref = bf16[128,256]{1,0:T(8,128)(2,1)S(1)} collective-permute-done((bf16[128,256]{1,0:T(8,128)(2,1)S(1)}, bf16[128,256]{1,0:T(8,128)(2,1)S(1)}, u32[]{:S(2)}, u32[]{:S(2)}) %collective-permute-start.11) | collective-permute-done | bytes 65568 | tf_op jit(solution)/shard_map/ppermute | solution.py:393
  62.2 1.7 %attention_edges.1 = bf16[1024,128]{1,0:T(8,128)(2,1)} custom-call(f32[8,16,128]{2,1,0:T(8,128)S(1)} %get-tuple-element.30.steps_ref, bf16[1024,128]{1,0:T(8,128)(2,1)S(1)} %get-tuple-element.31.q_ref, bf16[1024,256]{1,0:T(8,128)(2,1)S(1)} %get-tuple-element.34.kv_ref, bf16[128,256]{1,0:T(8,128)(2,1)S(1)} %collective-permute-done.11.low_ref.high_ref, ...), custom_call_target="tpu_custom_call" | custom-call | flops 67108864 | bytes 1048576 | tf_op jit(solution)/shard_map/attention_edges/pallas_call | solution.py:504
  63.9 7.8 %all-to-all-start.1 = ((bf16[16,64,128]{2,1,0:T(8,128)(2,1)}), bf16[16,64,128]{2,1,0:T(8,128)(2,1)}, u32[]{:S(2)}, u32[]{:S(2)}) async-start(bf16[16,64,128]{2,1,0:T(8,128)(2,1)} %bitcast.12), calls=%async_computation.1 | async-start | bytes 524288 | tf_op jit(solution)/shard_map/all_to_all | solution.py:389
  72.2 0.7 copy-done.2
  73.1 0.7 copy-done.4
  75.4 1.0 copy-done.3
  76.4 1.0 copy-done.5
  77.4 1.0 copy-done.7
  78.3 0.9 copy-done.15
  79.2 0.9 copy-done.17
  80.1 0.8 copy-done.18
  80.9 1.4 %assemble.1 = (bf16[2,4,2,64,1152]{4,3,2,1,0:T(8,128)(2,1)S(1)}, bf16[2,64,1024]{2,1,0:T(8,128)(2,1)S(1)}, f32[100,128]{1,0:T(8,128)S(1)}) custom-call(s32[6]{0:T(128)S(1)} %copy-done.21, bf16[2,64,1152]{2,1,0:T(8,128)(2,1)S(1)} %bitcast.30, bf16[2,64,1152]{2,1,0:T(8,128)(2,1)S(1)} %copy-done.3, bf16[2,64,1152]{2,1,0:T(8,128)(2,1)S(1)} %copy-done.5, ...), custom_call_target="tpu_custom_call" | custom-call | bytes 4194304 | tf_op jit(solution)/shard_map/assemble/pallas_call | solution.py:517
  82.3 0.7 copy-done.13
  83.7 1.0 copy-done.14
  84.7 0.8 copy-done.20
  85.5 2.9 %mix_loss_backward.1 = (f32[100,128]{1,0:T(8,128)S(1)}, bf16[16,64,128]{2,1,0:T(8,128)(2,1)S(1)}) custom-call(s32[6]{0:T(128)S(1)} %copy-done.21, bf16[16,64,128]{2,1,0:T(8,128)(2,1)} %all-to-all-done.1.att_ref, bf16[2,64,1024]{2,1,0:T(8,128)(2,1)S(1)} %copy-done.14, bf16[2,4,2,64,1152]{4,3,2,1,0:T(8,128)(2,1)S(1)} %get-tuple-element.40.w, ...), custom_call_target="tpu_custom_call" | custom-call | flops 603979776 | bytes 4194304 | tf_op jit(solution)/shard_map/mix_loss_backward/pallas_call | solution.py:531
  88.4 11.9 %all_to_all.20 = bf16[16,64,128]{2,1,0:T(8,128)(2,1)S(1)} all-to-all(bf16[16,64,128]{2,1,0:T(8,128)(2,1)S(1)} %get-tuple-element.42), channel_id=1, replica_groups=mesh['half'=2,'quad'=4,'core'=2,'ens'=2] {'quad','core','ens'}, dimensions={0} | all-to-all | bytes 524288 | tf_op jit(solution)/shard_map/all_to_all | solution.py:389
  100.3 1.9 %attention_edges_back.1 = (f32[2,256,256]{2,1,0:T(8,128)S(1)}, bf16[128,256]{1,0:T(8,128)(2,1)S(1)}) custom-call(s32[6]{0:T(128)S(1)} %copy-done.21, f32[8,16,128]{2,1,0:T(8,128)S(1)} %copy-done.1, bf16[1024,128]{1,0:T(8,128)(2,1)S(1)} %get-tuple-element.31.q_ref, bf16[1024,256]{1,0:T(8,128)(2,1)S(1)} %get-tuple-element.34.kv_ref, ...), custom_call_target="tpu_custom_call" | custom-call | flops 167772160 | bytes 1048576 | tf_op jit(solution)/shard_map/attention_edges_back/pallas_call | solution.py:546
  102.2 0.7 collective-permute-start.19
  103.0 3.9 %attention_interior_back.1.grads_ref = f32[1024,256]{1,0:T(8,128)S(1)} custom-call(f32[8,16,128]{2,1,0:T(8,128)S(1)} %copy-done.1, bf16[1024,128]{1,0:T(8,128)(2,1)S(1)} %get-tuple-element.31.q_ref, bf16[1024,256]{1,0:T(8,128)(2,1)S(1)} %get-tuple-element.34.kv_ref, bf16[1024,128]{1,0:T(8,128)(2,1)S(1)} %bitcast.24, ...), custom_call_target="tpu_custom_call" | custom-call | flops 536870912 | bytes 4194304 | tf_op jit(solution)/shard_map/attention_interior_back/pallas_call | solution.py:556
  106.8 1.7 %collective-permute-done.19.from_low_ref.from_high_ref = bf16[128,256]{1,0:T(8,128)(2,1)S(1)} collective-permute-done((bf16[128,256]{1,0:T(8,128)(2,1)S(1)}, bf16[128,256]{1,0:T(8,128)(2,1)S(1)}, u32[]{:S(2)}, u32[]{:S(2)}) %collective-permute-start.19) | collective-permute-done | bytes 65568 | tf_op jit(solution)/shard_map/ppermute | solution.py:393
  108.6 2.7 %product.1 = bf16[1024,256]{1,0:T(8,128)(2,1)} custom-call(s32[6]{0:T(128)S(1)} %copy-done.21, bf16[1024,1024]{1,0:T(8,128)(2,1)S(1)} %copy-done.24, bf16[128,256]{1,0:T(8,128)(2,1)S(1)} %collective-permute-done.19.from_low_ref.from_high_ref, bf16[128,256]{1,0:T(8,128)(2,1)S(1)} %collective-permute-done.19.from_low_ref.from_high_ref, ...), custom_call_target="tpu_custom_call" | custom-call | flops 1073741824 | bytes 4194304 | tf_op jit(solution)/shard_map/product/pallas_call | solution.py:566
  111.2 2.8 %all-to-all-start.3 = ((bf16[32,32,256]{2,1,0:T(8,128)(2,1)}), bf16[32,32,256]{2,1,0:T(8,128)(2,1)S(1)}, u32[]{:S(2)}, u32[]{:S(2)}) async-start(bf16[32,32,256]{2,1,0:T(8,128)(2,1)} %bitcast.16), calls=%async_computation.3 | async-start | bytes 1048576 | tf_op jit(solution)/shard_map/all_to_all | solution.py:389
  114.0 1.5 %collective-permute-start.20 = (f32[100,128]{1,0:T(8,128)S(1)}, f32[100,128]{1,0:T(8,128)S(1)}, u32[]{:S(2)}, u32[]{:S(2)}) collective-permute-start(f32[100,128]{1,0:T(8,128)S(1)} %get-tuple-element.46), channel_id=1, source_target_pairs={{0,1},{1,0},{2,3},{3,2},{4,5},{5,4},{6,7},{7,6},{8,9},{9,8},{10,11... | collective-permute-start | bytes 153608 | tf_op jit(solution)/shard_map/ppermute | solution.py:393
  115.5 4.5 %collective-permute-done.20 = f32[100,128]{1,0:T(8,128)S(1)} collective-permute-done((f32[100,128]{1,0:T(8,128)S(1)}, f32[100,128]{1,0:T(8,128)S(1)}, u32[]{:S(2)}, u32[]{:S(2)}) %collective-permute-start.20) | collective-permute-done | bytes 51232 | tf_op jit(solution)/shard_map/ppermute | solution.py:393
  120.9 9.1 %all-to-all-done.3 = bf16[32,32,256]{2,1,0:T(8,128)(2,1)S(1)} async-done(((bf16[32,32,256]{2,1,0:T(8,128)(2,1)}), bf16[32,32,256]{2,1,0:T(8,128)(2,1)S(1)}, u32[]{:S(2)}, u32[]{:S(2)}) %all-to-all-start.3) | async-done | bytes 524320 | tf_op jit(solution)/shard_map/all_to_all | solution.py:389
  129.9 0.8 gather_sums.1
  (72 shorter events, 7.0 us)
Async XLA Ops:
  1.3 39.6 %copy-start.21 = (s32[6]{0:T(128)S(1)}, s32[6]{0:T(128)}, u32[]{:S(2)}) copy-start(s32[6]{0:T(128)} %stack.41.where_ref) | copy-start | bytes 76
  4.2 36.6 %copy-start.8 = (bf16[144,1024]{1,0:T(8,128)(2,1)S(1)}, bf16[144,1024]{1,0:T(8,128)(2,1)}, u32[]{:S(2)}) copy-start(bf16[144,1024]{1,0:T(8,128)(2,1)} %get-tuple-element.25.refs_0_) | copy-start | bytes 884740
  4.2 11.5 %collective-permute-start.9 = (bf16[32,1152]{1,0:T(8,128)(2,1)}, bf16[32,1152]{1,0:T(8,128)(2,1)S(1)}, u32[]{:S(2)}, u32[]{:S(2)}) collective-permute-start(bf16[32,1152]{1,0:T(8,128)(2,1)} %get-tuple-element.32), channel_id=1, source_target_pairs={{0,16},{16,0},{1,17},{17,1},{2,18},{18,2},{3,19},{19,3},{4,20},{20... | collective-permute-start | bytes 221192 | tf_op jit(solution)/shard_map/ppermute | solution.py:393
  7.4 19.0 %collective-permute-start = (bf16[144,1024]{1,0:T(8,128)(2,1)}, bf16[144,1024]{1,0:T(8,128)(2,1)S(1)}, u32[]{:S(2)}, u32[]{:S(2)}) collective-permute-start(bf16[144,1024]{1,0:T(8,128)(2,1)} %get-tuple-element.25.refs_0_), channel_id=1, source_target_pairs={{0,4},{4,0},{8,12},{12,8},{1,5},{5,1},{9,13},{13,9},{2,6},{6,2},{1... | collective-permute-start | bytes 884744 | tf_op jit(solution)/shard_map/ppermute | solution.py:393
  8.7 17.8 %collective-permute-start.1 = (bf16[144,1024]{1,0:T(8,128)(2,1)}, bf16[144,1024]{1,0:T(8,128)(2,1)S(1)}, u32[]{:S(2)}, u32[]{:S(2)}) collective-permute-start(bf16[144,1024]{1,0:T(8,128)(2,1)} %get-tuple-element.25.refs_0_), channel_id=1, source_target_pairs={{0,8},{4,12},{8,0},{12,4},{1,9},{5,13},{9,1},{13,5},{2,10},{6,14},... | collective-permute-start | bytes 884744 | tf_op jit(solution)/shard_map/ppermute | solution.py:393
  10.0 17.0 %collective-permute-start.2 = (bf16[144,1024]{1,0:T(8,128)(2,1)}, bf16[144,1024]{1,0:T(8,128)(2,1)S(1)}, u32[]{:S(2)}, u32[]{:S(2)}) collective-permute-start(bf16[144,1024]{1,0:T(8,128)(2,1)} %get-tuple-element.25.refs_0_), channel_id=1, source_target_pairs={{0,12},{4,8},{8,4},{12,0},{1,13},{5,9},{9,5},{13,1},{2,14},{6,10},... | collective-permute-start | bytes 884744 | tf_op jit(solution)/shard_map/ppermute | solution.py:393
  10.1 20.5 %all-to-all-start = ((bf16[16,32,384]{2,1,0:T(8,128)(2,1)}), bf16[16,32,384]{2,1,0:T(8,128)(2,1)S(1)}, u32[]{:S(2)}, u32[]{:S(2)}) async-start(bf16[16,32,384]{2,1,0:T(8,128)(2,1)} %bitcast.32), calls=%async_computation | async-start | bytes 786432 | tf_op jit(solution)/shard_map/all_to_all | solution.py:389
  16.7 12.9 %collective-permute-start.10 = (bf16[2,32,1152]{2,1,0:T(8,128)(2,1)S(1)}, bf16[2,32,1152]{2,1,0:T(8,128)(2,1)S(1)}, u32[]{:S(2)}, u32[]{:S(2)}) collective-permute-start(bf16[2,32,1152]{2,1,0:T(8,128)(2,1)S(1)} %pad_maximum_fusion.1), channel_id=1, source_target_pairs={{0,1},{1,0},{2,3},{3,2},{4,5},{5,4},{6,7},{7,6},{8,9},{9,8},{10,11... | collective-permute-start | bytes 442376 | tf_op jit(solution)/shard_map/ppermute | solution.py:393
  18.0 7.0 %collective-permute-start.8 = (bf16[1,64,1024]{2,1,0:T(8,128)(2,1)}, bf16[1,64,1024]{2,1,0:T(8,128)(2,1)S(1)}, u32[]{:S(2)}, u32[]{:S(2)}) collective-permute-start(bf16[1,64,1024]{2,1,0:T(8,128)(2,1)} %get-tuple-element.27), channel_id=1, source_target_pairs={{0,1},{1,0},{2,3},{3,2},{4,5},{5,4},{6,7},{7,6},{8,9},{9,8},{10,11... | collective-permute-start | bytes 393224 | tf_op jit(solution)/shard_map/ppermute | solution.py:393
  24.9 0.6 copy-start.16
  25.6 13.8 %collective-permute-start.3 = (bf16[144,1024]{1,0:T(8,128)(2,1)}, bf16[144,1024]{1,0:T(8,128)(2,1)S(1)}, u32[]{:S(2)}, u32[]{:S(2)}) collective-permute-start(bf16[144,1024]{1,0:T(8,128)(2,1)} %get-tuple-element.25.refs_0_), channel_id=1, source_target_pairs={{0,2},{2,0},{1,3},{3,1},{4,6},{6,4},{5,7},{7,5},{8,10},{10,8},{9,1... | collective-permute-start | bytes 884744 | tf_op jit(solution)/shard_map/ppermute | solution.py:393
  26.5 12.9 %collective-permute-start.4 = (bf16[144,1024]{1,0:T(8,128)(2,1)S(1)}, bf16[144,1024]{1,0:T(8,128)(2,1)S(1)}, u32[]{:S(2)}, u32[]{:S(2)}) collective-permute-start(bf16[144,1024]{1,0:T(8,128)(2,1)S(1)} %collective-permute-done.refs_1_), channel_id=1, source_target_pairs={{0,2},{2,0},{1,3},{3,1},{4,6},{6,4},{5,7},{7,5},{8,10},{10,8},{9,1... | collective-permute-start | bytes 884744 | tf_op jit(solution)/shard_map/ppermute | solution.py:393
  26.5 12.9 %collective-permute-start.5 = (bf16[144,1024]{1,0:T(8,128)(2,1)S(1)}, bf16[144,1024]{1,0:T(8,128)(2,1)S(1)}, u32[]{:S(2)}, u32[]{:S(2)}) collective-permute-start(bf16[144,1024]{1,0:T(8,128)(2,1)S(1)} %collective-permute-done.1.refs_2_), channel_id=1, source_target_pairs={{0,2},{2,0},{1,3},{3,1},{4,6},{6,4},{5,7},{7,5},{8,10},{10,8},{9,1... | collective-permute-start | bytes 884744 | tf_op jit(solution)/shard_map/ppermute | solution.py:393
  27.0 13.1 %collective-permute-start.6 = (bf16[144,1024]{1,0:T(8,128)(2,1)S(1)}, bf16[144,1024]{1,0:T(8,128)(2,1)S(1)}, u32[]{:S(2)}, u32[]{:S(2)}) collective-permute-start(bf16[144,1024]{1,0:T(8,128)(2,1)S(1)} %collective-permute-done.2.refs_3_), channel_id=1, source_target_pairs={{0,2},{2,0},{1,3},{3,1},{4,6},{6,4},{5,7},{7,5},{8,10},{10,8},{9,1... | collective-permute-start | bytes 884744 | tf_op jit(solution)/shard_map/ppermute | solution.py:393
  30.6 8.8 %collective-permute-start.7 = (bf16[16,32,384]{2,1,0:T(8,128)(2,1)S(1)}, bf16[16,32,384]{2,1,0:T(8,128)(2,1)S(1)}, u32[]{:S(2)}, u32[]{:S(2)}) collective-permute-start(bf16[16,32,384]{2,1,0:T(8,128)(2,1)S(1)} %all-to-all-done.refs_8_), channel_id=1, source_target_pairs={{0,1},{1,0},{2,3},{3,2},{4,5},{5,4},{6,7},{7,6},{8,9},{9,8},{10,11... | collective-permute-start | bytes 1179656 | tf_op jit(solution)/shard_map/ppermute | solution.py:393
  39.4 0.7 copy-start.9
  40.1 0.7 copy-start.11
  40.8 1.0 copy-start.10
  41.8 1.0 copy-start.12
  45.1 18.7 %copy-start = (f32[8,16,128]{2,1,0:T(8,128)}, f32[8,16,128]{2,1,0:T(8,128)S(1)}, u32[]{:S(2)}) copy-start(f32[8,16,128]{2,1,0:T(8,128)S(1)} %get-tuple-element.30.steps_ref) | copy-start | bytes 196612
  45.1 18.7 %copy-start.23 = (bf16[1024,1024]{1,0:T(8,128)(2,1)}, bf16[1024,1024]{1,0:T(8,128)(2,1)S(1)}, u32[]{:S(2)}) copy-start(bf16[1024,1024]{1,0:T(8,128)(2,1)S(1)} %get-tuple-element.29.normed_ref) | copy-start | bytes 6291460
  45.1 26.7 %collective-permute-start.12 = (bf16[2,64,1152]{2,1,0:T(8,128)(2,1)S(1)}, bf16[2,64,1152]{2,1,0:T(8,128)(2,1)S(1)}, u32[]{:S(2)}, u32[]{:S(2)}) collective-permute-start(bf16[2,64,1152]{2,1,0:T(8,128)(2,1)S(1)} %bitcast.26), channel_id=1, source_target_pairs={{0,4},{4,0},{8,12},{12,8},{1,5},{5,1},{9,13},{13,9},{2,6},{6,2},{1... | collective-permute-start | bytes 884744 | tf_op jit(solution)/shard_map/ppermute | solution.py:393
  48.4 24.5 %collective-permute-start.13 = (bf16[2,64,1152]{2,1,0:T(8,128)(2,1)S(1)}, bf16[2,64,1152]{2,1,0:T(8,128)(2,1)S(1)}, u32[]{:S(2)}, u32[]{:S(2)}) collective-permute-start(bf16[2,64,1152]{2,1,0:T(8,128)(2,1)S(1)} %bitcast.27), channel_id=1, source_target_pairs={{0,8},{4,12},{8,0},{12,4},{1,9},{5,13},{9,1},{13,5},{2,10},{6,14},... | collective-permute-start | bytes 884744 | tf_op jit(solution)/shard_map/ppermute | solution.py:393
  48.6 25.3 %collective-permute-start.14 = (bf16[2,64,1152]{2,1,0:T(8,128)(2,1)S(1)}, bf16[2,64,1152]{2,1,0:T(8,128)(2,1)S(1)}, u32[]{:S(2)}, u32[]{:S(2)}) collective-permute-start(bf16[2,64,1152]{2,1,0:T(8,128)(2,1)S(1)} %bitcast.28), channel_id=1, source_target_pairs={{0,12},{4,8},{8,4},{12,0},{1,13},{5,9},{9,5},{13,1},{2,14},{6,10},... | collective-permute-start | bytes 884744 | tf_op jit(solution)/shard_map/ppermute | solution.py:393
  49.7 12.5 %collective-permute-start.11 = (bf16[128,256]{1,0:T(8,128)(2,1)S(1)}, bf16[128,256]{1,0:T(8,128)(2,1)S(1)}, u32[]{:S(2)}, u32[]{:S(2)}) collective-permute-start(bf16[128,256]{1,0:T(8,128)(2,1)S(1)} %get-tuple-element.35), channel_id=1, source_target_pairs={{0,16},{16,0},{1,17},{17,1},{2,18},{18,2},{3,19},{19,3},{4,20},{20... | collective-permute-start | bytes 196616 | tf_op jit(solution)/shard_map/ppermute | solution.py:393
  54.4 29.3 %copy-start.22 = (f32[128]{0:T(128)S(1)}, f32[128]{0:T(128)}, u32[]{:S(2)}) copy-start(f32[128]{0:T(128)} %param.12) | copy-start | bytes 1540
  63.9 19.8 %all-to-all-start.1 = ((bf16[16,64,128]{2,1,0:T(8,128)(2,1)}), bf16[16,64,128]{2,1,0:T(8,128)(2,1)}, u32[]{:S(2)}, u32[]{:S(2)}) async-start(bf16[16,64,128]{2,1,0:T(8,128)(2,1)} %bitcast.12), calls=%async_computation.1 | async-start | bytes 524288 | tf_op jit(solution)/shard_map/all_to_all | solution.py:389
  71.7 3.2 %collective-permute-start.15 = (bf16[2,64,1152]{2,1,0:T(8,128)(2,1)S(1)}, bf16[2,64,1152]{2,1,0:T(8,128)(2,1)S(1)}, u32[]{:S(2)}, u32[]{:S(2)}) collective-permute-start(bf16[2,64,1152]{2,1,0:T(8,128)(2,1)S(1)} %bitcast.29), channel_id=1, source_target_pairs={{0,2},{2,0},{1,3},{3,1},{4,6},{6,4},{5,7},{7,5},{8,10},{10,8},{9,1... | collective-permute-start | bytes 884744 | tf_op jit(solution)/shard_map/ppermute | solution.py:393
  71.9 3.0 %collective-permute-start.16 = (bf16[2,64,1152]{2,1,0:T(8,128)(2,1)S(1)}, bf16[2,64,1152]{2,1,0:T(8,128)(2,1)S(1)}, u32[]{:S(2)}, u32[]{:S(2)}) collective-permute-start(bf16[2,64,1152]{2,1,0:T(8,128)(2,1)S(1)} %collective-permute-done.12.refs_1_), channel_id=1, source_target_pairs={{0,2},{2,0},{1,3},{3,1},{4,6},{6,4},{5,7},{7,5},{8,10},{10,8},{9,1... | collective-permute-start | bytes 884744 | tf_op jit(solution)/shard_map/ppermute | solution.py:393
  72.2 0.7 copy-start.2
  72.9 1.9 %collective-permute-start.17 = (bf16[2,64,1152]{2,1,0:T(8,128)(2,1)S(1)}, bf16[2,64,1152]{2,1,0:T(8,128)(2,1)S(1)}, u32[]{:S(2)}, u32[]{:S(2)}) collective-permute-start(bf16[2,64,1152]{2,1,0:T(8,128)(2,1)S(1)} %collective-permute-done.13.refs_2_), channel_id=1, source_target_pairs={{0,2},{2,0},{1,3},{3,1},{4,6},{6,4},{5,7},{7,5},{8,10},{10,8},{9,1... | collective-permute-start | bytes 884744 | tf_op jit(solution)/shard_map/ppermute | solution.py:393
  73.1 0.7 copy-start.4
  73.8 1.6 %collective-permute-start.18 = (bf16[2,64,1152]{2,1,0:T(8,128)(2,1)S(1)}, bf16[2,64,1152]{2,1,0:T(8,128)(2,1)S(1)}, u32[]{:S(2)}, u32[]{:S(2)}) collective-permute-start(bf16[2,64,1152]{2,1,0:T(8,128)(2,1)S(1)} %collective-permute-done.14.refs_3_), channel_id=1, source_target_pairs={{0,2},{2,0},{1,3},{3,1},{4,6},{6,4},{5,7},{7,5},{8,10},{10,8},{9,1... | collective-permute-start | bytes 884744 | tf_op jit(solution)/shard_map/ppermute | solution.py:393
  74.1 0.7 copy-start.6
  75.4 1.0 copy-start.3
  76.4 1.0 copy-start.5
  77.3 1.0 copy-start.7
  78.3 0.9 copy-start.15
  79.2 0.9 copy-start.17
  80.1 0.8 copy-start.18
  82.3 0.7 copy-start.13
  83.7 16.6 %copy-start.1 = (f32[8,16,128]{2,1,0:T(8,128)S(1)}, f32[8,16,128]{2,1,0:T(8,128)}, u32[]{:S(2)}) copy-start(f32[8,16,128]{2,1,0:T(8,128)} %copy-done) | copy-start | bytes 196612
  83.7 1.0 copy-start.14
  84.7 0.8 copy-start.20
  88.4 20.1 %copy-start.24 = (bf16[1024,1024]{1,0:T(8,128)(2,1)S(1)}, bf16[1024,1024]{1,0:T(8,128)(2,1)}, u32[]{:S(2)}) copy-start(bf16[1024,1024]{1,0:T(8,128)(2,1)} %copy-done.23) | copy-start | bytes 6291460
  102.2 6.3 %collective-permute-start.19 = (bf16[128,256]{1,0:T(8,128)(2,1)S(1)}, bf16[128,256]{1,0:T(8,128)(2,1)S(1)}, u32[]{:S(2)}, u32[]{:S(2)}) collective-permute-start(bf16[128,256]{1,0:T(8,128)(2,1)S(1)} %get-tuple-element.43), channel_id=1, source_target_pairs={{0,16},{16,0},{1,17},{17,1},{2,18},{18,2},{3,19},{19,3},{4,20},{20... | collective-permute-start | bytes 196616 | tf_op jit(solution)/shard_map/ppermute | solution.py:393
  111.2 18.7 %all-to-all-start.3 = ((bf16[32,32,256]{2,1,0:T(8,128)(2,1)}), bf16[32,32,256]{2,1,0:T(8,128)(2,1)S(1)}, u32[]{:S(2)}, u32[]{:S(2)}) async-start(bf16[32,32,256]{2,1,0:T(8,128)(2,1)} %bitcast.16), calls=%async_computation.3 | async-start | bytes 1048576 | tf_op jit(solution)/shard_map/all_to_all | solution.py:389
  114.0 6.0 %collective-permute-start.20 = (f32[100,128]{1,0:T(8,128)S(1)}, f32[100,128]{1,0:T(8,128)S(1)}, u32[]{:S(2)}, u32[]{:S(2)}) collective-permute-start(f32[100,128]{1,0:T(8,128)S(1)} %get-tuple-element.46), channel_id=1, source_target_pairs={{0,1},{1,0},{2,3},{3,2},{4,5},{5,4},{6,7},{7,6},{8,9},{9,8},{10,11... | collective-permute-start | bytes 153608 | tf_op jit(solution)/shard_map/ppermute | solution.py:393
  (1 other events, 0.6 us)

commit v8 on v7

--- a/solution.py
+++ b/solution.py
@@ -25,6 +25,7 @@
 WINDOW = (PAIR + 2 * RADIUS) * TILE
 NOWHERE = 100
 NOTE_ROWS = 16
+CHUNKS = 4
 
 NORM_EPS = 1e-06
 SOFT_WIDTH = 0.0625
@@ -35,151 +36,178 @@
 
 VMEM = pl.BlockSpec(memory_space=pltpu.VMEM)
 SMEM = pl.BlockSpec(memory_space=pltpu.SMEM)
-ANYWHERE = pl.BlockSpec(memory_space=pltpu.HBM)
+HBM = pl.BlockSpec(memory_space=pltpu.HBM)
+ANYWHERE = pl.BlockSpec(memory_space=pl.ANY)
 OVER_ROWS = (((0,), (0,)), ((), ()))
 OVER_COLUMNS = (((1,), (1,)), ((), ()))
 
 
 def call(kernel, name, outs, ins, scratch=(), flops=0, moved=0, exps=0, room=8, results=None):
-    spaces = {"s": SMEM, "v": VMEM, "a": ANYWHERE}
-    return pl.pallas_call(
+    results = results or "v" * len(outs)
+    spaces = {"s": SMEM, "v": VMEM, "h": HBM, "a": ANYWHERE}
+    made = pl.pallas_call(
         kernel,
-        out_shape=[jax.ShapeDtypeStruct(shape, kind) for shape, kind in outs],
+        out_shape=[
+            pltpu.HBM(shape, kind) if space == "h" else jax.ShapeDtypeStruct(shape, kind)
+            for (shape, kind), space in zip(outs, results)
+        ],
         in_specs=[spaces[space] for space in ins],
-        out_specs=[spaces[space] for space in results or "v" * len(outs)],
+        out_specs=[spaces[space] for space in results],
         scratch_shapes=list(scratch),
         compiler_params=pltpu.CompilerParams(vmem_limit_bytes=room * 2**20),
         cost_estimate=pl.CostEstimate(flops=flops, bytes_accessed=moved, transcendentals=exps),
         name=name,
     )
 
-
-def fetch(pairs, sems):
+    def run(*args):
+        return made(
+            *[
+                pltpu.with_memory_space_constraint(arg, pltpu.HBM) if space == "h" else arg
+                for arg, space in zip(args, ins)
+            ]
+        )
+
+    return run
+
+
+def fetch(pairs, sems, first=0):
     copies = [
-        pltpu.make_async_copy(source, target, sems.at[at]) for at, (source, target) in enumerate(pairs)
+        pltpu.make_async_copy(source, target, sems.at[first + at])
+        for at, (source, target) in enumerate(pairs)
     ]
     for copy in copies:
         copy.start()
     return copies
 
 
+def wait(copies):
+    for copy in copies:
+        copy.wait()
+
+
 def prepare_kernel(
-    where_ref,
     near_ref,
     source_any,
     w_any,
     mix_any,
     readout_any,
-    normed_ref,
-    columns_ref,
-    packed_ref,
+    normed_any,
+    columns_any,
+    packed_any,
     *refs,
 ):
-    parts, (source_ref, w_ref, readout_ref, sems) = refs[:-4], refs[-4:]
-    copies = fetch(
-        [
-            (w_any, w_ref),
-            (source_any, source_ref),
-            (readout_any, readout_ref),
-            (mix_any, packed_ref.at[:, :LATENT_DIM]),
-        ],
-        sems,
-    )
-    copies[1].wait()
-    rows = source_ref.shape[0]
-    source = source_ref[...].astype(F32)
-    inverse = lax.rsqrt(jnp.mean(source * source, axis=-1, keepdims=True) + NORM_EPS)
-    normed_ref[:rows, :] = (source * inverse).astype(BF16)
-    if len(parts) == 1:
-        parts[0][...] = source_ref[...].reshape(parts[0].shape)
-    else:
-        for step, part_ref in enumerate(parts):
-            part = part_ref.shape[1]
-            place = pl.multiple_of((where_ref[2] ^ step) * part, part)
-            part_ref[0] = source_ref[pl.ds(place, part), :]
-    normed_ref[rows:, :] = jnp.zeros((NOTE_ROWS, LATENT_DIM), BF16)
+    parts, (source, normed, w, columns, readout, readout_pad, sems) = refs[:-7], refs[-7:]
+    ens = lax.axis_index("ens")
+    copies = fetch([(source_any, source), (w_any, w), (readout_any, readout)], sems)
+    moves = [(mix_any, packed_any.at[:, :LATENT_DIM])]
+    for step, part_any in enumerate(parts):
+        if len(parts) == 1:
+            moves += [
+                (source_any.at[pl.ds(m * part_any.shape[1], part_any.shape[1])], part_any.at[m])
+                for m in range(part_any.shape[0])
+            ]
+        else:
+            part = part_any.shape[1]
+            place = pl.multiple_of((ens ^ step) * part, part)
+            moves.append((source_any.at[pl.ds(place, part)], part_any.at[0]))
+    moves = fetch(moves, sems, 3)
+    rows = source.shape[0]
     row = lax.broadcasted_iota(jnp.int32, (NOTE_ROWS, 128), 0)
     lane = lax.broadcasted_iota(jnp.int32, (NOTE_ROWS, 128), 1)
     note = jnp.zeros((NOTE_ROWS, 128), F32)
-    for tile in range(near_ref.shape[0]):
+    tiles = near_ref.shape[0]
+    first_tile = lax.axis_index(("half", "quad", "core")) * tiles
+    for tile in range(tiles):
         for slot in range(K_NB):
             at = near_ref[tile, slot]
-            step = jnp.where(at >= 0, at - where_ref[3] - tile, NOWHERE).astype(F32)
+            step = jnp.where(at >= 0, at - first_tile - tile, NOWHERE).astype(F32)
             note = jnp.where((row == tile) & (lane == slot), step, note)
-    normed_ref[rows:, :128] = note.astype(BF16)
+    normed[rows:, :] = jnp.zeros((NOTE_ROWS, LATENT_DIM), BF16)
+    normed[rows:, :128] = note.astype(BF16)
     copies[0].wait()
-    halves, _, members_num = columns_ref.shape[:3]
+    states = source[...].astype(F32)
+    inverse = lax.rsqrt(jnp.mean(states * states, axis=-1, keepdims=True) + NORM_EPS)
+    normed[:rows, :] = (states * inverse).astype(BF16)
+    first = 3 + len(moves)
+    out = fetch([(normed, normed_any)], sems, first)
+    copies[1].wait()
     for g in range(GROUP):
-        chunk = jnp.concatenate(
-            [w_ref[:, (part * GROUP + g) * COLS : (part * GROUP + g + 1) * COLS] for part in range(3)],
-            axis=1,
-        )
-        for half in range(halves):
-            for m in range(members_num):
-                columns_ref[half, g, m] = chunk
+        for part in range(3):
+            at = (part * GROUP + g) * COLS
+            columns[g, :, part * COLS : (part + 1) * COLS] = w[:, at : at + COLS]
+    halves, _, members_num = columns_any.shape[:3]
+    out += fetch(
+        [
+            (columns, columns_any.at[half, :, m])
+            for half in range(halves)
+            for m in range(members_num)
+        ],
+        sems,
+        first + 1,
+    )
     copies[2].wait()
-    packed_ref[:, LATENT_DIM:] = jnp.zeros((packed_ref.shape[0], FIELD_PAD), BF16)
-    packed_ref[:, LATENT_DIM : LATENT_DIM + FIELD_NUM] = readout_ref[...]
-    copies[3].wait()
-
-
-def owners(where_ref):
-    core, quad = where_ref[0], where_ref[1]
+    readout_pad[...] = jnp.zeros_like(readout_pad)
+    readout_pad[:, :FIELD_NUM] = readout[...]
+    out += fetch([(readout_pad, packed_any.at[:, LATENT_DIM:])], sems, first + len(out))
+    wait(moves + out)
+
+
+def owners():
+    core, quad = lax.axis_index("core"), lax.axis_index("quad")
     return [(quad ^ step) * CORES + (core ^ flip) for flip in range(CORES) for step in range(QUAD)]
 
 
-def put_rims(where_ref, rims, first, last):
+def collect_kernel(*refs):
+    blocks, (normed_any, steps_ref, notes, sems) = refs[:GROUP], refs[GROUP:]
+    block = blocks[0].shape[0] - NOTE_ROWS
+    pairs = []
+    for rows_ref, owner in zip(blocks, owners()):
+        place = pl.ds(pl.multiple_of(owner * block, block), block)
+        pairs.append((rows_ref.at[:block], normed_any.at[place]))
+        pairs.append((rows_ref.at[block:, :128], notes.at[owner]))
+    wait(fetch(pairs, sems))
+    steps_ref[...] = notes[...].astype(F32)
+
+
+def put_rims(rims, first, last):
     if len(rims) == 1:
-        rims[0][...] = jnp.where(where_ref[4] == 0, last, first)
+        rims[0][...] = jnp.where(lax.axis_index("half") == 0, last, first)
     else:
         rims[0][...], rims[1][...] = first, last
 
 
-def project_kernel(parts, where_ref, *refs):
-    blocks, refs = refs[:GROUP], refs[GROUP:]
-    columns, refs = refs[:parts], refs[parts:]
-    q_ref, kv_ref, steps_ref, normed_any, *rims = refs[:-4]
-    notes, normed, w, sems = refs[-4:]
-    block = blocks[0].shape[0] - NOTE_ROWS
-    pairs = []
-    for at, (rows_ref, owner) in enumerate(zip(blocks, owners(where_ref))):
-        place = pl.ds(pl.multiple_of(owner * block, block), block)
-        pairs.append((rows_ref.at[:block], normed.at[place]))
-        pairs.append((rows_ref.at[block:, :128], notes.at[owner]))
+def project_kernel(normed_any, *refs):
+    columns, (normed, w, sems) = refs[:-3], refs[-3:]
+    columns, (q_ref, kv_ref, *rims) = columns[: w.shape[1] if len(w.shape) == 4 else 1], columns[
+        w.shape[1] if len(w.shape) == 4 else 1 :
+    ]
+    count = normed.shape[0]
+    chunk = count // CHUNKS
+    rows = [slice(at * chunk, (at + 1) * chunk) for at in range(CHUNKS)]
     if len(columns) == 1:
-        pairs.append((columns[0], w))
+        pairs = [(columns[0], w)]
     else:
-        for step, part in enumerate(columns):
-            pairs.append((part, w.at[:, where_ref[2] ^ step]))
-    copies = fetch(pairs, sems)
-    for copy in copies:
+        ens = lax.axis_index("ens")
+        pairs = [(part, w.at[:, ens ^ step]) for step, part in enumerate(columns)]
+    copies = fetch(pairs + [(normed_any.at[part], normed.at[part]) for part in rows], sems)
+    wait(copies[: len(pairs)])
+    weights = w[...].reshape(LATENT_DIM, 3 * COLS)
+    for part, copy in zip(rows, copies[len(pairs) :]):
         copy.wait()
-    keep = pltpu.make_async_copy(normed, normed_any, sems.at[0])
-    keep.start()
-    weights = w[...].reshape(LATENT_DIM, 3 * COLS)
-    projected = jnp.dot(normed[...], weights, preferred_element_type=F32).astype(BF16)
-    q_ref[...] = projected[:, :COLS]
-    kv_ref[...] = projected[:, COLS:]
-    last = GROUP * block - RIM
-    put_rims(where_ref, rims, projected[:RIM, COLS:], projected[last:, COLS:])
-    steps_ref[...] = notes[...].astype(F32)
-    keep.wait()
-
-
-def assemble_kernel(where_ref, *refs):
-    pieces, refs = refs[:GROUP], refs[GROUP:]
-    sources, (truth_any, w_ref, source_ref, truth_ref, sems) = refs[:-5], refs[-5:]
-    core, quad, ens = where_ref[0], where_ref[1], where_ref[2]
-    pairs = [(truth_any, truth_ref)]
-    if len(sources) == 1:
-        pairs.append((sources[0], source_ref))
-    else:
-        for step, part in enumerate(sources):
-            pairs.append((part.at[0], source_ref.at[ens ^ step]))
-    for at, piece in enumerate(pieces):
-        pairs.append((piece, w_ref.at[:, quad ^ (at % QUAD), core ^ (at // QUAD)]))
-    for copy in fetch(pairs, sems):
-        copy.wait()
+        projected = jnp.dot(normed[part, :], weights, preferred_element_type=F32).astype(BF16)
+        q_ref[part, :] = projected[:, :COLS]
+        kv_ref[part, :] = projected[:, COLS:]
+    put_rims(rims, kv_ref[:RIM, :], kv_ref[count - RIM :, :])
+
+
+def assemble_kernel(*refs):
+    pieces, (w_any, sems) = refs[:GROUP], refs[GROUP:]
+    core, quad = lax.axis_index("core"), lax.axis_index("quad")
+    pairs = [
+        (piece, w_any.at[:, quad ^ (at % QUAD), core ^ (at // QUAD)])
+        for at, piece in enumerate(pieces)
+    ]
+    wait(fetch(pairs, sems))
 
 
 def by_head(rows):
@@ -255,7 +283,7 @@
 
 
 def edge_back_kernel(
-    where_ref, steps_ref, q_ref, kv_ref, low_ref, high_ref, g_ref, part_ref, *rims
+    steps_ref, q_ref, kv_ref, low_ref, high_ref, g_ref, part_ref, *rims
 ):
     outer = []
     step = PAIR * TILE
@@ -274,7 +302,7 @@
             columns = slice(at * COLS, (at + 1) * COLS)
             part_ref[edge, :, columns] = grad[own]
         outer.append(jnp.concatenate([grad[rim].astype(BF16) for grad in grads], axis=1))
-    put_rims(where_ref, rims, *outer)
+    put_rims(rims, *outer)
 
 
 def interior_back_kernel(steps_ref, q_ref, kv_ref, g_ref, part_ref, out_ref):
@@ -304,26 +332,42 @@
     return spread * lax.rsqrt(spread * spread + SOFT_WIDTH)
 
 
-def mix_kernel(
-    where_ref, att_ref, source_ref, w, truth_ref, factor_ref, pred_ref, grad_ref, a, truth
-):
-    members_num, part, _ = source_ref.shape
+def mix_kernel(att_ref, factor_ref, truth_any, w_any, *refs):
+    sources, refs = refs[:-8], refs[-8:]
+    pred_ref, grad_ref, a, truth_ref, truth, source, w, sems = refs
+    members_num, part, _ = source.shape
+    halves = w.shape[0]
+    ens = lax.axis_index("ens")
+    copies = fetch([(w_any.at[half], w.at[half]) for half in range(halves)], sems)
+    pairs = [(truth_any, truth_ref)]
+    if len(sources) == 1:
+        pairs.append((sources[0], source))
+    else:
+        pairs += [(rows.at[0], source.at[ens ^ step]) for step, rows in enumerate(sources)]
+    others = fetch(pairs, sems, halves)
     for g in range(GROUP):
         for m in range(members_num):
             a[m * part : (m + 1) * part, g * COLS : (g + 1) * COLS] = att_ref[g * members_num + m]
+    wait(others)
     lane_part = lax.broadcasted_iota(jnp.int32, (1, a.shape[0]), 1) // part
     own_truth, own_factor = truth_ref[...], factor_ref[...]
     for turn in range(1, members_num):
         at = lane_part - turn
-        here = jnp.where(at < 0, at + members_num, at) == where_ref[2]
+        here = jnp.where(at < 0, at + members_num, at) == ens
         own_truth = jnp.where(here, pltpu.roll(truth_ref[...], turn * part, 1), own_truth)
         own_factor = jnp.where(here, pltpu.roll(factor_ref[...], turn * part, 1), own_factor)
     truth[...] = jnp.zeros_like(truth)
     truth[:FIELD_NUM, :] = own_truth
+    hidden = source[...].reshape(a.shape).astype(F32)
+    count = LATENT_DIM // halves
+    for half in range(halves):
+        copies[half].wait()
+        mix = w[half].reshape(count, LATENT_DIM + FIELD_PAD)[:, :LATENT_DIM]
+        hidden += jnp.dot(
+            a[:, half * count : (half + 1) * count], mix, preferred_element_type=F32
+        )
     both = w[...].reshape(LATENT_DIM, LATENT_DIM + FIELD_PAD)
     mix, readout = both[:, :LATENT_DIM], both[:, LATENT_DIM:]
-    source = source_ref[...].reshape(a.shape).astype(F32)
-    hidden = source + jnp.dot(a[...], mix, preferred_element_type=F32)
     inverse = lax.rsqrt(jnp.mean(hidden * hidden, axis=-1, keepdims=True) + NORM_EPS)
     decoded = (hidden * inverse).astype(BF16)
     prediction = lax.dot_general(
@@ -352,10 +396,11 @@
             ]
 
 
-def product_kernel(where_ref, normed_ref, from_low_ref, from_high_ref, grads_ref, out_ref):
+def product_kernel(normed_ref, from_low_ref, from_high_ref, grads_ref, out_ref):
     count = normed_ref.shape[0]
-    from_low = jnp.where(where_ref[4] > 0, from_low_ref[...].astype(F32), 0.0)
-    from_high = jnp.where(where_ref[4] < where_ref[5], from_high_ref[...].astype(F32), 0.0)
+    half, last = lax.axis_index("half"), lax.axis_size("half") - 1
+    from_low = jnp.where(half > 0, from_low_ref[...].astype(F32), 0.0)
+    from_high = jnp.where(half < last, from_high_ref[...].astype(F32), 0.0)
     grads = grads_ref[...]
     grads = jnp.concatenate(
         [
@@ -411,13 +456,11 @@
     part = node_rows // members_num
     up = [(i, i + 1) for i in range(halves - 1)]
     down = [(target, source) for source, target in up]
-    core, quad, ens = (lax.axis_index(axis) for axis in ("core", "quad", "ens"))
-    first_tile = lax.axis_index(("half", "quad", "core")) * neighbours.shape[0]
-    half = lax.axis_index("half")
-    where = jnp.stack([core, quad, ens, first_tile, half, halves - 1]).astype(jnp.int32)
+    ens = lax.axis_index("ens")
     width = LATENT_DIM + FIELD_PAD
     paired = members_num == 2
     copies = 1 if paired else members_num
+    source_parts = 2 if paired else 1
 
     normed, columns, packed, *sources = call(
         prepare_kernel,
@@ -427,18 +470,21 @@
             ((halves, GROUP, copies, shard, 3 * COLS), BF16),
             ((shard, width), BF16),
         ]
-        + [((1 if paired else members_num, part, LATENT_DIM), BF16)] * (2 if paired else 1),
-        "ssaaaa",
+        + [((1 if paired else members_num, part, LATENT_DIM), BF16)] * source_parts,
+        "shhhh",
         [
             pltpu.VMEM((node_rows, LATENT_DIM), BF16),
+            pltpu.VMEM((node_rows + NOTE_ROWS, LATENT_DIM), BF16),
             pltpu.VMEM(w_attn.shape, BF16),
+            pltpu.VMEM((GROUP, shard, 3 * COLS), BF16),
             pltpu.VMEM(readout_matrix.shape, BF16),
-            pltpu.SemaphoreType.DMA((4,)),
+            pltpu.VMEM((shard, FIELD_PAD), BF16),
+            pltpu.SemaphoreType.DMA((6 + max(2, members_num) + halves * copies,)),
         ],
         flops=2**20,
         moved=2**20,
-        room=56,
-    )(where, neighbours, members.reshape(node_rows, LATENT_DIM), w_attn, w_mix, readout_matrix)
+        results="hhh" + "h" * source_parts,
+    )(neighbours, members.reshape(node_rows, LATENT_DIM), w_attn, w_mix, readout_matrix)
 
     packed = in_order(packed, "half", 0)
     near = [normed] + [swap(normed, "quad", step) for step in range(1, QUAD)]
@@ -449,6 +495,15 @@
         columns = [exchange(columns.reshape(-1, shard, 3 * COLS), everyone)]
         columns = [columns[0].reshape(LATENT_DIM, 3 * COLS)]
     far = [swap(piece, "core", 1) for piece in near]
+    normed, steps = call(
+        collect_kernel,
+        "collect",
+        [((rows, LATENT_DIM), BF16), ((GROUP, NOTE_ROWS, 128), F32)],
+        "a" * (2 * QUAD),
+        [pltpu.VMEM((GROUP, NOTE_ROWS, 128), BF16), pltpu.SemaphoreType.DMA((2 * GROUP,))],
+        moved=4 * 2**20,
+        results="hv",
+    )(*near, *far)
 
     packed = in_order(packed, "ens", 1).reshape(halves, members_num * shard, width)
     if paired:
@@ -456,33 +511,27 @@
         columns[1], sources[1] = lax.optimization_barrier((columns[1], sources[1]))
     else:
         sources = [exchange(sources[0], "ens")]
+    packed, far[3], columns[0] = lax.optimization_barrier((packed, far[3], columns[0]))
+    pieces = [packed] + [swap(packed, "quad", step) for step in range(1, QUAD)]
 
     rim = ((RIM, 2 * COLS), BF16)
     rims = [rim] if halves == 2 else [rim, rim]
-    queries, own, steps, normed, *inner = call(
-        functools.partial(project_kernel, len(columns)),
+    queries, own, *inner = call(
+        project_kernel,
         "project",
+        [((rows, COLS), BF16), ((rows, 2 * COLS), BF16)] + rims,
+        "h" + "a" * len(columns),
         [
-            ((rows, COLS), BF16),
-            ((rows, 2 * COLS), BF16),
-            ((GROUP, NOTE_ROWS, 128), F32),
-            ((rows, LATENT_DIM), BF16),
-        ]
-        + rims,
-        "s" + "a" * (GROUP + len(columns)),
-        [
-            pltpu.VMEM((GROUP, NOTE_ROWS, 128), BF16),
             pltpu.VMEM((rows, LATENT_DIM), BF16),
             pltpu.VMEM(
                 (GROUP * halves, 2, shard, 3 * COLS) if paired else (LATENT_DIM, 3 * COLS), BF16
             ),
-            pltpu.SemaphoreType.DMA((2 * GROUP + 2,)),
+            pltpu.SemaphoreType.DMA((CHUNKS + 2,)),
         ],
         flops=rows * LATENT_DIM * 6 * COLS,
         moved=4 * 2**20,
-        room=14,
-        results="vvvavv"[: 4 + len(rims)],
-    )(where, *near, *far, *columns)
+        room=10,
+    )(normed, *columns)
 
     def across(inner):
         if halves == 2:
@@ -510,48 +559,48 @@
         moved=2**20,
         exps=rows * 128,
     )(steps, queries, own, low, high, outcome)
-    packed, own = lax.optimization_barrier((packed, own))
-    pieces = [packed] + [swap(packed, "quad", step) for step in range(1, QUAD)]
+    *pieces, own = lax.optimization_barrier((*pieces, own))
     pieces = pieces + [swap(piece, "core", 1) for piece in pieces]
     attended = exchange(outcome.reshape(GROUP * members_num, part, COLS), ("quad", "core", "ens"))
-    weights, sources, truth = call(
+    block = (halves, QUAD, CORES, members_num * shard, width)
+    (weights,) = call(
         assemble_kernel,
         "assemble",
-        [
-            ((halves, QUAD, CORES, members_num * shard, width), BF16),
-            ((members_num, part, LATENT_DIM), BF16),
-            (observed_truth.shape, F32),
-        ],
-        "s" + "a" * (len(pieces) + len(sources) + 1),
-        [pltpu.SemaphoreType.DMA((GROUP + len(sources) + 1,))],
+        [(block, BF16)],
+        "a" * len(pieces),
+        [pltpu.SemaphoreType.DMA((GROUP,))],
         moved=4 * 2**20,
-        room=48,
-    )(where, *pieces, *sources, observed_truth)
+        results="h",
+    )(*pieces)
 
     prediction, grads = call(
         mix_kernel,
         "mix_loss_backward",
         [((FIELD_NUM, node_rows), F32), ((GROUP * members_num, part, COLS), BF16)],
-        "svvvvv",
+        "vvhh" + "a" * len(sources),
         [
             pltpu.VMEM((node_rows, LATENT_DIM), BF16),
+            pltpu.VMEM(observed_truth.shape, F32),
             pltpu.VMEM((FIELD_PAD, node_rows), F32),
+            pltpu.VMEM((members_num, part, LATENT_DIM), BF16),
+            pltpu.VMEM(block, BF16),
+            pltpu.SemaphoreType.DMA((halves + 1 + len(sources),)),
         ],
         flops=node_rows * LATENT_DIM * 4 * width,
         moved=2**22,
         room=14,
-    )(where, attended, sources, weights, truth, cell_surface_factor[None])
+    )(attended, cell_surface_factor[None], observed_truth, weights, *sources)
     grads = exchange(grads, ("quad", "core", "ens")).reshape(rows, COLS)
 
     edges, *inner = call(
         edge_back_kernel,
         "attention_edges_back",
         [((2, WINDOW - RIM, 2 * COLS), F32)] + rims,
-        "svvvvvv",
+        "vvvvvv",
         flops=rows * COLS * 1280,
         moved=2**20,
         exps=rows * 128,
-    )(where, steps, queries, own, low, high, grads)
+    )(steps, queries, own, low, high, grads)
     from_low, from_high = across(inner)
     (kv_grads,) = call(
         interior_back_kernel,
@@ -567,11 +616,11 @@
         product_kernel,
         "product",
         [((LATENT_DIM, 2 * COLS), BF16)],
-        "svvvv",
+        "vvvv",
         flops=rows * LATENT_DIM * 8 * COLS,
         moved=2**22,
         room=16,
-    )(where, normed, from_low, from_high, kv_grads)
+    )(normed, from_low, from_high, kv_grads)
     term, prediction = lax.optimization_barrier((term, prediction))
     term = exchange(term.reshape(-1, shard, 2 * COLS), everyone)
     (grad_kv,) = call(

time: 132 us -> 119 us (0.902)
  local copies, waits for them, and re-layouts: 16.2 us -> 1.47 us
  Pallas kernels: 23.1 us -> 33.7 us
  waiting for transfers between devices: 39 us -> 30.3 us
  starting transfers between devices: 38.6 us -> 40.9 us
  blocking collectives: 11.9 us -> 9.89 us
    unnamed x51 -> x11, local copies, waits for them, and re-layouts: 15.5 us -> 1.37 us
    ppermute x21, waiting for transfers between devices: 28.8 us -> 18.3 us  [swap(): lax.ppermute(value, axis, [(i, i ^ step) for i in range(lax.axis_size(axi...]
    pallas_call x10 -> x11, Pallas kernels: 23.1 us -> 33.7 us  [run(): made(*[pltpu.with_memory_space_constraint(arg, pltpu.HBM) if space == 'h'...]
    ppermute x21, starting transfers between devices: 22.4 us -> 25.4 us  [swap(): lax.ppermute(value, axis, [(i, i ^ step) for i in range(lax.axis_size(axi...]
    all_to_all x1, blocking collectives: 11.9 us -> 9.89 us  [exchange(): return lax.all_to_all(chunks, axes, 0, 0)]
    all_to_all x3, waiting for transfers between devices: 10.1 us -> 12 us  [exchange(): return lax.all_to_all(chunks, axes, 0, 0)]
  transfers between devices with their start and end apart: 24 -> 24, of which waited for: 8 -> 11; matrix products, arithmetic and copies ran while one was open for 1% -> 2% of each run, Pallas kernels for 7% -> 12%
where the time goes in v8:
time: 119 us; the launch traced here: 118 us
  starting transfers between devices  40.9 us (34%)
  Pallas kernels  33.7 us (28%)
  waiting for transfers between devices  30.3 us (25%)
  blocking collectives  9.89 us (8%)
  local copies, waits for them, and re-layouts  1.47 us (1%)
    pallas_call x11, Pallas kernels, run(): made(*[pltpu.with_memory_space_constraint(arg, pltpu.HBM) if space == 'h'...  33.7 us
    ppermute x21, starting transfers between devices, swap(): lax.ppermute(value, axis, [(i, i ^ step) for i in range(lax.axis_size(axi...  25.4 us
    ppermute x21, waiting for transfers between devices, swap(): lax.ppermute(value, axis, [(i, i ^ step) for i in range(lax.axis_size(axi...  18.3 us
    all_to_all x3, starting transfers between devices, exchange(): return lax.all_to_all(chunks, axes, 0, 0)  15.5 us
    all_to_all x3, waiting for transfers between devices, exchange(): return lax.all_to_all(chunks, axes, 0, 0)  12 us
    all_to_all x1, blocking collectives, exchange(): return lax.all_to_all(chunks, axes, 0, 0)  9.89 us
  transfers between devices with their start and end apart: 24, of which 11 were waited for; matrix products, arithmetic and copies ran while one was open for 2% of the time, Pallas kernels for 12%

profile of v8, /device:TPU:1, one launch (start us, length us, event | category | flops | bytes accessed | tf_op | source)
XLA Modules:
  0.0 118.2 jit_solution(12082191086419644314)
XLA Ops:
  0.6 0.7 copy-done.2
  1.3 11.7 %prepare.1 = (bf16[144,1024]{1,0:T(8,128)(2,1)}, bf16[2,8,1,32,384]{4,3,2,1,0:T(8,128)(2,1)}, bf16[32,1152]{1,0:T(8,128)(2,1)}, bf16[1,64,1024]{2,1,0:T(8,128)(2,1)}, bf16[1,64,1024]{2,1,0:T(8,128)(2,1)}) custom-call(s32[2,4]{1,0:T(2,128)S(1)} %copy-done.2, bf16[128,1024]{1,0:T(8,128)(2,1)} %bitcast.28, bf16[32,3072]{1,0:T(8,128)(2,1)} %w_any.1, ...), custom_call_target="tpu_custom_call" | custom-call | flops 1048576 | bytes 1048576 | tf_op jit(solution)/shard_map/prepare/pallas_call | solution.py:63
  13.0 3.2 %collective-permute-start.7 = (bf16[32,1152]{1,0:T(8,128)(2,1)}, bf16[32,1152]{1,0:T(8,128)(2,1)S(1)}, u32[]{:S(2)}, u32[]{:S(2)}) collective-permute-start(bf16[32,1152]{1,0:T(8,128)(2,1)} %get-tuple-element.30), channel_id=1, source_target_pairs={{0,16},{16,0},{1,17},{17,1},{2,18},{18,2},{3,19},{19,3},{4,20},{20... | collective-permute-start | bytes 221192 | tf_op jit(solution)/shard_map/ppermute | solution.py:438
  16.2 2.3 %collective-permute-start.2 = (bf16[144,1024]{1,0:T(8,128)(2,1)}, bf16[144,1024]{1,0:T(8,128)(2,1)S(1)}, u32[]{:S(2)}, u32[]{:S(2)}) collective-permute-start(bf16[144,1024]{1,0:T(8,128)(2,1)} %get-tuple-element.27.refs_0_), channel_id=1, source_target_pairs={{0,12},{4,8},{8,4},{12,0},{1,13},{5,9},{9,5},{13,1},{2,14},{6,10},... | collective-permute-start | bytes 884744 | tf_op jit(solution)/shard_map/ppermute | solution.py:438
  18.5 0.2 collective-permute-start
  18.9 5.6 %all-to-all-start = ((bf16[16,32,384]{2,1,0:T(8,128)(2,1)}), bf16[16,32,384]{2,1,0:T(8,128)(2,1)S(1)}, u32[]{:S(2)}, u32[]{:S(2)}) async-start(bf16[16,32,384]{2,1,0:T(8,128)(2,1)} %bitcast.27), calls=%async_computation | async-start | bytes 786432 | tf_op jit(solution)/shard_map/all_to_all | solution.py:434
  24.5 0.9 select_bitcast_fusion.3
  25.4 1.3 %collective-permute-start.8 = (bf16[2,32,1152]{2,1,0:T(8,128)(2,1)S(1)}, bf16[2,32,1152]{2,1,0:T(8,128)(2,1)S(1)}, u32[]{:S(2)}, u32[]{:S(2)}) collective-permute-start(bf16[2,32,1152]{2,1,0:T(8,128)(2,1)S(1)} %pad_maximum_fusion.1), channel_id=1, source_target_pairs={{0,1},{1,0},{2,3},{3,2},{4,5},{5,4},{6,7},{7,6},{8,9},{9,8},{10,11... | collective-permute-start | bytes 442376 | tf_op jit(solution)/shard_map/ppermute | solution.py:438
  26.7 0.4 collective-permute-start.3
  27.1 1.3 %collective-permute-start.6 = (bf16[144,1024]{1,0:T(8,128)(2,1)S(1)}, bf16[144,1024]{1,0:T(8,128)(2,1)S(1)}, u32[]{:S(2)}, u32[]{:S(2)}) collective-permute-start(bf16[144,1024]{1,0:T(8,128)(2,1)S(1)} %collective-permute-done.2.refs_3_), channel_id=1, source_target_pairs={{0,2},{2,0},{1,3},{3,1},{4,6},{6,4},{5,7},{7,5},{8,10},{10,8},{9,1... | collective-permute-start | bytes 884744 | tf_op jit(solution)/shard_map/ppermute | solution.py:438
  28.4 5.7 %collective-permute-done.refs_1_ = bf16[144,1024]{1,0:T(8,128)(2,1)S(1)} collective-permute-done((bf16[144,1024]{1,0:T(8,128)(2,1)}, bf16[144,1024]{1,0:T(8,128)(2,1)S(1)}, u32[]{:S(2)}, u32[]{:S(2)}) %collective-permute-start) | collective-permute-done | bytes 294944 | tf_op jit(solution)/shard_map/ppermute | solution.py:438
  34.1 0.9 collective-permute-start.4
  35.0 3.4 %collective-permute-start.5 = (bf16[144,1024]{1,0:T(8,128)(2,1)S(1)}, bf16[144,1024]{1,0:T(8,128)(2,1)S(1)}, u32[]{:S(2)}, u32[]{:S(2)}) collective-permute-start(bf16[144,1024]{1,0:T(8,128)(2,1)S(1)} %collective-permute-done.1.refs_2_), channel_id=1, source_target_pairs={{0,2},{2,0},{1,3},{3,1},{4,6},{6,4},{5,7},{7,5},{8,10},{10,8},{9,1... | collective-permute-start | bytes 884744 | tf_op jit(solution)/shard_map/ppermute | solution.py:438
  38.4 0.6 all-to-all-done.refs_0_
  39.0 1.4 %collective-permute-start.9 = (bf16[16,32,384]{2,1,0:T(8,128)(2,1)S(1)}, bf16[16,32,384]{2,1,0:T(8,128)(2,1)S(1)}, u32[]{:S(2)}, u32[]{:S(2)}) collective-permute-start(bf16[16,32,384]{2,1,0:T(8,128)(2,1)S(1)} %all-to-all-done.refs_0_), channel_id=1, source_target_pairs={{0,1},{1,0},{2,3},{3,2},{4,5},{5,4},{6,7},{7,6},{8,9},{9,8},{10,11... | collective-permute-start | bytes 1179656 | tf_op jit(solution)/shard_map/ppermute | solution.py:438
  40.7 1.5 %collect.1 = (bf16[1024,1024]{1,0:T(8,128)(2,1)}, f32[8,16,128]{2,1,0:T(8,128)S(1)}) custom-call(bf16[144,1024]{1,0:T(8,128)(2,1)S(1)} %copy-done, bf16[144,1024]{1,0:T(8,128)(2,1)S(1)} %collective-permute-done.refs_1_, bf16[144,1024]{1,0:T(8,128)(2,1)S(1)} %collective-permute-done.1.refs_2_, bf16[144,1024]{1,0:T(8,128)(2,1)S(1)} %collective-permute-done.2.refs_3_, ...), custom_call_target="tpu_custom_call" | custom-call | bytes 4194304 | tf_op jit(solution)/shard_map/collect/pallas_call | solution.py:63
  42.2 1.2 %collective-permute-start.11 = (bf16[2,64,1152]{2,1,0:T(8,128)(2,1)S(1)}, bf16[2,64,1152]{2,1,0:T(8,128)(2,1)S(1)}, u32[]{:S(2)}, u32[]{:S(2)}) collective-permute-start(bf16[2,64,1152]{2,1,0:T(8,128)(2,1)S(1)} %bitcast.21), channel_id=1, source_target_pairs={{0,4},{4,0},{8,12},{12,8},{1,5},{5,1},{9,13},{13,9},{2,6},{6,2},{1... | collective-permute-start | bytes 884744 | tf_op jit(solution)/shard_map/ppermute | solution.py:438
  43.4 0.4 collective-permute-start.12
  43.8 1.2 collective-permute-start.13
  44.9 5.8 %collective-permute-done.10.refs_1_ = bf16[1,64,1024]{2,1,0:T(8,128)(2,1)S(1)} collective-permute-done((bf16[1,64,1024]{2,1,0:T(8,128)(2,1)}, bf16[1,64,1024]{2,1,0:T(8,128)(2,1)S(1)}, u32[]{:S(2)}, u32[]{:S(2)}) %collective-permute-start.10) | collective-permute-done | bytes 131104 | tf_op jit(solution)/shard_map/ppermute | solution.py:438
  50.7 2.9 %project.1 = (bf16[1024,128]{1,0:T(8,128)(2,1)S(1)}, bf16[1024,256]{1,0:T(8,128)(2,1)S(1)}, bf16[128,256]{1,0:T(8,128)(2,1)S(1)}) custom-call(bf16[1024,1024]{1,0:T(8,128)(2,1)} %get-tuple-element.28.normed_any.normed_ref, bf16[16,32,384]{2,1,0:T(8,128)(2,1)S(1)} %all-to-all-done.refs_0_, bf16[16,32,384]{2,1,0:T(8,128)(2,1)S(1)} %collective-permute-done.9.refs_1_), custom_call_target="tpu_custom_call" | custom-call | flops 805306368 | bytes 4194304 | tf_op jit(solution)/shard_map/project/pallas_call | solution.py:63
  53.6 3.5 %collective-permute-start.14 = (bf16[128,256]{1,0:T(8,128)(2,1)S(1)}, bf16[128,256]{1,0:T(8,128)(2,1)S(1)}, u32[]{:S(2)}, u32[]{:S(2)}) collective-permute-start(bf16[128,256]{1,0:T(8,128)(2,1)S(1)} %get-tuple-element.39), channel_id=1, source_target_pairs={{0,16},{16,0},{1,17},{17,1},{2,18},{18,2},{3,19},{19,3},{4,20},{20... | collective-permute-start | bytes 196616 | tf_op jit(solution)/shard_map/ppermute | solution.py:438
  57.1 2.6 %attention_interior.1.done_ref = bf16[1024,128]{1,0:T(8,128)(2,1)S(1)} custom-call(f32[8,16,128]{2,1,0:T(8,128)S(1)} %get-tuple-element.29.steps_ref, bf16[1024,128]{1,0:T(8,128)(2,1)S(1)} %get-tuple-element.35.q_ref, bf16[1024,256]{1,0:T(8,128)(2,1)S(1)} %get-tuple-element.38.kv_ref), custom_call_target="tpu_custom_call" | custom-call | flops 268435456 | bytes 2097152 | tf_op jit(solution)/shard_map/attention_interior/pallas_call | solution.py:63
  59.7 1.7 %attention_edges.1 = bf16[1024,128]{1,0:T(8,128)(2,1)} custom-call(f32[8,16,128]{2,1,0:T(8,128)S(1)} %get-tuple-element.29.steps_ref, bf16[1024,128]{1,0:T(8,128)(2,1)S(1)} %get-tuple-element.35.q_ref, bf16[1024,256]{1,0:T(8,128)(2,1)S(1)} %get-tuple-element.38.kv_ref, bf16[128,256]{1,0:T(8,128)(2,1)S(1)} %collective-permute-done.14.low_ref.high_ref, ...), custom_call_target="tpu_custom_call" | custom-call | flops 67108864 | bytes 1048576 | tf_op jit(solution)/shard_map/attention_edges/pallas_call | solution.py:63
  61.4 6.3 %all-to-all-start.1 = ((bf16[16,64,128]{2,1,0:T(8,128)(2,1)}), bf16[16,64,128]{2,1,0:T(8,128)(2,1)S(1)}, u32[]{:S(2)}, u32[]{:S(2)}) async-start(bf16[16,64,128]{2,1,0:T(8,128)(2,1)} %bitcast.7), calls=%async_computation.1 | async-start | bytes 524288 | tf_op jit(solution)/shard_map/all_to_all | solution.py:434
  67.8 0.3 collective-permute-start.15
  68.1 0.3 collective-permute-start.16
  68.4 0.2 collective-permute-start.17
  68.6 0.3 collective-permute-start.18
  68.9 0.6 collective-permute-done.15.refs_4_
  69.4 0.4 collective-permute-done.16.refs_5_
  69.9 0.4 collective-permute-done.17.refs_6_
  70.3 0.4 collective-permute-done.18.refs_7_
  70.7 1.5 %assemble.1.w_any = bf16[2,4,2,64,1152]{4,3,2,1,0:T(8,128)(2,1)} custom-call(bf16[2,64,1152]{2,1,0:T(8,128)(2,1)S(1)} %bitcast.25, bf16[2,64,1152]{2,1,0:T(8,128)(2,1)S(1)} %collective-permute-done.11.refs_1_, bf16[2,64,1152]{2,1,0:T(8,128)(2,1)S(1)} %collective-permute-done.12.refs_2_, bf16[2,64,1152]{2,1,0:T(8,128)(2,1)S(1)} %collective-permute-done.13.refs_3_, ...), custom_call_target="tpu_custom_call" | custom-call | bytes 4194304 | tf_op jit(solution)/shard_map/assemble/pallas_call | solution.py:63
  72.2 2.5 %all-to-all-done.1.att_ref = bf16[16,64,128]{2,1,0:T(8,128)(2,1)S(1)} async-done(((bf16[16,64,128]{2,1,0:T(8,128)(2,1)}), bf16[16,64,128]{2,1,0:T(8,128)(2,1)S(1)}, u32[]{:S(2)}, u32[]{:S(2)}) %all-to-all-start.1) | async-done | bytes 262176 | tf_op jit(solution)/shard_map/all_to_all | solution.py:434
  74.7 3.7 %mix_loss_backward.1 = (f32[100,128]{1,0:T(8,128)S(1)}, bf16[16,64,128]{2,1,0:T(8,128)(2,1)S(1)}) custom-call(bf16[16,64,128]{2,1,0:T(8,128)(2,1)S(1)} %all-to-all-done.1.att_ref, f32[1,128]{1,0:T(1,128)S(1)} %bitcast.26, f32[100,128]{1,0:T(8,128)} %truth_any.1, bf16[2,4,2,64,1152]{4,3,2,1,0:T(8,128)(2,1)} %assemble.1.w_any, ...), custom_call_target="tpu_custom_call" | custom-call | flops 603979776 | bytes 4194304 | tf_op jit(solution)/shard_map/mix_loss_backward/pallas_call | solution.py:63
  78.4 9.9 %all_to_all.20 = bf16[16,64,128]{2,1,0:T(8,128)(2,1)S(1)} all-to-all(bf16[16,64,128]{2,1,0:T(8,128)(2,1)S(1)} %get-tuple-element.46), channel_id=1, replica_groups=mesh['half'=2,'quad'=4,'core'=2,'ens'=2] {'quad','core','ens'}, dimensions={0} | all-to-all | bytes 524288 | tf_op jit(solution)/shard_map/all_to_all | solution.py:434
  88.3 1.4 %attention_edges_back.1 = (f32[2,256,256]{2,1,0:T(8,128)S(1)}, bf16[128,256]{1,0:T(8,128)(2,1)S(1)}) custom-call(f32[8,16,128]{2,1,0:T(8,128)S(1)} %get-tuple-element.29.steps_ref, bf16[1024,128]{1,0:T(8,128)(2,1)S(1)} %get-tuple-element.35.q_ref, bf16[1024,256]{1,0:T(8,128)(2,1)S(1)} %get-tuple-element.38.kv_ref, ...), custom_call_target="tpu_custom_call" | custom-call | flops 167772160 | bytes 1048576 | tf_op jit(solution)/shard_map/attention_edges_back/pallas_call | solution.py:63
  89.7 2.0 %collective-permute-start.19 = (bf16[128,256]{1,0:T(8,128)(2,1)S(1)}, bf16[128,256]{1,0:T(8,128)(2,1)S(1)}, u32[]{:S(2)}, u32[]{:S(2)}) collective-permute-start(bf16[128,256]{1,0:T(8,128)(2,1)S(1)} %get-tuple-element.47), channel_id=1, source_target_pairs={{0,16},{16,0},{1,17},{17,1},{2,18},{18,2},{3,19},{19,3},{4,20},{20... | collective-permute-start | bytes 196616 | tf_op jit(solution)/shard_map/ppermute | solution.py:438
  91.7 3.9 %attention_interior_back.1.grads_ref = f32[1024,256]{1,0:T(8,128)S(1)} custom-call(f32[8,16,128]{2,1,0:T(8,128)S(1)} %get-tuple-element.29.steps_ref, bf16[1024,128]{1,0:T(8,128)(2,1)S(1)} %get-tuple-element.35.q_ref, bf16[1024,256]{1,0:T(8,128)(2,1)S(1)} %get-tuple-element.38.kv_ref, bf16[1024,128]{1,0:T(8,128)(2,1)S(1)} %bitcast.19, ...), custom_call_target="tpu_custom_call" | custom-call | flops 536870912 | bytes 4194304 | tf_op jit(solution)/shard_map/attention_interior_back/pallas_call | solution.py:63
  95.6 0.4 collective-permute-done.19.from_low_ref.from_high_ref
  96.0 2.1 %product.1 = bf16[1024,256]{1,0:T(8,128)(2,1)} custom-call(bf16[1024,1024]{1,0:T(8,128)(2,1)S(1)} %copy-done.4, bf16[128,256]{1,0:T(8,128)(2,1)S(1)} %collective-permute-done.19.from_low_ref.from_high_ref, bf16[128,256]{1,0:T(8,128)(2,1)S(1)} %collective-permute-done.19.from_low_ref.from_high_ref, f32[1024,256]{1,0:T(8,128)S(1)} %attention_interior_back.1.grads_ref), custom_call_target="tpu_custom_call" | custom-call | flops 1073741824 | bytes 4194304 | tf_op jit(solution)/shard_map/product/pallas_call | solution.py:63
  98.1 3.5 %all-to-all-start.3 = ((bf16[32,32,256]{2,1,0:T(8,128)(2,1)}), bf16[32,32,256]{2,1,0:T(8,128)(2,1)S(1)}, u32[]{:S(2)}, u32[]{:S(2)}) async-start(bf16[32,32,256]{2,1,0:T(8,128)(2,1)} %bitcast.11), calls=%async_computation.3 | async-start | bytes 1048576 | tf_op jit(solution)/shard_map/all_to_all | solution.py:434
  101.6 1.5 %collective-permute-start.20 = (f32[100,128]{1,0:T(8,128)S(1)}, f32[100,128]{1,0:T(8,128)S(1)}, u32[]{:S(2)}, u32[]{:S(2)}) collective-permute-start(f32[100,128]{1,0:T(8,128)S(1)} %get-tuple-element.50), channel_id=1, source_target_pairs={{0,1},{1,0},{2,3},{3,2},{4,5},{5,4},{6,7},{7,6},{8,9},{9,8},{10,11... | collective-permute-start | bytes 153608 | tf_op jit(solution)/shard_map/ppermute | solution.py:438
  103.1 4.5 %collective-permute-done.20 = f32[100,128]{1,0:T(8,128)S(1)} collective-permute-done((f32[100,128]{1,0:T(8,128)S(1)}, f32[100,128]{1,0:T(8,128)S(1)}, u32[]{:S(2)}, u32[]{:S(2)}) %collective-permute-start.20) | collective-permute-done | bytes 51232 | tf_op jit(solution)/shard_map/ppermute | solution.py:438
  107.8 0.7 copy.10
  108.5 9.0 %all-to-all-done.3 = bf16[32,32,256]{2,1,0:T(8,128)(2,1)S(1)} async-done(((bf16[32,32,256]{2,1,0:T(8,128)(2,1)}), bf16[32,32,256]{2,1,0:T(8,128)(2,1)S(1)}, u32[]{:S(2)}, u32[]{:S(2)}) %all-to-all-start.3) | async-done | bytes 524320 | tf_op jit(solution)/shard_map/all_to_all | solution.py:434
  117.4 0.8 gather_sums.1
  (32 shorter events, 0.7 us)
Async XLA Ops:
  0.6 0.7 copy-start.2
  13.0 27.7 %copy-start = (bf16[144,1024]{1,0:T(8,128)(2,1)S(1)}, bf16[144,1024]{1,0:T(8,128)(2,1)}, u32[]{:S(2)}) copy-start(bf16[144,1024]{1,0:T(8,128)(2,1)} %get-tuple-element.27.refs_0_) | copy-start | bytes 884740
  13.0 11.5 %collective-permute-start.7 = (bf16[32,1152]{1,0:T(8,128)(2,1)}, bf16[32,1152]{1,0:T(8,128)(2,1)S(1)}, u32[]{:S(2)}, u32[]{:S(2)}) collective-permute-start(bf16[32,1152]{1,0:T(8,128)(2,1)} %get-tuple-element.30), channel_id=1, source_target_pairs={{0,16},{16,0},{1,17},{17,1},{2,18},{18,2},{3,19},{19,3},{4,20},{20... | collective-permute-start | bytes 221192 | tf_op jit(solution)/shard_map/ppermute | solution.py:438
  16.2 10.9 %collective-permute-start.2 = (bf16[144,1024]{1,0:T(8,128)(2,1)}, bf16[144,1024]{1,0:T(8,128)(2,1)S(1)}, u32[]{:S(2)}, u32[]{:S(2)}) collective-permute-start(bf16[144,1024]{1,0:T(8,128)(2,1)} %get-tuple-element.27.refs_0_), channel_id=1, source_target_pairs={{0,12},{4,8},{8,4},{12,0},{1,13},{5,9},{9,5},{13,1},{2,14},{6,10},... | collective-permute-start | bytes 884744 | tf_op jit(solution)/shard_map/ppermute | solution.py:438
  18.5 15.6 %collective-permute-start = (bf16[144,1024]{1,0:T(8,128)(2,1)}, bf16[144,1024]{1,0:T(8,128)(2,1)S(1)}, u32[]{:S(2)}, u32[]{:S(2)}) collective-permute-start(bf16[144,1024]{1,0:T(8,128)(2,1)} %get-tuple-element.27.refs_0_), channel_id=1, source_target_pairs={{0,4},{4,0},{8,12},{12,8},{1,5},{5,1},{9,13},{13,9},{2,6},{6,2},{1... | collective-permute-start | bytes 884744 | tf_op jit(solution)/shard_map/ppermute | solution.py:438
  18.7 16.3 %collective-permute-start.1 = (bf16[144,1024]{1,0:T(8,128)(2,1)}, bf16[144,1024]{1,0:T(8,128)(2,1)S(1)}, u32[]{:S(2)}, u32[]{:S(2)}) collective-permute-start(bf16[144,1024]{1,0:T(8,128)(2,1)} %get-tuple-element.27.refs_0_), channel_id=1, source_target_pairs={{0,8},{4,12},{8,0},{12,4},{1,9},{5,13},{9,1},{13,5},{2,10},{6,14},... | collective-permute-start | bytes 884744 | tf_op jit(solution)/shard_map/ppermute | solution.py:438
  18.9 20.1 %all-to-all-start = ((bf16[16,32,384]{2,1,0:T(8,128)(2,1)}), bf16[16,32,384]{2,1,0:T(8,128)(2,1)S(1)}, u32[]{:S(2)}, u32[]{:S(2)}) async-start(bf16[16,32,384]{2,1,0:T(8,128)(2,1)} %bitcast.27), calls=%async_computation | async-start | bytes 786432 | tf_op jit(solution)/shard_map/all_to_all | solution.py:434
  25.4 13.0 %collective-permute-start.8 = (bf16[2,32,1152]{2,1,0:T(8,128)(2,1)S(1)}, bf16[2,32,1152]{2,1,0:T(8,128)(2,1)S(1)}, u32[]{:S(2)}, u32[]{:S(2)}) collective-permute-start(bf16[2,32,1152]{2,1,0:T(8,128)(2,1)S(1)} %pad_maximum_fusion.1), channel_id=1, source_target_pairs={{0,1},{1,0},{2,3},{3,2},{4,5},{5,4},{6,7},{7,6},{8,9},{9,8},{10,11... | collective-permute-start | bytes 442376 | tf_op jit(solution)/shard_map/ppermute | solution.py:438
  26.7 13.7 %collective-permute-start.3 = (bf16[144,1024]{1,0:T(8,128)(2,1)}, bf16[144,1024]{1,0:T(8,128)(2,1)S(1)}, u32[]{:S(2)}, u32[]{:S(2)}) collective-permute-start(bf16[144,1024]{1,0:T(8,128)(2,1)} %get-tuple-element.27.refs_0_), channel_id=1, source_target_pairs={{0,2},{2,0},{1,3},{3,1},{4,6},{6,4},{5,7},{7,5},{8,10},{10,8},{9,1... | collective-permute-start | bytes 884744 | tf_op jit(solution)/shard_map/ppermute | solution.py:438
  27.1 13.5 %collective-permute-start.6 = (bf16[144,1024]{1,0:T(8,128)(2,1)S(1)}, bf16[144,1024]{1,0:T(8,128)(2,1)S(1)}, u32[]{:S(2)}, u32[]{:S(2)}) collective-permute-start(bf16[144,1024]{1,0:T(8,128)(2,1)S(1)} %collective-permute-done.2.refs_3_), channel_id=1, source_target_pairs={{0,2},{2,0},{1,3},{3,1},{4,6},{6,4},{5,7},{7,5},{8,10},{10,8},{9,1... | collective-permute-start | bytes 884744 | tf_op jit(solution)/shard_map/ppermute | solution.py:438
  34.1 6.6 %collective-permute-start.4 = (bf16[144,1024]{1,0:T(8,128)(2,1)S(1)}, bf16[144,1024]{1,0:T(8,128)(2,1)S(1)}, u32[]{:S(2)}, u32[]{:S(2)}) collective-permute-start(bf16[144,1024]{1,0:T(8,128)(2,1)S(1)} %collective-permute-done.refs_1_), channel_id=1, source_target_pairs={{0,2},{2,0},{1,3},{3,1},{4,6},{6,4},{5,7},{7,5},{8,10},{10,8},{9,1... | collective-permute-start | bytes 884744 | tf_op jit(solution)/shard_map/ppermute | solution.py:438
  35.0 5.7 %collective-permute-start.5 = (bf16[144,1024]{1,0:T(8,128)(2,1)S(1)}, bf16[144,1024]{1,0:T(8,128)(2,1)S(1)}, u32[]{:S(2)}, u32[]{:S(2)}) collective-permute-start(bf16[144,1024]{1,0:T(8,128)(2,1)S(1)} %collective-permute-done.1.refs_2_), channel_id=1, source_target_pairs={{0,2},{2,0},{1,3},{3,1},{4,6},{6,4},{5,7},{7,5},{8,10},{10,8},{9,1... | collective-permute-start | bytes 884744 | tf_op jit(solution)/shard_map/ppermute | solution.py:438
  39.0 11.7 %collective-permute-start.9 = (bf16[16,32,384]{2,1,0:T(8,128)(2,1)S(1)}, bf16[16,32,384]{2,1,0:T(8,128)(2,1)S(1)}, u32[]{:S(2)}, u32[]{:S(2)}) collective-permute-start(bf16[16,32,384]{2,1,0:T(8,128)(2,1)S(1)} %all-to-all-done.refs_0_), channel_id=1, source_target_pairs={{0,1},{1,0},{2,3},{3,2},{4,5},{5,4},{6,7},{7,6},{8,9},{9,8},{10,11... | collective-permute-start | bytes 1179656 | tf_op jit(solution)/shard_map/ppermute | solution.py:438
  40.4 10.3 %collective-permute-start.10 = (bf16[1,64,1024]{2,1,0:T(8,128)(2,1)}, bf16[1,64,1024]{2,1,0:T(8,128)(2,1)S(1)}, u32[]{:S(2)}, u32[]{:S(2)}) collective-permute-start(bf16[1,64,1024]{2,1,0:T(8,128)(2,1)} %get-tuple-element.33), channel_id=1, source_target_pairs={{0,1},{1,0},{2,3},{3,2},{4,5},{5,4},{6,7},{7,6},{8,9},{9,8},{10,11... | collective-permute-start | bytes 393224 | tf_op jit(solution)/shard_map/ppermute | solution.py:438
  42.2 25.5 %collective-permute-start.11 = (bf16[2,64,1152]{2,1,0:T(8,128)(2,1)S(1)}, bf16[2,64,1152]{2,1,0:T(8,128)(2,1)S(1)}, u32[]{:S(2)}, u32[]{:S(2)}) collective-permute-start(bf16[2,64,1152]{2,1,0:T(8,128)(2,1)S(1)} %bitcast.21), channel_id=1, source_target_pairs={{0,4},{4,0},{8,12},{12,8},{1,5},{5,1},{9,13},{13,9},{2,6},{6,2},{1... | collective-permute-start | bytes 884744 | tf_op jit(solution)/shard_map/ppermute | solution.py:438
  43.4 24.4 %collective-permute-start.12 = (bf16[2,64,1152]{2,1,0:T(8,128)(2,1)S(1)}, bf16[2,64,1152]{2,1,0:T(8,128)(2,1)S(1)}, u32[]{:S(2)}, u32[]{:S(2)}) collective-permute-start(bf16[2,64,1152]{2,1,0:T(8,128)(2,1)S(1)} %bitcast.22), channel_id=1, source_target_pairs={{0,8},{4,12},{8,0},{12,4},{1,9},{5,13},{9,1},{13,5},{2,10},{6,14},... | collective-permute-start | bytes 884744 | tf_op jit(solution)/shard_map/ppermute | solution.py:438
  43.8 24.0 %collective-permute-start.13 = (bf16[2,64,1152]{2,1,0:T(8,128)(2,1)S(1)}, bf16[2,64,1152]{2,1,0:T(8,128)(2,1)S(1)}, u32[]{:S(2)}, u32[]{:S(2)}) collective-permute-start(bf16[2,64,1152]{2,1,0:T(8,128)(2,1)S(1)} %bitcast.23), channel_id=1, source_target_pairs={{0,12},{4,8},{8,4},{12,0},{1,13},{5,9},{9,5},{13,1},{2,14},{6,10},... | collective-permute-start | bytes 884744 | tf_op jit(solution)/shard_map/ppermute | solution.py:438
  53.6 6.1 %collective-permute-start.14 = (bf16[128,256]{1,0:T(8,128)(2,1)S(1)}, bf16[128,256]{1,0:T(8,128)(2,1)S(1)}, u32[]{:S(2)}, u32[]{:S(2)}) collective-permute-start(bf16[128,256]{1,0:T(8,128)(2,1)S(1)} %get-tuple-element.39), channel_id=1, source_target_pairs={{0,16},{16,0},{1,17},{17,1},{2,18},{18,2},{3,19},{19,3},{4,20},{20... | collective-permute-start | bytes 196616 | tf_op jit(solution)/shard_map/ppermute | solution.py:438
  61.4 13.3 %all-to-all-start.1 = ((bf16[16,64,128]{2,1,0:T(8,128)(2,1)}), bf16[16,64,128]{2,1,0:T(8,128)(2,1)S(1)}, u32[]{:S(2)}, u32[]{:S(2)}) async-start(bf16[16,64,128]{2,1,0:T(8,128)(2,1)} %bitcast.7), calls=%async_computation.1 | async-start | bytes 524288 | tf_op jit(solution)/shard_map/all_to_all | solution.py:434
  67.7 6.9 %copy-start.1 = (bf16[1,64,1024]{2,1,0:T(8,128)(2,1)S(1)}, bf16[1,64,1024]{2,1,0:T(8,128)(2,1)}, u32[]{:S(2)}) copy-start(bf16[1,64,1024]{2,1,0:T(8,128)(2,1)} %get-tuple-element.44.refs_0_) | copy-start | bytes 393220
  67.7 6.9 %copy-start.3 = (f32[128]{0:T(128)S(1)}, f32[128]{0:T(128)}, u32[]{:S(2)}) copy-start(f32[128]{0:T(128)} %param.12) | copy-start | bytes 1540
  67.8 1.6 %collective-permute-start.15 = (bf16[2,64,1152]{2,1,0:T(8,128)(2,1)S(1)}, bf16[2,64,1152]{2,1,0:T(8,128)(2,1)S(1)}, u32[]{:S(2)}, u32[]{:S(2)}) collective-permute-start(bf16[2,64,1152]{2,1,0:T(8,128)(2,1)S(1)} %bitcast.24), channel_id=1, source_target_pairs={{0,2},{2,0},{1,3},{3,1},{4,6},{6,4},{5,7},{7,5},{8,10},{10,8},{9,1... | collective-permute-start | bytes 884744 | tf_op jit(solution)/shard_map/ppermute | solution.py:438
  68.1 1.8 %collective-permute-start.16 = (bf16[2,64,1152]{2,1,0:T(8,128)(2,1)S(1)}, bf16[2,64,1152]{2,1,0:T(8,128)(2,1)S(1)}, u32[]{:S(2)}, u32[]{:S(2)}) collective-permute-start(bf16[2,64,1152]{2,1,0:T(8,128)(2,1)S(1)} %collective-permute-done.11.refs_1_), channel_id=1, source_target_pairs={{0,2},{2,0},{1,3},{3,1},{4,6},{6,4},{5,7},{7,5},{8,10},{10,8},{9,1... | collective-permute-start | bytes 884744 | tf_op jit(solution)/shard_map/ppermute | solution.py:438
  68.4 1.9 %collective-permute-start.17 = (bf16[2,64,1152]{2,1,0:T(8,128)(2,1)S(1)}, bf16[2,64,1152]{2,1,0:T(8,128)(2,1)S(1)}, u32[]{:S(2)}, u32[]{:S(2)}) collective-permute-start(bf16[2,64,1152]{2,1,0:T(8,128)(2,1)S(1)} %collective-permute-done.12.refs_2_), channel_id=1, source_target_pairs={{0,2},{2,0},{1,3},{3,1},{4,6},{6,4},{5,7},{7,5},{8,10},{10,8},{9,1... | collective-permute-start | bytes 884744 | tf_op jit(solution)/shard_map/ppermute | solution.py:438
  68.6 2.1 %collective-permute-start.18 = (bf16[2,64,1152]{2,1,0:T(8,128)(2,1)S(1)}, bf16[2,64,1152]{2,1,0:T(8,128)(2,1)S(1)}, u32[]{:S(2)}, u32[]{:S(2)}) collective-permute-start(bf16[2,64,1152]{2,1,0:T(8,128)(2,1)S(1)} %collective-permute-done.13.refs_3_), channel_id=1, source_target_pairs={{0,2},{2,0},{1,3},{3,1},{4,6},{6,4},{5,7},{7,5},{8,10},{10,8},{9,1... | collective-permute-start | bytes 884744 | tf_op jit(solution)/shard_map/ppermute | solution.py:438
  78.4 17.6 %copy-start.4 = (bf16[1024,1024]{1,0:T(8,128)(2,1)S(1)}, bf16[1024,1024]{1,0:T(8,128)(2,1)}, u32[]{:S(2)}) copy-start(bf16[1024,1024]{1,0:T(8,128)(2,1)} %get-tuple-element.28.normed_any.normed_ref) | copy-start | bytes 6291460
  89.7 6.3 %collective-permute-start.19 = (bf16[128,256]{1,0:T(8,128)(2,1)S(1)}, bf16[128,256]{1,0:T(8,128)(2,1)S(1)}, u32[]{:S(2)}, u32[]{:S(2)}) collective-permute-start(bf16[128,256]{1,0:T(8,128)(2,1)S(1)} %get-tuple-element.47), channel_id=1, source_target_pairs={{0,16},{16,0},{1,17},{17,1},{2,18},{18,2},{3,19},{19,3},{4,20},{20... | collective-permute-start | bytes 196616 | tf_op jit(solution)/shard_map/ppermute | solution.py:438
  98.1 19.4 %all-to-all-start.3 = ((bf16[32,32,256]{2,1,0:T(8,128)(2,1)}), bf16[32,32,256]{2,1,0:T(8,128)(2,1)S(1)}, u32[]{:S(2)}, u32[]{:S(2)}) async-start(bf16[32,32,256]{2,1,0:T(8,128)(2,1)} %bitcast.11), calls=%async_computation.3 | async-start | bytes 1048576 | tf_op jit(solution)/shard_map/all_to_all | solution.py:434
  101.6 6.0 %collective-permute-start.20 = (f32[100,128]{1,0:T(8,128)S(1)}, f32[100,128]{1,0:T(8,128)S(1)}, u32[]{:S(2)}, u32[]{:S(2)}) collective-permute-start(f32[100,128]{1,0:T(8,128)S(1)} %get-tuple-element.50), channel_id=1, source_target_pairs={{0,1},{1,0},{2,3},{3,2},{4,5},{5,4},{6,7},{7,6},{8,9},{9,8},{10,11... | collective-permute-start | bytes 153608 | tf_op jit(solution)/shard_map/ppermute | solution.py:438

commit v9 on v8

--- a/solution.py
+++ b/solution.py
@@ -96,21 +96,17 @@
     packed_any,
     *refs,
 ):
-    parts, (source, normed, w, columns, readout, readout_pad, sems) = refs[:-7], refs[-7:]
+    parts, (source, normed, w, columns, readout, packed, sems) = refs[:-7], refs[-7:]
     ens = lax.axis_index("ens")
-    copies = fetch([(source_any, source), (w_any, w), (readout_any, readout)], sems)
-    moves = [(mix_any, packed_any.at[:, :LATENT_DIM])]
-    for step, part_any in enumerate(parts):
-        if len(parts) == 1:
-            moves += [
-                (source_any.at[pl.ds(m * part_any.shape[1], part_any.shape[1])], part_any.at[m])
-                for m in range(part_any.shape[0])
-            ]
-        else:
-            part = part_any.shape[1]
-            place = pl.multiple_of((ens ^ step) * part, part)
-            moves.append((source_any.at[pl.ds(place, part)], part_any.at[0]))
-    moves = fetch(moves, sems, 3)
+    copies = fetch(
+        [
+            (source_any, source),
+            (w_any, w),
+            (readout_any, readout),
+            (mix_any, packed.at[:, :LATENT_DIM]),
+        ],
+        sems,
+    )
     rows = source.shape[0]
     row = lax.broadcasted_iota(jnp.int32, (NOTE_ROWS, 128), 0)
     lane = lax.broadcasted_iota(jnp.int32, (NOTE_ROWS, 128), 1)
@@ -128,8 +124,14 @@
     states = source[...].astype(F32)
     inverse = lax.rsqrt(jnp.mean(states * states, axis=-1, keepdims=True) + NORM_EPS)
     normed[:rows, :] = (states * inverse).astype(BF16)
-    first = 3 + len(moves)
-    out = fetch([(normed, normed_any)], sems, first)
+    moves = [(normed, normed_any)]
+    for step, part_any in enumerate(parts):
+        count, part, _ = part_any.shape
+        for m in range(count):
+            place = (ens ^ step) if len(parts) == 2 else m
+            place = pl.multiple_of(place * part, part)
+            moves.append((source.at[pl.ds(place, part)], part_any.at[m]))
+    out = fetch(moves, sems, 4)
     copies[1].wait()
     for g in range(GROUP):
         for part in range(3):
@@ -143,13 +145,14 @@
             for m in range(members_num)
         ],
         sems,
-        first + 1,
+        4 + len(out),
     )
     copies[2].wait()
-    readout_pad[...] = jnp.zeros_like(readout_pad)
-    readout_pad[:, :FIELD_NUM] = readout[...]
-    out += fetch([(readout_pad, packed_any.at[:, LATENT_DIM:])], sems, first + len(out))
-    wait(moves + out)
+    copies[3].wait()
+    packed[:, LATENT_DIM:] = jnp.zeros((packed.shape[0], FIELD_PAD), BF16)
+    packed[:, LATENT_DIM : LATENT_DIM + FIELD_NUM] = readout[...]
+    out += fetch([(packed, packed_any)], sems, 4 + len(out))
+    wait(out)
 
 
 def owners():
@@ -176,28 +179,37 @@
         rims[0][...], rims[1][...] = first, last
 
 
-def project_kernel(normed_any, *refs):
-    columns, (normed, w, sems) = refs[:-3], refs[-3:]
-    columns, (q_ref, kv_ref, *rims) = columns[: w.shape[1] if len(w.shape) == 4 else 1], columns[
-        w.shape[1] if len(w.shape) == 4 else 1 :
-    ]
-    count = normed.shape[0]
-    chunk = count // CHUNKS
-    rows = [slice(at * chunk, (at + 1) * chunk) for at in range(CHUNKS)]
-    if len(columns) == 1:
+def rims_kernel(normed_any, *refs):
+    rows, sems = refs[-2:]
+    if len(refs[0].shape) == 2:
+        columns, w, rims = refs[:1], refs[1], refs[2:-2]
         pairs = [(columns[0], w)]
     else:
+        columns, w, rims = refs[:2], refs[2], refs[3:-2]
         ens = lax.axis_index("ens")
         pairs = [(part, w.at[:, ens ^ step]) for step, part in enumerate(columns)]
-    copies = fetch(pairs + [(normed_any.at[part], normed.at[part]) for part in rows], sems)
-    wait(copies[: len(pairs)])
-    weights = w[...].reshape(LATENT_DIM, 3 * COLS)
-    for part, copy in zip(rows, copies[len(pairs) :]):
+    last = normed_any.shape[0] - RIM
+    if len(rims) == 1:
+        place = pl.multiple_of(jnp.where(lax.axis_index("half") == 0, last, 0), RIM)
+        pairs.append((normed_any.at[pl.ds(place, RIM)], rows.at[0]))
+    else:
+        pairs += [(normed_any.at[:RIM], rows.at[0]), (normed_any.at[last:], rows.at[1])]
+    wait(fetch(pairs, sems))
+    weights = w[...].reshape(LATENT_DIM, 3 * COLS)[:, COLS:]
+    for at, rim_ref in enumerate(rims):
+        rim_ref[...] = jnp.dot(rows[at], weights, preferred_element_type=F32).astype(BF16)
+
+
+def project_kernel(normed_any, w_ref, q_ref, kv_ref, normed, sems):
+    chunk = normed.shape[0] // CHUNKS
+    rows = [slice(at * chunk, (at + 1) * chunk) for at in range(CHUNKS)]
+    copies = fetch([(normed_any.at[part], normed.at[part]) for part in rows], sems)
+    weights = w_ref[...].reshape(LATENT_DIM, 3 * COLS)
+    for part, copy in zip(rows, copies):
         copy.wait()
         projected = jnp.dot(normed[part, :], weights, preferred_element_type=F32).astype(BF16)
-        q_ref[part, :] = projected[:, :COLS]
+        q_ref[part, :] = projected[:, :COLS] * jnp.asarray(HEAD**-0.5, BF16)
         kv_ref[part, :] = projected[:, COLS:]
-    put_rims(rims, kv_ref[:RIM, :], kv_ref[count - RIM :, :])
 
 
 def assemble_kernel(*refs):
@@ -231,16 +243,16 @@
     return jnp.where(row == 0, masks[0], masks[1]) > 0
 
 
-def probabilities(queries, keys, usable):
-    scores = lax.dot_general(queries, keys, OVER_COLUMNS, preferred_element_type=F32) * (HEAD**-0.5)
+def raised_scores(queries, keys, usable):
+    scores = lax.dot_general(queries, keys, OVER_COLUMNS, preferred_element_type=F32)
     scores = jnp.where(usable, scores, MASKED)
     raised = jnp.exp(scores - jnp.max(scores, axis=-1, keepdims=True))
-    return raised * (1.0 / jnp.sum(raised, axis=-1, keepdims=True))
+    return raised, 1.0 / jnp.sum(raised, axis=-1, keepdims=True)
 
 
 def attend(steps_ref, pair, queries, keys, values):
-    probs = probabilities(by_head(queries), keys, usable_keys(steps_ref, pair))
-    both = jnp.dot(probs.astype(BF16), values, preferred_element_type=F32)
+    raised, share = raised_scores(by_head(queries), keys, usable_keys(steps_ref, pair))
+    both = jnp.dot(raised.astype(BF16), values, preferred_element_type=F32) * share
     lane = lax.broadcasted_iota(jnp.int32, queries.shape, 1)
     half = PAIR * TILE
     return jnp.where(lane < HEAD, both[:half], both[half:]).astype(BF16)
@@ -273,10 +285,11 @@
 
 def attend_back(steps_ref, pair, queries, grads, keys, values):
     queries, grads = by_head(queries), by_head(grads)
-    probs = probabilities(queries, keys, usable_keys(steps_ref, pair))
+    raised, share = raised_scores(queries, keys, usable_keys(steps_ref, pair))
+    probs = raised * share
     grad_probs = lax.dot_general(grads, values, OVER_COLUMNS, preferred_element_type=F32)
     row_delta = jnp.sum(probs * grad_probs, axis=-1, keepdims=True)
-    grad_scores = (probs * (grad_probs - row_delta) * (HEAD**-0.5)).astype(BF16)
+    grad_scores = (probs * (grad_probs - row_delta)).astype(BF16)
     key_grad = lax.dot_general(grad_scores, queries, OVER_ROWS, preferred_element_type=F32)
     value_grad = lax.dot_general(probs.astype(BF16), grads, OVER_ROWS, preferred_element_type=F32)
     return key_grad, value_grad
@@ -478,7 +491,7 @@
             pltpu.VMEM(w_attn.shape, BF16),
             pltpu.VMEM((GROUP, shard, 3 * COLS), BF16),
             pltpu.VMEM(readout_matrix.shape, BF16),
-            pltpu.VMEM((shard, FIELD_PAD), BF16),
+            pltpu.VMEM((shard, width), BF16),
             pltpu.SemaphoreType.DMA((6 + max(2, members_num) + halves * copies,)),
         ],
         flops=2**20,
@@ -486,7 +499,7 @@
         results="hhh" + "h" * source_parts,
     )(neighbours, members.reshape(node_rows, LATENT_DIM), w_attn, w_mix, readout_matrix)
 
-    packed = in_order(packed, "half", 0)
+    packed, normed = lax.optimization_barrier((in_order(packed, "half", 0), normed))
     near = [normed] + [swap(normed, "quad", step) for step in range(1, QUAD)]
     if paired:
         columns = exchange(columns.reshape(-1, shard, 3 * COLS), nodes)
@@ -516,23 +529,16 @@
 
     rim = ((RIM, 2 * COLS), BF16)
     rims = [rim] if halves == 2 else [rim, rim]
-    queries, own, *inner = call(
-        project_kernel,
-        "project",
-        [((rows, COLS), BF16), ((rows, 2 * COLS), BF16)] + rims,
+    w_shape = (GROUP * halves, 2, shard, 3 * COLS) if paired else (LATENT_DIM, 3 * COLS)
+    weights, *inner = call(
+        rims_kernel,
+        "project_rims",
+        [(w_shape, BF16)] + rims,
         "h" + "a" * len(columns),
-        [
-            pltpu.VMEM((rows, LATENT_DIM), BF16),
-            pltpu.VMEM(
-                (GROUP * halves, 2, shard, 3 * COLS) if paired else (LATENT_DIM, 3 * COLS), BF16
-            ),
-            pltpu.SemaphoreType.DMA((CHUNKS + 2,)),
-        ],
-        flops=rows * LATENT_DIM * 6 * COLS,
-        moved=4 * 2**20,
-        room=10,
+        [pltpu.VMEM((len(rims), RIM, LATENT_DIM), BF16), pltpu.SemaphoreType.DMA((4,))],
+        flops=RIM * LATENT_DIM * 4 * COLS,
+        moved=2**20,
     )(normed, *columns)
-
     def across(inner):
         if halves == 2:
             got = swap(inner[0], "half", 1)
@@ -540,6 +546,15 @@
         return lax.ppermute(inner[1], "half", up), lax.ppermute(inner[0], "half", down)
 
     low, high = across(inner)
+    queries, own = call(
+        project_kernel,
+        "project",
+        [((rows, COLS), BF16), ((rows, 2 * COLS), BF16)],
+        "hv",
+        [pltpu.VMEM((rows, LATENT_DIM), BF16), pltpu.SemaphoreType.DMA((CHUNKS,))],
+        flops=rows * LATENT_DIM * 6 * COLS,
+        moved=4 * 2**20,
+    )(normed, weights)
 
     (outcome,) = call(
         interior_kernel,

time: 119 us -> 113 us (0.950)
  waiting for transfers between devices: 30.3 us -> 39.2 us
  Pallas kernels: 33.7 us -> 24.9 us
  starting transfers between devices: 40.9 us -> 34.8 us
    ppermute x21, waiting for transfers between devices: 18.3 us -> 27.7 us  [swap(): lax.ppermute(value, axis, [(i, i ^ step) for i in range(lax.axis_size(axi...]
    pallas_call x11 -> x12, Pallas kernels: 33.7 us -> 24.9 us  [run(): made(*[pltpu.with_memory_space_constraint(arg, pltpu.HBM) if space == 'h'...]
    ppermute x21, starting transfers between devices: 25.4 us -> 22.3 us  [swap(): lax.ppermute(value, axis, [(i, i ^ step) for i in range(lax.axis_size(axi...]
    all_to_all x3, starting transfers between devices: 15.5 us -> 12.5 us  [exchange(): return lax.all_to_all(chunks, axes, 0, 0)]
  transfers between devices with their start and end apart: 24 -> 24, of which waited for: 11 -> 12; matrix products, arithmetic and copies ran while one was open for 2% -> 2% of each run, Pallas kernels for 12% -> 13%
where the time goes in v9:
time: 113 us; the launch traced here: 112 us
  waiting for transfers between devices  39.2 us (35%)
  starting transfers between devices  34.8 us (31%)
  Pallas kernels  24.9 us (22%)
  blocking collectives  9.88 us (9%)
  local copies, waits for them, and re-layouts  1.47 us (1%)
    ppermute x21, waiting for transfers between devices, swap(): lax.ppermute(value, axis, [(i, i ^ step) for i in range(lax.axis_size(axi...  27.7 us
    pallas_call x12, Pallas kernels, run(): made(*[pltpu.with_memory_space_constraint(arg, pltpu.HBM) if space == 'h'...  24.9 us
    ppermute x21, starting transfers between devices, swap(): lax.ppermute(value, axis, [(i, i ^ step) for i in range(lax.axis_size(axi...  22.3 us
    all_to_all x3, starting transfers between devices, exchange(): return lax.all_to_all(chunks, axes, 0, 0)  12.5 us
    all_to_all x3, waiting for transfers between devices, exchange(): return lax.all_to_all(chunks, axes, 0, 0)  11.5 us
    all_to_all x1, blocking collectives, exchange(): return lax.all_to_all(chunks, axes, 0, 0)  9.88 us
  transfers between devices with their start and end apart: 24, of which 12 were waited for; matrix products, arithmetic and copies ran while one was open for 2% of the time, Pallas kernels for 13%

profile of v9, /device:TPU:1, one launch (start us, length us, event | category | flops | bytes accessed | tf_op | source)
XLA Modules:
  0.0 112.3 jit_solution(16269674580222086603)
XLA Ops:
  0.6 0.7 copy-done.5
  1.3 2.7 %prepare.1 = (bf16[144,1024]{1,0:T(8,128)(2,1)}, bf16[2,8,1,32,384]{4,3,2,1,0:T(8,128)(2,1)}, bf16[32,1152]{1,0:T(8,128)(2,1)}, bf16[1,64,1024]{2,1,0:T(8,128)(2,1)}, bf16[1,64,1024]{2,1,0:T(8,128)(2,1)}) custom-call(s32[2,4]{1,0:T(2,128)S(1)} %copy-done.5, bf16[128,1024]{1,0:T(8,128)(2,1)} %bitcast.28, bf16[32,3072]{1,0:T(8,128)(2,1)} %w_any.1, ...), custom_call_target="tpu_custom_call" | custom-call | flops 1048576 | bytes 1048576 | tf_op jit(solution)/shard_map/prepare/pallas_call | solution.py:63
  4.0 3.2 %collective-permute-start = (bf16[32,1152]{1,0:T(8,128)(2,1)}, bf16[32,1152]{1,0:T(8,128)(2,1)S(1)}, u32[]{:S(2)}, u32[]{:S(2)}) collective-permute-start(bf16[32,1152]{1,0:T(8,128)(2,1)} %get-tuple-element.30), channel_id=1, source_target_pairs={{0,16},{16,0},{1,17},{17,1},{2,18},{18,2},{3,19},{19,3},{4,20},{20... | collective-permute-start | bytes 221192 | tf_op jit(solution)/shard_map/ppermute | solution.py:451
  7.2 4.8 %all-to-all-start = ((bf16[16,32,384]{2,1,0:T(8,128)(2,1)}), bf16[16,32,384]{2,1,0:T(8,128)(2,1)S(1)}, u32[]{:S(2)}, u32[]{:S(2)}) async-start(bf16[16,32,384]{2,1,0:T(8,128)(2,1)} %bitcast.27), calls=%async_computation | async-start | bytes 786432 | tf_op jit(solution)/shard_map/all_to_all | solution.py:447
  12.0 0.9 select_bitcast_fusion.3
  12.9 2.4 %collective-permute-start.3 = (bf16[144,1024]{1,0:T(8,128)(2,1)}, bf16[144,1024]{1,0:T(8,128)(2,1)S(1)}, u32[]{:S(2)}, u32[]{:S(2)}) collective-permute-start(bf16[144,1024]{1,0:T(8,128)(2,1)} %get-tuple-element.32.refs_0_), channel_id=1, source_target_pairs={{0,12},{4,8},{8,4},{12,0},{1,13},{5,9},{9,5},{13,1},{2,14},{6,10},... | collective-permute-start | bytes 884744 | tf_op jit(solution)/shard_map/ppermute | solution.py:451
  15.3 0.3 collective-permute-start.1
  15.6 1.2 %collective-permute-start.8 = (bf16[2,32,1152]{2,1,0:T(8,128)(2,1)S(1)}, bf16[2,32,1152]{2,1,0:T(8,128)(2,1)S(1)}, u32[]{:S(2)}, u32[]{:S(2)}) collective-permute-start(bf16[2,32,1152]{2,1,0:T(8,128)(2,1)S(1)} %pad_maximum_fusion.1), channel_id=1, source_target_pairs={{0,1},{1,0},{2,3},{3,2},{4,5},{5,4},{6,7},{7,6},{8,9},{9,8},{10,11... | collective-permute-start | bytes 442376 | tf_op jit(solution)/shard_map/ppermute | solution.py:451
  16.8 1.6 %collective-permute-start.4 = (bf16[144,1024]{1,0:T(8,128)(2,1)}, bf16[144,1024]{1,0:T(8,128)(2,1)S(1)}, u32[]{:S(2)}, u32[]{:S(2)}) collective-permute-start(bf16[144,1024]{1,0:T(8,128)(2,1)} %get-tuple-element.32.refs_0_), channel_id=1, source_target_pairs={{0,2},{2,0},{1,3},{3,1},{4,6},{6,4},{5,7},{7,5},{8,10},{10,8},{9,1... | collective-permute-start | bytes 884744 | tf_op jit(solution)/shard_map/ppermute | solution.py:451
  18.5 9.4 %collective-permute-done.3.refs_3_ = bf16[144,1024]{1,0:T(8,128)(2,1)S(1)} collective-permute-done((bf16[144,1024]{1,0:T(8,128)(2,1)}, bf16[144,1024]{1,0:T(8,128)(2,1)S(1)}, u32[]{:S(2)}, u32[]{:S(2)}) %collective-permute-start.3) | collective-permute-done | bytes 294944 | tf_op jit(solution)/shard_map/ppermute | solution.py:451
  27.9 1.3 %collective-permute-start.7 = (bf16[144,1024]{1,0:T(8,128)(2,1)S(1)}, bf16[144,1024]{1,0:T(8,128)(2,1)S(1)}, u32[]{:S(2)}, u32[]{:S(2)}) collective-permute-start(bf16[144,1024]{1,0:T(8,128)(2,1)S(1)} %collective-permute-done.3.refs_3_), channel_id=1, source_target_pairs={{0,2},{2,0},{1,3},{3,1},{4,6},{6,4},{5,7},{7,5},{8,10},{10,8},{9,1... | collective-permute-start | bytes 884744 | tf_op jit(solution)/shard_map/ppermute | solution.py:451
  29.2 2.9 %collective-permute-done.1.refs_1_ = bf16[144,1024]{1,0:T(8,128)(2,1)S(1)} collective-permute-done((bf16[144,1024]{1,0:T(8,128)(2,1)}, bf16[144,1024]{1,0:T(8,128)(2,1)S(1)}, u32[]{:S(2)}, u32[]{:S(2)}) %collective-permute-start.1) | collective-permute-done | bytes 294944 | tf_op jit(solution)/shard_map/ppermute | solution.py:451
  32.1 1.0 collective-permute-start.5
  33.3 0.9 collective-permute-start.6
  34.2 1.2 %collective-permute-start.9 = (bf16[16,32,384]{2,1,0:T(8,128)(2,1)S(1)}, bf16[16,32,384]{2,1,0:T(8,128)(2,1)S(1)}, u32[]{:S(2)}, u32[]{:S(2)}) collective-permute-start(bf16[16,32,384]{2,1,0:T(8,128)(2,1)S(1)} %all-to-all-done.refs_0_), channel_id=1, source_target_pairs={{0,1},{1,0},{2,3},{3,2},{4,5},{5,4},{6,7},{7,6},{8,9},{9,8},{10,11... | collective-permute-start | bytes 1179656 | tf_op jit(solution)/shard_map/ppermute | solution.py:451
  35.4 0.3 collective-permute-start.10
  35.9 1.6 %collect.1 = (bf16[1024,1024]{1,0:T(8,128)(2,1)}, f32[8,16,128]{2,1,0:T(8,128)S(1)}) custom-call(bf16[144,1024]{1,0:T(8,128)(2,1)S(1)} %copy-done.1, bf16[144,1024]{1,0:T(8,128)(2,1)S(1)} %collective-permute-done.1.refs_1_, bf16[144,1024]{1,0:T(8,128)(2,1)S(1)} %collective-permute-done.2.refs_2_, bf16[144,1024]{1,0:T(8,128)(2,1)S(1)} %collective-permute-done.3.refs_3_, ...), custom_call_target="tpu_custom_call" | custom-call | bytes 4194304 | tf_op jit(solution)/shard_map/collect/pallas_call | solution.py:63
  37.4 1.2 %collective-permute-start.11 = (bf16[2,64,1152]{2,1,0:T(8,128)(2,1)S(1)}, bf16[2,64,1152]{2,1,0:T(8,128)(2,1)S(1)}, u32[]{:S(2)}, u32[]{:S(2)}) collective-permute-start(bf16[2,64,1152]{2,1,0:T(8,128)(2,1)S(1)} %bitcast.21), channel_id=1, source_target_pairs={{0,4},{4,0},{8,12},{12,8},{1,5},{5,1},{9,13},{13,9},{2,6},{6,2},{1... | collective-permute-start | bytes 884744 | tf_op jit(solution)/shard_map/ppermute | solution.py:451
  38.7 0.9 collective-permute-start.12
  39.6 0.5 collective-permute-start.13
  40.1 7.5 %collective-permute-done.10.refs_1_ = bf16[1,64,1024]{2,1,0:T(8,128)(2,1)S(1)} collective-permute-done((bf16[1,64,1024]{2,1,0:T(8,128)(2,1)}, bf16[1,64,1024]{2,1,0:T(8,128)(2,1)S(1)}, u32[]{:S(2)}, u32[]{:S(2)}) %collective-permute-start.10) | collective-permute-done | bytes 131104 | tf_op jit(solution)/shard_map/ppermute | solution.py:451
  47.7 1.3 %project_rims.1 = (bf16[16,2,32,384]{3,2,1,0:T(8,128)(2,1)S(1)}, bf16[128,256]{1,0:T(8,128)(2,1)S(1)}) custom-call(bf16[1024,1024]{1,0:T(8,128)(2,1)} %get-tuple-element.33.normed_any.normed_ref, bf16[16,32,384]{2,1,0:T(8,128)(2,1)S(1)} %all-to-all-done.refs_0_, bf16[16,32,384]{2,1,0:T(8,128)(2,1)S(1)} %collective-permute-done.9.refs_1_), custom_call_target="tpu_custom_call" | custom-call | flops 67108864 | bytes 1048576 | tf_op jit(solution)/shard_map/project_rims/pallas_call | solution.py:63
  49.0 2.4 %collective-permute-start.14 = (bf16[128,256]{1,0:T(8,128)(2,1)S(1)}, bf16[128,256]{1,0:T(8,128)(2,1)S(1)}, u32[]{:S(2)}, u32[]{:S(2)}) collective-permute-start(bf16[128,256]{1,0:T(8,128)(2,1)S(1)} %get-tuple-element.45), channel_id=1, source_target_pairs={{0,16},{16,0},{1,17},{17,1},{2,18},{18,2},{3,19},{19,3},{4,20},{20... | collective-permute-start | bytes 196616 | tf_op jit(solution)/shard_map/ppermute | solution.py:451
  51.4 2.8 %project.1 = (bf16[1024,128]{1,0:T(8,128)(2,1)S(1)}, bf16[1024,256]{1,0:T(8,128)(2,1)S(1)}) custom-call(bf16[1024,1024]{1,0:T(8,128)(2,1)} %get-tuple-element.33.normed_any.normed_ref, bf16[16,2,32,384]{3,2,1,0:T(8,128)(2,1)S(1)} %get-tuple-element.40.w_ref), custom_call_target="tpu_custom_call" | custom-call | flops 805306368 | bytes 4194304 | tf_op jit(solution)/shard_map/project/pallas_call | solution.py:63
  54.2 1.9 %attention_interior.1.done_ref = bf16[1024,128]{1,0:T(8,128)(2,1)S(1)} custom-call(f32[8,16,128]{2,1,0:T(8,128)S(1)} %get-tuple-element.34.steps_ref, bf16[1024,128]{1,0:T(8,128)(2,1)S(1)} %get-tuple-element.41.q_ref, bf16[1024,256]{1,0:T(8,128)(2,1)S(1)} %get-tuple-element.44.kv_ref), custom_call_target="tpu_custom_call" | custom-call | flops 268435456 | bytes 2097152 | tf_op jit(solution)/shard_map/attention_interior/pallas_call | solution.py:63
  56.1 1.4 %attention_edges.1 = bf16[1024,128]{1,0:T(8,128)(2,1)} custom-call(f32[8,16,128]{2,1,0:T(8,128)S(1)} %get-tuple-element.34.steps_ref, bf16[1024,128]{1,0:T(8,128)(2,1)S(1)} %get-tuple-element.41.q_ref, bf16[1024,256]{1,0:T(8,128)(2,1)S(1)} %get-tuple-element.44.kv_ref, bf16[128,256]{1,0:T(8,128)(2,1)S(1)} %collective-permute-done.14.low_ref.high_ref, ...), custom_call_target="tpu_custom_call" | custom-call | flops 67108864 | bytes 1048576 | tf_op jit(solution)/shard_map/attention_edges/pallas_call | solution.py:63
  57.6 5.0 %all-to-all-start.1 = ((bf16[16,64,128]{2,1,0:T(8,128)(2,1)}), bf16[16,64,128]{2,1,0:T(8,128)(2,1)S(1)}, u32[]{:S(2)}, u32[]{:S(2)}) async-start(bf16[16,64,128]{2,1,0:T(8,128)(2,1)} %bitcast.7), calls=%async_computation.1 | async-start | bytes 524288 | tf_op jit(solution)/shard_map/all_to_all | solution.py:447
  62.8 0.4 collective-permute-start.16
  63.3 0.4 collective-permute-start.18
  63.7 0.6 collective-permute-done.15.refs_4_
  64.3 0.4 collective-permute-done.16.refs_5_
  64.7 0.4 collective-permute-done.17.refs_6_
  65.1 0.4 collective-permute-done.18.refs_7_
  65.6 1.5 %assemble.1.w_any = bf16[2,4,2,64,1152]{4,3,2,1,0:T(8,128)(2,1)} custom-call(bf16[2,64,1152]{2,1,0:T(8,128)(2,1)S(1)} %bitcast.25, bf16[2,64,1152]{2,1,0:T(8,128)(2,1)S(1)} %collective-permute-done.11.refs_1_, bf16[2,64,1152]{2,1,0:T(8,128)(2,1)S(1)} %collective-permute-done.12.refs_2_, bf16[2,64,1152]{2,1,0:T(8,128)(2,1)S(1)} %collective-permute-done.13.refs_3_, ...), custom_call_target="tpu_custom_call" | custom-call | bytes 4194304 | tf_op jit(solution)/shard_map/assemble/pallas_call | solution.py:63
  67.0 2.4 %all-to-all-done.1.att_ref = bf16[16,64,128]{2,1,0:T(8,128)(2,1)S(1)} async-done(((bf16[16,64,128]{2,1,0:T(8,128)(2,1)}), bf16[16,64,128]{2,1,0:T(8,128)(2,1)S(1)}, u32[]{:S(2)}, u32[]{:S(2)}) %all-to-all-start.1) | async-done | bytes 262176 | tf_op jit(solution)/shard_map/all_to_all | solution.py:447
  69.5 3.7 %mix_loss_backward.1 = (f32[100,128]{1,0:T(8,128)S(1)}, bf16[16,64,128]{2,1,0:T(8,128)(2,1)S(1)}) custom-call(bf16[16,64,128]{2,1,0:T(8,128)(2,1)S(1)} %all-to-all-done.1.att_ref, f32[1,128]{1,0:T(1,128)S(1)} %bitcast.26, f32[100,128]{1,0:T(8,128)} %truth_any.1, bf16[2,4,2,64,1152]{4,3,2,1,0:T(8,128)(2,1)} %assemble.1.w_any, ...), custom_call_target="tpu_custom_call" | custom-call | flops 603979776 | bytes 4194304 | tf_op jit(solution)/shard_map/mix_loss_backward/pallas_call | solution.py:63
  73.2 9.9 %all_to_all.20 = bf16[16,64,128]{2,1,0:T(8,128)(2,1)S(1)} all-to-all(bf16[16,64,128]{2,1,0:T(8,128)(2,1)S(1)} %get-tuple-element.52), channel_id=1, replica_groups=mesh['half'=2,'quad'=4,'core'=2,'ens'=2] {'quad','core','ens'}, dimensions={0} | all-to-all | bytes 524288 | tf_op jit(solution)/shard_map/all_to_all | solution.py:447
  83.1 1.4 %attention_edges_back.1 = (f32[2,256,256]{2,1,0:T(8,128)S(1)}, bf16[128,256]{1,0:T(8,128)(2,1)S(1)}) custom-call(f32[8,16,128]{2,1,0:T(8,128)S(1)} %get-tuple-element.34.steps_ref, bf16[1024,128]{1,0:T(8,128)(2,1)S(1)} %get-tuple-element.41.q_ref, bf16[1024,256]{1,0:T(8,128)(2,1)S(1)} %get-tuple-element.44.kv_ref, ...), custom_call_target="tpu_custom_call" | custom-call | flops 167772160 | bytes 1048576 | tf_op jit(solution)/shard_map/attention_edges_back/pallas_call | solution.py:63
  84.5 1.1 collective-permute-start.19
  85.6 3.8 %attention_interior_back.1.grads_ref = f32[1024,256]{1,0:T(8,128)S(1)} custom-call(f32[8,16,128]{2,1,0:T(8,128)S(1)} %get-tuple-element.34.steps_ref, bf16[1024,128]{1,0:T(8,128)(2,1)S(1)} %get-tuple-element.41.q_ref, bf16[1024,256]{1,0:T(8,128)(2,1)S(1)} %get-tuple-element.44.kv_ref, bf16[1024,128]{1,0:T(8,128)(2,1)S(1)} %bitcast.19, ...), custom_call_target="tpu_custom_call" | custom-call | flops 536870912 | bytes 4194304 | tf_op jit(solution)/shard_map/attention_interior_back/pallas_call | solution.py:63
  89.4 1.3 %collective-permute-done.19.from_low_ref.from_high_ref = bf16[128,256]{1,0:T(8,128)(2,1)S(1)} collective-permute-done((bf16[128,256]{1,0:T(8,128)(2,1)S(1)}, bf16[128,256]{1,0:T(8,128)(2,1)S(1)}, u32[]{:S(2)}, u32[]{:S(2)}) %collective-permute-start.19) | collective-permute-done | bytes 65568 | tf_op jit(solution)/shard_map/ppermute | solution.py:451
  90.7 2.1 %product.1 = bf16[1024,256]{1,0:T(8,128)(2,1)} custom-call(bf16[1024,1024]{1,0:T(8,128)(2,1)S(1)} %copy-done, bf16[128,256]{1,0:T(8,128)(2,1)S(1)} %collective-permute-done.19.from_low_ref.from_high_ref, bf16[128,256]{1,0:T(8,128)(2,1)S(1)} %collective-permute-done.19.from_low_ref.from_high_ref, f32[1024,256]{1,0:T(8,128)S(1)} %attention_interior_back.1.grads_ref), custom_call_target="tpu_custom_call" | custom-call | flops 1073741824 | bytes 4194304 | tf_op jit(solution)/shard_map/product/pallas_call | solution.py:63
  92.8 2.8 %all-to-all-start.3 = ((bf16[32,32,256]{2,1,0:T(8,128)(2,1)}), bf16[32,32,256]{2,1,0:T(8,128)(2,1)S(1)}, u32[]{:S(2)}, u32[]{:S(2)}) async-start(bf16[32,32,256]{2,1,0:T(8,128)(2,1)} %bitcast.11), calls=%async_computation.3 | async-start | bytes 1048576 | tf_op jit(solution)/shard_map/all_to_all | solution.py:447
  95.6 1.5 %collective-permute-start.20 = (f32[100,128]{1,0:T(8,128)S(1)}, f32[100,128]{1,0:T(8,128)S(1)}, u32[]{:S(2)}, u32[]{:S(2)}) collective-permute-start(f32[100,128]{1,0:T(8,128)S(1)} %get-tuple-element.56), channel_id=1, source_target_pairs={{0,1},{1,0},{2,3},{3,2},{4,5},{5,4},{6,7},{7,6},{8,9},{9,8},{10,11... | collective-permute-start | bytes 153608 | tf_op jit(solution)/shard_map/ppermute | solution.py:451
  97.1 4.5 %collective-permute-done.20 = f32[100,128]{1,0:T(8,128)S(1)} collective-permute-done((f32[100,128]{1,0:T(8,128)S(1)}, f32[100,128]{1,0:T(8,128)S(1)}, u32[]{:S(2)}, u32[]{:S(2)}) %collective-permute-start.20) | collective-permute-done | bytes 51232 | tf_op jit(solution)/shard_map/ppermute | solution.py:451
  101.8 0.7 copy.10
  102.5 9.1 %all-to-all-done.3 = bf16[32,32,256]{2,1,0:T(8,128)(2,1)S(1)} async-done(((bf16[32,32,256]{2,1,0:T(8,128)(2,1)}), bf16[32,32,256]{2,1,0:T(8,128)(2,1)S(1)}, u32[]{:S(2)}, u32[]{:S(2)}) %all-to-all-start.3) | async-done | bytes 524320 | tf_op jit(solution)/shard_map/all_to_all | solution.py:447
  111.5 0.8 gather_sums.1
  (37 shorter events, 0.9 us)
Async XLA Ops:
  0.6 0.7 copy-start.5
  4.0 31.9 %copy-start.1 = (bf16[144,1024]{1,0:T(8,128)(2,1)S(1)}, bf16[144,1024]{1,0:T(8,128)(2,1)}, u32[]{:S(2)}) copy-start(bf16[144,1024]{1,0:T(8,128)(2,1)} %get-tuple-element.32.refs_0_) | copy-start | bytes 884740
  4.0 8.0 %collective-permute-start = (bf16[32,1152]{1,0:T(8,128)(2,1)}, bf16[32,1152]{1,0:T(8,128)(2,1)S(1)}, u32[]{:S(2)}, u32[]{:S(2)}) collective-permute-start(bf16[32,1152]{1,0:T(8,128)(2,1)} %get-tuple-element.30), channel_id=1, source_target_pairs={{0,16},{16,0},{1,17},{17,1},{2,18},{18,2},{3,19},{19,3},{4,20},{20... | collective-permute-start | bytes 221192 | tf_op jit(solution)/shard_map/ppermute | solution.py:451
  7.2 27.0 %all-to-all-start = ((bf16[16,32,384]{2,1,0:T(8,128)(2,1)}), bf16[16,32,384]{2,1,0:T(8,128)(2,1)S(1)}, u32[]{:S(2)}, u32[]{:S(2)}) async-start(bf16[16,32,384]{2,1,0:T(8,128)(2,1)} %bitcast.27), calls=%async_computation | async-start | bytes 786432 | tf_op jit(solution)/shard_map/all_to_all | solution.py:447
  12.9 15.0 %collective-permute-start.3 = (bf16[144,1024]{1,0:T(8,128)(2,1)}, bf16[144,1024]{1,0:T(8,128)(2,1)S(1)}, u32[]{:S(2)}, u32[]{:S(2)}) collective-permute-start(bf16[144,1024]{1,0:T(8,128)(2,1)} %get-tuple-element.32.refs_0_), channel_id=1, source_target_pairs={{0,12},{4,8},{8,4},{12,0},{1,13},{5,9},{9,5},{13,1},{2,14},{6,10},... | collective-permute-start | bytes 884744 | tf_op jit(solution)/shard_map/ppermute | solution.py:451
  15.3 16.8 %collective-permute-start.1 = (bf16[144,1024]{1,0:T(8,128)(2,1)}, bf16[144,1024]{1,0:T(8,128)(2,1)S(1)}, u32[]{:S(2)}, u32[]{:S(2)}) collective-permute-start(bf16[144,1024]{1,0:T(8,128)(2,1)} %get-tuple-element.32.refs_0_), channel_id=1, source_target_pairs={{0,4},{4,0},{8,12},{12,8},{1,5},{5,1},{9,13},{13,9},{2,6},{6,2},{1... | collective-permute-start | bytes 884744 | tf_op jit(solution)/shard_map/ppermute | solution.py:451
  15.6 17.7 %collective-permute-start.2 = (bf16[144,1024]{1,0:T(8,128)(2,1)}, bf16[144,1024]{1,0:T(8,128)(2,1)S(1)}, u32[]{:S(2)}, u32[]{:S(2)}) collective-permute-start(bf16[144,1024]{1,0:T(8,128)(2,1)} %get-tuple-element.32.refs_0_), channel_id=1, source_target_pairs={{0,8},{4,12},{8,0},{12,4},{1,9},{5,13},{9,1},{13,5},{2,10},{6,14},... | collective-permute-start | bytes 884744 | tf_op jit(solution)/shard_map/ppermute | solution.py:451
  15.6 18.5 %collective-permute-start.8 = (bf16[2,32,1152]{2,1,0:T(8,128)(2,1)S(1)}, bf16[2,32,1152]{2,1,0:T(8,128)(2,1)S(1)}, u32[]{:S(2)}, u32[]{:S(2)}) collective-permute-start(bf16[2,32,1152]{2,1,0:T(8,128)(2,1)S(1)} %pad_maximum_fusion.1), channel_id=1, source_target_pairs={{0,1},{1,0},{2,3},{3,2},{4,5},{5,4},{6,7},{7,6},{8,9},{9,8},{10,11... | collective-permute-start | bytes 442376 | tf_op jit(solution)/shard_map/ppermute | solution.py:451
  16.8 18.6 %collective-permute-start.4 = (bf16[144,1024]{1,0:T(8,128)(2,1)}, bf16[144,1024]{1,0:T(8,128)(2,1)S(1)}, u32[]{:S(2)}, u32[]{:S(2)}) collective-permute-start(bf16[144,1024]{1,0:T(8,128)(2,1)} %get-tuple-element.32.refs_0_), channel_id=1, source_target_pairs={{0,2},{2,0},{1,3},{3,1},{4,6},{6,4},{5,7},{7,5},{8,10},{10,8},{9,1... | collective-permute-start | bytes 884744 | tf_op jit(solution)/shard_map/ppermute | solution.py:451
  27.9 8.0 %collective-permute-start.7 = (bf16[144,1024]{1,0:T(8,128)(2,1)S(1)}, bf16[144,1024]{1,0:T(8,128)(2,1)S(1)}, u32[]{:S(2)}, u32[]{:S(2)}) collective-permute-start(bf16[144,1024]{1,0:T(8,128)(2,1)S(1)} %collective-permute-done.3.refs_3_), channel_id=1, source_target_pairs={{0,2},{2,0},{1,3},{3,1},{4,6},{6,4},{5,7},{7,5},{8,10},{10,8},{9,1... | collective-permute-start | bytes 884744 | tf_op jit(solution)/shard_map/ppermute | solution.py:451
  32.1 3.8 %collective-permute-start.5 = (bf16[144,1024]{1,0:T(8,128)(2,1)S(1)}, bf16[144,1024]{1,0:T(8,128)(2,1)S(1)}, u32[]{:S(2)}, u32[]{:S(2)}) collective-permute-start(bf16[144,1024]{1,0:T(8,128)(2,1)S(1)} %collective-permute-done.1.refs_1_), channel_id=1, source_target_pairs={{0,2},{2,0},{1,3},{3,1},{4,6},{6,4},{5,7},{7,5},{8,10},{10,8},{9,1... | collective-permute-start | bytes 884744 | tf_op jit(solution)/shard_map/ppermute | solution.py:451
  33.3 2.6 %collective-permute-start.6 = (bf16[144,1024]{1,0:T(8,128)(2,1)S(1)}, bf16[144,1024]{1,0:T(8,128)(2,1)S(1)}, u32[]{:S(2)}, u32[]{:S(2)}) collective-permute-start(bf16[144,1024]{1,0:T(8,128)(2,1)S(1)} %collective-permute-done.2.refs_2_), channel_id=1, source_target_pairs={{0,2},{2,0},{1,3},{3,1},{4,6},{6,4},{5,7},{7,5},{8,10},{10,8},{9,1... | collective-permute-start | bytes 884744 | tf_op jit(solution)/shard_map/ppermute | solution.py:451
  34.2 13.5 %collective-permute-start.9 = (bf16[16,32,384]{2,1,0:T(8,128)(2,1)S(1)}, bf16[16,32,384]{2,1,0:T(8,128)(2,1)S(1)}, u32[]{:S(2)}, u32[]{:S(2)}) collective-permute-start(bf16[16,32,384]{2,1,0:T(8,128)(2,1)S(1)} %all-to-all-done.refs_0_), channel_id=1, source_target_pairs={{0,1},{1,0},{2,3},{3,2},{4,5},{5,4},{6,7},{7,6},{8,9},{9,8},{10,11... | collective-permute-start | bytes 1179656 | tf_op jit(solution)/shard_map/ppermute | solution.py:451
  35.4 12.2 %collective-permute-start.10 = (bf16[1,64,1024]{2,1,0:T(8,128)(2,1)}, bf16[1,64,1024]{2,1,0:T(8,128)(2,1)S(1)}, u32[]{:S(2)}, u32[]{:S(2)}) collective-permute-start(bf16[1,64,1024]{2,1,0:T(8,128)(2,1)} %get-tuple-element.38), channel_id=1, source_target_pairs={{0,1},{1,0},{2,3},{3,2},{4,5},{5,4},{6,7},{7,6},{8,9},{9,8},{10,11... | collective-permute-start | bytes 393224 | tf_op jit(solution)/shard_map/ppermute | solution.py:451
  37.4 25.2 %collective-permute-start.11 = (bf16[2,64,1152]{2,1,0:T(8,128)(2,1)S(1)}, bf16[2,64,1152]{2,1,0:T(8,128)(2,1)S(1)}, u32[]{:S(2)}, u32[]{:S(2)}) collective-permute-start(bf16[2,64,1152]{2,1,0:T(8,128)(2,1)S(1)} %bitcast.21), channel_id=1, source_target_pairs={{0,4},{4,0},{8,12},{12,8},{1,5},{5,1},{9,13},{13,9},{2,6},{6,2},{1... | collective-permute-start | bytes 884744 | tf_op jit(solution)/shard_map/ppermute | solution.py:451
  38.7 24.0 %collective-permute-start.12 = (bf16[2,64,1152]{2,1,0:T(8,128)(2,1)S(1)}, bf16[2,64,1152]{2,1,0:T(8,128)(2,1)S(1)}, u32[]{:S(2)}, u32[]{:S(2)}) collective-permute-start(bf16[2,64,1152]{2,1,0:T(8,128)(2,1)S(1)} %bitcast.22), channel_id=1, source_target_pairs={{0,8},{4,12},{8,0},{12,4},{1,9},{5,13},{9,1},{13,5},{2,10},{6,14},... | collective-permute-start | bytes 884744 | tf_op jit(solution)/shard_map/ppermute | solution.py:451
  39.6 23.0 %collective-permute-start.13 = (bf16[2,64,1152]{2,1,0:T(8,128)(2,1)S(1)}, bf16[2,64,1152]{2,1,0:T(8,128)(2,1)S(1)}, u32[]{:S(2)}, u32[]{:S(2)}) collective-permute-start(bf16[2,64,1152]{2,1,0:T(8,128)(2,1)S(1)} %bitcast.23), channel_id=1, source_target_pairs={{0,12},{4,8},{8,4},{12,0},{1,13},{5,9},{9,5},{13,1},{2,14},{6,10},... | collective-permute-start | bytes 884744 | tf_op jit(solution)/shard_map/ppermute | solution.py:451
  47.7 6.6 %copy-start.3 = (bf16[1,64,1024]{2,1,0:T(8,128)(2,1)}, bf16[1,64,1024]{2,1,0:T(8,128)(2,1)S(1)}, u32[]{:S(2)}) copy-start(bf16[1,64,1024]{2,1,0:T(8,128)(2,1)S(1)} %collective-permute-done.10.refs_1_) | copy-start | bytes 393220
  49.0 7.2 %collective-permute-start.14 = (bf16[128,256]{1,0:T(8,128)(2,1)S(1)}, bf16[128,256]{1,0:T(8,128)(2,1)S(1)}, u32[]{:S(2)}, u32[]{:S(2)}) collective-permute-start(bf16[128,256]{1,0:T(8,128)(2,1)S(1)} %get-tuple-element.45), channel_id=1, source_target_pairs={{0,16},{16,0},{1,17},{17,1},{2,18},{18,2},{3,19},{19,3},{4,20},{20... | collective-permute-start | bytes 196616 | tf_op jit(solution)/shard_map/ppermute | solution.py:451
  57.6 11.9 %all-to-all-start.1 = ((bf16[16,64,128]{2,1,0:T(8,128)(2,1)}), bf16[16,64,128]{2,1,0:T(8,128)(2,1)S(1)}, u32[]{:S(2)}, u32[]{:S(2)}) async-start(bf16[16,64,128]{2,1,0:T(8,128)(2,1)} %bitcast.7), calls=%async_computation.1 | async-start | bytes 524288 | tf_op jit(solution)/shard_map/all_to_all | solution.py:447
  62.6 6.9 %copy-start.2 = (bf16[1,64,1024]{2,1,0:T(8,128)(2,1)S(1)}, bf16[1,64,1024]{2,1,0:T(8,128)(2,1)}, u32[]{:S(2)}) copy-start(bf16[1,64,1024]{2,1,0:T(8,128)(2,1)} %get-tuple-element.50.refs_0_) | copy-start | bytes 393220
  62.6 6.9 %copy-start.4 = (bf16[1,64,1024]{2,1,0:T(8,128)(2,1)S(1)}, bf16[1,64,1024]{2,1,0:T(8,128)(2,1)}, u32[]{:S(2)}) copy-start(bf16[1,64,1024]{2,1,0:T(8,128)(2,1)} %copy-done.3) | copy-start | bytes 393220
  62.6 6.9 %copy-start.6 = (f32[128]{0:T(128)S(1)}, f32[128]{0:T(128)}, u32[]{:S(2)}) copy-start(f32[128]{0:T(128)} %param.12) | copy-start | bytes 1540
  62.7 1.6 %collective-permute-start.15 = (bf16[2,64,1152]{2,1,0:T(8,128)(2,1)S(1)}, bf16[2,64,1152]{2,1,0:T(8,128)(2,1)S(1)}, u32[]{:S(2)}, u32[]{:S(2)}) collective-permute-start(bf16[2,64,1152]{2,1,0:T(8,128)(2,1)S(1)} %bitcast.24), channel_id=1, source_target_pairs={{0,2},{2,0},{1,3},{3,1},{4,6},{6,4},{5,7},{7,5},{8,10},{10,8},{9,1... | collective-permute-start | bytes 884744 | tf_op jit(solution)/shard_map/ppermute | solution.py:451
  62.8 1.9 %collective-permute-start.16 = (bf16[2,64,1152]{2,1,0:T(8,128)(2,1)S(1)}, bf16[2,64,1152]{2,1,0:T(8,128)(2,1)S(1)}, u32[]{:S(2)}, u32[]{:S(2)}) collective-permute-start(bf16[2,64,1152]{2,1,0:T(8,128)(2,1)S(1)} %collective-permute-done.11.refs_1_), channel_id=1, source_target_pairs={{0,2},{2,0},{1,3},{3,1},{4,6},{6,4},{5,7},{7,5},{8,10},{10,8},{9,1... | collective-permute-start | bytes 884744 | tf_op jit(solution)/shard_map/ppermute | solution.py:451
  63.2 1.9 %collective-permute-start.17 = (bf16[2,64,1152]{2,1,0:T(8,128)(2,1)S(1)}, bf16[2,64,1152]{2,1,0:T(8,128)(2,1)S(1)}, u32[]{:S(2)}, u32[]{:S(2)}) collective-permute-start(bf16[2,64,1152]{2,1,0:T(8,128)(2,1)S(1)} %collective-permute-done.12.refs_2_), channel_id=1, source_target_pairs={{0,2},{2,0},{1,3},{3,1},{4,6},{6,4},{5,7},{7,5},{8,10},{10,8},{9,1... | collective-permute-start | bytes 884744 | tf_op jit(solution)/shard_map/ppermute | solution.py:451
  63.3 2.2 %collective-permute-start.18 = (bf16[2,64,1152]{2,1,0:T(8,128)(2,1)S(1)}, bf16[2,64,1152]{2,1,0:T(8,128)(2,1)S(1)}, u32[]{:S(2)}, u32[]{:S(2)}) collective-permute-start(bf16[2,64,1152]{2,1,0:T(8,128)(2,1)S(1)} %collective-permute-done.13.refs_3_), channel_id=1, source_target_pairs={{0,2},{2,0},{1,3},{3,1},{4,6},{6,4},{5,7},{7,5},{8,10},{10,8},{9,1... | collective-permute-start | bytes 884744 | tf_op jit(solution)/shard_map/ppermute | solution.py:451
  73.2 17.6 %copy-start = (bf16[1024,1024]{1,0:T(8,128)(2,1)S(1)}, bf16[1024,1024]{1,0:T(8,128)(2,1)}, u32[]{:S(2)}) copy-start(bf16[1024,1024]{1,0:T(8,128)(2,1)} %get-tuple-element.33.normed_any.normed_ref) | copy-start | bytes 6291460
  84.5 6.3 %collective-permute-start.19 = (bf16[128,256]{1,0:T(8,128)(2,1)S(1)}, bf16[128,256]{1,0:T(8,128)(2,1)S(1)}, u32[]{:S(2)}, u32[]{:S(2)}) collective-permute-start(bf16[128,256]{1,0:T(8,128)(2,1)S(1)} %get-tuple-element.53), channel_id=1, source_target_pairs={{0,16},{16,0},{1,17},{17,1},{2,18},{18,2},{3,19},{19,3},{4,20},{20... | collective-permute-start | bytes 196616 | tf_op jit(solution)/shard_map/ppermute | solution.py:451
  92.8 18.7 %all-to-all-start.3 = ((bf16[32,32,256]{2,1,0:T(8,128)(2,1)}), bf16[32,32,256]{2,1,0:T(8,128)(2,1)S(1)}, u32[]{:S(2)}, u32[]{:S(2)}) async-start(bf16[32,32,256]{2,1,0:T(8,128)(2,1)} %bitcast.11), calls=%async_computation.3 | async-start | bytes 1048576 | tf_op jit(solution)/shard_map/all_to_all | solution.py:447
  95.6 6.0 %collective-permute-start.20 = (f32[100,128]{1,0:T(8,128)S(1)}, f32[100,128]{1,0:T(8,128)S(1)}, u32[]{:S(2)}, u32[]{:S(2)}) collective-permute-start(f32[100,128]{1,0:T(8,128)S(1)} %get-tuple-element.56), channel_id=1, source_target_pairs={{0,1},{1,0},{2,3},{3,2},{4,5},{5,4},{6,7},{7,6},{8,9},{9,8},{10,11... | collective-permute-start | bytes 153608 | tf_op jit(solution)/shard_map/ppermute | solution.py:451

commit v10 on v9

--- a/solution.py
+++ b/solution.py
@@ -85,74 +85,63 @@
         copy.wait()
 
 
-def prepare_kernel(
-    near_ref,
-    source_any,
-    w_any,
-    mix_any,
-    readout_any,
-    normed_any,
-    columns_any,
-    packed_any,
-    *refs,
-):
-    parts, (source, normed, w, columns, readout, packed, sems) = refs[:-7], refs[-7:]
-    ens = lax.axis_index("ens")
+def weights_kernel(w_any, mix_any, readout_any, columns_any, packed_any, *refs):
+    w, columns, readout, packed, sems = refs
     copies = fetch(
+        [(w_any, w), (readout_any, readout), (mix_any, packed.at[:, :LATENT_DIM])], sems
+    )
+    copies[0].wait()
+    for g in range(GROUP):
+        for part in range(3):
+            at = (part * GROUP + g) * COLS
+            columns[g, :, part * COLS : (part + 1) * COLS] = w[:, at : at + COLS]
+    halves, _, members_num = columns_any.shape[:3]
+    out = fetch(
         [
-            (source_any, source),
-            (w_any, w),
-            (readout_any, readout),
-            (mix_any, packed.at[:, :LATENT_DIM]),
+            (columns, columns_any.at[half, :, m])
+            for half in range(halves)
+            for m in range(members_num)
         ],
         sems,
-    )
+        3,
+    )
+    wait(copies[1:])
+    packed[:, LATENT_DIM:] = jnp.zeros((packed.shape[0], FIELD_PAD), BF16)
+    packed[:, LATENT_DIM : LATENT_DIM + FIELD_NUM] = readout[...]
+    wait(out + fetch([(packed, packed_any)], sems, 3 + len(out)))
+
+
+def norm_kernel(near_any, source_any, normed_any, *refs):
+    parts, (near, source, normed, sems) = refs[:-4], refs[-4:]
+    ens = lax.axis_index("ens")
+    copies = fetch([(source_any, source), (near_any, near)], sems)
     rows = source.shape[0]
-    row = lax.broadcasted_iota(jnp.int32, (NOTE_ROWS, 128), 0)
-    lane = lax.broadcasted_iota(jnp.int32, (NOTE_ROWS, 128), 1)
-    note = jnp.zeros((NOTE_ROWS, 128), F32)
-    tiles = near_ref.shape[0]
-    first_tile = lax.axis_index(("half", "quad", "core")) * tiles
-    for tile in range(tiles):
-        for slot in range(K_NB):
-            at = near_ref[tile, slot]
-            step = jnp.where(at >= 0, at - first_tile - tile, NOWHERE).astype(F32)
-            note = jnp.where((row == tile) & (lane == slot), step, note)
-    normed[rows:, :] = jnp.zeros((NOTE_ROWS, LATENT_DIM), BF16)
-    normed[rows:, :128] = note.astype(BF16)
     copies[0].wait()
-    states = source[...].astype(F32)
-    inverse = lax.rsqrt(jnp.mean(states * states, axis=-1, keepdims=True) + NORM_EPS)
-    normed[:rows, :] = (states * inverse).astype(BF16)
-    moves = [(normed, normed_any)]
+    moves = []
     for step, part_any in enumerate(parts):
         count, part, _ = part_any.shape
         for m in range(count):
             place = (ens ^ step) if len(parts) == 2 else m
             place = pl.multiple_of(place * part, part)
             moves.append((source.at[pl.ds(place, part)], part_any.at[m]))
-    out = fetch(moves, sems, 4)
+    out = fetch(moves, sems, 2)
+    states = source[...].astype(F32)
+    inverse = lax.rsqrt(jnp.mean(states * states, axis=-1, keepdims=True) + NORM_EPS)
+    normed[:rows, :] = (states * inverse).astype(BF16)
     copies[1].wait()
-    for g in range(GROUP):
-        for part in range(3):
-            at = (part * GROUP + g) * COLS
-            columns[g, :, part * COLS : (part + 1) * COLS] = w[:, at : at + COLS]
-    halves, _, members_num = columns_any.shape[:3]
-    out += fetch(
-        [
-            (columns, columns_any.at[half, :, m])
-            for half in range(halves)
-            for m in range(members_num)
-        ],
-        sems,
-        4 + len(out),
-    )
-    copies[2].wait()
-    copies[3].wait()
-    packed[:, LATENT_DIM:] = jnp.zeros((packed.shape[0], FIELD_PAD), BF16)
-    packed[:, LATENT_DIM : LATENT_DIM + FIELD_NUM] = readout[...]
-    out += fetch([(packed, packed_any)], sems, 4 + len(out))
-    wait(out)
+    row = lax.broadcasted_iota(jnp.int32, (NOTE_ROWS, 128), 0)
+    lane = lax.broadcasted_iota(jnp.int32, (NOTE_ROWS, 128), 1)
+    note = jnp.zeros((NOTE_ROWS, 128), F32)
+    tiles = near.shape[0]
+    first_tile = lax.axis_index(("half", "quad", "core")) * tiles
+    for tile in range(tiles):
+        for slot in range(K_NB):
+            at = near[tile, slot]
+            step = jnp.where(at >= 0, at - first_tile - tile, NOWHERE).astype(F32)
+            note = jnp.where((row == tile) & (lane == slot), step, note)
+    normed[rows:, :] = jnp.zeros((NOTE_ROWS, LATENT_DIM), BF16)
+    normed[rows:, :128] = note.astype(BF16)
+    wait(out + fetch([(normed, normed_any)], sems, 2 + len(out)))
 
 
 def owners():
@@ -475,38 +464,49 @@
     copies = 1 if paired else members_num
     source_parts = 2 if paired else 1
 
-    normed, columns, packed, *sources = call(
-        prepare_kernel,
-        "prepare",
+    columns, packed = call(
+        weights_kernel,
+        "prepare_weights",
+        [((halves, GROUP, copies, shard, 3 * COLS), BF16), ((shard, width), BF16)],
+        "hhh",
         [
-            ((node_rows + NOTE_ROWS, LATENT_DIM), BF16),
-            ((halves, GROUP, copies, shard, 3 * COLS), BF16),
-            ((shard, width), BF16),
-        ]
-        + [((1 if paired else members_num, part, LATENT_DIM), BF16)] * source_parts,
-        "shhhh",
-        [
-            pltpu.VMEM((node_rows, LATENT_DIM), BF16),
-            pltpu.VMEM((node_rows + NOTE_ROWS, LATENT_DIM), BF16),
             pltpu.VMEM(w_attn.shape, BF16),
             pltpu.VMEM((GROUP, shard, 3 * COLS), BF16),
             pltpu.VMEM(readout_matrix.shape, BF16),
             pltpu.VMEM((shard, width), BF16),
-            pltpu.SemaphoreType.DMA((6 + max(2, members_num) + halves * copies,)),
+            pltpu.SemaphoreType.DMA((4 + halves * copies,)),
+        ],
+        moved=2**20,
+        results="hh",
+    )(w_attn, w_mix, readout_matrix)
+    normed, *sources = call(
+        norm_kernel,
+        "norm",
+        [((node_rows + NOTE_ROWS, LATENT_DIM), BF16)]
+        + [((1 if paired else members_num, part, LATENT_DIM), BF16)] * source_parts,
+        "hh",
+        [
+            pltpu.SMEM(neighbours.shape, jnp.int32),
+            pltpu.VMEM((node_rows, LATENT_DIM), BF16),
+            pltpu.VMEM((node_rows + NOTE_ROWS, LATENT_DIM), BF16),
+            pltpu.SemaphoreType.DMA((3 + max(2, members_num),)),
         ],
         flops=2**20,
         moved=2**20,
-        results="hhh" + "h" * source_parts,
-    )(neighbours, members.reshape(node_rows, LATENT_DIM), w_attn, w_mix, readout_matrix)
+        results="h" + "h" * source_parts,
+    )(neighbours, members.reshape(node_rows, LATENT_DIM))
 
     packed, normed = lax.optimization_barrier((in_order(packed, "half", 0), normed))
-    near = [normed] + [swap(normed, "quad", step) for step in range(1, QUAD)]
+    near = [normed, swap(normed, "quad", 1), None, swap(normed, "quad", 3)]
     if paired:
         columns = exchange(columns.reshape(-1, shard, 3 * COLS), nodes)
+        columns, late = lax.optimization_barrier((columns, normed))
         columns = [columns, swap(columns, "ens", 1)]
     else:
         columns = [exchange(columns.reshape(-1, shard, 3 * COLS), everyone)]
         columns = [columns[0].reshape(LATENT_DIM, 3 * COLS)]
+        late = normed
+    near[2] = swap(late, "quad", 2)
     far = [swap(piece, "core", 1) for piece in near]
     normed, steps = call(
         collect_kernel,
@@ -524,7 +524,7 @@
         columns[1], sources[1] = lax.optimization_barrier((columns[1], sources[1]))
     else:
         sources = [exchange(sources[0], "ens")]
-    packed, far[3], columns[0] = lax.optimization_barrier((packed, far[3], columns[0]))
+    packed, near[2] = lax.optimization_barrier((packed, near[2]))
     pieces = [packed] + [swap(packed, "quad", step) for step in range(1, QUAD)]
 
     rim = ((RIM, 2 * COLS), BF16)

time: 113 us -> 117 us (1.035)
  waiting for transfers between devices: 39.2 us -> 43.9 us
    all_to_all x3, waiting for transfers between devices: 11.5 us -> 17.3 us  [exchange(): return lax.all_to_all(chunks, axes, 0, 0)]
    ppermute x21, starting transfers between devices: 22.3 us -> 18.7 us  [swap(): lax.ppermute(value, axis, [(i, i ^ step) for i in range(lax.axis_size(axi...]
    all_to_all x3, starting transfers between devices: 12.5 us -> 14.9 us  [exchange(): return lax.all_to_all(chunks, axes, 0, 0)]
    pallas_call x12 -> x13, Pallas kernels: 24.9 us -> 25.9 us  [run(): made(*[pltpu.with_memory_space_constraint(arg, pltpu.HBM) if space == 'h'...]
  transfers between devices with their start and end apart: 24 -> 24, of which waited for: 12 -> 12; matrix products, arithmetic and copies ran while one was open for 2% -> 2% of each run, Pallas kernels for 13% -> 14%
where the time goes in v10:
time: 117 us; the launch traced here: 116 us
  waiting for transfers between devices  43.9 us (38%)
  starting transfers between devices  33.7 us (29%)
  Pallas kernels  25.9 us (22%)
  blocking collectives  9.89 us (8%)
    ppermute x21, waiting for transfers between devices, swap(): lax.ppermute(value, axis, [(i, i ^ step) for i in range(lax.axis_size(axi...  26.6 us
    pallas_call x13, Pallas kernels, run(): made(*[pltpu.with_memory_space_constraint(arg, pltpu.HBM) if space == 'h'...  25.9 us
    ppermute x21, starting transfers between devices, swap(): lax.ppermute(value, axis, [(i, i ^ step) for i in range(lax.axis_size(axi...  18.7 us
    all_to_all x3, waiting for transfers between devices, exchange(): return lax.all_to_all(chunks, axes, 0, 0)  17.3 us
    all_to_all x3, starting transfers between devices, exchange(): return lax.all_to_all(chunks, axes, 0, 0)  14.9 us
    all_to_all x1, blocking collectives, exchange(): return lax.all_to_all(chunks, axes, 0, 0)  9.89 us
  transfers between devices with their start and end apart: 24, of which 12 were waited for; matrix products, arithmetic and copies ran while one was open for 2% of the time, Pallas kernels for 14%

profile of v10, /device:TPU:1, one launch (start us, length us, event | category | flops | bytes accessed | tf_op | source)
XLA Modules:
  0.0 116.2 jit_solution(628229144472532717)
XLA Ops:
  0.6 1.8 %prepare_weights.1 = (bf16[2,8,1,32,384]{4,3,2,1,0:T(8,128)(2,1)}, bf16[32,1152]{1,0:T(8,128)(2,1)}) custom-call(bf16[32,3072]{1,0:T(8,128)(2,1)} %w_any.1, bf16[32,1024]{1,0:T(8,128)(2,1)} %mix_any.1, bf16[32,100]{1,0:T(8,128)(2,1)} %readout_any.1), custom_call_target="tpu_custom_call" | custom-call | bytes 1048576 | tf_op jit(solution)/shard_map/prepare_weights/pallas_call | solution.py:63
  2.4 3.2 %collective-permute-start = (bf16[32,1152]{1,0:T(8,128)(2,1)}, bf16[32,1152]{1,0:T(8,128)(2,1)S(1)}, u32[]{:S(2)}, u32[]{:S(2)}) collective-permute-start(bf16[32,1152]{1,0:T(8,128)(2,1)} %get-tuple-element.31), channel_id=1, source_target_pairs={{0,16},{16,0},{1,17},{17,1},{2,18},{18,2},{3,19},{19,3},{4,20},{20... | collective-permute-start | bytes 221192 | tf_op jit(solution)/shard_map/ppermute | solution.py:440
  5.6 4.8 %all-to-all-start = ((bf16[16,32,384]{2,1,0:T(8,128)(2,1)}), bf16[16,32,384]{2,1,0:T(8,128)(2,1)S(1)}, u32[]{:S(2)}, u32[]{:S(2)}) async-start(bf16[16,32,384]{2,1,0:T(8,128)(2,1)} %bitcast.27), calls=%async_computation | async-start | bytes 786432 | tf_op jit(solution)/shard_map/all_to_all | solution.py:436
  10.4 1.9 %norm.1 = (bf16[144,1024]{1,0:T(8,128)(2,1)}, bf16[1,64,1024]{2,1,0:T(8,128)(2,1)}, bf16[1,64,1024]{2,1,0:T(8,128)(2,1)}) custom-call(s32[2,4]{1,0:T(2,128)} %near_any.1, bf16[128,1024]{1,0:T(8,128)(2,1)} %bitcast.28), custom_call_target="tpu_custom_call" | custom-call | flops 1048576 | bytes 1048576 | tf_op jit(solution)/shard_map/norm/pallas_call | solution.py:63
  12.3 0.9 select_bitcast_fusion.3
  13.3 1.5 %collective-permute-start.1 = (bf16[144,1024]{1,0:T(8,128)(2,1)}, bf16[144,1024]{1,0:T(8,128)(2,1)S(1)}, u32[]{:S(2)}, u32[]{:S(2)}) collective-permute-start(bf16[144,1024]{1,0:T(8,128)(2,1)} %get-tuple-element.35.refs_0_), channel_id=1, source_target_pairs={{0,4},{4,0},{8,12},{12,8},{1,5},{5,1},{9,13},{13,9},{2,6},{6,2},{1... | collective-permute-start | bytes 884744 | tf_op jit(solution)/shard_map/ppermute | solution.py:440
  14.8 1.2 %collective-permute-start.3 = (bf16[144,1024]{1,0:T(8,128)(2,1)}, bf16[144,1024]{1,0:T(8,128)(2,1)S(1)}, u32[]{:S(2)}, u32[]{:S(2)}) collective-permute-start(bf16[144,1024]{1,0:T(8,128)(2,1)} %get-tuple-element.35.refs_0_), channel_id=1, source_target_pairs={{0,12},{4,8},{8,4},{12,0},{1,13},{5,9},{9,5},{13,1},{2,14},{6,10},... | collective-permute-start | bytes 884744 | tf_op jit(solution)/shard_map/ppermute | solution.py:440
  15.9 5.9 %all-to-all-done.refs_0_ = bf16[16,32,384]{2,1,0:T(8,128)(2,1)S(1)} async-done(((bf16[16,32,384]{2,1,0:T(8,128)(2,1)}), bf16[16,32,384]{2,1,0:T(8,128)(2,1)S(1)}, u32[]{:S(2)}, u32[]{:S(2)}) %all-to-all-start) | async-done | bytes 393248 | tf_op jit(solution)/shard_map/all_to_all | solution.py:436
  21.9 1.7 %collective-permute-start.2 = (bf16[144,1024]{1,0:T(8,128)(2,1)}, bf16[144,1024]{1,0:T(8,128)(2,1)S(1)}, u32[]{:S(2)}, u32[]{:S(2)}) collective-permute-start(bf16[144,1024]{1,0:T(8,128)(2,1)} %get-tuple-element.35.refs_0_), channel_id=1, source_target_pairs={{0,8},{4,12},{8,0},{12,4},{1,9},{5,13},{9,1},{13,5},{2,10},{6,14},... | collective-permute-start | bytes 884744 | tf_op jit(solution)/shard_map/ppermute | solution.py:440
  23.6 1.2 %collective-permute-start.10 = (bf16[2,32,1152]{2,1,0:T(8,128)(2,1)S(1)}, bf16[2,32,1152]{2,1,0:T(8,128)(2,1)S(1)}, u32[]{:S(2)}, u32[]{:S(2)}) collective-permute-start(bf16[2,32,1152]{2,1,0:T(8,128)(2,1)S(1)} %pad_maximum_fusion.1), channel_id=1, source_target_pairs={{0,1},{1,0},{2,3},{3,2},{4,5},{5,4},{6,7},{7,6},{8,9},{9,8},{10,11... | collective-permute-start | bytes 442376 | tf_op jit(solution)/shard_map/ppermute | solution.py:440
  25.1 6.9 %collective-permute-done.9.refs_1_ = bf16[1,64,1024]{2,1,0:T(8,128)(2,1)S(1)} collective-permute-done((bf16[1,64,1024]{2,1,0:T(8,128)(2,1)}, bf16[1,64,1024]{2,1,0:T(8,128)(2,1)S(1)}, u32[]{:S(2)}, u32[]{:S(2)}) %collective-permute-start.9) | collective-permute-done | bytes 131104 | tf_op jit(solution)/shard_map/ppermute | solution.py:440
  32.0 0.7 collective-permute-start.4
  32.7 0.5 collective-permute-start.7
  33.2 1.2 %collective-permute-start.8 = (bf16[16,32,384]{2,1,0:T(8,128)(2,1)S(1)}, bf16[16,32,384]{2,1,0:T(8,128)(2,1)S(1)}, u32[]{:S(2)}, u32[]{:S(2)}) collective-permute-start(bf16[16,32,384]{2,1,0:T(8,128)(2,1)S(1)} %all-to-all-done.refs_0_), channel_id=1, source_target_pairs={{0,1},{1,0},{2,3},{3,2},{4,5},{5,4},{6,7},{7,6},{8,9},{9,8},{10,11... | collective-permute-start | bytes 1179656 | tf_op jit(solution)/shard_map/ppermute | solution.py:440
  34.4 0.3 collective-permute-start.6
  34.9 9.0 %collective-permute-done.8.refs_1_ = bf16[16,32,384]{2,1,0:T(8,128)(2,1)S(1)} collective-permute-done((bf16[16,32,384]{2,1,0:T(8,128)(2,1)S(1)}, bf16[16,32,384]{2,1,0:T(8,128)(2,1)S(1)}, u32[]{:S(2)}, u32[]{:S(2)}) %collective-permute-start.8) | collective-permute-done | bytes 393248 | tf_op jit(solution)/shard_map/ppermute | solution.py:440
  43.9 0.7 collective-permute-start.11
  44.6 0.3 collective-permute-start.12
  44.9 1.6 %collective-permute-start.13 = (bf16[2,64,1152]{2,1,0:T(8,128)(2,1)S(1)}, bf16[2,64,1152]{2,1,0:T(8,128)(2,1)S(1)}, u32[]{:S(2)}, u32[]{:S(2)}) collective-permute-start(bf16[2,64,1152]{2,1,0:T(8,128)(2,1)S(1)} %bitcast.23), channel_id=1, source_target_pairs={{0,12},{4,8},{8,4},{12,0},{1,13},{5,9},{9,5},{13,1},{2,14},{6,10},... | collective-permute-start | bytes 884744 | tf_op jit(solution)/shard_map/ppermute | solution.py:440
  46.5 1.5 %collect.1 = (bf16[1024,1024]{1,0:T(8,128)(2,1)}, f32[8,16,128]{2,1,0:T(8,128)S(1)}) custom-call(bf16[144,1024]{1,0:T(8,128)(2,1)S(1)} %copy-done.1, bf16[144,1024]{1,0:T(8,128)(2,1)S(1)} %collective-permute-done.1.refs_1_, bf16[144,1024]{1,0:T(8,128)(2,1)S(1)} %collective-permute-done.2.refs_2_, bf16[144,1024]{1,0:T(8,128)(2,1)S(1)} %collective-permute-done.3.refs_3_, ...), custom_call_target="tpu_custom_call" | custom-call | bytes 4194304 | tf_op jit(solution)/shard_map/collect/pallas_call | solution.py:63
  48.1 1.3 %project_rims.1 = (bf16[16,2,32,384]{3,2,1,0:T(8,128)(2,1)S(1)}, bf16[128,256]{1,0:T(8,128)(2,1)S(1)}) custom-call(bf16[1024,1024]{1,0:T(8,128)(2,1)} %get-tuple-element.36.normed_any.normed_ref, bf16[16,32,384]{2,1,0:T(8,128)(2,1)S(1)} %all-to-all-done.refs_0_, bf16[16,32,384]{2,1,0:T(8,128)(2,1)S(1)} %collective-permute-done.8.refs_1_), custom_call_target="tpu_custom_call" | custom-call | flops 67108864 | bytes 1048576 | tf_op jit(solution)/shard_map/project_rims/pallas_call | solution.py:63
  49.4 0.4 collective-permute-start.14
  49.8 2.8 %project.1 = (bf16[1024,128]{1,0:T(8,128)(2,1)S(1)}, bf16[1024,256]{1,0:T(8,128)(2,1)S(1)}) custom-call(bf16[1024,1024]{1,0:T(8,128)(2,1)} %get-tuple-element.36.normed_any.normed_ref, bf16[16,2,32,384]{3,2,1,0:T(8,128)(2,1)S(1)} %get-tuple-element.41.w_ref), custom_call_target="tpu_custom_call" | custom-call | flops 805306368 | bytes 4194304 | tf_op jit(solution)/shard_map/project/pallas_call | solution.py:63
  52.6 1.9 %attention_interior.1.done_ref = bf16[1024,128]{1,0:T(8,128)(2,1)S(1)} custom-call(f32[8,16,128]{2,1,0:T(8,128)S(1)} %get-tuple-element.37.steps_ref, bf16[1024,128]{1,0:T(8,128)(2,1)S(1)} %get-tuple-element.42.q_ref, bf16[1024,256]{1,0:T(8,128)(2,1)S(1)} %get-tuple-element.46.kv_ref), custom_call_target="tpu_custom_call" | custom-call | flops 268435456 | bytes 2097152 | tf_op jit(solution)/shard_map/attention_interior/pallas_call | solution.py:63
  54.5 3.3 %collective-permute-done.14.low_ref.high_ref = bf16[128,256]{1,0:T(8,128)(2,1)S(1)} collective-permute-done((bf16[128,256]{1,0:T(8,128)(2,1)S(1)}, bf16[128,256]{1,0:T(8,128)(2,1)S(1)}, u32[]{:S(2)}, u32[]{:S(2)}) %collective-permute-start.14) | collective-permute-done | bytes 65568 | tf_op jit(solution)/shard_map/ppermute | solution.py:440
  57.8 1.4 %attention_edges.1 = bf16[1024,128]{1,0:T(8,128)(2,1)} custom-call(f32[8,16,128]{2,1,0:T(8,128)S(1)} %get-tuple-element.37.steps_ref, bf16[1024,128]{1,0:T(8,128)(2,1)S(1)} %get-tuple-element.42.q_ref, bf16[1024,256]{1,0:T(8,128)(2,1)S(1)} %get-tuple-element.46.kv_ref, bf16[128,256]{1,0:T(8,128)(2,1)S(1)} %collective-permute-done.14.low_ref.high_ref, ...), custom_call_target="tpu_custom_call" | custom-call | flops 67108864 | bytes 1048576 | tf_op jit(solution)/shard_map/attention_edges/pallas_call | solution.py:63
  59.2 7.2 %all-to-all-start.1 = ((bf16[16,64,128]{2,1,0:T(8,128)(2,1)}), bf16[16,64,128]{2,1,0:T(8,128)(2,1)S(1)}, u32[]{:S(2)}, u32[]{:S(2)}) async-start(bf16[16,64,128]{2,1,0:T(8,128)(2,1)} %bitcast.7), calls=%async_computation.1 | async-start | bytes 524288 | tf_op jit(solution)/shard_map/all_to_all | solution.py:436
  66.7 0.4 collective-permute-start.16
  67.2 0.4 collective-permute-start.18
  67.6 0.6 collective-permute-done.15.refs_4_
  68.1 0.4 collective-permute-done.16.refs_5_
  68.6 0.4 collective-permute-done.17.refs_6_
  69.0 0.4 collective-permute-done.18.refs_7_
  69.4 1.5 %assemble.1.w_any = bf16[2,4,2,64,1152]{4,3,2,1,0:T(8,128)(2,1)} custom-call(bf16[2,64,1152]{2,1,0:T(8,128)(2,1)S(1)} %bitcast.25, bf16[2,64,1152]{2,1,0:T(8,128)(2,1)S(1)} %collective-permute-done.11.refs_1_, bf16[2,64,1152]{2,1,0:T(8,128)(2,1)S(1)} %collective-permute-done.12.refs_2_, bf16[2,64,1152]{2,1,0:T(8,128)(2,1)S(1)} %collective-permute-done.13.refs_3_, ...), custom_call_target="tpu_custom_call" | custom-call | bytes 4194304 | tf_op jit(solution)/shard_map/assemble/pallas_call | solution.py:63
  70.9 2.4 %all-to-all-done.1.att_ref = bf16[16,64,128]{2,1,0:T(8,128)(2,1)S(1)} async-done(((bf16[16,64,128]{2,1,0:T(8,128)(2,1)}), bf16[16,64,128]{2,1,0:T(8,128)(2,1)S(1)}, u32[]{:S(2)}, u32[]{:S(2)}) %all-to-all-start.1) | async-done | bytes 262176 | tf_op jit(solution)/shard_map/all_to_all | solution.py:436
  73.3 3.7 %mix_loss_backward.1 = (f32[100,128]{1,0:T(8,128)S(1)}, bf16[16,64,128]{2,1,0:T(8,128)(2,1)S(1)}) custom-call(bf16[16,64,128]{2,1,0:T(8,128)(2,1)S(1)} %all-to-all-done.1.att_ref, f32[1,128]{1,0:T(1,128)S(1)} %bitcast.26, f32[100,128]{1,0:T(8,128)} %truth_any.1, bf16[2,4,2,64,1152]{4,3,2,1,0:T(8,128)(2,1)} %assemble.1.w_any, ...), custom_call_target="tpu_custom_call" | custom-call | flops 603979776 | bytes 4194304 | tf_op jit(solution)/shard_map/mix_loss_backward/pallas_call | solution.py:63
  77.0 9.9 %all_to_all.20 = bf16[16,64,128]{2,1,0:T(8,128)(2,1)S(1)} all-to-all(bf16[16,64,128]{2,1,0:T(8,128)(2,1)S(1)} %get-tuple-element.54), channel_id=1, replica_groups=mesh['half'=2,'quad'=4,'core'=2,'ens'=2] {'quad','core','ens'}, dimensions={0} | all-to-all | bytes 524288 | tf_op jit(solution)/shard_map/all_to_all | solution.py:436
  86.9 1.4 %attention_edges_back.1 = (f32[2,256,256]{2,1,0:T(8,128)S(1)}, bf16[128,256]{1,0:T(8,128)(2,1)S(1)}) custom-call(f32[8,16,128]{2,1,0:T(8,128)S(1)} %get-tuple-element.37.steps_ref, bf16[1024,128]{1,0:T(8,128)(2,1)S(1)} %get-tuple-element.42.q_ref, bf16[1024,256]{1,0:T(8,128)(2,1)S(1)} %get-tuple-element.46.kv_ref, ...), custom_call_target="tpu_custom_call" | custom-call | flops 167772160 | bytes 1048576 | tf_op jit(solution)/shard_map/attention_edges_back/pallas_call | solution.py:63
  88.3 1.4 %collective-permute-start.19 = (bf16[128,256]{1,0:T(8,128)(2,1)S(1)}, bf16[128,256]{1,0:T(8,128)(2,1)S(1)}, u32[]{:S(2)}, u32[]{:S(2)}) collective-permute-start(bf16[128,256]{1,0:T(8,128)(2,1)S(1)} %get-tuple-element.55), channel_id=1, source_target_pairs={{0,16},{16,0},{1,17},{17,1},{2,18},{18,2},{3,19},{19,3},{4,20},{20... | collective-permute-start | bytes 196616 | tf_op jit(solution)/shard_map/ppermute | solution.py:440
  89.7 3.8 %attention_interior_back.1.grads_ref = f32[1024,256]{1,0:T(8,128)S(1)} custom-call(f32[8,16,128]{2,1,0:T(8,128)S(1)} %get-tuple-element.37.steps_ref, bf16[1024,128]{1,0:T(8,128)(2,1)S(1)} %get-tuple-element.42.q_ref, bf16[1024,256]{1,0:T(8,128)(2,1)S(1)} %get-tuple-element.46.kv_ref, bf16[1024,128]{1,0:T(8,128)(2,1)S(1)} %bitcast.19, ...), custom_call_target="tpu_custom_call" | custom-call | flops 536870912 | bytes 4194304 | tf_op jit(solution)/shard_map/attention_interior_back/pallas_call | solution.py:63
  93.6 1.0 collective-permute-done.19.from_low_ref.from_high_ref
  94.6 2.1 %product.1 = bf16[1024,256]{1,0:T(8,128)(2,1)} custom-call(bf16[1024,1024]{1,0:T(8,128)(2,1)S(1)} %copy-done, bf16[128,256]{1,0:T(8,128)(2,1)S(1)} %collective-permute-done.19.from_low_ref.from_high_ref, bf16[128,256]{1,0:T(8,128)(2,1)S(1)} %collective-permute-done.19.from_low_ref.from_high_ref, f32[1024,256]{1,0:T(8,128)S(1)} %attention_interior_back.1.grads_ref), custom_call_target="tpu_custom_call" | custom-call | flops 1073741824 | bytes 4194304 | tf_op jit(solution)/shard_map/product/pallas_call | solution.py:63
  96.7 2.9 %all-to-all-start.3 = ((bf16[32,32,256]{2,1,0:T(8,128)(2,1)}), bf16[32,32,256]{2,1,0:T(8,128)(2,1)S(1)}, u32[]{:S(2)}, u32[]{:S(2)}) async-start(bf16[32,32,256]{2,1,0:T(8,128)(2,1)} %bitcast.11), calls=%async_computation.3 | async-start | bytes 1048576 | tf_op jit(solution)/shard_map/all_to_all | solution.py:436
  99.6 1.5 %collective-permute-start.20 = (f32[100,128]{1,0:T(8,128)S(1)}, f32[100,128]{1,0:T(8,128)S(1)}, u32[]{:S(2)}, u32[]{:S(2)}) collective-permute-start(f32[100,128]{1,0:T(8,128)S(1)} %get-tuple-element.58), channel_id=1, source_target_pairs={{0,1},{1,0},{2,3},{3,2},{4,5},{5,4},{6,7},{7,6},{8,9},{9,8},{10,11... | collective-permute-start | bytes 153608 | tf_op jit(solution)/shard_map/ppermute | solution.py:440
  101.1 4.5 %collective-permute-done.20 = f32[100,128]{1,0:T(8,128)S(1)} collective-permute-done((f32[100,128]{1,0:T(8,128)S(1)}, f32[100,128]{1,0:T(8,128)S(1)}, u32[]{:S(2)}, u32[]{:S(2)}) %collective-permute-start.20) | collective-permute-done | bytes 51232 | tf_op jit(solution)/shard_map/ppermute | solution.py:440
  105.8 0.7 copy.10
  106.5 9.0 %all-to-all-done.3 = bf16[32,32,256]{2,1,0:T(8,128)(2,1)S(1)} async-done(((bf16[32,32,256]{2,1,0:T(8,128)(2,1)}), bf16[32,32,256]{2,1,0:T(8,128)(2,1)S(1)}, u32[]{:S(2)}, u32[]{:S(2)}) %all-to-all-start.3) | async-done | bytes 524320 | tf_op jit(solution)/shard_map/all_to_all | solution.py:436
  115.4 0.8 gather_sums.1
  (32 shorter events, 0.9 us)
Async XLA Ops:
  2.4 9.9 %collective-permute-start = (bf16[32,1152]{1,0:T(8,128)(2,1)}, bf16[32,1152]{1,0:T(8,128)(2,1)S(1)}, u32[]{:S(2)}, u32[]{:S(2)}) collective-permute-start(bf16[32,1152]{1,0:T(8,128)(2,1)} %get-tuple-element.31), channel_id=1, source_target_pairs={{0,16},{16,0},{1,17},{17,1},{2,18},{18,2},{3,19},{19,3},{4,20},{20... | collective-permute-start | bytes 221192 | tf_op jit(solution)/shard_map/ppermute | solution.py:440
  5.6 16.2 %all-to-all-start = ((bf16[16,32,384]{2,1,0:T(8,128)(2,1)}), bf16[16,32,384]{2,1,0:T(8,128)(2,1)S(1)}, u32[]{:S(2)}, u32[]{:S(2)}) async-start(bf16[16,32,384]{2,1,0:T(8,128)(2,1)} %bitcast.27), calls=%async_computation | async-start | bytes 786432 | tf_op jit(solution)/shard_map/all_to_all | solution.py:436
  12.3 34.2 %copy-start.1 = (bf16[144,1024]{1,0:T(8,128)(2,1)S(1)}, bf16[144,1024]{1,0:T(8,128)(2,1)}, u32[]{:S(2)}) copy-start(bf16[144,1024]{1,0:T(8,128)(2,1)} %get-tuple-element.35.refs_0_) | copy-start | bytes 884740
  13.3 19.4 %collective-permute-start.1 = (bf16[144,1024]{1,0:T(8,128)(2,1)}, bf16[144,1024]{1,0:T(8,128)(2,1)S(1)}, u32[]{:S(2)}, u32[]{:S(2)}) collective-permute-start(bf16[144,1024]{1,0:T(8,128)(2,1)} %get-tuple-element.35.refs_0_), channel_id=1, source_target_pairs={{0,4},{4,0},{8,12},{12,8},{1,5},{5,1},{9,13},{13,9},{2,6},{6,2},{1... | collective-permute-start | bytes 884744 | tf_op jit(solution)/shard_map/ppermute | solution.py:440
  14.8 17.9 %collective-permute-start.3 = (bf16[144,1024]{1,0:T(8,128)(2,1)}, bf16[144,1024]{1,0:T(8,128)(2,1)S(1)}, u32[]{:S(2)}, u32[]{:S(2)}) collective-permute-start(bf16[144,1024]{1,0:T(8,128)(2,1)} %get-tuple-element.35.refs_0_), channel_id=1, source_target_pairs={{0,12},{4,8},{8,4},{12,0},{1,13},{5,9},{9,5},{13,1},{2,14},{6,10},... | collective-permute-start | bytes 884744 | tf_op jit(solution)/shard_map/ppermute | solution.py:440
  21.9 12.5 %collective-permute-start.2 = (bf16[144,1024]{1,0:T(8,128)(2,1)}, bf16[144,1024]{1,0:T(8,128)(2,1)S(1)}, u32[]{:S(2)}, u32[]{:S(2)}) collective-permute-start(bf16[144,1024]{1,0:T(8,128)(2,1)} %get-tuple-element.35.refs_0_), channel_id=1, source_target_pairs={{0,8},{4,12},{8,0},{12,4},{1,9},{5,13},{9,1},{13,5},{2,10},{6,14},... | collective-permute-start | bytes 884744 | tf_op jit(solution)/shard_map/ppermute | solution.py:440
  23.6 9.6 %collective-permute-start.10 = (bf16[2,32,1152]{2,1,0:T(8,128)(2,1)S(1)}, bf16[2,32,1152]{2,1,0:T(8,128)(2,1)S(1)}, u32[]{:S(2)}, u32[]{:S(2)}) collective-permute-start(bf16[2,32,1152]{2,1,0:T(8,128)(2,1)S(1)} %pad_maximum_fusion.1), channel_id=1, source_target_pairs={{0,1},{1,0},{2,3},{3,2},{4,5},{5,4},{6,7},{7,6},{8,9},{9,8},{10,11... | collective-permute-start | bytes 442376 | tf_op jit(solution)/shard_map/ppermute | solution.py:440
  24.8 7.2 %collective-permute-start.9 = (bf16[1,64,1024]{2,1,0:T(8,128)(2,1)}, bf16[1,64,1024]{2,1,0:T(8,128)(2,1)S(1)}, u32[]{:S(2)}, u32[]{:S(2)}) collective-permute-start(bf16[1,64,1024]{2,1,0:T(8,128)(2,1)} %get-tuple-element.39), channel_id=1, source_target_pairs={{0,1},{1,0},{2,3},{3,2},{4,5},{5,4},{6,7},{7,6},{8,9},{9,8},{10,11... | collective-permute-start | bytes 393224 | tf_op jit(solution)/shard_map/ppermute | solution.py:440
  32.0 12.6 %collective-permute-start.4 = (bf16[144,1024]{1,0:T(8,128)(2,1)}, bf16[144,1024]{1,0:T(8,128)(2,1)S(1)}, u32[]{:S(2)}, u32[]{:S(2)}) collective-permute-start(bf16[144,1024]{1,0:T(8,128)(2,1)} %get-tuple-element.35.refs_0_), channel_id=1, source_target_pairs={{0,2},{2,0},{1,3},{3,1},{4,6},{6,4},{5,7},{7,5},{8,10},{10,8},{9,1... | collective-permute-start | bytes 884744 | tf_op jit(solution)/shard_map/ppermute | solution.py:440
  32.7 12.2 %collective-permute-start.5 = (bf16[144,1024]{1,0:T(8,128)(2,1)S(1)}, bf16[144,1024]{1,0:T(8,128)(2,1)S(1)}, u32[]{:S(2)}, u32[]{:S(2)}) collective-permute-start(bf16[144,1024]{1,0:T(8,128)(2,1)S(1)} %collective-permute-done.1.refs_1_), channel_id=1, source_target_pairs={{0,2},{2,0},{1,3},{3,1},{4,6},{6,4},{5,7},{7,5},{8,10},{10,8},{9,1... | collective-permute-start | bytes 884744 | tf_op jit(solution)/shard_map/ppermute | solution.py:440
  32.7 13.8 %collective-permute-start.7 = (bf16[144,1024]{1,0:T(8,128)(2,1)S(1)}, bf16[144,1024]{1,0:T(8,128)(2,1)S(1)}, u32[]{:S(2)}, u32[]{:S(2)}) collective-permute-start(bf16[144,1024]{1,0:T(8,128)(2,1)S(1)} %collective-permute-done.3.refs_3_), channel_id=1, source_target_pairs={{0,2},{2,0},{1,3},{3,1},{4,6},{6,4},{5,7},{7,5},{8,10},{10,8},{9,1... | collective-permute-start | bytes 884744 | tf_op jit(solution)/shard_map/ppermute | solution.py:440
  33.2 10.7 %collective-permute-start.8 = (bf16[16,32,384]{2,1,0:T(8,128)(2,1)S(1)}, bf16[16,32,384]{2,1,0:T(8,128)(2,1)S(1)}, u32[]{:S(2)}, u32[]{:S(2)}) collective-permute-start(bf16[16,32,384]{2,1,0:T(8,128)(2,1)S(1)} %all-to-all-done.refs_0_), channel_id=1, source_target_pairs={{0,1},{1,0},{2,3},{3,2},{4,5},{5,4},{6,7},{7,6},{8,9},{9,8},{10,11... | collective-permute-start | bytes 1179656 | tf_op jit(solution)/shard_map/ppermute | solution.py:440
  34.4 12.1 %collective-permute-start.6 = (bf16[144,1024]{1,0:T(8,128)(2,1)S(1)}, bf16[144,1024]{1,0:T(8,128)(2,1)S(1)}, u32[]{:S(2)}, u32[]{:S(2)}) collective-permute-start(bf16[144,1024]{1,0:T(8,128)(2,1)S(1)} %collective-permute-done.2.refs_2_), channel_id=1, source_target_pairs={{0,2},{2,0},{1,3},{3,1},{4,6},{6,4},{5,7},{7,5},{8,10},{10,8},{9,1... | collective-permute-start | bytes 884744 | tf_op jit(solution)/shard_map/ppermute | solution.py:440
  43.9 22.6 %collective-permute-start.11 = (bf16[2,64,1152]{2,1,0:T(8,128)(2,1)S(1)}, bf16[2,64,1152]{2,1,0:T(8,128)(2,1)S(1)}, u32[]{:S(2)}, u32[]{:S(2)}) collective-permute-start(bf16[2,64,1152]{2,1,0:T(8,128)(2,1)S(1)} %bitcast.21), channel_id=1, source_target_pairs={{0,4},{4,0},{8,12},{12,8},{1,5},{5,1},{9,13},{13,9},{2,6},{6,2},{1... | collective-permute-start | bytes 884744 | tf_op jit(solution)/shard_map/ppermute | solution.py:440
  44.6 21.9 %collective-permute-start.12 = (bf16[2,64,1152]{2,1,0:T(8,128)(2,1)S(1)}, bf16[2,64,1152]{2,1,0:T(8,128)(2,1)S(1)}, u32[]{:S(2)}, u32[]{:S(2)}) collective-permute-start(bf16[2,64,1152]{2,1,0:T(8,128)(2,1)S(1)} %bitcast.22), channel_id=1, source_target_pairs={{0,8},{4,12},{8,0},{12,4},{1,9},{5,13},{9,1},{13,5},{2,10},{6,14},... | collective-permute-start | bytes 884744 | tf_op jit(solution)/shard_map/ppermute | solution.py:440
  44.9 21.6 %collective-permute-start.13 = (bf16[2,64,1152]{2,1,0:T(8,128)(2,1)S(1)}, bf16[2,64,1152]{2,1,0:T(8,128)(2,1)S(1)}, u32[]{:S(2)}, u32[]{:S(2)}) collective-permute-start(bf16[2,64,1152]{2,1,0:T(8,128)(2,1)S(1)} %bitcast.23), channel_id=1, source_target_pairs={{0,12},{4,8},{8,4},{12,0},{1,13},{5,9},{9,5},{13,1},{2,14},{6,10},... | collective-permute-start | bytes 884744 | tf_op jit(solution)/shard_map/ppermute | solution.py:440
  49.4 8.4 %collective-permute-start.14 = (bf16[128,256]{1,0:T(8,128)(2,1)S(1)}, bf16[128,256]{1,0:T(8,128)(2,1)S(1)}, u32[]{:S(2)}, u32[]{:S(2)}) collective-permute-start(bf16[128,256]{1,0:T(8,128)(2,1)S(1)} %get-tuple-element.47), channel_id=1, source_target_pairs={{0,16},{16,0},{1,17},{17,1},{2,18},{18,2},{3,19},{19,3},{4,20},{20... | collective-permute-start | bytes 196616 | tf_op jit(solution)/shard_map/ppermute | solution.py:440
  59.2 14.1 %all-to-all-start.1 = ((bf16[16,64,128]{2,1,0:T(8,128)(2,1)}), bf16[16,64,128]{2,1,0:T(8,128)(2,1)S(1)}, u32[]{:S(2)}, u32[]{:S(2)}) async-start(bf16[16,64,128]{2,1,0:T(8,128)(2,1)} %bitcast.7), calls=%async_computation.1 | async-start | bytes 524288 | tf_op jit(solution)/shard_map/all_to_all | solution.py:436
  66.4 6.9 %copy-start.2 = (bf16[1,64,1024]{2,1,0:T(8,128)(2,1)S(1)}, bf16[1,64,1024]{2,1,0:T(8,128)(2,1)}, u32[]{:S(2)}) copy-start(bf16[1,64,1024]{2,1,0:T(8,128)(2,1)} %get-tuple-element.52.refs_0_) | copy-start | bytes 393220
  66.4 6.9 %copy-start.3 = (f32[128]{0:T(128)S(1)}, f32[128]{0:T(128)}, u32[]{:S(2)}) copy-start(f32[128]{0:T(128)} %param.12) | copy-start | bytes 1540
  66.5 1.6 %collective-permute-start.15 = (bf16[2,64,1152]{2,1,0:T(8,128)(2,1)S(1)}, bf16[2,64,1152]{2,1,0:T(8,128)(2,1)S(1)}, u32[]{:S(2)}, u32[]{:S(2)}) collective-permute-start(bf16[2,64,1152]{2,1,0:T(8,128)(2,1)S(1)} %bitcast.24), channel_id=1, source_target_pairs={{0,2},{2,0},{1,3},{3,1},{4,6},{6,4},{5,7},{7,5},{8,10},{10,8},{9,1... | collective-permute-start | bytes 884744 | tf_op jit(solution)/shard_map/ppermute | solution.py:440
  66.7 1.9 %collective-permute-start.16 = (bf16[2,64,1152]{2,1,0:T(8,128)(2,1)S(1)}, bf16[2,64,1152]{2,1,0:T(8,128)(2,1)S(1)}, u32[]{:S(2)}, u32[]{:S(2)}) collective-permute-start(bf16[2,64,1152]{2,1,0:T(8,128)(2,1)S(1)} %collective-permute-done.11.refs_1_), channel_id=1, source_target_pairs={{0,2},{2,0},{1,3},{3,1},{4,6},{6,4},{5,7},{7,5},{8,10},{10,8},{9,1... | collective-permute-start | bytes 884744 | tf_op jit(solution)/shard_map/ppermute | solution.py:440
  67.1 1.9 %collective-permute-start.17 = (bf16[2,64,1152]{2,1,0:T(8,128)(2,1)S(1)}, bf16[2,64,1152]{2,1,0:T(8,128)(2,1)S(1)}, u32[]{:S(2)}, u32[]{:S(2)}) collective-permute-start(bf16[2,64,1152]{2,1,0:T(8,128)(2,1)S(1)} %collective-permute-done.12.refs_2_), channel_id=1, source_target_pairs={{0,2},{2,0},{1,3},{3,1},{4,6},{6,4},{5,7},{7,5},{8,10},{10,8},{9,1... | collective-permute-start | bytes 884744 | tf_op jit(solution)/shard_map/ppermute | solution.py:440
  67.2 2.2 %collective-permute-start.18 = (bf16[2,64,1152]{2,1,0:T(8,128)(2,1)S(1)}, bf16[2,64,1152]{2,1,0:T(8,128)(2,1)S(1)}, u32[]{:S(2)}, u32[]{:S(2)}) collective-permute-start(bf16[2,64,1152]{2,1,0:T(8,128)(2,1)S(1)} %collective-permute-done.13.refs_3_), channel_id=1, source_target_pairs={{0,2},{2,0},{1,3},{3,1},{4,6},{6,4},{5,7},{7,5},{8,10},{10,8},{9,1... | collective-permute-start | bytes 884744 | tf_op jit(solution)/shard_map/ppermute | solution.py:440
  77.0 17.6 %copy-start = (bf16[1024,1024]{1,0:T(8,128)(2,1)S(1)}, bf16[1024,1024]{1,0:T(8,128)(2,1)}, u32[]{:S(2)}) copy-start(bf16[1024,1024]{1,0:T(8,128)(2,1)} %get-tuple-element.36.normed_any.normed_ref) | copy-start | bytes 6291460
  88.3 6.3 %collective-permute-start.19 = (bf16[128,256]{1,0:T(8,128)(2,1)S(1)}, bf16[128,256]{1,0:T(8,128)(2,1)S(1)}, u32[]{:S(2)}, u32[]{:S(2)}) collective-permute-start(bf16[128,256]{1,0:T(8,128)(2,1)S(1)} %get-tuple-element.55), channel_id=1, source_target_pairs={{0,16},{16,0},{1,17},{17,1},{2,18},{18,2},{3,19},{19,3},{4,20},{20... | collective-permute-start | bytes 196616 | tf_op jit(solution)/shard_map/ppermute | solution.py:440
  96.7 18.8 %all-to-all-start.3 = ((bf16[32,32,256]{2,1,0:T(8,128)(2,1)}), bf16[32,32,256]{2,1,0:T(8,128)(2,1)S(1)}, u32[]{:S(2)}, u32[]{:S(2)}) async-start(bf16[32,32,256]{2,1,0:T(8,128)(2,1)} %bitcast.11), calls=%async_computation.3 | async-start | bytes 1048576 | tf_op jit(solution)/shard_map/all_to_all | solution.py:436
  99.6 6.0 %collective-permute-start.20 = (f32[100,128]{1,0:T(8,128)S(1)}, f32[100,128]{1,0:T(8,128)S(1)}, u32[]{:S(2)}, u32[]{:S(2)}) collective-permute-start(f32[100,128]{1,0:T(8,128)S(1)} %get-tuple-element.58), channel_id=1, source_target_pairs={{0,1},{1,0},{2,3},{3,2},{4,5},{5,4},{6,7},{7,6},{8,9},{9,8},{10,11... | collective-permute-start | bytes 153608 | tf_op jit(solution)/shard_map/ppermute | solution.py:440

commit v11 on v10

--- a/solution.py
+++ b/solution.py
@@ -500,12 +500,14 @@
     near = [normed, swap(normed, "quad", 1), None, swap(normed, "quad", 3)]
     if paired:
         columns = exchange(columns.reshape(-1, shard, 3 * COLS), nodes)
-        columns, late = lax.optimization_barrier((columns, normed))
+        packed = in_order(packed, "ens", 1)
+        columns, late, packed = lax.optimization_barrier((columns, normed, packed))
         columns = [columns, swap(columns, "ens", 1)]
     else:
         columns = [exchange(columns.reshape(-1, shard, 3 * COLS), everyone)]
         columns = [columns[0].reshape(LATENT_DIM, 3 * COLS)]
         late = normed
+        packed = in_order(packed, "ens", 1)
     near[2] = swap(late, "quad", 2)
     far = [swap(piece, "core", 1) for piece in near]
     normed, steps = call(
@@ -518,12 +520,7 @@
         results="hv",
     )(*near, *far)
 
-    packed = in_order(packed, "ens", 1).reshape(halves, members_num * shard, width)
-    if paired:
-        sources = [sources[0], swap(sources[1], "ens", 1)]
-        columns[1], sources[1] = lax.optimization_barrier((columns[1], sources[1]))
-    else:
-        sources = [exchange(sources[0], "ens")]
+    packed = packed.reshape(halves, members_num * shard, width)
     packed, near[2] = lax.optimization_barrier((packed, near[2]))
     pieces = [packed] + [swap(packed, "quad", step) for step in range(1, QUAD)]
 
@@ -574,7 +571,11 @@
         moved=2**20,
         exps=rows * 128,
     )(steps, queries, own, low, high, outcome)
-    *pieces, own = lax.optimization_barrier((*pieces, own))
+    *pieces, sources[-1], own = lax.optimization_barrier((*pieces, sources[-1], own))
+    if paired:
+        sources[1] = swap(sources[1], "ens", 1)
+    else:
+        sources = [exchange(sources[0], "ens")]
     pieces = pieces + [swap(piece, "core", 1) for piece in pieces]
     attended = exchange(outcome.reshape(GROUP * members_num, part, COLS), ("quad", "core", "ens"))
     block = (halves, QUAD, CORES, members_num * shard, width)

time: 117 us -> 118 us (level)
  waiting for transfers between devices: 43.9 us -> 37.9 us
  starting transfers between devices: 33.7 us -> 39.6 us
  blocking collectives: 9.89 us -> 11.2 us
    ppermute x21, waiting for transfers between devices: 26.6 us -> 20 us  [swap(): lax.ppermute(value, axis, [(i, i ^ step) for i in range(lax.axis_size(axi...]
    all_to_all x3, starting transfers between devices: 14.9 us -> 18.3 us  [exchange(): return lax.all_to_all(chunks, axes, 0, 0)]
    ppermute x21, starting transfers between devices: 18.7 us -> 21.3 us  [swap(): lax.ppermute(value, axis, [(i, i ^ step) for i in range(lax.axis_size(axi...]
    all_to_all x1, blocking collectives: 9.89 us -> 11.2 us  [exchange(): return lax.all_to_all(chunks, axes, 0, 0)]
  transfers between devices with their start and end apart: 24 -> 24, of which waited for: 12 -> 10; matrix products, arithmetic and copies ran while one was open for 2% -> 1% of each run, Pallas kernels for 14% -> 14%
where the time goes in v11:
time: 118 us; the launch traced here: 117 us
  starting transfers between devices  39.6 us (34%)
  waiting for transfers between devices  37.9 us (32%)
  Pallas kernels  25.9 us (22%)
  blocking collectives  11.2 us (9%)
    pallas_call x13, Pallas kernels, run(): made(*[pltpu.with_memory_space_constraint(arg, pltpu.HBM) if space == 'h'...  25.9 us
    ppermute x21, starting transfers between devices, swap(): lax.ppermute(value, axis, [(i, i ^ step) for i in range(lax.axis_size(axi...  21.3 us
    ppermute x21, waiting for transfers between devices, swap(): lax.ppermute(value, axis, [(i, i ^ step) for i in range(lax.axis_size(axi...  20 us
    all_to_all x3, starting transfers between devices, exchange(): return lax.all_to_all(chunks, axes, 0, 0)  18.3 us
    all_to_all x3, waiting for transfers between devices, exchange(): return lax.all_to_all(chunks, axes, 0, 0)  17.9 us
    all_to_all x1, blocking collectives, exchange(): return lax.all_to_all(chunks, axes, 0, 0)  11.2 us
  transfers between devices with their start and end apart: 24, of which 10 were waited for; matrix products, arithmetic and copies ran while one was open for 1% of the time, Pallas kernels for 14%

profile of v11, /device:TPU:1, one launch (start us, length us, event | category | flops | bytes accessed | tf_op | source)
XLA Modules:
  0.0 117.4 jit_solution(1615629995765348343)
XLA Ops:
  0.6 1.8 %prepare_weights.1 = (bf16[2,8,1,32,384]{4,3,2,1,0:T(8,128)(2,1)}, bf16[32,1152]{1,0:T(8,128)(2,1)}) custom-call(bf16[32,3072]{1,0:T(8,128)(2,1)} %w_any.1, bf16[32,1024]{1,0:T(8,128)(2,1)} %mix_any.1, bf16[32,100]{1,0:T(8,128)(2,1)} %readout_any.1), custom_call_target="tpu_custom_call" | custom-call | bytes 1048576 | tf_op jit(solution)/shard_map/prepare_weights/pallas_call | solution.py:63
  2.4 3.2 %collective-permute-start = (bf16[32,1152]{1,0:T(8,128)(2,1)}, bf16[32,1152]{1,0:T(8,128)(2,1)S(1)}, u32[]{:S(2)}, u32[]{:S(2)}) collective-permute-start(bf16[32,1152]{1,0:T(8,128)(2,1)} %get-tuple-element.31), channel_id=1, source_target_pairs={{0,16},{16,0},{1,17},{17,1},{2,18},{18,2},{3,19},{19,3},{4,20},{20... | collective-permute-start | bytes 221192 | tf_op jit(solution)/shard_map/ppermute | solution.py:440
  5.6 1.9 %norm.1 = (bf16[144,1024]{1,0:T(8,128)(2,1)}, bf16[1,64,1024]{2,1,0:T(8,128)(2,1)}, bf16[1,64,1024]{2,1,0:T(8,128)(2,1)}) custom-call(s32[2,4]{1,0:T(2,128)} %near_any.1, bf16[128,1024]{1,0:T(8,128)(2,1)} %bitcast.28), custom_call_target="tpu_custom_call" | custom-call | flops 1048576 | bytes 1048576 | tf_op jit(solution)/shard_map/norm/pallas_call | solution.py:63
  7.6 0.9 select_bitcast_fusion.3
  8.5 1.3 %collective-permute-start.2 = (bf16[2,32,1152]{2,1,0:T(8,128)(2,1)S(1)}, bf16[2,32,1152]{2,1,0:T(8,128)(2,1)S(1)}, u32[]{:S(2)}, u32[]{:S(2)}) collective-permute-start(bf16[2,32,1152]{2,1,0:T(8,128)(2,1)S(1)} %pad_maximum_fusion.1), channel_id=1, source_target_pairs={{0,1},{1,0},{2,3},{3,2},{4,5},{5,4},{6,7},{7,6},{8,9},{9,8},{10,11... | collective-permute-start | bytes 442376 | tf_op jit(solution)/shard_map/ppermute | solution.py:440
  9.8 9.1 %all-to-all-start = ((bf16[16,32,384]{2,1,0:T(8,128)(2,1)}), bf16[16,32,384]{2,1,0:T(8,128)(2,1)S(1)}, u32[]{:S(2)}, u32[]{:S(2)}) async-start(bf16[16,32,384]{2,1,0:T(8,128)(2,1)} %bitcast.27), calls=%async_computation | async-start | bytes 786432 | tf_op jit(solution)/shard_map/all_to_all | solution.py:436
  18.9 1.4 %collective-permute-start.1 = (bf16[144,1024]{1,0:T(8,128)(2,1)}, bf16[144,1024]{1,0:T(8,128)(2,1)S(1)}, u32[]{:S(2)}, u32[]{:S(2)}) collective-permute-start(bf16[144,1024]{1,0:T(8,128)(2,1)} %get-tuple-element.36.refs_0_), channel_id=1, source_target_pairs={{0,4},{4,0},{8,12},{12,8},{1,5},{5,1},{9,13},{13,9},{2,6},{6,2},{1... | collective-permute-start | bytes 884744 | tf_op jit(solution)/shard_map/ppermute | solution.py:440
  20.3 1.2 %collective-permute-start.4 = (bf16[144,1024]{1,0:T(8,128)(2,1)}, bf16[144,1024]{1,0:T(8,128)(2,1)S(1)}, u32[]{:S(2)}, u32[]{:S(2)}) collective-permute-start(bf16[144,1024]{1,0:T(8,128)(2,1)} %get-tuple-element.36.refs_0_), channel_id=1, source_target_pairs={{0,12},{4,8},{8,4},{12,0},{1,13},{5,9},{9,5},{13,1},{2,14},{6,10},... | collective-permute-start | bytes 884744 | tf_op jit(solution)/shard_map/ppermute | solution.py:440
  21.6 8.8 %all-to-all-done.refs_0_ = bf16[16,32,384]{2,1,0:T(8,128)(2,1)S(1)} async-done(((bf16[16,32,384]{2,1,0:T(8,128)(2,1)}), bf16[16,32,384]{2,1,0:T(8,128)(2,1)S(1)}, u32[]{:S(2)}, u32[]{:S(2)}) %all-to-all-start) | async-done | bytes 393248 | tf_op jit(solution)/shard_map/all_to_all | solution.py:436
  30.4 1.7 %collective-permute-start.3 = (bf16[144,1024]{1,0:T(8,128)(2,1)S(1)}, bf16[144,1024]{1,0:T(8,128)(2,1)S(1)}, u32[]{:S(2)}, u32[]{:S(2)}) collective-permute-start(bf16[144,1024]{1,0:T(8,128)(2,1)S(1)} %copy-done.1), channel_id=1, source_target_pairs={{0,8},{4,12},{8,0},{12,4},{1,9},{5,13},{9,1},{13,5},{2,10},{6,14},... | collective-permute-start | bytes 884744 | tf_op jit(solution)/shard_map/ppermute | solution.py:440
  32.1 0.3 collective-permute-start.9
  32.3 0.2 collective-permute-start.5
  32.5 5.6 %collective-permute-done.1.refs_1_ = bf16[144,1024]{1,0:T(8,128)(2,1)S(1)} collective-permute-done((bf16[144,1024]{1,0:T(8,128)(2,1)}, bf16[144,1024]{1,0:T(8,128)(2,1)S(1)}, u32[]{:S(2)}, u32[]{:S(2)}) %collective-permute-start.1) | collective-permute-done | bytes 294944 | tf_op jit(solution)/shard_map/ppermute | solution.py:440
  38.1 0.9 collective-permute-start.6
  39.0 1.2 collective-permute-done.3.refs_2_
  40.1 0.9 collective-permute-start.7
  41.1 1.2 %collective-permute-start.10 = (bf16[2,64,1152]{2,1,0:T(8,128)(2,1)S(1)}, bf16[2,64,1152]{2,1,0:T(8,128)(2,1)S(1)}, u32[]{:S(2)}, u32[]{:S(2)}) collective-permute-start(bf16[2,64,1152]{2,1,0:T(8,128)(2,1)S(1)} %bitcast.21), channel_id=1, source_target_pairs={{0,4},{4,0},{8,12},{12,8},{1,5},{5,1},{9,13},{13,9},{2,6},{6,2},{1... | collective-permute-start | bytes 884744 | tf_op jit(solution)/shard_map/ppermute | solution.py:440
  42.4 0.9 collective-permute-start.11
  43.3 0.5 collective-permute-start.12
  43.9 1.5 %collect.1 = (bf16[1024,1024]{1,0:T(8,128)(2,1)}, f32[8,16,128]{2,1,0:T(8,128)S(1)}) custom-call(bf16[144,1024]{1,0:T(8,128)(2,1)S(1)} %copy-done.1, bf16[144,1024]{1,0:T(8,128)(2,1)S(1)} %collective-permute-done.1.refs_1_, bf16[144,1024]{1,0:T(8,128)(2,1)S(1)} %collective-permute-done.3.refs_2_, bf16[144,1024]{1,0:T(8,128)(2,1)S(1)} %collective-permute-done.4.refs_3_, ...), custom_call_target="tpu_custom_call" | custom-call | bytes 4194304 | tf_op jit(solution)/shard_map/collect/pallas_call | solution.py:63
  45.4 1.3 %project_rims.1 = (bf16[16,2,32,384]{3,2,1,0:T(8,128)(2,1)S(1)}, bf16[128,256]{1,0:T(8,128)(2,1)S(1)}) custom-call(bf16[1024,1024]{1,0:T(8,128)(2,1)} %get-tuple-element.37.normed_any.normed_ref, bf16[16,32,384]{2,1,0:T(8,128)(2,1)S(1)} %all-to-all-done.refs_0_, bf16[16,32,384]{2,1,0:T(8,128)(2,1)S(1)} %collective-permute-done.9.refs_1_), custom_call_target="tpu_custom_call" | custom-call | flops 67108864 | bytes 1048576 | tf_op jit(solution)/shard_map/project_rims/pallas_call | solution.py:63
  46.7 2.4 %collective-permute-start.13 = (bf16[128,256]{1,0:T(8,128)(2,1)S(1)}, bf16[128,256]{1,0:T(8,128)(2,1)S(1)}, u32[]{:S(2)}, u32[]{:S(2)}) collective-permute-start(bf16[128,256]{1,0:T(8,128)(2,1)S(1)} %get-tuple-element.47), channel_id=1, source_target_pairs={{0,16},{16,0},{1,17},{17,1},{2,18},{18,2},{3,19},{19,3},{4,20},{20... | collective-permute-start | bytes 196616 | tf_op jit(solution)/shard_map/ppermute | solution.py:440
  49.1 2.9 %project.1 = (bf16[1024,128]{1,0:T(8,128)(2,1)S(1)}, bf16[1024,256]{1,0:T(8,128)(2,1)S(1)}) custom-call(bf16[1024,1024]{1,0:T(8,128)(2,1)} %get-tuple-element.37.normed_any.normed_ref, bf16[16,2,32,384]{3,2,1,0:T(8,128)(2,1)S(1)} %get-tuple-element.40.w_ref), custom_call_target="tpu_custom_call" | custom-call | flops 805306368 | bytes 4194304 | tf_op jit(solution)/shard_map/project/pallas_call | solution.py:63
  52.0 1.9 %attention_interior.1.done_ref = bf16[1024,128]{1,0:T(8,128)(2,1)S(1)} custom-call(f32[8,16,128]{2,1,0:T(8,128)S(1)} %get-tuple-element.38.steps_ref, bf16[1024,128]{1,0:T(8,128)(2,1)S(1)} %get-tuple-element.41.q_ref, bf16[1024,256]{1,0:T(8,128)(2,1)S(1)} %get-tuple-element.46.kv_ref), custom_call_target="tpu_custom_call" | custom-call | flops 268435456 | bytes 2097152 | tf_op jit(solution)/shard_map/attention_interior/pallas_call | solution.py:63
  53.9 3.3 %collective-permute-done.13.low_ref.high_ref = bf16[128,256]{1,0:T(8,128)(2,1)S(1)} collective-permute-done((bf16[128,256]{1,0:T(8,128)(2,1)S(1)}, bf16[128,256]{1,0:T(8,128)(2,1)S(1)}, u32[]{:S(2)}, u32[]{:S(2)}) %collective-permute-start.13) | collective-permute-done | bytes 65568 | tf_op jit(solution)/shard_map/ppermute | solution.py:440
  57.2 1.4 %attention_edges.1 = bf16[1024,128]{1,0:T(8,128)(2,1)} custom-call(f32[8,16,128]{2,1,0:T(8,128)S(1)} %get-tuple-element.38.steps_ref, bf16[1024,128]{1,0:T(8,128)(2,1)S(1)} %get-tuple-element.41.q_ref, bf16[1024,256]{1,0:T(8,128)(2,1)S(1)} %get-tuple-element.46.kv_ref, bf16[128,256]{1,0:T(8,128)(2,1)S(1)} %collective-permute-done.13.low_ref.high_ref, ...), custom_call_target="tpu_custom_call" | custom-call | flops 67108864 | bytes 1048576 | tf_op jit(solution)/shard_map/attention_edges/pallas_call | solution.py:63
  58.6 6.5 %all-to-all-start.1 = ((bf16[16,64,128]{2,1,0:T(8,128)(2,1)}), bf16[16,64,128]{2,1,0:T(8,128)(2,1)S(1)}, u32[]{:S(2)}, u32[]{:S(2)}) async-start(bf16[16,64,128]{2,1,0:T(8,128)(2,1)} %bitcast.7), calls=%async_computation.1 | async-start | bytes 524288 | tf_op jit(solution)/shard_map/all_to_all | solution.py:436
  65.1 0.2 collective-permute-start.14
  65.3 0.4 collective-permute-start.15
  65.7 0.1 collective-permute-start.16
  65.8 0.4 collective-permute-start.17
  66.2 1.4 %collective-permute-start.18 = (bf16[1,64,1024]{2,1,0:T(8,128)(2,1)S(1)}, bf16[1,64,1024]{2,1,0:T(8,128)(2,1)S(1)}, u32[]{:S(2)}, u32[]{:S(2)}) collective-permute-start(bf16[1,64,1024]{2,1,0:T(8,128)(2,1)S(1)} %copy-done.4), channel_id=1, source_target_pairs={{0,1},{1,0},{2,3},{3,2},{4,5},{5,4},{6,7},{7,6},{8,9},{9,8},{10,11... | collective-permute-start | bytes 393224 | tf_op jit(solution)/shard_map/ppermute | solution.py:440
  67.6 0.4 collective-permute-done.17.refs_7_
  68.1 1.5 %assemble.1.w_any = bf16[2,4,2,64,1152]{4,3,2,1,0:T(8,128)(2,1)} custom-call(bf16[2,64,1152]{2,1,0:T(8,128)(2,1)S(1)} %bitcast.25, bf16[2,64,1152]{2,1,0:T(8,128)(2,1)S(1)} %collective-permute-done.10.refs_1_, bf16[2,64,1152]{2,1,0:T(8,128)(2,1)S(1)} %collective-permute-done.11.refs_2_, bf16[2,64,1152]{2,1,0:T(8,128)(2,1)S(1)} %collective-permute-done.12.refs_3_, ...), custom_call_target="tpu_custom_call" | custom-call | bytes 4194304 | tf_op jit(solution)/shard_map/assemble/pallas_call | solution.py:63
  69.5 3.6 %collective-permute-done.18.refs_1_ = bf16[1,64,1024]{2,1,0:T(8,128)(2,1)S(1)} collective-permute-done((bf16[1,64,1024]{2,1,0:T(8,128)(2,1)S(1)}, bf16[1,64,1024]{2,1,0:T(8,128)(2,1)S(1)}, u32[]{:S(2)}, u32[]{:S(2)}) %collective-permute-start.18) | collective-permute-done | bytes 131104 | tf_op jit(solution)/shard_map/ppermute | solution.py:440
  73.2 3.7 %mix_loss_backward.1 = (f32[100,128]{1,0:T(8,128)S(1)}, bf16[16,64,128]{2,1,0:T(8,128)(2,1)S(1)}) custom-call(bf16[16,64,128]{2,1,0:T(8,128)(2,1)S(1)} %all-to-all-done.1.att_ref, f32[1,128]{1,0:T(1,128)S(1)} %bitcast.26, f32[100,128]{1,0:T(8,128)} %truth_any.1, bf16[2,4,2,64,1152]{4,3,2,1,0:T(8,128)(2,1)} %assemble.1.w_any, ...), custom_call_target="tpu_custom_call" | custom-call | flops 603979776 | bytes 4194304 | tf_op jit(solution)/shard_map/mix_loss_backward/pallas_call | solution.py:63
  76.9 11.2 %all_to_all.20 = bf16[16,64,128]{2,1,0:T(8,128)(2,1)S(1)} all-to-all(bf16[16,64,128]{2,1,0:T(8,128)(2,1)S(1)} %get-tuple-element.54), channel_id=1, replica_groups=mesh['half'=2,'quad'=4,'core'=2,'ens'=2] {'quad','core','ens'}, dimensions={0} | all-to-all | bytes 524288 | tf_op jit(solution)/shard_map/all_to_all | solution.py:436
  88.1 1.4 %attention_edges_back.1 = (f32[2,256,256]{2,1,0:T(8,128)S(1)}, bf16[128,256]{1,0:T(8,128)(2,1)S(1)}) custom-call(f32[8,16,128]{2,1,0:T(8,128)S(1)} %get-tuple-element.38.steps_ref, bf16[1024,128]{1,0:T(8,128)(2,1)S(1)} %get-tuple-element.41.q_ref, bf16[1024,256]{1,0:T(8,128)(2,1)S(1)} %get-tuple-element.46.kv_ref, ...), custom_call_target="tpu_custom_call" | custom-call | flops 167772160 | bytes 1048576 | tf_op jit(solution)/shard_map/attention_edges_back/pallas_call | solution.py:63
  89.5 1.2 %collective-permute-start.19 = (bf16[128,256]{1,0:T(8,128)(2,1)S(1)}, bf16[128,256]{1,0:T(8,128)(2,1)S(1)}, u32[]{:S(2)}, u32[]{:S(2)}) collective-permute-start(bf16[128,256]{1,0:T(8,128)(2,1)S(1)} %get-tuple-element.55), channel_id=1, source_target_pairs={{0,16},{16,0},{1,17},{17,1},{2,18},{18,2},{3,19},{19,3},{4,20},{20... | collective-permute-start | bytes 196616 | tf_op jit(solution)/shard_map/ppermute | solution.py:440
  90.7 3.9 %attention_interior_back.1.grads_ref = f32[1024,256]{1,0:T(8,128)S(1)} custom-call(f32[8,16,128]{2,1,0:T(8,128)S(1)} %get-tuple-element.38.steps_ref, bf16[1024,128]{1,0:T(8,128)(2,1)S(1)} %get-tuple-element.41.q_ref, bf16[1024,256]{1,0:T(8,128)(2,1)S(1)} %get-tuple-element.46.kv_ref, bf16[1024,128]{1,0:T(8,128)(2,1)S(1)} %bitcast.19, ...), custom_call_target="tpu_custom_call" | custom-call | flops 536870912 | bytes 4194304 | tf_op jit(solution)/shard_map/attention_interior_back/pallas_call | solution.py:63
  94.6 1.3 %collective-permute-done.19.from_low_ref.from_high_ref = bf16[128,256]{1,0:T(8,128)(2,1)S(1)} collective-permute-done((bf16[128,256]{1,0:T(8,128)(2,1)S(1)}, bf16[128,256]{1,0:T(8,128)(2,1)S(1)}, u32[]{:S(2)}, u32[]{:S(2)}) %collective-permute-start.19) | collective-permute-done | bytes 65568 | tf_op jit(solution)/shard_map/ppermute | solution.py:440
  95.8 2.1 %product.1 = bf16[1024,256]{1,0:T(8,128)(2,1)} custom-call(bf16[1024,1024]{1,0:T(8,128)(2,1)S(1)} %copy-done, bf16[128,256]{1,0:T(8,128)(2,1)S(1)} %collective-permute-done.19.from_low_ref.from_high_ref, bf16[128,256]{1,0:T(8,128)(2,1)S(1)} %collective-permute-done.19.from_low_ref.from_high_ref, f32[1024,256]{1,0:T(8,128)S(1)} %attention_interior_back.1.grads_ref), custom_call_target="tpu_custom_call" | custom-call | flops 1073741824 | bytes 4194304 | tf_op jit(solution)/shard_map/product/pallas_call | solution.py:63
  97.9 2.8 %all-to-all-start.3 = ((bf16[32,32,256]{2,1,0:T(8,128)(2,1)}), bf16[32,32,256]{2,1,0:T(8,128)(2,1)S(1)}, u32[]{:S(2)}, u32[]{:S(2)}) async-start(bf16[32,32,256]{2,1,0:T(8,128)(2,1)} %bitcast.11), calls=%async_computation.3 | async-start | bytes 1048576 | tf_op jit(solution)/shard_map/all_to_all | solution.py:436
  100.7 1.5 %collective-permute-start.20 = (f32[100,128]{1,0:T(8,128)S(1)}, f32[100,128]{1,0:T(8,128)S(1)}, u32[]{:S(2)}, u32[]{:S(2)}) collective-permute-start(f32[100,128]{1,0:T(8,128)S(1)} %get-tuple-element.58), channel_id=1, source_target_pairs={{0,1},{1,0},{2,3},{3,2},{4,5},{5,4},{6,7},{7,6},{8,9},{9,8},{10,11... | collective-permute-start | bytes 153608 | tf_op jit(solution)/shard_map/ppermute | solution.py:440
  102.2 4.5 %collective-permute-done.20 = f32[100,128]{1,0:T(8,128)S(1)} collective-permute-done((f32[100,128]{1,0:T(8,128)S(1)}, f32[100,128]{1,0:T(8,128)S(1)}, u32[]{:S(2)}, u32[]{:S(2)}) %collective-permute-start.20) | collective-permute-done | bytes 51232 | tf_op jit(solution)/shard_map/ppermute | solution.py:440
  106.9 0.7 copy.10
  107.6 9.1 %all-to-all-done.3 = bf16[32,32,256]{2,1,0:T(8,128)(2,1)S(1)} async-done(((bf16[32,32,256]{2,1,0:T(8,128)(2,1)}), bf16[32,32,256]{2,1,0:T(8,128)(2,1)S(1)}, u32[]{:S(2)}, u32[]{:S(2)}) %all-to-all-start.3) | async-done | bytes 524320 | tf_op jit(solution)/shard_map/all_to_all | solution.py:436
  116.6 0.8 gather_sums.1
  (34 shorter events, 0.4 us)
Async XLA Ops:
  2.4 5.2 %collective-permute-start = (bf16[32,1152]{1,0:T(8,128)(2,1)}, bf16[32,1152]{1,0:T(8,128)(2,1)S(1)}, u32[]{:S(2)}, u32[]{:S(2)}) collective-permute-start(bf16[32,1152]{1,0:T(8,128)(2,1)} %get-tuple-element.31), channel_id=1, source_target_pairs={{0,16},{16,0},{1,17},{17,1},{2,18},{18,2},{3,19},{19,3},{4,20},{20... | collective-permute-start | bytes 221192 | tf_op jit(solution)/shard_map/ppermute | solution.py:440
  7.5 22.9 %copy-start.1 = (bf16[144,1024]{1,0:T(8,128)(2,1)S(1)}, bf16[144,1024]{1,0:T(8,128)(2,1)}, u32[]{:S(2)}) copy-start(bf16[144,1024]{1,0:T(8,128)(2,1)} %get-tuple-element.36.refs_0_) | copy-start | bytes 884740
  8.5 12.9 %collective-permute-start.2 = (bf16[2,32,1152]{2,1,0:T(8,128)(2,1)S(1)}, bf16[2,32,1152]{2,1,0:T(8,128)(2,1)S(1)}, u32[]{:S(2)}, u32[]{:S(2)}) collective-permute-start(bf16[2,32,1152]{2,1,0:T(8,128)(2,1)S(1)} %pad_maximum_fusion.1), channel_id=1, source_target_pairs={{0,1},{1,0},{2,3},{3,2},{4,5},{5,4},{6,7},{7,6},{8,9},{9,8},{10,11... | collective-permute-start | bytes 442376 | tf_op jit(solution)/shard_map/ppermute | solution.py:440
  9.8 20.5 %all-to-all-start = ((bf16[16,32,384]{2,1,0:T(8,128)(2,1)}), bf16[16,32,384]{2,1,0:T(8,128)(2,1)S(1)}, u32[]{:S(2)}, u32[]{:S(2)}) async-start(bf16[16,32,384]{2,1,0:T(8,128)(2,1)} %bitcast.27), calls=%async_computation | async-start | bytes 786432 | tf_op jit(solution)/shard_map/all_to_all | solution.py:436
  18.9 19.2 %collective-permute-start.1 = (bf16[144,1024]{1,0:T(8,128)(2,1)}, bf16[144,1024]{1,0:T(8,128)(2,1)S(1)}, u32[]{:S(2)}, u32[]{:S(2)}) collective-permute-start(bf16[144,1024]{1,0:T(8,128)(2,1)} %get-tuple-element.36.refs_0_), channel_id=1, source_target_pairs={{0,4},{4,0},{8,12},{12,8},{1,5},{5,1},{9,13},{13,9},{2,6},{6,2},{1... | collective-permute-start | bytes 884744 | tf_op jit(solution)/shard_map/ppermute | solution.py:440
  20.3 18.7 %collective-permute-start.4 = (bf16[144,1024]{1,0:T(8,128)(2,1)}, bf16[144,1024]{1,0:T(8,128)(2,1)S(1)}, u32[]{:S(2)}, u32[]{:S(2)}) collective-permute-start(bf16[144,1024]{1,0:T(8,128)(2,1)} %get-tuple-element.36.refs_0_), channel_id=1, source_target_pairs={{0,12},{4,8},{8,4},{12,0},{1,13},{5,9},{9,5},{13,1},{2,14},{6,10},... | collective-permute-start | bytes 884744 | tf_op jit(solution)/shard_map/ppermute | solution.py:440
  30.4 9.8 %collective-permute-start.3 = (bf16[144,1024]{1,0:T(8,128)(2,1)S(1)}, bf16[144,1024]{1,0:T(8,128)(2,1)S(1)}, u32[]{:S(2)}, u32[]{:S(2)}) collective-permute-start(bf16[144,1024]{1,0:T(8,128)(2,1)S(1)} %copy-done.1), channel_id=1, source_target_pairs={{0,8},{4,12},{8,0},{12,4},{1,9},{5,13},{9,1},{13,5},{2,10},{6,14},... | collective-permute-start | bytes 884744 | tf_op jit(solution)/shard_map/ppermute | solution.py:440
  32.1 13.3 %collective-permute-start.9 = (bf16[16,32,384]{2,1,0:T(8,128)(2,1)S(1)}, bf16[16,32,384]{2,1,0:T(8,128)(2,1)S(1)}, u32[]{:S(2)}, u32[]{:S(2)}) collective-permute-start(bf16[16,32,384]{2,1,0:T(8,128)(2,1)S(1)} %all-to-all-done.refs_0_), channel_id=1, source_target_pairs={{0,1},{1,0},{2,3},{3,2},{4,5},{5,4},{6,7},{7,6},{8,9},{9,8},{10,11... | collective-permute-start | bytes 1179656 | tf_op jit(solution)/shard_map/ppermute | solution.py:440
  32.3 8.8 %collective-permute-start.5 = (bf16[144,1024]{1,0:T(8,128)(2,1)S(1)}, bf16[144,1024]{1,0:T(8,128)(2,1)S(1)}, u32[]{:S(2)}, u32[]{:S(2)}) collective-permute-start(bf16[144,1024]{1,0:T(8,128)(2,1)S(1)} %copy-done.1), channel_id=1, source_target_pairs={{0,2},{2,0},{1,3},{3,1},{4,6},{6,4},{5,7},{7,5},{8,10},{10,8},{9,1... | collective-permute-start | bytes 884744 | tf_op jit(solution)/shard_map/ppermute | solution.py:440
  38.1 4.3 %collective-permute-start.6 = (bf16[144,1024]{1,0:T(8,128)(2,1)S(1)}, bf16[144,1024]{1,0:T(8,128)(2,1)S(1)}, u32[]{:S(2)}, u32[]{:S(2)}) collective-permute-start(bf16[144,1024]{1,0:T(8,128)(2,1)S(1)} %collective-permute-done.1.refs_1_), channel_id=1, source_target_pairs={{0,2},{2,0},{1,3},{3,1},{4,6},{6,4},{5,7},{7,5},{8,10},{10,8},{9,1... | collective-permute-start | bytes 884744 | tf_op jit(solution)/shard_map/ppermute | solution.py:440
  39.0 4.3 %collective-permute-start.8 = (bf16[144,1024]{1,0:T(8,128)(2,1)S(1)}, bf16[144,1024]{1,0:T(8,128)(2,1)S(1)}, u32[]{:S(2)}, u32[]{:S(2)}) collective-permute-start(bf16[144,1024]{1,0:T(8,128)(2,1)S(1)} %collective-permute-done.4.refs_3_), channel_id=1, source_target_pairs={{0,2},{2,0},{1,3},{3,1},{4,6},{6,4},{5,7},{7,5},{8,10},{10,8},{9,1... | collective-permute-start | bytes 884744 | tf_op jit(solution)/shard_map/ppermute | solution.py:440
  40.1 3.7 %collective-permute-start.7 = (bf16[144,1024]{1,0:T(8,128)(2,1)S(1)}, bf16[144,1024]{1,0:T(8,128)(2,1)S(1)}, u32[]{:S(2)}, u32[]{:S(2)}) collective-permute-start(bf16[144,1024]{1,0:T(8,128)(2,1)S(1)} %collective-permute-done.3.refs_2_), channel_id=1, source_target_pairs={{0,2},{2,0},{1,3},{3,1},{4,6},{6,4},{5,7},{7,5},{8,10},{10,8},{9,1... | collective-permute-start | bytes 884744 | tf_op jit(solution)/shard_map/ppermute | solution.py:440
  41.1 24.0 %collective-permute-start.10 = (bf16[2,64,1152]{2,1,0:T(8,128)(2,1)S(1)}, bf16[2,64,1152]{2,1,0:T(8,128)(2,1)S(1)}, u32[]{:S(2)}, u32[]{:S(2)}) collective-permute-start(bf16[2,64,1152]{2,1,0:T(8,128)(2,1)S(1)} %bitcast.21), channel_id=1, source_target_pairs={{0,4},{4,0},{8,12},{12,8},{1,5},{5,1},{9,13},{13,9},{2,6},{6,2},{1... | collective-permute-start | bytes 884744 | tf_op jit(solution)/shard_map/ppermute | solution.py:440
  42.4 22.7 %collective-permute-start.11 = (bf16[2,64,1152]{2,1,0:T(8,128)(2,1)S(1)}, bf16[2,64,1152]{2,1,0:T(8,128)(2,1)S(1)}, u32[]{:S(2)}, u32[]{:S(2)}) collective-permute-start(bf16[2,64,1152]{2,1,0:T(8,128)(2,1)S(1)} %bitcast.22), channel_id=1, source_target_pairs={{0,8},{4,12},{8,0},{12,4},{1,9},{5,13},{9,1},{13,5},{2,10},{6,14},... | collective-permute-start | bytes 884744 | tf_op jit(solution)/shard_map/ppermute | solution.py:440
  43.3 21.8 %collective-permute-start.12 = (bf16[2,64,1152]{2,1,0:T(8,128)(2,1)S(1)}, bf16[2,64,1152]{2,1,0:T(8,128)(2,1)S(1)}, u32[]{:S(2)}, u32[]{:S(2)}) collective-permute-start(bf16[2,64,1152]{2,1,0:T(8,128)(2,1)S(1)} %bitcast.23), channel_id=1, source_target_pairs={{0,12},{4,8},{8,4},{12,0},{1,13},{5,9},{9,5},{13,1},{2,14},{6,10},... | collective-permute-start | bytes 884744 | tf_op jit(solution)/shard_map/ppermute | solution.py:440
  46.7 10.5 %collective-permute-start.13 = (bf16[128,256]{1,0:T(8,128)(2,1)S(1)}, bf16[128,256]{1,0:T(8,128)(2,1)S(1)}, u32[]{:S(2)}, u32[]{:S(2)}) collective-permute-start(bf16[128,256]{1,0:T(8,128)(2,1)S(1)} %get-tuple-element.47), channel_id=1, source_target_pairs={{0,16},{16,0},{1,17},{17,1},{2,18},{18,2},{3,19},{19,3},{4,20},{20... | collective-permute-start | bytes 196616 | tf_op jit(solution)/shard_map/ppermute | solution.py:440
  49.1 17.1 %copy-start.4 = (bf16[1,64,1024]{2,1,0:T(8,128)(2,1)S(1)}, bf16[1,64,1024]{2,1,0:T(8,128)(2,1)}, u32[]{:S(2)}) copy-start(bf16[1,64,1024]{2,1,0:T(8,128)(2,1)} %get-tuple-element.53) | copy-start | bytes 393220
  58.6 14.6 %all-to-all-start.1 = ((bf16[16,64,128]{2,1,0:T(8,128)(2,1)}), bf16[16,64,128]{2,1,0:T(8,128)(2,1)S(1)}, u32[]{:S(2)}, u32[]{:S(2)}) async-start(bf16[16,64,128]{2,1,0:T(8,128)(2,1)} %bitcast.7), calls=%async_computation.1 | async-start | bytes 524288 | tf_op jit(solution)/shard_map/all_to_all | solution.py:436
  65.1 8.1 %copy-start.2 = (bf16[1,64,1024]{2,1,0:T(8,128)(2,1)S(1)}, bf16[1,64,1024]{2,1,0:T(8,128)(2,1)}, u32[]{:S(2)}) copy-start(bf16[1,64,1024]{2,1,0:T(8,128)(2,1)} %get-tuple-element.52.refs_0_) | copy-start | bytes 393220
  65.1 8.1 %copy-start.3 = (f32[128]{0:T(128)S(1)}, f32[128]{0:T(128)}, u32[]{:S(2)}) copy-start(f32[128]{0:T(128)} %param.12) | copy-start | bytes 1540
  65.1 2.5 %collective-permute-start.14 = (bf16[2,64,1152]{2,1,0:T(8,128)(2,1)S(1)}, bf16[2,64,1152]{2,1,0:T(8,128)(2,1)S(1)}, u32[]{:S(2)}, u32[]{:S(2)}) collective-permute-start(bf16[2,64,1152]{2,1,0:T(8,128)(2,1)S(1)} %bitcast.24), channel_id=1, source_target_pairs={{0,2},{2,0},{1,3},{3,1},{4,6},{6,4},{5,7},{7,5},{8,10},{10,8},{9,1... | collective-permute-start | bytes 884744 | tf_op jit(solution)/shard_map/ppermute | solution.py:440
  65.3 2.3 %collective-permute-start.15 = (bf16[2,64,1152]{2,1,0:T(8,128)(2,1)S(1)}, bf16[2,64,1152]{2,1,0:T(8,128)(2,1)S(1)}, u32[]{:S(2)}, u32[]{:S(2)}) collective-permute-start(bf16[2,64,1152]{2,1,0:T(8,128)(2,1)S(1)} %collective-permute-done.10.refs_1_), channel_id=1, source_target_pairs={{0,2},{2,0},{1,3},{3,1},{4,6},{6,4},{5,7},{7,5},{8,10},{10,8},{9,1... | collective-permute-start | bytes 884744 | tf_op jit(solution)/shard_map/ppermute | solution.py:440
  65.7 1.9 %collective-permute-start.16 = (bf16[2,64,1152]{2,1,0:T(8,128)(2,1)S(1)}, bf16[2,64,1152]{2,1,0:T(8,128)(2,1)S(1)}, u32[]{:S(2)}, u32[]{:S(2)}) collective-permute-start(bf16[2,64,1152]{2,1,0:T(8,128)(2,1)S(1)} %collective-permute-done.11.refs_2_), channel_id=1, source_target_pairs={{0,2},{2,0},{1,3},{3,1},{4,6},{6,4},{5,7},{7,5},{8,10},{10,8},{9,1... | collective-permute-start | bytes 884744 | tf_op jit(solution)/shard_map/ppermute | solution.py:440
  65.8 2.2 %collective-permute-start.17 = (bf16[2,64,1152]{2,1,0:T(8,128)(2,1)S(1)}, bf16[2,64,1152]{2,1,0:T(8,128)(2,1)S(1)}, u32[]{:S(2)}, u32[]{:S(2)}) collective-permute-start(bf16[2,64,1152]{2,1,0:T(8,128)(2,1)S(1)} %collective-permute-done.12.refs_3_), channel_id=1, source_target_pairs={{0,2},{2,0},{1,3},{3,1},{4,6},{6,4},{5,7},{7,5},{8,10},{10,8},{9,1... | collective-permute-start | bytes 884744 | tf_op jit(solution)/shard_map/ppermute | solution.py:440
  66.2 6.9 %collective-permute-start.18 = (bf16[1,64,1024]{2,1,0:T(8,128)(2,1)S(1)}, bf16[1,64,1024]{2,1,0:T(8,128)(2,1)S(1)}, u32[]{:S(2)}, u32[]{:S(2)}) collective-permute-start(bf16[1,64,1024]{2,1,0:T(8,128)(2,1)S(1)} %copy-done.4), channel_id=1, source_target_pairs={{0,1},{1,0},{2,3},{3,2},{4,5},{5,4},{6,7},{7,6},{8,9},{9,8},{10,11... | collective-permute-start | bytes 393224 | tf_op jit(solution)/shard_map/ppermute | solution.py:440
  76.9 18.9 %copy-start = (bf16[1024,1024]{1,0:T(8,128)(2,1)S(1)}, bf16[1024,1024]{1,0:T(8,128)(2,1)}, u32[]{:S(2)}) copy-start(bf16[1024,1024]{1,0:T(8,128)(2,1)} %get-tuple-element.37.normed_any.normed_ref) | copy-start | bytes 6291460
  89.5 6.3 %collective-permute-start.19 = (bf16[128,256]{1,0:T(8,128)(2,1)S(1)}, bf16[128,256]{1,0:T(8,128)(2,1)S(1)}, u32[]{:S(2)}, u32[]{:S(2)}) collective-permute-start(bf16[128,256]{1,0:T(8,128)(2,1)S(1)} %get-tuple-element.55), channel_id=1, source_target_pairs={{0,16},{16,0},{1,17},{17,1},{2,18},{18,2},{3,19},{19,3},{4,20},{20... | collective-permute-start | bytes 196616 | tf_op jit(solution)/shard_map/ppermute | solution.py:440
  97.9 18.7 %all-to-all-start.3 = ((bf16[32,32,256]{2,1,0:T(8,128)(2,1)}), bf16[32,32,256]{2,1,0:T(8,128)(2,1)S(1)}, u32[]{:S(2)}, u32[]{:S(2)}) async-start(bf16[32,32,256]{2,1,0:T(8,128)(2,1)} %bitcast.11), calls=%async_computation.3 | async-start | bytes 1048576 | tf_op jit(solution)/shard_map/all_to_all | solution.py:436
  100.7 6.0 %collective-permute-start.20 = (f32[100,128]{1,0:T(8,128)S(1)}, f32[100,128]{1,0:T(8,128)S(1)}, u32[]{:S(2)}, u32[]{:S(2)}) collective-permute-start(f32[100,128]{1,0:T(8,128)S(1)} %get-tuple-element.58), channel_id=1, source_target_pairs={{0,1},{1,0},{2,3},{3,2},{4,5},{5,4},{6,7},{7,6},{8,9},{9,8},{10,11... | collective-permute-start | bytes 153608 | tf_op jit(solution)/shard_map/ppermute | solution.py:440

commit v12 on v11

--- a/solution.py
+++ b/solution.py
@@ -497,18 +497,15 @@
     )(neighbours, members.reshape(node_rows, LATENT_DIM))
 
     packed, normed = lax.optimization_barrier((in_order(packed, "half", 0), normed))
-    near = [normed, swap(normed, "quad", 1), None, swap(normed, "quad", 3)]
+    near = [normed, swap(normed, "quad", 1), swap(normed, "quad", 2)]
+    packed, last = lax.optimization_barrier((in_order(packed, "ens", 1), normed))
+    near.append(swap(last, "quad", 3))
     if paired:
         columns = exchange(columns.reshape(-1, shard, 3 * COLS), nodes)
-        packed = in_order(packed, "ens", 1)
-        columns, late, packed = lax.optimization_barrier((columns, normed, packed))
         columns = [columns, swap(columns, "ens", 1)]
     else:
         columns = [exchange(columns.reshape(-1, shard, 3 * COLS), everyone)]
         columns = [columns[0].reshape(LATENT_DIM, 3 * COLS)]
-        late = normed
-        packed = in_order(packed, "ens", 1)
-    near[2] = swap(late, "quad", 2)
     far = [swap(piece, "core", 1) for piece in near]
     normed, steps = call(
         collect_kernel,

time: 118 us -> 118 us (level)
    all_to_all x3, starting transfers between devices: 18.3 us -> 19.6 us  [exchange(): return lax.all_to_all(chunks, axes, 0, 0)]
where the time goes in v12:
time: 118 us
  starting transfers between devices  39.8 us (34%)
  waiting for transfers between devices  38.1 us (32%)
  Pallas kernels  25.9 us (22%)
  blocking collectives  11.2 us (9%)
    pallas_call x13, Pallas kernels, run(): made(*[pltpu.with_memory_space_constraint(arg, pltpu.HBM) if space == 'h'...  25.9 us
    ppermute x21, waiting for transfers between devices, swap(): lax.ppermute(value, axis, [(i, i ^ step) for i in range(lax.axis_size(axi...  20.4 us
    ppermute x21, starting transfers between devices, swap(): lax.ppermute(value, axis, [(i, i ^ step) for i in range(lax.axis_size(axi...  20.3 us
    all_to_all x3, starting transfers between devices, exchange(): return lax.all_to_all(chunks, axes, 0, 0)  19.6 us
    all_to_all x3, waiting for transfers between devices, exchange(): return lax.all_to_all(chunks, axes, 0, 0)  17.7 us
    all_to_all x1, blocking collectives, exchange(): return lax.all_to_all(chunks, axes, 0, 0)  11.2 us
  transfers between devices with their start and end apart: 24, of which 10 were waited for; matrix products, arithmetic and copies ran while one was open for 1% of the time, Pallas kernels for 14%

profile of v12, /device:TPU:1, one launch (start us, length us, event | category | flops | bytes accessed | tf_op | source)
XLA Modules:
  0.0 117.9 jit_solution(9700771472853656694)
XLA Ops:
  0.6 1.8 %prepare_weights.1 = (bf16[2,8,1,32,384]{4,3,2,1,0:T(8,128)(2,1)}, bf16[32,1152]{1,0:T(8,128)(2,1)}) custom-call(bf16[32,3072]{1,0:T(8,128)(2,1)} %w_any.1, bf16[32,1024]{1,0:T(8,128)(2,1)} %mix_any.1, bf16[32,100]{1,0:T(8,128)(2,1)} %readout_any.1), custom_call_target="tpu_custom_call" | custom-call | bytes 1048576 | tf_op jit(solution)/shard_map/prepare_weights/pallas_call | solution.py:63
  2.4 3.2 %collective-permute-start = (bf16[32,1152]{1,0:T(8,128)(2,1)}, bf16[32,1152]{1,0:T(8,128)(2,1)S(1)}, u32[]{:S(2)}, u32[]{:S(2)}) collective-permute-start(bf16[32,1152]{1,0:T(8,128)(2,1)} %get-tuple-element.30), channel_id=1, source_target_pairs={{0,16},{16,0},{1,17},{17,1},{2,18},{18,2},{3,19},{19,3},{4,20},{20... | collective-permute-start | bytes 221192 | tf_op jit(solution)/shard_map/ppermute | solution.py:440
  5.6 1.9 %norm.1 = (bf16[144,1024]{1,0:T(8,128)(2,1)}, bf16[1,64,1024]{2,1,0:T(8,128)(2,1)}, bf16[1,64,1024]{2,1,0:T(8,128)(2,1)}) custom-call(s32[2,4]{1,0:T(2,128)} %near_any.1, bf16[128,1024]{1,0:T(8,128)(2,1)} %bitcast.28), custom_call_target="tpu_custom_call" | custom-call | flops 1048576 | bytes 1048576 | tf_op jit(solution)/shard_map/norm/pallas_call | solution.py:63
  7.6 0.9 select_bitcast_fusion.3
  8.5 1.3 %collective-permute-start.3 = (bf16[2,32,1152]{2,1,0:T(8,128)(2,1)S(1)}, bf16[2,32,1152]{2,1,0:T(8,128)(2,1)S(1)}, u32[]{:S(2)}, u32[]{:S(2)}) collective-permute-start(bf16[2,32,1152]{2,1,0:T(8,128)(2,1)S(1)} %pad_maximum_fusion.1), channel_id=1, source_target_pairs={{0,1},{1,0},{2,3},{3,2},{4,5},{5,4},{6,7},{7,6},{8,9},{9,8},{10,11... | collective-permute-start | bytes 442376 | tf_op jit(solution)/shard_map/ppermute | solution.py:440
  9.8 9.1 %all-to-all-start = ((bf16[16,32,384]{2,1,0:T(8,128)(2,1)}), bf16[16,32,384]{2,1,0:T(8,128)(2,1)S(1)}, u32[]{:S(2)}, u32[]{:S(2)}) async-start(bf16[16,32,384]{2,1,0:T(8,128)(2,1)} %bitcast.27), calls=%async_computation | async-start | bytes 786432 | tf_op jit(solution)/shard_map/all_to_all | solution.py:436
  18.9 1.4 %collective-permute-start.2 = (bf16[144,1024]{1,0:T(8,128)(2,1)}, bf16[144,1024]{1,0:T(8,128)(2,1)S(1)}, u32[]{:S(2)}, u32[]{:S(2)}) collective-permute-start(bf16[144,1024]{1,0:T(8,128)(2,1)} %get-tuple-element.34.refs_0_), channel_id=1, source_target_pairs={{0,8},{4,12},{8,0},{12,4},{1,9},{5,13},{9,1},{13,5},{2,10},{6,14},... | collective-permute-start | bytes 884744 | tf_op jit(solution)/shard_map/ppermute | solution.py:440
  20.3 1.2 %collective-permute-start.1 = (bf16[144,1024]{1,0:T(8,128)(2,1)}, bf16[144,1024]{1,0:T(8,128)(2,1)S(1)}, u32[]{:S(2)}, u32[]{:S(2)}) collective-permute-start(bf16[144,1024]{1,0:T(8,128)(2,1)} %get-tuple-element.34.refs_0_), channel_id=1, source_target_pairs={{0,4},{4,0},{8,12},{12,8},{1,5},{5,1},{9,13},{13,9},{2,6},{6,2},{1... | collective-permute-start | bytes 884744 | tf_op jit(solution)/shard_map/ppermute | solution.py:440
  21.6 0.1 collective-permute-start.4
  21.7 8.6 %all-to-all-done.refs_0_ = bf16[16,32,384]{2,1,0:T(8,128)(2,1)S(1)} async-done(((bf16[16,32,384]{2,1,0:T(8,128)(2,1)}), bf16[16,32,384]{2,1,0:T(8,128)(2,1)S(1)}, u32[]{:S(2)}, u32[]{:S(2)}) %all-to-all-start) | async-done | bytes 393248 | tf_op jit(solution)/shard_map/all_to_all | solution.py:436
  30.3 0.3 collective-permute-start.9
  30.6 1.7 %collective-permute-start.5 = (bf16[144,1024]{1,0:T(8,128)(2,1)S(1)}, bf16[144,1024]{1,0:T(8,128)(2,1)S(1)}, u32[]{:S(2)}, u32[]{:S(2)}) collective-permute-start(bf16[144,1024]{1,0:T(8,128)(2,1)S(1)} %copy-done.1), channel_id=1, source_target_pairs={{0,2},{2,0},{1,3},{3,1},{4,6},{6,4},{5,7},{7,5},{8,10},{10,8},{9,1... | collective-permute-start | bytes 884744 | tf_op jit(solution)/shard_map/ppermute | solution.py:440
  32.2 1.7 %collective-permute-done.2.refs_2_ = bf16[144,1024]{1,0:T(8,128)(2,1)S(1)} collective-permute-done((bf16[144,1024]{1,0:T(8,128)(2,1)}, bf16[144,1024]{1,0:T(8,128)(2,1)S(1)}, u32[]{:S(2)}, u32[]{:S(2)}) %collective-permute-start.2) | collective-permute-done | bytes 294944 | tf_op jit(solution)/shard_map/ppermute | solution.py:440
  33.9 1.3 %collective-permute-start.7 = (bf16[144,1024]{1,0:T(8,128)(2,1)S(1)}, bf16[144,1024]{1,0:T(8,128)(2,1)S(1)}, u32[]{:S(2)}, u32[]{:S(2)}) collective-permute-start(bf16[144,1024]{1,0:T(8,128)(2,1)S(1)} %collective-permute-done.2.refs_2_), channel_id=1, source_target_pairs={{0,2},{2,0},{1,3},{3,1},{4,6},{6,4},{5,7},{7,5},{8,10},{10,8},{9,1... | collective-permute-start | bytes 884744 | tf_op jit(solution)/shard_map/ppermute | solution.py:440
  35.3 5.9 %collective-permute-done.4.refs_3_ = bf16[144,1024]{1,0:T(8,128)(2,1)S(1)} collective-permute-done((bf16[144,1024]{1,0:T(8,128)(2,1)S(1)}, bf16[144,1024]{1,0:T(8,128)(2,1)S(1)}, u32[]{:S(2)}, u32[]{:S(2)}) %collective-permute-start.4) | collective-permute-done | bytes 294944 | tf_op jit(solution)/shard_map/ppermute | solution.py:440
  41.1 0.9 collective-permute-start.8
  42.0 0.3 collective-permute-start.10
  42.4 0.2 collective-permute-start.11
  42.6 2.2 %collective-permute-start.12 = (bf16[2,64,1152]{2,1,0:T(8,128)(2,1)S(1)}, bf16[2,64,1152]{2,1,0:T(8,128)(2,1)S(1)}, u32[]{:S(2)}, u32[]{:S(2)}) collective-permute-start(bf16[2,64,1152]{2,1,0:T(8,128)(2,1)S(1)} %bitcast.23), channel_id=1, source_target_pairs={{0,12},{4,8},{8,4},{12,0},{1,13},{5,9},{9,5},{13,1},{2,14},{6,10},... | collective-permute-start | bytes 884744 | tf_op jit(solution)/shard_map/ppermute | solution.py:440
  44.8 1.5 %collect.1 = (bf16[1024,1024]{1,0:T(8,128)(2,1)}, f32[8,16,128]{2,1,0:T(8,128)S(1)}) custom-call(bf16[144,1024]{1,0:T(8,128)(2,1)S(1)} %copy-done.1, bf16[144,1024]{1,0:T(8,128)(2,1)S(1)} %collective-permute-done.1.refs_1_, bf16[144,1024]{1,0:T(8,128)(2,1)S(1)} %collective-permute-done.2.refs_2_, bf16[144,1024]{1,0:T(8,128)(2,1)S(1)} %collective-permute-done.4.refs_3_, ...), custom_call_target="tpu_custom_call" | custom-call | bytes 4194304 | tf_op jit(solution)/shard_map/collect/pallas_call | solution.py:63
  46.3 1.3 %project_rims.1 = (bf16[16,2,32,384]{3,2,1,0:T(8,128)(2,1)S(1)}, bf16[128,256]{1,0:T(8,128)(2,1)S(1)}) custom-call(bf16[1024,1024]{1,0:T(8,128)(2,1)} %get-tuple-element.35.normed_any.normed_ref, bf16[16,32,384]{2,1,0:T(8,128)(2,1)S(1)} %all-to-all-done.refs_0_, bf16[16,32,384]{2,1,0:T(8,128)(2,1)S(1)} %collective-permute-done.9.refs_1_), custom_call_target="tpu_custom_call" | custom-call | flops 67108864 | bytes 1048576 | tf_op jit(solution)/shard_map/project_rims/pallas_call | solution.py:63
  47.6 2.2 %collective-permute-start.13 = (bf16[128,256]{1,0:T(8,128)(2,1)S(1)}, bf16[128,256]{1,0:T(8,128)(2,1)S(1)}, u32[]{:S(2)}, u32[]{:S(2)}) collective-permute-start(bf16[128,256]{1,0:T(8,128)(2,1)S(1)} %get-tuple-element.45), channel_id=1, source_target_pairs={{0,16},{16,0},{1,17},{17,1},{2,18},{18,2},{3,19},{19,3},{4,20},{20... | collective-permute-start | bytes 196616 | tf_op jit(solution)/shard_map/ppermute | solution.py:440
  49.8 2.9 %project.1 = (bf16[1024,128]{1,0:T(8,128)(2,1)S(1)}, bf16[1024,256]{1,0:T(8,128)(2,1)S(1)}) custom-call(bf16[1024,1024]{1,0:T(8,128)(2,1)} %get-tuple-element.35.normed_any.normed_ref, bf16[16,2,32,384]{3,2,1,0:T(8,128)(2,1)S(1)} %get-tuple-element.38.w_ref), custom_call_target="tpu_custom_call" | custom-call | flops 805306368 | bytes 4194304 | tf_op jit(solution)/shard_map/project/pallas_call | solution.py:63
  52.7 1.9 %attention_interior.1.done_ref = bf16[1024,128]{1,0:T(8,128)(2,1)S(1)} custom-call(f32[8,16,128]{2,1,0:T(8,128)S(1)} %get-tuple-element.36.steps_ref, bf16[1024,128]{1,0:T(8,128)(2,1)S(1)} %get-tuple-element.39.q_ref, bf16[1024,256]{1,0:T(8,128)(2,1)S(1)} %get-tuple-element.44.kv_ref), custom_call_target="tpu_custom_call" | custom-call | flops 268435456 | bytes 2097152 | tf_op jit(solution)/shard_map/attention_interior/pallas_call | solution.py:63
  54.6 1.8 %collective-permute-done.13.low_ref.high_ref = bf16[128,256]{1,0:T(8,128)(2,1)S(1)} collective-permute-done((bf16[128,256]{1,0:T(8,128)(2,1)S(1)}, bf16[128,256]{1,0:T(8,128)(2,1)S(1)}, u32[]{:S(2)}, u32[]{:S(2)}) %collective-permute-start.13) | collective-permute-done | bytes 65568 | tf_op jit(solution)/shard_map/ppermute | solution.py:440
  56.4 1.4 %attention_edges.1 = bf16[1024,128]{1,0:T(8,128)(2,1)} custom-call(f32[8,16,128]{2,1,0:T(8,128)S(1)} %get-tuple-element.36.steps_ref, bf16[1024,128]{1,0:T(8,128)(2,1)S(1)} %get-tuple-element.39.q_ref, bf16[1024,256]{1,0:T(8,128)(2,1)S(1)} %get-tuple-element.44.kv_ref, bf16[128,256]{1,0:T(8,128)(2,1)S(1)} %collective-permute-done.13.low_ref.high_ref, ...), custom_call_target="tpu_custom_call" | custom-call | flops 67108864 | bytes 1048576 | tf_op jit(solution)/shard_map/attention_edges/pallas_call | solution.py:63
  57.8 7.7 %all-to-all-start.1 = ((bf16[16,64,128]{2,1,0:T(8,128)(2,1)}), bf16[16,64,128]{2,1,0:T(8,128)(2,1)S(1)}, u32[]{:S(2)}, u32[]{:S(2)}) async-start(bf16[16,64,128]{2,1,0:T(8,128)(2,1)} %bitcast.7), calls=%async_computation.1 | async-start | bytes 524288 | tf_op jit(solution)/shard_map/all_to_all | solution.py:436
  65.6 0.2 collective-permute-start.14
  65.8 0.4 collective-permute-start.15
  66.2 0.1 collective-permute-start.16
  66.3 0.4 collective-permute-start.17
  66.7 1.4 %collective-permute-start.18 = (bf16[1,64,1024]{2,1,0:T(8,128)(2,1)S(1)}, bf16[1,64,1024]{2,1,0:T(8,128)(2,1)S(1)}, u32[]{:S(2)}, u32[]{:S(2)}) collective-permute-start(bf16[1,64,1024]{2,1,0:T(8,128)(2,1)S(1)} %copy-done.4), channel_id=1, source_target_pairs={{0,1},{1,0},{2,3},{3,2},{4,5},{5,4},{6,7},{7,6},{8,9},{9,8},{10,11... | collective-permute-start | bytes 393224 | tf_op jit(solution)/shard_map/ppermute | solution.py:440
  68.1 0.4 collective-permute-done.17.refs_7_
  68.5 1.5 %assemble.1.w_any = bf16[2,4,2,64,1152]{4,3,2,1,0:T(8,128)(2,1)} custom-call(bf16[2,64,1152]{2,1,0:T(8,128)(2,1)S(1)} %bitcast.25, bf16[2,64,1152]{2,1,0:T(8,128)(2,1)S(1)} %collective-permute-done.10.refs_1_, bf16[2,64,1152]{2,1,0:T(8,128)(2,1)S(1)} %collective-permute-done.11.refs_2_, bf16[2,64,1152]{2,1,0:T(8,128)(2,1)S(1)} %collective-permute-done.12.refs_3_, ...), custom_call_target="tpu_custom_call" | custom-call | bytes 4194304 | tf_op jit(solution)/shard_map/assemble/pallas_call | solution.py:63
  70.0 3.6 %collective-permute-done.18.refs_1_ = bf16[1,64,1024]{2,1,0:T(8,128)(2,1)S(1)} collective-permute-done((bf16[1,64,1024]{2,1,0:T(8,128)(2,1)S(1)}, bf16[1,64,1024]{2,1,0:T(8,128)(2,1)S(1)}, u32[]{:S(2)}, u32[]{:S(2)}) %collective-permute-start.18) | collective-permute-done | bytes 131104 | tf_op jit(solution)/shard_map/ppermute | solution.py:440
  73.7 3.7 %mix_loss_backward.1 = (f32[100,128]{1,0:T(8,128)S(1)}, bf16[16,64,128]{2,1,0:T(8,128)(2,1)S(1)}) custom-call(bf16[16,64,128]{2,1,0:T(8,128)(2,1)S(1)} %all-to-all-done.1.att_ref, f32[1,128]{1,0:T(1,128)S(1)} %bitcast.26, f32[100,128]{1,0:T(8,128)} %truth_any.1, bf16[2,4,2,64,1152]{4,3,2,1,0:T(8,128)(2,1)} %assemble.1.w_any, ...), custom_call_target="tpu_custom_call" | custom-call | flops 603979776 | bytes 4194304 | tf_op jit(solution)/shard_map/mix_loss_backward/pallas_call | solution.py:63
  77.4 11.2 %all_to_all.20 = bf16[16,64,128]{2,1,0:T(8,128)(2,1)S(1)} all-to-all(bf16[16,64,128]{2,1,0:T(8,128)(2,1)S(1)} %get-tuple-element.52), channel_id=1, replica_groups=mesh['half'=2,'quad'=4,'core'=2,'ens'=2] {'quad','core','ens'}, dimensions={0} | all-to-all | bytes 524288 | tf_op jit(solution)/shard_map/all_to_all | solution.py:436
  88.6 1.4 %attention_edges_back.1 = (f32[2,256,256]{2,1,0:T(8,128)S(1)}, bf16[128,256]{1,0:T(8,128)(2,1)S(1)}) custom-call(f32[8,16,128]{2,1,0:T(8,128)S(1)} %get-tuple-element.36.steps_ref, bf16[1024,128]{1,0:T(8,128)(2,1)S(1)} %get-tuple-element.39.q_ref, bf16[1024,256]{1,0:T(8,128)(2,1)S(1)} %get-tuple-element.44.kv_ref, ...), custom_call_target="tpu_custom_call" | custom-call | flops 167772160 | bytes 1048576 | tf_op jit(solution)/shard_map/attention_edges_back/pallas_call | solution.py:63
  90.1 3.9 %attention_interior_back.1.grads_ref = f32[1024,256]{1,0:T(8,128)S(1)} custom-call(f32[8,16,128]{2,1,0:T(8,128)S(1)} %get-tuple-element.36.steps_ref, bf16[1024,128]{1,0:T(8,128)(2,1)S(1)} %get-tuple-element.39.q_ref, bf16[1024,256]{1,0:T(8,128)(2,1)S(1)} %get-tuple-element.44.kv_ref, bf16[1024,128]{1,0:T(8,128)(2,1)S(1)} %bitcast.19, ...), custom_call_target="tpu_custom_call" | custom-call | flops 536870912 | bytes 4194304 | tf_op jit(solution)/shard_map/attention_interior_back/pallas_call | solution.py:63
  93.9 2.4 %collective-permute-done.19.from_low_ref.from_high_ref = bf16[128,256]{1,0:T(8,128)(2,1)S(1)} collective-permute-done((bf16[128,256]{1,0:T(8,128)(2,1)S(1)}, bf16[128,256]{1,0:T(8,128)(2,1)S(1)}, u32[]{:S(2)}, u32[]{:S(2)}) %collective-permute-start.19) | collective-permute-done | bytes 65568 | tf_op jit(solution)/shard_map/ppermute | solution.py:440
  96.3 2.1 %product.1 = bf16[1024,256]{1,0:T(8,128)(2,1)} custom-call(bf16[1024,1024]{1,0:T(8,128)(2,1)S(1)} %copy-done, bf16[128,256]{1,0:T(8,128)(2,1)S(1)} %collective-permute-done.19.from_low_ref.from_high_ref, bf16[128,256]{1,0:T(8,128)(2,1)S(1)} %collective-permute-done.19.from_low_ref.from_high_ref, f32[1024,256]{1,0:T(8,128)S(1)} %attention_interior_back.1.grads_ref), custom_call_target="tpu_custom_call" | custom-call | flops 1073741824 | bytes 4194304 | tf_op jit(solution)/shard_map/product/pallas_call | solution.py:63
  98.4 2.8 %all-to-all-start.3 = ((bf16[32,32,256]{2,1,0:T(8,128)(2,1)}), bf16[32,32,256]{2,1,0:T(8,128)(2,1)S(1)}, u32[]{:S(2)}, u32[]{:S(2)}) async-start(bf16[32,32,256]{2,1,0:T(8,128)(2,1)} %bitcast.11), calls=%async_computation.3 | async-start | bytes 1048576 | tf_op jit(solution)/shard_map/all_to_all | solution.py:436
  101.2 1.5 %collective-permute-start.20 = (f32[100,128]{1,0:T(8,128)S(1)}, f32[100,128]{1,0:T(8,128)S(1)}, u32[]{:S(2)}, u32[]{:S(2)}) collective-permute-start(f32[100,128]{1,0:T(8,128)S(1)} %get-tuple-element.56), channel_id=1, source_target_pairs={{0,1},{1,0},{2,3},{3,2},{4,5},{5,4},{6,7},{7,6},{8,9},{9,8},{10,11... | collective-permute-start | bytes 153608 | tf_op jit(solution)/shard_map/ppermute | solution.py:440
  102.6 4.5 %collective-permute-done.20 = f32[100,128]{1,0:T(8,128)S(1)} collective-permute-done((f32[100,128]{1,0:T(8,128)S(1)}, f32[100,128]{1,0:T(8,128)S(1)}, u32[]{:S(2)}, u32[]{:S(2)}) %collective-permute-start.20) | collective-permute-done | bytes 51232 | tf_op jit(solution)/shard_map/ppermute | solution.py:440
  107.3 0.1 fusion
  107.4 0.7 copy.10
  108.0 9.1 %all-to-all-done.3 = bf16[32,32,256]{2,1,0:T(8,128)(2,1)S(1)} async-done(((bf16[32,32,256]{2,1,0:T(8,128)(2,1)}), bf16[32,32,256]{2,1,0:T(8,128)(2,1)S(1)}, u32[]{:S(2)}, u32[]{:S(2)}) %all-to-all-start.3) | async-done | bytes 524320 | tf_op jit(solution)/shard_map/all_to_all | solution.py:436
  117.1 0.8 gather_sums.1
  (34 shorter events, 0.4 us)
Async XLA Ops:
  2.4 5.2 %collective-permute-start = (bf16[32,1152]{1,0:T(8,128)(2,1)}, bf16[32,1152]{1,0:T(8,128)(2,1)S(1)}, u32[]{:S(2)}, u32[]{:S(2)}) collective-permute-start(bf16[32,1152]{1,0:T(8,128)(2,1)} %get-tuple-element.30), channel_id=1, source_target_pairs={{0,16},{16,0},{1,17},{17,1},{2,18},{18,2},{3,19},{19,3},{4,20},{20... | collective-permute-start | bytes 221192 | tf_op jit(solution)/shard_map/ppermute | solution.py:440
  7.5 14.1 %copy-start.1 = (bf16[144,1024]{1,0:T(8,128)(2,1)S(1)}, bf16[144,1024]{1,0:T(8,128)(2,1)}, u32[]{:S(2)}) copy-start(bf16[144,1024]{1,0:T(8,128)(2,1)} %get-tuple-element.34.refs_0_) | copy-start | bytes 884740
  8.5 12.9 %collective-permute-start.3 = (bf16[2,32,1152]{2,1,0:T(8,128)(2,1)S(1)}, bf16[2,32,1152]{2,1,0:T(8,128)(2,1)S(1)}, u32[]{:S(2)}, u32[]{:S(2)}) collective-permute-start(bf16[2,32,1152]{2,1,0:T(8,128)(2,1)S(1)} %pad_maximum_fusion.1), channel_id=1, source_target_pairs={{0,1},{1,0},{2,3},{3,2},{4,5},{5,4},{6,7},{7,6},{8,9},{9,8},{10,11... | collective-permute-start | bytes 442376 | tf_op jit(solution)/shard_map/ppermute | solution.py:440
  9.8 20.5 %all-to-all-start = ((bf16[16,32,384]{2,1,0:T(8,128)(2,1)}), bf16[16,32,384]{2,1,0:T(8,128)(2,1)S(1)}, u32[]{:S(2)}, u32[]{:S(2)}) async-start(bf16[16,32,384]{2,1,0:T(8,128)(2,1)} %bitcast.27), calls=%async_computation | async-start | bytes 786432 | tf_op jit(solution)/shard_map/all_to_all | solution.py:436
  18.9 15.0 %collective-permute-start.2 = (bf16[144,1024]{1,0:T(8,128)(2,1)}, bf16[144,1024]{1,0:T(8,128)(2,1)S(1)}, u32[]{:S(2)}, u32[]{:S(2)}) collective-permute-start(bf16[144,1024]{1,0:T(8,128)(2,1)} %get-tuple-element.34.refs_0_), channel_id=1, source_target_pairs={{0,8},{4,12},{8,0},{12,4},{1,9},{5,13},{9,1},{13,5},{2,10},{6,14},... | collective-permute-start | bytes 884744 | tf_op jit(solution)/shard_map/ppermute | solution.py:440
  20.3 15.0 %collective-permute-start.1 = (bf16[144,1024]{1,0:T(8,128)(2,1)}, bf16[144,1024]{1,0:T(8,128)(2,1)S(1)}, u32[]{:S(2)}, u32[]{:S(2)}) collective-permute-start(bf16[144,1024]{1,0:T(8,128)(2,1)} %get-tuple-element.34.refs_0_), channel_id=1, source_target_pairs={{0,4},{4,0},{8,12},{12,8},{1,5},{5,1},{9,13},{13,9},{2,6},{6,2},{1... | collective-permute-start | bytes 884744 | tf_op jit(solution)/shard_map/ppermute | solution.py:440
  21.6 19.6 %collective-permute-start.4 = (bf16[144,1024]{1,0:T(8,128)(2,1)S(1)}, bf16[144,1024]{1,0:T(8,128)(2,1)S(1)}, u32[]{:S(2)}, u32[]{:S(2)}) collective-permute-start(bf16[144,1024]{1,0:T(8,128)(2,1)S(1)} %copy-done.1), channel_id=1, source_target_pairs={{0,12},{4,8},{8,4},{12,0},{1,13},{5,9},{9,5},{13,1},{2,14},{6,10},... | collective-permute-start | bytes 884744 | tf_op jit(solution)/shard_map/ppermute | solution.py:440
  30.3 16.0 %collective-permute-start.9 = (bf16[16,32,384]{2,1,0:T(8,128)(2,1)S(1)}, bf16[16,32,384]{2,1,0:T(8,128)(2,1)S(1)}, u32[]{:S(2)}, u32[]{:S(2)}) collective-permute-start(bf16[16,32,384]{2,1,0:T(8,128)(2,1)S(1)} %all-to-all-done.refs_0_), channel_id=1, source_target_pairs={{0,1},{1,0},{2,3},{3,2},{4,5},{5,4},{6,7},{7,6},{8,9},{9,8},{10,11... | collective-permute-start | bytes 1179656 | tf_op jit(solution)/shard_map/ppermute | solution.py:440
  30.6 11.5 %collective-permute-start.5 = (bf16[144,1024]{1,0:T(8,128)(2,1)S(1)}, bf16[144,1024]{1,0:T(8,128)(2,1)S(1)}, u32[]{:S(2)}, u32[]{:S(2)}) collective-permute-start(bf16[144,1024]{1,0:T(8,128)(2,1)S(1)} %copy-done.1), channel_id=1, source_target_pairs={{0,2},{2,0},{1,3},{3,1},{4,6},{6,4},{5,7},{7,5},{8,10},{10,8},{9,1... | collective-permute-start | bytes 884744 | tf_op jit(solution)/shard_map/ppermute | solution.py:440
  33.9 8.5 %collective-permute-start.7 = (bf16[144,1024]{1,0:T(8,128)(2,1)S(1)}, bf16[144,1024]{1,0:T(8,128)(2,1)S(1)}, u32[]{:S(2)}, u32[]{:S(2)}) collective-permute-start(bf16[144,1024]{1,0:T(8,128)(2,1)S(1)} %collective-permute-done.2.refs_2_), channel_id=1, source_target_pairs={{0,2},{2,0},{1,3},{3,1},{4,6},{6,4},{5,7},{7,5},{8,10},{10,8},{9,1... | collective-permute-start | bytes 884744 | tf_op jit(solution)/shard_map/ppermute | solution.py:440
  35.2 7.3 %collective-permute-start.6 = (bf16[144,1024]{1,0:T(8,128)(2,1)S(1)}, bf16[144,1024]{1,0:T(8,128)(2,1)S(1)}, u32[]{:S(2)}, u32[]{:S(2)}) collective-permute-start(bf16[144,1024]{1,0:T(8,128)(2,1)S(1)} %collective-permute-done.1.refs_1_), channel_id=1, source_target_pairs={{0,2},{2,0},{1,3},{3,1},{4,6},{6,4},{5,7},{7,5},{8,10},{10,8},{9,1... | collective-permute-start | bytes 884744 | tf_op jit(solution)/shard_map/ppermute | solution.py:440
  41.1 3.6 %collective-permute-start.8 = (bf16[144,1024]{1,0:T(8,128)(2,1)S(1)}, bf16[144,1024]{1,0:T(8,128)(2,1)S(1)}, u32[]{:S(2)}, u32[]{:S(2)}) collective-permute-start(bf16[144,1024]{1,0:T(8,128)(2,1)S(1)} %collective-permute-done.4.refs_3_), channel_id=1, source_target_pairs={{0,2},{2,0},{1,3},{3,1},{4,6},{6,4},{5,7},{7,5},{8,10},{10,8},{9,1... | collective-permute-start | bytes 884744 | tf_op jit(solution)/shard_map/ppermute | solution.py:440
  42.0 23.5 %collective-permute-start.10 = (bf16[2,64,1152]{2,1,0:T(8,128)(2,1)S(1)}, bf16[2,64,1152]{2,1,0:T(8,128)(2,1)S(1)}, u32[]{:S(2)}, u32[]{:S(2)}) collective-permute-start(bf16[2,64,1152]{2,1,0:T(8,128)(2,1)S(1)} %bitcast.21), channel_id=1, source_target_pairs={{0,4},{4,0},{8,12},{12,8},{1,5},{5,1},{9,13},{13,9},{2,6},{6,2},{1... | collective-permute-start | bytes 884744 | tf_op jit(solution)/shard_map/ppermute | solution.py:440
  42.4 23.2 %collective-permute-start.11 = (bf16[2,64,1152]{2,1,0:T(8,128)(2,1)S(1)}, bf16[2,64,1152]{2,1,0:T(8,128)(2,1)S(1)}, u32[]{:S(2)}, u32[]{:S(2)}) collective-permute-start(bf16[2,64,1152]{2,1,0:T(8,128)(2,1)S(1)} %bitcast.22), channel_id=1, source_target_pairs={{0,8},{4,12},{8,0},{12,4},{1,9},{5,13},{9,1},{13,5},{2,10},{6,14},... | collective-permute-start | bytes 884744 | tf_op jit(solution)/shard_map/ppermute | solution.py:440
  42.6 23.0 %collective-permute-start.12 = (bf16[2,64,1152]{2,1,0:T(8,128)(2,1)S(1)}, bf16[2,64,1152]{2,1,0:T(8,128)(2,1)S(1)}, u32[]{:S(2)}, u32[]{:S(2)}) collective-permute-start(bf16[2,64,1152]{2,1,0:T(8,128)(2,1)S(1)} %bitcast.23), channel_id=1, source_target_pairs={{0,12},{4,8},{8,4},{12,0},{1,13},{5,9},{9,5},{13,1},{2,14},{6,10},... | collective-permute-start | bytes 884744 | tf_op jit(solution)/shard_map/ppermute | solution.py:440
  47.6 8.8 %collective-permute-start.13 = (bf16[128,256]{1,0:T(8,128)(2,1)S(1)}, bf16[128,256]{1,0:T(8,128)(2,1)S(1)}, u32[]{:S(2)}, u32[]{:S(2)}) collective-permute-start(bf16[128,256]{1,0:T(8,128)(2,1)S(1)} %get-tuple-element.45), channel_id=1, source_target_pairs={{0,16},{16,0},{1,17},{17,1},{2,18},{18,2},{3,19},{19,3},{4,20},{20... | collective-permute-start | bytes 196616 | tf_op jit(solution)/shard_map/ppermute | solution.py:440
  49.8 16.9 %copy-start.4 = (bf16[1,64,1024]{2,1,0:T(8,128)(2,1)S(1)}, bf16[1,64,1024]{2,1,0:T(8,128)(2,1)}, u32[]{:S(2)}) copy-start(bf16[1,64,1024]{2,1,0:T(8,128)(2,1)} %get-tuple-element.51) | copy-start | bytes 393220
  57.8 15.8 %all-to-all-start.1 = ((bf16[16,64,128]{2,1,0:T(8,128)(2,1)}), bf16[16,64,128]{2,1,0:T(8,128)(2,1)S(1)}, u32[]{:S(2)}, u32[]{:S(2)}) async-start(bf16[16,64,128]{2,1,0:T(8,128)(2,1)} %bitcast.7), calls=%async_computation.1 | async-start | bytes 524288 | tf_op jit(solution)/shard_map/all_to_all | solution.py:436
  65.6 8.1 %copy-start.2 = (bf16[1,64,1024]{2,1,0:T(8,128)(2,1)S(1)}, bf16[1,64,1024]{2,1,0:T(8,128)(2,1)}, u32[]{:S(2)}) copy-start(bf16[1,64,1024]{2,1,0:T(8,128)(2,1)} %get-tuple-element.50.refs_0_) | copy-start | bytes 393220
  65.6 8.1 %copy-start.3 = (f32[128]{0:T(128)S(1)}, f32[128]{0:T(128)}, u32[]{:S(2)}) copy-start(f32[128]{0:T(128)} %param.12) | copy-start | bytes 1540
  65.6 2.5 %collective-permute-start.14 = (bf16[2,64,1152]{2,1,0:T(8,128)(2,1)S(1)}, bf16[2,64,1152]{2,1,0:T(8,128)(2,1)S(1)}, u32[]{:S(2)}, u32[]{:S(2)}) collective-permute-start(bf16[2,64,1152]{2,1,0:T(8,128)(2,1)S(1)} %bitcast.24), channel_id=1, source_target_pairs={{0,2},{2,0},{1,3},{3,1},{4,6},{6,4},{5,7},{7,5},{8,10},{10,8},{9,1... | collective-permute-start | bytes 884744 | tf_op jit(solution)/shard_map/ppermute | solution.py:440
  65.8 2.3 %collective-permute-start.15 = (bf16[2,64,1152]{2,1,0:T(8,128)(2,1)S(1)}, bf16[2,64,1152]{2,1,0:T(8,128)(2,1)S(1)}, u32[]{:S(2)}, u32[]{:S(2)}) collective-permute-start(bf16[2,64,1152]{2,1,0:T(8,128)(2,1)S(1)} %collective-permute-done.10.refs_1_), channel_id=1, source_target_pairs={{0,2},{2,0},{1,3},{3,1},{4,6},{6,4},{5,7},{7,5},{8,10},{10,8},{9,1... | collective-permute-start | bytes 884744 | tf_op jit(solution)/shard_map/ppermute | solution.py:440
  66.2 1.9 %collective-permute-start.16 = (bf16[2,64,1152]{2,1,0:T(8,128)(2,1)S(1)}, bf16[2,64,1152]{2,1,0:T(8,128)(2,1)S(1)}, u32[]{:S(2)}, u32[]{:S(2)}) collective-permute-start(bf16[2,64,1152]{2,1,0:T(8,128)(2,1)S(1)} %collective-permute-done.11.refs_2_), channel_id=1, source_target_pairs={{0,2},{2,0},{1,3},{3,1},{4,6},{6,4},{5,7},{7,5},{8,10},{10,8},{9,1... | collective-permute-start | bytes 884744 | tf_op jit(solution)/shard_map/ppermute | solution.py:440
  66.3 2.2 %collective-permute-start.17 = (bf16[2,64,1152]{2,1,0:T(8,128)(2,1)S(1)}, bf16[2,64,1152]{2,1,0:T(8,128)(2,1)S(1)}, u32[]{:S(2)}, u32[]{:S(2)}) collective-permute-start(bf16[2,64,1152]{2,1,0:T(8,128)(2,1)S(1)} %collective-permute-done.12.refs_3_), channel_id=1, source_target_pairs={{0,2},{2,0},{1,3},{3,1},{4,6},{6,4},{5,7},{7,5},{8,10},{10,8},{9,1... | collective-permute-start | bytes 884744 | tf_op jit(solution)/shard_map/ppermute | solution.py:440
  66.7 6.9 %collective-permute-start.18 = (bf16[1,64,1024]{2,1,0:T(8,128)(2,1)S(1)}, bf16[1,64,1024]{2,1,0:T(8,128)(2,1)S(1)}, u32[]{:S(2)}, u32[]{:S(2)}) collective-permute-start(bf16[1,64,1024]{2,1,0:T(8,128)(2,1)S(1)} %copy-done.4), channel_id=1, source_target_pairs={{0,1},{1,0},{2,3},{3,2},{4,5},{5,4},{6,7},{7,6},{8,9},{9,8},{10,11... | collective-permute-start | bytes 393224 | tf_op jit(solution)/shard_map/ppermute | solution.py:440
  77.4 18.9 %copy-start = (bf16[1024,1024]{1,0:T(8,128)(2,1)S(1)}, bf16[1024,1024]{1,0:T(8,128)(2,1)}, u32[]{:S(2)}) copy-start(bf16[1024,1024]{1,0:T(8,128)(2,1)} %get-tuple-element.35.normed_any.normed_ref) | copy-start | bytes 6291460
  90.0 6.3 %collective-permute-start.19 = (bf16[128,256]{1,0:T(8,128)(2,1)S(1)}, bf16[128,256]{1,0:T(8,128)(2,1)S(1)}, u32[]{:S(2)}, u32[]{:S(2)}) collective-permute-start(bf16[128,256]{1,0:T(8,128)(2,1)S(1)} %get-tuple-element.53), channel_id=1, source_target_pairs={{0,16},{16,0},{1,17},{17,1},{2,18},{18,2},{3,19},{19,3},{4,20},{20... | collective-permute-start | bytes 196616 | tf_op jit(solution)/shard_map/ppermute | solution.py:440
  98.4 18.7 %all-to-all-start.3 = ((bf16[32,32,256]{2,1,0:T(8,128)(2,1)}), bf16[32,32,256]{2,1,0:T(8,128)(2,1)S(1)}, u32[]{:S(2)}, u32[]{:S(2)}) async-start(bf16[32,32,256]{2,1,0:T(8,128)(2,1)} %bitcast.11), calls=%async_computation.3 | async-start | bytes 1048576 | tf_op jit(solution)/shard_map/all_to_all | solution.py:436
  101.2 6.0 %collective-permute-start.20 = (f32[100,128]{1,0:T(8,128)S(1)}, f32[100,128]{1,0:T(8,128)S(1)}, u32[]{:S(2)}, u32[]{:S(2)}) collective-permute-start(f32[100,128]{1,0:T(8,128)S(1)} %get-tuple-element.56), channel_id=1, source_target_pairs={{0,1},{1,0},{2,3},{3,2},{4,5},{5,4},{6,7},{7,6},{8,9},{9,8},{10,11... | collective-permute-start | bytes 153608 | tf_op jit(solution)/shard_map/ppermute | solution.py:440

commit v13 on v10

--- a/solution.py
+++ b/solution.py
@@ -519,11 +519,6 @@
     )(*near, *far)
 
     packed = in_order(packed, "ens", 1).reshape(halves, members_num * shard, width)
-    if paired:
-        sources = [sources[0], swap(sources[1], "ens", 1)]
-        columns[1], sources[1] = lax.optimization_barrier((columns[1], sources[1]))
-    else:
-        sources = [exchange(sources[0], "ens")]
     packed, near[2] = lax.optimization_barrier((packed, near[2]))
     pieces = [packed] + [swap(packed, "quad", step) for step in range(1, QUAD)]
 
@@ -545,6 +540,8 @@
             return got, got
         return lax.ppermute(inner[1], "half", up), lax.ppermute(inner[0], "half", down)
 
+    weights, sources[-1] = lax.optimization_barrier((weights, sources[-1]))
+    sources = [sources[0], swap(sources[1], "ens", 1)] if paired else [exchange(sources[0], "ens")]
     low, high = across(inner)
     queries, own = call(
         project_kernel,

time: 117 us -> 110 us (0.940)
  waiting for transfers between devices: 43.9 us -> 33.9 us
  starting transfers between devices: 33.7 us -> 36.1 us
  blocking collectives: 9.89 us -> 11.2 us
    ppermute x21, waiting for transfers between devices: 26.6 us -> 18.9 us  [swap(): lax.ppermute(value, axis, [(i, i ^ step) for i in range(lax.axis_size(axi...]
    ppermute x21, starting transfers between devices: 18.7 us -> 22.7 us  [swap(): lax.ppermute(value, axis, [(i, i ^ step) for i in range(lax.axis_size(axi...]
    all_to_all x3, waiting for transfers between devices: 17.3 us -> 15 us  [exchange(): return lax.all_to_all(chunks, axes, 0, 0)]
    all_to_all x3, starting transfers between devices: 14.9 us -> 13.4 us  [exchange(): return lax.all_to_all(chunks, axes, 0, 0)]
    all_to_all x1, blocking collectives: 9.89 us -> 11.2 us  [exchange(): return lax.all_to_all(chunks, axes, 0, 0)]
  transfers between devices with their start and end apart: 24 -> 24, of which waited for: 12 -> 8; matrix products, arithmetic and copies ran while one was open for 2% -> 2% of each run, Pallas kernels for 14% -> 15%
where the time goes in v13:
time: 110 us
  starting transfers between devices  36.1 us (33%)
  waiting for transfers between devices  33.9 us (31%)
  Pallas kernels  25.9 us (24%)
  blocking collectives  11.2 us (10%)
  other arithmetic  1.13 us (1%)
    pallas_call x13, Pallas kernels, run(): made(*[pltpu.with_memory_space_constraint(arg, pltpu.HBM) if space == 'h'...  25.9 us
    ppermute x21, starting transfers between devices, swap(): lax.ppermute(value, axis, [(i, i ^ step) for i in range(lax.axis_size(axi...  22.7 us
    ppermute x21, waiting for transfers between devices, swap(): lax.ppermute(value, axis, [(i, i ^ step) for i in range(lax.axis_size(axi...  18.9 us
    all_to_all x3, waiting for transfers between devices, exchange(): return lax.all_to_all(chunks, axes, 0, 0)  15 us
    all_to_all x3, starting transfers between devices, exchange(): return lax.all_to_all(chunks, axes, 0, 0)  13.4 us
    all_to_all x1, blocking collectives, exchange(): return lax.all_to_all(chunks, axes, 0, 0)  11.2 us
  transfers between devices with their start and end apart: 24, of which 8 were waited for; matrix products, arithmetic and copies ran while one was open for 2% of the time, Pallas kernels for 15%

profile of v13, /device:TPU:1, one launch (start us, length us, event | category | flops | bytes accessed | tf_op | source)
XLA Modules:
  0.0 109.9 jit_solution(13701870297894029906)
XLA Ops:
  0.6 1.8 %prepare_weights.1 = (bf16[2,8,1,32,384]{4,3,2,1,0:T(8,128)(2,1)}, bf16[32,1152]{1,0:T(8,128)(2,1)}) custom-call(bf16[32,3072]{1,0:T(8,128)(2,1)} %w_any.1, bf16[32,1024]{1,0:T(8,128)(2,1)} %mix_any.1, bf16[32,100]{1,0:T(8,128)(2,1)} %readout_any.1), custom_call_target="tpu_custom_call" | custom-call | bytes 1048576 | tf_op jit(solution)/shard_map/prepare_weights/pallas_call | solution.py:63
  2.4 3.2 %collective-permute-start = (bf16[32,1152]{1,0:T(8,128)(2,1)}, bf16[32,1152]{1,0:T(8,128)(2,1)S(1)}, u32[]{:S(2)}, u32[]{:S(2)}) collective-permute-start(bf16[32,1152]{1,0:T(8,128)(2,1)} %get-tuple-element.31), channel_id=1, source_target_pairs={{0,16},{16,0},{1,17},{17,1},{2,18},{18,2},{3,19},{19,3},{4,20},{20... | collective-permute-start | bytes 221192 | tf_op jit(solution)/shard_map/ppermute | solution.py:440
  5.6 4.8 %all-to-all-start = ((bf16[16,32,384]{2,1,0:T(8,128)(2,1)}), bf16[16,32,384]{2,1,0:T(8,128)(2,1)S(1)}, u32[]{:S(2)}, u32[]{:S(2)}) async-start(bf16[16,32,384]{2,1,0:T(8,128)(2,1)} %bitcast.27), calls=%async_computation | async-start | bytes 786432 | tf_op jit(solution)/shard_map/all_to_all | solution.py:436
  10.4 1.9 %norm.1 = (bf16[144,1024]{1,0:T(8,128)(2,1)}, bf16[1,64,1024]{2,1,0:T(8,128)(2,1)}, bf16[1,64,1024]{2,1,0:T(8,128)(2,1)}) custom-call(s32[2,4]{1,0:T(2,128)} %near_any.1, bf16[128,1024]{1,0:T(8,128)(2,1)} %bitcast.28), custom_call_target="tpu_custom_call" | custom-call | flops 1048576 | bytes 1048576 | tf_op jit(solution)/shard_map/norm/pallas_call | solution.py:63
  12.3 0.9 select_bitcast_fusion.3
  13.3 1.5 %collective-permute-start.1 = (bf16[144,1024]{1,0:T(8,128)(2,1)}, bf16[144,1024]{1,0:T(8,128)(2,1)S(1)}, u32[]{:S(2)}, u32[]{:S(2)}) collective-permute-start(bf16[144,1024]{1,0:T(8,128)(2,1)} %get-tuple-element.35.refs_0_), channel_id=1, source_target_pairs={{0,4},{4,0},{8,12},{12,8},{1,5},{5,1},{9,13},{13,9},{2,6},{6,2},{1... | collective-permute-start | bytes 884744 | tf_op jit(solution)/shard_map/ppermute | solution.py:440
  14.7 1.2 %collective-permute-start.3 = (bf16[144,1024]{1,0:T(8,128)(2,1)}, bf16[144,1024]{1,0:T(8,128)(2,1)S(1)}, u32[]{:S(2)}, u32[]{:S(2)}) collective-permute-start(bf16[144,1024]{1,0:T(8,128)(2,1)} %get-tuple-element.35.refs_0_), channel_id=1, source_target_pairs={{0,12},{4,8},{8,4},{12,0},{1,13},{5,9},{9,5},{13,1},{2,14},{6,10},... | collective-permute-start | bytes 884744 | tf_op jit(solution)/shard_map/ppermute | solution.py:440
  15.9 5.9 %all-to-all-done.refs_0_ = bf16[16,32,384]{2,1,0:T(8,128)(2,1)S(1)} async-done(((bf16[16,32,384]{2,1,0:T(8,128)(2,1)}), bf16[16,32,384]{2,1,0:T(8,128)(2,1)S(1)}, u32[]{:S(2)}, u32[]{:S(2)}) %all-to-all-start) | async-done | bytes 393248 | tf_op jit(solution)/shard_map/all_to_all | solution.py:436
  21.8 1.7 %collective-permute-start.2 = (bf16[144,1024]{1,0:T(8,128)(2,1)}, bf16[144,1024]{1,0:T(8,128)(2,1)S(1)}, u32[]{:S(2)}, u32[]{:S(2)}) collective-permute-start(bf16[144,1024]{1,0:T(8,128)(2,1)} %get-tuple-element.35.refs_0_), channel_id=1, source_target_pairs={{0,8},{4,12},{8,0},{12,4},{1,9},{5,13},{9,1},{13,5},{2,10},{6,14},... | collective-permute-start | bytes 884744 | tf_op jit(solution)/shard_map/ppermute | solution.py:440
  23.6 1.2 %collective-permute-start.9 = (bf16[2,32,1152]{2,1,0:T(8,128)(2,1)S(1)}, bf16[2,32,1152]{2,1,0:T(8,128)(2,1)S(1)}, u32[]{:S(2)}, u32[]{:S(2)}) collective-permute-start(bf16[2,32,1152]{2,1,0:T(8,128)(2,1)S(1)} %pad_maximum_fusion.1), channel_id=1, source_target_pairs={{0,1},{1,0},{2,3},{3,2},{4,5},{5,4},{6,7},{7,6},{8,9},{9,8},{10,11... | collective-permute-start | bytes 442376 | tf_op jit(solution)/shard_map/ppermute | solution.py:440
  24.8 0.2 collective-permute-start.4
  25.0 5.3 %collective-permute-done.1.refs_1_ = bf16[144,1024]{1,0:T(8,128)(2,1)S(1)} collective-permute-done((bf16[144,1024]{1,0:T(8,128)(2,1)}, bf16[144,1024]{1,0:T(8,128)(2,1)S(1)}, u32[]{:S(2)}, u32[]{:S(2)}) %collective-permute-start.1) | collective-permute-done | bytes 294944 | tf_op jit(solution)/shard_map/ppermute | solution.py:440
  30.3 0.9 collective-permute-start.5
  31.2 1.3 %collective-permute-start.8 = (bf16[16,32,384]{2,1,0:T(8,128)(2,1)S(1)}, bf16[16,32,384]{2,1,0:T(8,128)(2,1)S(1)}, u32[]{:S(2)}, u32[]{:S(2)}) collective-permute-start(bf16[16,32,384]{2,1,0:T(8,128)(2,1)S(1)} %all-to-all-done.refs_0_), channel_id=1, source_target_pairs={{0,1},{1,0},{2,3},{3,2},{4,5},{5,4},{6,7},{7,6},{8,9},{9,8},{10,11... | collective-permute-start | bytes 1179656 | tf_op jit(solution)/shard_map/ppermute | solution.py:440
  32.5 0.7 collective-permute-start.6
  33.3 1.3 %collective-permute-start.10 = (bf16[2,64,1152]{2,1,0:T(8,128)(2,1)S(1)}, bf16[2,64,1152]{2,1,0:T(8,128)(2,1)S(1)}, u32[]{:S(2)}, u32[]{:S(2)}) collective-permute-start(bf16[2,64,1152]{2,1,0:T(8,128)(2,1)S(1)} %bitcast.21), channel_id=1, source_target_pairs={{0,4},{4,0},{8,12},{12,8},{1,5},{5,1},{9,13},{13,9},{2,6},{6,2},{1... | collective-permute-start | bytes 884744 | tf_op jit(solution)/shard_map/ppermute | solution.py:440
  34.7 1.2 %collective-permute-start.11 = (bf16[2,64,1152]{2,1,0:T(8,128)(2,1)S(1)}, bf16[2,64,1152]{2,1,0:T(8,128)(2,1)S(1)}, u32[]{:S(2)}, u32[]{:S(2)}) collective-permute-start(bf16[2,64,1152]{2,1,0:T(8,128)(2,1)S(1)} %bitcast.22), channel_id=1, source_target_pairs={{0,8},{4,12},{8,0},{12,4},{1,9},{5,13},{9,1},{13,5},{2,10},{6,14},... | collective-permute-start | bytes 884744 | tf_op jit(solution)/shard_map/ppermute | solution.py:440
  35.8 0.5 collective-permute-start.12
  36.3 1.5 %collect.1 = (bf16[1024,1024]{1,0:T(8,128)(2,1)}, f32[8,16,128]{2,1,0:T(8,128)S(1)}) custom-call(bf16[144,1024]{1,0:T(8,128)(2,1)S(1)} %copy-done.1, bf16[144,1024]{1,0:T(8,128)(2,1)S(1)} %collective-permute-done.1.refs_1_, bf16[144,1024]{1,0:T(8,128)(2,1)S(1)} %collective-permute-done.2.refs_2_, bf16[144,1024]{1,0:T(8,128)(2,1)S(1)} %collective-permute-done.3.refs_3_, ...), custom_call_target="tpu_custom_call" | custom-call | bytes 4194304 | tf_op jit(solution)/shard_map/collect/pallas_call | solution.py:63
  37.8 3.7 %collective-permute-done.8.refs_1_ = bf16[16,32,384]{2,1,0:T(8,128)(2,1)S(1)} collective-permute-done((bf16[16,32,384]{2,1,0:T(8,128)(2,1)S(1)}, bf16[16,32,384]{2,1,0:T(8,128)(2,1)S(1)}, u32[]{:S(2)}, u32[]{:S(2)}) %collective-permute-start.8) | collective-permute-done | bytes 393248 | tf_op jit(solution)/shard_map/ppermute | solution.py:440
  41.5 1.3 %project_rims.1 = (bf16[16,2,32,384]{3,2,1,0:T(8,128)(2,1)S(1)}, bf16[128,256]{1,0:T(8,128)(2,1)S(1)}) custom-call(bf16[1024,1024]{1,0:T(8,128)(2,1)} %get-tuple-element.36.normed_any.normed_ref, bf16[16,32,384]{2,1,0:T(8,128)(2,1)S(1)} %all-to-all-done.refs_0_, bf16[16,32,384]{2,1,0:T(8,128)(2,1)S(1)} %collective-permute-done.8.refs_1_), custom_call_target="tpu_custom_call" | custom-call | flops 67108864 | bytes 1048576 | tf_op jit(solution)/shard_map/project_rims/pallas_call | solution.py:63
  42.8 2.7 %collective-permute-start.13 = (bf16[128,256]{1,0:T(8,128)(2,1)S(1)}, bf16[128,256]{1,0:T(8,128)(2,1)S(1)}, u32[]{:S(2)}, u32[]{:S(2)}) collective-permute-start(bf16[128,256]{1,0:T(8,128)(2,1)S(1)} %get-tuple-element.47), channel_id=1, source_target_pairs={{0,16},{16,0},{1,17},{17,1},{2,18},{18,2},{3,19},{19,3},{4,20},{20... | collective-permute-start | bytes 196616 | tf_op jit(solution)/shard_map/ppermute | solution.py:440
  45.5 2.8 %project.1 = (bf16[1024,128]{1,0:T(8,128)(2,1)S(1)}, bf16[1024,256]{1,0:T(8,128)(2,1)S(1)}) custom-call(bf16[1024,1024]{1,0:T(8,128)(2,1)} %get-tuple-element.36.normed_any.normed_ref, bf16[16,2,32,384]{3,2,1,0:T(8,128)(2,1)S(1)} %get-tuple-element.41.w_ref), custom_call_target="tpu_custom_call" | custom-call | flops 805306368 | bytes 4194304 | tf_op jit(solution)/shard_map/project/pallas_call | solution.py:63
  48.4 1.9 %attention_interior.1.done_ref = bf16[1024,128]{1,0:T(8,128)(2,1)S(1)} custom-call(f32[8,16,128]{2,1,0:T(8,128)S(1)} %get-tuple-element.37.steps_ref, bf16[1024,128]{1,0:T(8,128)(2,1)S(1)} %get-tuple-element.42.q_ref, bf16[1024,256]{1,0:T(8,128)(2,1)S(1)} %get-tuple-element.46.kv_ref), custom_call_target="tpu_custom_call" | custom-call | flops 268435456 | bytes 2097152 | tf_op jit(solution)/shard_map/attention_interior/pallas_call | solution.py:63
  50.3 1.4 %attention_edges.1 = bf16[1024,128]{1,0:T(8,128)(2,1)} custom-call(f32[8,16,128]{2,1,0:T(8,128)S(1)} %get-tuple-element.37.steps_ref, bf16[1024,128]{1,0:T(8,128)(2,1)S(1)} %get-tuple-element.42.q_ref, bf16[1024,256]{1,0:T(8,128)(2,1)S(1)} %get-tuple-element.46.kv_ref, bf16[128,256]{1,0:T(8,128)(2,1)S(1)} %collective-permute-done.13.low_ref.high_ref, ...), custom_call_target="tpu_custom_call" | custom-call | flops 67108864 | bytes 1048576 | tf_op jit(solution)/shard_map/attention_edges/pallas_call | solution.py:63
  51.7 5.9 %all-to-all-start.1 = ((bf16[16,64,128]{2,1,0:T(8,128)(2,1)}), bf16[16,64,128]{2,1,0:T(8,128)(2,1)S(1)}, u32[]{:S(2)}, u32[]{:S(2)}) async-start(bf16[16,64,128]{2,1,0:T(8,128)(2,1)} %bitcast.7), calls=%async_computation.1 | async-start | bytes 524288 | tf_op jit(solution)/shard_map/all_to_all | solution.py:436
  57.6 0.2 collective-permute-start.14
  57.8 0.4 collective-permute-start.15
  58.2 0.1 collective-permute-start.16
  58.3 0.4 collective-permute-start.17
  58.7 1.4 %collective-permute-start.18 = (bf16[1,64,1024]{2,1,0:T(8,128)(2,1)S(1)}, bf16[1,64,1024]{2,1,0:T(8,128)(2,1)S(1)}, u32[]{:S(2)}, u32[]{:S(2)}) collective-permute-start(bf16[1,64,1024]{2,1,0:T(8,128)(2,1)S(1)} %copy-done.4), channel_id=1, source_target_pairs={{0,1},{1,0},{2,3},{3,2},{4,5},{5,4},{6,7},{7,6},{8,9},{9,8},{10,11... | collective-permute-start | bytes 393224 | tf_op jit(solution)/shard_map/ppermute | solution.py:440
  60.1 0.4 collective-permute-done.17.refs_7_
  60.5 1.5 %assemble.1.w_any = bf16[2,4,2,64,1152]{4,3,2,1,0:T(8,128)(2,1)} custom-call(bf16[2,64,1152]{2,1,0:T(8,128)(2,1)S(1)} %bitcast.25, bf16[2,64,1152]{2,1,0:T(8,128)(2,1)S(1)} %collective-permute-done.10.refs_1_, bf16[2,64,1152]{2,1,0:T(8,128)(2,1)S(1)} %collective-permute-done.11.refs_2_, bf16[2,64,1152]{2,1,0:T(8,128)(2,1)S(1)} %collective-permute-done.12.refs_3_, ...), custom_call_target="tpu_custom_call" | custom-call | bytes 4194304 | tf_op jit(solution)/shard_map/assemble/pallas_call | solution.py:63
  62.0 3.6 %collective-permute-done.18.refs_1_ = bf16[1,64,1024]{2,1,0:T(8,128)(2,1)S(1)} collective-permute-done((bf16[1,64,1024]{2,1,0:T(8,128)(2,1)S(1)}, bf16[1,64,1024]{2,1,0:T(8,128)(2,1)S(1)}, u32[]{:S(2)}, u32[]{:S(2)}) %collective-permute-start.18) | collective-permute-done | bytes 131104 | tf_op jit(solution)/shard_map/ppermute | solution.py:440
  65.7 3.7 %mix_loss_backward.1 = (f32[100,128]{1,0:T(8,128)S(1)}, bf16[16,64,128]{2,1,0:T(8,128)(2,1)S(1)}) custom-call(bf16[16,64,128]{2,1,0:T(8,128)(2,1)S(1)} %all-to-all-done.1.att_ref, f32[1,128]{1,0:T(1,128)S(1)} %bitcast.26, f32[100,128]{1,0:T(8,128)} %truth_any.1, bf16[2,4,2,64,1152]{4,3,2,1,0:T(8,128)(2,1)} %assemble.1.w_any, ...), custom_call_target="tpu_custom_call" | custom-call | flops 603979776 | bytes 4194304 | tf_op jit(solution)/shard_map/mix_loss_backward/pallas_call | solution.py:63
  69.4 11.2 %all_to_all.20 = bf16[16,64,128]{2,1,0:T(8,128)(2,1)S(1)} all-to-all(bf16[16,64,128]{2,1,0:T(8,128)(2,1)S(1)} %get-tuple-element.54), channel_id=1, replica_groups=mesh['half'=2,'quad'=4,'core'=2,'ens'=2] {'quad','core','ens'}, dimensions={0} | all-to-all | bytes 524288 | tf_op jit(solution)/shard_map/all_to_all | solution.py:436
  80.6 1.4 %attention_edges_back.1 = (f32[2,256,256]{2,1,0:T(8,128)S(1)}, bf16[128,256]{1,0:T(8,128)(2,1)S(1)}) custom-call(f32[8,16,128]{2,1,0:T(8,128)S(1)} %get-tuple-element.37.steps_ref, bf16[1024,128]{1,0:T(8,128)(2,1)S(1)} %get-tuple-element.42.q_ref, bf16[1024,256]{1,0:T(8,128)(2,1)S(1)} %get-tuple-element.46.kv_ref, ...), custom_call_target="tpu_custom_call" | custom-call | flops 167772160 | bytes 1048576 | tf_op jit(solution)/shard_map/attention_edges_back/pallas_call | solution.py:63
  82.0 1.2 %collective-permute-start.19 = (bf16[128,256]{1,0:T(8,128)(2,1)S(1)}, bf16[128,256]{1,0:T(8,128)(2,1)S(1)}, u32[]{:S(2)}, u32[]{:S(2)}) collective-permute-start(bf16[128,256]{1,0:T(8,128)(2,1)S(1)} %get-tuple-element.55), channel_id=1, source_target_pairs={{0,16},{16,0},{1,17},{17,1},{2,18},{18,2},{3,19},{19,3},{4,20},{20... | collective-permute-start | bytes 196616 | tf_op jit(solution)/shard_map/ppermute | solution.py:440
  83.2 3.9 %attention_interior_back.1.grads_ref = f32[1024,256]{1,0:T(8,128)S(1)} custom-call(f32[8,16,128]{2,1,0:T(8,128)S(1)} %get-tuple-element.37.steps_ref, bf16[1024,128]{1,0:T(8,128)(2,1)S(1)} %get-tuple-element.42.q_ref, bf16[1024,256]{1,0:T(8,128)(2,1)S(1)} %get-tuple-element.46.kv_ref, bf16[1024,128]{1,0:T(8,128)(2,1)S(1)} %bitcast.19, ...), custom_call_target="tpu_custom_call" | custom-call | flops 536870912 | bytes 4194304 | tf_op jit(solution)/shard_map/attention_interior_back/pallas_call | solution.py:63
  87.1 1.3 %collective-permute-done.19.from_low_ref.from_high_ref = bf16[128,256]{1,0:T(8,128)(2,1)S(1)} collective-permute-done((bf16[128,256]{1,0:T(8,128)(2,1)S(1)}, bf16[128,256]{1,0:T(8,128)(2,1)S(1)}, u32[]{:S(2)}, u32[]{:S(2)}) %collective-permute-start.19) | collective-permute-done | bytes 65568 | tf_op jit(solution)/shard_map/ppermute | solution.py:440
  88.3 2.1 %product.1 = bf16[1024,256]{1,0:T(8,128)(2,1)} custom-call(bf16[1024,1024]{1,0:T(8,128)(2,1)S(1)} %copy-done, bf16[128,256]{1,0:T(8,128)(2,1)S(1)} %collective-permute-done.19.from_low_ref.from_high_ref, bf16[128,256]{1,0:T(8,128)(2,1)S(1)} %collective-permute-done.19.from_low_ref.from_high_ref, f32[1024,256]{1,0:T(8,128)S(1)} %attention_interior_back.1.grads_ref), custom_call_target="tpu_custom_call" | custom-call | flops 1073741824 | bytes 4194304 | tf_op jit(solution)/shard_map/product/pallas_call | solution.py:63
  90.4 2.8 %all-to-all-start.3 = ((bf16[32,32,256]{2,1,0:T(8,128)(2,1)}), bf16[32,32,256]{2,1,0:T(8,128)(2,1)S(1)}, u32[]{:S(2)}, u32[]{:S(2)}) async-start(bf16[32,32,256]{2,1,0:T(8,128)(2,1)} %bitcast.11), calls=%async_computation.3 | async-start | bytes 1048576 | tf_op jit(solution)/shard_map/all_to_all | solution.py:436
  93.2 1.5 %collective-permute-start.20 = (f32[100,128]{1,0:T(8,128)S(1)}, f32[100,128]{1,0:T(8,128)S(1)}, u32[]{:S(2)}, u32[]{:S(2)}) collective-permute-start(f32[100,128]{1,0:T(8,128)S(1)} %get-tuple-element.58), channel_id=1, source_target_pairs={{0,1},{1,0},{2,3},{3,2},{4,5},{5,4},{6,7},{7,6},{8,9},{9,8},{10,11... | collective-permute-start | bytes 153608 | tf_op jit(solution)/shard_map/ppermute | solution.py:440
  94.6 4.5 %collective-permute-done.20 = f32[100,128]{1,0:T(8,128)S(1)} collective-permute-done((f32[100,128]{1,0:T(8,128)S(1)}, f32[100,128]{1,0:T(8,128)S(1)}, u32[]{:S(2)}, u32[]{:S(2)}) %collective-permute-start.20) | collective-permute-done | bytes 51232 | tf_op jit(solution)/shard_map/ppermute | solution.py:440
  99.3 0.1 fusion
  99.4 0.7 copy.10
  100.0 9.1 %all-to-all-done.3 = bf16[32,32,256]{2,1,0:T(8,128)(2,1)S(1)} async-done(((bf16[32,32,256]{2,1,0:T(8,128)(2,1)}), bf16[32,32,256]{2,1,0:T(8,128)(2,1)S(1)}, u32[]{:S(2)}, u32[]{:S(2)}) %all-to-all-start.3) | async-done | bytes 524320 | tf_op jit(solution)/shard_map/all_to_all | solution.py:436
  109.1 0.8 gather_sums.1
  (34 shorter events, 0.3 us)
Async XLA Ops:
  2.4 9.9 %collective-permute-start = (bf16[32,1152]{1,0:T(8,128)(2,1)}, bf16[32,1152]{1,0:T(8,128)(2,1)S(1)}, u32[]{:S(2)}, u32[]{:S(2)}) collective-permute-start(bf16[32,1152]{1,0:T(8,128)(2,1)} %get-tuple-element.31), channel_id=1, source_target_pairs={{0,16},{16,0},{1,17},{17,1},{2,18},{18,2},{3,19},{19,3},{4,20},{20... | collective-permute-start | bytes 221192 | tf_op jit(solution)/shard_map/ppermute | solution.py:440
  5.6 16.2 %all-to-all-start = ((bf16[16,32,384]{2,1,0:T(8,128)(2,1)}), bf16[16,32,384]{2,1,0:T(8,128)(2,1)S(1)}, u32[]{:S(2)}, u32[]{:S(2)}) async-start(bf16[16,32,384]{2,1,0:T(8,128)(2,1)} %bitcast.27), calls=%async_computation | async-start | bytes 786432 | tf_op jit(solution)/shard_map/all_to_all | solution.py:436
  12.3 24.0 %copy-start.1 = (bf16[144,1024]{1,0:T(8,128)(2,1)S(1)}, bf16[144,1024]{1,0:T(8,128)(2,1)}, u32[]{:S(2)}) copy-start(bf16[144,1024]{1,0:T(8,128)(2,1)} %get-tuple-element.35.refs_0_) | copy-start | bytes 884740
  13.3 17.0 %collective-permute-start.1 = (bf16[144,1024]{1,0:T(8,128)(2,1)}, bf16[144,1024]{1,0:T(8,128)(2,1)S(1)}, u32[]{:S(2)}, u32[]{:S(2)}) collective-permute-start(bf16[144,1024]{1,0:T(8,128)(2,1)} %get-tuple-element.35.refs_0_), channel_id=1, source_target_pairs={{0,4},{4,0},{8,12},{12,8},{1,5},{5,1},{9,13},{13,9},{2,6},{6,2},{1... | collective-permute-start | bytes 884744 | tf_op jit(solution)/shard_map/ppermute | solution.py:440
  14.7 16.4 %collective-permute-start.3 = (bf16[144,1024]{1,0:T(8,128)(2,1)}, bf16[144,1024]{1,0:T(8,128)(2,1)S(1)}, u32[]{:S(2)}, u32[]{:S(2)}) collective-permute-start(bf16[144,1024]{1,0:T(8,128)(2,1)} %get-tuple-element.35.refs_0_), channel_id=1, source_target_pairs={{0,12},{4,8},{8,4},{12,0},{1,13},{5,9},{9,5},{13,1},{2,14},{6,10},... | collective-permute-start | bytes 884744 | tf_op jit(solution)/shard_map/ppermute | solution.py:440
  21.8 10.6 %collective-permute-start.2 = (bf16[144,1024]{1,0:T(8,128)(2,1)}, bf16[144,1024]{1,0:T(8,128)(2,1)S(1)}, u32[]{:S(2)}, u32[]{:S(2)}) collective-permute-start(bf16[144,1024]{1,0:T(8,128)(2,1)} %get-tuple-element.35.refs_0_), channel_id=1, source_target_pairs={{0,8},{4,12},{8,0},{12,4},{1,9},{5,13},{9,1},{13,5},{2,10},{6,14},... | collective-permute-start | bytes 884744 | tf_op jit(solution)/shard_map/ppermute | solution.py:440
  23.6 7.6 %collective-permute-start.9 = (bf16[2,32,1152]{2,1,0:T(8,128)(2,1)S(1)}, bf16[2,32,1152]{2,1,0:T(8,128)(2,1)S(1)}, u32[]{:S(2)}, u32[]{:S(2)}) collective-permute-start(bf16[2,32,1152]{2,1,0:T(8,128)(2,1)S(1)} %pad_maximum_fusion.1), channel_id=1, source_target_pairs={{0,1},{1,0},{2,3},{3,2},{4,5},{5,4},{6,7},{7,6},{8,9},{9,8},{10,11... | collective-permute-start | bytes 442376 | tf_op jit(solution)/shard_map/ppermute | solution.py:440
  24.8 8.5 %collective-permute-start.4 = (bf16[144,1024]{1,0:T(8,128)(2,1)}, bf16[144,1024]{1,0:T(8,128)(2,1)S(1)}, u32[]{:S(2)}, u32[]{:S(2)}) collective-permute-start(bf16[144,1024]{1,0:T(8,128)(2,1)} %get-tuple-element.35.refs_0_), channel_id=1, source_target_pairs={{0,2},{2,0},{1,3},{3,1},{4,6},{6,4},{5,7},{7,5},{8,10},{10,8},{9,1... | collective-permute-start | bytes 884744 | tf_op jit(solution)/shard_map/ppermute | solution.py:440
  30.3 4.4 %collective-permute-start.5 = (bf16[144,1024]{1,0:T(8,128)(2,1)S(1)}, bf16[144,1024]{1,0:T(8,128)(2,1)S(1)}, u32[]{:S(2)}, u32[]{:S(2)}) collective-permute-start(bf16[144,1024]{1,0:T(8,128)(2,1)S(1)} %collective-permute-done.1.refs_1_), channel_id=1, source_target_pairs={{0,2},{2,0},{1,3},{3,1},{4,6},{6,4},{5,7},{7,5},{8,10},{10,8},{9,1... | collective-permute-start | bytes 884744 | tf_op jit(solution)/shard_map/ppermute | solution.py:440
  31.2 4.7 %collective-permute-start.7 = (bf16[144,1024]{1,0:T(8,128)(2,1)S(1)}, bf16[144,1024]{1,0:T(8,128)(2,1)S(1)}, u32[]{:S(2)}, u32[]{:S(2)}) collective-permute-start(bf16[144,1024]{1,0:T(8,128)(2,1)S(1)} %collective-permute-done.3.refs_3_), channel_id=1, source_target_pairs={{0,2},{2,0},{1,3},{3,1},{4,6},{6,4},{5,7},{7,5},{8,10},{10,8},{9,1... | collective-permute-start | bytes 884744 | tf_op jit(solution)/shard_map/ppermute | solution.py:440
  31.2 10.3 %collective-permute-start.8 = (bf16[16,32,384]{2,1,0:T(8,128)(2,1)S(1)}, bf16[16,32,384]{2,1,0:T(8,128)(2,1)S(1)}, u32[]{:S(2)}, u32[]{:S(2)}) collective-permute-start(bf16[16,32,384]{2,1,0:T(8,128)(2,1)S(1)} %all-to-all-done.refs_0_), channel_id=1, source_target_pairs={{0,1},{1,0},{2,3},{3,2},{4,5},{5,4},{6,7},{7,6},{8,9},{9,8},{10,11... | collective-permute-start | bytes 1179656 | tf_op jit(solution)/shard_map/ppermute | solution.py:440
  32.5 3.8 %collective-permute-start.6 = (bf16[144,1024]{1,0:T(8,128)(2,1)S(1)}, bf16[144,1024]{1,0:T(8,128)(2,1)S(1)}, u32[]{:S(2)}, u32[]{:S(2)}) collective-permute-start(bf16[144,1024]{1,0:T(8,128)(2,1)S(1)} %collective-permute-done.2.refs_2_), channel_id=1, source_target_pairs={{0,2},{2,0},{1,3},{3,1},{4,6},{6,4},{5,7},{7,5},{8,10},{10,8},{9,1... | collective-permute-start | bytes 884744 | tf_op jit(solution)/shard_map/ppermute | solution.py:440
  33.3 24.3 %collective-permute-start.10 = (bf16[2,64,1152]{2,1,0:T(8,128)(2,1)S(1)}, bf16[2,64,1152]{2,1,0:T(8,128)(2,1)S(1)}, u32[]{:S(2)}, u32[]{:S(2)}) collective-permute-start(bf16[2,64,1152]{2,1,0:T(8,128)(2,1)S(1)} %bitcast.21), channel_id=1, source_target_pairs={{0,4},{4,0},{8,12},{12,8},{1,5},{5,1},{9,13},{13,9},{2,6},{6,2},{1... | collective-permute-start | bytes 884744 | tf_op jit(solution)/shard_map/ppermute | solution.py:440
  34.7 23.0 %collective-permute-start.11 = (bf16[2,64,1152]{2,1,0:T(8,128)(2,1)S(1)}, bf16[2,64,1152]{2,1,0:T(8,128)(2,1)S(1)}, u32[]{:S(2)}, u32[]{:S(2)}) collective-permute-start(bf16[2,64,1152]{2,1,0:T(8,128)(2,1)S(1)} %bitcast.22), channel_id=1, source_target_pairs={{0,8},{4,12},{8,0},{12,4},{1,9},{5,13},{9,1},{13,5},{2,10},{6,14},... | collective-permute-start | bytes 884744 | tf_op jit(solution)/shard_map/ppermute | solution.py:440
  35.8 21.8 %collective-permute-start.12 = (bf16[2,64,1152]{2,1,0:T(8,128)(2,1)S(1)}, bf16[2,64,1152]{2,1,0:T(8,128)(2,1)S(1)}, u32[]{:S(2)}, u32[]{:S(2)}) collective-permute-start(bf16[2,64,1152]{2,1,0:T(8,128)(2,1)S(1)} %bitcast.23), channel_id=1, source_target_pairs={{0,12},{4,8},{8,4},{12,0},{1,13},{5,9},{9,5},{13,1},{2,14},{6,10},... | collective-permute-start | bytes 884744 | tf_op jit(solution)/shard_map/ppermute | solution.py:440
  42.8 15.9 %copy-start.4 = (bf16[1,64,1024]{2,1,0:T(8,128)(2,1)S(1)}, bf16[1,64,1024]{2,1,0:T(8,128)(2,1)}, u32[]{:S(2)}) copy-start(bf16[1,64,1024]{2,1,0:T(8,128)(2,1)} %get-tuple-element.53) | copy-start | bytes 393220
  42.8 7.5 %collective-permute-start.13 = (bf16[128,256]{1,0:T(8,128)(2,1)S(1)}, bf16[128,256]{1,0:T(8,128)(2,1)S(1)}, u32[]{:S(2)}, u32[]{:S(2)}) collective-permute-start(bf16[128,256]{1,0:T(8,128)(2,1)S(1)} %get-tuple-element.47), channel_id=1, source_target_pairs={{0,16},{16,0},{1,17},{17,1},{2,18},{18,2},{3,19},{19,3},{4,20},{20... | collective-permute-start | bytes 196616 | tf_op jit(solution)/shard_map/ppermute | solution.py:440
  51.7 14.0 %all-to-all-start.1 = ((bf16[16,64,128]{2,1,0:T(8,128)(2,1)}), bf16[16,64,128]{2,1,0:T(8,128)(2,1)S(1)}, u32[]{:S(2)}, u32[]{:S(2)}) async-start(bf16[16,64,128]{2,1,0:T(8,128)(2,1)} %bitcast.7), calls=%async_computation.1 | async-start | bytes 524288 | tf_op jit(solution)/shard_map/all_to_all | solution.py:436
  57.6 8.1 %copy-start.2 = (bf16[1,64,1024]{2,1,0:T(8,128)(2,1)S(1)}, bf16[1,64,1024]{2,1,0:T(8,128)(2,1)}, u32[]{:S(2)}) copy-start(bf16[1,64,1024]{2,1,0:T(8,128)(2,1)} %get-tuple-element.52.refs_0_) | copy-start | bytes 393220
  57.6 8.1 %copy-start.3 = (f32[128]{0:T(128)S(1)}, f32[128]{0:T(128)}, u32[]{:S(2)}) copy-start(f32[128]{0:T(128)} %param.12) | copy-start | bytes 1540
  57.6 2.5 %collective-permute-start.14 = (bf16[2,64,1152]{2,1,0:T(8,128)(2,1)S(1)}, bf16[2,64,1152]{2,1,0:T(8,128)(2,1)S(1)}, u32[]{:S(2)}, u32[]{:S(2)}) collective-permute-start(bf16[2,64,1152]{2,1,0:T(8,128)(2,1)S(1)} %bitcast.24), channel_id=1, source_target_pairs={{0,2},{2,0},{1,3},{3,1},{4,6},{6,4},{5,7},{7,5},{8,10},{10,8},{9,1... | collective-permute-start | bytes 884744 | tf_op jit(solution)/shard_map/ppermute | solution.py:440
  57.8 2.3 %collective-permute-start.15 = (bf16[2,64,1152]{2,1,0:T(8,128)(2,1)S(1)}, bf16[2,64,1152]{2,1,0:T(8,128)(2,1)S(1)}, u32[]{:S(2)}, u32[]{:S(2)}) collective-permute-start(bf16[2,64,1152]{2,1,0:T(8,128)(2,1)S(1)} %collective-permute-done.10.refs_1_), channel_id=1, source_target_pairs={{0,2},{2,0},{1,3},{3,1},{4,6},{6,4},{5,7},{7,5},{8,10},{10,8},{9,1... | collective-permute-start | bytes 884744 | tf_op jit(solution)/shard_map/ppermute | solution.py:440
  58.2 1.9 %collective-permute-start.16 = (bf16[2,64,1152]{2,1,0:T(8,128)(2,1)S(1)}, bf16[2,64,1152]{2,1,0:T(8,128)(2,1)S(1)}, u32[]{:S(2)}, u32[]{:S(2)}) collective-permute-start(bf16[2,64,1152]{2,1,0:T(8,128)(2,1)S(1)} %collective-permute-done.11.refs_2_), channel_id=1, source_target_pairs={{0,2},{2,0},{1,3},{3,1},{4,6},{6,4},{5,7},{7,5},{8,10},{10,8},{9,1... | collective-permute-start | bytes 884744 | tf_op jit(solution)/shard_map/ppermute | solution.py:440
  58.3 2.2 %collective-permute-start.17 = (bf16[2,64,1152]{2,1,0:T(8,128)(2,1)S(1)}, bf16[2,64,1152]{2,1,0:T(8,128)(2,1)S(1)}, u32[]{:S(2)}, u32[]{:S(2)}) collective-permute-start(bf16[2,64,1152]{2,1,0:T(8,128)(2,1)S(1)} %collective-permute-done.12.refs_3_), channel_id=1, source_target_pairs={{0,2},{2,0},{1,3},{3,1},{4,6},{6,4},{5,7},{7,5},{8,10},{10,8},{9,1... | collective-permute-start | bytes 884744 | tf_op jit(solution)/shard_map/ppermute | solution.py:440
  58.7 6.9 %collective-permute-start.18 = (bf16[1,64,1024]{2,1,0:T(8,128)(2,1)S(1)}, bf16[1,64,1024]{2,1,0:T(8,128)(2,1)S(1)}, u32[]{:S(2)}, u32[]{:S(2)}) collective-permute-start(bf16[1,64,1024]{2,1,0:T(8,128)(2,1)S(1)} %copy-done.4), channel_id=1, source_target_pairs={{0,1},{1,0},{2,3},{3,2},{4,5},{5,4},{6,7},{7,6},{8,9},{9,8},{10,11... | collective-permute-start | bytes 393224 | tf_op jit(solution)/shard_map/ppermute | solution.py:440
  69.4 18.9 %copy-start = (bf16[1024,1024]{1,0:T(8,128)(2,1)S(1)}, bf16[1024,1024]{1,0:T(8,128)(2,1)}, u32[]{:S(2)}) copy-start(bf16[1024,1024]{1,0:T(8,128)(2,1)} %get-tuple-element.36.normed_any.normed_ref) | copy-start | bytes 6291460
  82.0 6.3 %collective-permute-start.19 = (bf16[128,256]{1,0:T(8,128)(2,1)S(1)}, bf16[128,256]{1,0:T(8,128)(2,1)S(1)}, u32[]{:S(2)}, u32[]{:S(2)}) collective-permute-start(bf16[128,256]{1,0:T(8,128)(2,1)S(1)} %get-tuple-element.55), channel_id=1, source_target_pairs={{0,16},{16,0},{1,17},{17,1},{2,18},{18,2},{3,19},{19,3},{4,20},{20... | collective-permute-start | bytes 196616 | tf_op jit(solution)/shard_map/ppermute | solution.py:440
  90.4 18.7 %all-to-all-start.3 = ((bf16[32,32,256]{2,1,0:T(8,128)(2,1)}), bf16[32,32,256]{2,1,0:T(8,128)(2,1)S(1)}, u32[]{:S(2)}, u32[]{:S(2)}) async-start(bf16[32,32,256]{2,1,0:T(8,128)(2,1)} %bitcast.11), calls=%async_computation.3 | async-start | bytes 1048576 | tf_op jit(solution)/shard_map/all_to_all | solution.py:436
  93.2 6.0 %collective-permute-start.20 = (f32[100,128]{1,0:T(8,128)S(1)}, f32[100,128]{1,0:T(8,128)S(1)}, u32[]{:S(2)}, u32[]{:S(2)}) collective-permute-start(f32[100,128]{1,0:T(8,128)S(1)} %get-tuple-element.58), channel_id=1, source_target_pairs={{0,1},{1,0},{2,3},{3,2},{4,5},{5,4},{6,7},{7,6},{8,9},{9,8},{10,11... | collective-permute-start | bytes 153608 | tf_op jit(solution)/shard_map/ppermute | solution.py:440

commit v14 on v13

--- a/solution.py
+++ b/solution.py
@@ -518,6 +518,7 @@
         results="hv",
     )(*near, *far)
 
+    packed, near[1] = lax.optimization_barrier((packed, near[1]))
     packed = in_order(packed, "ens", 1).reshape(halves, members_num * shard, width)
     packed, near[2] = lax.optimization_barrier((packed, near[2]))
     pieces = [packed] + [swap(packed, "quad", step) for step in range(1, QUAD)]
@@ -573,6 +574,7 @@
     )(steps, queries, own, low, high, outcome)
     *pieces, own = lax.optimization_barrier((*pieces, own))
     pieces = pieces + [swap(piece, "core", 1) for piece in pieces]
+    outcome, sources[-1] = lax.optimization_barrier((outcome, sources[-1]))
     attended = exchange(outcome.reshape(GROUP * members_num, part, COLS), ("quad", "core", "ens"))
     block = (halves, QUAD, CORES, members_num * shard, width)
     (weights,) = call(

time: 110 us -> 121 us (1.10)
  waiting for transfers between devices: 33.9 us -> 39.6 us
  starting transfers between devices: 36.1 us -> 41.7 us
  blocking collectives: 11.2 us -> 9.88 us
    all_to_all x3, starting transfers between devices: 13.4 us -> 16.9 us  [exchange(): return lax.all_to_all(chunks, axes, 0, 0)]
    ppermute x21, waiting for transfers between devices: 18.9 us -> 22.1 us  [swap(): lax.ppermute(value, axis, [(i, i ^ step) for i in range(lax.axis_size(axi...]
    all_to_all x3, waiting for transfers between devices: 15 us -> 17.5 us  [exchange(): return lax.all_to_all(chunks, axes, 0, 0)]
    ppermute x21, starting transfers between devices: 22.7 us -> 24.8 us  [swap(): lax.ppermute(value, axis, [(i, i ^ step) for i in range(lax.axis_size(axi...]
    all_to_all x1, blocking collectives: 11.2 us -> 9.88 us  [exchange(): return lax.all_to_all(chunks, axes, 0, 0)]
  transfers between devices with their start and end apart: 24 -> 24, of which waited for: 8 -> 14; matrix products, arithmetic and copies ran while one was open for 2% -> 2% of each run, Pallas kernels for 15% -> 12%
where the time goes in v14:
time: 121 us
  starting transfers between devices  41.7 us (34%)
  waiting for transfers between devices  39.6 us (33%)
  Pallas kernels  25.9 us (21%)
  blocking collectives  9.88 us (8%)
  local copies, waits for them, and re-layouts  1.75 us (1%)
    pallas_call x13, Pallas kernels, run(): made(*[pltpu.with_memory_space_constraint(arg, pltpu.HBM) if space == 'h'...  25.9 us
    ppermute x21, starting transfers between devices, swap(): lax.ppermute(value, axis, [(i, i ^ step) for i in range(lax.axis_size(axi...  24.8 us
    ppermute x21, waiting for transfers between devices, swap(): lax.ppermute(value, axis, [(i, i ^ step) for i in range(lax.axis_size(axi...  22.1 us
    all_to_all x3, waiting for transfers between devices, exchange(): return lax.all_to_all(chunks, axes, 0, 0)  17.5 us
    all_to_all x3, starting transfers between devices, exchange(): return lax.all_to_all(chunks, axes, 0, 0)  16.9 us
    all_to_all x1, blocking collectives, exchange(): return lax.all_to_all(chunks, axes, 0, 0)  9.88 us
  transfers between devices with their start and end apart: 24, of which 14 were waited for; matrix products, arithmetic and copies ran while one was open for 2% of the time, Pallas kernels for 12%

profile of v14, /device:TPU:1, one launch (start us, length us, event | category | flops | bytes accessed | tf_op | source)
XLA Modules:
  0.0 120.7 jit_solution(6856115778744854619)
XLA Ops:
  0.6 1.8 %prepare_weights.1 = (bf16[2,8,1,32,384]{4,3,2,1,0:T(8,128)(2,1)}, bf16[32,1152]{1,0:T(8,128)(2,1)}) custom-call(bf16[32,3072]{1,0:T(8,128)(2,1)} %w_any.1, bf16[32,1024]{1,0:T(8,128)(2,1)} %mix_any.1, bf16[32,100]{1,0:T(8,128)(2,1)} %readout_any.1), custom_call_target="tpu_custom_call" | custom-call | bytes 1048576 | tf_op jit(solution)/shard_map/prepare_weights/pallas_call | solution.py:63
  2.4 3.2 %collective-permute-start = (bf16[32,1152]{1,0:T(8,128)(2,1)}, bf16[32,1152]{1,0:T(8,128)(2,1)S(1)}, u32[]{:S(2)}, u32[]{:S(2)}) collective-permute-start(bf16[32,1152]{1,0:T(8,128)(2,1)} %get-tuple-element.34), channel_id=1, source_target_pairs={{0,16},{16,0},{1,17},{17,1},{2,18},{18,2},{3,19},{19,3},{4,20},{20... | collective-permute-start | bytes 221192 | tf_op jit(solution)/shard_map/ppermute | solution.py:440
  5.6 4.8 %all-to-all-start = ((bf16[16,32,384]{2,1,0:T(8,128)(2,1)}), bf16[16,32,384]{2,1,0:T(8,128)(2,1)S(1)}, u32[]{:S(2)}, u32[]{:S(2)}) async-start(bf16[16,32,384]{2,1,0:T(8,128)(2,1)} %bitcast.27), calls=%async_computation | async-start | bytes 786432 | tf_op jit(solution)/shard_map/all_to_all | solution.py:436
  10.4 1.9 %norm.1 = (bf16[144,1024]{1,0:T(8,128)(2,1)}, bf16[1,64,1024]{2,1,0:T(8,128)(2,1)}, bf16[1,64,1024]{2,1,0:T(8,128)(2,1)}) custom-call(s32[2,4]{1,0:T(2,128)} %near_any.1, bf16[128,1024]{1,0:T(8,128)(2,1)} %bitcast.28), custom_call_target="tpu_custom_call" | custom-call | flops 1048576 | bytes 1048576 | tf_op jit(solution)/shard_map/norm/pallas_call | solution.py:63
  12.3 0.9 select_bitcast_fusion.3
  13.2 1.5 %collective-permute-start.1 = (bf16[144,1024]{1,0:T(8,128)(2,1)}, bf16[144,1024]{1,0:T(8,128)(2,1)S(1)}, u32[]{:S(2)}, u32[]{:S(2)}) collective-permute-start(bf16[144,1024]{1,0:T(8,128)(2,1)} %get-tuple-element.38.refs_0_), channel_id=1, source_target_pairs={{0,4},{4,0},{8,12},{12,8},{1,5},{5,1},{9,13},{13,9},{2,6},{6,2},{1... | collective-permute-start | bytes 884744 | tf_op jit(solution)/shard_map/ppermute | solution.py:440
  14.7 1.2 collective-permute-start.3
  15.9 6.0 %all-to-all-done.refs_0_ = bf16[16,32,384]{2,1,0:T(8,128)(2,1)S(1)} async-done(((bf16[16,32,384]{2,1,0:T(8,128)(2,1)}), bf16[16,32,384]{2,1,0:T(8,128)(2,1)S(1)}, u32[]{:S(2)}, u32[]{:S(2)}) %all-to-all-start) | async-done | bytes 393248 | tf_op jit(solution)/shard_map/all_to_all | solution.py:436
  21.9 1.7 %collective-permute-start.2 = (bf16[144,1024]{1,0:T(8,128)(2,1)}, bf16[144,1024]{1,0:T(8,128)(2,1)S(1)}, u32[]{:S(2)}, u32[]{:S(2)}) collective-permute-start(bf16[144,1024]{1,0:T(8,128)(2,1)} %get-tuple-element.38.refs_0_), channel_id=1, source_target_pairs={{0,8},{4,12},{8,0},{12,4},{1,9},{5,13},{9,1},{13,5},{2,10},{6,14},... | collective-permute-start | bytes 884744 | tf_op jit(solution)/shard_map/ppermute | solution.py:440
  23.6 6.7 %collective-permute-done.1.refs_1_ = bf16[144,1024]{1,0:T(8,128)(2,1)S(1)} collective-permute-done((bf16[144,1024]{1,0:T(8,128)(2,1)}, bf16[144,1024]{1,0:T(8,128)(2,1)S(1)}, u32[]{:S(2)}, u32[]{:S(2)}) %collective-permute-start.1) | collective-permute-done | bytes 294944 | tf_op jit(solution)/shard_map/ppermute | solution.py:440
  30.3 1.2 %collective-permute-start.9 = (bf16[2,32,1152]{2,1,0:T(8,128)(2,1)S(1)}, bf16[2,32,1152]{2,1,0:T(8,128)(2,1)S(1)}, u32[]{:S(2)}, u32[]{:S(2)}) collective-permute-start(bf16[2,32,1152]{2,1,0:T(8,128)(2,1)S(1)} %pad_maximum_fusion.1), channel_id=1, source_target_pairs={{0,1},{1,0},{2,3},{3,2},{4,5},{5,4},{6,7},{7,6},{8,9},{9,8},{10,11... | collective-permute-start | bytes 442376 | tf_op jit(solution)/shard_map/ppermute | solution.py:440
  31.5 1.2 collective-permute-start.4
  32.6 0.5 collective-permute-start.7
  33.1 1.6 %collective-permute-done.9 = bf16[2,32,1152]{2,1,0:T(8,128)(2,1)S(1)} collective-permute-done((bf16[2,32,1152]{2,1,0:T(8,128)(2,1)S(1)}, bf16[2,32,1152]{2,1,0:T(8,128)(2,1)S(1)}, u32[]{:S(2)}, u32[]{:S(2)}) %collective-permute-start.9) | collective-permute-done | bytes 147488 | tf_op jit(solution)/shard_map/ppermute | solution.py:440
  34.8 1.2 %collective-permute-start.8 = (bf16[16,32,384]{2,1,0:T(8,128)(2,1)S(1)}, bf16[16,32,384]{2,1,0:T(8,128)(2,1)S(1)}, u32[]{:S(2)}, u32[]{:S(2)}) collective-permute-start(bf16[16,32,384]{2,1,0:T(8,128)(2,1)S(1)} %all-to-all-done.refs_0_), channel_id=1, source_target_pairs={{0,1},{1,0},{2,3},{3,2},{4,5},{5,4},{6,7},{7,6},{8,9},{9,8},{10,11... | collective-permute-start | bytes 1179656 | tf_op jit(solution)/shard_map/ppermute | solution.py:440
  36.0 2.1 %collective-permute-start.6 = (bf16[144,1024]{1,0:T(8,128)(2,1)S(1)}, bf16[144,1024]{1,0:T(8,128)(2,1)S(1)}, u32[]{:S(2)}, u32[]{:S(2)}) collective-permute-start(bf16[144,1024]{1,0:T(8,128)(2,1)S(1)} %collective-permute-done.2.refs_2_), channel_id=1, source_target_pairs={{0,2},{2,0},{1,3},{3,1},{4,6},{6,4},{5,7},{7,5},{8,10},{10,8},{9,1... | collective-permute-start | bytes 884744 | tf_op jit(solution)/shard_map/ppermute | solution.py:440
  38.1 1.1 collective-permute-done.6.refs_6_
  39.2 1.0 copy-done.1
  40.2 1.5 %collect.1 = (bf16[1024,1024]{1,0:T(8,128)(2,1)}, f32[8,16,128]{2,1,0:T(8,128)S(1)}) custom-call(bf16[144,1024]{1,0:T(8,128)(2,1)S(1)} %copy-done.1, bf16[144,1024]{1,0:T(8,128)(2,1)S(1)} %collective-permute-done.1.refs_1_, bf16[144,1024]{1,0:T(8,128)(2,1)S(1)} %collective-permute-done.2.refs_2_, bf16[144,1024]{1,0:T(8,128)(2,1)S(1)} %collective-permute-done.3.refs_3_, ...), custom_call_target="tpu_custom_call" | custom-call | bytes 4194304 | tf_op jit(solution)/shard_map/collect/pallas_call | solution.py:63
  41.7 1.9 %collective-permute-done.8.refs_1_ = bf16[16,32,384]{2,1,0:T(8,128)(2,1)S(1)} collective-permute-done((bf16[16,32,384]{2,1,0:T(8,128)(2,1)S(1)}, bf16[16,32,384]{2,1,0:T(8,128)(2,1)S(1)}, u32[]{:S(2)}, u32[]{:S(2)}) %collective-permute-start.8) | collective-permute-done | bytes 393248 | tf_op jit(solution)/shard_map/ppermute | solution.py:440
  43.6 1.3 %project_rims.1 = (bf16[16,2,32,384]{3,2,1,0:T(8,128)(2,1)S(1)}, bf16[128,256]{1,0:T(8,128)(2,1)S(1)}) custom-call(bf16[1024,1024]{1,0:T(8,128)(2,1)} %get-tuple-element.39.normed_any.normed_ref, bf16[16,32,384]{2,1,0:T(8,128)(2,1)S(1)} %all-to-all-done.refs_0_, bf16[16,32,384]{2,1,0:T(8,128)(2,1)S(1)} %collective-permute-done.8.refs_1_), custom_call_target="tpu_custom_call" | custom-call | flops 67108864 | bytes 1048576 | tf_op jit(solution)/shard_map/project_rims/pallas_call | solution.py:63
  44.9 1.3 %collective-permute-start.14 = (bf16[1,64,1024]{2,1,0:T(8,128)(2,1)S(1)}, bf16[1,64,1024]{2,1,0:T(8,128)(2,1)S(1)}, u32[]{:S(2)}, u32[]{:S(2)}) collective-permute-start(bf16[1,64,1024]{2,1,0:T(8,128)(2,1)S(1)} %copy-done.4), channel_id=1, source_target_pairs={{0,1},{1,0},{2,3},{3,2},{4,5},{5,4},{6,7},{7,6},{8,9},{9,8},{10,11... | collective-permute-start | bytes 393224 | tf_op jit(solution)/shard_map/ppermute | solution.py:440
  46.2 2.0 %collective-permute-start.10 = (bf16[2,64,1152]{2,1,0:T(8,128)(2,1)S(1)}, bf16[2,64,1152]{2,1,0:T(8,128)(2,1)S(1)}, u32[]{:S(2)}, u32[]{:S(2)}) collective-permute-start(bf16[2,64,1152]{2,1,0:T(8,128)(2,1)S(1)} %bitcast.21), channel_id=1, source_target_pairs={{0,4},{4,0},{8,12},{12,8},{1,5},{5,1},{9,13},{13,9},{2,6},{6,2},{1... | collective-permute-start | bytes 884744 | tf_op jit(solution)/shard_map/ppermute | solution.py:440
  48.3 1.0 collective-permute-start.11
  49.5 2.8 %collective-permute-start.13 = (bf16[128,256]{1,0:T(8,128)(2,1)S(1)}, bf16[128,256]{1,0:T(8,128)(2,1)S(1)}, u32[]{:S(2)}, u32[]{:S(2)}) collective-permute-start(bf16[128,256]{1,0:T(8,128)(2,1)S(1)} %get-tuple-element.51), channel_id=1, source_target_pairs={{0,16},{16,0},{1,17},{17,1},{2,18},{18,2},{3,19},{19,3},{4,20},{20... | collective-permute-start | bytes 196616 | tf_op jit(solution)/shard_map/ppermute | solution.py:440
  52.3 2.8 %project.1 = (bf16[1024,128]{1,0:T(8,128)(2,1)S(1)}, bf16[1024,256]{1,0:T(8,128)(2,1)S(1)}) custom-call(bf16[1024,1024]{1,0:T(8,128)(2,1)} %get-tuple-element.39.normed_any.normed_ref, bf16[16,2,32,384]{3,2,1,0:T(8,128)(2,1)S(1)} %get-tuple-element.44.w_ref), custom_call_target="tpu_custom_call" | custom-call | flops 805306368 | bytes 4194304 | tf_op jit(solution)/shard_map/project/pallas_call | solution.py:63
  55.2 1.9 %attention_interior.1.done_ref = bf16[1024,128]{1,0:T(8,128)(2,1)S(1)} custom-call(f32[8,16,128]{2,1,0:T(8,128)S(1)} %get-tuple-element.40.steps_ref, bf16[1024,128]{1,0:T(8,128)(2,1)S(1)} %get-tuple-element.45.q_ref, bf16[1024,256]{1,0:T(8,128)(2,1)S(1)} %get-tuple-element.50.kv_ref), custom_call_target="tpu_custom_call" | custom-call | flops 268435456 | bytes 2097152 | tf_op jit(solution)/shard_map/attention_interior/pallas_call | solution.py:63
  57.1 3.2 %collective-permute-done.13.low_ref.high_ref = bf16[128,256]{1,0:T(8,128)(2,1)S(1)} collective-permute-done((bf16[128,256]{1,0:T(8,128)(2,1)S(1)}, bf16[128,256]{1,0:T(8,128)(2,1)S(1)}, u32[]{:S(2)}, u32[]{:S(2)}) %collective-permute-start.13) | collective-permute-done | bytes 65568 | tf_op jit(solution)/shard_map/ppermute | solution.py:440
  60.2 1.4 %attention_edges.1 = bf16[1024,128]{1,0:T(8,128)(2,1)} custom-call(f32[8,16,128]{2,1,0:T(8,128)S(1)} %get-tuple-element.40.steps_ref, bf16[1024,128]{1,0:T(8,128)(2,1)S(1)} %get-tuple-element.45.q_ref, bf16[1024,256]{1,0:T(8,128)(2,1)S(1)} %get-tuple-element.50.kv_ref, bf16[128,256]{1,0:T(8,128)(2,1)S(1)} %collective-permute-done.13.low_ref.high_ref, ...), custom_call_target="tpu_custom_call" | custom-call | flops 67108864 | bytes 1048576 | tf_op jit(solution)/shard_map/attention_edges/pallas_call | solution.py:63
  61.7 9.3 %all-to-all-start.1 = ((bf16[16,64,128]{2,1,0:T(8,128)(2,1)}), bf16[16,64,128]{2,1,0:T(8,128)(2,1)S(1)}, u32[]{:S(2)}, u32[]{:S(2)}) async-start(bf16[16,64,128]{2,1,0:T(8,128)(2,1)} %bitcast.7), calls=%async_computation.1 | async-start | bytes 524288 | tf_op jit(solution)/shard_map/all_to_all | solution.py:436
  72.1 0.6 collective-permute-done.15.refs_4_
  72.7 0.4 collective-permute-done.16.refs_5_
  73.1 0.4 collective-permute-done.17.refs_6_
  74.0 1.5 %assemble.1.w_any = bf16[2,4,2,64,1152]{4,3,2,1,0:T(8,128)(2,1)} custom-call(bf16[2,64,1152]{2,1,0:T(8,128)(2,1)S(1)} %bitcast.25, bf16[2,64,1152]{2,1,0:T(8,128)(2,1)S(1)} %collective-permute-done.10.refs_1_, bf16[2,64,1152]{2,1,0:T(8,128)(2,1)S(1)} %collective-permute-done.11.refs_2_, bf16[2,64,1152]{2,1,0:T(8,128)(2,1)S(1)} %collective-permute-done.12.refs_3_, ...), custom_call_target="tpu_custom_call" | custom-call | bytes 4194304 | tf_op jit(solution)/shard_map/assemble/pallas_call | solution.py:63
  75.4 2.4 %all-to-all-done.1.att_ref = bf16[16,64,128]{2,1,0:T(8,128)(2,1)S(1)} async-done(((bf16[16,64,128]{2,1,0:T(8,128)(2,1)}), bf16[16,64,128]{2,1,0:T(8,128)(2,1)S(1)}, u32[]{:S(2)}, u32[]{:S(2)}) %all-to-all-start.1) | async-done | bytes 262176 | tf_op jit(solution)/shard_map/all_to_all | solution.py:436
  77.9 3.7 %mix_loss_backward.1 = (f32[100,128]{1,0:T(8,128)S(1)}, bf16[16,64,128]{2,1,0:T(8,128)(2,1)S(1)}) custom-call(bf16[16,64,128]{2,1,0:T(8,128)(2,1)S(1)} %all-to-all-done.1.att_ref, f32[1,128]{1,0:T(1,128)S(1)} %bitcast.26, f32[100,128]{1,0:T(8,128)} %truth_any.1, bf16[2,4,2,64,1152]{4,3,2,1,0:T(8,128)(2,1)} %assemble.1.w_any, ...), custom_call_target="tpu_custom_call" | custom-call | flops 603979776 | bytes 4194304 | tf_op jit(solution)/shard_map/mix_loss_backward/pallas_call | solution.py:63
  81.6 9.9 %all_to_all.20 = bf16[16,64,128]{2,1,0:T(8,128)(2,1)S(1)} all-to-all(bf16[16,64,128]{2,1,0:T(8,128)(2,1)S(1)} %get-tuple-element.60), channel_id=1, replica_groups=mesh['half'=2,'quad'=4,'core'=2,'ens'=2] {'quad','core','ens'}, dimensions={0} | all-to-all | bytes 524288 | tf_op jit(solution)/shard_map/all_to_all | solution.py:436
  91.5 1.4 %attention_edges_back.1 = (f32[2,256,256]{2,1,0:T(8,128)S(1)}, bf16[128,256]{1,0:T(8,128)(2,1)S(1)}) custom-call(f32[8,16,128]{2,1,0:T(8,128)S(1)} %get-tuple-element.40.steps_ref, bf16[1024,128]{1,0:T(8,128)(2,1)S(1)} %get-tuple-element.45.q_ref, bf16[1024,256]{1,0:T(8,128)(2,1)S(1)} %get-tuple-element.50.kv_ref, ...), custom_call_target="tpu_custom_call" | custom-call | flops 167772160 | bytes 1048576 | tf_op jit(solution)/shard_map/attention_edges_back/pallas_call | solution.py:63
  92.9 1.2 %collective-permute-start.19 = (bf16[128,256]{1,0:T(8,128)(2,1)S(1)}, bf16[128,256]{1,0:T(8,128)(2,1)S(1)}, u32[]{:S(2)}, u32[]{:S(2)}) collective-permute-start(bf16[128,256]{1,0:T(8,128)(2,1)S(1)} %get-tuple-element.61), channel_id=1, source_target_pairs={{0,16},{16,0},{1,17},{17,1},{2,18},{18,2},{3,19},{19,3},{4,20},{20... | collective-permute-start | bytes 196616 | tf_op jit(solution)/shard_map/ppermute | solution.py:440
  94.1 3.8 %attention_interior_back.1.grads_ref = f32[1024,256]{1,0:T(8,128)S(1)} custom-call(f32[8,16,128]{2,1,0:T(8,128)S(1)} %get-tuple-element.40.steps_ref, bf16[1024,128]{1,0:T(8,128)(2,1)S(1)} %get-tuple-element.45.q_ref, bf16[1024,256]{1,0:T(8,128)(2,1)S(1)} %get-tuple-element.50.kv_ref, bf16[1024,128]{1,0:T(8,128)(2,1)S(1)} %bitcast.19, ...), custom_call_target="tpu_custom_call" | custom-call | flops 536870912 | bytes 4194304 | tf_op jit(solution)/shard_map/attention_interior_back/pallas_call | solution.py:63
  98.0 1.2 collective-permute-done.19.from_low_ref.from_high_ref
  99.2 2.1 %product.1 = bf16[1024,256]{1,0:T(8,128)(2,1)} custom-call(bf16[1024,1024]{1,0:T(8,128)(2,1)S(1)} %copy-done, bf16[128,256]{1,0:T(8,128)(2,1)S(1)} %collective-permute-done.19.from_low_ref.from_high_ref, bf16[128,256]{1,0:T(8,128)(2,1)S(1)} %collective-permute-done.19.from_low_ref.from_high_ref, f32[1024,256]{1,0:T(8,128)S(1)} %attention_interior_back.1.grads_ref), custom_call_target="tpu_custom_call" | custom-call | flops 1073741824 | bytes 4194304 | tf_op jit(solution)/shard_map/product/pallas_call | solution.py:63
  101.2 2.8 %all-to-all-start.3 = ((bf16[32,32,256]{2,1,0:T(8,128)(2,1)}), bf16[32,32,256]{2,1,0:T(8,128)(2,1)S(1)}, u32[]{:S(2)}, u32[]{:S(2)}) async-start(bf16[32,32,256]{2,1,0:T(8,128)(2,1)} %bitcast.11), calls=%async_computation.3 | async-start | bytes 1048576 | tf_op jit(solution)/shard_map/all_to_all | solution.py:436
  104.0 1.5 %collective-permute-start.20 = (f32[100,128]{1,0:T(8,128)S(1)}, f32[100,128]{1,0:T(8,128)S(1)}, u32[]{:S(2)}, u32[]{:S(2)}) collective-permute-start(f32[100,128]{1,0:T(8,128)S(1)} %get-tuple-element.64), channel_id=1, source_target_pairs={{0,1},{1,0},{2,3},{3,2},{4,5},{5,4},{6,7},{7,6},{8,9},{9,8},{10,11... | collective-permute-start | bytes 153608 | tf_op jit(solution)/shard_map/ppermute | solution.py:440
  105.5 4.5 %collective-permute-done.20 = f32[100,128]{1,0:T(8,128)S(1)} collective-permute-done((f32[100,128]{1,0:T(8,128)S(1)}, f32[100,128]{1,0:T(8,128)S(1)}, u32[]{:S(2)}, u32[]{:S(2)}) %collective-permute-start.20) | collective-permute-done | bytes 51232 | tf_op jit(solution)/shard_map/ppermute | solution.py:440
  110.2 0.7 copy.10
  110.9 9.1 %all-to-all-done.3 = bf16[32,32,256]{2,1,0:T(8,128)(2,1)S(1)} async-done(((bf16[32,32,256]{2,1,0:T(8,128)(2,1)}), bf16[32,32,256]{2,1,0:T(8,128)(2,1)S(1)}, u32[]{:S(2)}, u32[]{:S(2)}) %all-to-all-start.3) | async-done | bytes 524320 | tf_op jit(solution)/shard_map/all_to_all | solution.py:436
  119.9 0.8 gather_sums.1
  (34 shorter events, 2.1 us)
Async XLA Ops:
  2.4 9.9 %collective-permute-start = (bf16[32,1152]{1,0:T(8,128)(2,1)}, bf16[32,1152]{1,0:T(8,128)(2,1)S(1)}, u32[]{:S(2)}, u32[]{:S(2)}) collective-permute-start(bf16[32,1152]{1,0:T(8,128)(2,1)} %get-tuple-element.34), channel_id=1, source_target_pairs={{0,16},{16,0},{1,17},{17,1},{2,18},{18,2},{3,19},{19,3},{4,20},{20... | collective-permute-start | bytes 221192 | tf_op jit(solution)/shard_map/ppermute | solution.py:440
  5.6 16.2 %all-to-all-start = ((bf16[16,32,384]{2,1,0:T(8,128)(2,1)}), bf16[16,32,384]{2,1,0:T(8,128)(2,1)S(1)}, u32[]{:S(2)}, u32[]{:S(2)}) async-start(bf16[16,32,384]{2,1,0:T(8,128)(2,1)} %bitcast.27), calls=%async_computation | async-start | bytes 786432 | tf_op jit(solution)/shard_map/all_to_all | solution.py:436
  13.2 17.0 %collective-permute-start.1 = (bf16[144,1024]{1,0:T(8,128)(2,1)}, bf16[144,1024]{1,0:T(8,128)(2,1)S(1)}, u32[]{:S(2)}, u32[]{:S(2)}) collective-permute-start(bf16[144,1024]{1,0:T(8,128)(2,1)} %get-tuple-element.38.refs_0_), channel_id=1, source_target_pairs={{0,4},{4,0},{8,12},{12,8},{1,5},{5,1},{9,13},{13,9},{2,6},{6,2},{1... | collective-permute-start | bytes 884744 | tf_op jit(solution)/shard_map/ppermute | solution.py:440
  14.7 17.9 %collective-permute-start.3 = (bf16[144,1024]{1,0:T(8,128)(2,1)}, bf16[144,1024]{1,0:T(8,128)(2,1)S(1)}, u32[]{:S(2)}, u32[]{:S(2)}) collective-permute-start(bf16[144,1024]{1,0:T(8,128)(2,1)} %get-tuple-element.38.refs_0_), channel_id=1, source_target_pairs={{0,12},{4,8},{8,4},{12,0},{1,13},{5,9},{9,5},{13,1},{2,14},{6,10},... | collective-permute-start | bytes 884744 | tf_op jit(solution)/shard_map/ppermute | solution.py:440
  21.9 14.1 %collective-permute-start.2 = (bf16[144,1024]{1,0:T(8,128)(2,1)}, bf16[144,1024]{1,0:T(8,128)(2,1)S(1)}, u32[]{:S(2)}, u32[]{:S(2)}) collective-permute-start(bf16[144,1024]{1,0:T(8,128)(2,1)} %get-tuple-element.38.refs_0_), channel_id=1, source_target_pairs={{0,8},{4,12},{8,0},{12,4},{1,9},{5,13},{9,1},{13,5},{2,10},{6,14},... | collective-permute-start | bytes 884744 | tf_op jit(solution)/shard_map/ppermute | solution.py:440
  30.3 4.5 %collective-permute-start.9 = (bf16[2,32,1152]{2,1,0:T(8,128)(2,1)S(1)}, bf16[2,32,1152]{2,1,0:T(8,128)(2,1)S(1)}, u32[]{:S(2)}, u32[]{:S(2)}) collective-permute-start(bf16[2,32,1152]{2,1,0:T(8,128)(2,1)S(1)} %pad_maximum_fusion.1), channel_id=1, source_target_pairs={{0,1},{1,0},{2,3},{3,2},{4,5},{5,4},{6,7},{7,6},{8,9},{9,8},{10,11... | collective-permute-start | bytes 442376 | tf_op jit(solution)/shard_map/ppermute | solution.py:440
  31.5 6.6 %collective-permute-start.4 = (bf16[144,1024]{1,0:T(8,128)(2,1)}, bf16[144,1024]{1,0:T(8,128)(2,1)S(1)}, u32[]{:S(2)}, u32[]{:S(2)}) collective-permute-start(bf16[144,1024]{1,0:T(8,128)(2,1)} %get-tuple-element.38.refs_0_), channel_id=1, source_target_pairs={{0,2},{2,0},{1,3},{3,1},{4,6},{6,4},{5,7},{7,5},{8,10},{10,8},{9,1... | collective-permute-start | bytes 884744 | tf_op jit(solution)/shard_map/ppermute | solution.py:440
  32.6 5.4 %collective-permute-start.5 = (bf16[144,1024]{1,0:T(8,128)(2,1)S(1)}, bf16[144,1024]{1,0:T(8,128)(2,1)S(1)}, u32[]{:S(2)}, u32[]{:S(2)}) collective-permute-start(bf16[144,1024]{1,0:T(8,128)(2,1)S(1)} %collective-permute-done.1.refs_1_), channel_id=1, source_target_pairs={{0,2},{2,0},{1,3},{3,1},{4,6},{6,4},{5,7},{7,5},{8,10},{10,8},{9,1... | collective-permute-start | bytes 884744 | tf_op jit(solution)/shard_map/ppermute | solution.py:440
  32.6 5.5 %collective-permute-start.7 = (bf16[144,1024]{1,0:T(8,128)(2,1)S(1)}, bf16[144,1024]{1,0:T(8,128)(2,1)S(1)}, u32[]{:S(2)}, u32[]{:S(2)}) collective-permute-start(bf16[144,1024]{1,0:T(8,128)(2,1)S(1)} %collective-permute-done.3.refs_3_), channel_id=1, source_target_pairs={{0,2},{2,0},{1,3},{3,1},{4,6},{6,4},{5,7},{7,5},{8,10},{10,8},{9,1... | collective-permute-start | bytes 884744 | tf_op jit(solution)/shard_map/ppermute | solution.py:440
  34.8 8.8 %collective-permute-start.8 = (bf16[16,32,384]{2,1,0:T(8,128)(2,1)S(1)}, bf16[16,32,384]{2,1,0:T(8,128)(2,1)S(1)}, u32[]{:S(2)}, u32[]{:S(2)}) collective-permute-start(bf16[16,32,384]{2,1,0:T(8,128)(2,1)S(1)} %all-to-all-done.refs_0_), channel_id=1, source_target_pairs={{0,1},{1,0},{2,3},{3,2},{4,5},{5,4},{6,7},{7,6},{8,9},{9,8},{10,11... | collective-permute-start | bytes 1179656 | tf_op jit(solution)/shard_map/ppermute | solution.py:440
  36.0 3.3 %collective-permute-start.6 = (bf16[144,1024]{1,0:T(8,128)(2,1)S(1)}, bf16[144,1024]{1,0:T(8,128)(2,1)S(1)}, u32[]{:S(2)}, u32[]{:S(2)}) collective-permute-start(bf16[144,1024]{1,0:T(8,128)(2,1)S(1)} %collective-permute-done.2.refs_2_), channel_id=1, source_target_pairs={{0,2},{2,0},{1,3},{3,1},{4,6},{6,4},{5,7},{7,5},{8,10},{10,8},{9,1... | collective-permute-start | bytes 884744 | tf_op jit(solution)/shard_map/ppermute | solution.py:440
  38.0 6.9 %copy-start.4 = (bf16[1,64,1024]{2,1,0:T(8,128)(2,1)S(1)}, bf16[1,64,1024]{2,1,0:T(8,128)(2,1)}, u32[]{:S(2)}) copy-start(bf16[1,64,1024]{2,1,0:T(8,128)(2,1)} %get-tuple-element.52) | copy-start | bytes 393220
  39.2 1.0 copy-start.1
  44.9 16.8 %collective-permute-start.14 = (bf16[1,64,1024]{2,1,0:T(8,128)(2,1)S(1)}, bf16[1,64,1024]{2,1,0:T(8,128)(2,1)S(1)}, u32[]{:S(2)}, u32[]{:S(2)}) collective-permute-start(bf16[1,64,1024]{2,1,0:T(8,128)(2,1)S(1)} %copy-done.4), channel_id=1, source_target_pairs={{0,1},{1,0},{2,3},{3,2},{4,5},{5,4},{6,7},{7,6},{8,9},{9,8},{10,11... | collective-permute-start | bytes 393224 | tf_op jit(solution)/shard_map/ppermute | solution.py:440
  46.2 24.8 %collective-permute-start.10 = (bf16[2,64,1152]{2,1,0:T(8,128)(2,1)S(1)}, bf16[2,64,1152]{2,1,0:T(8,128)(2,1)S(1)}, u32[]{:S(2)}, u32[]{:S(2)}) collective-permute-start(bf16[2,64,1152]{2,1,0:T(8,128)(2,1)S(1)} %bitcast.21), channel_id=1, source_target_pairs={{0,4},{4,0},{8,12},{12,8},{1,5},{5,1},{9,13},{13,9},{2,6},{6,2},{1... | collective-permute-start | bytes 884744 | tf_op jit(solution)/shard_map/ppermute | solution.py:440
  48.3 22.8 %collective-permute-start.11 = (bf16[2,64,1152]{2,1,0:T(8,128)(2,1)S(1)}, bf16[2,64,1152]{2,1,0:T(8,128)(2,1)S(1)}, u32[]{:S(2)}, u32[]{:S(2)}) collective-permute-start(bf16[2,64,1152]{2,1,0:T(8,128)(2,1)S(1)} %bitcast.22), channel_id=1, source_target_pairs={{0,8},{4,12},{8,0},{12,4},{1,9},{5,13},{9,1},{13,5},{2,10},{6,14},... | collective-permute-start | bytes 884744 | tf_op jit(solution)/shard_map/ppermute | solution.py:440
  49.3 21.7 %collective-permute-start.12 = (bf16[2,64,1152]{2,1,0:T(8,128)(2,1)S(1)}, bf16[2,64,1152]{2,1,0:T(8,128)(2,1)S(1)}, u32[]{:S(2)}, u32[]{:S(2)}) collective-permute-start(bf16[2,64,1152]{2,1,0:T(8,128)(2,1)S(1)} %bitcast.23), channel_id=1, source_target_pairs={{0,12},{4,8},{8,4},{12,0},{1,13},{5,9},{9,5},{13,1},{2,14},{6,10},... | collective-permute-start | bytes 884744 | tf_op jit(solution)/shard_map/ppermute | solution.py:440
  49.5 10.7 %collective-permute-start.13 = (bf16[128,256]{1,0:T(8,128)(2,1)S(1)}, bf16[128,256]{1,0:T(8,128)(2,1)S(1)}, u32[]{:S(2)}, u32[]{:S(2)}) collective-permute-start(bf16[128,256]{1,0:T(8,128)(2,1)S(1)} %get-tuple-element.51), channel_id=1, source_target_pairs={{0,16},{16,0},{1,17},{17,1},{2,18},{18,2},{3,19},{19,3},{4,20},{20... | collective-permute-start | bytes 196616 | tf_op jit(solution)/shard_map/ppermute | solution.py:440
  61.7 16.2 %all-to-all-start.1 = ((bf16[16,64,128]{2,1,0:T(8,128)(2,1)}), bf16[16,64,128]{2,1,0:T(8,128)(2,1)S(1)}, u32[]{:S(2)}, u32[]{:S(2)}) async-start(bf16[16,64,128]{2,1,0:T(8,128)(2,1)} %bitcast.7), calls=%async_computation.1 | async-start | bytes 524288 | tf_op jit(solution)/shard_map/all_to_all | solution.py:436
  71.0 6.9 %copy-start.2 = (bf16[1,64,1024]{2,1,0:T(8,128)(2,1)S(1)}, bf16[1,64,1024]{2,1,0:T(8,128)(2,1)}, u32[]{:S(2)}) copy-start(bf16[1,64,1024]{2,1,0:T(8,128)(2,1)} %get-tuple-element.58.refs_0_) | copy-start | bytes 393220
  71.0 6.9 %copy-start.3 = (f32[128]{0:T(128)S(1)}, f32[128]{0:T(128)}, u32[]{:S(2)}) copy-start(f32[128]{0:T(128)} %param.12) | copy-start | bytes 1540
  71.1 1.6 %collective-permute-start.15 = (bf16[2,64,1152]{2,1,0:T(8,128)(2,1)S(1)}, bf16[2,64,1152]{2,1,0:T(8,128)(2,1)S(1)}, u32[]{:S(2)}, u32[]{:S(2)}) collective-permute-start(bf16[2,64,1152]{2,1,0:T(8,128)(2,1)S(1)} %bitcast.24), channel_id=1, source_target_pairs={{0,2},{2,0},{1,3},{3,1},{4,6},{6,4},{5,7},{7,5},{8,10},{10,8},{9,1... | collective-permute-start | bytes 884744 | tf_op jit(solution)/shard_map/ppermute | solution.py:440
  71.2 1.9 %collective-permute-start.16 = (bf16[2,64,1152]{2,1,0:T(8,128)(2,1)S(1)}, bf16[2,64,1152]{2,1,0:T(8,128)(2,1)S(1)}, u32[]{:S(2)}, u32[]{:S(2)}) collective-permute-start(bf16[2,64,1152]{2,1,0:T(8,128)(2,1)S(1)} %collective-permute-done.10.refs_1_), channel_id=1, source_target_pairs={{0,2},{2,0},{1,3},{3,1},{4,6},{6,4},{5,7},{7,5},{8,10},{10,8},{9,1... | collective-permute-start | bytes 884744 | tf_op jit(solution)/shard_map/ppermute | solution.py:440
  71.6 1.9 %collective-permute-start.17 = (bf16[2,64,1152]{2,1,0:T(8,128)(2,1)S(1)}, bf16[2,64,1152]{2,1,0:T(8,128)(2,1)S(1)}, u32[]{:S(2)}, u32[]{:S(2)}) collective-permute-start(bf16[2,64,1152]{2,1,0:T(8,128)(2,1)S(1)} %collective-permute-done.11.refs_2_), channel_id=1, source_target_pairs={{0,2},{2,0},{1,3},{3,1},{4,6},{6,4},{5,7},{7,5},{8,10},{10,8},{9,1... | collective-permute-start | bytes 884744 | tf_op jit(solution)/shard_map/ppermute | solution.py:440
  71.7 2.2 %collective-permute-start.18 = (bf16[2,64,1152]{2,1,0:T(8,128)(2,1)S(1)}, bf16[2,64,1152]{2,1,0:T(8,128)(2,1)S(1)}, u32[]{:S(2)}, u32[]{:S(2)}) collective-permute-start(bf16[2,64,1152]{2,1,0:T(8,128)(2,1)S(1)} %collective-permute-done.12.refs_3_), channel_id=1, source_target_pairs={{0,2},{2,0},{1,3},{3,1},{4,6},{6,4},{5,7},{7,5},{8,10},{10,8},{9,1... | collective-permute-start | bytes 884744 | tf_op jit(solution)/shard_map/ppermute | solution.py:440
  81.6 17.6 %copy-start = (bf16[1024,1024]{1,0:T(8,128)(2,1)S(1)}, bf16[1024,1024]{1,0:T(8,128)(2,1)}, u32[]{:S(2)}) copy-start(bf16[1024,1024]{1,0:T(8,128)(2,1)} %get-tuple-element.39.normed_any.normed_ref) | copy-start | bytes 6291460
  92.9 6.3 %collective-permute-start.19 = (bf16[128,256]{1,0:T(8,128)(2,1)S(1)}, bf16[128,256]{1,0:T(8,128)(2,1)S(1)}, u32[]{:S(2)}, u32[]{:S(2)}) collective-permute-start(bf16[128,256]{1,0:T(8,128)(2,1)S(1)} %get-tuple-element.61), channel_id=1, source_target_pairs={{0,16},{16,0},{1,17},{17,1},{2,18},{18,2},{3,19},{19,3},{4,20},{20... | collective-permute-start | bytes 196616 | tf_op jit(solution)/shard_map/ppermute | solution.py:440
  101.2 18.7 %all-to-all-start.3 = ((bf16[32,32,256]{2,1,0:T(8,128)(2,1)}), bf16[32,32,256]{2,1,0:T(8,128)(2,1)S(1)}, u32[]{:S(2)}, u32[]{:S(2)}) async-start(bf16[32,32,256]{2,1,0:T(8,128)(2,1)} %bitcast.11), calls=%async_computation.3 | async-start | bytes 1048576 | tf_op jit(solution)/shard_map/all_to_all | solution.py:436
  104.0 6.0 %collective-permute-start.20 = (f32[100,128]{1,0:T(8,128)S(1)}, f32[100,128]{1,0:T(8,128)S(1)}, u32[]{:S(2)}, u32[]{:S(2)}) collective-permute-start(f32[100,128]{1,0:T(8,128)S(1)} %get-tuple-element.64), channel_id=1, source_target_pairs={{0,1},{1,0},{2,3},{3,2},{4,5},{5,4},{6,7},{7,6},{8,9},{9,8},{10,11... | collective-permute-start | bytes 153608 | tf_op jit(solution)/shard_map/ppermute | solution.py:440

commit v15 on v13

--- a/solution.py
+++ b/solution.py
@@ -497,7 +497,7 @@
     )(neighbours, members.reshape(node_rows, LATENT_DIM))
 
     packed, normed = lax.optimization_barrier((in_order(packed, "half", 0), normed))
-    near = [normed, swap(normed, "quad", 1), None, swap(normed, "quad", 3)]
+    near = [normed, swap(normed, "quad", 1)]
     if paired:
         columns = exchange(columns.reshape(-1, shard, 3 * COLS), nodes)
         columns, late = lax.optimization_barrier((columns, normed))
@@ -506,7 +506,7 @@
         columns = [exchange(columns.reshape(-1, shard, 3 * COLS), everyone)]
         columns = [columns[0].reshape(LATENT_DIM, 3 * COLS)]
         late = normed
-    near[2] = swap(late, "quad", 2)
+    near += [swap(late, "quad", step) for step in range(2, QUAD)]
     far = [swap(piece, "core", 1) for piece in near]
     normed, steps = call(
         collect_kernel,
@@ -514,7 +514,6 @@
         [((rows, LATENT_DIM), BF16), ((GROUP, NOTE_ROWS, 128), F32)],
         "a" * (2 * QUAD),
         [pltpu.VMEM((GROUP, NOTE_ROWS, 128), BF16), pltpu.SemaphoreType.DMA((2 * GROUP,))],
-        moved=4 * 2**20,
         results="hv",
     )(*near, *far)
 

time: 110 us -> 115 us (1.045)
  waiting for transfers between devices: 33.9 us -> 39.1 us
    ppermute x21, waiting for transfers between devices: 18.9 us -> 22.6 us  [swap(): lax.ppermute(value, axis, [(i, i ^ step) for i in range(lax.axis_size(axi...]
    all_to_all x3, waiting for transfers between devices: 15 us -> 16.5 us  [exchange(): return lax.all_to_all(chunks, axes, 0, 0)]
    ppermute x21, starting transfers between devices: 22.7 us -> 21.5 us  [swap(): lax.ppermute(value, axis, [(i, i ^ step) for i in range(lax.axis_size(axi...]
  transfers between devices with their start and end apart: 24 -> 24, of which waited for: 8 -> 10; matrix products, arithmetic and copies ran while one was open for 2% -> 2% of each run, Pallas kernels for 15% -> 14%
where the time goes in v15:
time: 115 us; the launch traced here: 114 us
  waiting for transfers between devices  39.1 us (34%)
  starting transfers between devices  35.4 us (31%)
  Pallas kernels  25.9 us (23%)
  blocking collectives  11.2 us (10%)
    pallas_call x13, Pallas kernels, run(): made(*[pltpu.with_memory_space_constraint(arg, pltpu.HBM) if space == 'h'...  25.9 us
    ppermute x21, waiting for transfers between devices, swap(): lax.ppermute(value, axis, [(i, i ^ step) for i in range(lax.axis_size(axi...  22.6 us
    ppermute x21, starting transfers between devices, swap(): lax.ppermute(value, axis, [(i, i ^ step) for i in range(lax.axis_size(axi...  21.5 us
    all_to_all x3, waiting for transfers between devices, exchange(): return lax.all_to_all(chunks, axes, 0, 0)  16.5 us
    all_to_all x3, starting transfers between devices, exchange(): return lax.all_to_all(chunks, axes, 0, 0)  13.9 us
    all_to_all x1, blocking collectives, exchange(): return lax.all_to_all(chunks, axes, 0, 0)  11.2 us
  transfers between devices with their start and end apart: 24, of which 10 were waited for; matrix products, arithmetic and copies ran while one was open for 2% of the time, Pallas kernels for 14%

profile of v15, /device:TPU:1, one launch (start us, length us, event | category | flops | bytes accessed | tf_op | source)
XLA Modules:
  0.0 114.4 jit_solution(5901359516509178137)
XLA Ops:
  0.6 1.8 %prepare_weights.1 = (bf16[2,8,1,32,384]{4,3,2,1,0:T(8,128)(2,1)}, bf16[32,1152]{1,0:T(8,128)(2,1)}) custom-call(bf16[32,3072]{1,0:T(8,128)(2,1)} %w_any.1, bf16[32,1024]{1,0:T(8,128)(2,1)} %mix_any.1, bf16[32,100]{1,0:T(8,128)(2,1)} %readout_any.1), custom_call_target="tpu_custom_call" | custom-call | bytes 1048576 | tf_op jit(solution)/shard_map/prepare_weights/pallas_call | solution.py:63
  2.4 3.2 %collective-permute-start = (bf16[32,1152]{1,0:T(8,128)(2,1)}, bf16[32,1152]{1,0:T(8,128)(2,1)S(1)}, u32[]{:S(2)}, u32[]{:S(2)}) collective-permute-start(bf16[32,1152]{1,0:T(8,128)(2,1)} %get-tuple-element.31), channel_id=1, source_target_pairs={{0,16},{16,0},{1,17},{17,1},{2,18},{18,2},{3,19},{19,3},{4,20},{20... | collective-permute-start | bytes 221192 | tf_op jit(solution)/shard_map/ppermute | solution.py:440
  5.6 4.8 %all-to-all-start = ((bf16[16,32,384]{2,1,0:T(8,128)(2,1)}), bf16[16,32,384]{2,1,0:T(8,128)(2,1)S(1)}, u32[]{:S(2)}, u32[]{:S(2)}) async-start(bf16[16,32,384]{2,1,0:T(8,128)(2,1)} %bitcast.27), calls=%async_computation | async-start | bytes 786432 | tf_op jit(solution)/shard_map/all_to_all | solution.py:436
  10.4 1.9 %norm.1 = (bf16[144,1024]{1,0:T(8,128)(2,1)}, bf16[1,64,1024]{2,1,0:T(8,128)(2,1)}, bf16[1,64,1024]{2,1,0:T(8,128)(2,1)}) custom-call(s32[2,4]{1,0:T(2,128)} %near_any.1, bf16[128,1024]{1,0:T(8,128)(2,1)} %bitcast.28), custom_call_target="tpu_custom_call" | custom-call | flops 1048576 | bytes 1048576 | tf_op jit(solution)/shard_map/norm/pallas_call | solution.py:63
  12.3 0.9 select_bitcast_fusion.3
  13.3 1.5 %collective-permute-start.1 = (bf16[144,1024]{1,0:T(8,128)(2,1)}, bf16[144,1024]{1,0:T(8,128)(2,1)S(1)}, u32[]{:S(2)}, u32[]{:S(2)}) collective-permute-start(bf16[144,1024]{1,0:T(8,128)(2,1)} %get-tuple-element.35.refs_0_), channel_id=1, source_target_pairs={{0,4},{4,0},{8,12},{12,8},{1,5},{5,1},{9,13},{13,9},{2,6},{6,2},{1... | collective-permute-start | bytes 884744 | tf_op jit(solution)/shard_map/ppermute | solution.py:440
  14.7 7.6 %all-to-all-done.refs_0_ = bf16[16,32,384]{2,1,0:T(8,128)(2,1)S(1)} async-done(((bf16[16,32,384]{2,1,0:T(8,128)(2,1)}), bf16[16,32,384]{2,1,0:T(8,128)(2,1)S(1)}, u32[]{:S(2)}, u32[]{:S(2)}) %all-to-all-start) | async-done | bytes 393248 | tf_op jit(solution)/shard_map/all_to_all | solution.py:436
  22.3 1.0 collective-permute-start.2
  23.3 0.8 collective-permute-start.3
  24.0 1.2 %collective-permute-start.9 = (bf16[2,32,1152]{2,1,0:T(8,128)(2,1)S(1)}, bf16[2,32,1152]{2,1,0:T(8,128)(2,1)S(1)}, u32[]{:S(2)}, u32[]{:S(2)}) collective-permute-start(bf16[2,32,1152]{2,1,0:T(8,128)(2,1)S(1)} %pad_maximum_fusion.1), channel_id=1, source_target_pairs={{0,1},{1,0},{2,3},{3,2},{4,5},{5,4},{6,7},{7,6},{8,9},{9,8},{10,11... | collective-permute-start | bytes 442376 | tf_op jit(solution)/shard_map/ppermute | solution.py:440
  25.3 0.6 collective-permute-start.4
  25.8 3.3 %collective-permute-done.9 = bf16[2,32,1152]{2,1,0:T(8,128)(2,1)S(1)} collective-permute-done((bf16[2,32,1152]{2,1,0:T(8,128)(2,1)S(1)}, bf16[2,32,1152]{2,1,0:T(8,128)(2,1)S(1)}, u32[]{:S(2)}, u32[]{:S(2)}) %collective-permute-start.9) | collective-permute-done | bytes 147488 | tf_op jit(solution)/shard_map/ppermute | solution.py:440
  29.2 1.2 %collective-permute-start.8 = (bf16[16,32,384]{2,1,0:T(8,128)(2,1)S(1)}, bf16[16,32,384]{2,1,0:T(8,128)(2,1)S(1)}, u32[]{:S(2)}, u32[]{:S(2)}) collective-permute-start(bf16[16,32,384]{2,1,0:T(8,128)(2,1)S(1)} %all-to-all-done.refs_0_), channel_id=1, source_target_pairs={{0,1},{1,0},{2,3},{3,2},{4,5},{5,4},{6,7},{7,6},{8,9},{9,8},{10,11... | collective-permute-start | bytes 1179656 | tf_op jit(solution)/shard_map/ppermute | solution.py:440
  30.4 0.3 collective-permute-done.2.refs_2_
  30.7 2.1 %collective-permute-start.6 = (bf16[144,1024]{1,0:T(8,128)(2,1)S(1)}, bf16[144,1024]{1,0:T(8,128)(2,1)S(1)}, u32[]{:S(2)}, u32[]{:S(2)}) collective-permute-start(bf16[144,1024]{1,0:T(8,128)(2,1)S(1)} %collective-permute-done.2.refs_2_), channel_id=1, source_target_pairs={{0,2},{2,0},{1,3},{3,1},{4,6},{6,4},{5,7},{7,5},{8,10},{10,8},{9,1... | collective-permute-start | bytes 884744 | tf_op jit(solution)/shard_map/ppermute | solution.py:440
  32.8 5.1 %collective-permute-done.3.refs_3_ = bf16[144,1024]{1,0:T(8,128)(2,1)S(1)} collective-permute-done((bf16[144,1024]{1,0:T(8,128)(2,1)}, bf16[144,1024]{1,0:T(8,128)(2,1)S(1)}, u32[]{:S(2)}, u32[]{:S(2)}) %collective-permute-start.3) | collective-permute-done | bytes 294944 | tf_op jit(solution)/shard_map/ppermute | solution.py:440
  37.9 0.6 collective-permute-start.7
  38.7 1.0 collective-permute-start.10
  39.6 1.0 collective-permute-start.11
  40.6 0.8 collective-permute-start.12
  41.4 1.5 %collect.1 = (bf16[1024,1024]{1,0:T(8,128)(2,1)}, f32[8,16,128]{2,1,0:T(8,128)S(1)}) custom-call(bf16[144,1024]{1,0:T(8,128)(2,1)S(1)} %copy-done.1, bf16[144,1024]{1,0:T(8,128)(2,1)S(1)} %collective-permute-done.1.refs_1_, bf16[144,1024]{1,0:T(8,128)(2,1)S(1)} %collective-permute-done.2.refs_2_, bf16[144,1024]{1,0:T(8,128)(2,1)S(1)} %collective-permute-done.3.refs_3_, ...), custom_call_target="tpu_custom_call" | custom-call | tf_op jit(solution)/shard_map/collect/pallas_call | solution.py:63
  42.9 1.3 %project_rims.1 = (bf16[16,2,32,384]{3,2,1,0:T(8,128)(2,1)S(1)}, bf16[128,256]{1,0:T(8,128)(2,1)S(1)}) custom-call(bf16[1024,1024]{1,0:T(8,128)(2,1)} %get-tuple-element.36.normed_any.normed_ref, bf16[16,32,384]{2,1,0:T(8,128)(2,1)S(1)} %all-to-all-done.refs_0_, bf16[16,32,384]{2,1,0:T(8,128)(2,1)S(1)} %collective-permute-done.8.refs_1_), custom_call_target="tpu_custom_call" | custom-call | flops 67108864 | bytes 1048576 | tf_op jit(solution)/shard_map/project_rims/pallas_call | solution.py:63
  44.2 0.8 collective-permute-start.13
  45.1 2.8 %project.1 = (bf16[1024,128]{1,0:T(8,128)(2,1)S(1)}, bf16[1024,256]{1,0:T(8,128)(2,1)S(1)}) custom-call(bf16[1024,1024]{1,0:T(8,128)(2,1)} %get-tuple-element.36.normed_any.normed_ref, bf16[16,2,32,384]{3,2,1,0:T(8,128)(2,1)S(1)} %get-tuple-element.41.w_ref), custom_call_target="tpu_custom_call" | custom-call | flops 805306368 | bytes 4194304 | tf_op jit(solution)/shard_map/project/pallas_call | solution.py:63
  47.9 1.9 %attention_interior.1.done_ref = bf16[1024,128]{1,0:T(8,128)(2,1)S(1)} custom-call(f32[8,16,128]{2,1,0:T(8,128)S(1)} %get-tuple-element.37.steps_ref, bf16[1024,128]{1,0:T(8,128)(2,1)S(1)} %get-tuple-element.42.q_ref, bf16[1024,256]{1,0:T(8,128)(2,1)S(1)} %get-tuple-element.46.kv_ref), custom_call_target="tpu_custom_call" | custom-call | flops 268435456 | bytes 2097152 | tf_op jit(solution)/shard_map/attention_interior/pallas_call | solution.py:63
  49.8 4.6 %collective-permute-done.13.low_ref.high_ref = bf16[128,256]{1,0:T(8,128)(2,1)S(1)} collective-permute-done((bf16[128,256]{1,0:T(8,128)(2,1)S(1)}, bf16[128,256]{1,0:T(8,128)(2,1)S(1)}, u32[]{:S(2)}, u32[]{:S(2)}) %collective-permute-start.13) | collective-permute-done | bytes 65568 | tf_op jit(solution)/shard_map/ppermute | solution.py:440
  54.5 1.4 %attention_edges.1 = bf16[1024,128]{1,0:T(8,128)(2,1)} custom-call(f32[8,16,128]{2,1,0:T(8,128)S(1)} %get-tuple-element.37.steps_ref, bf16[1024,128]{1,0:T(8,128)(2,1)S(1)} %get-tuple-element.42.q_ref, bf16[1024,256]{1,0:T(8,128)(2,1)S(1)} %get-tuple-element.46.kv_ref, bf16[128,256]{1,0:T(8,128)(2,1)S(1)} %collective-permute-done.13.low_ref.high_ref, ...), custom_call_target="tpu_custom_call" | custom-call | flops 67108864 | bytes 1048576 | tf_op jit(solution)/shard_map/attention_edges/pallas_call | solution.py:63
  55.9 5.8 %all-to-all-start.1 = ((bf16[16,64,128]{2,1,0:T(8,128)(2,1)}), bf16[16,64,128]{2,1,0:T(8,128)(2,1)S(1)}, u32[]{:S(2)}, u32[]{:S(2)}) async-start(bf16[16,64,128]{2,1,0:T(8,128)(2,1)} %bitcast.7), calls=%async_computation.1 | async-start | bytes 524288 | tf_op jit(solution)/shard_map/all_to_all | solution.py:436
  61.7 0.2 collective-permute-start.14
  61.9 0.4 collective-permute-start.15
  62.4 0.4 collective-permute-start.17
  62.8 1.4 %collective-permute-start.18 = (bf16[1,64,1024]{2,1,0:T(8,128)(2,1)S(1)}, bf16[1,64,1024]{2,1,0:T(8,128)(2,1)S(1)}, u32[]{:S(2)}, u32[]{:S(2)}) collective-permute-start(bf16[1,64,1024]{2,1,0:T(8,128)(2,1)S(1)} %copy-done.4), channel_id=1, source_target_pairs={{0,1},{1,0},{2,3},{3,2},{4,5},{5,4},{6,7},{7,6},{8,9},{9,8},{10,11... | collective-permute-start | bytes 393224 | tf_op jit(solution)/shard_map/ppermute | solution.py:440
  64.2 0.4 collective-permute-done.17.refs_7_
  64.7 1.5 %assemble.1.w_any = bf16[2,4,2,64,1152]{4,3,2,1,0:T(8,128)(2,1)} custom-call(bf16[2,64,1152]{2,1,0:T(8,128)(2,1)S(1)} %bitcast.25, bf16[2,64,1152]{2,1,0:T(8,128)(2,1)S(1)} %collective-permute-done.10.refs_1_, bf16[2,64,1152]{2,1,0:T(8,128)(2,1)S(1)} %collective-permute-done.11.refs_2_, bf16[2,64,1152]{2,1,0:T(8,128)(2,1)S(1)} %collective-permute-done.12.refs_3_, ...), custom_call_target="tpu_custom_call" | custom-call | bytes 4194304 | tf_op jit(solution)/shard_map/assemble/pallas_call | solution.py:63
  66.1 3.6 %collective-permute-done.18.refs_1_ = bf16[1,64,1024]{2,1,0:T(8,128)(2,1)S(1)} collective-permute-done((bf16[1,64,1024]{2,1,0:T(8,128)(2,1)S(1)}, bf16[1,64,1024]{2,1,0:T(8,128)(2,1)S(1)}, u32[]{:S(2)}, u32[]{:S(2)}) %collective-permute-start.18) | collective-permute-done | bytes 131104 | tf_op jit(solution)/shard_map/ppermute | solution.py:440
  69.8 3.7 %mix_loss_backward.1 = (f32[100,128]{1,0:T(8,128)S(1)}, bf16[16,64,128]{2,1,0:T(8,128)(2,1)S(1)}) custom-call(bf16[16,64,128]{2,1,0:T(8,128)(2,1)S(1)} %all-to-all-done.1.att_ref, f32[1,128]{1,0:T(1,128)S(1)} %bitcast.26, f32[100,128]{1,0:T(8,128)} %truth_any.1, bf16[2,4,2,64,1152]{4,3,2,1,0:T(8,128)(2,1)} %assemble.1.w_any, ...), custom_call_target="tpu_custom_call" | custom-call | flops 603979776 | bytes 4194304 | tf_op jit(solution)/shard_map/mix_loss_backward/pallas_call | solution.py:63
  73.5 11.2 %all_to_all.20 = bf16[16,64,128]{2,1,0:T(8,128)(2,1)S(1)} all-to-all(bf16[16,64,128]{2,1,0:T(8,128)(2,1)S(1)} %get-tuple-element.54), channel_id=1, replica_groups=mesh['half'=2,'quad'=4,'core'=2,'ens'=2] {'quad','core','ens'}, dimensions={0} | all-to-all | bytes 524288 | tf_op jit(solution)/shard_map/all_to_all | solution.py:436
  84.7 1.4 %attention_edges_back.1 = (f32[2,256,256]{2,1,0:T(8,128)S(1)}, bf16[128,256]{1,0:T(8,128)(2,1)S(1)}) custom-call(f32[8,16,128]{2,1,0:T(8,128)S(1)} %get-tuple-element.37.steps_ref, bf16[1024,128]{1,0:T(8,128)(2,1)S(1)} %get-tuple-element.42.q_ref, bf16[1024,256]{1,0:T(8,128)(2,1)S(1)} %get-tuple-element.46.kv_ref, ...), custom_call_target="tpu_custom_call" | custom-call | flops 167772160 | bytes 1048576 | tf_op jit(solution)/shard_map/attention_edges_back/pallas_call | solution.py:63
  86.1 1.9 %collective-permute-start.19 = (bf16[128,256]{1,0:T(8,128)(2,1)S(1)}, bf16[128,256]{1,0:T(8,128)(2,1)S(1)}, u32[]{:S(2)}, u32[]{:S(2)}) collective-permute-start(bf16[128,256]{1,0:T(8,128)(2,1)S(1)} %get-tuple-element.55), channel_id=1, source_target_pairs={{0,16},{16,0},{1,17},{17,1},{2,18},{18,2},{3,19},{19,3},{4,20},{20... | collective-permute-start | bytes 196616 | tf_op jit(solution)/shard_map/ppermute | solution.py:440
  88.0 3.9 %attention_interior_back.1.grads_ref = f32[1024,256]{1,0:T(8,128)S(1)} custom-call(f32[8,16,128]{2,1,0:T(8,128)S(1)} %get-tuple-element.37.steps_ref, bf16[1024,128]{1,0:T(8,128)(2,1)S(1)} %get-tuple-element.42.q_ref, bf16[1024,256]{1,0:T(8,128)(2,1)S(1)} %get-tuple-element.46.kv_ref, bf16[1024,128]{1,0:T(8,128)(2,1)S(1)} %bitcast.19, ...), custom_call_target="tpu_custom_call" | custom-call | flops 536870912 | bytes 4194304 | tf_op jit(solution)/shard_map/attention_interior_back/pallas_call | solution.py:63
  91.9 0.6 collective-permute-done.19.from_low_ref.from_high_ref
  92.5 2.1 %product.1 = bf16[1024,256]{1,0:T(8,128)(2,1)} custom-call(bf16[1024,1024]{1,0:T(8,128)(2,1)S(1)} %copy-done, bf16[128,256]{1,0:T(8,128)(2,1)S(1)} %collective-permute-done.19.from_low_ref.from_high_ref, bf16[128,256]{1,0:T(8,128)(2,1)S(1)} %collective-permute-done.19.from_low_ref.from_high_ref, f32[1024,256]{1,0:T(8,128)S(1)} %attention_interior_back.1.grads_ref), custom_call_target="tpu_custom_call" | custom-call | flops 1073741824 | bytes 4194304 | tf_op jit(solution)/shard_map/product/pallas_call | solution.py:63
  94.5 3.3 %all-to-all-start.3 = ((bf16[32,32,256]{2,1,0:T(8,128)(2,1)}), bf16[32,32,256]{2,1,0:T(8,128)(2,1)S(1)}, u32[]{:S(2)}, u32[]{:S(2)}) async-start(bf16[32,32,256]{2,1,0:T(8,128)(2,1)} %bitcast.11), calls=%async_computation.3 | async-start | bytes 1048576 | tf_op jit(solution)/shard_map/all_to_all | solution.py:436
  97.8 1.5 %collective-permute-start.20 = (f32[100,128]{1,0:T(8,128)S(1)}, f32[100,128]{1,0:T(8,128)S(1)}, u32[]{:S(2)}, u32[]{:S(2)}) collective-permute-start(f32[100,128]{1,0:T(8,128)S(1)} %get-tuple-element.58), channel_id=1, source_target_pairs={{0,1},{1,0},{2,3},{3,2},{4,5},{5,4},{6,7},{7,6},{8,9},{9,8},{10,11... | collective-permute-start | bytes 153608 | tf_op jit(solution)/shard_map/ppermute | solution.py:440
  99.3 4.5 %collective-permute-done.20 = f32[100,128]{1,0:T(8,128)S(1)} collective-permute-done((f32[100,128]{1,0:T(8,128)S(1)}, f32[100,128]{1,0:T(8,128)S(1)}, u32[]{:S(2)}, u32[]{:S(2)}) %collective-permute-start.20) | collective-permute-done | bytes 51232 | tf_op jit(solution)/shard_map/ppermute | solution.py:440
  104.0 0.7 copy.10
  104.7 9.0 %all-to-all-done.3 = bf16[32,32,256]{2,1,0:T(8,128)(2,1)S(1)} async-done(((bf16[32,32,256]{2,1,0:T(8,128)(2,1)}), bf16[32,32,256]{2,1,0:T(8,128)(2,1)S(1)}, u32[]{:S(2)}, u32[]{:S(2)}) %all-to-all-start.3) | async-done | bytes 524320 | tf_op jit(solution)/shard_map/all_to_all | solution.py:436
  113.7 0.8 gather_sums.1
  (34 shorter events, 0.5 us)
Async XLA Ops:
  2.4 9.9 %collective-permute-start = (bf16[32,1152]{1,0:T(8,128)(2,1)}, bf16[32,1152]{1,0:T(8,128)(2,1)S(1)}, u32[]{:S(2)}, u32[]{:S(2)}) collective-permute-start(bf16[32,1152]{1,0:T(8,128)(2,1)} %get-tuple-element.31), channel_id=1, source_target_pairs={{0,16},{16,0},{1,17},{17,1},{2,18},{18,2},{3,19},{19,3},{4,20},{20... | collective-permute-start | bytes 221192 | tf_op jit(solution)/shard_map/ppermute | solution.py:440
  5.6 16.7 %all-to-all-start = ((bf16[16,32,384]{2,1,0:T(8,128)(2,1)}), bf16[16,32,384]{2,1,0:T(8,128)(2,1)S(1)}, u32[]{:S(2)}, u32[]{:S(2)}) async-start(bf16[16,32,384]{2,1,0:T(8,128)(2,1)} %bitcast.27), calls=%async_computation | async-start | bytes 786432 | tf_op jit(solution)/shard_map/all_to_all | solution.py:436
  12.3 29.1 %copy-start.1 = (bf16[144,1024]{1,0:T(8,128)(2,1)S(1)}, bf16[144,1024]{1,0:T(8,128)(2,1)}, u32[]{:S(2)}) copy-start(bf16[144,1024]{1,0:T(8,128)(2,1)} %get-tuple-element.35.refs_0_) | copy-start | bytes 884740
  13.3 12.6 %collective-permute-start.1 = (bf16[144,1024]{1,0:T(8,128)(2,1)}, bf16[144,1024]{1,0:T(8,128)(2,1)S(1)}, u32[]{:S(2)}, u32[]{:S(2)}) collective-permute-start(bf16[144,1024]{1,0:T(8,128)(2,1)} %get-tuple-element.35.refs_0_), channel_id=1, source_target_pairs={{0,4},{4,0},{8,12},{12,8},{1,5},{5,1},{9,13},{13,9},{2,6},{6,2},{1... | collective-permute-start | bytes 884744 | tf_op jit(solution)/shard_map/ppermute | solution.py:440
  22.3 8.4 %collective-permute-start.2 = (bf16[144,1024]{1,0:T(8,128)(2,1)}, bf16[144,1024]{1,0:T(8,128)(2,1)S(1)}, u32[]{:S(2)}, u32[]{:S(2)}) collective-permute-start(bf16[144,1024]{1,0:T(8,128)(2,1)} %get-tuple-element.35.refs_0_), channel_id=1, source_target_pairs={{0,8},{4,12},{8,0},{12,4},{1,9},{5,13},{9,1},{13,5},{2,10},{6,14},... | collective-permute-start | bytes 884744 | tf_op jit(solution)/shard_map/ppermute | solution.py:440
  23.3 14.7 %collective-permute-start.3 = (bf16[144,1024]{1,0:T(8,128)(2,1)}, bf16[144,1024]{1,0:T(8,128)(2,1)S(1)}, u32[]{:S(2)}, u32[]{:S(2)}) collective-permute-start(bf16[144,1024]{1,0:T(8,128)(2,1)} %get-tuple-element.35.refs_0_), channel_id=1, source_target_pairs={{0,12},{4,8},{8,4},{12,0},{1,13},{5,9},{9,5},{13,1},{2,14},{6,10},... | collective-permute-start | bytes 884744 | tf_op jit(solution)/shard_map/ppermute | solution.py:440
  24.0 5.1 %collective-permute-start.9 = (bf16[2,32,1152]{2,1,0:T(8,128)(2,1)S(1)}, bf16[2,32,1152]{2,1,0:T(8,128)(2,1)S(1)}, u32[]{:S(2)}, u32[]{:S(2)}) collective-permute-start(bf16[2,32,1152]{2,1,0:T(8,128)(2,1)S(1)} %pad_maximum_fusion.1), channel_id=1, source_target_pairs={{0,1},{1,0},{2,3},{3,2},{4,5},{5,4},{6,7},{7,6},{8,9},{9,8},{10,11... | collective-permute-start | bytes 442376 | tf_op jit(solution)/shard_map/ppermute | solution.py:440
  25.3 13.4 %collective-permute-start.4 = (bf16[144,1024]{1,0:T(8,128)(2,1)}, bf16[144,1024]{1,0:T(8,128)(2,1)S(1)}, u32[]{:S(2)}, u32[]{:S(2)}) collective-permute-start(bf16[144,1024]{1,0:T(8,128)(2,1)} %get-tuple-element.35.refs_0_), channel_id=1, source_target_pairs={{0,2},{2,0},{1,3},{3,1},{4,6},{6,4},{5,7},{7,5},{8,10},{10,8},{9,1... | collective-permute-start | bytes 884744 | tf_op jit(solution)/shard_map/ppermute | solution.py:440
  25.8 13.8 %collective-permute-start.5 = (bf16[144,1024]{1,0:T(8,128)(2,1)S(1)}, bf16[144,1024]{1,0:T(8,128)(2,1)S(1)}, u32[]{:S(2)}, u32[]{:S(2)}) collective-permute-start(bf16[144,1024]{1,0:T(8,128)(2,1)S(1)} %collective-permute-done.1.refs_1_), channel_id=1, source_target_pairs={{0,2},{2,0},{1,3},{3,1},{4,6},{6,4},{5,7},{7,5},{8,10},{10,8},{9,1... | collective-permute-start | bytes 884744 | tf_op jit(solution)/shard_map/ppermute | solution.py:440
  29.2 13.7 %collective-permute-start.8 = (bf16[16,32,384]{2,1,0:T(8,128)(2,1)S(1)}, bf16[16,32,384]{2,1,0:T(8,128)(2,1)S(1)}, u32[]{:S(2)}, u32[]{:S(2)}) collective-permute-start(bf16[16,32,384]{2,1,0:T(8,128)(2,1)S(1)} %all-to-all-done.refs_0_), channel_id=1, source_target_pairs={{0,1},{1,0},{2,3},{3,2},{4,5},{5,4},{6,7},{7,6},{8,9},{9,8},{10,11... | collective-permute-start | bytes 1179656 | tf_op jit(solution)/shard_map/ppermute | solution.py:440
  30.7 10.0 %collective-permute-start.6 = (bf16[144,1024]{1,0:T(8,128)(2,1)S(1)}, bf16[144,1024]{1,0:T(8,128)(2,1)S(1)}, u32[]{:S(2)}, u32[]{:S(2)}) collective-permute-start(bf16[144,1024]{1,0:T(8,128)(2,1)S(1)} %collective-permute-done.2.refs_2_), channel_id=1, source_target_pairs={{0,2},{2,0},{1,3},{3,1},{4,6},{6,4},{5,7},{7,5},{8,10},{10,8},{9,1... | collective-permute-start | bytes 884744 | tf_op jit(solution)/shard_map/ppermute | solution.py:440
  37.9 3.4 %collective-permute-start.7 = (bf16[144,1024]{1,0:T(8,128)(2,1)S(1)}, bf16[144,1024]{1,0:T(8,128)(2,1)S(1)}, u32[]{:S(2)}, u32[]{:S(2)}) collective-permute-start(bf16[144,1024]{1,0:T(8,128)(2,1)S(1)} %collective-permute-done.3.refs_3_), channel_id=1, source_target_pairs={{0,2},{2,0},{1,3},{3,1},{4,6},{6,4},{5,7},{7,5},{8,10},{10,8},{9,1... | collective-permute-start | bytes 884744 | tf_op jit(solution)/shard_map/ppermute | solution.py:440
  38.7 23.1 %collective-permute-start.10 = (bf16[2,64,1152]{2,1,0:T(8,128)(2,1)S(1)}, bf16[2,64,1152]{2,1,0:T(8,128)(2,1)S(1)}, u32[]{:S(2)}, u32[]{:S(2)}) collective-permute-start(bf16[2,64,1152]{2,1,0:T(8,128)(2,1)S(1)} %bitcast.21), channel_id=1, source_target_pairs={{0,4},{4,0},{8,12},{12,8},{1,5},{5,1},{9,13},{13,9},{2,6},{6,2},{1... | collective-permute-start | bytes 884744 | tf_op jit(solution)/shard_map/ppermute | solution.py:440
  39.6 22.1 %collective-permute-start.11 = (bf16[2,64,1152]{2,1,0:T(8,128)(2,1)S(1)}, bf16[2,64,1152]{2,1,0:T(8,128)(2,1)S(1)}, u32[]{:S(2)}, u32[]{:S(2)}) collective-permute-start(bf16[2,64,1152]{2,1,0:T(8,128)(2,1)S(1)} %bitcast.22), channel_id=1, source_target_pairs={{0,8},{4,12},{8,0},{12,4},{1,9},{5,13},{9,1},{13,5},{2,10},{6,14},... | collective-permute-start | bytes 884744 | tf_op jit(solution)/shard_map/ppermute | solution.py:440
  40.6 21.1 %collective-permute-start.12 = (bf16[2,64,1152]{2,1,0:T(8,128)(2,1)S(1)}, bf16[2,64,1152]{2,1,0:T(8,128)(2,1)S(1)}, u32[]{:S(2)}, u32[]{:S(2)}) collective-permute-start(bf16[2,64,1152]{2,1,0:T(8,128)(2,1)S(1)} %bitcast.23), channel_id=1, source_target_pairs={{0,12},{4,8},{8,4},{12,0},{1,13},{5,9},{9,5},{13,1},{2,14},{6,10},... | collective-permute-start | bytes 884744 | tf_op jit(solution)/shard_map/ppermute | solution.py:440
  44.2 18.6 %copy-start.4 = (bf16[1,64,1024]{2,1,0:T(8,128)(2,1)S(1)}, bf16[1,64,1024]{2,1,0:T(8,128)(2,1)}, u32[]{:S(2)}) copy-start(bf16[1,64,1024]{2,1,0:T(8,128)(2,1)} %get-tuple-element.53) | copy-start | bytes 393220
  44.2 10.2 %collective-permute-start.13 = (bf16[128,256]{1,0:T(8,128)(2,1)S(1)}, bf16[128,256]{1,0:T(8,128)(2,1)S(1)}, u32[]{:S(2)}, u32[]{:S(2)}) collective-permute-start(bf16[128,256]{1,0:T(8,128)(2,1)S(1)} %get-tuple-element.47), channel_id=1, source_target_pairs={{0,16},{16,0},{1,17},{17,1},{2,18},{18,2},{3,19},{19,3},{4,20},{20... | collective-permute-start | bytes 196616 | tf_op jit(solution)/shard_map/ppermute | solution.py:440
  55.9 13.9 %all-to-all-start.1 = ((bf16[16,64,128]{2,1,0:T(8,128)(2,1)}), bf16[16,64,128]{2,1,0:T(8,128)(2,1)S(1)}, u32[]{:S(2)}, u32[]{:S(2)}) async-start(bf16[16,64,128]{2,1,0:T(8,128)(2,1)} %bitcast.7), calls=%async_computation.1 | async-start | bytes 524288 | tf_op jit(solution)/shard_map/all_to_all | solution.py:436
  61.7 8.1 %copy-start.2 = (bf16[1,64,1024]{2,1,0:T(8,128)(2,1)S(1)}, bf16[1,64,1024]{2,1,0:T(8,128)(2,1)}, u32[]{:S(2)}) copy-start(bf16[1,64,1024]{2,1,0:T(8,128)(2,1)} %get-tuple-element.52.refs_0_) | copy-start | bytes 393220
  61.7 8.1 %copy-start.3 = (f32[128]{0:T(128)S(1)}, f32[128]{0:T(128)}, u32[]{:S(2)}) copy-start(f32[128]{0:T(128)} %param.12) | copy-start | bytes 1540
  61.7 2.5 %collective-permute-start.14 = (bf16[2,64,1152]{2,1,0:T(8,128)(2,1)S(1)}, bf16[2,64,1152]{2,1,0:T(8,128)(2,1)S(1)}, u32[]{:S(2)}, u32[]{:S(2)}) collective-permute-start(bf16[2,64,1152]{2,1,0:T(8,128)(2,1)S(1)} %bitcast.24), channel_id=1, source_target_pairs={{0,2},{2,0},{1,3},{3,1},{4,6},{6,4},{5,7},{7,5},{8,10},{10,8},{9,1... | collective-permute-start | bytes 884744 | tf_op jit(solution)/shard_map/ppermute | solution.py:440
  61.9 2.3 %collective-permute-start.15 = (bf16[2,64,1152]{2,1,0:T(8,128)(2,1)S(1)}, bf16[2,64,1152]{2,1,0:T(8,128)(2,1)S(1)}, u32[]{:S(2)}, u32[]{:S(2)}) collective-permute-start(bf16[2,64,1152]{2,1,0:T(8,128)(2,1)S(1)} %collective-permute-done.10.refs_1_), channel_id=1, source_target_pairs={{0,2},{2,0},{1,3},{3,1},{4,6},{6,4},{5,7},{7,5},{8,10},{10,8},{9,1... | collective-permute-start | bytes 884744 | tf_op jit(solution)/shard_map/ppermute | solution.py:440
  62.3 1.9 %collective-permute-start.16 = (bf16[2,64,1152]{2,1,0:T(8,128)(2,1)S(1)}, bf16[2,64,1152]{2,1,0:T(8,128)(2,1)S(1)}, u32[]{:S(2)}, u32[]{:S(2)}) collective-permute-start(bf16[2,64,1152]{2,1,0:T(8,128)(2,1)S(1)} %collective-permute-done.11.refs_2_), channel_id=1, source_target_pairs={{0,2},{2,0},{1,3},{3,1},{4,6},{6,4},{5,7},{7,5},{8,10},{10,8},{9,1... | collective-permute-start | bytes 884744 | tf_op jit(solution)/shard_map/ppermute | solution.py:440
  62.4 2.2 %collective-permute-start.17 = (bf16[2,64,1152]{2,1,0:T(8,128)(2,1)S(1)}, bf16[2,64,1152]{2,1,0:T(8,128)(2,1)S(1)}, u32[]{:S(2)}, u32[]{:S(2)}) collective-permute-start(bf16[2,64,1152]{2,1,0:T(8,128)(2,1)S(1)} %collective-permute-done.12.refs_3_), channel_id=1, source_target_pairs={{0,2},{2,0},{1,3},{3,1},{4,6},{6,4},{5,7},{7,5},{8,10},{10,8},{9,1... | collective-permute-start | bytes 884744 | tf_op jit(solution)/shard_map/ppermute | solution.py:440
  62.8 6.9 %collective-permute-start.18 = (bf16[1,64,1024]{2,1,0:T(8,128)(2,1)S(1)}, bf16[1,64,1024]{2,1,0:T(8,128)(2,1)S(1)}, u32[]{:S(2)}, u32[]{:S(2)}) collective-permute-start(bf16[1,64,1024]{2,1,0:T(8,128)(2,1)S(1)} %copy-done.4), channel_id=1, source_target_pairs={{0,1},{1,0},{2,3},{3,2},{4,5},{5,4},{6,7},{7,6},{8,9},{9,8},{10,11... | collective-permute-start | bytes 393224 | tf_op jit(solution)/shard_map/ppermute | solution.py:440
  73.5 18.9 %copy-start = (bf16[1024,1024]{1,0:T(8,128)(2,1)S(1)}, bf16[1024,1024]{1,0:T(8,128)(2,1)}, u32[]{:S(2)}) copy-start(bf16[1024,1024]{1,0:T(8,128)(2,1)} %get-tuple-element.36.normed_any.normed_ref) | copy-start | bytes 6291460
  86.1 6.3 %collective-permute-start.19 = (bf16[128,256]{1,0:T(8,128)(2,1)S(1)}, bf16[128,256]{1,0:T(8,128)(2,1)S(1)}, u32[]{:S(2)}, u32[]{:S(2)}) collective-permute-start(bf16[128,256]{1,0:T(8,128)(2,1)S(1)} %get-tuple-element.55), channel_id=1, source_target_pairs={{0,16},{16,0},{1,17},{17,1},{2,18},{18,2},{3,19},{19,3},{4,20},{20... | collective-permute-start | bytes 196616 | tf_op jit(solution)/shard_map/ppermute | solution.py:440
  94.5 19.1 %all-to-all-start.3 = ((bf16[32,32,256]{2,1,0:T(8,128)(2,1)}), bf16[32,32,256]{2,1,0:T(8,128)(2,1)S(1)}, u32[]{:S(2)}, u32[]{:S(2)}) async-start(bf16[32,32,256]{2,1,0:T(8,128)(2,1)} %bitcast.11), calls=%async_computation.3 | async-start | bytes 1048576 | tf_op jit(solution)/shard_map/all_to_all | solution.py:436
  97.8 6.0 %collective-permute-start.20 = (f32[100,128]{1,0:T(8,128)S(1)}, f32[100,128]{1,0:T(8,128)S(1)}, u32[]{:S(2)}, u32[]{:S(2)}) collective-permute-start(f32[100,128]{1,0:T(8,128)S(1)} %get-tuple-element.58), channel_id=1, source_target_pairs={{0,1},{1,0},{2,3},{3,2},{4,5},{5,4},{6,7},{7,6},{8,9},{9,8},{10,11... | collective-permute-start | bytes 153608 | tf_op jit(solution)/shard_map/ppermute | solution.py:440

commit v16 on v13

--- a/solution.py
+++ b/solution.py
@@ -202,12 +202,17 @@
 
 
 def assemble_kernel(*refs):
-    pieces, (w_any, sems) = refs[:GROUP], refs[GROUP:]
-    core, quad = lax.axis_index("core"), lax.axis_index("quad")
-    pairs = [
-        (piece, w_any.at[:, quad ^ (at % QUAD), core ^ (at // QUAD)])
-        for at, piece in enumerate(pieces)
-    ]
+    pieces, (w_any, sems) = refs[:-2], refs[-2:]
+    core, quad, ens = (lax.axis_index(axis) for axis in ("core", "quad", "ens"))
+    pairs = []
+    for at, piece in enumerate(pieces):
+        if len(pieces) == GROUP:
+            pairs.append((piece, w_any.at[:, quad ^ (at % QUAD), core ^ (at // QUAD), 0]))
+        else:
+            pairs += [
+                (piece.at[step], w_any.at[:, quad ^ step, core ^ (at // 2), ens ^ (at % 2)])
+                for step in range(QUAD)
+            ]
     wait(fetch(pairs, sems))
 
 
@@ -518,8 +523,9 @@
         results="hv",
     )(*near, *far)
 
-    packed = in_order(packed, "ens", 1).reshape(halves, members_num * shard, width)
-    packed, near[2] = lax.optimization_barrier((packed, near[2]))
+    if not paired:
+        packed = in_order(packed, "ens", 1).reshape(halves, members_num * shard, width)
+    packed, near[3] = lax.optimization_barrier((packed, near[3]))
     pieces = [packed] + [swap(packed, "quad", step) for step in range(1, QUAD)]
 
     rim = ((RIM, 2 * COLS), BF16)
@@ -540,6 +546,10 @@
             return got, got
         return lax.ppermute(inner[1], "half", up), lax.ppermute(inner[0], "half", down)
 
+    if paired:
+        pieces = jnp.stack(pieces)
+        weights, pieces = lax.optimization_barrier((weights, pieces))
+        pieces = [pieces, swap(pieces, "ens", 1)]
     weights, sources[-1] = lax.optimization_barrier((weights, sources[-1]))
     sources = [sources[0], swap(sources[1], "ens", 1)] if paired else [exchange(sources[0], "ens")]
     low, high = across(inner)
@@ -574,13 +584,13 @@
     *pieces, own = lax.optimization_barrier((*pieces, own))
     pieces = pieces + [swap(piece, "core", 1) for piece in pieces]
     attended = exchange(outcome.reshape(GROUP * members_num, part, COLS), ("quad", "core", "ens"))
-    block = (halves, QUAD, CORES, members_num * shard, width)
+    block = (halves, QUAD, CORES) + ((2, shard) if paired else (1, members_num * shard)) + (width,)
     (weights,) = call(
         assemble_kernel,
         "assemble",
         [(block, BF16)],
         "a" * len(pieces),
-        [pltpu.SemaphoreType.DMA((GROUP,))],
+        [pltpu.SemaphoreType.DMA((2 * GROUP,))],
         moved=4 * 2**20,
         results="h",
     )(*pieces)

time: 110 us -> 129 us (1.17)
  waiting for transfers between devices: 33.9 us -> 48.2 us
  local copies, waits for them, and re-layouts: 0.8 us -> 4.18 us
    ppermute x21 -> x19, waiting for transfers between devices: 18.9 us -> 33.3 us  [swap(): lax.ppermute(value, axis, [(i, i ^ step) for i in range(lax.axis_size(axi...]
    unnamed x11 -> x13, local copies, waits for them, and re-layouts: 0.7 us -> 4.1 us
    ppermute x21 -> x19, starting transfers between devices: 22.7 us -> 24.1 us  [swap(): lax.ppermute(value, axis, [(i, i ^ step) for i in range(lax.axis_size(axi...]
  transfers between devices with their start and end apart: 24 -> 22, of which waited for: 8 -> 13; matrix products, arithmetic and copies ran while one was open for 2% -> 1% of each run, Pallas kernels for 15% -> 12%
where the time goes in v16:
time: 129 us
  waiting for transfers between devices  48.2 us (37%)
  starting transfers between devices  36.9 us (29%)
  Pallas kernels  26 us (20%)
  blocking collectives  11.4 us (9%)
  local copies, waits for them, and re-layouts  4.18 us (3%)
    ppermute x19, waiting for transfers between devices, swap(): lax.ppermute(value, axis, [(i, i ^ step) for i in range(lax.axis_size(axi...  33.3 us
    pallas_call x13, Pallas kernels, run(): made(*[pltpu.with_memory_space_constraint(arg, pltpu.HBM) if space == 'h'...  26 us
    ppermute x19, starting transfers between devices, swap(): lax.ppermute(value, axis, [(i, i ^ step) for i in range(lax.axis_size(axi...  24.1 us
    all_to_all x3, waiting for transfers between devices, exchange(): return lax.all_to_all(chunks, axes, 0, 0)  14.9 us
    all_to_all x3, starting transfers between devices, exchange(): return lax.all_to_all(chunks, axes, 0, 0)  12.8 us
    all_to_all x1, blocking collectives, exchange(): return lax.all_to_all(chunks, axes, 0, 0)  11.4 us
    unnamed x13, local copies, waits for them, and re-layouts  4.1 us
  transfers between devices with their start and end apart: 22, of which 13 were waited for; matrix products, arithmetic and copies ran while one was open for 1% of the time, Pallas kernels for 12%

profile of v16, /device:TPU:1, one launch (start us, length us, event | category | flops | bytes accessed | tf_op | source)
XLA Modules:
  0.0 128.6 jit_solution(17612274280653043165)
XLA Ops:
  0.6 1.8 %prepare_weights.1 = (bf16[2,8,1,32,384]{4,3,2,1,0:T(8,128)(2,1)}, bf16[32,1152]{1,0:T(8,128)(2,1)}) custom-call(bf16[32,3072]{1,0:T(8,128)(2,1)} %w_any.1, bf16[32,1024]{1,0:T(8,128)(2,1)} %mix_any.1, bf16[32,100]{1,0:T(8,128)(2,1)} %readout_any.1), custom_call_target="tpu_custom_call" | custom-call | bytes 1048576 | tf_op jit(solution)/shard_map/prepare_weights/pallas_call | solution.py:63
  2.4 3.2 %collective-permute-start = (bf16[32,1152]{1,0:T(8,128)(2,1)}, bf16[32,1152]{1,0:T(8,128)(2,1)S(1)}, u32[]{:S(2)}, u32[]{:S(2)}) collective-permute-start(bf16[32,1152]{1,0:T(8,128)(2,1)} %get-tuple-element.31), channel_id=1, source_target_pairs={{0,16},{16,0},{1,17},{17,1},{2,18},{18,2},{3,19},{19,3},{4,20},{20... | collective-permute-start | bytes 221192 | tf_op jit(solution)/shard_map/ppermute | solution.py:445
  5.6 4.8 %all-to-all-start = ((bf16[16,32,384]{2,1,0:T(8,128)(2,1)}), bf16[16,32,384]{2,1,0:T(8,128)(2,1)S(1)}, u32[]{:S(2)}, u32[]{:S(2)}) async-start(bf16[16,32,384]{2,1,0:T(8,128)(2,1)} %bitcast.22), calls=%async_computation | async-start | bytes 786432 | tf_op jit(solution)/shard_map/all_to_all | solution.py:441
  10.4 1.9 %norm.1 = (bf16[144,1024]{1,0:T(8,128)(2,1)}, bf16[1,64,1024]{2,1,0:T(8,128)(2,1)}, bf16[1,64,1024]{2,1,0:T(8,128)(2,1)}) custom-call(s32[2,4]{1,0:T(2,128)} %near_any.1, bf16[128,1024]{1,0:T(8,128)(2,1)} %bitcast.23), custom_call_target="tpu_custom_call" | custom-call | flops 1048576 | bytes 1048576 | tf_op jit(solution)/shard_map/norm/pallas_call | solution.py:63
  12.3 0.9 select_bitcast_fusion.1
  13.2 2.4 %collective-permute-start.3 = (bf16[144,1024]{1,0:T(8,128)(2,1)}, bf16[144,1024]{1,0:T(8,128)(2,1)S(1)}, u32[]{:S(2)}, u32[]{:S(2)}) collective-permute-start(bf16[144,1024]{1,0:T(8,128)(2,1)} %get-tuple-element.35.refs_0_), channel_id=1, source_target_pairs={{0,12},{4,8},{8,4},{12,0},{1,13},{5,9},{9,5},{13,1},{2,14},{6,10},... | collective-permute-start | bytes 884744 | tf_op jit(solution)/shard_map/ppermute | solution.py:445
  15.9 6.0 %all-to-all-done.refs_0_ = bf16[16,32,384]{2,1,0:T(8,128)(2,1)S(1)} async-done(((bf16[16,32,384]{2,1,0:T(8,128)(2,1)}), bf16[16,32,384]{2,1,0:T(8,128)(2,1)S(1)}, u32[]{:S(2)}, u32[]{:S(2)}) %all-to-all-start) | async-done | bytes 393248 | tf_op jit(solution)/shard_map/all_to_all | solution.py:441
  21.8 1.7 %collective-permute-start.2 = (bf16[144,1024]{1,0:T(8,128)(2,1)}, bf16[144,1024]{1,0:T(8,128)(2,1)S(1)}, u32[]{:S(2)}, u32[]{:S(2)}) collective-permute-start(bf16[144,1024]{1,0:T(8,128)(2,1)} %get-tuple-element.35.refs_0_), channel_id=1, source_target_pairs={{0,8},{4,12},{8,0},{12,4},{1,9},{5,13},{9,1},{13,5},{2,10},{6,14},... | collective-permute-start | bytes 884744 | tf_op jit(solution)/shard_map/ppermute | solution.py:445
  23.6 2.9 %collective-permute-done.3.refs_3_ = bf16[144,1024]{1,0:T(8,128)(2,1)S(1)} collective-permute-done((bf16[144,1024]{1,0:T(8,128)(2,1)}, bf16[144,1024]{1,0:T(8,128)(2,1)S(1)}, u32[]{:S(2)}, u32[]{:S(2)}) %collective-permute-start.3) | collective-permute-done | bytes 294944 | tf_op jit(solution)/shard_map/ppermute | solution.py:445
  26.6 1.6 %collective-permute-start.10 = (bf16[2,32,1152]{2,1,0:T(8,128)(2,1)S(1)}, bf16[2,32,1152]{2,1,0:T(8,128)(2,1)S(1)}, u32[]{:S(2)}, u32[]{:S(2)}) collective-permute-start(bf16[2,32,1152]{2,1,0:T(8,128)(2,1)S(1)} %pad_maximum_fusion.1), channel_id=1, source_target_pairs={{0,8},{4,12},{8,0},{12,4},{1,9},{5,13},{9,1},{13,5},{2,10},{6,14},... | collective-permute-start | bytes 442376 | tf_op jit(solution)/shard_map/ppermute | solution.py:445
  28.2 0.8 collective-permute-start.11
  29.1 2.7 %collective-permute-done.1.refs_1_ = bf16[144,1024]{1,0:T(8,128)(2,1)S(1)} collective-permute-done((bf16[144,1024]{1,0:T(8,128)(2,1)}, bf16[144,1024]{1,0:T(8,128)(2,1)S(1)}, u32[]{:S(2)}, u32[]{:S(2)}) %collective-permute-start.1) | collective-permute-done | bytes 294944 | tf_op jit(solution)/shard_map/ppermute | solution.py:445
  31.7 1.2 collective-permute-start.8
  32.9 1.9 %collective-permute-done.9 = bf16[2,32,1152]{2,1,0:T(8,128)(2,1)S(1)} collective-permute-done((bf16[2,32,1152]{2,1,0:T(8,128)(2,1)S(1)}, bf16[2,32,1152]{2,1,0:T(8,128)(2,1)S(1)}, u32[]{:S(2)}, u32[]{:S(2)}) %collective-permute-start.9) | collective-permute-done | bytes 147488 | tf_op jit(solution)/shard_map/ppermute | solution.py:445
  34.9 0.7 collective-permute-start.4
  35.6 0.9 collective-permute-start.7
  36.5 2.6 %collective-permute-done.11 = bf16[2,32,1152]{2,1,0:T(8,128)(2,1)S(1)} collective-permute-done((bf16[2,32,1152]{2,1,0:T(8,128)(2,1)S(1)}, bf16[2,32,1152]{2,1,0:T(8,128)(2,1)S(1)}, u32[]{:S(2)}, u32[]{:S(2)}) %collective-permute-start.11) | collective-permute-done | bytes 147488 | tf_op jit(solution)/shard_map/ppermute | solution.py:445
  39.1 0.7 collective-permute-start.5
  39.9 1.1 collective-permute-done.5.refs_5_
  41.4 1.0 copy-done.1
  42.4 1.5 %collect.1 = (bf16[1024,1024]{1,0:T(8,128)(2,1)}, f32[8,16,128]{2,1,0:T(8,128)S(1)}) custom-call(bf16[144,1024]{1,0:T(8,128)(2,1)S(1)} %copy-done.1, bf16[144,1024]{1,0:T(8,128)(2,1)S(1)} %collective-permute-done.1.refs_1_, bf16[144,1024]{1,0:T(8,128)(2,1)S(1)} %collective-permute-done.2.refs_2_, bf16[144,1024]{1,0:T(8,128)(2,1)S(1)} %collective-permute-done.3.refs_3_, ...), custom_call_target="tpu_custom_call" | custom-call | bytes 4194304 | tf_op jit(solution)/shard_map/collect/pallas_call | solution.py:63
  43.9 1.3 %project_rims.1 = (bf16[16,2,32,384]{3,2,1,0:T(8,128)(2,1)S(1)}, bf16[128,256]{1,0:T(8,128)(2,1)S(1)}) custom-call(bf16[1024,1024]{1,0:T(8,128)(2,1)} %get-tuple-element.36.normed_any.normed_ref, bf16[16,32,384]{2,1,0:T(8,128)(2,1)S(1)} %all-to-all-done.refs_0_, bf16[16,32,384]{2,1,0:T(8,128)(2,1)S(1)} %collective-permute-done.8.refs_1_), custom_call_target="tpu_custom_call" | custom-call | flops 67108864 | bytes 1048576 | tf_op jit(solution)/shard_map/project_rims/pallas_call | solution.py:63
  45.2 1.3 collective-permute-start.12
  46.5 2.8 %project.1 = (bf16[1024,128]{1,0:T(8,128)(2,1)S(1)}, bf16[1024,256]{1,0:T(8,128)(2,1)S(1)}) custom-call(bf16[1024,1024]{1,0:T(8,128)(2,1)} %get-tuple-element.36.normed_any.normed_ref, bf16[16,2,32,384]{3,2,1,0:T(8,128)(2,1)S(1)} %get-tuple-element.44.w_ref), custom_call_target="tpu_custom_call" | custom-call | flops 805306368 | bytes 4194304 | tf_op jit(solution)/shard_map/project/pallas_call | solution.py:63
  49.4 10.5 %collective-permute-done.12.refs_1_ = bf16[4,2,32,1152]{3,2,1,0:T(8,128)(2,1)S(1)} collective-permute-done((bf16[4,2,32,1152]{3,2,1,0:T(8,128)(2,1)S(1)}, bf16[4,2,32,1152]{3,2,1,0:T(8,128)(2,1)S(1)}, u32[]{:S(2)}, u32[]{:S(2)}) %collective-permute-start.12) | collective-permute-done | bytes 589856 | tf_op jit(solution)/shard_map/ppermute | solution.py:445
  59.8 1.2 collective-permute-start.14
  61.0 2.6 %collective-permute-start.13 = (bf16[128,256]{1,0:T(8,128)(2,1)S(1)}, bf16[128,256]{1,0:T(8,128)(2,1)S(1)}, u32[]{:S(2)}, u32[]{:S(2)}) collective-permute-start(bf16[128,256]{1,0:T(8,128)(2,1)S(1)} %get-tuple-element.49), channel_id=1, source_target_pairs={{0,16},{16,0},{1,17},{17,1},{2,18},{18,2},{3,19},{19,3},{4,20},{20... | collective-permute-start | bytes 196616 | tf_op jit(solution)/shard_map/ppermute | solution.py:445
  63.6 1.9 %attention_interior.1.done_ref = bf16[1024,128]{1,0:T(8,128)(2,1)S(1)} custom-call(f32[8,16,128]{2,1,0:T(8,128)S(1)} %get-tuple-element.37.steps_ref, bf16[1024,128]{1,0:T(8,128)(2,1)S(1)} %get-tuple-element.45.q_ref, bf16[1024,256]{1,0:T(8,128)(2,1)S(1)} %get-tuple-element.48.kv_ref), custom_call_target="tpu_custom_call" | custom-call | flops 268435456 | bytes 2097152 | tf_op jit(solution)/shard_map/attention_interior/pallas_call | solution.py:63
  65.5 1.7 %collective-permute-done.13.low_ref.high_ref = bf16[128,256]{1,0:T(8,128)(2,1)S(1)} collective-permute-done((bf16[128,256]{1,0:T(8,128)(2,1)S(1)}, bf16[128,256]{1,0:T(8,128)(2,1)S(1)}, u32[]{:S(2)}, u32[]{:S(2)}) %collective-permute-start.13) | collective-permute-done | bytes 65568 | tf_op jit(solution)/shard_map/ppermute | solution.py:445
  67.1 1.4 %attention_edges.1 = bf16[1024,128]{1,0:T(8,128)(2,1)} custom-call(f32[8,16,128]{2,1,0:T(8,128)S(1)} %get-tuple-element.37.steps_ref, bf16[1024,128]{1,0:T(8,128)(2,1)S(1)} %get-tuple-element.45.q_ref, bf16[1024,256]{1,0:T(8,128)(2,1)S(1)} %get-tuple-element.48.kv_ref, bf16[128,256]{1,0:T(8,128)(2,1)S(1)} %collective-permute-done.13.low_ref.high_ref, ...), custom_call_target="tpu_custom_call" | custom-call | flops 67108864 | bytes 1048576 | tf_op jit(solution)/shard_map/attention_edges/pallas_call | solution.py:63
  68.6 4.2 %all-to-all-start.1 = ((bf16[16,64,128]{2,1,0:T(8,128)(2,1)}), bf16[16,64,128]{2,1,0:T(8,128)(2,1)S(1)}, u32[]{:S(2)}, u32[]{:S(2)}) async-start(bf16[16,64,128]{2,1,0:T(8,128)(2,1)} %bitcast.8), calls=%async_computation.1 | async-start | bytes 524288 | tf_op jit(solution)/shard_map/all_to_all | solution.py:441
  72.8 1.4 %collective-permute-start.16 = (bf16[1,64,1024]{2,1,0:T(8,128)(2,1)}, bf16[1,64,1024]{2,1,0:T(8,128)(2,1)S(1)}, u32[]{:S(2)}, u32[]{:S(2)}) collective-permute-start(bf16[1,64,1024]{2,1,0:T(8,128)(2,1)} %get-tuple-element.53), channel_id=1, source_target_pairs={{0,1},{1,0},{2,3},{3,2},{4,5},{5,4},{6,7},{7,6},{8,9},{9,8},{10,11... | collective-permute-start | bytes 393224 | tf_op jit(solution)/shard_map/ppermute | solution.py:445
  74.3 1.5 %assemble.1.w_any = bf16[2,4,2,2,32,1152]{5,4,3,2,1,0:T(8,128)(2,1)} custom-call(bf16[4,2,32,1152]{3,2,1,0:T(8,128)(2,1)S(1)} %pad_maximum_fusion.refs_0_, bf16[4,2,32,1152]{3,2,1,0:T(8,128)(2,1)S(1)} %collective-permute-done.12.refs_1_, bf16[4,2,32,1152]{3,2,1,0:T(8,128)(2,1)S(1)} %collective-permute-done.14.refs_2_, ...), custom_call_target="tpu_custom_call" | custom-call | bytes 4194304 | tf_op jit(solution)/shard_map/assemble/pallas_call | solution.py:63
  75.8 5.0 %collective-permute-done.16.refs_1_ = bf16[1,64,1024]{2,1,0:T(8,128)(2,1)S(1)} collective-permute-done((bf16[1,64,1024]{2,1,0:T(8,128)(2,1)}, bf16[1,64,1024]{2,1,0:T(8,128)(2,1)S(1)}, u32[]{:S(2)}, u32[]{:S(2)}) %collective-permute-start.16) | collective-permute-done | bytes 131104 | tf_op jit(solution)/shard_map/ppermute | solution.py:445
  81.4 0.9 copy-done.2
  82.3 0.9 copy-done.4
  83.2 3.7 %mix_loss_backward.1 = (f32[100,128]{1,0:T(8,128)S(1)}, bf16[16,64,128]{2,1,0:T(8,128)(2,1)S(1)}) custom-call(bf16[16,64,128]{2,1,0:T(8,128)(2,1)S(1)} %all-to-all-done.1.att_ref, f32[1,128]{1,0:T(1,128)S(1)} %bitcast.20, f32[100,128]{1,0:T(8,128)} %truth_any.1, bf16[2,4,2,2,32,1152]{5,4,3,2,1,0:T(8,128)(2,1)} %assemble.1.w_any, ...), custom_call_target="tpu_custom_call" | custom-call | flops 603979776 | bytes 4194304 | tf_op jit(solution)/shard_map/mix_loss_backward/pallas_call | solution.py:63
  87.0 11.4 %all_to_all.20 = bf16[16,64,128]{2,1,0:T(8,128)(2,1)S(1)} all-to-all(bf16[16,64,128]{2,1,0:T(8,128)(2,1)S(1)} %get-tuple-element.54), channel_id=1, replica_groups=mesh['half'=2,'quad'=4,'core'=2,'ens'=2] {'quad','core','ens'}, dimensions={0} | all-to-all | bytes 524288 | tf_op jit(solution)/shard_map/all_to_all | solution.py:441
  98.4 1.4 %attention_edges_back.1 = (f32[2,256,256]{2,1,0:T(8,128)S(1)}, bf16[128,256]{1,0:T(8,128)(2,1)S(1)}) custom-call(f32[8,16,128]{2,1,0:T(8,128)S(1)} %get-tuple-element.37.steps_ref, bf16[1024,128]{1,0:T(8,128)(2,1)S(1)} %get-tuple-element.45.q_ref, bf16[1024,256]{1,0:T(8,128)(2,1)S(1)} %get-tuple-element.48.kv_ref, ...), custom_call_target="tpu_custom_call" | custom-call | flops 167772160 | bytes 1048576 | tf_op jit(solution)/shard_map/attention_edges_back/pallas_call | solution.py:63
  99.8 2.4 %collective-permute-start.17 = (bf16[128,256]{1,0:T(8,128)(2,1)S(1)}, bf16[128,256]{1,0:T(8,128)(2,1)S(1)}, u32[]{:S(2)}, u32[]{:S(2)}) collective-permute-start(bf16[128,256]{1,0:T(8,128)(2,1)S(1)} %get-tuple-element.55), channel_id=1, source_target_pairs={{0,16},{16,0},{1,17},{17,1},{2,18},{18,2},{3,19},{19,3},{4,20},{20... | collective-permute-start | bytes 196616 | tf_op jit(solution)/shard_map/ppermute | solution.py:445
  102.2 3.9 %attention_interior_back.1.grads_ref = f32[1024,256]{1,0:T(8,128)S(1)} custom-call(f32[8,16,128]{2,1,0:T(8,128)S(1)} %get-tuple-element.37.steps_ref, bf16[1024,128]{1,0:T(8,128)(2,1)S(1)} %get-tuple-element.45.q_ref, bf16[1024,256]{1,0:T(8,128)(2,1)S(1)} %get-tuple-element.48.kv_ref, bf16[1024,128]{1,0:T(8,128)(2,1)S(1)} %bitcast.18, ...), custom_call_target="tpu_custom_call" | custom-call | flops 536870912 | bytes 4194304 | tf_op jit(solution)/shard_map/attention_interior_back/pallas_call | solution.py:63
  106.1 2.1 %product.1 = bf16[1024,256]{1,0:T(8,128)(2,1)} custom-call(bf16[1024,1024]{1,0:T(8,128)(2,1)S(1)} %copy-done, bf16[128,256]{1,0:T(8,128)(2,1)S(1)} %collective-permute-done.17.from_low_ref.from_high_ref, bf16[128,256]{1,0:T(8,128)(2,1)S(1)} %collective-permute-done.17.from_low_ref.from_high_ref, f32[1024,256]{1,0:T(8,128)S(1)} %attention_interior_back.1.grads_ref), custom_call_target="tpu_custom_call" | custom-call | flops 1073741824 | bytes 4194304 | tf_op jit(solution)/shard_map/product/pallas_call | solution.py:63
  108.2 3.8 %all-to-all-start.3 = ((bf16[32,32,256]{2,1,0:T(8,128)(2,1)}), bf16[32,32,256]{2,1,0:T(8,128)(2,1)S(1)}, u32[]{:S(2)}, u32[]{:S(2)}) async-start(bf16[32,32,256]{2,1,0:T(8,128)(2,1)} %bitcast.12), calls=%async_computation.3 | async-start | bytes 1048576 | tf_op jit(solution)/shard_map/all_to_all | solution.py:441
  112.0 1.5 %collective-permute-start.18 = (f32[100,128]{1,0:T(8,128)S(1)}, f32[100,128]{1,0:T(8,128)S(1)}, u32[]{:S(2)}, u32[]{:S(2)}) collective-permute-start(f32[100,128]{1,0:T(8,128)S(1)} %get-tuple-element.58), channel_id=1, source_target_pairs={{0,1},{1,0},{2,3},{3,2},{4,5},{5,4},{6,7},{7,6},{8,9},{9,8},{10,11... | collective-permute-start | bytes 153608 | tf_op jit(solution)/shard_map/ppermute | solution.py:445
  113.5 4.5 %collective-permute-done.18 = f32[100,128]{1,0:T(8,128)S(1)} collective-permute-done((f32[100,128]{1,0:T(8,128)S(1)}, f32[100,128]{1,0:T(8,128)S(1)}, u32[]{:S(2)}, u32[]{:S(2)}) %collective-permute-start.18) | collective-permute-done | bytes 51232 | tf_op jit(solution)/shard_map/ppermute | solution.py:445
  118.2 0.7 copy.9
  118.9 9.0 %all-to-all-done.3 = bf16[32,32,256]{2,1,0:T(8,128)(2,1)S(1)} async-done(((bf16[32,32,256]{2,1,0:T(8,128)(2,1)}), bf16[32,32,256]{2,1,0:T(8,128)(2,1)S(1)}, u32[]{:S(2)}, u32[]{:S(2)}) %all-to-all-start.3) | async-done | bytes 524320 | tf_op jit(solution)/shard_map/all_to_all | solution.py:441
  127.8 0.8 gather_sums.1
  (30 shorter events, 2.0 us)
Async XLA Ops:
  2.4 9.9 %collective-permute-start = (bf16[32,1152]{1,0:T(8,128)(2,1)}, bf16[32,1152]{1,0:T(8,128)(2,1)S(1)}, u32[]{:S(2)}, u32[]{:S(2)}) collective-permute-start(bf16[32,1152]{1,0:T(8,128)(2,1)} %get-tuple-element.31), channel_id=1, source_target_pairs={{0,16},{16,0},{1,17},{17,1},{2,18},{18,2},{3,19},{19,3},{4,20},{20... | collective-permute-start | bytes 221192 | tf_op jit(solution)/shard_map/ppermute | solution.py:445
  5.6 16.2 %all-to-all-start = ((bf16[16,32,384]{2,1,0:T(8,128)(2,1)}), bf16[16,32,384]{2,1,0:T(8,128)(2,1)S(1)}, u32[]{:S(2)}, u32[]{:S(2)}) async-start(bf16[16,32,384]{2,1,0:T(8,128)(2,1)} %bitcast.22), calls=%async_computation | async-start | bytes 786432 | tf_op jit(solution)/shard_map/all_to_all | solution.py:441
  13.2 13.2 %collective-permute-start.3 = (bf16[144,1024]{1,0:T(8,128)(2,1)}, bf16[144,1024]{1,0:T(8,128)(2,1)S(1)}, u32[]{:S(2)}, u32[]{:S(2)}) collective-permute-start(bf16[144,1024]{1,0:T(8,128)(2,1)} %get-tuple-element.35.refs_0_), channel_id=1, source_target_pairs={{0,12},{4,8},{8,4},{12,0},{1,13},{5,9},{9,5},{13,1},{2,14},{6,10},... | collective-permute-start | bytes 884744 | tf_op jit(solution)/shard_map/ppermute | solution.py:445
  15.6 16.1 %collective-permute-start.1 = (bf16[144,1024]{1,0:T(8,128)(2,1)}, bf16[144,1024]{1,0:T(8,128)(2,1)S(1)}, u32[]{:S(2)}, u32[]{:S(2)}) collective-permute-start(bf16[144,1024]{1,0:T(8,128)(2,1)} %get-tuple-element.35.refs_0_), channel_id=1, source_target_pairs={{0,4},{4,0},{8,12},{12,8},{1,5},{5,1},{9,13},{13,9},{2,6},{6,2},{1... | collective-permute-start | bytes 884744 | tf_op jit(solution)/shard_map/ppermute | solution.py:445
  21.8 18.0 %collective-permute-start.2 = (bf16[144,1024]{1,0:T(8,128)(2,1)}, bf16[144,1024]{1,0:T(8,128)(2,1)S(1)}, u32[]{:S(2)}, u32[]{:S(2)}) collective-permute-start(bf16[144,1024]{1,0:T(8,128)(2,1)} %get-tuple-element.35.refs_0_), channel_id=1, source_target_pairs={{0,8},{4,12},{8,0},{12,4},{1,9},{5,13},{9,1},{13,5},{2,10},{6,14},... | collective-permute-start | bytes 884744 | tf_op jit(solution)/shard_map/ppermute | solution.py:445
  26.4 8.5 %collective-permute-start.9 = (bf16[2,32,1152]{2,1,0:T(8,128)(2,1)S(1)}, bf16[2,32,1152]{2,1,0:T(8,128)(2,1)S(1)}, u32[]{:S(2)}, u32[]{:S(2)}) collective-permute-start(bf16[2,32,1152]{2,1,0:T(8,128)(2,1)S(1)} %pad_maximum_fusion.1), channel_id=1, source_target_pairs={{0,4},{4,0},{8,12},{12,8},{1,5},{5,1},{9,13},{13,9},{2,6},{6,2},{1... | collective-permute-start | bytes 442376 | tf_op jit(solution)/shard_map/ppermute | solution.py:445
  26.6 9.0 %collective-permute-start.10 = (bf16[2,32,1152]{2,1,0:T(8,128)(2,1)S(1)}, bf16[2,32,1152]{2,1,0:T(8,128)(2,1)S(1)}, u32[]{:S(2)}, u32[]{:S(2)}) collective-permute-start(bf16[2,32,1152]{2,1,0:T(8,128)(2,1)S(1)} %pad_maximum_fusion.1), channel_id=1, source_target_pairs={{0,8},{4,12},{8,0},{12,4},{1,9},{5,13},{9,1},{13,5},{2,10},{6,14},... | collective-permute-start | bytes 442376 | tf_op jit(solution)/shard_map/ppermute | solution.py:445
  28.2 10.8 %collective-permute-start.11 = (bf16[2,32,1152]{2,1,0:T(8,128)(2,1)S(1)}, bf16[2,32,1152]{2,1,0:T(8,128)(2,1)S(1)}, u32[]{:S(2)}, u32[]{:S(2)}) collective-permute-start(bf16[2,32,1152]{2,1,0:T(8,128)(2,1)S(1)} %pad_maximum_fusion.1), channel_id=1, source_target_pairs={{0,12},{4,8},{8,4},{12,0},{1,13},{5,9},{9,5},{13,1},{2,14},{6,10},... | collective-permute-start | bytes 442376 | tf_op jit(solution)/shard_map/ppermute | solution.py:445
  31.7 12.2 %collective-permute-start.8 = (bf16[16,32,384]{2,1,0:T(8,128)(2,1)S(1)}, bf16[16,32,384]{2,1,0:T(8,128)(2,1)S(1)}, u32[]{:S(2)}, u32[]{:S(2)}) collective-permute-start(bf16[16,32,384]{2,1,0:T(8,128)(2,1)S(1)} %all-to-all-done.refs_0_), channel_id=1, source_target_pairs={{0,1},{1,0},{2,3},{3,2},{4,5},{5,4},{6,7},{7,6},{8,9},{9,8},{10,11... | collective-permute-start | bytes 1179656 | tf_op jit(solution)/shard_map/ppermute | solution.py:445
  34.9 5.0 %collective-permute-start.4 = (bf16[144,1024]{1,0:T(8,128)(2,1)}, bf16[144,1024]{1,0:T(8,128)(2,1)S(1)}, u32[]{:S(2)}, u32[]{:S(2)}) collective-permute-start(bf16[144,1024]{1,0:T(8,128)(2,1)} %get-tuple-element.35.refs_0_), channel_id=1, source_target_pairs={{0,2},{2,0},{1,3},{3,1},{4,6},{6,4},{5,7},{7,5},{8,10},{10,8},{9,1... | collective-permute-start | bytes 884744 | tf_op jit(solution)/shard_map/ppermute | solution.py:445
  35.6 4.3 %collective-permute-start.7 = (bf16[144,1024]{1,0:T(8,128)(2,1)S(1)}, bf16[144,1024]{1,0:T(8,128)(2,1)S(1)}, u32[]{:S(2)}, u32[]{:S(2)}) collective-permute-start(bf16[144,1024]{1,0:T(8,128)(2,1)S(1)} %collective-permute-done.3.refs_3_), channel_id=1, source_target_pairs={{0,2},{2,0},{1,3},{3,1},{4,6},{6,4},{5,7},{7,5},{8,10},{10,8},{9,1... | collective-permute-start | bytes 884744 | tf_op jit(solution)/shard_map/ppermute | solution.py:445
  39.1 1.9 %collective-permute-start.5 = (bf16[144,1024]{1,0:T(8,128)(2,1)S(1)}, bf16[144,1024]{1,0:T(8,128)(2,1)S(1)}, u32[]{:S(2)}, u32[]{:S(2)}) collective-permute-start(bf16[144,1024]{1,0:T(8,128)(2,1)S(1)} %collective-permute-done.1.refs_1_), channel_id=1, source_target_pairs={{0,2},{2,0},{1,3},{3,1},{4,6},{6,4},{5,7},{7,5},{8,10},{10,8},{9,1... | collective-permute-start | bytes 884744 | tf_op jit(solution)/shard_map/ppermute | solution.py:445
  39.8 1.6 %collective-permute-start.6 = (bf16[144,1024]{1,0:T(8,128)(2,1)S(1)}, bf16[144,1024]{1,0:T(8,128)(2,1)S(1)}, u32[]{:S(2)}, u32[]{:S(2)}) collective-permute-start(bf16[144,1024]{1,0:T(8,128)(2,1)S(1)} %collective-permute-done.2.refs_2_), channel_id=1, source_target_pairs={{0,2},{2,0},{1,3},{3,1},{4,6},{6,4},{5,7},{7,5},{8,10},{10,8},{9,1... | collective-permute-start | bytes 884744 | tf_op jit(solution)/shard_map/ppermute | solution.py:445
  41.4 1.0 copy-start.1
  45.2 14.6 %collective-permute-start.12 = (bf16[4,2,32,1152]{3,2,1,0:T(8,128)(2,1)S(1)}, bf16[4,2,32,1152]{3,2,1,0:T(8,128)(2,1)S(1)}, u32[]{:S(2)}, u32[]{:S(2)}) collective-permute-start(bf16[4,2,32,1152]{3,2,1,0:T(8,128)(2,1)S(1)} %pad_maximum_fusion.refs_0_), channel_id=1, source_target_pairs={{0,1},{1,0},{2,3},{3,2},{4,5},{5,4},{6,7},{7,6},{8,9},{9,8},{10,11... | collective-permute-start | bytes 1769480 | tf_op jit(solution)/shard_map/ppermute | solution.py:445
  59.8 14.4 %collective-permute-start.14 = (bf16[4,2,32,1152]{3,2,1,0:T(8,128)(2,1)S(1)}, bf16[4,2,32,1152]{3,2,1,0:T(8,128)(2,1)S(1)}, u32[]{:S(2)}, u32[]{:S(2)}) collective-permute-start(bf16[4,2,32,1152]{3,2,1,0:T(8,128)(2,1)S(1)} %pad_maximum_fusion.refs_0_), channel_id=1, source_target_pairs={{0,2},{2,0},{1,3},{3,1},{4,6},{6,4},{5,7},{7,5},{8,10},{10,8},{9,1... | collective-permute-start | bytes 1769480 | tf_op jit(solution)/shard_map/ppermute | solution.py:445
  61.0 13.2 %collective-permute-start.15 = (bf16[4,2,32,1152]{3,2,1,0:T(8,128)(2,1)S(1)}, bf16[4,2,32,1152]{3,2,1,0:T(8,128)(2,1)S(1)}, u32[]{:S(2)}, u32[]{:S(2)}) collective-permute-start(bf16[4,2,32,1152]{3,2,1,0:T(8,128)(2,1)S(1)} %collective-permute-done.12.refs_1_), channel_id=1, source_target_pairs={{0,2},{2,0},{1,3},{3,1},{4,6},{6,4},{5,7},{7,5},{8,10},{10,8},{9,1... | collective-permute-start | bytes 1769480 | tf_op jit(solution)/shard_map/ppermute | solution.py:445
  61.0 6.1 %collective-permute-start.13 = (bf16[128,256]{1,0:T(8,128)(2,1)S(1)}, bf16[128,256]{1,0:T(8,128)(2,1)S(1)}, u32[]{:S(2)}, u32[]{:S(2)}) collective-permute-start(bf16[128,256]{1,0:T(8,128)(2,1)S(1)} %get-tuple-element.49), channel_id=1, source_target_pairs={{0,16},{16,0},{1,17},{17,1},{2,18},{18,2},{3,19},{19,3},{4,20},{20... | collective-permute-start | bytes 196616 | tf_op jit(solution)/shard_map/ppermute | solution.py:445
  68.6 12.8 %all-to-all-start.1 = ((bf16[16,64,128]{2,1,0:T(8,128)(2,1)}), bf16[16,64,128]{2,1,0:T(8,128)(2,1)S(1)}, u32[]{:S(2)}, u32[]{:S(2)}) async-start(bf16[16,64,128]{2,1,0:T(8,128)(2,1)} %bitcast.8), calls=%async_computation.1 | async-start | bytes 524288 | tf_op jit(solution)/shard_map/all_to_all | solution.py:441
  72.8 8.6 %copy-start.5 = (f32[128]{0:T(128)S(1)}, f32[128]{0:T(128)}, u32[]{:S(2)}) copy-start(f32[128]{0:T(128)} %param.12) | copy-start | bytes 1540
  72.8 8.0 %collective-permute-start.16 = (bf16[1,64,1024]{2,1,0:T(8,128)(2,1)}, bf16[1,64,1024]{2,1,0:T(8,128)(2,1)S(1)}, u32[]{:S(2)}, u32[]{:S(2)}) collective-permute-start(bf16[1,64,1024]{2,1,0:T(8,128)(2,1)} %get-tuple-element.53), channel_id=1, source_target_pairs={{0,1},{1,0},{2,3},{3,2},{4,5},{5,4},{6,7},{7,6},{8,9},{9,8},{10,11... | collective-permute-start | bytes 393224 | tf_op jit(solution)/shard_map/ppermute | solution.py:445
  80.8 0.6 copy-start.3
  81.4 0.9 copy-start.2
  82.3 0.9 copy-start.4
  87.0 19.1 %copy-start = (bf16[1024,1024]{1,0:T(8,128)(2,1)S(1)}, bf16[1024,1024]{1,0:T(8,128)(2,1)}, u32[]{:S(2)}) copy-start(bf16[1024,1024]{1,0:T(8,128)(2,1)} %get-tuple-element.36.normed_any.normed_ref) | copy-start | bytes 6291460
  99.8 6.3 %collective-permute-start.17 = (bf16[128,256]{1,0:T(8,128)(2,1)S(1)}, bf16[128,256]{1,0:T(8,128)(2,1)S(1)}, u32[]{:S(2)}, u32[]{:S(2)}) collective-permute-start(bf16[128,256]{1,0:T(8,128)(2,1)S(1)} %get-tuple-element.55), channel_id=1, source_target_pairs={{0,16},{16,0},{1,17},{17,1},{2,18},{18,2},{3,19},{19,3},{4,20},{20... | collective-permute-start | bytes 196616 | tf_op jit(solution)/shard_map/ppermute | solution.py:445
  108.2 19.7 %all-to-all-start.3 = ((bf16[32,32,256]{2,1,0:T(8,128)(2,1)}), bf16[32,32,256]{2,1,0:T(8,128)(2,1)S(1)}, u32[]{:S(2)}, u32[]{:S(2)}) async-start(bf16[32,32,256]{2,1,0:T(8,128)(2,1)} %bitcast.12), calls=%async_computation.3 | async-start | bytes 1048576 | tf_op jit(solution)/shard_map/all_to_all | solution.py:441
  112.0 6.0 %collective-permute-start.18 = (f32[100,128]{1,0:T(8,128)S(1)}, f32[100,128]{1,0:T(8,128)S(1)}, u32[]{:S(2)}, u32[]{:S(2)}) collective-permute-start(f32[100,128]{1,0:T(8,128)S(1)} %get-tuple-element.58), channel_id=1, source_target_pairs={{0,1},{1,0},{2,3},{3,2},{4,5},{5,4},{6,7},{7,6},{8,9},{9,8},{10,11... | collective-permute-start | bytes 153608 | tf_op jit(solution)/shard_map/ppermute | solution.py:445

commit v17 on v13

--- a/solution.py
+++ b/solution.py
@@ -204,10 +204,17 @@
 def assemble_kernel(*refs):
     pieces, (w_any, sems) = refs[:GROUP], refs[GROUP:]
     core, quad = lax.axis_index("core"), lax.axis_index("quad")
-    pairs = [
-        (piece, w_any.at[:, quad ^ (at % QUAD), core ^ (at // QUAD)])
-        for at, piece in enumerate(pieces)
-    ]
+    pairs = []
+    for at, piece in enumerate(pieces):
+        place = (quad ^ (at % QUAD), core ^ (at // QUAD))
+        if piece.shape[0] == w_any.shape[0]:
+            pairs.append((piece, w_any.at[:, place[0], place[1], 0]))
+        else:
+            half, ens = lax.axis_index("half"), lax.axis_index("ens")
+            pairs += [
+                (piece.at[step], w_any.at[half ^ (step % 2), place[0], place[1], ens ^ (step // 2)])
+                for step in range(4)
+            ]
     wait(fetch(pairs, sems))
 
 
@@ -496,7 +503,14 @@
         results="h" + "h" * source_parts,
     )(neighbours, members.reshape(node_rows, LATENT_DIM))
 
-    packed, normed = lax.optimization_barrier((in_order(packed, "half", 0), normed))
+    square = paired and halves == 2
+    if square:
+        both = [(at, at ^ 3) for at in range(4)]
+        spread = [swap(packed, "half", 1), swap(packed, "ens", 1)]
+        spread = [packed] + spread + [lax.ppermute(packed, ("half", "ens"), both)]
+        spread[1], normed = lax.optimization_barrier((spread[1], normed))
+    else:
+        packed, normed = lax.optimization_barrier((in_order(packed, "half", 0), normed))
     near = [normed, swap(normed, "quad", 1), None, swap(normed, "quad", 3)]
     if paired:
         columns = exchange(columns.reshape(-1, shard, 3 * COLS), nodes)
@@ -514,13 +528,13 @@
         [((rows, LATENT_DIM), BF16), ((GROUP, NOTE_ROWS, 128), F32)],
         "a" * (2 * QUAD),
         [pltpu.VMEM((GROUP, NOTE_ROWS, 128), BF16), pltpu.SemaphoreType.DMA((2 * GROUP,))],
-        moved=4 * 2**20,
         results="hv",
     )(*near, *far)
 
-    packed = in_order(packed, "ens", 1).reshape(halves, members_num * shard, width)
-    packed, near[2] = lax.optimization_barrier((packed, near[2]))
-    pieces = [packed] + [swap(packed, "quad", step) for step in range(1, QUAD)]
+    if square:
+        packed = jnp.stack(spread)
+    else:
+        packed = in_order(packed, "ens", 1).reshape(halves, members_num * shard, width)
 
     rim = ((RIM, 2 * COLS), BF16)
     rims = [rim] if halves == 2 else [rim, rim]
@@ -540,9 +554,10 @@
             return got, got
         return lax.ppermute(inner[1], "half", up), lax.ppermute(inner[0], "half", down)
 
-    weights, sources[-1] = lax.optimization_barrier((weights, sources[-1]))
+    weights, sources[-1], packed = lax.optimization_barrier((weights, sources[-1], packed))
     sources = [sources[0], swap(sources[1], "ens", 1)] if paired else [exchange(sources[0], "ens")]
     low, high = across(inner)
+    pieces = [packed] + [swap(packed, "quad", step) for step in range(1, QUAD)]
     queries, own = call(
         project_kernel,
         "project",
@@ -574,13 +589,13 @@
     *pieces, own = lax.optimization_barrier((*pieces, own))
     pieces = pieces + [swap(piece, "core", 1) for piece in pieces]
     attended = exchange(outcome.reshape(GROUP * members_num, part, COLS), ("quad", "core", "ens"))
-    block = (halves, QUAD, CORES, members_num * shard, width)
+    block = (halves, QUAD, CORES) + ((2, shard) if square else (1, members_num * shard)) + (width,)
     (weights,) = call(
         assemble_kernel,
         "assemble",
         [(block, BF16)],
         "a" * len(pieces),
-        [pltpu.SemaphoreType.DMA((GROUP,))],
+        [pltpu.SemaphoreType.DMA((4 * GROUP,))],
         moved=4 * 2**20,
         results="h",
     )(*pieces)

time: 110 us -> 126 us (1.15)
  waiting for transfers between devices: 33.9 us -> 45.1 us
  starting transfers between devices: 36.1 us -> 39.3 us
    ppermute x21, waiting for transfers between devices: 18.9 us -> 28.5 us  [swap(): lax.ppermute(value, axis, [(i, i ^ step) for i in range(lax.axis_size(axi...]
    ppermute x0 -> x1, waiting for transfers between devices: none -> 7.51 us  [body(): spread = [packed] + spread + [lax.ppermute(packed, ('half', 'ens'), both)]]
    all_to_all x3, waiting for transfers between devices: 15 us -> 9.09 us  [exchange(): return lax.all_to_all(chunks, axes, 0, 0)]
    all_to_all x3, starting transfers between devices: 13.4 us -> 17 us  [exchange(): return lax.all_to_all(chunks, axes, 0, 0)]
    ppermute x21, starting transfers between devices: 22.7 us -> 21.1 us  [swap(): lax.ppermute(value, axis, [(i, i ^ step) for i in range(lax.axis_size(axi...]
  transfers between devices with their start and end apart: 24 -> 25, of which waited for: 8 -> 10; matrix products, arithmetic and copies ran while one was open for 2% -> 1% of each run, Pallas kernels for 15% -> 12%
where the time goes in v17:
time: 126 us; the launch traced here: 125 us
  waiting for transfers between devices  45.1 us (36%)
  starting transfers between devices  39.3 us (31%)
  Pallas kernels  26.1 us (21%)
  blocking collectives  11.2 us (9%)
  local copies, waits for them, and re-layouts  1.73 us (1%)
    ppermute x21, waiting for transfers between devices, swap(): lax.ppermute(value, axis, [(i, i ^ step) for i in range(lax.axis_size(axi...  28.5 us
    pallas_call x13, Pallas kernels, run(): made(*[pltpu.with_memory_space_constraint(arg, pltpu.HBM) if space == 'h'...  26.1 us
    ppermute x21, starting transfers between devices, swap(): lax.ppermute(value, axis, [(i, i ^ step) for i in range(lax.axis_size(axi...  21.1 us
    all_to_all x3, starting transfers between devices, exchange(): return lax.all_to_all(chunks, axes, 0, 0)  17 us
    all_to_all x1, blocking collectives, exchange(): return lax.all_to_all(chunks, axes, 0, 0)  11.2 us
    all_to_all x3, waiting for transfers between devices, exchange(): return lax.all_to_all(chunks, axes, 0, 0)  9.09 us
    ppermute x1, waiting for transfers between devices, body(): spread = [packed] + spread + [lax.ppermute(packed, ('half', 'ens'), both)]  7.51 us
  transfers between devices with their start and end apart: 25, of which 10 were waited for; matrix products, arithmetic and copies ran while one was open for 1% of the time, Pallas kernels for 12%

profile of v17, /device:TPU:1, one launch (start us, length us, event | category | flops | bytes accessed | tf_op | source)
XLA Modules:
  0.0 125.3 jit_solution(6194795889012915045)
XLA Ops:
  0.6 1.8 %prepare_weights.1 = (bf16[2,8,1,32,384]{4,3,2,1,0:T(8,128)(2,1)}, bf16[32,1152]{1,0:T(8,128)(2,1)}) custom-call(bf16[32,3072]{1,0:T(8,128)(2,1)} %w_any.1, bf16[32,1024]{1,0:T(8,128)(2,1)} %mix_any.1, bf16[32,100]{1,0:T(8,128)(2,1)} %readout_any.1), custom_call_target="tpu_custom_call" | custom-call | bytes 1048576 | tf_op jit(solution)/shard_map/prepare_weights/pallas_call | solution.py:63
  2.4 7.4 %all-to-all-start = ((bf16[16,32,384]{2,1,0:T(8,128)(2,1)}), bf16[16,32,384]{2,1,0:T(8,128)(2,1)S(1)}, u32[]{:S(2)}, u32[]{:S(2)}) async-start(bf16[16,32,384]{2,1,0:T(8,128)(2,1)} %bitcast.17), calls=%async_computation | async-start | bytes 786432 | tf_op jit(solution)/shard_map/all_to_all | solution.py:443
  9.8 2.3 %collective-permute-start = (bf16[32,1152]{1,0:T(8,128)(2,1)}, bf16[32,1152]{1,0:T(8,128)(2,1)S(1)}, u32[]{:S(2)}, u32[]{:S(2)}) collective-permute-start(bf16[32,1152]{1,0:T(8,128)(2,1)} %get-tuple-element.31), channel_id=1, source_target_pairs={{0,16},{16,0},{1,17},{17,1},{2,18},{18,2},{3,19},{19,3},{4,20},{20... | collective-permute-start | bytes 221192 | tf_op jit(solution)/shard_map/ppermute | solution.py:447
  12.1 1.9 %norm.1 = (bf16[144,1024]{1,0:T(8,128)(2,1)}, bf16[1,64,1024]{2,1,0:T(8,128)(2,1)}, bf16[1,64,1024]{2,1,0:T(8,128)(2,1)}) custom-call(s32[2,4]{1,0:T(2,128)} %near_any.1, bf16[128,1024]{1,0:T(8,128)(2,1)} %bitcast.18), custom_call_target="tpu_custom_call" | custom-call | flops 1048576 | bytes 1048576 | tf_op jit(solution)/shard_map/norm/pallas_call | solution.py:63
  14.0 10.7 %collective-permute-done = bf16[32,1152]{1,0:T(8,128)(2,1)S(1)} collective-permute-done((bf16[32,1152]{1,0:T(8,128)(2,1)}, bf16[32,1152]{1,0:T(8,128)(2,1)S(1)}, u32[]{:S(2)}, u32[]{:S(2)}) %collective-permute-start) | collective-permute-done | bytes 73760 | tf_op jit(solution)/shard_map/ppermute | solution.py:447
  24.6 1.2 collective-permute-start.1
  25.8 1.5 %collective-permute-start.2 = (bf16[144,1024]{1,0:T(8,128)(2,1)}, bf16[144,1024]{1,0:T(8,128)(2,1)S(1)}, u32[]{:S(2)}, u32[]{:S(2)}) collective-permute-start(bf16[144,1024]{1,0:T(8,128)(2,1)} %get-tuple-element.35.refs_0_), channel_id=1, source_target_pairs={{0,8},{4,12},{8,0},{12,4},{1,9},{5,13},{9,1},{13,5},{2,10},{6,14},... | collective-permute-start | bytes 884744 | tf_op jit(solution)/shard_map/ppermute | solution.py:447
  27.3 1.2 collective-permute-start.9
  28.5 0.3 collective-permute-start.8
  28.7 2.2 %collective-permute-done.9 = bf16[32,1152]{1,0:T(8,128)(2,1)S(1)} collective-permute-done((bf16[32,1152]{1,0:T(8,128)(2,1)}, bf16[32,1152]{1,0:T(8,128)(2,1)S(1)}, u32[]{:S(2)}, u32[]{:S(2)}) %collective-permute-start.9) | collective-permute-done | bytes 73760 | tf_op jit(solution)/shard_map/ppermute | solution.py:447
  31.0 1.1 collective-permute-start.10
  32.1 7.5 %collective-permute-done.10 = bf16[32,1152]{1,0:T(8,128)(2,1)S(1)} collective-permute-done((bf16[32,1152]{1,0:T(8,128)(2,1)}, bf16[32,1152]{1,0:T(8,128)(2,1)S(1)}, u32[]{:S(2)}, u32[]{:S(2)}) %collective-permute-start.10) | collective-permute-done | bytes 73760 | tf_op jit(solution)/shard_map/ppermute | solution.py:510
  39.6 1.7 %collective-permute-start.4 = (bf16[144,1024]{1,0:T(8,128)(2,1)}, bf16[144,1024]{1,0:T(8,128)(2,1)S(1)}, u32[]{:S(2)}, u32[]{:S(2)}) collective-permute-start(bf16[144,1024]{1,0:T(8,128)(2,1)} %get-tuple-element.35.refs_0_), channel_id=1, source_target_pairs={{0,2},{2,0},{1,3},{3,1},{4,6},{6,4},{5,7},{7,5},{8,10},{10,8},{9,1... | collective-permute-start | bytes 884744 | tf_op jit(solution)/shard_map/ppermute | solution.py:447
  41.3 0.5 collective-permute-start.7
  41.8 1.5 %collective-permute-start.6 = (bf16[144,1024]{1,0:T(8,128)(2,1)S(1)}, bf16[144,1024]{1,0:T(8,128)(2,1)S(1)}, u32[]{:S(2)}, u32[]{:S(2)}) collective-permute-start(bf16[144,1024]{1,0:T(8,128)(2,1)S(1)} %collective-permute-done.2.refs_2_), channel_id=1, source_target_pairs={{0,2},{2,0},{1,3},{3,1},{4,6},{6,4},{5,7},{7,5},{8,10},{10,8},{9,1... | collective-permute-start | bytes 884744 | tf_op jit(solution)/shard_map/ppermute | solution.py:447
  43.4 0.9 pad_maximum_fusion.refs_0_
  44.3 0.2 collective-permute-done.6.refs_6_
  44.6 1.0 copy-done.1
  45.6 1.5 %collect.1 = (bf16[1024,1024]{1,0:T(8,128)(2,1)}, f32[8,16,128]{2,1,0:T(8,128)S(1)}) custom-call(bf16[144,1024]{1,0:T(8,128)(2,1)S(1)} %copy-done.1, bf16[144,1024]{1,0:T(8,128)(2,1)S(1)} %collective-permute-done.1.refs_1_, bf16[144,1024]{1,0:T(8,128)(2,1)S(1)} %collective-permute-done.2.refs_2_, bf16[144,1024]{1,0:T(8,128)(2,1)S(1)} %collective-permute-done.3.refs_3_, ...), custom_call_target="tpu_custom_call" | custom-call | tf_op jit(solution)/shard_map/collect/pallas_call | solution.py:63
  47.1 1.3 %project_rims.1 = (bf16[16,2,32,384]{3,2,1,0:T(8,128)(2,1)S(1)}, bf16[128,256]{1,0:T(8,128)(2,1)S(1)}) custom-call(bf16[1024,1024]{1,0:T(8,128)(2,1)} %get-tuple-element.36.normed_any.normed_ref, bf16[16,32,384]{2,1,0:T(8,128)(2,1)S(1)} %all-to-all-done.refs_0_, bf16[16,32,384]{2,1,0:T(8,128)(2,1)S(1)} %collective-permute-done.8.refs_1_), custom_call_target="tpu_custom_call" | custom-call | flops 67108864 | bytes 1048576 | tf_op jit(solution)/shard_map/project_rims/pallas_call | solution.py:63
  48.4 1.2 collective-permute-start.11
  49.6 1.6 %collective-permute-start.12 = (bf16[4,32,1152]{2,1,0:T(8,128)(2,1)S(1)}, bf16[4,32,1152]{2,1,0:T(8,128)(2,1)S(1)}, u32[]{:S(2)}, u32[]{:S(2)}) collective-permute-start(bf16[4,32,1152]{2,1,0:T(8,128)(2,1)S(1)} %pad_maximum_fusion.refs_0_), channel_id=1, source_target_pairs={{0,8},{4,12},{8,0},{12,4},{1,9},{5,13},{9,1},{13,5},{2,10},{6,14},... | collective-permute-start | bytes 884744 | tf_op jit(solution)/shard_map/ppermute | solution.py:447
  51.2 0.9 collective-permute-start.13
  52.1 2.2 %collective-permute-start.14 = (bf16[128,256]{1,0:T(8,128)(2,1)S(1)}, bf16[128,256]{1,0:T(8,128)(2,1)S(1)}, u32[]{:S(2)}, u32[]{:S(2)}) collective-permute-start(bf16[128,256]{1,0:T(8,128)(2,1)S(1)} %get-tuple-element.47), channel_id=1, source_target_pairs={{0,16},{16,0},{1,17},{17,1},{2,18},{18,2},{3,19},{19,3},{4,20},{20... | collective-permute-start | bytes 196616 | tf_op jit(solution)/shard_map/ppermute | solution.py:447
  54.3 2.8 %project.1 = (bf16[1024,128]{1,0:T(8,128)(2,1)S(1)}, bf16[1024,256]{1,0:T(8,128)(2,1)S(1)}) custom-call(bf16[1024,1024]{1,0:T(8,128)(2,1)} %get-tuple-element.36.normed_any.normed_ref, bf16[16,2,32,384]{3,2,1,0:T(8,128)(2,1)S(1)} %get-tuple-element.42.w_ref), custom_call_target="tpu_custom_call" | custom-call | flops 805306368 | bytes 4194304 | tf_op jit(solution)/shard_map/project/pallas_call | solution.py:63
  57.1 1.9 %attention_interior.1.done_ref = bf16[1024,128]{1,0:T(8,128)(2,1)S(1)} custom-call(f32[8,16,128]{2,1,0:T(8,128)S(1)} %get-tuple-element.37.steps_ref, bf16[1024,128]{1,0:T(8,128)(2,1)S(1)} %get-tuple-element.43.q_ref, bf16[1024,256]{1,0:T(8,128)(2,1)S(1)} %get-tuple-element.46.kv_ref), custom_call_target="tpu_custom_call" | custom-call | flops 268435456 | bytes 2097152 | tf_op jit(solution)/shard_map/attention_interior/pallas_call | solution.py:63
  59.0 5.6 %collective-permute-done.14.low_ref.high_ref = bf16[128,256]{1,0:T(8,128)(2,1)S(1)} collective-permute-done((bf16[128,256]{1,0:T(8,128)(2,1)S(1)}, bf16[128,256]{1,0:T(8,128)(2,1)S(1)}, u32[]{:S(2)}, u32[]{:S(2)}) %collective-permute-start.14) | collective-permute-done | bytes 65568 | tf_op jit(solution)/shard_map/ppermute | solution.py:447
  64.6 1.4 %attention_edges.1 = bf16[1024,128]{1,0:T(8,128)(2,1)} custom-call(f32[8,16,128]{2,1,0:T(8,128)S(1)} %get-tuple-element.37.steps_ref, bf16[1024,128]{1,0:T(8,128)(2,1)S(1)} %get-tuple-element.43.q_ref, bf16[1024,256]{1,0:T(8,128)(2,1)S(1)} %get-tuple-element.46.kv_ref, bf16[128,256]{1,0:T(8,128)(2,1)S(1)} %collective-permute-done.14.low_ref.high_ref, ...), custom_call_target="tpu_custom_call" | custom-call | flops 67108864 | bytes 1048576 | tf_op jit(solution)/shard_map/attention_edges/pallas_call | solution.py:63
  66.1 6.9 %all-to-all-start.1 = ((bf16[16,64,128]{2,1,0:T(8,128)(2,1)}), bf16[16,64,128]{2,1,0:T(8,128)(2,1)S(1)}, u32[]{:S(2)}, u32[]{:S(2)}) async-start(bf16[16,64,128]{2,1,0:T(8,128)(2,1)} %bitcast.6), calls=%async_computation.1 | async-start | bytes 524288 | tf_op jit(solution)/shard_map/all_to_all | solution.py:443
  73.2 0.4 collective-permute-start.16
  73.7 0.4 collective-permute-start.18
  74.1 1.4 %collective-permute-start.19 = (bf16[1,64,1024]{2,1,0:T(8,128)(2,1)S(1)}, bf16[1,64,1024]{2,1,0:T(8,128)(2,1)S(1)}, u32[]{:S(2)}, u32[]{:S(2)}) collective-permute-start(bf16[1,64,1024]{2,1,0:T(8,128)(2,1)S(1)} %copy-done.4), channel_id=1, source_target_pairs={{0,1},{1,0},{2,3},{3,2},{4,5},{5,4},{6,7},{7,6},{8,9},{9,8},{10,11... | collective-permute-start | bytes 393224 | tf_op jit(solution)/shard_map/ppermute | solution.py:447
  75.5 0.4 collective-permute-done.18.refs_7_
  75.9 1.7 %assemble.1.w_any = bf16[2,4,2,2,32,1152]{5,4,3,2,1,0:T(8,128)(2,1)} custom-call(bf16[4,32,1152]{2,1,0:T(8,128)(2,1)S(1)} %pad_maximum_fusion.refs_0_, bf16[4,32,1152]{2,1,0:T(8,128)(2,1)S(1)} %collective-permute-done.11.refs_1_, bf16[4,32,1152]{2,1,0:T(8,128)(2,1)S(1)} %collective-permute-done.12.refs_2_, ...), custom_call_target="tpu_custom_call" | custom-call | bytes 4194304 | tf_op jit(solution)/shard_map/assemble/pallas_call | solution.py:63
  77.6 3.4 %collective-permute-done.19.refs_1_ = bf16[1,64,1024]{2,1,0:T(8,128)(2,1)S(1)} collective-permute-done((bf16[1,64,1024]{2,1,0:T(8,128)(2,1)S(1)}, bf16[1,64,1024]{2,1,0:T(8,128)(2,1)S(1)}, u32[]{:S(2)}, u32[]{:S(2)}) %collective-permute-start.19) | collective-permute-done | bytes 131104 | tf_op jit(solution)/shard_map/ppermute | solution.py:447
  81.0 3.7 %mix_loss_backward.1 = (f32[100,128]{1,0:T(8,128)S(1)}, bf16[16,64,128]{2,1,0:T(8,128)(2,1)S(1)}) custom-call(bf16[16,64,128]{2,1,0:T(8,128)(2,1)S(1)} %all-to-all-done.1.att_ref, f32[1,128]{1,0:T(1,128)S(1)} %bitcast.16, f32[100,128]{1,0:T(8,128)} %truth_any.1, bf16[2,4,2,2,32,1152]{5,4,3,2,1,0:T(8,128)(2,1)} %assemble.1.w_any, ...), custom_call_target="tpu_custom_call" | custom-call | flops 603979776 | bytes 4194304 | tf_op jit(solution)/shard_map/mix_loss_backward/pallas_call | solution.py:63
  84.8 11.2 %all_to_all.20 = bf16[16,64,128]{2,1,0:T(8,128)(2,1)S(1)} all-to-all(bf16[16,64,128]{2,1,0:T(8,128)(2,1)S(1)} %get-tuple-element.54), channel_id=1, replica_groups=mesh['half'=2,'quad'=4,'core'=2,'ens'=2] {'quad','core','ens'}, dimensions={0} | all-to-all | bytes 524288 | tf_op jit(solution)/shard_map/all_to_all | solution.py:443
  96.0 1.4 %attention_edges_back.1 = (f32[2,256,256]{2,1,0:T(8,128)S(1)}, bf16[128,256]{1,0:T(8,128)(2,1)S(1)}) custom-call(f32[8,16,128]{2,1,0:T(8,128)S(1)} %get-tuple-element.37.steps_ref, bf16[1024,128]{1,0:T(8,128)(2,1)S(1)} %get-tuple-element.43.q_ref, bf16[1024,256]{1,0:T(8,128)(2,1)S(1)} %get-tuple-element.46.kv_ref, ...), custom_call_target="tpu_custom_call" | custom-call | flops 167772160 | bytes 1048576 | tf_op jit(solution)/shard_map/attention_edges_back/pallas_call | solution.py:63
  97.4 1.2 collective-permute-start.20
  98.6 3.9 %attention_interior_back.1.grads_ref = f32[1024,256]{1,0:T(8,128)S(1)} custom-call(f32[8,16,128]{2,1,0:T(8,128)S(1)} %get-tuple-element.37.steps_ref, bf16[1024,128]{1,0:T(8,128)(2,1)S(1)} %get-tuple-element.43.q_ref, bf16[1024,256]{1,0:T(8,128)(2,1)S(1)} %get-tuple-element.46.kv_ref, bf16[1024,128]{1,0:T(8,128)(2,1)S(1)} %bitcast.14, ...), custom_call_target="tpu_custom_call" | custom-call | flops 536870912 | bytes 4194304 | tf_op jit(solution)/shard_map/attention_interior_back/pallas_call | solution.py:63
  102.4 1.3 %collective-permute-done.20.from_low_ref.from_high_ref = bf16[128,256]{1,0:T(8,128)(2,1)S(1)} collective-permute-done((bf16[128,256]{1,0:T(8,128)(2,1)S(1)}, bf16[128,256]{1,0:T(8,128)(2,1)S(1)}, u32[]{:S(2)}, u32[]{:S(2)}) %collective-permute-start.20) | collective-permute-done | bytes 65568 | tf_op jit(solution)/shard_map/ppermute | solution.py:447
  103.7 2.1 %product.1 = bf16[1024,256]{1,0:T(8,128)(2,1)} custom-call(bf16[1024,1024]{1,0:T(8,128)(2,1)S(1)} %copy-done, bf16[128,256]{1,0:T(8,128)(2,1)S(1)} %collective-permute-done.20.from_low_ref.from_high_ref, bf16[128,256]{1,0:T(8,128)(2,1)S(1)} %collective-permute-done.20.from_low_ref.from_high_ref, f32[1024,256]{1,0:T(8,128)S(1)} %attention_interior_back.1.grads_ref), custom_call_target="tpu_custom_call" | custom-call | flops 1073741824 | bytes 4194304 | tf_op jit(solution)/shard_map/product/pallas_call | solution.py:63
  105.8 2.8 %all-to-all-start.3 = ((bf16[32,32,256]{2,1,0:T(8,128)(2,1)}), bf16[32,32,256]{2,1,0:T(8,128)(2,1)S(1)}, u32[]{:S(2)}, u32[]{:S(2)}) async-start(bf16[32,32,256]{2,1,0:T(8,128)(2,1)} %bitcast.10), calls=%async_computation.3 | async-start | bytes 1048576 | tf_op jit(solution)/shard_map/all_to_all | solution.py:443
  108.5 1.5 %collective-permute-start.21 = (f32[100,128]{1,0:T(8,128)S(1)}, f32[100,128]{1,0:T(8,128)S(1)}, u32[]{:S(2)}, u32[]{:S(2)}) collective-permute-start(f32[100,128]{1,0:T(8,128)S(1)} %get-tuple-element.58), channel_id=1, source_target_pairs={{0,1},{1,0},{2,3},{3,2},{4,5},{5,4},{6,7},{7,6},{8,9},{9,8},{10,11... | collective-permute-start | bytes 153608 | tf_op jit(solution)/shard_map/ppermute | solution.py:447
  110.0 4.5 %collective-permute-done.21 = f32[100,128]{1,0:T(8,128)S(1)} collective-permute-done((f32[100,128]{1,0:T(8,128)S(1)}, f32[100,128]{1,0:T(8,128)S(1)}, u32[]{:S(2)}, u32[]{:S(2)}) %collective-permute-start.21) | collective-permute-done | bytes 51232 | tf_op jit(solution)/shard_map/ppermute | solution.py:447
  114.7 0.7 copy.9
  115.4 9.1 %all-to-all-done.3 = bf16[32,32,256]{2,1,0:T(8,128)(2,1)S(1)} async-done(((bf16[32,32,256]{2,1,0:T(8,128)(2,1)}), bf16[32,32,256]{2,1,0:T(8,128)(2,1)S(1)}, u32[]{:S(2)}, u32[]{:S(2)}) %all-to-all-start.3) | async-done | bytes 524320 | tf_op jit(solution)/shard_map/all_to_all | solution.py:443
  124.5 0.8 gather_sums.1
  (32 shorter events, 0.5 us)
Async XLA Ops:
  2.4 23.4 %all-to-all-start = ((bf16[16,32,384]{2,1,0:T(8,128)(2,1)}), bf16[16,32,384]{2,1,0:T(8,128)(2,1)S(1)}, u32[]{:S(2)}, u32[]{:S(2)}) async-start(bf16[16,32,384]{2,1,0:T(8,128)(2,1)} %bitcast.17), calls=%async_computation | async-start | bytes 786432 | tf_op jit(solution)/shard_map/all_to_all | solution.py:443
  9.8 14.8 %collective-permute-start = (bf16[32,1152]{1,0:T(8,128)(2,1)}, bf16[32,1152]{1,0:T(8,128)(2,1)S(1)}, u32[]{:S(2)}, u32[]{:S(2)}) collective-permute-start(bf16[32,1152]{1,0:T(8,128)(2,1)} %get-tuple-element.31), channel_id=1, source_target_pairs={{0,16},{16,0},{1,17},{17,1},{2,18},{18,2},{3,19},{19,3},{4,20},{20... | collective-permute-start | bytes 221192 | tf_op jit(solution)/shard_map/ppermute | solution.py:447
  24.6 16.7 %collective-permute-start.1 = (bf16[144,1024]{1,0:T(8,128)(2,1)}, bf16[144,1024]{1,0:T(8,128)(2,1)S(1)}, u32[]{:S(2)}, u32[]{:S(2)}) collective-permute-start(bf16[144,1024]{1,0:T(8,128)(2,1)} %get-tuple-element.35.refs_0_), channel_id=1, source_target_pairs={{0,4},{4,0},{8,12},{12,8},{1,5},{5,1},{9,13},{13,9},{2,6},{6,2},{1... | collective-permute-start | bytes 884744 | tf_op jit(solution)/shard_map/ppermute | solution.py:447
  25.8 15.5 %collective-permute-start.3 = (bf16[144,1024]{1,0:T(8,128)(2,1)}, bf16[144,1024]{1,0:T(8,128)(2,1)S(1)}, u32[]{:S(2)}, u32[]{:S(2)}) collective-permute-start(bf16[144,1024]{1,0:T(8,128)(2,1)} %get-tuple-element.35.refs_0_), channel_id=1, source_target_pairs={{0,12},{4,8},{8,4},{12,0},{1,13},{5,9},{9,5},{13,1},{2,14},{6,10},... | collective-permute-start | bytes 884744 | tf_op jit(solution)/shard_map/ppermute | solution.py:447
  25.8 16.0 %collective-permute-start.2 = (bf16[144,1024]{1,0:T(8,128)(2,1)}, bf16[144,1024]{1,0:T(8,128)(2,1)S(1)}, u32[]{:S(2)}, u32[]{:S(2)}) collective-permute-start(bf16[144,1024]{1,0:T(8,128)(2,1)} %get-tuple-element.35.refs_0_), channel_id=1, source_target_pairs={{0,8},{4,12},{8,0},{12,4},{1,9},{5,13},{9,1},{13,5},{2,10},{6,14},... | collective-permute-start | bytes 884744 | tf_op jit(solution)/shard_map/ppermute | solution.py:447
  27.3 3.7 %collective-permute-start.9 = (bf16[32,1152]{1,0:T(8,128)(2,1)}, bf16[32,1152]{1,0:T(8,128)(2,1)S(1)}, u32[]{:S(2)}, u32[]{:S(2)}) collective-permute-start(bf16[32,1152]{1,0:T(8,128)(2,1)} %get-tuple-element.31), channel_id=1, source_target_pairs={{0,1},{1,0},{2,3},{3,2},{4,5},{5,4},{6,7},{7,6},{8,9},{9,8},{10,11... | collective-permute-start | bytes 221192 | tf_op jit(solution)/shard_map/ppermute | solution.py:447
  28.5 18.6 %collective-permute-start.8 = (bf16[16,32,384]{2,1,0:T(8,128)(2,1)S(1)}, bf16[16,32,384]{2,1,0:T(8,128)(2,1)S(1)}, u32[]{:S(2)}, u32[]{:S(2)}) collective-permute-start(bf16[16,32,384]{2,1,0:T(8,128)(2,1)S(1)} %all-to-all-done.refs_0_), channel_id=1, source_target_pairs={{0,1},{1,0},{2,3},{3,2},{4,5},{5,4},{6,7},{7,6},{8,9},{9,8},{10,11... | collective-permute-start | bytes 1179656 | tf_op jit(solution)/shard_map/ppermute | solution.py:447
  31.0 8.6 %collective-permute-start.10 = (bf16[32,1152]{1,0:T(8,128)(2,1)}, bf16[32,1152]{1,0:T(8,128)(2,1)S(1)}, u32[]{:S(2)}, u32[]{:S(2)}) collective-permute-start(bf16[32,1152]{1,0:T(8,128)(2,1)} %get-tuple-element.31), channel_id=1, source_target_pairs={{0,17},{1,16},{16,1},{17,0},{2,19},{3,18},{18,3},{19,2},{4,21},{5,... | collective-permute-start | bytes 221192 | tf_op jit(solution)/shard_map/ppermute | solution.py:510
  39.6 4.7 %collective-permute-start.4 = (bf16[144,1024]{1,0:T(8,128)(2,1)}, bf16[144,1024]{1,0:T(8,128)(2,1)S(1)}, u32[]{:S(2)}, u32[]{:S(2)}) collective-permute-start(bf16[144,1024]{1,0:T(8,128)(2,1)} %get-tuple-element.35.refs_0_), channel_id=1, source_target_pairs={{0,2},{2,0},{1,3},{3,1},{4,6},{6,4},{5,7},{7,5},{8,10},{10,8},{9,1... | collective-permute-start | bytes 884744 | tf_op jit(solution)/shard_map/ppermute | solution.py:447
  41.3 3.0 %collective-permute-start.5 = (bf16[144,1024]{1,0:T(8,128)(2,1)S(1)}, bf16[144,1024]{1,0:T(8,128)(2,1)S(1)}, u32[]{:S(2)}, u32[]{:S(2)}) collective-permute-start(bf16[144,1024]{1,0:T(8,128)(2,1)S(1)} %collective-permute-done.1.refs_1_), channel_id=1, source_target_pairs={{0,2},{2,0},{1,3},{3,1},{4,6},{6,4},{5,7},{7,5},{8,10},{10,8},{9,1... | collective-permute-start | bytes 884744 | tf_op jit(solution)/shard_map/ppermute | solution.py:447
  41.3 3.0 %collective-permute-start.7 = (bf16[144,1024]{1,0:T(8,128)(2,1)S(1)}, bf16[144,1024]{1,0:T(8,128)(2,1)S(1)}, u32[]{:S(2)}, u32[]{:S(2)}) collective-permute-start(bf16[144,1024]{1,0:T(8,128)(2,1)S(1)} %collective-permute-done.3.refs_3_), channel_id=1, source_target_pairs={{0,2},{2,0},{1,3},{3,1},{4,6},{6,4},{5,7},{7,5},{8,10},{10,8},{9,1... | collective-permute-start | bytes 884744 | tf_op jit(solution)/shard_map/ppermute | solution.py:447
  41.8 2.7 %collective-permute-start.6 = (bf16[144,1024]{1,0:T(8,128)(2,1)S(1)}, bf16[144,1024]{1,0:T(8,128)(2,1)S(1)}, u32[]{:S(2)}, u32[]{:S(2)}) collective-permute-start(bf16[144,1024]{1,0:T(8,128)(2,1)S(1)} %collective-permute-done.2.refs_2_), channel_id=1, source_target_pairs={{0,2},{2,0},{1,3},{3,1},{4,6},{6,4},{5,7},{7,5},{8,10},{10,8},{9,1... | collective-permute-start | bytes 884744 | tf_op jit(solution)/shard_map/ppermute | solution.py:447
  44.6 1.0 copy-start.1
  48.4 24.6 %collective-permute-start.11 = (bf16[4,32,1152]{2,1,0:T(8,128)(2,1)S(1)}, bf16[4,32,1152]{2,1,0:T(8,128)(2,1)S(1)}, u32[]{:S(2)}, u32[]{:S(2)}) collective-permute-start(bf16[4,32,1152]{2,1,0:T(8,128)(2,1)S(1)} %pad_maximum_fusion.refs_0_), channel_id=1, source_target_pairs={{0,4},{4,0},{8,12},{12,8},{1,5},{5,1},{9,13},{13,9},{2,6},{6,2},{1... | collective-permute-start | bytes 884744 | tf_op jit(solution)/shard_map/ppermute | solution.py:447
  49.6 23.3 %collective-permute-start.12 = (bf16[4,32,1152]{2,1,0:T(8,128)(2,1)S(1)}, bf16[4,32,1152]{2,1,0:T(8,128)(2,1)S(1)}, u32[]{:S(2)}, u32[]{:S(2)}) collective-permute-start(bf16[4,32,1152]{2,1,0:T(8,128)(2,1)S(1)} %pad_maximum_fusion.refs_0_), channel_id=1, source_target_pairs={{0,8},{4,12},{8,0},{12,4},{1,9},{5,13},{9,1},{13,5},{2,10},{6,14},... | collective-permute-start | bytes 884744 | tf_op jit(solution)/shard_map/ppermute | solution.py:447
  51.2 21.8 %collective-permute-start.13 = (bf16[4,32,1152]{2,1,0:T(8,128)(2,1)S(1)}, bf16[4,32,1152]{2,1,0:T(8,128)(2,1)S(1)}, u32[]{:S(2)}, u32[]{:S(2)}) collective-permute-start(bf16[4,32,1152]{2,1,0:T(8,128)(2,1)S(1)} %pad_maximum_fusion.refs_0_), channel_id=1, source_target_pairs={{0,12},{4,8},{8,4},{12,0},{1,13},{5,9},{9,5},{13,1},{2,14},{6,10},... | collective-permute-start | bytes 884744 | tf_op jit(solution)/shard_map/ppermute | solution.py:447
  52.1 22.0 %copy-start.4 = (bf16[1,64,1024]{2,1,0:T(8,128)(2,1)S(1)}, bf16[1,64,1024]{2,1,0:T(8,128)(2,1)}, u32[]{:S(2)}) copy-start(bf16[1,64,1024]{2,1,0:T(8,128)(2,1)} %get-tuple-element.53) | copy-start | bytes 393220
  52.1 12.6 %collective-permute-start.14 = (bf16[128,256]{1,0:T(8,128)(2,1)S(1)}, bf16[128,256]{1,0:T(8,128)(2,1)S(1)}, u32[]{:S(2)}, u32[]{:S(2)}) collective-permute-start(bf16[128,256]{1,0:T(8,128)(2,1)S(1)} %get-tuple-element.47), channel_id=1, source_target_pairs={{0,16},{16,0},{1,17},{17,1},{2,18},{18,2},{3,19},{19,3},{4,20},{20... | collective-permute-start | bytes 196616 | tf_op jit(solution)/shard_map/ppermute | solution.py:447
  66.1 15.0 %all-to-all-start.1 = ((bf16[16,64,128]{2,1,0:T(8,128)(2,1)}), bf16[16,64,128]{2,1,0:T(8,128)(2,1)S(1)}, u32[]{:S(2)}, u32[]{:S(2)}) async-start(bf16[16,64,128]{2,1,0:T(8,128)(2,1)} %bitcast.6), calls=%async_computation.1 | async-start | bytes 524288 | tf_op jit(solution)/shard_map/all_to_all | solution.py:443
  72.9 8.1 %copy-start.2 = (bf16[1,64,1024]{2,1,0:T(8,128)(2,1)S(1)}, bf16[1,64,1024]{2,1,0:T(8,128)(2,1)}, u32[]{:S(2)}) copy-start(bf16[1,64,1024]{2,1,0:T(8,128)(2,1)} %get-tuple-element.52.refs_0_) | copy-start | bytes 393220
  72.9 8.1 %copy-start.3 = (f32[128]{0:T(128)S(1)}, f32[128]{0:T(128)}, u32[]{:S(2)}) copy-start(f32[128]{0:T(128)} %param.12) | copy-start | bytes 1540
  73.0 2.5 %collective-permute-start.15 = (bf16[4,32,1152]{2,1,0:T(8,128)(2,1)S(1)}, bf16[4,32,1152]{2,1,0:T(8,128)(2,1)S(1)}, u32[]{:S(2)}, u32[]{:S(2)}) collective-permute-start(bf16[4,32,1152]{2,1,0:T(8,128)(2,1)S(1)} %pad_maximum_fusion.refs_0_), channel_id=1, source_target_pairs={{0,2},{2,0},{1,3},{3,1},{4,6},{6,4},{5,7},{7,5},{8,10},{10,8},{9,1... | collective-permute-start | bytes 884744 | tf_op jit(solution)/shard_map/ppermute | solution.py:447
  73.2 2.3 %collective-permute-start.16 = (bf16[4,32,1152]{2,1,0:T(8,128)(2,1)S(1)}, bf16[4,32,1152]{2,1,0:T(8,128)(2,1)S(1)}, u32[]{:S(2)}, u32[]{:S(2)}) collective-permute-start(bf16[4,32,1152]{2,1,0:T(8,128)(2,1)S(1)} %collective-permute-done.11.refs_1_), channel_id=1, source_target_pairs={{0,2},{2,0},{1,3},{3,1},{4,6},{6,4},{5,7},{7,5},{8,10},{10,8},{9,1... | collective-permute-start | bytes 884744 | tf_op jit(solution)/shard_map/ppermute | solution.py:447
  73.6 1.9 %collective-permute-start.17 = (bf16[4,32,1152]{2,1,0:T(8,128)(2,1)S(1)}, bf16[4,32,1152]{2,1,0:T(8,128)(2,1)S(1)}, u32[]{:S(2)}, u32[]{:S(2)}) collective-permute-start(bf16[4,32,1152]{2,1,0:T(8,128)(2,1)S(1)} %collective-permute-done.12.refs_2_), channel_id=1, source_target_pairs={{0,2},{2,0},{1,3},{3,1},{4,6},{6,4},{5,7},{7,5},{8,10},{10,8},{9,1... | collective-permute-start | bytes 884744 | tf_op jit(solution)/shard_map/ppermute | solution.py:447
  73.7 2.2 %collective-permute-start.18 = (bf16[4,32,1152]{2,1,0:T(8,128)(2,1)S(1)}, bf16[4,32,1152]{2,1,0:T(8,128)(2,1)S(1)}, u32[]{:S(2)}, u32[]{:S(2)}) collective-permute-start(bf16[4,32,1152]{2,1,0:T(8,128)(2,1)S(1)} %collective-permute-done.13.refs_3_), channel_id=1, source_target_pairs={{0,2},{2,0},{1,3},{3,1},{4,6},{6,4},{5,7},{7,5},{8,10},{10,8},{9,1... | collective-permute-start | bytes 884744 | tf_op jit(solution)/shard_map/ppermute | solution.py:447
  74.1 6.9 %collective-permute-start.19 = (bf16[1,64,1024]{2,1,0:T(8,128)(2,1)S(1)}, bf16[1,64,1024]{2,1,0:T(8,128)(2,1)S(1)}, u32[]{:S(2)}, u32[]{:S(2)}) collective-permute-start(bf16[1,64,1024]{2,1,0:T(8,128)(2,1)S(1)} %copy-done.4), channel_id=1, source_target_pairs={{0,1},{1,0},{2,3},{3,2},{4,5},{5,4},{6,7},{7,6},{8,9},{9,8},{10,11... | collective-permute-start | bytes 393224 | tf_op jit(solution)/shard_map/ppermute | solution.py:447
  84.7 19.0 %copy-start = (bf16[1024,1024]{1,0:T(8,128)(2,1)S(1)}, bf16[1024,1024]{1,0:T(8,128)(2,1)}, u32[]{:S(2)}) copy-start(bf16[1024,1024]{1,0:T(8,128)(2,1)} %get-tuple-element.36.normed_any.normed_ref) | copy-start | bytes 6291460
  97.4 6.3 %collective-permute-start.20 = (bf16[128,256]{1,0:T(8,128)(2,1)S(1)}, bf16[128,256]{1,0:T(8,128)(2,1)S(1)}, u32[]{:S(2)}, u32[]{:S(2)}) collective-permute-start(bf16[128,256]{1,0:T(8,128)(2,1)S(1)} %get-tuple-element.55), channel_id=1, source_target_pairs={{0,16},{16,0},{1,17},{17,1},{2,18},{18,2},{3,19},{19,3},{4,20},{20... | collective-permute-start | bytes 196616 | tf_op jit(solution)/shard_map/ppermute | solution.py:447
  105.8 18.7 %all-to-all-start.3 = ((bf16[32,32,256]{2,1,0:T(8,128)(2,1)}), bf16[32,32,256]{2,1,0:T(8,128)(2,1)S(1)}, u32[]{:S(2)}, u32[]{:S(2)}) async-start(bf16[32,32,256]{2,1,0:T(8,128)(2,1)} %bitcast.10), calls=%async_computation.3 | async-start | bytes 1048576 | tf_op jit(solution)/shard_map/all_to_all | solution.py:443
  108.5 6.0 %collective-permute-start.21 = (f32[100,128]{1,0:T(8,128)S(1)}, f32[100,128]{1,0:T(8,128)S(1)}, u32[]{:S(2)}, u32[]{:S(2)}) collective-permute-start(f32[100,128]{1,0:T(8,128)S(1)} %get-tuple-element.58), channel_id=1, source_target_pairs={{0,1},{1,0},{2,3},{3,2},{4,5},{5,4},{6,7},{7,6},{8,9},{9,8},{10,11... | collective-permute-start | bytes 153608 | tf_op jit(solution)/shard_map/ppermute | solution.py:447

commit v18 on v13

--- a/solution.py
+++ b/solution.py
@@ -142,6 +142,23 @@
     normed[rows:, :] = jnp.zeros((NOTE_ROWS, LATENT_DIM), BF16)
     normed[rows:, :128] = note.astype(BF16)
     wait(out + fetch([(normed, normed_any)], sems, 2 + len(out)))
+
+
+def merge_halves_kernel(mine_ref, other_ref, sent_ref, out_ref):
+    half = lax.axis_index("half")
+    width = mine_ref.shape[1]
+    out_ref[half, :, :width] = mine_ref[...]
+    out_ref[half ^ 1, :, :width] = other_ref[...]
+    out_ref[:, :, width:] = sent_ref[...].reshape(2, -1, LATENT_DIM)
+
+
+def merge_members_kernel(mine_ref, other_ref, packed_ref, source_ref):
+    ens = lax.axis_index("ens")
+    width = packed_ref.shape[3]
+    for half in range(2):
+        packed_ref[half, ens] = mine_ref[half, :, :width]
+        packed_ref[half, ens ^ 1] = other_ref[half, :, :width]
+    source_ref[...] = other_ref[:, :, width:].reshape(source_ref.shape)
 
 
 def owners():
@@ -496,7 +513,18 @@
         results="h" + "h" * source_parts,
     )(neighbours, members.reshape(node_rows, LATENT_DIM))
 
-    packed, normed = lax.optimization_barrier((in_order(packed, "half", 0), normed))
+    square = paired and halves == 2 and shard % 16 == 0
+    if square:
+        (packed,) = call(
+            merge_halves_kernel,
+            "merge_halves",
+            [((2, shard, width + LATENT_DIM), BF16)],
+            "vvv",
+            moved=2**18,
+        )(packed, swap(packed, "half", 1), sources[1])
+    else:
+        packed = in_order(packed, "half", 0)
+    packed, normed = lax.optimization_barrier((packed, normed))
     near = [normed, swap(normed, "quad", 1), None, swap(normed, "quad", 3)]
     if paired:
         columns = exchange(columns.reshape(-1, shard, 3 * COLS), nodes)
@@ -518,7 +546,18 @@
         results="hv",
     )(*near, *far)
 
-    packed = in_order(packed, "ens", 1).reshape(halves, members_num * shard, width)
+    if square:
+        packed, arrived = call(
+            merge_members_kernel,
+            "merge_members",
+            [((2, 2, shard, width), BF16), ((1, part, LATENT_DIM), BF16)],
+            "vv",
+            moved=2**19,
+        )(packed, swap(packed, "ens", 1))
+        packed = packed.reshape(2, 2 * shard, width)
+        sources = [sources[0], arrived]
+    else:
+        packed = in_order(packed, "ens", 1).reshape(halves, members_num * shard, width)
     packed, near[2] = lax.optimization_barrier((packed, near[2]))
     pieces = [packed] + [swap(packed, "quad", step) for step in range(1, QUAD)]
 
@@ -540,8 +579,10 @@
             return got, got
         return lax.ppermute(inner[1], "half", up), lax.ppermute(inner[0], "half", down)
 
-    weights, sources[-1] = lax.optimization_barrier((weights, sources[-1]))
-    sources = [sources[0], swap(sources[1], "ens", 1)] if paired else [exchange(sources[0], "ens")]
+    if not paired:
+        sources = [exchange(sources[0], "ens")]
+    elif not square:
+        sources = [sources[0], swap(sources[1], "ens", 1)]
     low, high = across(inner)
     queries, own = call(
         project_kernel,

time: 110 us -> 117 us (1.064)
  waiting for transfers between devices: 33.9 us -> 38.2 us
  local copies, waits for them, and re-layouts: 0.8 us -> 3.52 us
  starting transfers between devices: 36.1 us -> 37.8 us
  blocking collectives: 11.2 us -> 9.88 us
    ppermute x21 -> x20, waiting for transfers between devices: 18.9 us -> 26.9 us  [swap(): lax.ppermute(value, axis, [(i, i ^ step) for i in range(lax.axis_size(axi...]
    all_to_all x3, waiting for transfers between devices: 15 us -> 11.4 us  [exchange(): return lax.all_to_all(chunks, axes, 0, 0)]
    all_to_all x3, starting transfers between devices: 13.4 us -> 16.2 us  [exchange(): return lax.all_to_all(chunks, axes, 0, 0)]
    unnamed x11 -> x13, local copies, waits for them, and re-layouts: 0.7 us -> 3.44 us
    all_to_all x1, blocking collectives: 11.2 us -> 9.88 us  [exchange(): return lax.all_to_all(chunks, axes, 0, 0)]
    ppermute x21 -> x20, starting transfers between devices: 22.7 us -> 21.5 us  [swap(): lax.ppermute(value, axis, [(i, i ^ step) for i in range(lax.axis_size(axi...]
    pallas_call x13 -> x15, Pallas kernels: 25.9 us -> 26 us  [run(): made(*[pltpu.with_memory_space_constraint(arg, pltpu.HBM) if space == 'h'...]
  transfers between devices with their start and end apart: 24 -> 23, of which waited for: 8 -> 12; matrix products, arithmetic and copies ran while one was open for 2% -> 1% of each run, Pallas kernels for 15% -> 14%
where the time goes in v18:
time: 117 us; the launch traced here: 116 us
  waiting for transfers between devices  38.2 us (33%)
  starting transfers between devices  37.8 us (32%)
  Pallas kernels  26 us (22%)
  blocking collectives  9.88 us (8%)
  local copies, waits for them, and re-layouts  3.52 us (3%)
    ppermute x20, waiting for transfers between devices, swap(): lax.ppermute(value, axis, [(i, i ^ step) for i in range(lax.axis_size(axi...  26.9 us
    pallas_call x15, Pallas kernels, run(): made(*[pltpu.with_memory_space_constraint(arg, pltpu.HBM) if space == 'h'...  26 us
    ppermute x20, starting transfers between devices, swap(): lax.ppermute(value, axis, [(i, i ^ step) for i in range(lax.axis_size(axi...  21.5 us
    all_to_all x3, starting transfers between devices, exchange(): return lax.all_to_all(chunks, axes, 0, 0)  16.2 us
    all_to_all x3, waiting for transfers between devices, exchange(): return lax.all_to_all(chunks, axes, 0, 0)  11.4 us
    all_to_all x1, blocking collectives, exchange(): return lax.all_to_all(chunks, axes, 0, 0)  9.88 us
    unnamed x13, local copies, waits for them, and re-layouts  3.44 us
  transfers between devices with their start and end apart: 23, of which 12 were waited for; matrix products, arithmetic and copies ran while one was open for 1% of the time, Pallas kernels for 14%

profile of v18, /device:TPU:1, one launch (start us, length us, event | category | flops | bytes accessed | tf_op | source)
XLA Modules:
  0.0 116.3 jit_solution(16946979302868349110)
XLA Ops:
  0.6 1.8 %prepare_weights.1 = (bf16[2,8,1,32,384]{4,3,2,1,0:T(8,128)(2,1)}, bf16[32,1152]{1,0:T(8,128)(2,1)}) custom-call(bf16[32,3072]{1,0:T(8,128)(2,1)} %w_any.1, bf16[32,1024]{1,0:T(8,128)(2,1)} %mix_any.1, bf16[32,100]{1,0:T(8,128)(2,1)} %readout_any.1), custom_call_target="tpu_custom_call" | custom-call | bytes 1048576 | tf_op jit(solution)/shard_map/prepare_weights/pallas_call | solution.py:63
  2.4 7.4 %all-to-all-start = ((bf16[16,32,384]{2,1,0:T(8,128)(2,1)}), bf16[16,32,384]{2,1,0:T(8,128)(2,1)S(1)}, u32[]{:S(2)}, u32[]{:S(2)}) async-start(bf16[16,32,384]{2,1,0:T(8,128)(2,1)} %bitcast.19), calls=%async_computation | async-start | bytes 786432 | tf_op jit(solution)/shard_map/all_to_all | solution.py:453
  9.8 2.3 %collective-permute-start = (bf16[32,1152]{1,0:T(8,128)(2,1)}, bf16[32,1152]{1,0:T(8,128)(2,1)S(1)}, u32[]{:S(2)}, u32[]{:S(2)}) collective-permute-start(bf16[32,1152]{1,0:T(8,128)(2,1)} %get-tuple-element.31.mine_ref), channel_id=1, source_target_pairs={{0,16},{16,0},{1,17},{17,1},{2,18},{18,2},{3,19},{19,3},{4,20},{20... | collective-permute-start | bytes 221192 | tf_op jit(solution)/shard_map/ppermute | solution.py:457
  12.1 1.9 %norm.1 = (bf16[144,1024]{1,0:T(8,128)(2,1)}, bf16[1,64,1024]{2,1,0:T(8,128)(2,1)}, bf16[1,64,1024]{2,1,0:T(8,128)(2,1)}) custom-call(s32[2,4]{1,0:T(2,128)} %near_any.1, bf16[128,1024]{1,0:T(8,128)(2,1)} %bitcast.20), custom_call_target="tpu_custom_call" | custom-call | flops 1048576 | bytes 1048576 | tf_op jit(solution)/shard_map/norm/pallas_call | solution.py:63
  14.0 10.7 %collective-permute-done.other_ref = bf16[32,1152]{1,0:T(8,128)(2,1)S(1)} collective-permute-done((bf16[32,1152]{1,0:T(8,128)(2,1)}, bf16[32,1152]{1,0:T(8,128)(2,1)S(1)}, u32[]{:S(2)}, u32[]{:S(2)}) %collective-permute-start) | collective-permute-done | bytes 73760 | tf_op jit(solution)/shard_map/ppermute | solution.py:457
  24.6 0.9 copy-done.3
  25.5 0.9 copy-done.4
  26.5 1.2 %collective-permute-start.1 = (bf16[144,1024]{1,0:T(8,128)(2,1)}, bf16[144,1024]{1,0:T(8,128)(2,1)S(1)}, u32[]{:S(2)}, u32[]{:S(2)}) collective-permute-start(bf16[144,1024]{1,0:T(8,128)(2,1)} %get-tuple-element.36.refs_0_), channel_id=1, source_target_pairs={{0,4},{4,0},{8,12},{12,8},{1,5},{5,1},{9,13},{13,9},{2,6},{6,2},{1... | collective-permute-start | bytes 884744 | tf_op jit(solution)/shard_map/ppermute | solution.py:457
  27.7 1.5 %collective-permute-start.2 = (bf16[144,1024]{1,0:T(8,128)(2,1)}, bf16[144,1024]{1,0:T(8,128)(2,1)S(1)}, u32[]{:S(2)}, u32[]{:S(2)}) collective-permute-start(bf16[144,1024]{1,0:T(8,128)(2,1)} %get-tuple-element.36.refs_0_), channel_id=1, source_target_pairs={{0,8},{4,12},{8,0},{12,4},{1,9},{5,13},{9,1},{13,5},{2,10},{6,14},... | collective-permute-start | bytes 884744 | tf_op jit(solution)/shard_map/ppermute | solution.py:457
  29.2 1.2 %collective-permute-start.9 = (bf16[2,32,2176]{2,1,0:T(8,128)(2,1)S(1)}, bf16[2,32,2176]{2,1,0:T(8,128)(2,1)S(1)}, u32[]{:S(2)}, u32[]{:S(2)}) collective-permute-start(bf16[2,32,2176]{2,1,0:T(8,128)(2,1)S(1)} %merge_halves.1.mine_ref), channel_id=1, source_target_pairs={{0,1},{1,0},{2,3},{3,2},{4,5},{5,4},{6,7},{7,6},{8,9},{9,8},{10,11... | collective-permute-start | bytes 835592 | tf_op jit(solution)/shard_map/ppermute | solution.py:457
  30.4 0.3 collective-permute-start.8
  30.7 5.0 %collective-permute-done.9.other_ref = bf16[2,32,2176]{2,1,0:T(8,128)(2,1)S(1)} collective-permute-done((bf16[2,32,2176]{2,1,0:T(8,128)(2,1)S(1)}, bf16[2,32,2176]{2,1,0:T(8,128)(2,1)S(1)}, u32[]{:S(2)}, u32[]{:S(2)}) %collective-permute-start.9) | collective-permute-done | bytes 278560 | tf_op jit(solution)/shard_map/ppermute | solution.py:457
  35.6 4.9 %collective-permute-start.4 = (bf16[144,1024]{1,0:T(8,128)(2,1)}, bf16[144,1024]{1,0:T(8,128)(2,1)S(1)}, u32[]{:S(2)}, u32[]{:S(2)}) collective-permute-start(bf16[144,1024]{1,0:T(8,128)(2,1)} %get-tuple-element.36.refs_0_), channel_id=1, source_target_pairs={{0,2},{2,0},{1,3},{3,1},{4,6},{6,4},{5,7},{7,5},{8,10},{10,8},{9,1... | collective-permute-start | bytes 884744 | tf_op jit(solution)/shard_map/ppermute | solution.py:457
  40.5 0.2 collective-permute-done.1.refs_1_
  40.7 1.8 %collective-permute-start.5 = (bf16[144,1024]{1,0:T(8,128)(2,1)S(1)}, bf16[144,1024]{1,0:T(8,128)(2,1)S(1)}, u32[]{:S(2)}, u32[]{:S(2)}) collective-permute-start(bf16[144,1024]{1,0:T(8,128)(2,1)S(1)} %collective-permute-done.1.refs_1_), channel_id=1, source_target_pairs={{0,2},{2,0},{1,3},{3,1},{4,6},{6,4},{5,7},{7,5},{8,10},{10,8},{9,1... | collective-permute-start | bytes 884744 | tf_op jit(solution)/shard_map/ppermute | solution.py:457
  42.5 1.2 %collective-permute-start.6 = (bf16[144,1024]{1,0:T(8,128)(2,1)S(1)}, bf16[144,1024]{1,0:T(8,128)(2,1)S(1)}, u32[]{:S(2)}, u32[]{:S(2)}) collective-permute-start(bf16[144,1024]{1,0:T(8,128)(2,1)S(1)} %collective-permute-done.2.refs_2_), channel_id=1, source_target_pairs={{0,2},{2,0},{1,3},{3,1},{4,6},{6,4},{5,7},{7,5},{8,10},{10,8},{9,1... | collective-permute-start | bytes 884744 | tf_op jit(solution)/shard_map/ppermute | solution.py:457
  43.8 1.2 %collective-permute-start.10 = (bf16[2,64,1152]{2,1,0:T(8,128)(2,1)S(1)}, bf16[2,64,1152]{2,1,0:T(8,128)(2,1)S(1)}, u32[]{:S(2)}, u32[]{:S(2)}) collective-permute-start(bf16[2,64,1152]{2,1,0:T(8,128)(2,1)S(1)} %bitcast.13), channel_id=1, source_target_pairs={{0,4},{4,0},{8,12},{12,8},{1,5},{5,1},{9,13},{13,9},{2,6},{6,2},{1... | collective-permute-start | bytes 884744 | tf_op jit(solution)/shard_map/ppermute | solution.py:457
  45.0 1.5 %collective-permute-start.12 = (bf16[2,64,1152]{2,1,0:T(8,128)(2,1)S(1)}, bf16[2,64,1152]{2,1,0:T(8,128)(2,1)S(1)}, u32[]{:S(2)}, u32[]{:S(2)}) collective-permute-start(bf16[2,64,1152]{2,1,0:T(8,128)(2,1)S(1)} %bitcast.15), channel_id=1, source_target_pairs={{0,12},{4,8},{8,4},{12,0},{1,13},{5,9},{9,5},{13,1},{2,14},{6,10},... | collective-permute-start | bytes 884744 | tf_op jit(solution)/shard_map/ppermute | solution.py:457
  46.5 1.0 copy-done.1
  47.5 1.5 %collect.1 = (bf16[1024,1024]{1,0:T(8,128)(2,1)}, f32[8,16,128]{2,1,0:T(8,128)S(1)}) custom-call(bf16[144,1024]{1,0:T(8,128)(2,1)S(1)} %copy-done.1, bf16[144,1024]{1,0:T(8,128)(2,1)S(1)} %collective-permute-done.1.refs_1_, bf16[144,1024]{1,0:T(8,128)(2,1)S(1)} %collective-permute-done.2.refs_2_, bf16[144,1024]{1,0:T(8,128)(2,1)S(1)} %collective-permute-done.3.refs_3_, ...), custom_call_target="tpu_custom_call" | custom-call | bytes 4194304 | tf_op jit(solution)/shard_map/collect/pallas_call | solution.py:63
  49.0 1.3 %project_rims.1 = (bf16[16,2,32,384]{3,2,1,0:T(8,128)(2,1)S(1)}, bf16[128,256]{1,0:T(8,128)(2,1)S(1)}) custom-call(bf16[1024,1024]{1,0:T(8,128)(2,1)} %get-tuple-element.37.normed_any.normed_ref, bf16[16,32,384]{2,1,0:T(8,128)(2,1)S(1)} %all-to-all-done.refs_0_, bf16[16,32,384]{2,1,0:T(8,128)(2,1)S(1)} %collective-permute-done.8.refs_1_), custom_call_target="tpu_custom_call" | custom-call | flops 67108864 | bytes 1048576 | tf_op jit(solution)/shard_map/project_rims/pallas_call | solution.py:63
  50.3 0.3 collective-permute-start.13
  50.6 2.8 %project.1 = (bf16[1024,128]{1,0:T(8,128)(2,1)S(1)}, bf16[1024,256]{1,0:T(8,128)(2,1)S(1)}) custom-call(bf16[1024,1024]{1,0:T(8,128)(2,1)} %get-tuple-element.37.normed_any.normed_ref, bf16[16,2,32,384]{3,2,1,0:T(8,128)(2,1)S(1)} %get-tuple-element.40.w_ref), custom_call_target="tpu_custom_call" | custom-call | flops 805306368 | bytes 4194304 | tf_op jit(solution)/shard_map/project/pallas_call | solution.py:63
  53.4 1.9 %attention_interior.1.done_ref = bf16[1024,128]{1,0:T(8,128)(2,1)S(1)} custom-call(f32[8,16,128]{2,1,0:T(8,128)S(1)} %get-tuple-element.38.steps_ref, bf16[1024,128]{1,0:T(8,128)(2,1)S(1)} %get-tuple-element.41.q_ref, bf16[1024,256]{1,0:T(8,128)(2,1)S(1)} %get-tuple-element.46.kv_ref), custom_call_target="tpu_custom_call" | custom-call | flops 268435456 | bytes 2097152 | tf_op jit(solution)/shard_map/attention_interior/pallas_call | solution.py:63
  55.3 3.9 %collective-permute-done.13.low_ref.high_ref = bf16[128,256]{1,0:T(8,128)(2,1)S(1)} collective-permute-done((bf16[128,256]{1,0:T(8,128)(2,1)S(1)}, bf16[128,256]{1,0:T(8,128)(2,1)S(1)}, u32[]{:S(2)}, u32[]{:S(2)}) %collective-permute-start.13) | collective-permute-done | bytes 65568 | tf_op jit(solution)/shard_map/ppermute | solution.py:457
  59.2 1.4 %attention_edges.1 = bf16[1024,128]{1,0:T(8,128)(2,1)} custom-call(f32[8,16,128]{2,1,0:T(8,128)S(1)} %get-tuple-element.38.steps_ref, bf16[1024,128]{1,0:T(8,128)(2,1)S(1)} %get-tuple-element.41.q_ref, bf16[1024,256]{1,0:T(8,128)(2,1)S(1)} %get-tuple-element.46.kv_ref, bf16[128,256]{1,0:T(8,128)(2,1)S(1)} %collective-permute-done.13.low_ref.high_ref, ...), custom_call_target="tpu_custom_call" | custom-call | flops 67108864 | bytes 1048576 | tf_op jit(solution)/shard_map/attention_edges/pallas_call | solution.py:63
  60.6 5.7 %all-to-all-start.1 = ((bf16[16,64,128]{2,1,0:T(8,128)(2,1)}), bf16[16,64,128]{2,1,0:T(8,128)(2,1)S(1)}, u32[]{:S(2)}, u32[]{:S(2)}) async-start(bf16[16,64,128]{2,1,0:T(8,128)(2,1)} %bitcast.3), calls=%async_computation.1 | async-start | bytes 524288 | tf_op jit(solution)/shard_map/all_to_all | solution.py:453
  66.5 0.4 collective-permute-start.15
  67.0 0.4 collective-permute-start.17
  67.5 0.6 collective-permute-done.14.refs_4_
  68.0 0.4 collective-permute-done.15.refs_5_
  68.4 0.4 collective-permute-done.16.refs_6_
  68.9 0.4 collective-permute-done.17.refs_7_
  69.3 1.5 %assemble.1.w_any = bf16[2,4,2,64,1152]{4,3,2,1,0:T(8,128)(2,1)} custom-call(bf16[2,64,1152]{2,1,0:T(8,128)(2,1)S(1)} %bitcast.17, bf16[2,64,1152]{2,1,0:T(8,128)(2,1)S(1)} %collective-permute-done.10.refs_1_, bf16[2,64,1152]{2,1,0:T(8,128)(2,1)S(1)} %collective-permute-done.11.refs_2_, bf16[2,64,1152]{2,1,0:T(8,128)(2,1)S(1)} %collective-permute-done.12.refs_3_, ...), custom_call_target="tpu_custom_call" | custom-call | bytes 4194304 | tf_op jit(solution)/shard_map/assemble/pallas_call | solution.py:63
  70.8 2.4 %all-to-all-done.1.att_ref = bf16[16,64,128]{2,1,0:T(8,128)(2,1)S(1)} async-done(((bf16[16,64,128]{2,1,0:T(8,128)(2,1)}), bf16[16,64,128]{2,1,0:T(8,128)(2,1)S(1)}, u32[]{:S(2)}, u32[]{:S(2)}) %all-to-all-start.1) | async-done | bytes 262176 | tf_op jit(solution)/shard_map/all_to_all | solution.py:453
  73.2 3.7 %mix_loss_backward.1 = (f32[100,128]{1,0:T(8,128)S(1)}, bf16[16,64,128]{2,1,0:T(8,128)(2,1)S(1)}) custom-call(bf16[16,64,128]{2,1,0:T(8,128)(2,1)S(1)} %all-to-all-done.1.att_ref, f32[1,128]{1,0:T(1,128)S(1)} %bitcast.18, f32[100,128]{1,0:T(8,128)} %truth_any.1, bf16[2,4,2,64,1152]{4,3,2,1,0:T(8,128)(2,1)} %assemble.1.w_any, ...), custom_call_target="tpu_custom_call" | custom-call | flops 603979776 | bytes 4194304 | tf_op jit(solution)/shard_map/mix_loss_backward/pallas_call | solution.py:63
  76.9 9.9 %all_to_all.20 = bf16[16,64,128]{2,1,0:T(8,128)(2,1)S(1)} all-to-all(bf16[16,64,128]{2,1,0:T(8,128)(2,1)S(1)} %get-tuple-element.54), channel_id=1, replica_groups=mesh['half'=2,'quad'=4,'core'=2,'ens'=2] {'quad','core','ens'}, dimensions={0} | all-to-all | bytes 524288 | tf_op jit(solution)/shard_map/all_to_all | solution.py:453
  86.8 1.4 %attention_edges_back.1 = (f32[2,256,256]{2,1,0:T(8,128)S(1)}, bf16[128,256]{1,0:T(8,128)(2,1)S(1)}) custom-call(f32[8,16,128]{2,1,0:T(8,128)S(1)} %get-tuple-element.38.steps_ref, bf16[1024,128]{1,0:T(8,128)(2,1)S(1)} %get-tuple-element.41.q_ref, bf16[1024,256]{1,0:T(8,128)(2,1)S(1)} %get-tuple-element.46.kv_ref, ...), custom_call_target="tpu_custom_call" | custom-call | flops 167772160 | bytes 1048576 | tf_op jit(solution)/shard_map/attention_edges_back/pallas_call | solution.py:63
  88.2 1.7 %collective-permute-start.18 = (bf16[128,256]{1,0:T(8,128)(2,1)S(1)}, bf16[128,256]{1,0:T(8,128)(2,1)S(1)}, u32[]{:S(2)}, u32[]{:S(2)}) collective-permute-start(bf16[128,256]{1,0:T(8,128)(2,1)S(1)} %get-tuple-element.55), channel_id=1, source_target_pairs={{0,16},{16,0},{1,17},{17,1},{2,18},{18,2},{3,19},{19,3},{4,20},{20... | collective-permute-start | bytes 196616 | tf_op jit(solution)/shard_map/ppermute | solution.py:457
  89.8 3.8 %attention_interior_back.1.grads_ref = f32[1024,256]{1,0:T(8,128)S(1)} custom-call(f32[8,16,128]{2,1,0:T(8,128)S(1)} %get-tuple-element.38.steps_ref, bf16[1024,128]{1,0:T(8,128)(2,1)S(1)} %get-tuple-element.41.q_ref, bf16[1024,256]{1,0:T(8,128)(2,1)S(1)} %get-tuple-element.46.kv_ref, bf16[1024,128]{1,0:T(8,128)(2,1)S(1)} %bitcast.11, ...), custom_call_target="tpu_custom_call" | custom-call | flops 536870912 | bytes 4194304 | tf_op jit(solution)/shard_map/attention_interior_back/pallas_call | solution.py:63
  93.7 0.8 collective-permute-done.18.from_low_ref.from_high_ref
  94.5 2.1 %product.1 = bf16[1024,256]{1,0:T(8,128)(2,1)} custom-call(bf16[1024,1024]{1,0:T(8,128)(2,1)S(1)} %copy-done, bf16[128,256]{1,0:T(8,128)(2,1)S(1)} %collective-permute-done.18.from_low_ref.from_high_ref, bf16[128,256]{1,0:T(8,128)(2,1)S(1)} %collective-permute-done.18.from_low_ref.from_high_ref, f32[1024,256]{1,0:T(8,128)S(1)} %attention_interior_back.1.grads_ref), custom_call_target="tpu_custom_call" | custom-call | flops 1073741824 | bytes 4194304 | tf_op jit(solution)/shard_map/product/pallas_call | solution.py:63
  96.5 3.2 %all-to-all-start.3 = ((bf16[32,32,256]{2,1,0:T(8,128)(2,1)}), bf16[32,32,256]{2,1,0:T(8,128)(2,1)S(1)}, u32[]{:S(2)}, u32[]{:S(2)}) async-start(bf16[32,32,256]{2,1,0:T(8,128)(2,1)} %bitcast.7), calls=%async_computation.3 | async-start | bytes 1048576 | tf_op jit(solution)/shard_map/all_to_all | solution.py:453
  99.7 1.5 %collective-permute-start.19 = (f32[100,128]{1,0:T(8,128)S(1)}, f32[100,128]{1,0:T(8,128)S(1)}, u32[]{:S(2)}, u32[]{:S(2)}) collective-permute-start(f32[100,128]{1,0:T(8,128)S(1)} %get-tuple-element.58), channel_id=1, source_target_pairs={{0,1},{1,0},{2,3},{3,2},{4,5},{5,4},{6,7},{7,6},{8,9},{9,8},{10,11... | collective-permute-start | bytes 153608 | tf_op jit(solution)/shard_map/ppermute | solution.py:457
  101.2 4.5 %collective-permute-done.19 = f32[100,128]{1,0:T(8,128)S(1)} collective-permute-done((f32[100,128]{1,0:T(8,128)S(1)}, f32[100,128]{1,0:T(8,128)S(1)}, u32[]{:S(2)}, u32[]{:S(2)}) %collective-permute-start.19) | collective-permute-done | bytes 51232 | tf_op jit(solution)/shard_map/ppermute | solution.py:457
  105.9 0.7 copy.9
  106.6 9.0 %all-to-all-done.3 = bf16[32,32,256]{2,1,0:T(8,128)(2,1)S(1)} async-done(((bf16[32,32,256]{2,1,0:T(8,128)(2,1)}), bf16[32,32,256]{2,1,0:T(8,128)(2,1)S(1)}, u32[]{:S(2)}, u32[]{:S(2)}) %all-to-all-start.3) | async-done | bytes 524320 | tf_op jit(solution)/shard_map/all_to_all | solution.py:453
  115.5 0.8 gather_sums.1
  (31 shorter events, 0.6 us)
Async XLA Ops:
  2.4 25.3 %all-to-all-start = ((bf16[16,32,384]{2,1,0:T(8,128)(2,1)}), bf16[16,32,384]{2,1,0:T(8,128)(2,1)S(1)}, u32[]{:S(2)}, u32[]{:S(2)}) async-start(bf16[16,32,384]{2,1,0:T(8,128)(2,1)} %bitcast.19), calls=%async_computation | async-start | bytes 786432 | tf_op jit(solution)/shard_map/all_to_all | solution.py:453
  9.8 14.8 %collective-permute-start = (bf16[32,1152]{1,0:T(8,128)(2,1)}, bf16[32,1152]{1,0:T(8,128)(2,1)S(1)}, u32[]{:S(2)}, u32[]{:S(2)}) collective-permute-start(bf16[32,1152]{1,0:T(8,128)(2,1)} %get-tuple-element.31.mine_ref), channel_id=1, source_target_pairs={{0,16},{16,0},{1,17},{17,1},{2,18},{18,2},{3,19},{19,3},{4,20},{20... | collective-permute-start | bytes 221192 | tf_op jit(solution)/shard_map/ppermute | solution.py:457
  24.6 0.9 copy-start.3
  25.5 0.9 copy-start.4
  26.5 14.2 %collective-permute-start.1 = (bf16[144,1024]{1,0:T(8,128)(2,1)}, bf16[144,1024]{1,0:T(8,128)(2,1)S(1)}, u32[]{:S(2)}, u32[]{:S(2)}) collective-permute-start(bf16[144,1024]{1,0:T(8,128)(2,1)} %get-tuple-element.36.refs_0_), channel_id=1, source_target_pairs={{0,4},{4,0},{8,12},{12,8},{1,5},{5,1},{9,13},{13,9},{2,6},{6,2},{1... | collective-permute-start | bytes 884744 | tf_op jit(solution)/shard_map/ppermute | solution.py:457
  27.7 14.8 %collective-permute-start.3 = (bf16[144,1024]{1,0:T(8,128)(2,1)}, bf16[144,1024]{1,0:T(8,128)(2,1)S(1)}, u32[]{:S(2)}, u32[]{:S(2)}) collective-permute-start(bf16[144,1024]{1,0:T(8,128)(2,1)} %get-tuple-element.36.refs_0_), channel_id=1, source_target_pairs={{0,12},{4,8},{8,4},{12,0},{1,13},{5,9},{9,5},{13,1},{2,14},{6,10},... | collective-permute-start | bytes 884744 | tf_op jit(solution)/shard_map/ppermute | solution.py:457
  27.7 14.8 %collective-permute-start.2 = (bf16[144,1024]{1,0:T(8,128)(2,1)}, bf16[144,1024]{1,0:T(8,128)(2,1)S(1)}, u32[]{:S(2)}, u32[]{:S(2)}) collective-permute-start(bf16[144,1024]{1,0:T(8,128)(2,1)} %get-tuple-element.36.refs_0_), channel_id=1, source_target_pairs={{0,8},{4,12},{8,0},{12,4},{1,9},{5,13},{9,1},{13,5},{2,10},{6,14},... | collective-permute-start | bytes 884744 | tf_op jit(solution)/shard_map/ppermute | solution.py:457
  29.2 6.4 %collective-permute-start.9 = (bf16[2,32,2176]{2,1,0:T(8,128)(2,1)S(1)}, bf16[2,32,2176]{2,1,0:T(8,128)(2,1)S(1)}, u32[]{:S(2)}, u32[]{:S(2)}) collective-permute-start(bf16[2,32,2176]{2,1,0:T(8,128)(2,1)S(1)} %merge_halves.1.mine_ref), channel_id=1, source_target_pairs={{0,1},{1,0},{2,3},{3,2},{4,5},{5,4},{6,7},{7,6},{8,9},{9,8},{10,11... | collective-permute-start | bytes 835592 | tf_op jit(solution)/shard_map/ppermute | solution.py:457
  30.4 18.6 %collective-permute-start.8 = (bf16[16,32,384]{2,1,0:T(8,128)(2,1)S(1)}, bf16[16,32,384]{2,1,0:T(8,128)(2,1)S(1)}, u32[]{:S(2)}, u32[]{:S(2)}) collective-permute-start(bf16[16,32,384]{2,1,0:T(8,128)(2,1)S(1)} %all-to-all-done.refs_0_), channel_id=1, source_target_pairs={{0,1},{1,0},{2,3},{3,2},{4,5},{5,4},{6,7},{7,6},{8,9},{9,8},{10,11... | collective-permute-start | bytes 1179656 | tf_op jit(solution)/shard_map/ppermute | solution.py:457
  35.6 8.1 %collective-permute-start.4 = (bf16[144,1024]{1,0:T(8,128)(2,1)}, bf16[144,1024]{1,0:T(8,128)(2,1)S(1)}, u32[]{:S(2)}, u32[]{:S(2)}) collective-permute-start(bf16[144,1024]{1,0:T(8,128)(2,1)} %get-tuple-element.36.refs_0_), channel_id=1, source_target_pairs={{0,2},{2,0},{1,3},{3,1},{4,6},{6,4},{5,7},{7,5},{8,10},{10,8},{9,1... | collective-permute-start | bytes 884744 | tf_op jit(solution)/shard_map/ppermute | solution.py:457
  40.7 4.3 %collective-permute-start.5 = (bf16[144,1024]{1,0:T(8,128)(2,1)S(1)}, bf16[144,1024]{1,0:T(8,128)(2,1)S(1)}, u32[]{:S(2)}, u32[]{:S(2)}) collective-permute-start(bf16[144,1024]{1,0:T(8,128)(2,1)S(1)} %collective-permute-done.1.refs_1_), channel_id=1, source_target_pairs={{0,2},{2,0},{1,3},{3,1},{4,6},{6,4},{5,7},{7,5},{8,10},{10,8},{9,1... | collective-permute-start | bytes 884744 | tf_op jit(solution)/shard_map/ppermute | solution.py:457
  42.5 2.5 %collective-permute-start.7 = (bf16[144,1024]{1,0:T(8,128)(2,1)S(1)}, bf16[144,1024]{1,0:T(8,128)(2,1)S(1)}, u32[]{:S(2)}, u32[]{:S(2)}) collective-permute-start(bf16[144,1024]{1,0:T(8,128)(2,1)S(1)} %collective-permute-done.3.refs_3_), channel_id=1, source_target_pairs={{0,2},{2,0},{1,3},{3,1},{4,6},{6,4},{5,7},{7,5},{8,10},{10,8},{9,1... | collective-permute-start | bytes 884744 | tf_op jit(solution)/shard_map/ppermute | solution.py:457
  42.5 4.0 %collective-permute-start.6 = (bf16[144,1024]{1,0:T(8,128)(2,1)S(1)}, bf16[144,1024]{1,0:T(8,128)(2,1)S(1)}, u32[]{:S(2)}, u32[]{:S(2)}) collective-permute-start(bf16[144,1024]{1,0:T(8,128)(2,1)S(1)} %collective-permute-done.2.refs_2_), channel_id=1, source_target_pairs={{0,2},{2,0},{1,3},{3,1},{4,6},{6,4},{5,7},{7,5},{8,10},{10,8},{9,1... | collective-permute-start | bytes 884744 | tf_op jit(solution)/shard_map/ppermute | solution.py:457
  43.8 22.6 %collective-permute-start.10 = (bf16[2,64,1152]{2,1,0:T(8,128)(2,1)S(1)}, bf16[2,64,1152]{2,1,0:T(8,128)(2,1)S(1)}, u32[]{:S(2)}, u32[]{:S(2)}) collective-permute-start(bf16[2,64,1152]{2,1,0:T(8,128)(2,1)S(1)} %bitcast.13), channel_id=1, source_target_pairs={{0,4},{4,0},{8,12},{12,8},{1,5},{5,1},{9,13},{13,9},{2,6},{6,2},{1... | collective-permute-start | bytes 884744 | tf_op jit(solution)/shard_map/ppermute | solution.py:457
  45.0 21.3 %collective-permute-start.11 = (bf16[2,64,1152]{2,1,0:T(8,128)(2,1)S(1)}, bf16[2,64,1152]{2,1,0:T(8,128)(2,1)S(1)}, u32[]{:S(2)}, u32[]{:S(2)}) collective-permute-start(bf16[2,64,1152]{2,1,0:T(8,128)(2,1)S(1)} %bitcast.14), channel_id=1, source_target_pairs={{0,8},{4,12},{8,0},{12,4},{1,9},{5,13},{9,1},{13,5},{2,10},{6,14},... | collective-permute-start | bytes 884744 | tf_op jit(solution)/shard_map/ppermute | solution.py:457
  45.0 21.3 %collective-permute-start.12 = (bf16[2,64,1152]{2,1,0:T(8,128)(2,1)S(1)}, bf16[2,64,1152]{2,1,0:T(8,128)(2,1)S(1)}, u32[]{:S(2)}, u32[]{:S(2)}) collective-permute-start(bf16[2,64,1152]{2,1,0:T(8,128)(2,1)S(1)} %bitcast.15), channel_id=1, source_target_pairs={{0,12},{4,8},{8,4},{12,0},{1,13},{5,9},{9,5},{13,1},{2,14},{6,10},... | collective-permute-start | bytes 884744 | tf_op jit(solution)/shard_map/ppermute | solution.py:457
  46.5 1.0 copy-start.1
  50.3 8.9 %collective-permute-start.13 = (bf16[128,256]{1,0:T(8,128)(2,1)S(1)}, bf16[128,256]{1,0:T(8,128)(2,1)S(1)}, u32[]{:S(2)}, u32[]{:S(2)}) collective-permute-start(bf16[128,256]{1,0:T(8,128)(2,1)S(1)} %get-tuple-element.47), channel_id=1, source_target_pairs={{0,16},{16,0},{1,17},{17,1},{2,18},{18,2},{3,19},{19,3},{4,20},{20... | collective-permute-start | bytes 196616 | tf_op jit(solution)/shard_map/ppermute | solution.py:457
  60.6 12.6 %all-to-all-start.1 = ((bf16[16,64,128]{2,1,0:T(8,128)(2,1)}), bf16[16,64,128]{2,1,0:T(8,128)(2,1)S(1)}, u32[]{:S(2)}, u32[]{:S(2)}) async-start(bf16[16,64,128]{2,1,0:T(8,128)(2,1)} %bitcast.3), calls=%async_computation.1 | async-start | bytes 524288 | tf_op jit(solution)/shard_map/all_to_all | solution.py:453
  66.3 6.9 %copy-start.2 = (bf16[1,64,1024]{2,1,0:T(8,128)(2,1)S(1)}, bf16[1,64,1024]{2,1,0:T(8,128)(2,1)}, u32[]{:S(2)}) copy-start(bf16[1,64,1024]{2,1,0:T(8,128)(2,1)} %get-tuple-element.52.refs_0_) | copy-start | bytes 393220
  66.3 6.9 %copy-start.5 = (f32[128]{0:T(128)S(1)}, f32[128]{0:T(128)}, u32[]{:S(2)}) copy-start(f32[128]{0:T(128)} %param.12) | copy-start | bytes 1540
  66.4 1.6 %collective-permute-start.14 = (bf16[2,64,1152]{2,1,0:T(8,128)(2,1)S(1)}, bf16[2,64,1152]{2,1,0:T(8,128)(2,1)S(1)}, u32[]{:S(2)}, u32[]{:S(2)}) collective-permute-start(bf16[2,64,1152]{2,1,0:T(8,128)(2,1)S(1)} %bitcast.16), channel_id=1, source_target_pairs={{0,2},{2,0},{1,3},{3,1},{4,6},{6,4},{5,7},{7,5},{8,10},{10,8},{9,1... | collective-permute-start | bytes 884744 | tf_op jit(solution)/shard_map/ppermute | solution.py:457
  66.5 1.9 %collective-permute-start.15 = (bf16[2,64,1152]{2,1,0:T(8,128)(2,1)S(1)}, bf16[2,64,1152]{2,1,0:T(8,128)(2,1)S(1)}, u32[]{:S(2)}, u32[]{:S(2)}) collective-permute-start(bf16[2,64,1152]{2,1,0:T(8,128)(2,1)S(1)} %collective-permute-done.10.refs_1_), channel_id=1, source_target_pairs={{0,2},{2,0},{1,3},{3,1},{4,6},{6,4},{5,7},{7,5},{8,10},{10,8},{9,1... | collective-permute-start | bytes 884744 | tf_op jit(solution)/shard_map/ppermute | solution.py:457
  66.9 1.9 %collective-permute-start.16 = (bf16[2,64,1152]{2,1,0:T(8,128)(2,1)S(1)}, bf16[2,64,1152]{2,1,0:T(8,128)(2,1)S(1)}, u32[]{:S(2)}, u32[]{:S(2)}) collective-permute-start(bf16[2,64,1152]{2,1,0:T(8,128)(2,1)S(1)} %collective-permute-done.11.refs_2_), channel_id=1, source_target_pairs={{0,2},{2,0},{1,3},{3,1},{4,6},{6,4},{5,7},{7,5},{8,10},{10,8},{9,1... | collective-permute-start | bytes 884744 | tf_op jit(solution)/shard_map/ppermute | solution.py:457
  67.0 2.2 %collective-permute-start.17 = (bf16[2,64,1152]{2,1,0:T(8,128)(2,1)S(1)}, bf16[2,64,1152]{2,1,0:T(8,128)(2,1)S(1)}, u32[]{:S(2)}, u32[]{:S(2)}) collective-permute-start(bf16[2,64,1152]{2,1,0:T(8,128)(2,1)S(1)} %collective-permute-done.12.refs_3_), channel_id=1, source_target_pairs={{0,2},{2,0},{1,3},{3,1},{4,6},{6,4},{5,7},{7,5},{8,10},{10,8},{9,1... | collective-permute-start | bytes 884744 | tf_op jit(solution)/shard_map/ppermute | solution.py:457
  76.9 17.6 %copy-start = (bf16[1024,1024]{1,0:T(8,128)(2,1)S(1)}, bf16[1024,1024]{1,0:T(8,128)(2,1)}, u32[]{:S(2)}) copy-start(bf16[1024,1024]{1,0:T(8,128)(2,1)} %get-tuple-element.37.normed_any.normed_ref) | copy-start | bytes 6291460
  88.2 6.3 %collective-permute-start.18 = (bf16[128,256]{1,0:T(8,128)(2,1)S(1)}, bf16[128,256]{1,0:T(8,128)(2,1)S(1)}, u32[]{:S(2)}, u32[]{:S(2)}) collective-permute-start(bf16[128,256]{1,0:T(8,128)(2,1)S(1)} %get-tuple-element.55), channel_id=1, source_target_pairs={{0,16},{16,0},{1,17},{17,1},{2,18},{18,2},{3,19},{19,3},{4,20},{20... | collective-permute-start | bytes 196616 | tf_op jit(solution)/shard_map/ppermute | solution.py:457
  96.5 19.0 %all-to-all-start.3 = ((bf16[32,32,256]{2,1,0:T(8,128)(2,1)}), bf16[32,32,256]{2,1,0:T(8,128)(2,1)S(1)}, u32[]{:S(2)}, u32[]{:S(2)}) async-start(bf16[32,32,256]{2,1,0:T(8,128)(2,1)} %bitcast.7), calls=%async_computation.3 | async-start | bytes 1048576 | tf_op jit(solution)/shard_map/all_to_all | solution.py:453
  99.7 6.0 %collective-permute-start.19 = (f32[100,128]{1,0:T(8,128)S(1)}, f32[100,128]{1,0:T(8,128)S(1)}, u32[]{:S(2)}, u32[]{:S(2)}) collective-permute-start(f32[100,128]{1,0:T(8,128)S(1)} %get-tuple-element.58), channel_id=1, source_target_pairs={{0,1},{1,0},{2,3},{3,2},{4,5},{5,4},{6,7},{7,6},{8,9},{9,8},{10,11... | collective-permute-start | bytes 153608 | tf_op jit(solution)/shard_map/ppermute | solution.py:457

commit v19 on v18

--- a/solution.py
+++ b/solution.py
@@ -515,16 +515,17 @@
 
     square = paired and halves == 2 and shard % 16 == 0
     if square:
+        other = swap(packed, "half", 1)
+        columns, other, normed = lax.optimization_barrier((columns, other, normed))
         (packed,) = call(
             merge_halves_kernel,
             "merge_halves",
             [((2, shard, width + LATENT_DIM), BF16)],
             "vvv",
             moved=2**18,
-        )(packed, swap(packed, "half", 1), sources[1])
+        )(packed, other, sources[1])
     else:
         packed = in_order(packed, "half", 0)
-    packed, normed = lax.optimization_barrier((packed, normed))
     near = [normed, swap(normed, "quad", 1), None, swap(normed, "quad", 3)]
     if paired:
         columns = exchange(columns.reshape(-1, shard, 3 * COLS), nodes)

time: 117 us -> 117 us (level)
    all_to_all x3, waiting for transfers between devices: 11.4 us -> 20.3 us  [exchange(): return lax.all_to_all(chunks, axes, 0, 0)]
    ppermute x20, waiting for transfers between devices: 26.9 us -> 18.5 us  [swap(): lax.ppermute(value, axis, [(i, i ^ step) for i in range(lax.axis_size(axi...]
    ppermute x20, starting transfers between devices: 21.5 us -> 18.3 us  [swap(): lax.ppermute(value, axis, [(i, i ^ step) for i in range(lax.axis_size(axi...]
    all_to_all x3, starting transfers between devices: 16.2 us -> 18.7 us  [exchange(): return lax.all_to_all(chunks, axes, 0, 0)]
  transfers between devices with their start and end apart: 23 -> 23, of which waited for: 12 -> 14; matrix products, arithmetic and copies ran while one was open for 1% -> 1% of each run, Pallas kernels for 14% -> 14%
where the time goes in v19:
time: 117 us; the launch traced here: 116 us
  waiting for transfers between devices  38.9 us (33%)
  starting transfers between devices  37 us (32%)
  Pallas kernels  26 us (22%)
  blocking collectives  9.9 us (8%)
  local copies, waits for them, and re-layouts  3.51 us (3%)
    pallas_call x15, Pallas kernels, run(): made(*[pltpu.with_memory_space_constraint(arg, pltpu.HBM) if space == 'h'...  26 us
    all_to_all x3, waiting for transfers between devices, exchange(): return lax.all_to_all(chunks, axes, 0, 0)  20.3 us
    all_to_all x3, starting transfers between devices, exchange(): return lax.all_to_all(chunks, axes, 0, 0)  18.7 us
    ppermute x20, waiting for transfers between devices, swap(): lax.ppermute(value, axis, [(i, i ^ step) for i in range(lax.axis_size(axi...  18.5 us
    ppermute x20, starting transfers between devices, swap(): lax.ppermute(value, axis, [(i, i ^ step) for i in range(lax.axis_size(axi...  18.3 us
    all_to_all x1, blocking collectives, exchange(): return lax.all_to_all(chunks, axes, 0, 0)  9.9 us
    unnamed x13, local copies, waits for them, and re-layouts  3.44 us
  transfers between devices with their start and end apart: 23, of which 14 were waited for; matrix products, arithmetic and copies ran while one was open for 1% of the time, Pallas kernels for 14%

profile of v19, /device:TPU:1, one launch (start us, length us, event | category | flops | bytes accessed | tf_op | source)
XLA Modules:
  0.0 116.2 jit_solution(8975396807345113475)
XLA Ops:
  0.6 1.8 %prepare_weights.1 = (bf16[2,8,1,32,384]{4,3,2,1,0:T(8,128)(2,1)}, bf16[32,1152]{1,0:T(8,128)(2,1)}) custom-call(bf16[32,3072]{1,0:T(8,128)(2,1)} %w_any.1, bf16[32,1024]{1,0:T(8,128)(2,1)} %mix_any.1, bf16[32,100]{1,0:T(8,128)(2,1)} %readout_any.1), custom_call_target="tpu_custom_call" | custom-call | bytes 1048576 | tf_op jit(solution)/shard_map/prepare_weights/pallas_call | solution.py:63
  2.4 3.2 %collective-permute-start = (bf16[32,1152]{1,0:T(8,128)(2,1)}, bf16[32,1152]{1,0:T(8,128)(2,1)S(1)}, u32[]{:S(2)}, u32[]{:S(2)}) collective-permute-start(bf16[32,1152]{1,0:T(8,128)(2,1)} %get-tuple-element.33.mine_ref), channel_id=1, source_target_pairs={{0,16},{16,0},{1,17},{17,1},{2,18},{18,2},{3,19},{19,3},{4,20},{20... | collective-permute-start | bytes 221192 | tf_op jit(solution)/shard_map/ppermute | solution.py:457
  5.6 1.9 %norm.1 = (bf16[144,1024]{1,0:T(8,128)(2,1)}, bf16[1,64,1024]{2,1,0:T(8,128)(2,1)}, bf16[1,64,1024]{2,1,0:T(8,128)(2,1)}) custom-call(s32[2,4]{1,0:T(2,128)} %near_any.1, bf16[128,1024]{1,0:T(8,128)(2,1)} %bitcast.20), custom_call_target="tpu_custom_call" | custom-call | flops 1048576 | bytes 1048576 | tf_op jit(solution)/shard_map/norm/pallas_call | solution.py:63
  7.6 8.8 %all-to-all-start = ((bf16[16,32,384]{2,1,0:T(8,128)(2,1)}), bf16[16,32,384]{2,1,0:T(8,128)(2,1)S(1)}, u32[]{:S(2)}, u32[]{:S(2)}) async-start(bf16[16,32,384]{2,1,0:T(8,128)(2,1)} %bitcast.19), calls=%async_computation | async-start | bytes 786432 | tf_op jit(solution)/shard_map/all_to_all | solution.py:453
  16.4 1.4 %collective-permute-start.1 = (bf16[144,1024]{1,0:T(8,128)(2,1)}, bf16[144,1024]{1,0:T(8,128)(2,1)S(1)}, u32[]{:S(2)}, u32[]{:S(2)}) collective-permute-start(bf16[144,1024]{1,0:T(8,128)(2,1)} %get-tuple-element.37.refs_0_), channel_id=1, source_target_pairs={{0,4},{4,0},{8,12},{12,8},{1,5},{5,1},{9,13},{13,9},{2,6},{6,2},{1... | collective-permute-start | bytes 884744 | tf_op jit(solution)/shard_map/ppermute | solution.py:457
  17.8 1.2 %collective-permute-start.3 = (bf16[144,1024]{1,0:T(8,128)(2,1)}, bf16[144,1024]{1,0:T(8,128)(2,1)S(1)}, u32[]{:S(2)}, u32[]{:S(2)}) collective-permute-start(bf16[144,1024]{1,0:T(8,128)(2,1)} %get-tuple-element.37.refs_0_), channel_id=1, source_target_pairs={{0,12},{4,8},{8,4},{12,0},{1,13},{5,9},{9,5},{13,1},{2,14},{6,10},... | collective-permute-start | bytes 884744 | tf_op jit(solution)/shard_map/ppermute | solution.py:457
  19.0 8.9 %all-to-all-done.refs_0_ = bf16[16,32,384]{2,1,0:T(8,128)(2,1)S(1)} async-done(((bf16[16,32,384]{2,1,0:T(8,128)(2,1)}), bf16[16,32,384]{2,1,0:T(8,128)(2,1)S(1)}, u32[]{:S(2)}, u32[]{:S(2)}) %all-to-all-start) | async-done | bytes 393248 | tf_op jit(solution)/shard_map/all_to_all | solution.py:453
  27.9 1.7 %collective-permute-start.2 = (bf16[144,1024]{1,0:T(8,128)(2,1)}, bf16[144,1024]{1,0:T(8,128)(2,1)S(1)}, u32[]{:S(2)}, u32[]{:S(2)}) collective-permute-start(bf16[144,1024]{1,0:T(8,128)(2,1)} %get-tuple-element.37.refs_0_), channel_id=1, source_target_pairs={{0,8},{4,12},{8,0},{12,4},{1,9},{5,13},{9,1},{13,5},{2,10},{6,14},... | collective-permute-start | bytes 884744 | tf_op jit(solution)/shard_map/ppermute | solution.py:457
  29.6 0.9 copy-done.3
  30.5 0.9 copy-done.4
  31.4 1.3 %collective-permute-start.9 = (bf16[2,32,2176]{2,1,0:T(8,128)(2,1)S(1)}, bf16[2,32,2176]{2,1,0:T(8,128)(2,1)S(1)}, u32[]{:S(2)}, u32[]{:S(2)}) collective-permute-start(bf16[2,32,2176]{2,1,0:T(8,128)(2,1)S(1)} %merge_halves.1.mine_ref), channel_id=1, source_target_pairs={{0,1},{1,0},{2,3},{3,2},{4,5},{5,4},{6,7},{7,6},{8,9},{9,8},{10,11... | collective-permute-start | bytes 835592 | tf_op jit(solution)/shard_map/ppermute | solution.py:457
  33.0 7.0 %collective-permute-done.9.other_ref = bf16[2,32,2176]{2,1,0:T(8,128)(2,1)S(1)} collective-permute-done((bf16[2,32,2176]{2,1,0:T(8,128)(2,1)S(1)}, bf16[2,32,2176]{2,1,0:T(8,128)(2,1)S(1)}, u32[]{:S(2)}, u32[]{:S(2)}) %collective-permute-start.9) | collective-permute-done | bytes 278560 | tf_op jit(solution)/shard_map/ppermute | solution.py:457
  39.9 0.9 collective-permute-start.4
  40.8 0.5 collective-permute-start.7
  41.5 1.1 collective-permute-done.4.refs_4_
  42.6 1.4 %collective-permute-start.10 = (bf16[2,64,1152]{2,1,0:T(8,128)(2,1)S(1)}, bf16[2,64,1152]{2,1,0:T(8,128)(2,1)S(1)}, u32[]{:S(2)}, u32[]{:S(2)}) collective-permute-start(bf16[2,64,1152]{2,1,0:T(8,128)(2,1)S(1)} %bitcast.13), channel_id=1, source_target_pairs={{0,4},{4,0},{8,12},{12,8},{1,5},{5,1},{9,13},{13,9},{2,6},{6,2},{1... | collective-permute-start | bytes 884744 | tf_op jit(solution)/shard_map/ppermute | solution.py:457
  44.2 1.2 %collective-permute-start.12 = (bf16[2,64,1152]{2,1,0:T(8,128)(2,1)S(1)}, bf16[2,64,1152]{2,1,0:T(8,128)(2,1)S(1)}, u32[]{:S(2)}, u32[]{:S(2)}) collective-permute-start(bf16[2,64,1152]{2,1,0:T(8,128)(2,1)S(1)} %bitcast.15), channel_id=1, source_target_pairs={{0,12},{4,8},{8,4},{12,0},{1,13},{5,9},{9,5},{13,1},{2,14},{6,10},... | collective-permute-start | bytes 884744 | tf_op jit(solution)/shard_map/ppermute | solution.py:457
  45.5 1.0 copy-done.1
  46.5 1.5 %collect.1 = (bf16[1024,1024]{1,0:T(8,128)(2,1)}, f32[8,16,128]{2,1,0:T(8,128)S(1)}) custom-call(bf16[144,1024]{1,0:T(8,128)(2,1)S(1)} %copy-done.1, bf16[144,1024]{1,0:T(8,128)(2,1)S(1)} %collective-permute-done.1.refs_1_, bf16[144,1024]{1,0:T(8,128)(2,1)S(1)} %collective-permute-done.2.refs_2_, bf16[144,1024]{1,0:T(8,128)(2,1)S(1)} %collective-permute-done.3.refs_3_, ...), custom_call_target="tpu_custom_call" | custom-call | bytes 4194304 | tf_op jit(solution)/shard_map/collect/pallas_call | solution.py:63
  48.0 0.4 collective-permute-done.8.refs_1_
  48.3 1.3 %project_rims.1 = (bf16[16,2,32,384]{3,2,1,0:T(8,128)(2,1)S(1)}, bf16[128,256]{1,0:T(8,128)(2,1)S(1)}) custom-call(bf16[1024,1024]{1,0:T(8,128)(2,1)} %get-tuple-element.38.normed_any.normed_ref, bf16[16,32,384]{2,1,0:T(8,128)(2,1)S(1)} %all-to-all-done.refs_0_, bf16[16,32,384]{2,1,0:T(8,128)(2,1)S(1)} %collective-permute-done.8.refs_1_), custom_call_target="tpu_custom_call" | custom-call | flops 67108864 | bytes 1048576 | tf_op jit(solution)/shard_map/project_rims/pallas_call | solution.py:63
  49.6 1.1 collective-permute-start.13
  50.8 2.8 %project.1 = (bf16[1024,128]{1,0:T(8,128)(2,1)S(1)}, bf16[1024,256]{1,0:T(8,128)(2,1)S(1)}) custom-call(bf16[1024,1024]{1,0:T(8,128)(2,1)} %get-tuple-element.38.normed_any.normed_ref, bf16[16,2,32,384]{3,2,1,0:T(8,128)(2,1)S(1)} %get-tuple-element.41.w_ref), custom_call_target="tpu_custom_call" | custom-call | flops 805306368 | bytes 4194304 | tf_op jit(solution)/shard_map/project/pallas_call | solution.py:63
  53.6 1.9 %attention_interior.1.done_ref = bf16[1024,128]{1,0:T(8,128)(2,1)S(1)} custom-call(f32[8,16,128]{2,1,0:T(8,128)S(1)} %get-tuple-element.39.steps_ref, bf16[1024,128]{1,0:T(8,128)(2,1)S(1)} %get-tuple-element.42.q_ref, bf16[1024,256]{1,0:T(8,128)(2,1)S(1)} %get-tuple-element.48.kv_ref), custom_call_target="tpu_custom_call" | custom-call | flops 268435456 | bytes 2097152 | tf_op jit(solution)/shard_map/attention_interior/pallas_call | solution.py:63
  55.5 2.4 %collective-permute-done.13.low_ref.high_ref = bf16[128,256]{1,0:T(8,128)(2,1)S(1)} collective-permute-done((bf16[128,256]{1,0:T(8,128)(2,1)S(1)}, bf16[128,256]{1,0:T(8,128)(2,1)S(1)}, u32[]{:S(2)}, u32[]{:S(2)}) %collective-permute-start.13) | collective-permute-done | bytes 65568 | tf_op jit(solution)/shard_map/ppermute | solution.py:457
  58.0 1.4 %attention_edges.1 = bf16[1024,128]{1,0:T(8,128)(2,1)} custom-call(f32[8,16,128]{2,1,0:T(8,128)S(1)} %get-tuple-element.39.steps_ref, bf16[1024,128]{1,0:T(8,128)(2,1)S(1)} %get-tuple-element.42.q_ref, bf16[1024,256]{1,0:T(8,128)(2,1)S(1)} %get-tuple-element.48.kv_ref, bf16[128,256]{1,0:T(8,128)(2,1)S(1)} %collective-permute-done.13.low_ref.high_ref, ...), custom_call_target="tpu_custom_call" | custom-call | flops 67108864 | bytes 1048576 | tf_op jit(solution)/shard_map/attention_edges/pallas_call | solution.py:63
  59.4 7.0 %all-to-all-start.1 = ((bf16[16,64,128]{2,1,0:T(8,128)(2,1)}), bf16[16,64,128]{2,1,0:T(8,128)(2,1)S(1)}, u32[]{:S(2)}, u32[]{:S(2)}) async-start(bf16[16,64,128]{2,1,0:T(8,128)(2,1)} %bitcast.3), calls=%async_computation.1 | async-start | bytes 524288 | tf_op jit(solution)/shard_map/all_to_all | solution.py:453
  66.7 0.4 collective-permute-start.15
  67.2 0.4 collective-permute-start.17
  67.6 0.6 collective-permute-done.14.refs_4_
  68.1 0.4 collective-permute-done.15.refs_5_
  68.6 0.4 collective-permute-done.16.refs_6_
  69.0 0.4 collective-permute-done.17.refs_7_
  69.4 1.5 %assemble.1.w_any = bf16[2,4,2,64,1152]{4,3,2,1,0:T(8,128)(2,1)} custom-call(bf16[2,64,1152]{2,1,0:T(8,128)(2,1)S(1)} %bitcast.17, bf16[2,64,1152]{2,1,0:T(8,128)(2,1)S(1)} %collective-permute-done.10.refs_1_, bf16[2,64,1152]{2,1,0:T(8,128)(2,1)S(1)} %collective-permute-done.11.refs_2_, bf16[2,64,1152]{2,1,0:T(8,128)(2,1)S(1)} %collective-permute-done.12.refs_3_, ...), custom_call_target="tpu_custom_call" | custom-call | bytes 4194304 | tf_op jit(solution)/shard_map/assemble/pallas_call | solution.py:63
  70.9 2.4 %all-to-all-done.1.att_ref = bf16[16,64,128]{2,1,0:T(8,128)(2,1)S(1)} async-done(((bf16[16,64,128]{2,1,0:T(8,128)(2,1)}), bf16[16,64,128]{2,1,0:T(8,128)(2,1)S(1)}, u32[]{:S(2)}, u32[]{:S(2)}) %all-to-all-start.1) | async-done | bytes 262176 | tf_op jit(solution)/shard_map/all_to_all | solution.py:453
  73.3 3.7 %mix_loss_backward.1 = (f32[100,128]{1,0:T(8,128)S(1)}, bf16[16,64,128]{2,1,0:T(8,128)(2,1)S(1)}) custom-call(bf16[16,64,128]{2,1,0:T(8,128)(2,1)S(1)} %all-to-all-done.1.att_ref, f32[1,128]{1,0:T(1,128)S(1)} %bitcast.18, f32[100,128]{1,0:T(8,128)} %truth_any.1, bf16[2,4,2,64,1152]{4,3,2,1,0:T(8,128)(2,1)} %assemble.1.w_any, ...), custom_call_target="tpu_custom_call" | custom-call | flops 603979776 | bytes 4194304 | tf_op jit(solution)/shard_map/mix_loss_backward/pallas_call | solution.py:63
  77.0 9.9 %all_to_all.20 = bf16[16,64,128]{2,1,0:T(8,128)(2,1)S(1)} all-to-all(bf16[16,64,128]{2,1,0:T(8,128)(2,1)S(1)} %get-tuple-element.56), channel_id=1, replica_groups=mesh['half'=2,'quad'=4,'core'=2,'ens'=2] {'quad','core','ens'}, dimensions={0} | all-to-all | bytes 524288 | tf_op jit(solution)/shard_map/all_to_all | solution.py:453
  86.9 1.4 %attention_edges_back.1 = (f32[2,256,256]{2,1,0:T(8,128)S(1)}, bf16[128,256]{1,0:T(8,128)(2,1)S(1)}) custom-call(f32[8,16,128]{2,1,0:T(8,128)S(1)} %get-tuple-element.39.steps_ref, bf16[1024,128]{1,0:T(8,128)(2,1)S(1)} %get-tuple-element.42.q_ref, bf16[1024,256]{1,0:T(8,128)(2,1)S(1)} %get-tuple-element.48.kv_ref, ...), custom_call_target="tpu_custom_call" | custom-call | flops 167772160 | bytes 1048576 | tf_op jit(solution)/shard_map/attention_edges_back/pallas_call | solution.py:63
  88.3 1.3 %collective-permute-start.18 = (bf16[128,256]{1,0:T(8,128)(2,1)S(1)}, bf16[128,256]{1,0:T(8,128)(2,1)S(1)}, u32[]{:S(2)}, u32[]{:S(2)}) collective-permute-start(bf16[128,256]{1,0:T(8,128)(2,1)S(1)} %get-tuple-element.57), channel_id=1, source_target_pairs={{0,16},{16,0},{1,17},{17,1},{2,18},{18,2},{3,19},{19,3},{4,20},{20... | collective-permute-start | bytes 196616 | tf_op jit(solution)/shard_map/ppermute | solution.py:457
  89.6 3.8 %attention_interior_back.1.grads_ref = f32[1024,256]{1,0:T(8,128)S(1)} custom-call(f32[8,16,128]{2,1,0:T(8,128)S(1)} %get-tuple-element.39.steps_ref, bf16[1024,128]{1,0:T(8,128)(2,1)S(1)} %get-tuple-element.42.q_ref, bf16[1024,256]{1,0:T(8,128)(2,1)S(1)} %get-tuple-element.48.kv_ref, bf16[1024,128]{1,0:T(8,128)(2,1)S(1)} %bitcast.11, ...), custom_call_target="tpu_custom_call" | custom-call | flops 536870912 | bytes 4194304 | tf_op jit(solution)/shard_map/attention_interior_back/pallas_call | solution.py:63
  93.4 1.2 collective-permute-done.18.from_low_ref.from_high_ref
  94.6 2.1 %product.1 = bf16[1024,256]{1,0:T(8,128)(2,1)} custom-call(bf16[1024,1024]{1,0:T(8,128)(2,1)S(1)} %copy-done, bf16[128,256]{1,0:T(8,128)(2,1)S(1)} %collective-permute-done.18.from_low_ref.from_high_ref, bf16[128,256]{1,0:T(8,128)(2,1)S(1)} %collective-permute-done.18.from_low_ref.from_high_ref, f32[1024,256]{1,0:T(8,128)S(1)} %attention_interior_back.1.grads_ref), custom_call_target="tpu_custom_call" | custom-call | flops 1073741824 | bytes 4194304 | tf_op jit(solution)/shard_map/product/pallas_call | solution.py:63
  96.7 2.8 %all-to-all-start.3 = ((bf16[32,32,256]{2,1,0:T(8,128)(2,1)}), bf16[32,32,256]{2,1,0:T(8,128)(2,1)S(1)}, u32[]{:S(2)}, u32[]{:S(2)}) async-start(bf16[32,32,256]{2,1,0:T(8,128)(2,1)} %bitcast.7), calls=%async_computation.3 | async-start | bytes 1048576 | tf_op jit(solution)/shard_map/all_to_all | solution.py:453
  99.5 1.5 %collective-permute-start.19 = (f32[100,128]{1,0:T(8,128)S(1)}, f32[100,128]{1,0:T(8,128)S(1)}, u32[]{:S(2)}, u32[]{:S(2)}) collective-permute-start(f32[100,128]{1,0:T(8,128)S(1)} %get-tuple-element.60), channel_id=1, source_target_pairs={{0,1},{1,0},{2,3},{3,2},{4,5},{5,4},{6,7},{7,6},{8,9},{9,8},{10,11... | collective-permute-start | bytes 153608 | tf_op jit(solution)/shard_map/ppermute | solution.py:457
  101.0 4.5 %collective-permute-done.19 = f32[100,128]{1,0:T(8,128)S(1)} collective-permute-done((f32[100,128]{1,0:T(8,128)S(1)}, f32[100,128]{1,0:T(8,128)S(1)}, u32[]{:S(2)}, u32[]{:S(2)}) %collective-permute-start.19) | collective-permute-done | bytes 51232 | tf_op jit(solution)/shard_map/ppermute | solution.py:457
  105.7 0.7 copy.9
  106.3 9.1 %all-to-all-done.3 = bf16[32,32,256]{2,1,0:T(8,128)(2,1)S(1)} async-done(((bf16[32,32,256]{2,1,0:T(8,128)(2,1)}), bf16[32,32,256]{2,1,0:T(8,128)(2,1)S(1)}, u32[]{:S(2)}, u32[]{:S(2)}) %all-to-all-start.3) | async-done | bytes 524320 | tf_op jit(solution)/shard_map/all_to_all | solution.py:453
  115.4 0.8 gather_sums.1
  (31 shorter events, 1.2 us)
Async XLA Ops:
  2.4 5.2 %collective-permute-start = (bf16[32,1152]{1,0:T(8,128)(2,1)}, bf16[32,1152]{1,0:T(8,128)(2,1)S(1)}, u32[]{:S(2)}, u32[]{:S(2)}) collective-permute-start(bf16[32,1152]{1,0:T(8,128)(2,1)} %get-tuple-element.33.mine_ref), channel_id=1, source_target_pairs={{0,16},{16,0},{1,17},{17,1},{2,18},{18,2},{3,19},{19,3},{4,20},{20... | collective-permute-start | bytes 221192 | tf_op jit(solution)/shard_map/ppermute | solution.py:457
  7.6 20.3 %all-to-all-start = ((bf16[16,32,384]{2,1,0:T(8,128)(2,1)}), bf16[16,32,384]{2,1,0:T(8,128)(2,1)S(1)}, u32[]{:S(2)}, u32[]{:S(2)}) async-start(bf16[16,32,384]{2,1,0:T(8,128)(2,1)} %bitcast.19), calls=%async_computation | async-start | bytes 786432 | tf_op jit(solution)/shard_map/all_to_all | solution.py:453
  16.4 24.4 %collective-permute-start.1 = (bf16[144,1024]{1,0:T(8,128)(2,1)}, bf16[144,1024]{1,0:T(8,128)(2,1)S(1)}, u32[]{:S(2)}, u32[]{:S(2)}) collective-permute-start(bf16[144,1024]{1,0:T(8,128)(2,1)} %get-tuple-element.37.refs_0_), channel_id=1, source_target_pairs={{0,4},{4,0},{8,12},{12,8},{1,5},{5,1},{9,13},{13,9},{2,6},{6,2},{1... | collective-permute-start | bytes 884744 | tf_op jit(solution)/shard_map/ppermute | solution.py:457
  17.8 23.0 %collective-permute-start.3 = (bf16[144,1024]{1,0:T(8,128)(2,1)}, bf16[144,1024]{1,0:T(8,128)(2,1)S(1)}, u32[]{:S(2)}, u32[]{:S(2)}) collective-permute-start(bf16[144,1024]{1,0:T(8,128)(2,1)} %get-tuple-element.37.refs_0_), channel_id=1, source_target_pairs={{0,12},{4,8},{8,4},{12,0},{1,13},{5,9},{9,5},{13,1},{2,14},{6,10},... | collective-permute-start | bytes 884744 | tf_op jit(solution)/shard_map/ppermute | solution.py:457
  27.9 13.5 %collective-permute-start.2 = (bf16[144,1024]{1,0:T(8,128)(2,1)}, bf16[144,1024]{1,0:T(8,128)(2,1)S(1)}, u32[]{:S(2)}, u32[]{:S(2)}) collective-permute-start(bf16[144,1024]{1,0:T(8,128)(2,1)} %get-tuple-element.37.refs_0_), channel_id=1, source_target_pairs={{0,8},{4,12},{8,0},{12,4},{1,9},{5,13},{9,1},{13,5},{2,10},{6,14},... | collective-permute-start | bytes 884744 | tf_op jit(solution)/shard_map/ppermute | solution.py:457
  29.6 0.9 copy-start.3
  30.5 0.9 copy-start.4
  31.4 8.5 %collective-permute-start.9 = (bf16[2,32,2176]{2,1,0:T(8,128)(2,1)S(1)}, bf16[2,32,2176]{2,1,0:T(8,128)(2,1)S(1)}, u32[]{:S(2)}, u32[]{:S(2)}) collective-permute-start(bf16[2,32,2176]{2,1,0:T(8,128)(2,1)S(1)} %merge_halves.1.mine_ref), channel_id=1, source_target_pairs={{0,1},{1,0},{2,3},{3,2},{4,5},{5,4},{6,7},{7,6},{8,9},{9,8},{10,11... | collective-permute-start | bytes 835592 | tf_op jit(solution)/shard_map/ppermute | solution.py:457
  32.7 15.6 %collective-permute-start.8 = (bf16[16,32,384]{2,1,0:T(8,128)(2,1)S(1)}, bf16[16,32,384]{2,1,0:T(8,128)(2,1)S(1)}, u32[]{:S(2)}, u32[]{:S(2)}) collective-permute-start(bf16[16,32,384]{2,1,0:T(8,128)(2,1)S(1)} %all-to-all-done.refs_0_), channel_id=1, source_target_pairs={{0,1},{1,0},{2,3},{3,2},{4,5},{5,4},{6,7},{7,6},{8,9},{9,8},{10,11... | collective-permute-start | bytes 1179656 | tf_op jit(solution)/shard_map/ppermute | solution.py:457
  39.9 2.7 %collective-permute-start.4 = (bf16[144,1024]{1,0:T(8,128)(2,1)}, bf16[144,1024]{1,0:T(8,128)(2,1)S(1)}, u32[]{:S(2)}, u32[]{:S(2)}) collective-permute-start(bf16[144,1024]{1,0:T(8,128)(2,1)} %get-tuple-element.37.refs_0_), channel_id=1, source_target_pairs={{0,2},{2,0},{1,3},{3,1},{4,6},{6,4},{5,7},{7,5},{8,10},{10,8},{9,1... | collective-permute-start | bytes 884744 | tf_op jit(solution)/shard_map/ppermute | solution.py:457
  40.8 3.1 %collective-permute-start.5 = (bf16[144,1024]{1,0:T(8,128)(2,1)S(1)}, bf16[144,1024]{1,0:T(8,128)(2,1)S(1)}, u32[]{:S(2)}, u32[]{:S(2)}) collective-permute-start(bf16[144,1024]{1,0:T(8,128)(2,1)S(1)} %collective-permute-done.1.refs_1_), channel_id=1, source_target_pairs={{0,2},{2,0},{1,3},{3,1},{4,6},{6,4},{5,7},{7,5},{8,10},{10,8},{9,1... | collective-permute-start | bytes 884744 | tf_op jit(solution)/shard_map/ppermute | solution.py:457
  40.8 3.4 %collective-permute-start.7 = (bf16[144,1024]{1,0:T(8,128)(2,1)S(1)}, bf16[144,1024]{1,0:T(8,128)(2,1)S(1)}, u32[]{:S(2)}, u32[]{:S(2)}) collective-permute-start(bf16[144,1024]{1,0:T(8,128)(2,1)S(1)} %collective-permute-done.3.refs_3_), channel_id=1, source_target_pairs={{0,2},{2,0},{1,3},{3,1},{4,6},{6,4},{5,7},{7,5},{8,10},{10,8},{9,1... | collective-permute-start | bytes 884744 | tf_op jit(solution)/shard_map/ppermute | solution.py:457
  41.4 4.1 %collective-permute-start.6 = (bf16[144,1024]{1,0:T(8,128)(2,1)S(1)}, bf16[144,1024]{1,0:T(8,128)(2,1)S(1)}, u32[]{:S(2)}, u32[]{:S(2)}) collective-permute-start(bf16[144,1024]{1,0:T(8,128)(2,1)S(1)} %collective-permute-done.2.refs_2_), channel_id=1, source_target_pairs={{0,2},{2,0},{1,3},{3,1},{4,6},{6,4},{5,7},{7,5},{8,10},{10,8},{9,1... | collective-permute-start | bytes 884744 | tf_op jit(solution)/shard_map/ppermute | solution.py:457
  42.6 23.9 %collective-permute-start.10 = (bf16[2,64,1152]{2,1,0:T(8,128)(2,1)S(1)}, bf16[2,64,1152]{2,1,0:T(8,128)(2,1)S(1)}, u32[]{:S(2)}, u32[]{:S(2)}) collective-permute-start(bf16[2,64,1152]{2,1,0:T(8,128)(2,1)S(1)} %bitcast.13), channel_id=1, source_target_pairs={{0,4},{4,0},{8,12},{12,8},{1,5},{5,1},{9,13},{13,9},{2,6},{6,2},{1... | collective-permute-start | bytes 884744 | tf_op jit(solution)/shard_map/ppermute | solution.py:457
  43.9 22.5 %collective-permute-start.11 = (bf16[2,64,1152]{2,1,0:T(8,128)(2,1)S(1)}, bf16[2,64,1152]{2,1,0:T(8,128)(2,1)S(1)}, u32[]{:S(2)}, u32[]{:S(2)}) collective-permute-start(bf16[2,64,1152]{2,1,0:T(8,128)(2,1)S(1)} %bitcast.14), channel_id=1, source_target_pairs={{0,8},{4,12},{8,0},{12,4},{1,9},{5,13},{9,1},{13,5},{2,10},{6,14},... | collective-permute-start | bytes 884744 | tf_op jit(solution)/shard_map/ppermute | solution.py:457
  44.2 22.3 %collective-permute-start.12 = (bf16[2,64,1152]{2,1,0:T(8,128)(2,1)S(1)}, bf16[2,64,1152]{2,1,0:T(8,128)(2,1)S(1)}, u32[]{:S(2)}, u32[]{:S(2)}) collective-permute-start(bf16[2,64,1152]{2,1,0:T(8,128)(2,1)S(1)} %bitcast.15), channel_id=1, source_target_pairs={{0,12},{4,8},{8,4},{12,0},{1,13},{5,9},{9,5},{13,1},{2,14},{6,10},... | collective-permute-start | bytes 884744 | tf_op jit(solution)/shard_map/ppermute | solution.py:457
  45.5 1.0 copy-start.1
  49.6 8.3 %collective-permute-start.13 = (bf16[128,256]{1,0:T(8,128)(2,1)S(1)}, bf16[128,256]{1,0:T(8,128)(2,1)S(1)}, u32[]{:S(2)}, u32[]{:S(2)}) collective-permute-start(bf16[128,256]{1,0:T(8,128)(2,1)S(1)} %get-tuple-element.49), channel_id=1, source_target_pairs={{0,16},{16,0},{1,17},{17,1},{2,18},{18,2},{3,19},{19,3},{4,20},{20... | collective-permute-start | bytes 196616 | tf_op jit(solution)/shard_map/ppermute | solution.py:457
  59.4 13.9 %all-to-all-start.1 = ((bf16[16,64,128]{2,1,0:T(8,128)(2,1)}), bf16[16,64,128]{2,1,0:T(8,128)(2,1)S(1)}, u32[]{:S(2)}, u32[]{:S(2)}) async-start(bf16[16,64,128]{2,1,0:T(8,128)(2,1)} %bitcast.3), calls=%async_computation.1 | async-start | bytes 524288 | tf_op jit(solution)/shard_map/all_to_all | solution.py:453
  66.4 6.9 %copy-start.2 = (bf16[1,64,1024]{2,1,0:T(8,128)(2,1)S(1)}, bf16[1,64,1024]{2,1,0:T(8,128)(2,1)}, u32[]{:S(2)}) copy-start(bf16[1,64,1024]{2,1,0:T(8,128)(2,1)} %get-tuple-element.54.refs_0_) | copy-start | bytes 393220
  66.5 6.9 %copy-start.5 = (f32[128]{0:T(128)S(1)}, f32[128]{0:T(128)}, u32[]{:S(2)}) copy-start(f32[128]{0:T(128)} %param.12) | copy-start | bytes 1540
  66.5 1.6 %collective-permute-start.14 = (bf16[2,64,1152]{2,1,0:T(8,128)(2,1)S(1)}, bf16[2,64,1152]{2,1,0:T(8,128)(2,1)S(1)}, u32[]{:S(2)}, u32[]{:S(2)}) collective-permute-start(bf16[2,64,1152]{2,1,0:T(8,128)(2,1)S(1)} %bitcast.16), channel_id=1, source_target_pairs={{0,2},{2,0},{1,3},{3,1},{4,6},{6,4},{5,7},{7,5},{8,10},{10,8},{9,1... | collective-permute-start | bytes 884744 | tf_op jit(solution)/shard_map/ppermute | solution.py:457
  66.7 1.9 %collective-permute-start.15 = (bf16[2,64,1152]{2,1,0:T(8,128)(2,1)S(1)}, bf16[2,64,1152]{2,1,0:T(8,128)(2,1)S(1)}, u32[]{:S(2)}, u32[]{:S(2)}) collective-permute-start(bf16[2,64,1152]{2,1,0:T(8,128)(2,1)S(1)} %collective-permute-done.10.refs_1_), channel_id=1, source_target_pairs={{0,2},{2,0},{1,3},{3,1},{4,6},{6,4},{5,7},{7,5},{8,10},{10,8},{9,1... | collective-permute-start | bytes 884744 | tf_op jit(solution)/shard_map/ppermute | solution.py:457
  67.1 1.9 %collective-permute-start.16 = (bf16[2,64,1152]{2,1,0:T(8,128)(2,1)S(1)}, bf16[2,64,1152]{2,1,0:T(8,128)(2,1)S(1)}, u32[]{:S(2)}, u32[]{:S(2)}) collective-permute-start(bf16[2,64,1152]{2,1,0:T(8,128)(2,1)S(1)} %collective-permute-done.11.refs_2_), channel_id=1, source_target_pairs={{0,2},{2,0},{1,3},{3,1},{4,6},{6,4},{5,7},{7,5},{8,10},{10,8},{9,1... | collective-permute-start | bytes 884744 | tf_op jit(solution)/shard_map/ppermute | solution.py:457
  67.2 2.2 %collective-permute-start.17 = (bf16[2,64,1152]{2,1,0:T(8,128)(2,1)S(1)}, bf16[2,64,1152]{2,1,0:T(8,128)(2,1)S(1)}, u32[]{:S(2)}, u32[]{:S(2)}) collective-permute-start(bf16[2,64,1152]{2,1,0:T(8,128)(2,1)S(1)} %collective-permute-done.12.refs_3_), channel_id=1, source_target_pairs={{0,2},{2,0},{1,3},{3,1},{4,6},{6,4},{5,7},{7,5},{8,10},{10,8},{9,1... | collective-permute-start | bytes 884744 | tf_op jit(solution)/shard_map/ppermute | solution.py:457
  77.0 17.6 %copy-start = (bf16[1024,1024]{1,0:T(8,128)(2,1)S(1)}, bf16[1024,1024]{1,0:T(8,128)(2,1)}, u32[]{:S(2)}) copy-start(bf16[1024,1024]{1,0:T(8,128)(2,1)} %get-tuple-element.38.normed_any.normed_ref) | copy-start | bytes 6291460
  88.3 6.3 %collective-permute-start.18 = (bf16[128,256]{1,0:T(8,128)(2,1)S(1)}, bf16[128,256]{1,0:T(8,128)(2,1)S(1)}, u32[]{:S(2)}, u32[]{:S(2)}) collective-permute-start(bf16[128,256]{1,0:T(8,128)(2,1)S(1)} %get-tuple-element.57), channel_id=1, source_target_pairs={{0,16},{16,0},{1,17},{17,1},{2,18},{18,2},{3,19},{19,3},{4,20},{20... | collective-permute-start | bytes 196616 | tf_op jit(solution)/shard_map/ppermute | solution.py:457
  96.7 18.7 %all-to-all-start.3 = ((bf16[32,32,256]{2,1,0:T(8,128)(2,1)}), bf16[32,32,256]{2,1,0:T(8,128)(2,1)S(1)}, u32[]{:S(2)}, u32[]{:S(2)}) async-start(bf16[32,32,256]{2,1,0:T(8,128)(2,1)} %bitcast.7), calls=%async_computation.3 | async-start | bytes 1048576 | tf_op jit(solution)/shard_map/all_to_all | solution.py:453
  99.5 6.0 %collective-permute-start.19 = (f32[100,128]{1,0:T(8,128)S(1)}, f32[100,128]{1,0:T(8,128)S(1)}, u32[]{:S(2)}, u32[]{:S(2)}) collective-permute-start(f32[100,128]{1,0:T(8,128)S(1)} %get-tuple-element.60), channel_id=1, source_target_pairs={{0,1},{1,0},{2,3},{3,2},{4,5},{5,4},{6,7},{7,6},{8,9},{9,8},{10,11... | collective-permute-start | bytes 153608 | tf_op jit(solution)/shard_map/ppermute | solution.py:457

commit v20 on v13

--- a/solution.py
+++ b/solution.py
@@ -507,6 +507,7 @@
         columns = [columns[0].reshape(LATENT_DIM, 3 * COLS)]
         late = normed
     near[2] = swap(late, "quad", 2)
+    near = list(lax.optimization_barrier(tuple(near)))
     far = [swap(piece, "core", 1) for piece in near]
     normed, steps = call(
         collect_kernel,

time: 110 us -> 112 us (1.018)
  waiting for transfers between devices: 33.9 us -> 36 us
    ppermute x21, starting transfers between devices: 22.7 us -> 20 us  [swap(): lax.ppermute(value, axis, [(i, i ^ step) for i in range(lax.axis_size(axi...]
    all_to_all x3, starting transfers between devices: 13.4 us -> 15.7 us  [exchange(): return lax.all_to_all(chunks, axes, 0, 0)]
    ppermute x21, waiting for transfers between devices: 18.9 us -> 21 us  [swap(): lax.ppermute(value, axis, [(i, i ^ step) for i in range(lax.axis_size(axi...]
  transfers between devices with their start and end apart: 24 -> 24, of which waited for: 8 -> 10; matrix products, arithmetic and copies ran while one was open for 2% -> 2% of each run, Pallas kernels for 15% -> 15%
where the time goes in v20:
time: 112 us
  waiting for transfers between devices  36 us (32%)
  starting transfers between devices  35.6 us (32%)
  Pallas kernels  25.9 us (23%)
  blocking collectives  11.2 us (10%)
  other arithmetic  1.13 us (1%)
    pallas_call x13, Pallas kernels, run(): made(*[pltpu.with_memory_space_constraint(arg, pltpu.HBM) if space == 'h'...  25.9 us
    ppermute x21, waiting for transfers between devices, swap(): lax.ppermute(value, axis, [(i, i ^ step) for i in range(lax.axis_size(axi...  21 us
    ppermute x21, starting transfers between devices, swap(): lax.ppermute(value, axis, [(i, i ^ step) for i in range(lax.axis_size(axi...  20 us
    all_to_all x3, starting transfers between devices, exchange(): return lax.all_to_all(chunks, axes, 0, 0)  15.7 us
    all_to_all x3, waiting for transfers between devices, exchange(): return lax.all_to_all(chunks, axes, 0, 0)  15 us
    all_to_all x1, blocking collectives, exchange(): return lax.all_to_all(chunks, axes, 0, 0)  11.2 us
  transfers between devices with their start and end apart: 24, of which 10 were waited for; matrix products, arithmetic and copies ran while one was open for 2% of the time, Pallas kernels for 15%

profile of v20, /device:TPU:1, one launch (start us, length us, event | category | flops | bytes accessed | tf_op | source)
XLA Modules:
  0.0 111.6 jit_solution(7137788977512988780)
XLA Ops:
  0.6 1.8 %prepare_weights.1 = (bf16[2,8,1,32,384]{4,3,2,1,0:T(8,128)(2,1)}, bf16[32,1152]{1,0:T(8,128)(2,1)}) custom-call(bf16[32,3072]{1,0:T(8,128)(2,1)} %w_any.1, bf16[32,1024]{1,0:T(8,128)(2,1)} %mix_any.1, bf16[32,100]{1,0:T(8,128)(2,1)} %readout_any.1), custom_call_target="tpu_custom_call" | custom-call | bytes 1048576 | tf_op jit(solution)/shard_map/prepare_weights/pallas_call | solution.py:63
  2.4 3.2 %collective-permute-start = (bf16[32,1152]{1,0:T(8,128)(2,1)}, bf16[32,1152]{1,0:T(8,128)(2,1)S(1)}, u32[]{:S(2)}, u32[]{:S(2)}) collective-permute-start(bf16[32,1152]{1,0:T(8,128)(2,1)} %get-tuple-element.35), channel_id=1, source_target_pairs={{0,16},{16,0},{1,17},{17,1},{2,18},{18,2},{3,19},{19,3},{4,20},{20... | collective-permute-start | bytes 221192 | tf_op jit(solution)/shard_map/ppermute | solution.py:440
  5.6 4.8 %all-to-all-start = ((bf16[16,32,384]{2,1,0:T(8,128)(2,1)}), bf16[16,32,384]{2,1,0:T(8,128)(2,1)S(1)}, u32[]{:S(2)}, u32[]{:S(2)}) async-start(bf16[16,32,384]{2,1,0:T(8,128)(2,1)} %bitcast.27), calls=%async_computation | async-start | bytes 786432 | tf_op jit(solution)/shard_map/all_to_all | solution.py:436
  10.4 1.9 %norm.1 = (bf16[144,1024]{1,0:T(8,128)(2,1)}, bf16[1,64,1024]{2,1,0:T(8,128)(2,1)}, bf16[1,64,1024]{2,1,0:T(8,128)(2,1)}) custom-call(s32[2,4]{1,0:T(2,128)} %near_any.1, bf16[128,1024]{1,0:T(8,128)(2,1)} %bitcast.28), custom_call_target="tpu_custom_call" | custom-call | flops 1048576 | bytes 1048576 | tf_op jit(solution)/shard_map/norm/pallas_call | solution.py:63
  12.3 0.9 select_bitcast_fusion.3
  13.3 1.5 %collective-permute-start.1 = (bf16[144,1024]{1,0:T(8,128)(2,1)}, bf16[144,1024]{1,0:T(8,128)(2,1)S(1)}, u32[]{:S(2)}, u32[]{:S(2)}) collective-permute-start(bf16[144,1024]{1,0:T(8,128)(2,1)} %get-tuple-element.40.refs_0_), channel_id=1, source_target_pairs={{0,4},{4,0},{8,12},{12,8},{1,5},{5,1},{9,13},{13,9},{2,6},{6,2},{1... | collective-permute-start | bytes 884744 | tf_op jit(solution)/shard_map/ppermute | solution.py:440
  14.7 1.2 %collective-permute-start.3 = (bf16[144,1024]{1,0:T(8,128)(2,1)}, bf16[144,1024]{1,0:T(8,128)(2,1)S(1)}, u32[]{:S(2)}, u32[]{:S(2)}) collective-permute-start(bf16[144,1024]{1,0:T(8,128)(2,1)} %get-tuple-element.40.refs_0_), channel_id=1, source_target_pairs={{0,12},{4,8},{8,4},{12,0},{1,13},{5,9},{9,5},{13,1},{2,14},{6,10},... | collective-permute-start | bytes 884744 | tf_op jit(solution)/shard_map/ppermute | solution.py:440
  15.9 5.9 %all-to-all-done.refs_0_ = bf16[16,32,384]{2,1,0:T(8,128)(2,1)S(1)} async-done(((bf16[16,32,384]{2,1,0:T(8,128)(2,1)}), bf16[16,32,384]{2,1,0:T(8,128)(2,1)S(1)}, u32[]{:S(2)}, u32[]{:S(2)}) %all-to-all-start) | async-done | bytes 393248 | tf_op jit(solution)/shard_map/all_to_all | solution.py:436
  21.8 1.7 %collective-permute-start.2 = (bf16[144,1024]{1,0:T(8,128)(2,1)}, bf16[144,1024]{1,0:T(8,128)(2,1)S(1)}, u32[]{:S(2)}, u32[]{:S(2)}) collective-permute-start(bf16[144,1024]{1,0:T(8,128)(2,1)} %get-tuple-element.40.refs_0_), channel_id=1, source_target_pairs={{0,8},{4,12},{8,0},{12,4},{1,9},{5,13},{9,1},{13,5},{2,10},{6,14},... | collective-permute-start | bytes 884744 | tf_op jit(solution)/shard_map/ppermute | solution.py:440
  23.6 1.2 %collective-permute-start.9 = (bf16[2,32,1152]{2,1,0:T(8,128)(2,1)S(1)}, bf16[2,32,1152]{2,1,0:T(8,128)(2,1)S(1)}, u32[]{:S(2)}, u32[]{:S(2)}) collective-permute-start(bf16[2,32,1152]{2,1,0:T(8,128)(2,1)S(1)} %pad_maximum_fusion.1), channel_id=1, source_target_pairs={{0,1},{1,0},{2,3},{3,2},{4,5},{5,4},{6,7},{7,6},{8,9},{9,8},{10,11... | collective-permute-start | bytes 442376 | tf_op jit(solution)/shard_map/ppermute | solution.py:440
  24.8 0.3 collective-permute-start.8
  25.0 5.3 %collective-permute-done.1.refs_1_ = bf16[144,1024]{1,0:T(8,128)(2,1)S(1)} collective-permute-done((bf16[144,1024]{1,0:T(8,128)(2,1)}, bf16[144,1024]{1,0:T(8,128)(2,1)S(1)}, u32[]{:S(2)}, u32[]{:S(2)}) %collective-permute-start.1) | collective-permute-done | bytes 294944 | tf_op jit(solution)/shard_map/ppermute | solution.py:440
  30.3 1.4 %collective-permute-done.2.refs_2_ = bf16[144,1024]{1,0:T(8,128)(2,1)S(1)} collective-permute-done((bf16[144,1024]{1,0:T(8,128)(2,1)}, bf16[144,1024]{1,0:T(8,128)(2,1)S(1)}, u32[]{:S(2)}, u32[]{:S(2)}) %collective-permute-start.2) | collective-permute-done | bytes 294944 | tf_op jit(solution)/shard_map/ppermute | solution.py:440
  31.7 1.0 collective-permute-start.6
  32.7 0.5 collective-permute-start.5
  33.3 1.0 collective-permute-done.6.refs_6_
  34.3 1.5 %collective-permute-start.10 = (bf16[2,64,1152]{2,1,0:T(8,128)(2,1)S(1)}, bf16[2,64,1152]{2,1,0:T(8,128)(2,1)S(1)}, u32[]{:S(2)}, u32[]{:S(2)}) collective-permute-start(bf16[2,64,1152]{2,1,0:T(8,128)(2,1)S(1)} %bitcast.21), channel_id=1, source_target_pairs={{0,4},{4,0},{8,12},{12,8},{1,5},{5,1},{9,13},{13,9},{2,6},{6,2},{1... | collective-permute-start | bytes 884744 | tf_op jit(solution)/shard_map/ppermute | solution.py:440
  35.8 0.5 collective-permute-start.11
  36.3 1.3 %collective-permute-start.12 = (bf16[2,64,1152]{2,1,0:T(8,128)(2,1)S(1)}, bf16[2,64,1152]{2,1,0:T(8,128)(2,1)S(1)}, u32[]{:S(2)}, u32[]{:S(2)}) collective-permute-start(bf16[2,64,1152]{2,1,0:T(8,128)(2,1)S(1)} %bitcast.23), channel_id=1, source_target_pairs={{0,12},{4,8},{8,4},{12,0},{1,13},{5,9},{9,5},{13,1},{2,14},{6,10},... | collective-permute-start | bytes 884744 | tf_op jit(solution)/shard_map/ppermute | solution.py:440
  37.6 1.5 %collect.1 = (bf16[1024,1024]{1,0:T(8,128)(2,1)}, f32[8,16,128]{2,1,0:T(8,128)S(1)}) custom-call(bf16[144,1024]{1,0:T(8,128)(2,1)S(1)} %copy-done.1, bf16[144,1024]{1,0:T(8,128)(2,1)S(1)} %collective-permute-done.1.refs_1_, bf16[144,1024]{1,0:T(8,128)(2,1)S(1)} %collective-permute-done.2.refs_2_, bf16[144,1024]{1,0:T(8,128)(2,1)S(1)} %collective-permute-done.3.refs_3_, ...), custom_call_target="tpu_custom_call" | custom-call | bytes 4194304 | tf_op jit(solution)/shard_map/collect/pallas_call | solution.py:63
  39.1 1.3 %project_rims.1 = (bf16[16,2,32,384]{3,2,1,0:T(8,128)(2,1)S(1)}, bf16[128,256]{1,0:T(8,128)(2,1)S(1)}) custom-call(bf16[1024,1024]{1,0:T(8,128)(2,1)} %get-tuple-element.44.normed_any.normed_ref, bf16[16,32,384]{2,1,0:T(8,128)(2,1)S(1)} %all-to-all-done.refs_0_, bf16[16,32,384]{2,1,0:T(8,128)(2,1)S(1)} %collective-permute-done.8.refs_1_), custom_call_target="tpu_custom_call" | custom-call | flops 67108864 | bytes 1048576 | tf_op jit(solution)/shard_map/project_rims/pallas_call | solution.py:63
  40.5 2.1 %collective-permute-start.13 = (bf16[128,256]{1,0:T(8,128)(2,1)S(1)}, bf16[128,256]{1,0:T(8,128)(2,1)S(1)}, u32[]{:S(2)}, u32[]{:S(2)}) collective-permute-start(bf16[128,256]{1,0:T(8,128)(2,1)S(1)} %get-tuple-element.55), channel_id=1, source_target_pairs={{0,16},{16,0},{1,17},{17,1},{2,18},{18,2},{3,19},{19,3},{4,20},{20... | collective-permute-start | bytes 196616 | tf_op jit(solution)/shard_map/ppermute | solution.py:440
  42.6 2.8 %project.1 = (bf16[1024,128]{1,0:T(8,128)(2,1)S(1)}, bf16[1024,256]{1,0:T(8,128)(2,1)S(1)}) custom-call(bf16[1024,1024]{1,0:T(8,128)(2,1)} %get-tuple-element.44.normed_any.normed_ref, bf16[16,2,32,384]{3,2,1,0:T(8,128)(2,1)S(1)} %get-tuple-element.49.w_ref), custom_call_target="tpu_custom_call" | custom-call | flops 805306368 | bytes 4194304 | tf_op jit(solution)/shard_map/project/pallas_call | solution.py:63
  45.5 1.9 %attention_interior.1.done_ref = bf16[1024,128]{1,0:T(8,128)(2,1)S(1)} custom-call(f32[8,16,128]{2,1,0:T(8,128)S(1)} %get-tuple-element.45.steps_ref, bf16[1024,128]{1,0:T(8,128)(2,1)S(1)} %get-tuple-element.50.q_ref, bf16[1024,256]{1,0:T(8,128)(2,1)S(1)} %get-tuple-element.54.kv_ref), custom_call_target="tpu_custom_call" | custom-call | flops 268435456 | bytes 2097152 | tf_op jit(solution)/shard_map/attention_interior/pallas_call | solution.py:63
  47.4 2.4 %collective-permute-done.13.low_ref.high_ref = bf16[128,256]{1,0:T(8,128)(2,1)S(1)} collective-permute-done((bf16[128,256]{1,0:T(8,128)(2,1)S(1)}, bf16[128,256]{1,0:T(8,128)(2,1)S(1)}, u32[]{:S(2)}, u32[]{:S(2)}) %collective-permute-start.13) | collective-permute-done | bytes 65568 | tf_op jit(solution)/shard_map/ppermute | solution.py:440
  49.7 1.4 %attention_edges.1 = bf16[1024,128]{1,0:T(8,128)(2,1)} custom-call(f32[8,16,128]{2,1,0:T(8,128)S(1)} %get-tuple-element.45.steps_ref, bf16[1024,128]{1,0:T(8,128)(2,1)S(1)} %get-tuple-element.50.q_ref, bf16[1024,256]{1,0:T(8,128)(2,1)S(1)} %get-tuple-element.54.kv_ref, bf16[128,256]{1,0:T(8,128)(2,1)S(1)} %collective-permute-done.13.low_ref.high_ref, ...), custom_call_target="tpu_custom_call" | custom-call | flops 67108864 | bytes 1048576 | tf_op jit(solution)/shard_map/attention_edges/pallas_call | solution.py:63
  51.2 8.1 %all-to-all-start.1 = ((bf16[16,64,128]{2,1,0:T(8,128)(2,1)}), bf16[16,64,128]{2,1,0:T(8,128)(2,1)S(1)}, u32[]{:S(2)}, u32[]{:S(2)}) async-start(bf16[16,64,128]{2,1,0:T(8,128)(2,1)} %bitcast.7), calls=%async_computation.1 | async-start | bytes 524288 | tf_op jit(solution)/shard_map/all_to_all | solution.py:436
  59.3 0.2 collective-permute-start.14
  59.5 0.4 collective-permute-start.15
  59.9 0.1 collective-permute-start.16
  60.0 0.4 collective-permute-start.17
  60.4 1.4 %collective-permute-start.18 = (bf16[1,64,1024]{2,1,0:T(8,128)(2,1)S(1)}, bf16[1,64,1024]{2,1,0:T(8,128)(2,1)S(1)}, u32[]{:S(2)}, u32[]{:S(2)}) collective-permute-start(bf16[1,64,1024]{2,1,0:T(8,128)(2,1)S(1)} %copy-done.4), channel_id=1, source_target_pairs={{0,1},{1,0},{2,3},{3,2},{4,5},{5,4},{6,7},{7,6},{8,9},{9,8},{10,11... | collective-permute-start | bytes 393224 | tf_op jit(solution)/shard_map/ppermute | solution.py:440
  61.8 0.4 collective-permute-done.17.refs_7_
  62.3 1.5 %assemble.1.w_any = bf16[2,4,2,64,1152]{4,3,2,1,0:T(8,128)(2,1)} custom-call(bf16[2,64,1152]{2,1,0:T(8,128)(2,1)S(1)} %bitcast.25, bf16[2,64,1152]{2,1,0:T(8,128)(2,1)S(1)} %collective-permute-done.10.refs_1_, bf16[2,64,1152]{2,1,0:T(8,128)(2,1)S(1)} %collective-permute-done.11.refs_2_, bf16[2,64,1152]{2,1,0:T(8,128)(2,1)S(1)} %collective-permute-done.12.refs_3_, ...), custom_call_target="tpu_custom_call" | custom-call | bytes 4194304 | tf_op jit(solution)/shard_map/assemble/pallas_call | solution.py:63
  63.7 3.6 %collective-permute-done.18.refs_1_ = bf16[1,64,1024]{2,1,0:T(8,128)(2,1)S(1)} collective-permute-done((bf16[1,64,1024]{2,1,0:T(8,128)(2,1)S(1)}, bf16[1,64,1024]{2,1,0:T(8,128)(2,1)S(1)}, u32[]{:S(2)}, u32[]{:S(2)}) %collective-permute-start.18) | collective-permute-done | bytes 131104 | tf_op jit(solution)/shard_map/ppermute | solution.py:440
  67.4 3.7 %mix_loss_backward.1 = (f32[100,128]{1,0:T(8,128)S(1)}, bf16[16,64,128]{2,1,0:T(8,128)(2,1)S(1)}) custom-call(bf16[16,64,128]{2,1,0:T(8,128)(2,1)S(1)} %all-to-all-done.1.att_ref, f32[1,128]{1,0:T(1,128)S(1)} %bitcast.26, f32[100,128]{1,0:T(8,128)} %truth_any.1, bf16[2,4,2,64,1152]{4,3,2,1,0:T(8,128)(2,1)} %assemble.1.w_any, ...), custom_call_target="tpu_custom_call" | custom-call | flops 603979776 | bytes 4194304 | tf_op jit(solution)/shard_map/mix_loss_backward/pallas_call | solution.py:63
  71.1 11.2 %all_to_all.20 = bf16[16,64,128]{2,1,0:T(8,128)(2,1)S(1)} all-to-all(bf16[16,64,128]{2,1,0:T(8,128)(2,1)S(1)} %get-tuple-element.62), channel_id=1, replica_groups=mesh['half'=2,'quad'=4,'core'=2,'ens'=2] {'quad','core','ens'}, dimensions={0} | all-to-all | bytes 524288 | tf_op jit(solution)/shard_map/all_to_all | solution.py:436
  82.3 1.4 %attention_edges_back.1 = (f32[2,256,256]{2,1,0:T(8,128)S(1)}, bf16[128,256]{1,0:T(8,128)(2,1)S(1)}) custom-call(f32[8,16,128]{2,1,0:T(8,128)S(1)} %get-tuple-element.45.steps_ref, bf16[1024,128]{1,0:T(8,128)(2,1)S(1)} %get-tuple-element.50.q_ref, bf16[1024,256]{1,0:T(8,128)(2,1)S(1)} %get-tuple-element.54.kv_ref, ...), custom_call_target="tpu_custom_call" | custom-call | flops 167772160 | bytes 1048576 | tf_op jit(solution)/shard_map/attention_edges_back/pallas_call | solution.py:63
  83.8 3.9 %attention_interior_back.1.grads_ref = f32[1024,256]{1,0:T(8,128)S(1)} custom-call(f32[8,16,128]{2,1,0:T(8,128)S(1)} %get-tuple-element.45.steps_ref, bf16[1024,128]{1,0:T(8,128)(2,1)S(1)} %get-tuple-element.50.q_ref, bf16[1024,256]{1,0:T(8,128)(2,1)S(1)} %get-tuple-element.54.kv_ref, bf16[1024,128]{1,0:T(8,128)(2,1)S(1)} %bitcast.19, ...), custom_call_target="tpu_custom_call" | custom-call | flops 536870912 | bytes 4194304 | tf_op jit(solution)/shard_map/attention_interior_back/pallas_call | solution.py:63
  87.7 2.4 %collective-permute-done.19.from_low_ref.from_high_ref = bf16[128,256]{1,0:T(8,128)(2,1)S(1)} collective-permute-done((bf16[128,256]{1,0:T(8,128)(2,1)S(1)}, bf16[128,256]{1,0:T(8,128)(2,1)S(1)}, u32[]{:S(2)}, u32[]{:S(2)}) %collective-permute-start.19) | collective-permute-done | bytes 65568 | tf_op jit(solution)/shard_map/ppermute | solution.py:440
  90.0 2.1 %product.1 = bf16[1024,256]{1,0:T(8,128)(2,1)} custom-call(bf16[1024,1024]{1,0:T(8,128)(2,1)S(1)} %copy-done, bf16[128,256]{1,0:T(8,128)(2,1)S(1)} %collective-permute-done.19.from_low_ref.from_high_ref, bf16[128,256]{1,0:T(8,128)(2,1)S(1)} %collective-permute-done.19.from_low_ref.from_high_ref, f32[1024,256]{1,0:T(8,128)S(1)} %attention_interior_back.1.grads_ref), custom_call_target="tpu_custom_call" | custom-call | flops 1073741824 | bytes 4194304 | tf_op jit(solution)/shard_map/product/pallas_call | solution.py:63
  92.1 2.8 %all-to-all-start.3 = ((bf16[32,32,256]{2,1,0:T(8,128)(2,1)}), bf16[32,32,256]{2,1,0:T(8,128)(2,1)S(1)}, u32[]{:S(2)}, u32[]{:S(2)}) async-start(bf16[32,32,256]{2,1,0:T(8,128)(2,1)} %bitcast.11), calls=%async_computation.3 | async-start | bytes 1048576 | tf_op jit(solution)/shard_map/all_to_all | solution.py:436
  94.9 1.5 %collective-permute-start.20 = (f32[100,128]{1,0:T(8,128)S(1)}, f32[100,128]{1,0:T(8,128)S(1)}, u32[]{:S(2)}, u32[]{:S(2)}) collective-permute-start(f32[100,128]{1,0:T(8,128)S(1)} %get-tuple-element.66), channel_id=1, source_target_pairs={{0,1},{1,0},{2,3},{3,2},{4,5},{5,4},{6,7},{7,6},{8,9},{9,8},{10,11... | collective-permute-start | bytes 153608 | tf_op jit(solution)/shard_map/ppermute | solution.py:440
  96.4 4.5 %collective-permute-done.20 = f32[100,128]{1,0:T(8,128)S(1)} collective-permute-done((f32[100,128]{1,0:T(8,128)S(1)}, f32[100,128]{1,0:T(8,128)S(1)}, u32[]{:S(2)}, u32[]{:S(2)}) %collective-permute-start.20) | collective-permute-done | bytes 51232 | tf_op jit(solution)/shard_map/ppermute | solution.py:440
  101.0 0.1 fusion
  101.1 0.7 copy.10
  101.8 9.1 %all-to-all-done.3 = bf16[32,32,256]{2,1,0:T(8,128)(2,1)S(1)} async-done(((bf16[32,32,256]{2,1,0:T(8,128)(2,1)}), bf16[32,32,256]{2,1,0:T(8,128)(2,1)S(1)}, u32[]{:S(2)}, u32[]{:S(2)}) %all-to-all-start.3) | async-done | bytes 524320 | tf_op jit(solution)/shard_map/all_to_all | solution.py:436
  110.8 0.8 gather_sums.1
  (34 shorter events, 0.3 us)
Async XLA Ops:
  2.4 9.9 %collective-permute-start = (bf16[32,1152]{1,0:T(8,128)(2,1)}, bf16[32,1152]{1,0:T(8,128)(2,1)S(1)}, u32[]{:S(2)}, u32[]{:S(2)}) collective-permute-start(bf16[32,1152]{1,0:T(8,128)(2,1)} %get-tuple-element.35), channel_id=1, source_target_pairs={{0,16},{16,0},{1,17},{17,1},{2,18},{18,2},{3,19},{19,3},{4,20},{20... | collective-permute-start | bytes 221192 | tf_op jit(solution)/shard_map/ppermute | solution.py:440
  5.6 16.2 %all-to-all-start = ((bf16[16,32,384]{2,1,0:T(8,128)(2,1)}), bf16[16,32,384]{2,1,0:T(8,128)(2,1)S(1)}, u32[]{:S(2)}, u32[]{:S(2)}) async-start(bf16[16,32,384]{2,1,0:T(8,128)(2,1)} %bitcast.27), calls=%async_computation | async-start | bytes 786432 | tf_op jit(solution)/shard_map/all_to_all | solution.py:436
  12.3 25.3 %copy-start.1 = (bf16[144,1024]{1,0:T(8,128)(2,1)S(1)}, bf16[144,1024]{1,0:T(8,128)(2,1)}, u32[]{:S(2)}) copy-start(bf16[144,1024]{1,0:T(8,128)(2,1)} %get-tuple-element.40.refs_0_) | copy-start | bytes 884740
  13.3 17.0 %collective-permute-start.1 = (bf16[144,1024]{1,0:T(8,128)(2,1)}, bf16[144,1024]{1,0:T(8,128)(2,1)S(1)}, u32[]{:S(2)}, u32[]{:S(2)}) collective-permute-start(bf16[144,1024]{1,0:T(8,128)(2,1)} %get-tuple-element.40.refs_0_), channel_id=1, source_target_pairs={{0,4},{4,0},{8,12},{12,8},{1,5},{5,1},{9,13},{13,9},{2,6},{6,2},{1... | collective-permute-start | bytes 884744 | tf_op jit(solution)/shard_map/ppermute | solution.py:440
  14.7 15.6 %collective-permute-start.3 = (bf16[144,1024]{1,0:T(8,128)(2,1)}, bf16[144,1024]{1,0:T(8,128)(2,1)S(1)}, u32[]{:S(2)}, u32[]{:S(2)}) collective-permute-start(bf16[144,1024]{1,0:T(8,128)(2,1)} %get-tuple-element.40.refs_0_), channel_id=1, source_target_pairs={{0,12},{4,8},{8,4},{12,0},{1,13},{5,9},{9,5},{13,1},{2,14},{6,10},... | collective-permute-start | bytes 884744 | tf_op jit(solution)/shard_map/ppermute | solution.py:440
  21.8 9.9 %collective-permute-start.2 = (bf16[144,1024]{1,0:T(8,128)(2,1)}, bf16[144,1024]{1,0:T(8,128)(2,1)S(1)}, u32[]{:S(2)}, u32[]{:S(2)}) collective-permute-start(bf16[144,1024]{1,0:T(8,128)(2,1)} %get-tuple-element.40.refs_0_), channel_id=1, source_target_pairs={{0,8},{4,12},{8,0},{12,4},{1,9},{5,13},{9,1},{13,5},{2,10},{6,14},... | collective-permute-start | bytes 884744 | tf_op jit(solution)/shard_map/ppermute | solution.py:440
  23.6 9.7 %collective-permute-start.9 = (bf16[2,32,1152]{2,1,0:T(8,128)(2,1)S(1)}, bf16[2,32,1152]{2,1,0:T(8,128)(2,1)S(1)}, u32[]{:S(2)}, u32[]{:S(2)}) collective-permute-start(bf16[2,32,1152]{2,1,0:T(8,128)(2,1)S(1)} %pad_maximum_fusion.1), channel_id=1, source_target_pairs={{0,1},{1,0},{2,3},{3,2},{4,5},{5,4},{6,7},{7,6},{8,9},{9,8},{10,11... | collective-permute-start | bytes 442376 | tf_op jit(solution)/shard_map/ppermute | solution.py:440
  24.8 14.4 %collective-permute-start.8 = (bf16[16,32,384]{2,1,0:T(8,128)(2,1)S(1)}, bf16[16,32,384]{2,1,0:T(8,128)(2,1)S(1)}, u32[]{:S(2)}, u32[]{:S(2)}) collective-permute-start(bf16[16,32,384]{2,1,0:T(8,128)(2,1)S(1)} %all-to-all-done.refs_0_), channel_id=1, source_target_pairs={{0,1},{1,0},{2,3},{3,2},{4,5},{5,4},{6,7},{7,6},{8,9},{9,8},{10,11... | collective-permute-start | bytes 1179656 | tf_op jit(solution)/shard_map/ppermute | solution.py:440
  31.7 2.6 %collective-permute-start.6 = (bf16[144,1024]{1,0:T(8,128)(2,1)S(1)}, bf16[144,1024]{1,0:T(8,128)(2,1)S(1)}, u32[]{:S(2)}, u32[]{:S(2)}) collective-permute-start(bf16[144,1024]{1,0:T(8,128)(2,1)S(1)} %collective-permute-done.2.refs_2_), channel_id=1, source_target_pairs={{0,2},{2,0},{1,3},{3,1},{4,6},{6,4},{5,7},{7,5},{8,10},{10,8},{9,1... | collective-permute-start | bytes 884744 | tf_op jit(solution)/shard_map/ppermute | solution.py:440
  32.7 3.1 %collective-permute-start.4 = (bf16[144,1024]{1,0:T(8,128)(2,1)}, bf16[144,1024]{1,0:T(8,128)(2,1)S(1)}, u32[]{:S(2)}, u32[]{:S(2)}) collective-permute-start(bf16[144,1024]{1,0:T(8,128)(2,1)} %get-tuple-element.40.refs_0_), channel_id=1, source_target_pairs={{0,2},{2,0},{1,3},{3,1},{4,6},{6,4},{5,7},{7,5},{8,10},{10,8},{9,1... | collective-permute-start | bytes 884744 | tf_op jit(solution)/shard_map/ppermute | solution.py:440
  32.7 3.6 %collective-permute-start.5 = (bf16[144,1024]{1,0:T(8,128)(2,1)S(1)}, bf16[144,1024]{1,0:T(8,128)(2,1)S(1)}, u32[]{:S(2)}, u32[]{:S(2)}) collective-permute-start(bf16[144,1024]{1,0:T(8,128)(2,1)S(1)} %collective-permute-done.1.refs_1_), channel_id=1, source_target_pairs={{0,2},{2,0},{1,3},{3,1},{4,6},{6,4},{5,7},{7,5},{8,10},{10,8},{9,1... | collective-permute-start | bytes 884744 | tf_op jit(solution)/shard_map/ppermute | solution.py:440
  33.2 4.4 %collective-permute-start.7 = (bf16[144,1024]{1,0:T(8,128)(2,1)S(1)}, bf16[144,1024]{1,0:T(8,128)(2,1)S(1)}, u32[]{:S(2)}, u32[]{:S(2)}) collective-permute-start(bf16[144,1024]{1,0:T(8,128)(2,1)S(1)} %collective-permute-done.3.refs_3_), channel_id=1, source_target_pairs={{0,2},{2,0},{1,3},{3,1},{4,6},{6,4},{5,7},{7,5},{8,10},{10,8},{9,1... | collective-permute-start | bytes 884744 | tf_op jit(solution)/shard_map/ppermute | solution.py:440
  34.3 25.0 %collective-permute-start.10 = (bf16[2,64,1152]{2,1,0:T(8,128)(2,1)S(1)}, bf16[2,64,1152]{2,1,0:T(8,128)(2,1)S(1)}, u32[]{:S(2)}, u32[]{:S(2)}) collective-permute-start(bf16[2,64,1152]{2,1,0:T(8,128)(2,1)S(1)} %bitcast.21), channel_id=1, source_target_pairs={{0,4},{4,0},{8,12},{12,8},{1,5},{5,1},{9,13},{13,9},{2,6},{6,2},{1... | collective-permute-start | bytes 884744 | tf_op jit(solution)/shard_map/ppermute | solution.py:440
  35.8 23.5 %collective-permute-start.11 = (bf16[2,64,1152]{2,1,0:T(8,128)(2,1)S(1)}, bf16[2,64,1152]{2,1,0:T(8,128)(2,1)S(1)}, u32[]{:S(2)}, u32[]{:S(2)}) collective-permute-start(bf16[2,64,1152]{2,1,0:T(8,128)(2,1)S(1)} %bitcast.22), channel_id=1, source_target_pairs={{0,8},{4,12},{8,0},{12,4},{1,9},{5,13},{9,1},{13,5},{2,10},{6,14},... | collective-permute-start | bytes 884744 | tf_op jit(solution)/shard_map/ppermute | solution.py:440
  36.3 23.0 %collective-permute-start.12 = (bf16[2,64,1152]{2,1,0:T(8,128)(2,1)S(1)}, bf16[2,64,1152]{2,1,0:T(8,128)(2,1)S(1)}, u32[]{:S(2)}, u32[]{:S(2)}) collective-permute-start(bf16[2,64,1152]{2,1,0:T(8,128)(2,1)S(1)} %bitcast.23), channel_id=1, source_target_pairs={{0,12},{4,8},{8,4},{12,0},{1,13},{5,9},{9,5},{13,1},{2,14},{6,10},... | collective-permute-start | bytes 884744 | tf_op jit(solution)/shard_map/ppermute | solution.py:440
  40.5 20.0 %copy-start.4 = (bf16[1,64,1024]{2,1,0:T(8,128)(2,1)S(1)}, bf16[1,64,1024]{2,1,0:T(8,128)(2,1)}, u32[]{:S(2)}) copy-start(bf16[1,64,1024]{2,1,0:T(8,128)(2,1)} %get-tuple-element.61) | copy-start | bytes 393220
  40.5 9.3 %collective-permute-start.13 = (bf16[128,256]{1,0:T(8,128)(2,1)S(1)}, bf16[128,256]{1,0:T(8,128)(2,1)S(1)}, u32[]{:S(2)}, u32[]{:S(2)}) collective-permute-start(bf16[128,256]{1,0:T(8,128)(2,1)S(1)} %get-tuple-element.55), channel_id=1, source_target_pairs={{0,16},{16,0},{1,17},{17,1},{2,18},{18,2},{3,19},{19,3},{4,20},{20... | collective-permute-start | bytes 196616 | tf_op jit(solution)/shard_map/ppermute | solution.py:440
  51.2 16.2 %all-to-all-start.1 = ((bf16[16,64,128]{2,1,0:T(8,128)(2,1)}), bf16[16,64,128]{2,1,0:T(8,128)(2,1)S(1)}, u32[]{:S(2)}, u32[]{:S(2)}) async-start(bf16[16,64,128]{2,1,0:T(8,128)(2,1)} %bitcast.7), calls=%async_computation.1 | async-start | bytes 524288 | tf_op jit(solution)/shard_map/all_to_all | solution.py:436
  59.3 8.1 %copy-start.2 = (bf16[1,64,1024]{2,1,0:T(8,128)(2,1)S(1)}, bf16[1,64,1024]{2,1,0:T(8,128)(2,1)}, u32[]{:S(2)}) copy-start(bf16[1,64,1024]{2,1,0:T(8,128)(2,1)} %get-tuple-element.60.refs_0_) | copy-start | bytes 393220
  59.3 8.1 %copy-start.3 = (f32[128]{0:T(128)S(1)}, f32[128]{0:T(128)}, u32[]{:S(2)}) copy-start(f32[128]{0:T(128)} %param.12) | copy-start | bytes 1540
  59.3 2.5 %collective-permute-start.14 = (bf16[2,64,1152]{2,1,0:T(8,128)(2,1)S(1)}, bf16[2,64,1152]{2,1,0:T(8,128)(2,1)S(1)}, u32[]{:S(2)}, u32[]{:S(2)}) collective-permute-start(bf16[2,64,1152]{2,1,0:T(8,128)(2,1)S(1)} %bitcast.24), channel_id=1, source_target_pairs={{0,2},{2,0},{1,3},{3,1},{4,6},{6,4},{5,7},{7,5},{8,10},{10,8},{9,1... | collective-permute-start | bytes 884744 | tf_op jit(solution)/shard_map/ppermute | solution.py:440
  59.5 2.3 %collective-permute-start.15 = (bf16[2,64,1152]{2,1,0:T(8,128)(2,1)S(1)}, bf16[2,64,1152]{2,1,0:T(8,128)(2,1)S(1)}, u32[]{:S(2)}, u32[]{:S(2)}) collective-permute-start(bf16[2,64,1152]{2,1,0:T(8,128)(2,1)S(1)} %collective-permute-done.10.refs_1_), channel_id=1, source_target_pairs={{0,2},{2,0},{1,3},{3,1},{4,6},{6,4},{5,7},{7,5},{8,10},{10,8},{9,1... | collective-permute-start | bytes 884744 | tf_op jit(solution)/shard_map/ppermute | solution.py:440
  59.9 1.9 %collective-permute-start.16 = (bf16[2,64,1152]{2,1,0:T(8,128)(2,1)S(1)}, bf16[2,64,1152]{2,1,0:T(8,128)(2,1)S(1)}, u32[]{:S(2)}, u32[]{:S(2)}) collective-permute-start(bf16[2,64,1152]{2,1,0:T(8,128)(2,1)S(1)} %collective-permute-done.11.refs_2_), channel_id=1, source_target_pairs={{0,2},{2,0},{1,3},{3,1},{4,6},{6,4},{5,7},{7,5},{8,10},{10,8},{9,1... | collective-permute-start | bytes 884744 | tf_op jit(solution)/shard_map/ppermute | solution.py:440
  60.0 2.2 %collective-permute-start.17 = (bf16[2,64,1152]{2,1,0:T(8,128)(2,1)S(1)}, bf16[2,64,1152]{2,1,0:T(8,128)(2,1)S(1)}, u32[]{:S(2)}, u32[]{:S(2)}) collective-permute-start(bf16[2,64,1152]{2,1,0:T(8,128)(2,1)S(1)} %collective-permute-done.12.refs_3_), channel_id=1, source_target_pairs={{0,2},{2,0},{1,3},{3,1},{4,6},{6,4},{5,7},{7,5},{8,10},{10,8},{9,1... | collective-permute-start | bytes 884744 | tf_op jit(solution)/shard_map/ppermute | solution.py:440
  60.4 6.9 %collective-permute-start.18 = (bf16[1,64,1024]{2,1,0:T(8,128)(2,1)S(1)}, bf16[1,64,1024]{2,1,0:T(8,128)(2,1)S(1)}, u32[]{:S(2)}, u32[]{:S(2)}) collective-permute-start(bf16[1,64,1024]{2,1,0:T(8,128)(2,1)S(1)} %copy-done.4), channel_id=1, source_target_pairs={{0,1},{1,0},{2,3},{3,2},{4,5},{5,4},{6,7},{7,6},{8,9},{9,8},{10,11... | collective-permute-start | bytes 393224 | tf_op jit(solution)/shard_map/ppermute | solution.py:440
  71.1 18.9 %copy-start = (bf16[1024,1024]{1,0:T(8,128)(2,1)S(1)}, bf16[1024,1024]{1,0:T(8,128)(2,1)}, u32[]{:S(2)}) copy-start(bf16[1024,1024]{1,0:T(8,128)(2,1)} %get-tuple-element.44.normed_any.normed_ref) | copy-start | bytes 6291460
  83.7 6.3 %collective-permute-start.19 = (bf16[128,256]{1,0:T(8,128)(2,1)S(1)}, bf16[128,256]{1,0:T(8,128)(2,1)S(1)}, u32[]{:S(2)}, u32[]{:S(2)}) collective-permute-start(bf16[128,256]{1,0:T(8,128)(2,1)S(1)} %get-tuple-element.63), channel_id=1, source_target_pairs={{0,16},{16,0},{1,17},{17,1},{2,18},{18,2},{3,19},{19,3},{4,20},{20... | collective-permute-start | bytes 196616 | tf_op jit(solution)/shard_map/ppermute | solution.py:440
  92.1 18.7 %all-to-all-start.3 = ((bf16[32,32,256]{2,1,0:T(8,128)(2,1)}), bf16[32,32,256]{2,1,0:T(8,128)(2,1)S(1)}, u32[]{:S(2)}, u32[]{:S(2)}) async-start(bf16[32,32,256]{2,1,0:T(8,128)(2,1)} %bitcast.11), calls=%async_computation.3 | async-start | bytes 1048576 | tf_op jit(solution)/shard_map/all_to_all | solution.py:436
  94.9 6.0 %collective-permute-start.20 = (f32[100,128]{1,0:T(8,128)S(1)}, f32[100,128]{1,0:T(8,128)S(1)}, u32[]{:S(2)}, u32[]{:S(2)}) collective-permute-start(f32[100,128]{1,0:T(8,128)S(1)} %get-tuple-element.66), channel_id=1, source_target_pairs={{0,1},{1,0},{2,3},{3,2},{4,5},{5,4},{6,7},{7,6},{8,9},{9,8},{10,11... | collective-permute-start | bytes 153608 | tf_op jit(solution)/shard_map/ppermute | solution.py:440

commit v21 on v18

--- a/solution.py
+++ b/solution.py
@@ -85,10 +85,21 @@
         copy.wait()
 
 
-def weights_kernel(w_any, mix_any, readout_any, columns_any, packed_any, *refs):
-    w, columns, readout, packed, sems = refs
+def weights_kernel(
+    w_any, mix_any, readout_any, source_any, columns_any, packed_any, sent_any, *refs
+):
+    w, columns, readout, packed, sent, sems = refs
+    part = sent.shape[0]
+    place = lax.axis_index("ens") ^ 1 if sent_any.shape[0] == 1 else 0
+    place = pl.multiple_of(place * part, part)
     copies = fetch(
-        [(w_any, w), (readout_any, readout), (mix_any, packed.at[:, :LATENT_DIM])], sems
+        [
+            (w_any, w),
+            (readout_any, readout),
+            (mix_any, packed.at[:, :LATENT_DIM]),
+            (source_any.at[pl.ds(place, part)], sent),
+        ],
+        sems,
     )
     copies[0].wait()
     for g in range(GROUP):
@@ -103,12 +114,13 @@
             for m in range(members_num)
         ],
         sems,
-        3,
+        4,
     )
     wait(copies[1:])
+    out += fetch([(sent, sent_any.at[0])], sems, 4 + len(out))
     packed[:, LATENT_DIM:] = jnp.zeros((packed.shape[0], FIELD_PAD), BF16)
     packed[:, LATENT_DIM : LATENT_DIM + FIELD_NUM] = readout[...]
-    wait(out + fetch([(packed, packed_any)], sems, 3 + len(out)))
+    wait(out + fetch([(packed, packed_any)], sems, 4 + len(out)))
 
 
 def norm_kernel(near_any, source_any, normed_any, *refs):
@@ -481,21 +493,26 @@
     copies = 1 if paired else members_num
     source_parts = 2 if paired else 1
 
-    columns, packed = call(
+    columns, packed, leaving = call(
         weights_kernel,
         "prepare_weights",
-        [((halves, GROUP, copies, shard, 3 * COLS), BF16), ((shard, width), BF16)],
-        "hhh",
+        [
+            ((halves, GROUP, copies, shard, 3 * COLS), BF16),
+            ((shard, width), BF16),
+            ((1 if paired else members_num, part, LATENT_DIM), BF16),
+        ],
+        "hhhh",
         [
             pltpu.VMEM(w_attn.shape, BF16),
             pltpu.VMEM((GROUP, shard, 3 * COLS), BF16),
             pltpu.VMEM(readout_matrix.shape, BF16),
             pltpu.VMEM((shard, width), BF16),
-            pltpu.SemaphoreType.DMA((4 + halves * copies,)),
+            pltpu.VMEM((part, LATENT_DIM), BF16),
+            pltpu.SemaphoreType.DMA((6 + halves * copies,)),
         ],
         moved=2**20,
-        results="hh",
-    )(w_attn, w_mix, readout_matrix)
+        results="hhh",
+    )(w_attn, w_mix, readout_matrix, members.reshape(node_rows, LATENT_DIM))
     normed, *sources = call(
         norm_kernel,
         "norm",
@@ -521,7 +538,7 @@
             [((2, shard, width + LATENT_DIM), BF16)],
             "vvv",
             moved=2**18,
-        )(packed, swap(packed, "half", 1), sources[1])
+        )(packed, swap(packed, "half", 1), leaving)
     else:
         packed = in_order(packed, "half", 0)
     packed, normed = lax.optimization_barrier((packed, normed))
@@ -535,6 +552,7 @@
         columns = [columns[0].reshape(LATENT_DIM, 3 * COLS)]
         late = normed
     near[2] = swap(late, "quad", 2)
+    near = list(lax.optimization_barrier(tuple(near)))
     far = [swap(piece, "core", 1) for piece in near]
     normed, steps = call(
         collect_kernel,

time: 117 us -> 119 us (1.017)
  waiting for transfers between devices: 38.2 us -> 44.7 us
  starting transfers between devices: 37.8 us -> 32.8 us
    ppermute x20, waiting for transfers between devices: 26.9 us -> 33.3 us  [swap(): lax.ppermute(value, axis, [(i, i ^ step) for i in range(lax.axis_size(axi...]
    ppermute x20, starting transfers between devices: 21.5 us -> 16.1 us  [swap(): lax.ppermute(value, axis, [(i, i ^ step) for i in range(lax.axis_size(axi...]
  transfers between devices with their start and end apart: 23 -> 23, of which waited for: 12 -> 13; matrix products, arithmetic and copies ran while one was open for 1% -> 1% of each run, Pallas kernels for 14% -> 14%
where the time goes in v21:
time: 119 us; the launch traced here: 118 us
  waiting for transfers between devices  44.7 us (38%)
  starting transfers between devices  32.8 us (28%)
  Pallas kernels  26.1 us (22%)
  blocking collectives  9.9 us (8%)
  local copies, waits for them, and re-layouts  3.52 us (3%)
    ppermute x20, waiting for transfers between devices, swap(): lax.ppermute(value, axis, [(i, i ^ step) for i in range(lax.axis_size(axi...  33.3 us
    pallas_call x15, Pallas kernels, run(): made(*[pltpu.with_memory_space_constraint(arg, pltpu.HBM) if space == 'h'...  26.1 us
    all_to_all x3, starting transfers between devices, exchange(): return lax.all_to_all(chunks, axes, 0, 0)  16.6 us
    ppermute x20, starting transfers between devices, swap(): lax.ppermute(value, axis, [(i, i ^ step) for i in range(lax.axis_size(axi...  16.1 us
    all_to_all x3, waiting for transfers between devices, exchange(): return lax.all_to_all(chunks, axes, 0, 0)  11.4 us
    all_to_all x1, blocking collectives, exchange(): return lax.all_to_all(chunks, axes, 0, 0)  9.9 us
    unnamed x13, local copies, waits for them, and re-layouts  3.44 us
  transfers between devices with their start and end apart: 23, of which 13 were waited for; matrix products, arithmetic and copies ran while one was open for 1% of the time, Pallas kernels for 14%

profile of v21, /device:TPU:1, one launch (start us, length us, event | category | flops | bytes accessed | tf_op | source)
XLA Modules:
  0.0 117.9 jit_solution(11979109161746602152)
XLA Ops:
  0.6 1.9 %prepare_weights.1 = (bf16[2,8,1,32,384]{4,3,2,1,0:T(8,128)(2,1)}, bf16[32,1152]{1,0:T(8,128)(2,1)}, bf16[1,64,1024]{2,1,0:T(8,128)(2,1)}) custom-call(bf16[32,3072]{1,0:T(8,128)(2,1)} %w_any.1, bf16[32,1024]{1,0:T(8,128)(2,1)} %mix_any.1, bf16[32,100]{1,0:T(8,128)(2,1)} %readout_any.1, bf16[128,1024]{1,0:T(8,128)(2,1)} %bitcast.19), custom_call_target="tpu_custom_call" | custom-call | bytes 1048576 | tf_op jit(solution)/shard_map/prepare_weights/pallas_call | solution.py:63
  2.5 7.4 %all-to-all-start = ((bf16[16,32,384]{2,1,0:T(8,128)(2,1)}), bf16[16,32,384]{2,1,0:T(8,128)(2,1)S(1)}, u32[]{:S(2)}, u32[]{:S(2)}) async-start(bf16[16,32,384]{2,1,0:T(8,128)(2,1)} %bitcast.21), calls=%async_computation | async-start | bytes 786432 | tf_op jit(solution)/shard_map/all_to_all | solution.py:465
  9.9 2.3 %collective-permute-start = (bf16[32,1152]{1,0:T(8,128)(2,1)}, bf16[32,1152]{1,0:T(8,128)(2,1)S(1)}, u32[]{:S(2)}, u32[]{:S(2)}) collective-permute-start(bf16[32,1152]{1,0:T(8,128)(2,1)} %get-tuple-element.35.mine_ref), channel_id=1, source_target_pairs={{0,16},{16,0},{1,17},{17,1},{2,18},{18,2},{3,19},{19,3},{4,20},{20... | collective-permute-start | bytes 221192 | tf_op jit(solution)/shard_map/ppermute | solution.py:469
  12.2 1.9 %norm.1 = (bf16[144,1024]{1,0:T(8,128)(2,1)}, bf16[1,64,1024]{2,1,0:T(8,128)(2,1)}, bf16[1,64,1024]{2,1,0:T(8,128)(2,1)}) custom-call(s32[2,4]{1,0:T(2,128)} %near_any.1, bf16[128,1024]{1,0:T(8,128)(2,1)} %bitcast.20), custom_call_target="tpu_custom_call" | custom-call | flops 1048576 | bytes 1048576 | tf_op jit(solution)/shard_map/norm/pallas_call | solution.py:63
  14.1 10.7 %collective-permute-done.other_ref = bf16[32,1152]{1,0:T(8,128)(2,1)S(1)} collective-permute-done((bf16[32,1152]{1,0:T(8,128)(2,1)}, bf16[32,1152]{1,0:T(8,128)(2,1)S(1)}, u32[]{:S(2)}, u32[]{:S(2)}) %collective-permute-start) | collective-permute-done | bytes 73760 | tf_op jit(solution)/shard_map/ppermute | solution.py:469
  24.7 0.9 copy-done.3
  25.6 0.9 copy-done.4
  26.5 1.2 %collective-permute-start.1 = (bf16[144,1024]{1,0:T(8,128)(2,1)}, bf16[144,1024]{1,0:T(8,128)(2,1)S(1)}, u32[]{:S(2)}, u32[]{:S(2)}) collective-permute-start(bf16[144,1024]{1,0:T(8,128)(2,1)} %get-tuple-element.41.refs_0_), channel_id=1, source_target_pairs={{0,4},{4,0},{8,12},{12,8},{1,5},{5,1},{9,13},{13,9},{2,6},{6,2},{1... | collective-permute-start | bytes 884744 | tf_op jit(solution)/shard_map/ppermute | solution.py:469
  27.8 1.5 %collective-permute-start.2 = (bf16[144,1024]{1,0:T(8,128)(2,1)}, bf16[144,1024]{1,0:T(8,128)(2,1)S(1)}, u32[]{:S(2)}, u32[]{:S(2)}) collective-permute-start(bf16[144,1024]{1,0:T(8,128)(2,1)} %get-tuple-element.41.refs_0_), channel_id=1, source_target_pairs={{0,8},{4,12},{8,0},{12,4},{1,9},{5,13},{9,1},{13,5},{2,10},{6,14},... | collective-permute-start | bytes 884744 | tf_op jit(solution)/shard_map/ppermute | solution.py:469
  29.3 1.2 %collective-permute-start.9 = (bf16[2,32,2176]{2,1,0:T(8,128)(2,1)S(1)}, bf16[2,32,2176]{2,1,0:T(8,128)(2,1)S(1)}, u32[]{:S(2)}, u32[]{:S(2)}) collective-permute-start(bf16[2,32,2176]{2,1,0:T(8,128)(2,1)S(1)} %merge_halves.1.mine_ref), channel_id=1, source_target_pairs={{0,1},{1,0},{2,3},{3,2},{4,5},{5,4},{6,7},{7,6},{8,9},{9,8},{10,11... | collective-permute-start | bytes 835592 | tf_op jit(solution)/shard_map/ppermute | solution.py:469
  30.5 0.3 collective-permute-start.8
  30.7 10.1 %collective-permute-done.1.refs_1_ = bf16[144,1024]{1,0:T(8,128)(2,1)S(1)} collective-permute-done((bf16[144,1024]{1,0:T(8,128)(2,1)}, bf16[144,1024]{1,0:T(8,128)(2,1)S(1)}, u32[]{:S(2)}, u32[]{:S(2)}) %collective-permute-start.1) | collective-permute-done | bytes 294944 | tf_op jit(solution)/shard_map/ppermute | solution.py:469
  40.8 1.0 collective-permute-done.2.refs_2_
  41.8 2.0 %collective-permute-start.6 = (bf16[144,1024]{1,0:T(8,128)(2,1)S(1)}, bf16[144,1024]{1,0:T(8,128)(2,1)S(1)}, u32[]{:S(2)}, u32[]{:S(2)}) collective-permute-start(bf16[144,1024]{1,0:T(8,128)(2,1)S(1)} %collective-permute-done.2.refs_2_), channel_id=1, source_target_pairs={{0,2},{2,0},{1,3},{3,1},{4,6},{6,4},{5,7},{7,5},{8,10},{10,8},{9,1... | collective-permute-start | bytes 884744 | tf_op jit(solution)/shard_map/ppermute | solution.py:469
  43.8 0.5 collective-permute-start.5
  44.4 1.0 collective-permute-done.6.refs_6_
  45.4 1.2 %collective-permute-start.10 = (bf16[2,64,1152]{2,1,0:T(8,128)(2,1)S(1)}, bf16[2,64,1152]{2,1,0:T(8,128)(2,1)S(1)}, u32[]{:S(2)}, u32[]{:S(2)}) collective-permute-start(bf16[2,64,1152]{2,1,0:T(8,128)(2,1)S(1)} %bitcast.13), channel_id=1, source_target_pairs={{0,4},{4,0},{8,12},{12,8},{1,5},{5,1},{9,13},{13,9},{2,6},{6,2},{1... | collective-permute-start | bytes 884744 | tf_op jit(solution)/shard_map/ppermute | solution.py:469
  46.6 1.8 %collective-permute-start.12 = (bf16[2,64,1152]{2,1,0:T(8,128)(2,1)S(1)}, bf16[2,64,1152]{2,1,0:T(8,128)(2,1)S(1)}, u32[]{:S(2)}, u32[]{:S(2)}) collective-permute-start(bf16[2,64,1152]{2,1,0:T(8,128)(2,1)S(1)} %bitcast.15), channel_id=1, source_target_pairs={{0,12},{4,8},{8,4},{12,0},{1,13},{5,9},{9,5},{13,1},{2,14},{6,10},... | collective-permute-start | bytes 884744 | tf_op jit(solution)/shard_map/ppermute | solution.py:469
  48.3 1.0 copy-done.1
  49.3 1.5 %collect.1 = (bf16[1024,1024]{1,0:T(8,128)(2,1)}, f32[8,16,128]{2,1,0:T(8,128)S(1)}) custom-call(bf16[144,1024]{1,0:T(8,128)(2,1)S(1)} %copy-done.1, bf16[144,1024]{1,0:T(8,128)(2,1)S(1)} %collective-permute-done.1.refs_1_, bf16[144,1024]{1,0:T(8,128)(2,1)S(1)} %collective-permute-done.2.refs_2_, bf16[144,1024]{1,0:T(8,128)(2,1)S(1)} %collective-permute-done.3.refs_3_, ...), custom_call_target="tpu_custom_call" | custom-call | bytes 4194304 | tf_op jit(solution)/shard_map/collect/pallas_call | solution.py:63
  50.8 1.3 %project_rims.1 = (bf16[16,2,32,384]{3,2,1,0:T(8,128)(2,1)S(1)}, bf16[128,256]{1,0:T(8,128)(2,1)S(1)}) custom-call(bf16[1024,1024]{1,0:T(8,128)(2,1)} %get-tuple-element.45.normed_any.normed_ref, bf16[16,32,384]{2,1,0:T(8,128)(2,1)S(1)} %all-to-all-done.refs_0_, bf16[16,32,384]{2,1,0:T(8,128)(2,1)S(1)} %collective-permute-done.8.refs_1_), custom_call_target="tpu_custom_call" | custom-call | flops 67108864 | bytes 1048576 | tf_op jit(solution)/shard_map/project_rims/pallas_call | solution.py:63
  52.2 0.2 collective-permute-start.13
  52.4 2.8 %project.1 = (bf16[1024,128]{1,0:T(8,128)(2,1)S(1)}, bf16[1024,256]{1,0:T(8,128)(2,1)S(1)}) custom-call(bf16[1024,1024]{1,0:T(8,128)(2,1)} %get-tuple-element.45.normed_any.normed_ref, bf16[16,2,32,384]{3,2,1,0:T(8,128)(2,1)S(1)} %get-tuple-element.48.w_ref), custom_call_target="tpu_custom_call" | custom-call | flops 805306368 | bytes 4194304 | tf_op jit(solution)/shard_map/project/pallas_call | solution.py:63
  55.2 1.9 %attention_interior.1.done_ref = bf16[1024,128]{1,0:T(8,128)(2,1)S(1)} custom-call(f32[8,16,128]{2,1,0:T(8,128)S(1)} %get-tuple-element.46.steps_ref, bf16[1024,128]{1,0:T(8,128)(2,1)S(1)} %get-tuple-element.49.q_ref, bf16[1024,256]{1,0:T(8,128)(2,1)S(1)} %get-tuple-element.54.kv_ref), custom_call_target="tpu_custom_call" | custom-call | flops 268435456 | bytes 2097152 | tf_op jit(solution)/shard_map/attention_interior/pallas_call | solution.py:63
  57.1 3.2 %collective-permute-done.13.low_ref.high_ref = bf16[128,256]{1,0:T(8,128)(2,1)S(1)} collective-permute-done((bf16[128,256]{1,0:T(8,128)(2,1)S(1)}, bf16[128,256]{1,0:T(8,128)(2,1)S(1)}, u32[]{:S(2)}, u32[]{:S(2)}) %collective-permute-start.13) | collective-permute-done | bytes 65568 | tf_op jit(solution)/shard_map/ppermute | solution.py:469
  60.3 1.4 %attention_edges.1 = bf16[1024,128]{1,0:T(8,128)(2,1)} custom-call(f32[8,16,128]{2,1,0:T(8,128)S(1)} %get-tuple-element.46.steps_ref, bf16[1024,128]{1,0:T(8,128)(2,1)S(1)} %get-tuple-element.49.q_ref, bf16[1024,256]{1,0:T(8,128)(2,1)S(1)} %get-tuple-element.54.kv_ref, bf16[128,256]{1,0:T(8,128)(2,1)S(1)} %collective-permute-done.13.low_ref.high_ref, ...), custom_call_target="tpu_custom_call" | custom-call | flops 67108864 | bytes 1048576 | tf_op jit(solution)/shard_map/attention_edges/pallas_call | solution.py:63
  61.8 6.4 %all-to-all-start.1 = ((bf16[16,64,128]{2,1,0:T(8,128)(2,1)}), bf16[16,64,128]{2,1,0:T(8,128)(2,1)S(1)}, u32[]{:S(2)}, u32[]{:S(2)}) async-start(bf16[16,64,128]{2,1,0:T(8,128)(2,1)} %bitcast.3), calls=%async_computation.1 | async-start | bytes 524288 | tf_op jit(solution)/shard_map/all_to_all | solution.py:465
  68.3 0.4 collective-permute-start.15
  68.9 0.4 collective-permute-start.17
  69.3 0.6 collective-permute-done.14.refs_4_
  69.8 0.4 collective-permute-done.15.refs_5_
  70.2 0.4 collective-permute-done.16.refs_6_
  70.7 0.4 collective-permute-done.17.refs_7_
  71.1 1.5 %assemble.1.w_any = bf16[2,4,2,64,1152]{4,3,2,1,0:T(8,128)(2,1)} custom-call(bf16[2,64,1152]{2,1,0:T(8,128)(2,1)S(1)} %bitcast.17, bf16[2,64,1152]{2,1,0:T(8,128)(2,1)S(1)} %collective-permute-done.10.refs_1_, bf16[2,64,1152]{2,1,0:T(8,128)(2,1)S(1)} %collective-permute-done.11.refs_2_, bf16[2,64,1152]{2,1,0:T(8,128)(2,1)S(1)} %collective-permute-done.12.refs_3_, ...), custom_call_target="tpu_custom_call" | custom-call | bytes 4194304 | tf_op jit(solution)/shard_map/assemble/pallas_call | solution.py:63
  72.6 2.4 %all-to-all-done.1.att_ref = bf16[16,64,128]{2,1,0:T(8,128)(2,1)S(1)} async-done(((bf16[16,64,128]{2,1,0:T(8,128)(2,1)}), bf16[16,64,128]{2,1,0:T(8,128)(2,1)S(1)}, u32[]{:S(2)}, u32[]{:S(2)}) %all-to-all-start.1) | async-done | bytes 262176 | tf_op jit(solution)/shard_map/all_to_all | solution.py:465
  75.0 3.7 %mix_loss_backward.1 = (f32[100,128]{1,0:T(8,128)S(1)}, bf16[16,64,128]{2,1,0:T(8,128)(2,1)S(1)}) custom-call(bf16[16,64,128]{2,1,0:T(8,128)(2,1)S(1)} %all-to-all-done.1.att_ref, f32[1,128]{1,0:T(1,128)S(1)} %bitcast.18, f32[100,128]{1,0:T(8,128)} %truth_any.1, bf16[2,4,2,64,1152]{4,3,2,1,0:T(8,128)(2,1)} %assemble.1.w_any, ...), custom_call_target="tpu_custom_call" | custom-call | flops 603979776 | bytes 4194304 | tf_op jit(solution)/shard_map/mix_loss_backward/pallas_call | solution.py:63
  78.7 9.9 %all_to_all.20 = bf16[16,64,128]{2,1,0:T(8,128)(2,1)S(1)} all-to-all(bf16[16,64,128]{2,1,0:T(8,128)(2,1)S(1)} %get-tuple-element.62), channel_id=1, replica_groups=mesh['half'=2,'quad'=4,'core'=2,'ens'=2] {'quad','core','ens'}, dimensions={0} | all-to-all | bytes 524288 | tf_op jit(solution)/shard_map/all_to_all | solution.py:465
  88.6 1.4 %attention_edges_back.1 = (f32[2,256,256]{2,1,0:T(8,128)S(1)}, bf16[128,256]{1,0:T(8,128)(2,1)S(1)}) custom-call(f32[8,16,128]{2,1,0:T(8,128)S(1)} %get-tuple-element.46.steps_ref, bf16[1024,128]{1,0:T(8,128)(2,1)S(1)} %get-tuple-element.49.q_ref, bf16[1024,256]{1,0:T(8,128)(2,1)S(1)} %get-tuple-element.54.kv_ref, ...), custom_call_target="tpu_custom_call" | custom-call | flops 167772160 | bytes 1048576 | tf_op jit(solution)/shard_map/attention_edges_back/pallas_call | solution.py:63
  90.0 1.4 %collective-permute-start.18 = (bf16[128,256]{1,0:T(8,128)(2,1)S(1)}, bf16[128,256]{1,0:T(8,128)(2,1)S(1)}, u32[]{:S(2)}, u32[]{:S(2)}) collective-permute-start(bf16[128,256]{1,0:T(8,128)(2,1)S(1)} %get-tuple-element.63), channel_id=1, source_target_pairs={{0,16},{16,0},{1,17},{17,1},{2,18},{18,2},{3,19},{19,3},{4,20},{20... | collective-permute-start | bytes 196616 | tf_op jit(solution)/shard_map/ppermute | solution.py:469
  91.4 3.8 %attention_interior_back.1.grads_ref = f32[1024,256]{1,0:T(8,128)S(1)} custom-call(f32[8,16,128]{2,1,0:T(8,128)S(1)} %get-tuple-element.46.steps_ref, bf16[1024,128]{1,0:T(8,128)(2,1)S(1)} %get-tuple-element.49.q_ref, bf16[1024,256]{1,0:T(8,128)(2,1)S(1)} %get-tuple-element.54.kv_ref, bf16[1024,128]{1,0:T(8,128)(2,1)S(1)} %bitcast.11, ...), custom_call_target="tpu_custom_call" | custom-call | flops 536870912 | bytes 4194304 | tf_op jit(solution)/shard_map/attention_interior_back/pallas_call | solution.py:63
  95.2 1.0 collective-permute-done.18.from_low_ref.from_high_ref
  96.3 2.1 %product.1 = bf16[1024,256]{1,0:T(8,128)(2,1)} custom-call(bf16[1024,1024]{1,0:T(8,128)(2,1)S(1)} %copy-done, bf16[128,256]{1,0:T(8,128)(2,1)S(1)} %collective-permute-done.18.from_low_ref.from_high_ref, bf16[128,256]{1,0:T(8,128)(2,1)S(1)} %collective-permute-done.18.from_low_ref.from_high_ref, f32[1024,256]{1,0:T(8,128)S(1)} %attention_interior_back.1.grads_ref), custom_call_target="tpu_custom_call" | custom-call | flops 1073741824 | bytes 4194304 | tf_op jit(solution)/shard_map/product/pallas_call | solution.py:63
  98.4 2.9 %all-to-all-start.3 = ((bf16[32,32,256]{2,1,0:T(8,128)(2,1)}), bf16[32,32,256]{2,1,0:T(8,128)(2,1)S(1)}, u32[]{:S(2)}, u32[]{:S(2)}) async-start(bf16[32,32,256]{2,1,0:T(8,128)(2,1)} %bitcast.7), calls=%async_computation.3 | async-start | bytes 1048576 | tf_op jit(solution)/shard_map/all_to_all | solution.py:465
  101.3 1.5 %collective-permute-start.19 = (f32[100,128]{1,0:T(8,128)S(1)}, f32[100,128]{1,0:T(8,128)S(1)}, u32[]{:S(2)}, u32[]{:S(2)}) collective-permute-start(f32[100,128]{1,0:T(8,128)S(1)} %get-tuple-element.66), channel_id=1, source_target_pairs={{0,1},{1,0},{2,3},{3,2},{4,5},{5,4},{6,7},{7,6},{8,9},{9,8},{10,11... | collective-permute-start | bytes 153608 | tf_op jit(solution)/shard_map/ppermute | solution.py:469
  102.7 4.5 %collective-permute-done.19 = f32[100,128]{1,0:T(8,128)S(1)} collective-permute-done((f32[100,128]{1,0:T(8,128)S(1)}, f32[100,128]{1,0:T(8,128)S(1)}, u32[]{:S(2)}, u32[]{:S(2)}) %collective-permute-start.19) | collective-permute-done | bytes 51232 | tf_op jit(solution)/shard_map/ppermute | solution.py:469
  107.5 0.7 copy.9
  108.1 9.0 %all-to-all-done.3 = bf16[32,32,256]{2,1,0:T(8,128)(2,1)S(1)} async-done(((bf16[32,32,256]{2,1,0:T(8,128)(2,1)}), bf16[32,32,256]{2,1,0:T(8,128)(2,1)S(1)}, u32[]{:S(2)}, u32[]{:S(2)}) %all-to-all-start.3) | async-done | bytes 524320 | tf_op jit(solution)/shard_map/all_to_all | solution.py:465
  117.1 0.8 gather_sums.1
  (31 shorter events, 0.6 us)
Async XLA Ops:
  2.5 25.3 %all-to-all-start = ((bf16[16,32,384]{2,1,0:T(8,128)(2,1)}), bf16[16,32,384]{2,1,0:T(8,128)(2,1)S(1)}, u32[]{:S(2)}, u32[]{:S(2)}) async-start(bf16[16,32,384]{2,1,0:T(8,128)(2,1)} %bitcast.21), calls=%async_computation | async-start | bytes 786432 | tf_op jit(solution)/shard_map/all_to_all | solution.py:465
  9.9 14.8 %collective-permute-start = (bf16[32,1152]{1,0:T(8,128)(2,1)}, bf16[32,1152]{1,0:T(8,128)(2,1)S(1)}, u32[]{:S(2)}, u32[]{:S(2)}) collective-permute-start(bf16[32,1152]{1,0:T(8,128)(2,1)} %get-tuple-element.35.mine_ref), channel_id=1, source_target_pairs={{0,16},{16,0},{1,17},{17,1},{2,18},{18,2},{3,19},{19,3},{4,20},{20... | collective-permute-start | bytes 221192 | tf_op jit(solution)/shard_map/ppermute | solution.py:469
  24.7 0.9 copy-start.3
  25.6 0.9 copy-start.4
  26.5 14.2 %collective-permute-start.1 = (bf16[144,1024]{1,0:T(8,128)(2,1)}, bf16[144,1024]{1,0:T(8,128)(2,1)S(1)}, u32[]{:S(2)}, u32[]{:S(2)}) collective-permute-start(bf16[144,1024]{1,0:T(8,128)(2,1)} %get-tuple-element.41.refs_0_), channel_id=1, source_target_pairs={{0,4},{4,0},{8,12},{12,8},{1,5},{5,1},{9,13},{13,9},{2,6},{6,2},{1... | collective-permute-start | bytes 884744 | tf_op jit(solution)/shard_map/ppermute | solution.py:469
  27.8 13.0 %collective-permute-start.3 = (bf16[144,1024]{1,0:T(8,128)(2,1)}, bf16[144,1024]{1,0:T(8,128)(2,1)S(1)}, u32[]{:S(2)}, u32[]{:S(2)}) collective-permute-start(bf16[144,1024]{1,0:T(8,128)(2,1)} %get-tuple-element.41.refs_0_), channel_id=1, source_target_pairs={{0,12},{4,8},{8,4},{12,0},{1,13},{5,9},{9,5},{13,1},{2,14},{6,10},... | collective-permute-start | bytes 884744 | tf_op jit(solution)/shard_map/ppermute | solution.py:469
  27.8 14.0 %collective-permute-start.2 = (bf16[144,1024]{1,0:T(8,128)(2,1)}, bf16[144,1024]{1,0:T(8,128)(2,1)S(1)}, u32[]{:S(2)}, u32[]{:S(2)}) collective-permute-start(bf16[144,1024]{1,0:T(8,128)(2,1)} %get-tuple-element.41.refs_0_), channel_id=1, source_target_pairs={{0,8},{4,12},{8,0},{12,4},{1,9},{5,13},{9,1},{13,5},{2,10},{6,14},... | collective-permute-start | bytes 884744 | tf_op jit(solution)/shard_map/ppermute | solution.py:469
  29.3 15.0 %collective-permute-start.9 = (bf16[2,32,2176]{2,1,0:T(8,128)(2,1)S(1)}, bf16[2,32,2176]{2,1,0:T(8,128)(2,1)S(1)}, u32[]{:S(2)}, u32[]{:S(2)}) collective-permute-start(bf16[2,32,2176]{2,1,0:T(8,128)(2,1)S(1)} %merge_halves.1.mine_ref), channel_id=1, source_target_pairs={{0,1},{1,0},{2,3},{3,2},{4,5},{5,4},{6,7},{7,6},{8,9},{9,8},{10,11... | collective-permute-start | bytes 835592 | tf_op jit(solution)/shard_map/ppermute | solution.py:469
  30.5 20.4 %collective-permute-start.8 = (bf16[16,32,384]{2,1,0:T(8,128)(2,1)S(1)}, bf16[16,32,384]{2,1,0:T(8,128)(2,1)S(1)}, u32[]{:S(2)}, u32[]{:S(2)}) collective-permute-start(bf16[16,32,384]{2,1,0:T(8,128)(2,1)S(1)} %all-to-all-done.refs_0_), channel_id=1, source_target_pairs={{0,1},{1,0},{2,3},{3,2},{4,5},{5,4},{6,7},{7,6},{8,9},{9,8},{10,11... | collective-permute-start | bytes 1179656 | tf_op jit(solution)/shard_map/ppermute | solution.py:469
  41.8 3.6 %collective-permute-start.6 = (bf16[144,1024]{1,0:T(8,128)(2,1)S(1)}, bf16[144,1024]{1,0:T(8,128)(2,1)S(1)}, u32[]{:S(2)}, u32[]{:S(2)}) collective-permute-start(bf16[144,1024]{1,0:T(8,128)(2,1)S(1)} %collective-permute-done.2.refs_2_), channel_id=1, source_target_pairs={{0,2},{2,0},{1,3},{3,1},{4,6},{6,4},{5,7},{7,5},{8,10},{10,8},{9,1... | collective-permute-start | bytes 884744 | tf_op jit(solution)/shard_map/ppermute | solution.py:469
  43.8 2.8 %collective-permute-start.4 = (bf16[144,1024]{1,0:T(8,128)(2,1)}, bf16[144,1024]{1,0:T(8,128)(2,1)S(1)}, u32[]{:S(2)}, u32[]{:S(2)}) collective-permute-start(bf16[144,1024]{1,0:T(8,128)(2,1)} %get-tuple-element.41.refs_0_), channel_id=1, source_target_pairs={{0,2},{2,0},{1,3},{3,1},{4,6},{6,4},{5,7},{7,5},{8,10},{10,8},{9,1... | collective-permute-start | bytes 884744 | tf_op jit(solution)/shard_map/ppermute | solution.py:469
  43.8 2.8 %collective-permute-start.5 = (bf16[144,1024]{1,0:T(8,128)(2,1)S(1)}, bf16[144,1024]{1,0:T(8,128)(2,1)S(1)}, u32[]{:S(2)}, u32[]{:S(2)}) collective-permute-start(bf16[144,1024]{1,0:T(8,128)(2,1)S(1)} %collective-permute-done.1.refs_1_), channel_id=1, source_target_pairs={{0,2},{2,0},{1,3},{3,1},{4,6},{6,4},{5,7},{7,5},{8,10},{10,8},{9,1... | collective-permute-start | bytes 884744 | tf_op jit(solution)/shard_map/ppermute | solution.py:469
  44.3 4.0 %collective-permute-start.7 = (bf16[144,1024]{1,0:T(8,128)(2,1)S(1)}, bf16[144,1024]{1,0:T(8,128)(2,1)S(1)}, u32[]{:S(2)}, u32[]{:S(2)}) collective-permute-start(bf16[144,1024]{1,0:T(8,128)(2,1)S(1)} %collective-permute-done.3.refs_3_), channel_id=1, source_target_pairs={{0,2},{2,0},{1,3},{3,1},{4,6},{6,4},{5,7},{7,5},{8,10},{10,8},{9,1... | collective-permute-start | bytes 884744 | tf_op jit(solution)/shard_map/ppermute | solution.py:469
  45.4 22.8 %collective-permute-start.10 = (bf16[2,64,1152]{2,1,0:T(8,128)(2,1)S(1)}, bf16[2,64,1152]{2,1,0:T(8,128)(2,1)S(1)}, u32[]{:S(2)}, u32[]{:S(2)}) collective-permute-start(bf16[2,64,1152]{2,1,0:T(8,128)(2,1)S(1)} %bitcast.13), channel_id=1, source_target_pairs={{0,4},{4,0},{8,12},{12,8},{1,5},{5,1},{9,13},{13,9},{2,6},{6,2},{1... | collective-permute-start | bytes 884744 | tf_op jit(solution)/shard_map/ppermute | solution.py:469
  46.6 21.6 %collective-permute-start.11 = (bf16[2,64,1152]{2,1,0:T(8,128)(2,1)S(1)}, bf16[2,64,1152]{2,1,0:T(8,128)(2,1)S(1)}, u32[]{:S(2)}, u32[]{:S(2)}) collective-permute-start(bf16[2,64,1152]{2,1,0:T(8,128)(2,1)S(1)} %bitcast.14), channel_id=1, source_target_pairs={{0,8},{4,12},{8,0},{12,4},{1,9},{5,13},{9,1},{13,5},{2,10},{6,14},... | collective-permute-start | bytes 884744 | tf_op jit(solution)/shard_map/ppermute | solution.py:469
  46.6 21.6 %collective-permute-start.12 = (bf16[2,64,1152]{2,1,0:T(8,128)(2,1)S(1)}, bf16[2,64,1152]{2,1,0:T(8,128)(2,1)S(1)}, u32[]{:S(2)}, u32[]{:S(2)}) collective-permute-start(bf16[2,64,1152]{2,1,0:T(8,128)(2,1)S(1)} %bitcast.15), channel_id=1, source_target_pairs={{0,12},{4,8},{8,4},{12,0},{1,13},{5,9},{9,5},{13,1},{2,14},{6,10},... | collective-permute-start | bytes 884744 | tf_op jit(solution)/shard_map/ppermute | solution.py:469
  48.3 1.0 copy-start.1
  52.2 8.2 %collective-permute-start.13 = (bf16[128,256]{1,0:T(8,128)(2,1)S(1)}, bf16[128,256]{1,0:T(8,128)(2,1)S(1)}, u32[]{:S(2)}, u32[]{:S(2)}) collective-permute-start(bf16[128,256]{1,0:T(8,128)(2,1)S(1)} %get-tuple-element.55), channel_id=1, source_target_pairs={{0,16},{16,0},{1,17},{17,1},{2,18},{18,2},{3,19},{19,3},{4,20},{20... | collective-permute-start | bytes 196616 | tf_op jit(solution)/shard_map/ppermute | solution.py:469
  61.8 13.2 %all-to-all-start.1 = ((bf16[16,64,128]{2,1,0:T(8,128)(2,1)}), bf16[16,64,128]{2,1,0:T(8,128)(2,1)S(1)}, u32[]{:S(2)}, u32[]{:S(2)}) async-start(bf16[16,64,128]{2,1,0:T(8,128)(2,1)} %bitcast.3), calls=%async_computation.1 | async-start | bytes 524288 | tf_op jit(solution)/shard_map/all_to_all | solution.py:465
  68.1 6.9 %copy-start.2 = (bf16[1,64,1024]{2,1,0:T(8,128)(2,1)S(1)}, bf16[1,64,1024]{2,1,0:T(8,128)(2,1)}, u32[]{:S(2)}) copy-start(bf16[1,64,1024]{2,1,0:T(8,128)(2,1)} %get-tuple-element.60.refs_0_) | copy-start | bytes 393220
  68.1 6.9 %copy-start.5 = (f32[128]{0:T(128)S(1)}, f32[128]{0:T(128)}, u32[]{:S(2)}) copy-start(f32[128]{0:T(128)} %param.12) | copy-start | bytes 1540
  68.2 1.6 %collective-permute-start.14 = (bf16[2,64,1152]{2,1,0:T(8,128)(2,1)S(1)}, bf16[2,64,1152]{2,1,0:T(8,128)(2,1)S(1)}, u32[]{:S(2)}, u32[]{:S(2)}) collective-permute-start(bf16[2,64,1152]{2,1,0:T(8,128)(2,1)S(1)} %bitcast.16), channel_id=1, source_target_pairs={{0,2},{2,0},{1,3},{3,1},{4,6},{6,4},{5,7},{7,5},{8,10},{10,8},{9,1... | collective-permute-start | bytes 884744 | tf_op jit(solution)/shard_map/ppermute | solution.py:469
  68.3 1.9 %collective-permute-start.15 = (bf16[2,64,1152]{2,1,0:T(8,128)(2,1)S(1)}, bf16[2,64,1152]{2,1,0:T(8,128)(2,1)S(1)}, u32[]{:S(2)}, u32[]{:S(2)}) collective-permute-start(bf16[2,64,1152]{2,1,0:T(8,128)(2,1)S(1)} %collective-permute-done.10.refs_1_), channel_id=1, source_target_pairs={{0,2},{2,0},{1,3},{3,1},{4,6},{6,4},{5,7},{7,5},{8,10},{10,8},{9,1... | collective-permute-start | bytes 884744 | tf_op jit(solution)/shard_map/ppermute | solution.py:469
  68.8 1.9 %collective-permute-start.16 = (bf16[2,64,1152]{2,1,0:T(8,128)(2,1)S(1)}, bf16[2,64,1152]{2,1,0:T(8,128)(2,1)S(1)}, u32[]{:S(2)}, u32[]{:S(2)}) collective-permute-start(bf16[2,64,1152]{2,1,0:T(8,128)(2,1)S(1)} %collective-permute-done.11.refs_2_), channel_id=1, source_target_pairs={{0,2},{2,0},{1,3},{3,1},{4,6},{6,4},{5,7},{7,5},{8,10},{10,8},{9,1... | collective-permute-start | bytes 884744 | tf_op jit(solution)/shard_map/ppermute | solution.py:469
  68.9 2.2 %collective-permute-start.17 = (bf16[2,64,1152]{2,1,0:T(8,128)(2,1)S(1)}, bf16[2,64,1152]{2,1,0:T(8,128)(2,1)S(1)}, u32[]{:S(2)}, u32[]{:S(2)}) collective-permute-start(bf16[2,64,1152]{2,1,0:T(8,128)(2,1)S(1)} %collective-permute-done.12.refs_3_), channel_id=1, source_target_pairs={{0,2},{2,0},{1,3},{3,1},{4,6},{6,4},{5,7},{7,5},{8,10},{10,8},{9,1... | collective-permute-start | bytes 884744 | tf_op jit(solution)/shard_map/ppermute | solution.py:469
  78.7 17.6 %copy-start = (bf16[1024,1024]{1,0:T(8,128)(2,1)S(1)}, bf16[1024,1024]{1,0:T(8,128)(2,1)}, u32[]{:S(2)}) copy-start(bf16[1024,1024]{1,0:T(8,128)(2,1)} %get-tuple-element.45.normed_any.normed_ref) | copy-start | bytes 6291460
  90.0 6.3 %collective-permute-start.18 = (bf16[128,256]{1,0:T(8,128)(2,1)S(1)}, bf16[128,256]{1,0:T(8,128)(2,1)S(1)}, u32[]{:S(2)}, u32[]{:S(2)}) collective-permute-start(bf16[128,256]{1,0:T(8,128)(2,1)S(1)} %get-tuple-element.63), channel_id=1, source_target_pairs={{0,16},{16,0},{1,17},{17,1},{2,18},{18,2},{3,19},{19,3},{4,20},{20... | collective-permute-start | bytes 196616 | tf_op jit(solution)/shard_map/ppermute | solution.py:469
  98.4 18.7 %all-to-all-start.3 = ((bf16[32,32,256]{2,1,0:T(8,128)(2,1)}), bf16[32,32,256]{2,1,0:T(8,128)(2,1)S(1)}, u32[]{:S(2)}, u32[]{:S(2)}) async-start(bf16[32,32,256]{2,1,0:T(8,128)(2,1)} %bitcast.7), calls=%async_computation.3 | async-start | bytes 1048576 | tf_op jit(solution)/shard_map/all_to_all | solution.py:465
  101.3 6.0 %collective-permute-start.19 = (f32[100,128]{1,0:T(8,128)S(1)}, f32[100,128]{1,0:T(8,128)S(1)}, u32[]{:S(2)}, u32[]{:S(2)}) collective-permute-start(f32[100,128]{1,0:T(8,128)S(1)} %get-tuple-element.66), channel_id=1, source_target_pairs={{0,1},{1,0},{2,3},{3,2},{4,5},{5,4},{6,7},{7,6},{8,9},{9,8},{10,11... | collective-permute-start | bytes 153608 | tf_op jit(solution)/shard_map/ppermute | solution.py:469

commit v22 on v21

--- a/solution.py
+++ b/solution.py
@@ -537,7 +537,7 @@
             "merge_halves",
             [((2, shard, width + LATENT_DIM), BF16)],
             "vvv",
-            moved=2**18,
+            moved=2**22,
         )(packed, swap(packed, "half", 1), leaving)
     else:
         packed = in_order(packed, "half", 0)

time: 119 us -> 119 us (level)
  no operation moved by 1% of the time
where the time goes in v22:
time: 119 us; the launch traced here: 118 us
  waiting for transfers between devices  44.7 us (38%)
  starting transfers between devices  32.8 us (28%)
  Pallas kernels  26.1 us (22%)
  blocking collectives  9.9 us (8%)
  local copies, waits for them, and re-layouts  3.52 us (3%)
    ppermute x20, waiting for transfers between devices, swap(): lax.ppermute(value, axis, [(i, i ^ step) for i in range(lax.axis_size(axi...  33.3 us
    pallas_call x15, Pallas kernels, run(): made(*[pltpu.with_memory_space_constraint(arg, pltpu.HBM) if space == 'h'...  26.1 us
    all_to_all x3, starting transfers between devices, exchange(): return lax.all_to_all(chunks, axes, 0, 0)  16.6 us
    ppermute x20, starting transfers between devices, swap(): lax.ppermute(value, axis, [(i, i ^ step) for i in range(lax.axis_size(axi...  16.1 us
    all_to_all x3, waiting for transfers between devices, exchange(): return lax.all_to_all(chunks, axes, 0, 0)  11.4 us
    all_to_all x1, blocking collectives, exchange(): return lax.all_to_all(chunks, axes, 0, 0)  9.9 us
    unnamed x13, local copies, waits for them, and re-layouts  3.44 us
  transfers between devices with their start and end apart: 23, of which 13 were waited for; matrix products, arithmetic and copies ran while one was open for 1% of the time, Pallas kernels for 14%

profile of v22, /device:TPU:1, one launch (start us, length us, event | category | flops | bytes accessed | tf_op | source)
XLA Modules:
  0.0 117.9 jit_solution(11979109161746602152)
XLA Ops:
  0.6 1.9 %prepare_weights.1 = (bf16[2,8,1,32,384]{4,3,2,1,0:T(8,128)(2,1)}, bf16[32,1152]{1,0:T(8,128)(2,1)}, bf16[1,64,1024]{2,1,0:T(8,128)(2,1)}) custom-call(bf16[32,3072]{1,0:T(8,128)(2,1)} %w_any.1, bf16[32,1024]{1,0:T(8,128)(2,1)} %mix_any.1, bf16[32,100]{1,0:T(8,128)(2,1)} %readout_any.1, bf16[128,1024]{1,0:T(8,128)(2,1)} %bitcast.19), custom_call_target="tpu_custom_call" | custom-call | bytes 1048576 | tf_op jit(solution)/shard_map/prepare_weights/pallas_call | solution.py:63
  2.5 7.4 %all-to-all-start = ((bf16[16,32,384]{2,1,0:T(8,128)(2,1)}), bf16[16,32,384]{2,1,0:T(8,128)(2,1)S(1)}, u32[]{:S(2)}, u32[]{:S(2)}) async-start(bf16[16,32,384]{2,1,0:T(8,128)(2,1)} %bitcast.21), calls=%async_computation | async-start | bytes 786432 | tf_op jit(solution)/shard_map/all_to_all | solution.py:465
  9.9 2.3 %collective-permute-start = (bf16[32,1152]{1,0:T(8,128)(2,1)}, bf16[32,1152]{1,0:T(8,128)(2,1)S(1)}, u32[]{:S(2)}, u32[]{:S(2)}) collective-permute-start(bf16[32,1152]{1,0:T(8,128)(2,1)} %get-tuple-element.35.mine_ref), channel_id=1, source_target_pairs={{0,16},{16,0},{1,17},{17,1},{2,18},{18,2},{3,19},{19,3},{4,20},{20... | collective-permute-start | bytes 221192 | tf_op jit(solution)/shard_map/ppermute | solution.py:469
  12.2 1.9 %norm.1 = (bf16[144,1024]{1,0:T(8,128)(2,1)}, bf16[1,64,1024]{2,1,0:T(8,128)(2,1)}, bf16[1,64,1024]{2,1,0:T(8,128)(2,1)}) custom-call(s32[2,4]{1,0:T(2,128)} %near_any.1, bf16[128,1024]{1,0:T(8,128)(2,1)} %bitcast.20), custom_call_target="tpu_custom_call" | custom-call | flops 1048576 | bytes 1048576 | tf_op jit(solution)/shard_map/norm/pallas_call | solution.py:63
  14.1 10.7 %collective-permute-done.other_ref = bf16[32,1152]{1,0:T(8,128)(2,1)S(1)} collective-permute-done((bf16[32,1152]{1,0:T(8,128)(2,1)}, bf16[32,1152]{1,0:T(8,128)(2,1)S(1)}, u32[]{:S(2)}, u32[]{:S(2)}) %collective-permute-start) | collective-permute-done | bytes 73760 | tf_op jit(solution)/shard_map/ppermute | solution.py:469
  24.7 0.9 copy-done.3
  25.6 0.9 copy-done.4
  26.5 1.2 %collective-permute-start.1 = (bf16[144,1024]{1,0:T(8,128)(2,1)}, bf16[144,1024]{1,0:T(8,128)(2,1)S(1)}, u32[]{:S(2)}, u32[]{:S(2)}) collective-permute-start(bf16[144,1024]{1,0:T(8,128)(2,1)} %get-tuple-element.41.refs_0_), channel_id=1, source_target_pairs={{0,4},{4,0},{8,12},{12,8},{1,5},{5,1},{9,13},{13,9},{2,6},{6,2},{1... | collective-permute-start | bytes 884744 | tf_op jit(solution)/shard_map/ppermute | solution.py:469
  27.8 1.5 %collective-permute-start.2 = (bf16[144,1024]{1,0:T(8,128)(2,1)}, bf16[144,1024]{1,0:T(8,128)(2,1)S(1)}, u32[]{:S(2)}, u32[]{:S(2)}) collective-permute-start(bf16[144,1024]{1,0:T(8,128)(2,1)} %get-tuple-element.41.refs_0_), channel_id=1, source_target_pairs={{0,8},{4,12},{8,0},{12,4},{1,9},{5,13},{9,1},{13,5},{2,10},{6,14},... | collective-permute-start | bytes 884744 | tf_op jit(solution)/shard_map/ppermute | solution.py:469
  29.3 1.2 %collective-permute-start.9 = (bf16[2,32,2176]{2,1,0:T(8,128)(2,1)S(1)}, bf16[2,32,2176]{2,1,0:T(8,128)(2,1)S(1)}, u32[]{:S(2)}, u32[]{:S(2)}) collective-permute-start(bf16[2,32,2176]{2,1,0:T(8,128)(2,1)S(1)} %merge_halves.1.mine_ref), channel_id=1, source_target_pairs={{0,1},{1,0},{2,3},{3,2},{4,5},{5,4},{6,7},{7,6},{8,9},{9,8},{10,11... | collective-permute-start | bytes 835592 | tf_op jit(solution)/shard_map/ppermute | solution.py:469
  30.5 0.3 collective-permute-start.8
  30.7 10.1 %collective-permute-done.1.refs_1_ = bf16[144,1024]{1,0:T(8,128)(2,1)S(1)} collective-permute-done((bf16[144,1024]{1,0:T(8,128)(2,1)}, bf16[144,1024]{1,0:T(8,128)(2,1)S(1)}, u32[]{:S(2)}, u32[]{:S(2)}) %collective-permute-start.1) | collective-permute-done | bytes 294944 | tf_op jit(solution)/shard_map/ppermute | solution.py:469
  40.8 1.0 collective-permute-done.2.refs_2_
  41.8 2.0 %collective-permute-start.6 = (bf16[144,1024]{1,0:T(8,128)(2,1)S(1)}, bf16[144,1024]{1,0:T(8,128)(2,1)S(1)}, u32[]{:S(2)}, u32[]{:S(2)}) collective-permute-start(bf16[144,1024]{1,0:T(8,128)(2,1)S(1)} %collective-permute-done.2.refs_2_), channel_id=1, source_target_pairs={{0,2},{2,0},{1,3},{3,1},{4,6},{6,4},{5,7},{7,5},{8,10},{10,8},{9,1... | collective-permute-start | bytes 884744 | tf_op jit(solution)/shard_map/ppermute | solution.py:469
  43.8 0.5 collective-permute-start.5
  44.4 1.0 collective-permute-done.6.refs_6_
  45.4 1.2 %collective-permute-start.10 = (bf16[2,64,1152]{2,1,0:T(8,128)(2,1)S(1)}, bf16[2,64,1152]{2,1,0:T(8,128)(2,1)S(1)}, u32[]{:S(2)}, u32[]{:S(2)}) collective-permute-start(bf16[2,64,1152]{2,1,0:T(8,128)(2,1)S(1)} %bitcast.13), channel_id=1, source_target_pairs={{0,4},{4,0},{8,12},{12,8},{1,5},{5,1},{9,13},{13,9},{2,6},{6,2},{1... | collective-permute-start | bytes 884744 | tf_op jit(solution)/shard_map/ppermute | solution.py:469
  46.6 1.8 %collective-permute-start.12 = (bf16[2,64,1152]{2,1,0:T(8,128)(2,1)S(1)}, bf16[2,64,1152]{2,1,0:T(8,128)(2,1)S(1)}, u32[]{:S(2)}, u32[]{:S(2)}) collective-permute-start(bf16[2,64,1152]{2,1,0:T(8,128)(2,1)S(1)} %bitcast.15), channel_id=1, source_target_pairs={{0,12},{4,8},{8,4},{12,0},{1,13},{5,9},{9,5},{13,1},{2,14},{6,10},... | collective-permute-start | bytes 884744 | tf_op jit(solution)/shard_map/ppermute | solution.py:469
  48.3 1.0 copy-done.1
  49.3 1.5 %collect.1 = (bf16[1024,1024]{1,0:T(8,128)(2,1)}, f32[8,16,128]{2,1,0:T(8,128)S(1)}) custom-call(bf16[144,1024]{1,0:T(8,128)(2,1)S(1)} %copy-done.1, bf16[144,1024]{1,0:T(8,128)(2,1)S(1)} %collective-permute-done.1.refs_1_, bf16[144,1024]{1,0:T(8,128)(2,1)S(1)} %collective-permute-done.2.refs_2_, bf16[144,1024]{1,0:T(8,128)(2,1)S(1)} %collective-permute-done.3.refs_3_, ...), custom_call_target="tpu_custom_call" | custom-call | bytes 4194304 | tf_op jit(solution)/shard_map/collect/pallas_call | solution.py:63
  50.8 1.3 %project_rims.1 = (bf16[16,2,32,384]{3,2,1,0:T(8,128)(2,1)S(1)}, bf16[128,256]{1,0:T(8,128)(2,1)S(1)}) custom-call(bf16[1024,1024]{1,0:T(8,128)(2,1)} %get-tuple-element.45.normed_any.normed_ref, bf16[16,32,384]{2,1,0:T(8,128)(2,1)S(1)} %all-to-all-done.refs_0_, bf16[16,32,384]{2,1,0:T(8,128)(2,1)S(1)} %collective-permute-done.8.refs_1_), custom_call_target="tpu_custom_call" | custom-call | flops 67108864 | bytes 1048576 | tf_op jit(solution)/shard_map/project_rims/pallas_call | solution.py:63
  52.2 0.2 collective-permute-start.13
  52.4 2.8 %project.1 = (bf16[1024,128]{1,0:T(8,128)(2,1)S(1)}, bf16[1024,256]{1,0:T(8,128)(2,1)S(1)}) custom-call(bf16[1024,1024]{1,0:T(8,128)(2,1)} %get-tuple-element.45.normed_any.normed_ref, bf16[16,2,32,384]{3,2,1,0:T(8,128)(2,1)S(1)} %get-tuple-element.48.w_ref), custom_call_target="tpu_custom_call" | custom-call | flops 805306368 | bytes 4194304 | tf_op jit(solution)/shard_map/project/pallas_call | solution.py:63
  55.2 1.9 %attention_interior.1.done_ref = bf16[1024,128]{1,0:T(8,128)(2,1)S(1)} custom-call(f32[8,16,128]{2,1,0:T(8,128)S(1)} %get-tuple-element.46.steps_ref, bf16[1024,128]{1,0:T(8,128)(2,1)S(1)} %get-tuple-element.49.q_ref, bf16[1024,256]{1,0:T(8,128)(2,1)S(1)} %get-tuple-element.54.kv_ref), custom_call_target="tpu_custom_call" | custom-call | flops 268435456 | bytes 2097152 | tf_op jit(solution)/shard_map/attention_interior/pallas_call | solution.py:63
  57.1 3.2 %collective-permute-done.13.low_ref.high_ref = bf16[128,256]{1,0:T(8,128)(2,1)S(1)} collective-permute-done((bf16[128,256]{1,0:T(8,128)(2,1)S(1)}, bf16[128,256]{1,0:T(8,128)(2,1)S(1)}, u32[]{:S(2)}, u32[]{:S(2)}) %collective-permute-start.13) | collective-permute-done | bytes 65568 | tf_op jit(solution)/shard_map/ppermute | solution.py:469
  60.3 1.4 %attention_edges.1 = bf16[1024,128]{1,0:T(8,128)(2,1)} custom-call(f32[8,16,128]{2,1,0:T(8,128)S(1)} %get-tuple-element.46.steps_ref, bf16[1024,128]{1,0:T(8,128)(2,1)S(1)} %get-tuple-element.49.q_ref, bf16[1024,256]{1,0:T(8,128)(2,1)S(1)} %get-tuple-element.54.kv_ref, bf16[128,256]{1,0:T(8,128)(2,1)S(1)} %collective-permute-done.13.low_ref.high_ref, ...), custom_call_target="tpu_custom_call" | custom-call | flops 67108864 | bytes 1048576 | tf_op jit(solution)/shard_map/attention_edges/pallas_call | solution.py:63
  61.8 6.4 %all-to-all-start.1 = ((bf16[16,64,128]{2,1,0:T(8,128)(2,1)}), bf16[16,64,128]{2,1,0:T(8,128)(2,1)S(1)}, u32[]{:S(2)}, u32[]{:S(2)}) async-start(bf16[16,64,128]{2,1,0:T(8,128)(2,1)} %bitcast.3), calls=%async_computation.1 | async-start | bytes 524288 | tf_op jit(solution)/shard_map/all_to_all | solution.py:465
  68.3 0.4 collective-permute-start.15
  68.9 0.4 collective-permute-start.17
  69.3 0.6 collective-permute-done.14.refs_4_
  69.8 0.4 collective-permute-done.15.refs_5_
  70.2 0.4 collective-permute-done.16.refs_6_
  70.7 0.4 collective-permute-done.17.refs_7_
  71.1 1.5 %assemble.1.w_any = bf16[2,4,2,64,1152]{4,3,2,1,0:T(8,128)(2,1)} custom-call(bf16[2,64,1152]{2,1,0:T(8,128)(2,1)S(1)} %bitcast.17, bf16[2,64,1152]{2,1,0:T(8,128)(2,1)S(1)} %collective-permute-done.10.refs_1_, bf16[2,64,1152]{2,1,0:T(8,128)(2,1)S(1)} %collective-permute-done.11.refs_2_, bf16[2,64,1152]{2,1,0:T(8,128)(2,1)S(1)} %collective-permute-done.12.refs_3_, ...), custom_call_target="tpu_custom_call" | custom-call | bytes 4194304 | tf_op jit(solution)/shard_map/assemble/pallas_call | solution.py:63
  72.6 2.4 %all-to-all-done.1.att_ref = bf16[16,64,128]{2,1,0:T(8,128)(2,1)S(1)} async-done(((bf16[16,64,128]{2,1,0:T(8,128)(2,1)}), bf16[16,64,128]{2,1,0:T(8,128)(2,1)S(1)}, u32[]{:S(2)}, u32[]{:S(2)}) %all-to-all-start.1) | async-done | bytes 262176 | tf_op jit(solution)/shard_map/all_to_all | solution.py:465
  75.0 3.7 %mix_loss_backward.1 = (f32[100,128]{1,0:T(8,128)S(1)}, bf16[16,64,128]{2,1,0:T(8,128)(2,1)S(1)}) custom-call(bf16[16,64,128]{2,1,0:T(8,128)(2,1)S(1)} %all-to-all-done.1.att_ref, f32[1,128]{1,0:T(1,128)S(1)} %bitcast.18, f32[100,128]{1,0:T(8,128)} %truth_any.1, bf16[2,4,2,64,1152]{4,3,2,1,0:T(8,128)(2,1)} %assemble.1.w_any, ...), custom_call_target="tpu_custom_call" | custom-call | flops 603979776 | bytes 4194304 | tf_op jit(solution)/shard_map/mix_loss_backward/pallas_call | solution.py:63
  78.7 9.9 %all_to_all.20 = bf16[16,64,128]{2,1,0:T(8,128)(2,1)S(1)} all-to-all(bf16[16,64,128]{2,1,0:T(8,128)(2,1)S(1)} %get-tuple-element.62), channel_id=1, replica_groups=mesh['half'=2,'quad'=4,'core'=2,'ens'=2] {'quad','core','ens'}, dimensions={0} | all-to-all | bytes 524288 | tf_op jit(solution)/shard_map/all_to_all | solution.py:465
  88.6 1.4 %attention_edges_back.1 = (f32[2,256,256]{2,1,0:T(8,128)S(1)}, bf16[128,256]{1,0:T(8,128)(2,1)S(1)}) custom-call(f32[8,16,128]{2,1,0:T(8,128)S(1)} %get-tuple-element.46.steps_ref, bf16[1024,128]{1,0:T(8,128)(2,1)S(1)} %get-tuple-element.49.q_ref, bf16[1024,256]{1,0:T(8,128)(2,1)S(1)} %get-tuple-element.54.kv_ref, ...), custom_call_target="tpu_custom_call" | custom-call | flops 167772160 | bytes 1048576 | tf_op jit(solution)/shard_map/attention_edges_back/pallas_call | solution.py:63
  90.0 1.4 %collective-permute-start.18 = (bf16[128,256]{1,0:T(8,128)(2,1)S(1)}, bf16[128,256]{1,0:T(8,128)(2,1)S(1)}, u32[]{:S(2)}, u32[]{:S(2)}) collective-permute-start(bf16[128,256]{1,0:T(8,128)(2,1)S(1)} %get-tuple-element.63), channel_id=1, source_target_pairs={{0,16},{16,0},{1,17},{17,1},{2,18},{18,2},{3,19},{19,3},{4,20},{20... | collective-permute-start | bytes 196616 | tf_op jit(solution)/shard_map/ppermute | solution.py:469
  91.4 3.8 %attention_interior_back.1.grads_ref = f32[1024,256]{1,0:T(8,128)S(1)} custom-call(f32[8,16,128]{2,1,0:T(8,128)S(1)} %get-tuple-element.46.steps_ref, bf16[1024,128]{1,0:T(8,128)(2,1)S(1)} %get-tuple-element.49.q_ref, bf16[1024,256]{1,0:T(8,128)(2,1)S(1)} %get-tuple-element.54.kv_ref, bf16[1024,128]{1,0:T(8,128)(2,1)S(1)} %bitcast.11, ...), custom_call_target="tpu_custom_call" | custom-call | flops 536870912 | bytes 4194304 | tf_op jit(solution)/shard_map/attention_interior_back/pallas_call | solution.py:63
  95.2 1.0 collective-permute-done.18.from_low_ref.from_high_ref
  96.3 2.1 %product.1 = bf16[1024,256]{1,0:T(8,128)(2,1)} custom-call(bf16[1024,1024]{1,0:T(8,128)(2,1)S(1)} %copy-done, bf16[128,256]{1,0:T(8,128)(2,1)S(1)} %collective-permute-done.18.from_low_ref.from_high_ref, bf16[128,256]{1,0:T(8,128)(2,1)S(1)} %collective-permute-done.18.from_low_ref.from_high_ref, f32[1024,256]{1,0:T(8,128)S(1)} %attention_interior_back.1.grads_ref), custom_call_target="tpu_custom_call" | custom-call | flops 1073741824 | bytes 4194304 | tf_op jit(solution)/shard_map/product/pallas_call | solution.py:63
  98.4 2.9 %all-to-all-start.3 = ((bf16[32,32,256]{2,1,0:T(8,128)(2,1)}), bf16[32,32,256]{2,1,0:T(8,128)(2,1)S(1)}, u32[]{:S(2)}, u32[]{:S(2)}) async-start(bf16[32,32,256]{2,1,0:T(8,128)(2,1)} %bitcast.7), calls=%async_computation.3 | async-start | bytes 1048576 | tf_op jit(solution)/shard_map/all_to_all | solution.py:465
  101.3 1.5 %collective-permute-start.19 = (f32[100,128]{1,0:T(8,128)S(1)}, f32[100,128]{1,0:T(8,128)S(1)}, u32[]{:S(2)}, u32[]{:S(2)}) collective-permute-start(f32[100,128]{1,0:T(8,128)S(1)} %get-tuple-element.66), channel_id=1, source_target_pairs={{0,1},{1,0},{2,3},{3,2},{4,5},{5,4},{6,7},{7,6},{8,9},{9,8},{10,11... | collective-permute-start | bytes 153608 | tf_op jit(solution)/shard_map/ppermute | solution.py:469
  102.7 4.5 %collective-permute-done.19 = f32[100,128]{1,0:T(8,128)S(1)} collective-permute-done((f32[100,128]{1,0:T(8,128)S(1)}, f32[100,128]{1,0:T(8,128)S(1)}, u32[]{:S(2)}, u32[]{:S(2)}) %collective-permute-start.19) | collective-permute-done | bytes 51232 | tf_op jit(solution)/shard_map/ppermute | solution.py:469
  107.5 0.7 copy.9
  108.1 9.0 %all-to-all-done.3 = bf16[32,32,256]{2,1,0:T(8,128)(2,1)S(1)} async-done(((bf16[32,32,256]{2,1,0:T(8,128)(2,1)}), bf16[32,32,256]{2,1,0:T(8,128)(2,1)S(1)}, u32[]{:S(2)}, u32[]{:S(2)}) %all-to-all-start.3) | async-done | bytes 524320 | tf_op jit(solution)/shard_map/all_to_all | solution.py:465
  117.1 0.8 gather_sums.1
  (31 shorter events, 0.6 us)
Async XLA Ops:
  2.5 25.3 %all-to-all-start = ((bf16[16,32,384]{2,1,0:T(8,128)(2,1)}), bf16[16,32,384]{2,1,0:T(8,128)(2,1)S(1)}, u32[]{:S(2)}, u32[]{:S(2)}) async-start(bf16[16,32,384]{2,1,0:T(8,128)(2,1)} %bitcast.21), calls=%async_computation | async-start | bytes 786432 | tf_op jit(solution)/shard_map/all_to_all | solution.py:465
  9.9 14.8 %collective-permute-start = (bf16[32,1152]{1,0:T(8,128)(2,1)}, bf16[32,1152]{1,0:T(8,128)(2,1)S(1)}, u32[]{:S(2)}, u32[]{:S(2)}) collective-permute-start(bf16[32,1152]{1,0:T(8,128)(2,1)} %get-tuple-element.35.mine_ref), channel_id=1, source_target_pairs={{0,16},{16,0},{1,17},{17,1},{2,18},{18,2},{3,19},{19,3},{4,20},{20... | collective-permute-start | bytes 221192 | tf_op jit(solution)/shard_map/ppermute | solution.py:469
  24.7 0.9 copy-start.3
  25.6 0.9 copy-start.4
  26.5 14.2 %collective-permute-start.1 = (bf16[144,1024]{1,0:T(8,128)(2,1)}, bf16[144,1024]{1,0:T(8,128)(2,1)S(1)}, u32[]{:S(2)}, u32[]{:S(2)}) collective-permute-start(bf16[144,1024]{1,0:T(8,128)(2,1)} %get-tuple-element.41.refs_0_), channel_id=1, source_target_pairs={{0,4},{4,0},{8,12},{12,8},{1,5},{5,1},{9,13},{13,9},{2,6},{6,2},{1... | collective-permute-start | bytes 884744 | tf_op jit(solution)/shard_map/ppermute | solution.py:469
  27.8 13.0 %collective-permute-start.3 = (bf16[144,1024]{1,0:T(8,128)(2,1)}, bf16[144,1024]{1,0:T(8,128)(2,1)S(1)}, u32[]{:S(2)}, u32[]{:S(2)}) collective-permute-start(bf16[144,1024]{1,0:T(8,128)(2,1)} %get-tuple-element.41.refs_0_), channel_id=1, source_target_pairs={{0,12},{4,8},{8,4},{12,0},{1,13},{5,9},{9,5},{13,1},{2,14},{6,10},... | collective-permute-start | bytes 884744 | tf_op jit(solution)/shard_map/ppermute | solution.py:469
  27.8 14.0 %collective-permute-start.2 = (bf16[144,1024]{1,0:T(8,128)(2,1)}, bf16[144,1024]{1,0:T(8,128)(2,1)S(1)}, u32[]{:S(2)}, u32[]{:S(2)}) collective-permute-start(bf16[144,1024]{1,0:T(8,128)(2,1)} %get-tuple-element.41.refs_0_), channel_id=1, source_target_pairs={{0,8},{4,12},{8,0},{12,4},{1,9},{5,13},{9,1},{13,5},{2,10},{6,14},... | collective-permute-start | bytes 884744 | tf_op jit(solution)/shard_map/ppermute | solution.py:469
  29.3 15.0 %collective-permute-start.9 = (bf16[2,32,2176]{2,1,0:T(8,128)(2,1)S(1)}, bf16[2,32,2176]{2,1,0:T(8,128)(2,1)S(1)}, u32[]{:S(2)}, u32[]{:S(2)}) collective-permute-start(bf16[2,32,2176]{2,1,0:T(8,128)(2,1)S(1)} %merge_halves.1.mine_ref), channel_id=1, source_target_pairs={{0,1},{1,0},{2,3},{3,2},{4,5},{5,4},{6,7},{7,6},{8,9},{9,8},{10,11... | collective-permute-start | bytes 835592 | tf_op jit(solution)/shard_map/ppermute | solution.py:469
  30.5 20.4 %collective-permute-start.8 = (bf16[16,32,384]{2,1,0:T(8,128)(2,1)S(1)}, bf16[16,32,384]{2,1,0:T(8,128)(2,1)S(1)}, u32[]{:S(2)}, u32[]{:S(2)}) collective-permute-start(bf16[16,32,384]{2,1,0:T(8,128)(2,1)S(1)} %all-to-all-done.refs_0_), channel_id=1, source_target_pairs={{0,1},{1,0},{2,3},{3,2},{4,5},{5,4},{6,7},{7,6},{8,9},{9,8},{10,11... | collective-permute-start | bytes 1179656 | tf_op jit(solution)/shard_map/ppermute | solution.py:469
  41.8 3.6 %collective-permute-start.6 = (bf16[144,1024]{1,0:T(8,128)(2,1)S(1)}, bf16[144,1024]{1,0:T(8,128)(2,1)S(1)}, u32[]{:S(2)}, u32[]{:S(2)}) collective-permute-start(bf16[144,1024]{1,0:T(8,128)(2,1)S(1)} %collective-permute-done.2.refs_2_), channel_id=1, source_target_pairs={{0,2},{2,0},{1,3},{3,1},{4,6},{6,4},{5,7},{7,5},{8,10},{10,8},{9,1... | collective-permute-start | bytes 884744 | tf_op jit(solution)/shard_map/ppermute | solution.py:469
  43.8 2.8 %collective-permute-start.4 = (bf16[144,1024]{1,0:T(8,128)(2,1)}, bf16[144,1024]{1,0:T(8,128)(2,1)S(1)}, u32[]{:S(2)}, u32[]{:S(2)}) collective-permute-start(bf16[144,1024]{1,0:T(8,128)(2,1)} %get-tuple-element.41.refs_0_), channel_id=1, source_target_pairs={{0,2},{2,0},{1,3},{3,1},{4,6},{6,4},{5,7},{7,5},{8,10},{10,8},{9,1... | collective-permute-start | bytes 884744 | tf_op jit(solution)/shard_map/ppermute | solution.py:469
  43.8 2.8 %collective-permute-start.5 = (bf16[144,1024]{1,0:T(8,128)(2,1)S(1)}, bf16[144,1024]{1,0:T(8,128)(2,1)S(1)}, u32[]{:S(2)}, u32[]{:S(2)}) collective-permute-start(bf16[144,1024]{1,0:T(8,128)(2,1)S(1)} %collective-permute-done.1.refs_1_), channel_id=1, source_target_pairs={{0,2},{2,0},{1,3},{3,1},{4,6},{6,4},{5,7},{7,5},{8,10},{10,8},{9,1... | collective-permute-start | bytes 884744 | tf_op jit(solution)/shard_map/ppermute | solution.py:469
  44.3 4.0 %collective-permute-start.7 = (bf16[144,1024]{1,0:T(8,128)(2,1)S(1)}, bf16[144,1024]{1,0:T(8,128)(2,1)S(1)}, u32[]{:S(2)}, u32[]{:S(2)}) collective-permute-start(bf16[144,1024]{1,0:T(8,128)(2,1)S(1)} %collective-permute-done.3.refs_3_), channel_id=1, source_target_pairs={{0,2},{2,0},{1,3},{3,1},{4,6},{6,4},{5,7},{7,5},{8,10},{10,8},{9,1... | collective-permute-start | bytes 884744 | tf_op jit(solution)/shard_map/ppermute | solution.py:469
  45.4 22.8 %collective-permute-start.10 = (bf16[2,64,1152]{2,1,0:T(8,128)(2,1)S(1)}, bf16[2,64,1152]{2,1,0:T(8,128)(2,1)S(1)}, u32[]{:S(2)}, u32[]{:S(2)}) collective-permute-start(bf16[2,64,1152]{2,1,0:T(8,128)(2,1)S(1)} %bitcast.13), channel_id=1, source_target_pairs={{0,4},{4,0},{8,12},{12,8},{1,5},{5,1},{9,13},{13,9},{2,6},{6,2},{1... | collective-permute-start | bytes 884744 | tf_op jit(solution)/shard_map/ppermute | solution.py:469
  46.6 21.6 %collective-permute-start.11 = (bf16[2,64,1152]{2,1,0:T(8,128)(2,1)S(1)}, bf16[2,64,1152]{2,1,0:T(8,128)(2,1)S(1)}, u32[]{:S(2)}, u32[]{:S(2)}) collective-permute-start(bf16[2,64,1152]{2,1,0:T(8,128)(2,1)S(1)} %bitcast.14), channel_id=1, source_target_pairs={{0,8},{4,12},{8,0},{12,4},{1,9},{5,13},{9,1},{13,5},{2,10},{6,14},... | collective-permute-start | bytes 884744 | tf_op jit(solution)/shard_map/ppermute | solution.py:469
  46.6 21.6 %collective-permute-start.12 = (bf16[2,64,1152]{2,1,0:T(8,128)(2,1)S(1)}, bf16[2,64,1152]{2,1,0:T(8,128)(2,1)S(1)}, u32[]{:S(2)}, u32[]{:S(2)}) collective-permute-start(bf16[2,64,1152]{2,1,0:T(8,128)(2,1)S(1)} %bitcast.15), channel_id=1, source_target_pairs={{0,12},{4,8},{8,4},{12,0},{1,13},{5,9},{9,5},{13,1},{2,14},{6,10},... | collective-permute-start | bytes 884744 | tf_op jit(solution)/shard_map/ppermute | solution.py:469
  48.3 1.0 copy-start.1
  52.2 8.2 %collective-permute-start.13 = (bf16[128,256]{1,0:T(8,128)(2,1)S(1)}, bf16[128,256]{1,0:T(8,128)(2,1)S(1)}, u32[]{:S(2)}, u32[]{:S(2)}) collective-permute-start(bf16[128,256]{1,0:T(8,128)(2,1)S(1)} %get-tuple-element.55), channel_id=1, source_target_pairs={{0,16},{16,0},{1,17},{17,1},{2,18},{18,2},{3,19},{19,3},{4,20},{20... | collective-permute-start | bytes 196616 | tf_op jit(solution)/shard_map/ppermute | solution.py:469
  61.8 13.2 %all-to-all-start.1 = ((bf16[16,64,128]{2,1,0:T(8,128)(2,1)}), bf16[16,64,128]{2,1,0:T(8,128)(2,1)S(1)}, u32[]{:S(2)}, u32[]{:S(2)}) async-start(bf16[16,64,128]{2,1,0:T(8,128)(2,1)} %bitcast.3), calls=%async_computation.1 | async-start | bytes 524288 | tf_op jit(solution)/shard_map/all_to_all | solution.py:465
  68.1 6.9 %copy-start.2 = (bf16[1,64,1024]{2,1,0:T(8,128)(2,1)S(1)}, bf16[1,64,1024]{2,1,0:T(8,128)(2,1)}, u32[]{:S(2)}) copy-start(bf16[1,64,1024]{2,1,0:T(8,128)(2,1)} %get-tuple-element.60.refs_0_) | copy-start | bytes 393220
  68.1 6.9 %copy-start.5 = (f32[128]{0:T(128)S(1)}, f32[128]{0:T(128)}, u32[]{:S(2)}) copy-start(f32[128]{0:T(128)} %param.12) | copy-start | bytes 1540
  68.2 1.6 %collective-permute-start.14 = (bf16[2,64,1152]{2,1,0:T(8,128)(2,1)S(1)}, bf16[2,64,1152]{2,1,0:T(8,128)(2,1)S(1)}, u32[]{:S(2)}, u32[]{:S(2)}) collective-permute-start(bf16[2,64,1152]{2,1,0:T(8,128)(2,1)S(1)} %bitcast.16), channel_id=1, source_target_pairs={{0,2},{2,0},{1,3},{3,1},{4,6},{6,4},{5,7},{7,5},{8,10},{10,8},{9,1... | collective-permute-start | bytes 884744 | tf_op jit(solution)/shard_map/ppermute | solution.py:469
  68.3 1.9 %collective-permute-start.15 = (bf16[2,64,1152]{2,1,0:T(8,128)(2,1)S(1)}, bf16[2,64,1152]{2,1,0:T(8,128)(2,1)S(1)}, u32[]{:S(2)}, u32[]{:S(2)}) collective-permute-start(bf16[2,64,1152]{2,1,0:T(8,128)(2,1)S(1)} %collective-permute-done.10.refs_1_), channel_id=1, source_target_pairs={{0,2},{2,0},{1,3},{3,1},{4,6},{6,4},{5,7},{7,5},{8,10},{10,8},{9,1... | collective-permute-start | bytes 884744 | tf_op jit(solution)/shard_map/ppermute | solution.py:469
  68.8 1.9 %collective-permute-start.16 = (bf16[2,64,1152]{2,1,0:T(8,128)(2,1)S(1)}, bf16[2,64,1152]{2,1,0:T(8,128)(2,1)S(1)}, u32[]{:S(2)}, u32[]{:S(2)}) collective-permute-start(bf16[2,64,1152]{2,1,0:T(8,128)(2,1)S(1)} %collective-permute-done.11.refs_2_), channel_id=1, source_target_pairs={{0,2},{2,0},{1,3},{3,1},{4,6},{6,4},{5,7},{7,5},{8,10},{10,8},{9,1... | collective-permute-start | bytes 884744 | tf_op jit(solution)/shard_map/ppermute | solution.py:469
  68.9 2.2 %collective-permute-start.17 = (bf16[2,64,1152]{2,1,0:T(8,128)(2,1)S(1)}, bf16[2,64,1152]{2,1,0:T(8,128)(2,1)S(1)}, u32[]{:S(2)}, u32[]{:S(2)}) collective-permute-start(bf16[2,64,1152]{2,1,0:T(8,128)(2,1)S(1)} %collective-permute-done.12.refs_3_), channel_id=1, source_target_pairs={{0,2},{2,0},{1,3},{3,1},{4,6},{6,4},{5,7},{7,5},{8,10},{10,8},{9,1... | collective-permute-start | bytes 884744 | tf_op jit(solution)/shard_map/ppermute | solution.py:469
  78.7 17.6 %copy-start = (bf16[1024,1024]{1,0:T(8,128)(2,1)S(1)}, bf16[1024,1024]{1,0:T(8,128)(2,1)}, u32[]{:S(2)}) copy-start(bf16[1024,1024]{1,0:T(8,128)(2,1)} %get-tuple-element.45.normed_any.normed_ref) | copy-start | bytes 6291460
  90.0 6.3 %collective-permute-start.18 = (bf16[128,256]{1,0:T(8,128)(2,1)S(1)}, bf16[128,256]{1,0:T(8,128)(2,1)S(1)}, u32[]{:S(2)}, u32[]{:S(2)}) collective-permute-start(bf16[128,256]{1,0:T(8,128)(2,1)S(1)} %get-tuple-element.63), channel_id=1, source_target_pairs={{0,16},{16,0},{1,17},{17,1},{2,18},{18,2},{3,19},{19,3},{4,20},{20... | collective-permute-start | bytes 196616 | tf_op jit(solution)/shard_map/ppermute | solution.py:469
  98.4 18.7 %all-to-all-start.3 = ((bf16[32,32,256]{2,1,0:T(8,128)(2,1)}), bf16[32,32,256]{2,1,0:T(8,128)(2,1)S(1)}, u32[]{:S(2)}, u32[]{:S(2)}) async-start(bf16[32,32,256]{2,1,0:T(8,128)(2,1)} %bitcast.7), calls=%async_computation.3 | async-start | bytes 1048576 | tf_op jit(solution)/shard_map/all_to_all | solution.py:465
  101.3 6.0 %collective-permute-start.19 = (f32[100,128]{1,0:T(8,128)S(1)}, f32[100,128]{1,0:T(8,128)S(1)}, u32[]{:S(2)}, u32[]{:S(2)}) collective-permute-start(f32[100,128]{1,0:T(8,128)S(1)} %get-tuple-element.66), channel_id=1, source_target_pairs={{0,1},{1,0},{2,3},{3,2},{4,5},{5,4},{6,7},{7,6},{8,9},{9,8},{10,11... | collective-permute-start | bytes 153608 | tf_op jit(solution)/shard_map/ppermute | solution.py:469

commit v23 on v18

--- a/solution.py
+++ b/solution.py
@@ -144,11 +144,9 @@
     wait(out + fetch([(normed, normed_any)], sems, 2 + len(out)))
 
 
-def merge_halves_kernel(mine_ref, other_ref, sent_ref, out_ref):
-    half = lax.axis_index("half")
-    width = mine_ref.shape[1]
-    out_ref[half, :, :width] = mine_ref[...]
-    out_ref[half ^ 1, :, :width] = other_ref[...]
+def attach_kernel(packed_ref, sent_ref, out_ref):
+    width = packed_ref.shape[2]
+    out_ref[:, :, :width] = packed_ref[...]
     out_ref[:, :, width:] = sent_ref[...].reshape(2, -1, LATENT_DIM)
 
 
@@ -513,18 +511,7 @@
         results="h" + "h" * source_parts,
     )(neighbours, members.reshape(node_rows, LATENT_DIM))
 
-    square = paired and halves == 2 and shard % 16 == 0
-    if square:
-        (packed,) = call(
-            merge_halves_kernel,
-            "merge_halves",
-            [((2, shard, width + LATENT_DIM), BF16)],
-            "vvv",
-            moved=2**18,
-        )(packed, swap(packed, "half", 1), sources[1])
-    else:
-        packed = in_order(packed, "half", 0)
-    packed, normed = lax.optimization_barrier((packed, normed))
+    packed, normed = lax.optimization_barrier((in_order(packed, "half", 0), normed))
     near = [normed, swap(normed, "quad", 1), None, swap(normed, "quad", 3)]
     if paired:
         columns = exchange(columns.reshape(-1, shard, 3 * COLS), nodes)
@@ -535,6 +522,7 @@
         columns = [columns[0].reshape(LATENT_DIM, 3 * COLS)]
         late = normed
     near[2] = swap(late, "quad", 2)
+    near = list(lax.optimization_barrier(tuple(near)))
     far = [swap(piece, "core", 1) for piece in near]
     normed, steps = call(
         collect_kernel,
@@ -546,14 +534,22 @@
         results="hv",
     )(*near, *far)
 
+    square = paired and halves == 2 and shard % 16 == 0
     if square:
+        (wide,) = call(
+            attach_kernel,
+            "attach_sources",
+            [((2, shard, width + LATENT_DIM), BF16)],
+            "vv",
+            moved=2**19,
+        )(packed, sources[1])
         packed, arrived = call(
             merge_members_kernel,
             "merge_members",
             [((2, 2, shard, width), BF16), ((1, part, LATENT_DIM), BF16)],
             "vv",
             moved=2**19,
-        )(packed, swap(packed, "ens", 1))
+        )(wide, swap(wide, "ens", 1))
         packed = packed.reshape(2, 2 * shard, width)
         sources = [sources[0], arrived]
     else:

time: 117 us -> 110 us (0.940)
  starting transfers between devices: 37.8 us -> 33.8 us
  waiting for transfers between devices: 38.2 us -> 34.9 us
    ppermute x20, waiting for transfers between devices: 26.9 us -> 17.4 us  [swap(): lax.ppermute(value, axis, [(i, i ^ step) for i in range(lax.axis_size(axi...]
    all_to_all x3, waiting for transfers between devices: 11.4 us -> 17.5 us  [exchange(): return lax.all_to_all(chunks, axes, 0, 0)]
    ppermute x20, starting transfers between devices: 21.5 us -> 18.1 us  [swap(): lax.ppermute(value, axis, [(i, i ^ step) for i in range(lax.axis_size(axi...]
    unnamed x13 -> x11, local copies, waits for them, and re-layouts: 3.44 us -> 2.55 us
  transfers between devices with their start and end apart: 23 -> 23, of which waited for: 12 -> 14; matrix products, arithmetic and copies ran while one was open for 1% -> 2% of each run, Pallas kernels for 14% -> 15%
where the time goes in v23:
time: 110 us; the launch traced here: 109 us
  waiting for transfers between devices  34.9 us (32%)
  starting transfers between devices  33.8 us (31%)
  Pallas kernels  26 us (24%)
  blocking collectives  9.88 us (9%)
  local copies, waits for them, and re-layouts  2.63 us (2%)
    pallas_call x15, Pallas kernels, run(): made(*[pltpu.with_memory_space_constraint(arg, pltpu.HBM) if space == 'h'...  26 us
    ppermute x20, starting transfers between devices, swap(): lax.ppermute(value, axis, [(i, i ^ step) for i in range(lax.axis_size(axi...  18.1 us
    all_to_all x3, waiting for transfers between devices, exchange(): return lax.all_to_all(chunks, axes, 0, 0)  17.5 us
    ppermute x20, waiting for transfers between devices, swap(): lax.ppermute(value, axis, [(i, i ^ step) for i in range(lax.axis_size(axi...  17.4 us
    all_to_all x3, starting transfers between devices, exchange(): return lax.all_to_all(chunks, axes, 0, 0)  15.7 us
    all_to_all x1, blocking collectives, exchange(): return lax.all_to_all(chunks, axes, 0, 0)  9.88 us
    unnamed x11, local copies, waits for them, and re-layouts  2.55 us
  transfers between devices with their start and end apart: 23, of which 14 were waited for; matrix products, arithmetic and copies ran while one was open for 2% of the time, Pallas kernels for 15%

profile of v23, /device:TPU:1, one launch (start us, length us, event | category | flops | bytes accessed | tf_op | source)
XLA Modules:
  0.0 109.0 jit_solution(5702760281522447006)
XLA Ops:
  0.6 1.8 %prepare_weights.1 = (bf16[2,8,1,32,384]{4,3,2,1,0:T(8,128)(2,1)}, bf16[32,1152]{1,0:T(8,128)(2,1)}) custom-call(bf16[32,3072]{1,0:T(8,128)(2,1)} %w_any.1, bf16[32,1024]{1,0:T(8,128)(2,1)} %mix_any.1, bf16[32,100]{1,0:T(8,128)(2,1)} %readout_any.1), custom_call_target="tpu_custom_call" | custom-call | bytes 1048576 | tf_op jit(solution)/shard_map/prepare_weights/pallas_call | solution.py:63
  2.4 3.2 %collective-permute-start = (bf16[32,1152]{1,0:T(8,128)(2,1)}, bf16[32,1152]{1,0:T(8,128)(2,1)S(1)}, u32[]{:S(2)}, u32[]{:S(2)}) collective-permute-start(bf16[32,1152]{1,0:T(8,128)(2,1)} %get-tuple-element.35), channel_id=1, source_target_pairs={{0,16},{16,0},{1,17},{17,1},{2,18},{18,2},{3,19},{19,3},{4,20},{20... | collective-permute-start | bytes 221192 | tf_op jit(solution)/shard_map/ppermute | solution.py:455
  5.6 4.8 %all-to-all-start = ((bf16[16,32,384]{2,1,0:T(8,128)(2,1)}), bf16[16,32,384]{2,1,0:T(8,128)(2,1)S(1)}, u32[]{:S(2)}, u32[]{:S(2)}) async-start(bf16[16,32,384]{2,1,0:T(8,128)(2,1)} %bitcast.23), calls=%async_computation | async-start | bytes 786432 | tf_op jit(solution)/shard_map/all_to_all | solution.py:451
  10.4 1.9 %norm.1 = (bf16[144,1024]{1,0:T(8,128)(2,1)}, bf16[1,64,1024]{2,1,0:T(8,128)(2,1)}, bf16[1,64,1024]{2,1,0:T(8,128)(2,1)}) custom-call(s32[2,4]{1,0:T(2,128)} %near_any.1, bf16[128,1024]{1,0:T(8,128)(2,1)} %bitcast.24), custom_call_target="tpu_custom_call" | custom-call | flops 1048576 | bytes 1048576 | tf_op jit(solution)/shard_map/norm/pallas_call | solution.py:63
  12.3 0.9 select_bitcast_fusion.1
  13.3 1.5 %collective-permute-start.1 = (bf16[144,1024]{1,0:T(8,128)(2,1)}, bf16[144,1024]{1,0:T(8,128)(2,1)S(1)}, u32[]{:S(2)}, u32[]{:S(2)}) collective-permute-start(bf16[144,1024]{1,0:T(8,128)(2,1)} %get-tuple-element.40.refs_0_), channel_id=1, source_target_pairs={{0,4},{4,0},{8,12},{12,8},{1,5},{5,1},{9,13},{13,9},{2,6},{6,2},{1... | collective-permute-start | bytes 884744 | tf_op jit(solution)/shard_map/ppermute | solution.py:455
  14.7 1.2 %collective-permute-start.3 = (bf16[144,1024]{1,0:T(8,128)(2,1)}, bf16[144,1024]{1,0:T(8,128)(2,1)S(1)}, u32[]{:S(2)}, u32[]{:S(2)}) collective-permute-start(bf16[144,1024]{1,0:T(8,128)(2,1)} %get-tuple-element.40.refs_0_), channel_id=1, source_target_pairs={{0,12},{4,8},{8,4},{12,0},{1,13},{5,9},{9,5},{13,1},{2,14},{6,10},... | collective-permute-start | bytes 884744 | tf_op jit(solution)/shard_map/ppermute | solution.py:455
  15.9 6.0 %all-to-all-done.refs_0_ = bf16[16,32,384]{2,1,0:T(8,128)(2,1)S(1)} async-done(((bf16[16,32,384]{2,1,0:T(8,128)(2,1)}), bf16[16,32,384]{2,1,0:T(8,128)(2,1)S(1)}, u32[]{:S(2)}, u32[]{:S(2)}) %all-to-all-start) | async-done | bytes 393248 | tf_op jit(solution)/shard_map/all_to_all | solution.py:451
  21.9 1.7 %collective-permute-start.2 = (bf16[144,1024]{1,0:T(8,128)(2,1)}, bf16[144,1024]{1,0:T(8,128)(2,1)S(1)}, u32[]{:S(2)}, u32[]{:S(2)}) collective-permute-start(bf16[144,1024]{1,0:T(8,128)(2,1)} %get-tuple-element.40.refs_0_), channel_id=1, source_target_pairs={{0,8},{4,12},{8,0},{12,4},{1,9},{5,13},{9,1},{13,5},{2,10},{6,14},... | collective-permute-start | bytes 884744 | tf_op jit(solution)/shard_map/ppermute | solution.py:455
  23.6 0.9 copy-done.3
  24.5 1.3 %collective-permute-start.9 = (bf16[2,32,2176]{2,1,0:T(8,128)(2,1)S(1)}, bf16[2,32,2176]{2,1,0:T(8,128)(2,1)S(1)}, u32[]{:S(2)}, u32[]{:S(2)}) collective-permute-start(bf16[2,32,2176]{2,1,0:T(8,128)(2,1)S(1)} %attach_sources.1.mine_ref), channel_id=1, source_target_pairs={{0,1},{1,0},{2,3},{3,2},{4,5},{5,4},{6,7},{7,6},{8,9},{9,8},{10,11... | collective-permute-start | bytes 835592 | tf_op jit(solution)/shard_map/ppermute | solution.py:455
  26.1 4.2 %collective-permute-done.1.refs_1_ = bf16[144,1024]{1,0:T(8,128)(2,1)S(1)} collective-permute-done((bf16[144,1024]{1,0:T(8,128)(2,1)}, bf16[144,1024]{1,0:T(8,128)(2,1)S(1)}, u32[]{:S(2)}, u32[]{:S(2)}) %collective-permute-start.1) | collective-permute-done | bytes 294944 | tf_op jit(solution)/shard_map/ppermute | solution.py:455
  30.3 1.4 %collective-permute-done.2.refs_2_ = bf16[144,1024]{1,0:T(8,128)(2,1)S(1)} collective-permute-done((bf16[144,1024]{1,0:T(8,128)(2,1)}, bf16[144,1024]{1,0:T(8,128)(2,1)S(1)}, u32[]{:S(2)}, u32[]{:S(2)}) %collective-permute-start.2) | collective-permute-done | bytes 294944 | tf_op jit(solution)/shard_map/ppermute | solution.py:455
  31.7 1.0 collective-permute-start.6
  32.7 0.5 collective-permute-start.5
  33.2 0.7 collective-permute-start.7
  34.3 1.6 %collective-permute-start.10 = (bf16[2,64,1152]{2,1,0:T(8,128)(2,1)S(1)}, bf16[2,64,1152]{2,1,0:T(8,128)(2,1)S(1)}, u32[]{:S(2)}, u32[]{:S(2)}) collective-permute-start(bf16[2,64,1152]{2,1,0:T(8,128)(2,1)S(1)} %bitcast.17), channel_id=1, source_target_pairs={{0,4},{4,0},{8,12},{12,8},{1,5},{5,1},{9,13},{13,9},{2,6},{6,2},{1... | collective-permute-start | bytes 884744 | tf_op jit(solution)/shard_map/ppermute | solution.py:455
  35.9 0.5 collective-permute-start.11
  36.3 1.3 %collective-permute-start.12 = (bf16[2,64,1152]{2,1,0:T(8,128)(2,1)S(1)}, bf16[2,64,1152]{2,1,0:T(8,128)(2,1)S(1)}, u32[]{:S(2)}, u32[]{:S(2)}) collective-permute-start(bf16[2,64,1152]{2,1,0:T(8,128)(2,1)S(1)} %bitcast.19), channel_id=1, source_target_pairs={{0,12},{4,8},{8,4},{12,0},{1,13},{5,9},{9,5},{13,1},{2,14},{6,10},... | collective-permute-start | bytes 884744 | tf_op jit(solution)/shard_map/ppermute | solution.py:455
  37.6 1.0 copy-done.1
  38.6 1.5 %collect.1 = (bf16[1024,1024]{1,0:T(8,128)(2,1)}, f32[8,16,128]{2,1,0:T(8,128)S(1)}) custom-call(bf16[144,1024]{1,0:T(8,128)(2,1)S(1)} %copy-done.1, bf16[144,1024]{1,0:T(8,128)(2,1)S(1)} %collective-permute-done.1.refs_1_, bf16[144,1024]{1,0:T(8,128)(2,1)S(1)} %collective-permute-done.2.refs_2_, bf16[144,1024]{1,0:T(8,128)(2,1)S(1)} %collective-permute-done.3.refs_3_, ...), custom_call_target="tpu_custom_call" | custom-call | bytes 4194304 | tf_op jit(solution)/shard_map/collect/pallas_call | solution.py:63
  40.1 1.3 %collective-permute-done.8.refs_1_ = bf16[16,32,384]{2,1,0:T(8,128)(2,1)S(1)} collective-permute-done((bf16[16,32,384]{2,1,0:T(8,128)(2,1)S(1)}, bf16[16,32,384]{2,1,0:T(8,128)(2,1)S(1)}, u32[]{:S(2)}, u32[]{:S(2)}) %collective-permute-start.8) | collective-permute-done | bytes 393248 | tf_op jit(solution)/shard_map/ppermute | solution.py:455
  41.4 1.3 %project_rims.1 = (bf16[16,2,32,384]{3,2,1,0:T(8,128)(2,1)S(1)}, bf16[128,256]{1,0:T(8,128)(2,1)S(1)}) custom-call(bf16[1024,1024]{1,0:T(8,128)(2,1)} %get-tuple-element.44.normed_any.normed_ref, bf16[16,32,384]{2,1,0:T(8,128)(2,1)S(1)} %all-to-all-done.refs_0_, bf16[16,32,384]{2,1,0:T(8,128)(2,1)S(1)} %collective-permute-done.8.refs_1_), custom_call_target="tpu_custom_call" | custom-call | flops 67108864 | bytes 1048576 | tf_op jit(solution)/shard_map/project_rims/pallas_call | solution.py:63
  42.7 0.9 collective-permute-start.13
  43.6 2.8 %project.1 = (bf16[1024,128]{1,0:T(8,128)(2,1)S(1)}, bf16[1024,256]{1,0:T(8,128)(2,1)S(1)}) custom-call(bf16[1024,1024]{1,0:T(8,128)(2,1)} %get-tuple-element.44.normed_any.normed_ref, bf16[16,2,32,384]{3,2,1,0:T(8,128)(2,1)S(1)} %get-tuple-element.47.w_ref), custom_call_target="tpu_custom_call" | custom-call | flops 805306368 | bytes 4194304 | tf_op jit(solution)/shard_map/project/pallas_call | solution.py:63
  46.4 1.9 %attention_interior.1.done_ref = bf16[1024,128]{1,0:T(8,128)(2,1)S(1)} custom-call(f32[8,16,128]{2,1,0:T(8,128)S(1)} %get-tuple-element.45.steps_ref, bf16[1024,128]{1,0:T(8,128)(2,1)S(1)} %get-tuple-element.48.q_ref, bf16[1024,256]{1,0:T(8,128)(2,1)S(1)} %get-tuple-element.54.kv_ref), custom_call_target="tpu_custom_call" | custom-call | flops 268435456 | bytes 2097152 | tf_op jit(solution)/shard_map/attention_interior/pallas_call | solution.py:63
  48.3 1.4 %collective-permute-done.13.low_ref.high_ref = bf16[128,256]{1,0:T(8,128)(2,1)S(1)} collective-permute-done((bf16[128,256]{1,0:T(8,128)(2,1)S(1)}, bf16[128,256]{1,0:T(8,128)(2,1)S(1)}, u32[]{:S(2)}, u32[]{:S(2)}) %collective-permute-start.13) | collective-permute-done | bytes 65568 | tf_op jit(solution)/shard_map/ppermute | solution.py:455
  49.8 1.4 %attention_edges.1 = bf16[1024,128]{1,0:T(8,128)(2,1)} custom-call(f32[8,16,128]{2,1,0:T(8,128)S(1)} %get-tuple-element.45.steps_ref, bf16[1024,128]{1,0:T(8,128)(2,1)S(1)} %get-tuple-element.48.q_ref, bf16[1024,256]{1,0:T(8,128)(2,1)S(1)} %get-tuple-element.54.kv_ref, bf16[128,256]{1,0:T(8,128)(2,1)S(1)} %collective-permute-done.13.low_ref.high_ref, ...), custom_call_target="tpu_custom_call" | custom-call | flops 67108864 | bytes 1048576 | tf_op jit(solution)/shard_map/attention_edges/pallas_call | solution.py:63
  51.2 8.1 %all-to-all-start.1 = ((bf16[16,64,128]{2,1,0:T(8,128)(2,1)}), bf16[16,64,128]{2,1,0:T(8,128)(2,1)S(1)}, u32[]{:S(2)}, u32[]{:S(2)}) async-start(bf16[16,64,128]{2,1,0:T(8,128)(2,1)} %bitcast.5), calls=%async_computation.1 | async-start | bytes 524288 | tf_op jit(solution)/shard_map/all_to_all | solution.py:451
  59.5 0.4 collective-permute-start.15
  60.4 0.6 collective-permute-done.14.refs_4_
  61.0 0.4 collective-permute-done.15.refs_5_
  61.4 0.4 collective-permute-done.16.refs_6_
  61.9 0.4 collective-permute-done.17.refs_7_
  62.3 1.5 %assemble.1.w_any = bf16[2,4,2,64,1152]{4,3,2,1,0:T(8,128)(2,1)} custom-call(bf16[2,64,1152]{2,1,0:T(8,128)(2,1)S(1)} %bitcast.21, bf16[2,64,1152]{2,1,0:T(8,128)(2,1)S(1)} %collective-permute-done.10.refs_1_, bf16[2,64,1152]{2,1,0:T(8,128)(2,1)S(1)} %collective-permute-done.11.refs_2_, bf16[2,64,1152]{2,1,0:T(8,128)(2,1)S(1)} %collective-permute-done.12.refs_3_, ...), custom_call_target="tpu_custom_call" | custom-call | bytes 4194304 | tf_op jit(solution)/shard_map/assemble/pallas_call | solution.py:63
  63.8 2.4 %all-to-all-done.1.att_ref = bf16[16,64,128]{2,1,0:T(8,128)(2,1)S(1)} async-done(((bf16[16,64,128]{2,1,0:T(8,128)(2,1)}), bf16[16,64,128]{2,1,0:T(8,128)(2,1)S(1)}, u32[]{:S(2)}, u32[]{:S(2)}) %all-to-all-start.1) | async-done | bytes 262176 | tf_op jit(solution)/shard_map/all_to_all | solution.py:451
  66.2 3.7 %mix_loss_backward.1 = (f32[100,128]{1,0:T(8,128)S(1)}, bf16[16,64,128]{2,1,0:T(8,128)(2,1)S(1)}) custom-call(bf16[16,64,128]{2,1,0:T(8,128)(2,1)S(1)} %all-to-all-done.1.att_ref, f32[1,128]{1,0:T(1,128)S(1)} %bitcast.22, f32[100,128]{1,0:T(8,128)} %truth_any.1, bf16[2,4,2,64,1152]{4,3,2,1,0:T(8,128)(2,1)} %assemble.1.w_any, ...), custom_call_target="tpu_custom_call" | custom-call | flops 603979776 | bytes 4194304 | tf_op jit(solution)/shard_map/mix_loss_backward/pallas_call | solution.py:63
  69.9 9.9 %all_to_all.20 = bf16[16,64,128]{2,1,0:T(8,128)(2,1)S(1)} all-to-all(bf16[16,64,128]{2,1,0:T(8,128)(2,1)S(1)} %get-tuple-element.62), channel_id=1, replica_groups=mesh['half'=2,'quad'=4,'core'=2,'ens'=2] {'quad','core','ens'}, dimensions={0} | all-to-all | bytes 524288 | tf_op jit(solution)/shard_map/all_to_all | solution.py:451
  79.8 1.4 %attention_edges_back.1 = (f32[2,256,256]{2,1,0:T(8,128)S(1)}, bf16[128,256]{1,0:T(8,128)(2,1)S(1)}) custom-call(f32[8,16,128]{2,1,0:T(8,128)S(1)} %get-tuple-element.45.steps_ref, bf16[1024,128]{1,0:T(8,128)(2,1)S(1)} %get-tuple-element.48.q_ref, bf16[1024,256]{1,0:T(8,128)(2,1)S(1)} %get-tuple-element.54.kv_ref, ...), custom_call_target="tpu_custom_call" | custom-call | flops 167772160 | bytes 1048576 | tf_op jit(solution)/shard_map/attention_edges_back/pallas_call | solution.py:63
  81.3 3.8 %attention_interior_back.1.grads_ref = f32[1024,256]{1,0:T(8,128)S(1)} custom-call(f32[8,16,128]{2,1,0:T(8,128)S(1)} %get-tuple-element.45.steps_ref, bf16[1024,128]{1,0:T(8,128)(2,1)S(1)} %get-tuple-element.48.q_ref, bf16[1024,256]{1,0:T(8,128)(2,1)S(1)} %get-tuple-element.54.kv_ref, bf16[1024,128]{1,0:T(8,128)(2,1)S(1)} %bitcast.15, ...), custom_call_target="tpu_custom_call" | custom-call | flops 536870912 | bytes 4194304 | tf_op jit(solution)/shard_map/attention_interior_back/pallas_call | solution.py:63
  85.1 2.3 %collective-permute-done.18.from_low_ref.from_high_ref = bf16[128,256]{1,0:T(8,128)(2,1)S(1)} collective-permute-done((bf16[128,256]{1,0:T(8,128)(2,1)S(1)}, bf16[128,256]{1,0:T(8,128)(2,1)S(1)}, u32[]{:S(2)}, u32[]{:S(2)}) %collective-permute-start.18) | collective-permute-done | bytes 65568 | tf_op jit(solution)/shard_map/ppermute | solution.py:455
  87.5 2.1 %product.1 = bf16[1024,256]{1,0:T(8,128)(2,1)} custom-call(bf16[1024,1024]{1,0:T(8,128)(2,1)S(1)} %copy-done, bf16[128,256]{1,0:T(8,128)(2,1)S(1)} %collective-permute-done.18.from_low_ref.from_high_ref, bf16[128,256]{1,0:T(8,128)(2,1)S(1)} %collective-permute-done.18.from_low_ref.from_high_ref, f32[1024,256]{1,0:T(8,128)S(1)} %attention_interior_back.1.grads_ref), custom_call_target="tpu_custom_call" | custom-call | flops 1073741824 | bytes 4194304 | tf_op jit(solution)/shard_map/product/pallas_call | solution.py:63
  89.5 2.8 %all-to-all-start.3 = ((bf16[32,32,256]{2,1,0:T(8,128)(2,1)}), bf16[32,32,256]{2,1,0:T(8,128)(2,1)S(1)}, u32[]{:S(2)}, u32[]{:S(2)}) async-start(bf16[32,32,256]{2,1,0:T(8,128)(2,1)} %bitcast.9), calls=%async_computation.3 | async-start | bytes 1048576 | tf_op jit(solution)/shard_map/all_to_all | solution.py:451
  92.3 1.5 %collective-permute-start.19 = (f32[100,128]{1,0:T(8,128)S(1)}, f32[100,128]{1,0:T(8,128)S(1)}, u32[]{:S(2)}, u32[]{:S(2)}) collective-permute-start(f32[100,128]{1,0:T(8,128)S(1)} %get-tuple-element.66), channel_id=1, source_target_pairs={{0,1},{1,0},{2,3},{3,2},{4,5},{5,4},{6,7},{7,6},{8,9},{9,8},{10,11... | collective-permute-start | bytes 153608 | tf_op jit(solution)/shard_map/ppermute | solution.py:455
  93.8 4.5 %collective-permute-done.19 = f32[100,128]{1,0:T(8,128)S(1)} collective-permute-done((f32[100,128]{1,0:T(8,128)S(1)}, f32[100,128]{1,0:T(8,128)S(1)}, u32[]{:S(2)}, u32[]{:S(2)}) %collective-permute-start.19) | collective-permute-done | bytes 51232 | tf_op jit(solution)/shard_map/ppermute | solution.py:455
  98.5 0.7 copy.9
  99.2 9.1 %all-to-all-done.3 = bf16[32,32,256]{2,1,0:T(8,128)(2,1)S(1)} async-done(((bf16[32,32,256]{2,1,0:T(8,128)(2,1)}), bf16[32,32,256]{2,1,0:T(8,128)(2,1)S(1)}, u32[]{:S(2)}, u32[]{:S(2)}) %all-to-all-start.3) | async-done | bytes 524320 | tf_op jit(solution)/shard_map/all_to_all | solution.py:451
  108.2 0.8 gather_sums.1
  (31 shorter events, 1.6 us)
Async XLA Ops:
  2.4 9.9 %collective-permute-start = (bf16[32,1152]{1,0:T(8,128)(2,1)}, bf16[32,1152]{1,0:T(8,128)(2,1)S(1)}, u32[]{:S(2)}, u32[]{:S(2)}) collective-permute-start(bf16[32,1152]{1,0:T(8,128)(2,1)} %get-tuple-element.35), channel_id=1, source_target_pairs={{0,16},{16,0},{1,17},{17,1},{2,18},{18,2},{3,19},{19,3},{4,20},{20... | collective-permute-start | bytes 221192 | tf_op jit(solution)/shard_map/ppermute | solution.py:455
  5.6 16.2 %all-to-all-start = ((bf16[16,32,384]{2,1,0:T(8,128)(2,1)}), bf16[16,32,384]{2,1,0:T(8,128)(2,1)S(1)}, u32[]{:S(2)}, u32[]{:S(2)}) async-start(bf16[16,32,384]{2,1,0:T(8,128)(2,1)} %bitcast.23), calls=%async_computation | async-start | bytes 786432 | tf_op jit(solution)/shard_map/all_to_all | solution.py:451
  13.3 17.0 %collective-permute-start.1 = (bf16[144,1024]{1,0:T(8,128)(2,1)}, bf16[144,1024]{1,0:T(8,128)(2,1)S(1)}, u32[]{:S(2)}, u32[]{:S(2)}) collective-permute-start(bf16[144,1024]{1,0:T(8,128)(2,1)} %get-tuple-element.40.refs_0_), channel_id=1, source_target_pairs={{0,4},{4,0},{8,12},{12,8},{1,5},{5,1},{9,13},{13,9},{2,6},{6,2},{1... | collective-permute-start | bytes 884744 | tf_op jit(solution)/shard_map/ppermute | solution.py:455
  14.7 15.6 %collective-permute-start.3 = (bf16[144,1024]{1,0:T(8,128)(2,1)}, bf16[144,1024]{1,0:T(8,128)(2,1)S(1)}, u32[]{:S(2)}, u32[]{:S(2)}) collective-permute-start(bf16[144,1024]{1,0:T(8,128)(2,1)} %get-tuple-element.40.refs_0_), channel_id=1, source_target_pairs={{0,12},{4,8},{8,4},{12,0},{1,13},{5,9},{9,5},{13,1},{2,14},{6,10},... | collective-permute-start | bytes 884744 | tf_op jit(solution)/shard_map/ppermute | solution.py:455
  21.9 9.8 %collective-permute-start.2 = (bf16[144,1024]{1,0:T(8,128)(2,1)}, bf16[144,1024]{1,0:T(8,128)(2,1)S(1)}, u32[]{:S(2)}, u32[]{:S(2)}) collective-permute-start(bf16[144,1024]{1,0:T(8,128)(2,1)} %get-tuple-element.40.refs_0_), channel_id=1, source_target_pairs={{0,8},{4,12},{8,0},{12,4},{1,9},{5,13},{9,1},{13,5},{2,10},{6,14},... | collective-permute-start | bytes 884744 | tf_op jit(solution)/shard_map/ppermute | solution.py:455
  23.6 0.9 copy-start.3
  24.5 8.7 %collective-permute-start.9 = (bf16[2,32,2176]{2,1,0:T(8,128)(2,1)S(1)}, bf16[2,32,2176]{2,1,0:T(8,128)(2,1)S(1)}, u32[]{:S(2)}, u32[]{:S(2)}) collective-permute-start(bf16[2,32,2176]{2,1,0:T(8,128)(2,1)S(1)} %attach_sources.1.mine_ref), channel_id=1, source_target_pairs={{0,1},{1,0},{2,3},{3,2},{4,5},{5,4},{6,7},{7,6},{8,9},{9,8},{10,11... | collective-permute-start | bytes 835592 | tf_op jit(solution)/shard_map/ppermute | solution.py:455
  25.8 15.6 %collective-permute-start.8 = (bf16[16,32,384]{2,1,0:T(8,128)(2,1)S(1)}, bf16[16,32,384]{2,1,0:T(8,128)(2,1)S(1)}, u32[]{:S(2)}, u32[]{:S(2)}) collective-permute-start(bf16[16,32,384]{2,1,0:T(8,128)(2,1)S(1)} %all-to-all-done.refs_0_), channel_id=1, source_target_pairs={{0,1},{1,0},{2,3},{3,2},{4,5},{5,4},{6,7},{7,6},{8,9},{9,8},{10,11... | collective-permute-start | bytes 1179656 | tf_op jit(solution)/shard_map/ppermute | solution.py:455
  31.7 2.6 %collective-permute-start.6 = (bf16[144,1024]{1,0:T(8,128)(2,1)S(1)}, bf16[144,1024]{1,0:T(8,128)(2,1)S(1)}, u32[]{:S(2)}, u32[]{:S(2)}) collective-permute-start(bf16[144,1024]{1,0:T(8,128)(2,1)S(1)} %collective-permute-done.2.refs_2_), channel_id=1, source_target_pairs={{0,2},{2,0},{1,3},{3,1},{4,6},{6,4},{5,7},{7,5},{8,10},{10,8},{9,1... | collective-permute-start | bytes 884744 | tf_op jit(solution)/shard_map/ppermute | solution.py:455
  32.7 3.1 %collective-permute-start.4 = (bf16[144,1024]{1,0:T(8,128)(2,1)}, bf16[144,1024]{1,0:T(8,128)(2,1)S(1)}, u32[]{:S(2)}, u32[]{:S(2)}) collective-permute-start(bf16[144,1024]{1,0:T(8,128)(2,1)} %get-tuple-element.40.refs_0_), channel_id=1, source_target_pairs={{0,2},{2,0},{1,3},{3,1},{4,6},{6,4},{5,7},{7,5},{8,10},{10,8},{9,1... | collective-permute-start | bytes 884744 | tf_op jit(solution)/shard_map/ppermute | solution.py:455
  32.7 3.6 %collective-permute-start.5 = (bf16[144,1024]{1,0:T(8,128)(2,1)S(1)}, bf16[144,1024]{1,0:T(8,128)(2,1)S(1)}, u32[]{:S(2)}, u32[]{:S(2)}) collective-permute-start(bf16[144,1024]{1,0:T(8,128)(2,1)S(1)} %collective-permute-done.1.refs_1_), channel_id=1, source_target_pairs={{0,2},{2,0},{1,3},{3,1},{4,6},{6,4},{5,7},{7,5},{8,10},{10,8},{9,1... | collective-permute-start | bytes 884744 | tf_op jit(solution)/shard_map/ppermute | solution.py:455
  33.2 4.4 %collective-permute-start.7 = (bf16[144,1024]{1,0:T(8,128)(2,1)S(1)}, bf16[144,1024]{1,0:T(8,128)(2,1)S(1)}, u32[]{:S(2)}, u32[]{:S(2)}) collective-permute-start(bf16[144,1024]{1,0:T(8,128)(2,1)S(1)} %collective-permute-done.3.refs_3_), channel_id=1, source_target_pairs={{0,2},{2,0},{1,3},{3,1},{4,6},{6,4},{5,7},{7,5},{8,10},{10,8},{9,1... | collective-permute-start | bytes 884744 | tf_op jit(solution)/shard_map/ppermute | solution.py:455
  34.3 25.0 %collective-permute-start.10 = (bf16[2,64,1152]{2,1,0:T(8,128)(2,1)S(1)}, bf16[2,64,1152]{2,1,0:T(8,128)(2,1)S(1)}, u32[]{:S(2)}, u32[]{:S(2)}) collective-permute-start(bf16[2,64,1152]{2,1,0:T(8,128)(2,1)S(1)} %bitcast.17), channel_id=1, source_target_pairs={{0,4},{4,0},{8,12},{12,8},{1,5},{5,1},{9,13},{13,9},{2,6},{6,2},{1... | collective-permute-start | bytes 884744 | tf_op jit(solution)/shard_map/ppermute | solution.py:455
  35.9 23.5 %collective-permute-start.11 = (bf16[2,64,1152]{2,1,0:T(8,128)(2,1)S(1)}, bf16[2,64,1152]{2,1,0:T(8,128)(2,1)S(1)}, u32[]{:S(2)}, u32[]{:S(2)}) collective-permute-start(bf16[2,64,1152]{2,1,0:T(8,128)(2,1)S(1)} %bitcast.18), channel_id=1, source_target_pairs={{0,8},{4,12},{8,0},{12,4},{1,9},{5,13},{9,1},{13,5},{2,10},{6,14},... | collective-permute-start | bytes 884744 | tf_op jit(solution)/shard_map/ppermute | solution.py:455
  36.3 23.0 %collective-permute-start.12 = (bf16[2,64,1152]{2,1,0:T(8,128)(2,1)S(1)}, bf16[2,64,1152]{2,1,0:T(8,128)(2,1)S(1)}, u32[]{:S(2)}, u32[]{:S(2)}) collective-permute-start(bf16[2,64,1152]{2,1,0:T(8,128)(2,1)S(1)} %bitcast.19), channel_id=1, source_target_pairs={{0,12},{4,8},{8,4},{12,0},{1,13},{5,9},{9,5},{13,1},{2,14},{6,10},... | collective-permute-start | bytes 884744 | tf_op jit(solution)/shard_map/ppermute | solution.py:455
  37.6 1.0 copy-start.1
  42.7 7.0 %collective-permute-start.13 = (bf16[128,256]{1,0:T(8,128)(2,1)S(1)}, bf16[128,256]{1,0:T(8,128)(2,1)S(1)}, u32[]{:S(2)}, u32[]{:S(2)}) collective-permute-start(bf16[128,256]{1,0:T(8,128)(2,1)S(1)} %get-tuple-element.55), channel_id=1, source_target_pairs={{0,16},{16,0},{1,17},{17,1},{2,18},{18,2},{3,19},{19,3},{4,20},{20... | collective-permute-start | bytes 196616 | tf_op jit(solution)/shard_map/ppermute | solution.py:455
  51.2 15.0 %all-to-all-start.1 = ((bf16[16,64,128]{2,1,0:T(8,128)(2,1)}), bf16[16,64,128]{2,1,0:T(8,128)(2,1)S(1)}, u32[]{:S(2)}, u32[]{:S(2)}) async-start(bf16[16,64,128]{2,1,0:T(8,128)(2,1)} %bitcast.5), calls=%async_computation.1 | async-start | bytes 524288 | tf_op jit(solution)/shard_map/all_to_all | solution.py:451
  59.3 6.9 %copy-start.2 = (bf16[1,64,1024]{2,1,0:T(8,128)(2,1)S(1)}, bf16[1,64,1024]{2,1,0:T(8,128)(2,1)}, u32[]{:S(2)}) copy-start(bf16[1,64,1024]{2,1,0:T(8,128)(2,1)} %get-tuple-element.60.refs_0_) | copy-start | bytes 393220
  59.3 6.9 %copy-start.4 = (f32[128]{0:T(128)S(1)}, f32[128]{0:T(128)}, u32[]{:S(2)}) copy-start(f32[128]{0:T(128)} %param.12) | copy-start | bytes 1540
  59.4 1.6 %collective-permute-start.14 = (bf16[2,64,1152]{2,1,0:T(8,128)(2,1)S(1)}, bf16[2,64,1152]{2,1,0:T(8,128)(2,1)S(1)}, u32[]{:S(2)}, u32[]{:S(2)}) collective-permute-start(bf16[2,64,1152]{2,1,0:T(8,128)(2,1)S(1)} %bitcast.20), channel_id=1, source_target_pairs={{0,2},{2,0},{1,3},{3,1},{4,6},{6,4},{5,7},{7,5},{8,10},{10,8},{9,1... | collective-permute-start | bytes 884744 | tf_op jit(solution)/shard_map/ppermute | solution.py:455
  59.5 1.9 %collective-permute-start.15 = (bf16[2,64,1152]{2,1,0:T(8,128)(2,1)S(1)}, bf16[2,64,1152]{2,1,0:T(8,128)(2,1)S(1)}, u32[]{:S(2)}, u32[]{:S(2)}) collective-permute-start(bf16[2,64,1152]{2,1,0:T(8,128)(2,1)S(1)} %collective-permute-done.10.refs_1_), channel_id=1, source_target_pairs={{0,2},{2,0},{1,3},{3,1},{4,6},{6,4},{5,7},{7,5},{8,10},{10,8},{9,1... | collective-permute-start | bytes 884744 | tf_op jit(solution)/shard_map/ppermute | solution.py:455
  59.9 1.9 %collective-permute-start.16 = (bf16[2,64,1152]{2,1,0:T(8,128)(2,1)S(1)}, bf16[2,64,1152]{2,1,0:T(8,128)(2,1)S(1)}, u32[]{:S(2)}, u32[]{:S(2)}) collective-permute-start(bf16[2,64,1152]{2,1,0:T(8,128)(2,1)S(1)} %collective-permute-done.11.refs_2_), channel_id=1, source_target_pairs={{0,2},{2,0},{1,3},{3,1},{4,6},{6,4},{5,7},{7,5},{8,10},{10,8},{9,1... | collective-permute-start | bytes 884744 | tf_op jit(solution)/shard_map/ppermute | solution.py:455
  60.0 2.2 %collective-permute-start.17 = (bf16[2,64,1152]{2,1,0:T(8,128)(2,1)S(1)}, bf16[2,64,1152]{2,1,0:T(8,128)(2,1)S(1)}, u32[]{:S(2)}, u32[]{:S(2)}) collective-permute-start(bf16[2,64,1152]{2,1,0:T(8,128)(2,1)S(1)} %collective-permute-done.12.refs_3_), channel_id=1, source_target_pairs={{0,2},{2,0},{1,3},{3,1},{4,6},{6,4},{5,7},{7,5},{8,10},{10,8},{9,1... | collective-permute-start | bytes 884744 | tf_op jit(solution)/shard_map/ppermute | solution.py:455
  69.9 17.6 %copy-start = (bf16[1024,1024]{1,0:T(8,128)(2,1)S(1)}, bf16[1024,1024]{1,0:T(8,128)(2,1)}, u32[]{:S(2)}) copy-start(bf16[1024,1024]{1,0:T(8,128)(2,1)} %get-tuple-element.44.normed_any.normed_ref) | copy-start | bytes 6291460
  81.2 6.3 %collective-permute-start.18 = (bf16[128,256]{1,0:T(8,128)(2,1)S(1)}, bf16[128,256]{1,0:T(8,128)(2,1)S(1)}, u32[]{:S(2)}, u32[]{:S(2)}) collective-permute-start(bf16[128,256]{1,0:T(8,128)(2,1)S(1)} %get-tuple-element.63), channel_id=1, source_target_pairs={{0,16},{16,0},{1,17},{17,1},{2,18},{18,2},{3,19},{19,3},{4,20},{20... | collective-permute-start | bytes 196616 | tf_op jit(solution)/shard_map/ppermute | solution.py:455
  89.5 18.7 %all-to-all-start.3 = ((bf16[32,32,256]{2,1,0:T(8,128)(2,1)}), bf16[32,32,256]{2,1,0:T(8,128)(2,1)S(1)}, u32[]{:S(2)}, u32[]{:S(2)}) async-start(bf16[32,32,256]{2,1,0:T(8,128)(2,1)} %bitcast.9), calls=%async_computation.3 | async-start | bytes 1048576 | tf_op jit(solution)/shard_map/all_to_all | solution.py:451
  92.3 6.0 %collective-permute-start.19 = (f32[100,128]{1,0:T(8,128)S(1)}, f32[100,128]{1,0:T(8,128)S(1)}, u32[]{:S(2)}, u32[]{:S(2)}) collective-permute-start(f32[100,128]{1,0:T(8,128)S(1)} %get-tuple-element.66), channel_id=1, source_target_pairs={{0,1},{1,0},{2,3},{3,2},{4,5},{5,4},{6,7},{7,6},{8,9},{9,8},{10,11... | collective-permute-start | bytes 153608 | tf_op jit(solution)/shard_map/ppermute | solution.py:455

commit v24 on v23

--- a/solution.py
+++ b/solution.py
@@ -144,10 +144,14 @@
     wait(out + fetch([(normed, normed_any)], sems, 2 + len(out)))
 
 
-def attach_kernel(packed_ref, sent_ref, out_ref):
-    width = packed_ref.shape[2]
+def attach_kernel(packed_ref, sent_any, out_ref, sems):
+    width, shard = packed_ref.shape[2], packed_ref.shape[1]
+    pairs = [
+        (sent_any.at[0, pl.ds(at * shard, shard)], out_ref.at[at, :, width:]) for at in range(2)
+    ]
+    copies = fetch(pairs, sems)
     out_ref[:, :, :width] = packed_ref[...]
-    out_ref[:, :, width:] = sent_ref[...].reshape(2, -1, LATENT_DIM)
+    wait(copies)
 
 
 def merge_members_kernel(mine_ref, other_ref, packed_ref, source_ref):
@@ -413,26 +417,37 @@
             ]
 
 
-def product_kernel(normed_ref, from_low_ref, from_high_ref, grads_ref, out_ref):
-    count = normed_ref.shape[0]
-    half, last = lax.axis_index("half"), lax.axis_size("half") - 1
-    from_low = jnp.where(half > 0, from_low_ref[...].astype(F32), 0.0)
-    from_high = jnp.where(half < last, from_high_ref[...].astype(F32), 0.0)
+def product_kernel(normed_ref, grads_ref, out_ref):
     grads = grads_ref[...]
-    grads = jnp.concatenate(
-        [
-            grads[:RIM] + from_low,
-            grads[RIM : count - RIM],
-            grads[count - RIM :] + from_high,
-        ],
-        axis=0,
-    )
     high = grads.astype(BF16)
     low = (grads - high.astype(F32)).astype(BF16)
     both = lax.dot_general(
         normed_ref[...], jnp.concatenate([high, low], axis=1), OVER_ROWS, preferred_element_type=F32
     )
-    out_ref[...] = (both[:, : 2 * COLS] + both[:, 2 * COLS :]).astype(BF16)
+    out_ref[...] = both[:, : 2 * COLS] + both[:, 2 * COLS :]
+
+
+def rim_product_kernel(normed_any, total_ref, *refs):
+    arrived, (out_ref, rows, sems) = refs[:-3], refs[-3:]
+    last_row = normed_any.shape[0] - RIM
+    half, last = lax.axis_index("half"), lax.axis_size("half") - 1
+    if len(arrived) == 1:
+        places = [pl.multiple_of(jnp.where(half == 0, last_row, 0), RIM)]
+    else:
+        places = [0, last_row]
+    wait(
+        fetch(
+            [(normed_any.at[pl.ds(place, RIM)], rows.at[at]) for at, place in enumerate(places)], sems
+        )
+    )
+    total = total_ref[...]
+    for at, arrived_ref in enumerate(arrived):
+        grads = arrived_ref[...]
+        if len(arrived) == 2:
+            grads = jnp.where((half > 0) if at == 0 else (half < last), grads.astype(F32), 0.0)
+            grads = grads.astype(BF16)
+        total += lax.dot_general(rows[at], grads, OVER_ROWS, preferred_element_type=F32)
+    out_ref[...] = total.astype(BF16)
 
 
 def gather_kernel(parts_ref, out_ref):
@@ -540,7 +555,8 @@
             attach_kernel,
             "attach_sources",
             [((2, shard, width + LATENT_DIM), BF16)],
-            "vv",
+            "vh",
+            [pltpu.SemaphoreType.DMA((2,))],
             moved=2**19,
         )(packed, sources[1])
         packed, arrived = call(
@@ -661,15 +677,25 @@
         exps=rows * 512,
         room=10,
     )(steps, queries, own, grads, edges)
-    (term,) = call(
+    (total,) = call(
         product_kernel,
         "product",
-        [((LATENT_DIM, 2 * COLS), BF16)],
-        "vvvv",
+        [((LATENT_DIM, 2 * COLS), F32)],
+        "vv",
         flops=rows * LATENT_DIM * 8 * COLS,
         moved=2**22,
         room=16,
-    )(normed, from_low, from_high, kv_grads)
+    )(normed, kv_grads)
+    arrived = [from_low] if halves == 2 else [from_low, from_high]
+    (term,) = call(
+        rim_product_kernel,
+        "product_rims",
+        [((LATENT_DIM, 2 * COLS), BF16)],
+        "hv" + "v" * len(arrived),
+        [pltpu.VMEM((len(arrived), RIM, LATENT_DIM), BF16), pltpu.SemaphoreType.DMA((2,))],
+        flops=RIM * LATENT_DIM * 4 * COLS,
+        moved=2**21,
+    )(normed, total, *arrived)
     term, prediction = lax.optimization_barrier((term, prediction))
     term = exchange(term.reshape(-1, shard, 2 * COLS), everyone)
     (grad_kv,) = call(

time: 110 us -> 114 us (1.036)
  waiting for transfers between devices: 34.9 us -> 37.5 us
  Pallas kernels: 26 us -> 28.2 us
    ppermute x20, waiting for transfers between devices: 17.4 us -> 20 us  [swap(): lax.ppermute(value, axis, [(i, i ^ step) for i in range(lax.axis_size(axi...]
    pallas_call x15 -> x16, Pallas kernels: 26 us -> 28.2 us  [run(): made(*[pltpu.with_memory_space_constraint(arg, pltpu.HBM) if space == 'h'...]
    unnamed x11 -> x9, local copies, waits for them, and re-layouts: 2.55 us -> 1.65 us
  transfers between devices with their start and end apart: 23 -> 23, of which waited for: 14 -> 14; matrix products, arithmetic and copies ran while one was open for 2% -> 2% of each run, Pallas kernels for 15% -> 13%
where the time goes in v24:
time: 114 us; the launch traced here: 113 us
  waiting for transfers between devices  37.5 us (33%)
  starting transfers between devices  33.8 us (30%)
  Pallas kernels  28.2 us (25%)
  blocking collectives  9.89 us (9%)
  local copies, waits for them, and re-layouts  1.73 us (2%)
    pallas_call x16, Pallas kernels, run(): made(*[pltpu.with_memory_space_constraint(arg, pltpu.HBM) if space == 'h'...  28.2 us
    ppermute x20, waiting for transfers between devices, swap(): lax.ppermute(value, axis, [(i, i ^ step) for i in range(lax.axis_size(axi...  20 us
    ppermute x20, starting transfers between devices, swap(): lax.ppermute(value, axis, [(i, i ^ step) for i in range(lax.axis_size(axi...  18.1 us
    all_to_all x3, waiting for transfers between devices, exchange(): return lax.all_to_all(chunks, axes, 0, 0)  17.5 us
    all_to_all x3, starting transfers between devices, exchange(): return lax.all_to_all(chunks, axes, 0, 0)  15.7 us
    all_to_all x1, blocking collectives, exchange(): return lax.all_to_all(chunks, axes, 0, 0)  9.89 us
  transfers between devices with their start and end apart: 23, of which 14 were waited for; matrix products, arithmetic and copies ran while one was open for 2% of the time, Pallas kernels for 13%

profile of v24, /device:TPU:1, one launch (start us, length us, event | category | flops | bytes accessed | tf_op | source)
XLA Modules:
  0.0 112.9 jit_solution(8086111999330354557)
XLA Ops:
  0.6 1.8 %prepare_weights.1 = (bf16[2,8,1,32,384]{4,3,2,1,0:T(8,128)(2,1)}, bf16[32,1152]{1,0:T(8,128)(2,1)}) custom-call(bf16[32,3072]{1,0:T(8,128)(2,1)} %w_any.1, bf16[32,1024]{1,0:T(8,128)(2,1)} %mix_any.1, bf16[32,100]{1,0:T(8,128)(2,1)} %readout_any.1), custom_call_target="tpu_custom_call" | custom-call | bytes 1048576 | tf_op jit(solution)/shard_map/prepare_weights/pallas_call | solution.py:63
  2.5 3.2 %collective-permute-start = (bf16[32,1152]{1,0:T(8,128)(2,1)}, bf16[32,1152]{1,0:T(8,128)(2,1)S(1)}, u32[]{:S(2)}, u32[]{:S(2)}) collective-permute-start(bf16[32,1152]{1,0:T(8,128)(2,1)} %get-tuple-element.35), channel_id=1, source_target_pairs={{0,16},{16,0},{1,17},{17,1},{2,18},{18,2},{3,19},{19,3},{4,20},{20... | collective-permute-start | bytes 221192 | tf_op jit(solution)/shard_map/ppermute | solution.py:470
  5.7 4.8 %all-to-all-start = ((bf16[16,32,384]{2,1,0:T(8,128)(2,1)}), bf16[16,32,384]{2,1,0:T(8,128)(2,1)S(1)}, u32[]{:S(2)}, u32[]{:S(2)}) async-start(bf16[16,32,384]{2,1,0:T(8,128)(2,1)} %bitcast.23), calls=%async_computation | async-start | bytes 786432 | tf_op jit(solution)/shard_map/all_to_all | solution.py:466
  10.4 1.9 %norm.1 = (bf16[144,1024]{1,0:T(8,128)(2,1)}, bf16[1,64,1024]{2,1,0:T(8,128)(2,1)}, bf16[1,64,1024]{2,1,0:T(8,128)(2,1)}) custom-call(s32[2,4]{1,0:T(2,128)} %near_any.1, bf16[128,1024]{1,0:T(8,128)(2,1)} %bitcast.24), custom_call_target="tpu_custom_call" | custom-call | flops 1048576 | bytes 1048576 | tf_op jit(solution)/shard_map/norm/pallas_call | solution.py:63
  12.3 0.9 select_bitcast_fusion.1
  13.3 1.5 %collective-permute-start.1 = (bf16[144,1024]{1,0:T(8,128)(2,1)}, bf16[144,1024]{1,0:T(8,128)(2,1)S(1)}, u32[]{:S(2)}, u32[]{:S(2)}) collective-permute-start(bf16[144,1024]{1,0:T(8,128)(2,1)} %get-tuple-element.40.refs_0_), channel_id=1, source_target_pairs={{0,4},{4,0},{8,12},{12,8},{1,5},{5,1},{9,13},{13,9},{2,6},{6,2},{1... | collective-permute-start | bytes 884744 | tf_op jit(solution)/shard_map/ppermute | solution.py:470
  14.7 1.2 %collective-permute-start.3 = (bf16[144,1024]{1,0:T(8,128)(2,1)}, bf16[144,1024]{1,0:T(8,128)(2,1)S(1)}, u32[]{:S(2)}, u32[]{:S(2)}) collective-permute-start(bf16[144,1024]{1,0:T(8,128)(2,1)} %get-tuple-element.40.refs_0_), channel_id=1, source_target_pairs={{0,12},{4,8},{8,4},{12,0},{1,13},{5,9},{9,5},{13,1},{2,14},{6,10},... | collective-permute-start | bytes 884744 | tf_op jit(solution)/shard_map/ppermute | solution.py:470
  15.9 6.0 %all-to-all-done.refs_0_ = bf16[16,32,384]{2,1,0:T(8,128)(2,1)S(1)} async-done(((bf16[16,32,384]{2,1,0:T(8,128)(2,1)}), bf16[16,32,384]{2,1,0:T(8,128)(2,1)S(1)}, u32[]{:S(2)}, u32[]{:S(2)}) %all-to-all-start) | async-done | bytes 393248 | tf_op jit(solution)/shard_map/all_to_all | solution.py:466
  21.9 1.7 %collective-permute-start.2 = (bf16[144,1024]{1,0:T(8,128)(2,1)}, bf16[144,1024]{1,0:T(8,128)(2,1)S(1)}, u32[]{:S(2)}, u32[]{:S(2)}) collective-permute-start(bf16[144,1024]{1,0:T(8,128)(2,1)} %get-tuple-element.40.refs_0_), channel_id=1, source_target_pairs={{0,8},{4,12},{8,0},{12,4},{1,9},{5,13},{9,1},{13,5},{2,10},{6,14},... | collective-permute-start | bytes 884744 | tf_op jit(solution)/shard_map/ppermute | solution.py:470
  23.6 0.9 attach_sources.1.mine_ref
  24.5 1.3 %collective-permute-start.9 = (bf16[2,32,2176]{2,1,0:T(8,128)(2,1)S(1)}, bf16[2,32,2176]{2,1,0:T(8,128)(2,1)S(1)}, u32[]{:S(2)}, u32[]{:S(2)}) collective-permute-start(bf16[2,32,2176]{2,1,0:T(8,128)(2,1)S(1)} %attach_sources.1.mine_ref), channel_id=1, source_target_pairs={{0,1},{1,0},{2,3},{3,2},{4,5},{5,4},{6,7},{7,6},{8,9},{9,8},{10,11... | collective-permute-start | bytes 835592 | tf_op jit(solution)/shard_map/ppermute | solution.py:470
  26.0 4.3 %collective-permute-done.1.refs_1_ = bf16[144,1024]{1,0:T(8,128)(2,1)S(1)} collective-permute-done((bf16[144,1024]{1,0:T(8,128)(2,1)}, bf16[144,1024]{1,0:T(8,128)(2,1)S(1)}, u32[]{:S(2)}, u32[]{:S(2)}) %collective-permute-start.1) | collective-permute-done | bytes 294944 | tf_op jit(solution)/shard_map/ppermute | solution.py:470
  30.3 1.4 %collective-permute-done.2.refs_2_ = bf16[144,1024]{1,0:T(8,128)(2,1)S(1)} collective-permute-done((bf16[144,1024]{1,0:T(8,128)(2,1)}, bf16[144,1024]{1,0:T(8,128)(2,1)S(1)}, u32[]{:S(2)}, u32[]{:S(2)}) %collective-permute-start.2) | collective-permute-done | bytes 294944 | tf_op jit(solution)/shard_map/ppermute | solution.py:470
  31.7 1.0 collective-permute-start.6
  32.7 0.5 collective-permute-start.5
  33.2 0.7 collective-permute-start.7
  34.3 1.5 %collective-permute-start.10 = (bf16[2,64,1152]{2,1,0:T(8,128)(2,1)S(1)}, bf16[2,64,1152]{2,1,0:T(8,128)(2,1)S(1)}, u32[]{:S(2)}, u32[]{:S(2)}) collective-permute-start(bf16[2,64,1152]{2,1,0:T(8,128)(2,1)S(1)} %bitcast.17), channel_id=1, source_target_pairs={{0,4},{4,0},{8,12},{12,8},{1,5},{5,1},{9,13},{13,9},{2,6},{6,2},{1... | collective-permute-start | bytes 884744 | tf_op jit(solution)/shard_map/ppermute | solution.py:470
  35.9 0.5 collective-permute-start.11
  36.4 1.3 %collective-permute-start.12 = (bf16[2,64,1152]{2,1,0:T(8,128)(2,1)S(1)}, bf16[2,64,1152]{2,1,0:T(8,128)(2,1)S(1)}, u32[]{:S(2)}, u32[]{:S(2)}) collective-permute-start(bf16[2,64,1152]{2,1,0:T(8,128)(2,1)S(1)} %bitcast.19), channel_id=1, source_target_pairs={{0,12},{4,8},{8,4},{12,0},{1,13},{5,9},{9,5},{13,1},{2,14},{6,10},... | collective-permute-start | bytes 884744 | tf_op jit(solution)/shard_map/ppermute | solution.py:470
  37.6 1.0 copy-done.1
  38.6 1.5 %collect.1 = (bf16[1024,1024]{1,0:T(8,128)(2,1)}, f32[8,16,128]{2,1,0:T(8,128)S(1)}) custom-call(bf16[144,1024]{1,0:T(8,128)(2,1)S(1)} %copy-done.1, bf16[144,1024]{1,0:T(8,128)(2,1)S(1)} %collective-permute-done.1.refs_1_, bf16[144,1024]{1,0:T(8,128)(2,1)S(1)} %collective-permute-done.2.refs_2_, bf16[144,1024]{1,0:T(8,128)(2,1)S(1)} %collective-permute-done.3.refs_3_, ...), custom_call_target="tpu_custom_call" | custom-call | bytes 4194304 | tf_op jit(solution)/shard_map/collect/pallas_call | solution.py:63
  40.1 1.3 %collective-permute-done.8.refs_1_ = bf16[16,32,384]{2,1,0:T(8,128)(2,1)S(1)} collective-permute-done((bf16[16,32,384]{2,1,0:T(8,128)(2,1)S(1)}, bf16[16,32,384]{2,1,0:T(8,128)(2,1)S(1)}, u32[]{:S(2)}, u32[]{:S(2)}) %collective-permute-start.8) | collective-permute-done | bytes 393248 | tf_op jit(solution)/shard_map/ppermute | solution.py:470
  41.4 1.3 %project_rims.1 = (bf16[16,2,32,384]{3,2,1,0:T(8,128)(2,1)S(1)}, bf16[128,256]{1,0:T(8,128)(2,1)S(1)}) custom-call(bf16[1024,1024]{1,0:T(8,128)(2,1)} %get-tuple-element.44.normed_any.normed_ref, bf16[16,32,384]{2,1,0:T(8,128)(2,1)S(1)} %all-to-all-done.refs_0_, bf16[16,32,384]{2,1,0:T(8,128)(2,1)S(1)} %collective-permute-done.8.refs_1_), custom_call_target="tpu_custom_call" | custom-call | flops 67108864 | bytes 1048576 | tf_op jit(solution)/shard_map/project_rims/pallas_call | solution.py:63
  42.7 0.9 collective-permute-start.13
  43.6 2.8 %project.1 = (bf16[1024,128]{1,0:T(8,128)(2,1)S(1)}, bf16[1024,256]{1,0:T(8,128)(2,1)S(1)}) custom-call(bf16[1024,1024]{1,0:T(8,128)(2,1)} %get-tuple-element.44.normed_any.normed_ref, bf16[16,2,32,384]{3,2,1,0:T(8,128)(2,1)S(1)} %get-tuple-element.47.w_ref), custom_call_target="tpu_custom_call" | custom-call | flops 805306368 | bytes 4194304 | tf_op jit(solution)/shard_map/project/pallas_call | solution.py:63
  46.5 1.9 %attention_interior.1.done_ref = bf16[1024,128]{1,0:T(8,128)(2,1)S(1)} custom-call(f32[8,16,128]{2,1,0:T(8,128)S(1)} %get-tuple-element.45.steps_ref, bf16[1024,128]{1,0:T(8,128)(2,1)S(1)} %get-tuple-element.48.q_ref, bf16[1024,256]{1,0:T(8,128)(2,1)S(1)} %get-tuple-element.54.kv_ref), custom_call_target="tpu_custom_call" | custom-call | flops 268435456 | bytes 2097152 | tf_op jit(solution)/shard_map/attention_interior/pallas_call | solution.py:63
  48.3 1.4 %collective-permute-done.13.low_ref.high_ref = bf16[128,256]{1,0:T(8,128)(2,1)S(1)} collective-permute-done((bf16[128,256]{1,0:T(8,128)(2,1)S(1)}, bf16[128,256]{1,0:T(8,128)(2,1)S(1)}, u32[]{:S(2)}, u32[]{:S(2)}) %collective-permute-start.13) | collective-permute-done | bytes 65568 | tf_op jit(solution)/shard_map/ppermute | solution.py:470
  49.8 1.4 %attention_edges.1 = bf16[1024,128]{1,0:T(8,128)(2,1)} custom-call(f32[8,16,128]{2,1,0:T(8,128)S(1)} %get-tuple-element.45.steps_ref, bf16[1024,128]{1,0:T(8,128)(2,1)S(1)} %get-tuple-element.48.q_ref, bf16[1024,256]{1,0:T(8,128)(2,1)S(1)} %get-tuple-element.54.kv_ref, bf16[128,256]{1,0:T(8,128)(2,1)S(1)} %collective-permute-done.13.low_ref.high_ref, ...), custom_call_target="tpu_custom_call" | custom-call | flops 67108864 | bytes 1048576 | tf_op jit(solution)/shard_map/attention_edges/pallas_call | solution.py:63
  51.2 8.1 %all-to-all-start.1 = ((bf16[16,64,128]{2,1,0:T(8,128)(2,1)}), bf16[16,64,128]{2,1,0:T(8,128)(2,1)S(1)}, u32[]{:S(2)}, u32[]{:S(2)}) async-start(bf16[16,64,128]{2,1,0:T(8,128)(2,1)} %bitcast.5), calls=%async_computation.1 | async-start | bytes 524288 | tf_op jit(solution)/shard_map/all_to_all | solution.py:466
  60.5 0.6 collective-permute-done.14.refs_4_
  61.0 0.4 collective-permute-done.15.refs_5_
  61.5 0.4 collective-permute-done.16.refs_6_
  61.9 0.4 collective-permute-done.17.refs_7_
  62.3 1.5 %assemble.1.w_any = bf16[2,4,2,64,1152]{4,3,2,1,0:T(8,128)(2,1)} custom-call(bf16[2,64,1152]{2,1,0:T(8,128)(2,1)S(1)} %bitcast.21, bf16[2,64,1152]{2,1,0:T(8,128)(2,1)S(1)} %collective-permute-done.10.refs_1_, bf16[2,64,1152]{2,1,0:T(8,128)(2,1)S(1)} %collective-permute-done.11.refs_2_, bf16[2,64,1152]{2,1,0:T(8,128)(2,1)S(1)} %collective-permute-done.12.refs_3_, ...), custom_call_target="tpu_custom_call" | custom-call | bytes 4194304 | tf_op jit(solution)/shard_map/assemble/pallas_call | solution.py:63
  63.8 2.4 %all-to-all-done.1.att_ref = bf16[16,64,128]{2,1,0:T(8,128)(2,1)S(1)} async-done(((bf16[16,64,128]{2,1,0:T(8,128)(2,1)}), bf16[16,64,128]{2,1,0:T(8,128)(2,1)S(1)}, u32[]{:S(2)}, u32[]{:S(2)}) %all-to-all-start.1) | async-done | bytes 262176 | tf_op jit(solution)/shard_map/all_to_all | solution.py:466
  66.2 3.7 %mix_loss_backward.1 = (f32[100,128]{1,0:T(8,128)S(1)}, bf16[16,64,128]{2,1,0:T(8,128)(2,1)S(1)}) custom-call(bf16[16,64,128]{2,1,0:T(8,128)(2,1)S(1)} %all-to-all-done.1.att_ref, f32[1,128]{1,0:T(1,128)S(1)} %bitcast.22, f32[100,128]{1,0:T(8,128)} %truth_any.1, bf16[2,4,2,64,1152]{4,3,2,1,0:T(8,128)(2,1)} %assemble.1.w_any, ...), custom_call_target="tpu_custom_call" | custom-call | flops 603979776 | bytes 4194304 | tf_op jit(solution)/shard_map/mix_loss_backward/pallas_call | solution.py:63
  69.9 9.9 %all_to_all.20 = bf16[16,64,128]{2,1,0:T(8,128)(2,1)S(1)} all-to-all(bf16[16,64,128]{2,1,0:T(8,128)(2,1)S(1)} %get-tuple-element.62), channel_id=1, replica_groups=mesh['half'=2,'quad'=4,'core'=2,'ens'=2] {'quad','core','ens'}, dimensions={0} | all-to-all | bytes 524288 | tf_op jit(solution)/shard_map/all_to_all | solution.py:466
  79.8 1.4 %attention_edges_back.1 = (f32[2,256,256]{2,1,0:T(8,128)S(1)}, bf16[128,256]{1,0:T(8,128)(2,1)S(1)}) custom-call(f32[8,16,128]{2,1,0:T(8,128)S(1)} %get-tuple-element.45.steps_ref, bf16[1024,128]{1,0:T(8,128)(2,1)S(1)} %get-tuple-element.48.q_ref, bf16[1024,256]{1,0:T(8,128)(2,1)S(1)} %get-tuple-element.54.kv_ref, ...), custom_call_target="tpu_custom_call" | custom-call | flops 167772160 | bytes 1048576 | tf_op jit(solution)/shard_map/attention_edges_back/pallas_call | solution.py:63
  81.2 3.8 %attention_interior_back.1.grads_ref = f32[1024,256]{1,0:T(8,128)S(1)} custom-call(f32[8,16,128]{2,1,0:T(8,128)S(1)} %get-tuple-element.45.steps_ref, bf16[1024,128]{1,0:T(8,128)(2,1)S(1)} %get-tuple-element.48.q_ref, bf16[1024,256]{1,0:T(8,128)(2,1)S(1)} %get-tuple-element.54.kv_ref, bf16[1024,128]{1,0:T(8,128)(2,1)S(1)} %bitcast.15, ...), custom_call_target="tpu_custom_call" | custom-call | flops 536870912 | bytes 4194304 | tf_op jit(solution)/shard_map/attention_interior_back/pallas_call | solution.py:63
  85.2 1.3 %product.1.total_ref = f32[1024,256]{1,0:T(8,128)S(1)} custom-call(bf16[1024,1024]{1,0:T(8,128)(2,1)S(1)} %copy-done, f32[1024,256]{1,0:T(8,128)S(1)} %attention_interior_back.1.grads_ref), custom_call_target="tpu_custom_call" | custom-call | flops 1073741824 | bytes 4194304 | tf_op jit(solution)/shard_map/product/pallas_call | solution.py:63
  86.4 4.9 %collective-permute-done.18.refs_0_ = bf16[128,256]{1,0:T(8,128)(2,1)S(1)} collective-permute-done((bf16[128,256]{1,0:T(8,128)(2,1)S(1)}, bf16[128,256]{1,0:T(8,128)(2,1)S(1)}, u32[]{:S(2)}, u32[]{:S(2)}) %collective-permute-start.18) | collective-permute-done | bytes 65568 | tf_op jit(solution)/shard_map/ppermute | solution.py:470
  91.3 2.1 %product_rims.1 = bf16[1024,256]{1,0:T(8,128)(2,1)} custom-call(bf16[1024,1024]{1,0:T(8,128)(2,1)} %get-tuple-element.44.normed_any.normed_ref, f32[1024,256]{1,0:T(8,128)S(1)} %product.1.total_ref, bf16[128,256]{1,0:T(8,128)(2,1)S(1)} %collective-permute-done.18.refs_0_), custom_call_target="tpu_custom_call" | custom-call | flops 67108864 | bytes 2097152 | tf_op jit(solution)/shard_map/product_rims/pallas_call | solution.py:63
  93.4 2.8 %all-to-all-start.3 = ((bf16[32,32,256]{2,1,0:T(8,128)(2,1)}), bf16[32,32,256]{2,1,0:T(8,128)(2,1)S(1)}, u32[]{:S(2)}, u32[]{:S(2)}) async-start(bf16[32,32,256]{2,1,0:T(8,128)(2,1)} %bitcast.9), calls=%async_computation.3 | async-start | bytes 1048576 | tf_op jit(solution)/shard_map/all_to_all | solution.py:466
  96.2 1.5 %collective-permute-start.19 = (f32[100,128]{1,0:T(8,128)S(1)}, f32[100,128]{1,0:T(8,128)S(1)}, u32[]{:S(2)}, u32[]{:S(2)}) collective-permute-start(f32[100,128]{1,0:T(8,128)S(1)} %get-tuple-element.66), channel_id=1, source_target_pairs={{0,1},{1,0},{2,3},{3,2},{4,5},{5,4},{6,7},{7,6},{8,9},{9,8},{10,11... | collective-permute-start | bytes 153608 | tf_op jit(solution)/shard_map/ppermute | solution.py:470
  97.7 4.5 %collective-permute-done.19 = f32[100,128]{1,0:T(8,128)S(1)} collective-permute-done((f32[100,128]{1,0:T(8,128)S(1)}, f32[100,128]{1,0:T(8,128)S(1)}, u32[]{:S(2)}, u32[]{:S(2)}) %collective-permute-start.19) | collective-permute-done | bytes 51232 | tf_op jit(solution)/shard_map/ppermute | solution.py:470
  102.4 0.7 copy.9
  103.1 9.1 %all-to-all-done.3 = bf16[32,32,256]{2,1,0:T(8,128)(2,1)S(1)} async-done(((bf16[32,32,256]{2,1,0:T(8,128)(2,1)}), bf16[32,32,256]{2,1,0:T(8,128)(2,1)S(1)}, u32[]{:S(2)}, u32[]{:S(2)}) %all-to-all-start.3) | async-done | bytes 524320 | tf_op jit(solution)/shard_map/all_to_all | solution.py:466
  112.2 0.8 gather_sums.1
  (30 shorter events, 2.1 us)
Async XLA Ops:
  2.5 9.9 %collective-permute-start = (bf16[32,1152]{1,0:T(8,128)(2,1)}, bf16[32,1152]{1,0:T(8,128)(2,1)S(1)}, u32[]{:S(2)}, u32[]{:S(2)}) collective-permute-start(bf16[32,1152]{1,0:T(8,128)(2,1)} %get-tuple-element.35), channel_id=1, source_target_pairs={{0,16},{16,0},{1,17},{17,1},{2,18},{18,2},{3,19},{19,3},{4,20},{20... | collective-permute-start | bytes 221192 | tf_op jit(solution)/shard_map/ppermute | solution.py:470
  5.7 16.2 %all-to-all-start = ((bf16[16,32,384]{2,1,0:T(8,128)(2,1)}), bf16[16,32,384]{2,1,0:T(8,128)(2,1)S(1)}, u32[]{:S(2)}, u32[]{:S(2)}) async-start(bf16[16,32,384]{2,1,0:T(8,128)(2,1)} %bitcast.23), calls=%async_computation | async-start | bytes 786432 | tf_op jit(solution)/shard_map/all_to_all | solution.py:466
  13.3 17.0 %collective-permute-start.1 = (bf16[144,1024]{1,0:T(8,128)(2,1)}, bf16[144,1024]{1,0:T(8,128)(2,1)S(1)}, u32[]{:S(2)}, u32[]{:S(2)}) collective-permute-start(bf16[144,1024]{1,0:T(8,128)(2,1)} %get-tuple-element.40.refs_0_), channel_id=1, source_target_pairs={{0,4},{4,0},{8,12},{12,8},{1,5},{5,1},{9,13},{13,9},{2,6},{6,2},{1... | collective-permute-start | bytes 884744 | tf_op jit(solution)/shard_map/ppermute | solution.py:470
  14.7 15.6 %collective-permute-start.3 = (bf16[144,1024]{1,0:T(8,128)(2,1)}, bf16[144,1024]{1,0:T(8,128)(2,1)S(1)}, u32[]{:S(2)}, u32[]{:S(2)}) collective-permute-start(bf16[144,1024]{1,0:T(8,128)(2,1)} %get-tuple-element.40.refs_0_), channel_id=1, source_target_pairs={{0,12},{4,8},{8,4},{12,0},{1,13},{5,9},{9,5},{13,1},{2,14},{6,10},... | collective-permute-start | bytes 884744 | tf_op jit(solution)/shard_map/ppermute | solution.py:470
  21.9 9.8 %collective-permute-start.2 = (bf16[144,1024]{1,0:T(8,128)(2,1)}, bf16[144,1024]{1,0:T(8,128)(2,1)S(1)}, u32[]{:S(2)}, u32[]{:S(2)}) collective-permute-start(bf16[144,1024]{1,0:T(8,128)(2,1)} %get-tuple-element.40.refs_0_), channel_id=1, source_target_pairs={{0,8},{4,12},{8,0},{12,4},{1,9},{5,13},{9,1},{13,5},{2,10},{6,14},... | collective-permute-start | bytes 884744 | tf_op jit(solution)/shard_map/ppermute | solution.py:470
  24.5 8.7 %collective-permute-start.9 = (bf16[2,32,2176]{2,1,0:T(8,128)(2,1)S(1)}, bf16[2,32,2176]{2,1,0:T(8,128)(2,1)S(1)}, u32[]{:S(2)}, u32[]{:S(2)}) collective-permute-start(bf16[2,32,2176]{2,1,0:T(8,128)(2,1)S(1)} %attach_sources.1.mine_ref), channel_id=1, source_target_pairs={{0,1},{1,0},{2,3},{3,2},{4,5},{5,4},{6,7},{7,6},{8,9},{9,8},{10,11... | collective-permute-start | bytes 835592 | tf_op jit(solution)/shard_map/ppermute | solution.py:470
  25.8 15.6 %collective-permute-start.8 = (bf16[16,32,384]{2,1,0:T(8,128)(2,1)S(1)}, bf16[16,32,384]{2,1,0:T(8,128)(2,1)S(1)}, u32[]{:S(2)}, u32[]{:S(2)}) collective-permute-start(bf16[16,32,384]{2,1,0:T(8,128)(2,1)S(1)} %all-to-all-done.refs_0_), channel_id=1, source_target_pairs={{0,1},{1,0},{2,3},{3,2},{4,5},{5,4},{6,7},{7,6},{8,9},{9,8},{10,11... | collective-permute-start | bytes 1179656 | tf_op jit(solution)/shard_map/ppermute | solution.py:470
  31.7 2.6 %collective-permute-start.6 = (bf16[144,1024]{1,0:T(8,128)(2,1)S(1)}, bf16[144,1024]{1,0:T(8,128)(2,1)S(1)}, u32[]{:S(2)}, u32[]{:S(2)}) collective-permute-start(bf16[144,1024]{1,0:T(8,128)(2,1)S(1)} %collective-permute-done.2.refs_2_), channel_id=1, source_target_pairs={{0,2},{2,0},{1,3},{3,1},{4,6},{6,4},{5,7},{7,5},{8,10},{10,8},{9,1... | collective-permute-start | bytes 884744 | tf_op jit(solution)/shard_map/ppermute | solution.py:470
  32.7 3.1 %collective-permute-start.4 = (bf16[144,1024]{1,0:T(8,128)(2,1)}, bf16[144,1024]{1,0:T(8,128)(2,1)S(1)}, u32[]{:S(2)}, u32[]{:S(2)}) collective-permute-start(bf16[144,1024]{1,0:T(8,128)(2,1)} %get-tuple-element.40.refs_0_), channel_id=1, source_target_pairs={{0,2},{2,0},{1,3},{3,1},{4,6},{6,4},{5,7},{7,5},{8,10},{10,8},{9,1... | collective-permute-start | bytes 884744 | tf_op jit(solution)/shard_map/ppermute | solution.py:470
  32.7 3.6 %collective-permute-start.5 = (bf16[144,1024]{1,0:T(8,128)(2,1)S(1)}, bf16[144,1024]{1,0:T(8,128)(2,1)S(1)}, u32[]{:S(2)}, u32[]{:S(2)}) collective-permute-start(bf16[144,1024]{1,0:T(8,128)(2,1)S(1)} %collective-permute-done.1.refs_1_), channel_id=1, source_target_pairs={{0,2},{2,0},{1,3},{3,1},{4,6},{6,4},{5,7},{7,5},{8,10},{10,8},{9,1... | collective-permute-start | bytes 884744 | tf_op jit(solution)/shard_map/ppermute | solution.py:470
  33.2 4.4 %collective-permute-start.7 = (bf16[144,1024]{1,0:T(8,128)(2,1)S(1)}, bf16[144,1024]{1,0:T(8,128)(2,1)S(1)}, u32[]{:S(2)}, u32[]{:S(2)}) collective-permute-start(bf16[144,1024]{1,0:T(8,128)(2,1)S(1)} %collective-permute-done.3.refs_3_), channel_id=1, source_target_pairs={{0,2},{2,0},{1,3},{3,1},{4,6},{6,4},{5,7},{7,5},{8,10},{10,8},{9,1... | collective-permute-start | bytes 884744 | tf_op jit(solution)/shard_map/ppermute | solution.py:470
  34.3 25.0 %collective-permute-start.10 = (bf16[2,64,1152]{2,1,0:T(8,128)(2,1)S(1)}, bf16[2,64,1152]{2,1,0:T(8,128)(2,1)S(1)}, u32[]{:S(2)}, u32[]{:S(2)}) collective-permute-start(bf16[2,64,1152]{2,1,0:T(8,128)(2,1)S(1)} %bitcast.17), channel_id=1, source_target_pairs={{0,4},{4,0},{8,12},{12,8},{1,5},{5,1},{9,13},{13,9},{2,6},{6,2},{1... | collective-permute-start | bytes 884744 | tf_op jit(solution)/shard_map/ppermute | solution.py:470
  35.9 23.5 %collective-permute-start.11 = (bf16[2,64,1152]{2,1,0:T(8,128)(2,1)S(1)}, bf16[2,64,1152]{2,1,0:T(8,128)(2,1)S(1)}, u32[]{:S(2)}, u32[]{:S(2)}) collective-permute-start(bf16[2,64,1152]{2,1,0:T(8,128)(2,1)S(1)} %bitcast.18), channel_id=1, source_target_pairs={{0,8},{4,12},{8,0},{12,4},{1,9},{5,13},{9,1},{13,5},{2,10},{6,14},... | collective-permute-start | bytes 884744 | tf_op jit(solution)/shard_map/ppermute | solution.py:470
  36.4 23.0 %collective-permute-start.12 = (bf16[2,64,1152]{2,1,0:T(8,128)(2,1)S(1)}, bf16[2,64,1152]{2,1,0:T(8,128)(2,1)S(1)}, u32[]{:S(2)}, u32[]{:S(2)}) collective-permute-start(bf16[2,64,1152]{2,1,0:T(8,128)(2,1)S(1)} %bitcast.19), channel_id=1, source_target_pairs={{0,12},{4,8},{8,4},{12,0},{1,13},{5,9},{9,5},{13,1},{2,14},{6,10},... | collective-permute-start | bytes 884744 | tf_op jit(solution)/shard_map/ppermute | solution.py:470
  37.6 1.0 copy-start.1
  42.7 7.1 %collective-permute-start.13 = (bf16[128,256]{1,0:T(8,128)(2,1)S(1)}, bf16[128,256]{1,0:T(8,128)(2,1)S(1)}, u32[]{:S(2)}, u32[]{:S(2)}) collective-permute-start(bf16[128,256]{1,0:T(8,128)(2,1)S(1)} %get-tuple-element.55), channel_id=1, source_target_pairs={{0,16},{16,0},{1,17},{17,1},{2,18},{18,2},{3,19},{19,3},{4,20},{20... | collective-permute-start | bytes 196616 | tf_op jit(solution)/shard_map/ppermute | solution.py:470
  51.2 15.0 %all-to-all-start.1 = ((bf16[16,64,128]{2,1,0:T(8,128)(2,1)}), bf16[16,64,128]{2,1,0:T(8,128)(2,1)S(1)}, u32[]{:S(2)}, u32[]{:S(2)}) async-start(bf16[16,64,128]{2,1,0:T(8,128)(2,1)} %bitcast.5), calls=%async_computation.1 | async-start | bytes 524288 | tf_op jit(solution)/shard_map/all_to_all | solution.py:466
  59.3 6.9 %copy-start.2 = (bf16[1,64,1024]{2,1,0:T(8,128)(2,1)S(1)}, bf16[1,64,1024]{2,1,0:T(8,128)(2,1)}, u32[]{:S(2)}) copy-start(bf16[1,64,1024]{2,1,0:T(8,128)(2,1)} %get-tuple-element.60.refs_0_) | copy-start | bytes 393220
  59.3 6.9 %copy-start.3 = (f32[128]{0:T(128)S(1)}, f32[128]{0:T(128)}, u32[]{:S(2)}) copy-start(f32[128]{0:T(128)} %param.12) | copy-start | bytes 1540
  59.4 1.6 %collective-permute-start.14 = (bf16[2,64,1152]{2,1,0:T(8,128)(2,1)S(1)}, bf16[2,64,1152]{2,1,0:T(8,128)(2,1)S(1)}, u32[]{:S(2)}, u32[]{:S(2)}) collective-permute-start(bf16[2,64,1152]{2,1,0:T(8,128)(2,1)S(1)} %bitcast.20), channel_id=1, source_target_pairs={{0,2},{2,0},{1,3},{3,1},{4,6},{6,4},{5,7},{7,5},{8,10},{10,8},{9,1... | collective-permute-start | bytes 884744 | tf_op jit(solution)/shard_map/ppermute | solution.py:470
  59.6 1.9 %collective-permute-start.15 = (bf16[2,64,1152]{2,1,0:T(8,128)(2,1)S(1)}, bf16[2,64,1152]{2,1,0:T(8,128)(2,1)S(1)}, u32[]{:S(2)}, u32[]{:S(2)}) collective-permute-start(bf16[2,64,1152]{2,1,0:T(8,128)(2,1)S(1)} %collective-permute-done.10.refs_1_), channel_id=1, source_target_pairs={{0,2},{2,0},{1,3},{3,1},{4,6},{6,4},{5,7},{7,5},{8,10},{10,8},{9,1... | collective-permute-start | bytes 884744 | tf_op jit(solution)/shard_map/ppermute | solution.py:470
  60.0 1.9 %collective-permute-start.16 = (bf16[2,64,1152]{2,1,0:T(8,128)(2,1)S(1)}, bf16[2,64,1152]{2,1,0:T(8,128)(2,1)S(1)}, u32[]{:S(2)}, u32[]{:S(2)}) collective-permute-start(bf16[2,64,1152]{2,1,0:T(8,128)(2,1)S(1)} %collective-permute-done.11.refs_2_), channel_id=1, source_target_pairs={{0,2},{2,0},{1,3},{3,1},{4,6},{6,4},{5,7},{7,5},{8,10},{10,8},{9,1... | collective-permute-start | bytes 884744 | tf_op jit(solution)/shard_map/ppermute | solution.py:470
  60.1 2.2 %collective-permute-start.17 = (bf16[2,64,1152]{2,1,0:T(8,128)(2,1)S(1)}, bf16[2,64,1152]{2,1,0:T(8,128)(2,1)S(1)}, u32[]{:S(2)}, u32[]{:S(2)}) collective-permute-start(bf16[2,64,1152]{2,1,0:T(8,128)(2,1)S(1)} %collective-permute-done.12.refs_3_), channel_id=1, source_target_pairs={{0,2},{2,0},{1,3},{3,1},{4,6},{6,4},{5,7},{7,5},{8,10},{10,8},{9,1... | collective-permute-start | bytes 884744 | tf_op jit(solution)/shard_map/ppermute | solution.py:470
  69.9 15.2 %copy-start = (bf16[1024,1024]{1,0:T(8,128)(2,1)S(1)}, bf16[1024,1024]{1,0:T(8,128)(2,1)}, u32[]{:S(2)}) copy-start(bf16[1024,1024]{1,0:T(8,128)(2,1)} %get-tuple-element.44.normed_any.normed_ref) | copy-start | bytes 6291460
  85.1 6.3 %collective-permute-start.18 = (bf16[128,256]{1,0:T(8,128)(2,1)S(1)}, bf16[128,256]{1,0:T(8,128)(2,1)S(1)}, u32[]{:S(2)}, u32[]{:S(2)}) collective-permute-start(bf16[128,256]{1,0:T(8,128)(2,1)S(1)} %get-tuple-element.64), channel_id=1, source_target_pairs={{0,16},{16,0},{1,17},{17,1},{2,18},{18,2},{3,19},{19,3},{4,20},{20... | collective-permute-start | bytes 196616 | tf_op jit(solution)/shard_map/ppermute | solution.py:470
  93.4 18.7 %all-to-all-start.3 = ((bf16[32,32,256]{2,1,0:T(8,128)(2,1)}), bf16[32,32,256]{2,1,0:T(8,128)(2,1)S(1)}, u32[]{:S(2)}, u32[]{:S(2)}) async-start(bf16[32,32,256]{2,1,0:T(8,128)(2,1)} %bitcast.9), calls=%async_computation.3 | async-start | bytes 1048576 | tf_op jit(solution)/shard_map/all_to_all | solution.py:466
  96.2 6.0 %collective-permute-start.19 = (f32[100,128]{1,0:T(8,128)S(1)}, f32[100,128]{1,0:T(8,128)S(1)}, u32[]{:S(2)}, u32[]{:S(2)}) collective-permute-start(f32[100,128]{1,0:T(8,128)S(1)} %get-tuple-element.66), channel_id=1, source_target_pairs={{0,1},{1,0},{2,3},{3,2},{4,5},{5,4},{6,7},{7,6},{8,9},{9,8},{10,11... | collective-permute-start | bytes 153608 | tf_op jit(solution)/shard_map/ppermute | solution.py:470

commit v25 on v24

--- a/solution.py
+++ b/solution.py
@@ -427,26 +427,22 @@
     out_ref[...] = both[:, : 2 * COLS] + both[:, 2 * COLS :]
 
 
-def rim_product_kernel(normed_any, total_ref, *refs):
-    arrived, (out_ref, rows, sems) = refs[:-3], refs[-3:]
-    last_row = normed_any.shape[0] - RIM
+def rim_product_kernel(normed_ref, total_ref, *refs):
+    arrived, out_ref = refs[:-1], refs[-1]
+    last_row = normed_ref.shape[0] - RIM
     half, last = lax.axis_index("half"), lax.axis_size("half") - 1
     if len(arrived) == 1:
         places = [pl.multiple_of(jnp.where(half == 0, last_row, 0), RIM)]
     else:
         places = [0, last_row]
-    wait(
-        fetch(
-            [(normed_any.at[pl.ds(place, RIM)], rows.at[at]) for at, place in enumerate(places)], sems
-        )
-    )
     total = total_ref[...]
     for at, arrived_ref in enumerate(arrived):
         grads = arrived_ref[...]
         if len(arrived) == 2:
             grads = jnp.where((half > 0) if at == 0 else (half < last), grads.astype(F32), 0.0)
             grads = grads.astype(BF16)
-        total += lax.dot_general(rows[at], grads, OVER_ROWS, preferred_element_type=F32)
+        rows = normed_ref[pl.ds(places[at], RIM), :]
+        total += lax.dot_general(rows, grads, OVER_ROWS, preferred_element_type=F32)
     out_ref[...] = total.astype(BF16)
 
 
@@ -682,8 +678,6 @@
         "product",
         [((LATENT_DIM, 2 * COLS), F32)],
         "vv",
-        flops=rows * LATENT_DIM * 8 * COLS,
-        moved=2**22,
         room=16,
     )(normed, kv_grads)
     arrived = [from_low] if halves == 2 else [from_low, from_high]
@@ -691,10 +685,10 @@
         rim_product_kernel,
         "product_rims",
         [((LATENT_DIM, 2 * COLS), BF16)],
-        "hv" + "v" * len(arrived),
-        [pltpu.VMEM((len(arrived), RIM, LATENT_DIM), BF16), pltpu.SemaphoreType.DMA((2,))],
+        "vv" + "v" * len(arrived),
         flops=RIM * LATENT_DIM * 4 * COLS,
         moved=2**21,
+        room=16,
     )(normed, total, *arrived)
     term, prediction = lax.optimization_barrier((term, prediction))
     term = exchange(term.reshape(-1, shard, 2 * COLS), everyone)

time: 114 us -> 109 us (0.956)
  waiting for transfers between devices: 37.5 us -> 33.5 us
    ppermute x20, waiting for transfers between devices: 20 us -> 16.2 us  [swap(): lax.ppermute(value, axis, [(i, i ^ step) for i in range(lax.axis_size(axi...]
  transfers between devices with their start and end apart: 23 -> 23, of which waited for: 14 -> 14; matrix products, arithmetic and copies ran while one was open for 2% -> 2% of each run, Pallas kernels for 13% -> 17%
where the time goes in v25:
time: 109 us; the launch traced here: 108 us
  starting transfers between devices  34 us (31%)
  waiting for transfers between devices  33.5 us (31%)
  Pallas kernels  27.2 us (25%)
  blocking collectives  9.89 us (9%)
  local copies, waits for them, and re-layouts  1.73 us (2%)
    pallas_call x16, Pallas kernels, run(): made(*[pltpu.with_memory_space_constraint(arg, pltpu.HBM) if space == 'h'...  27.2 us
    ppermute x20, starting transfers between devices, swap(): lax.ppermute(value, axis, [(i, i ^ step) for i in range(lax.axis_size(axi...  18.1 us
    all_to_all x3, waiting for transfers between devices, exchange(): return lax.all_to_all(chunks, axes, 0, 0)  17.3 us
    ppermute x20, waiting for transfers between devices, swap(): lax.ppermute(value, axis, [(i, i ^ step) for i in range(lax.axis_size(axi...  16.2 us
    all_to_all x3, starting transfers between devices, exchange(): return lax.all_to_all(chunks, axes, 0, 0)  15.9 us
    all_to_all x1, blocking collectives, exchange(): return lax.all_to_all(chunks, axes, 0, 0)  9.89 us
  transfers between devices with their start and end apart: 23, of which 14 were waited for; matrix products, arithmetic and copies ran while one was open for 2% of the time, Pallas kernels for 17%

profile of v25, /device:TPU:1, one launch (start us, length us, event | category | flops | bytes accessed | tf_op | source)
XLA Modules:
  0.0 108.2 jit_solution(2310760024966789300)
XLA Ops:
  0.6 1.8 %prepare_weights.1 = (bf16[2,8,1,32,384]{4,3,2,1,0:T(8,128)(2,1)}, bf16[32,1152]{1,0:T(8,128)(2,1)}) custom-call(bf16[32,3072]{1,0:T(8,128)(2,1)} %w_any.1, bf16[32,1024]{1,0:T(8,128)(2,1)} %mix_any.1, bf16[32,100]{1,0:T(8,128)(2,1)} %readout_any.1), custom_call_target="tpu_custom_call" | custom-call | bytes 1048576 | tf_op jit(solution)/shard_map/prepare_weights/pallas_call | solution.py:63
  2.5 3.2 %collective-permute-start = (bf16[32,1152]{1,0:T(8,128)(2,1)}, bf16[32,1152]{1,0:T(8,128)(2,1)S(1)}, u32[]{:S(2)}, u32[]{:S(2)}) collective-permute-start(bf16[32,1152]{1,0:T(8,128)(2,1)} %get-tuple-element.35), channel_id=1, source_target_pairs={{0,16},{16,0},{1,17},{17,1},{2,18},{18,2},{3,19},{19,3},{4,20},{20... | collective-permute-start | bytes 221192 | tf_op jit(solution)/shard_map/ppermute | solution.py:466
  5.7 4.8 %all-to-all-start = ((bf16[16,32,384]{2,1,0:T(8,128)(2,1)}), bf16[16,32,384]{2,1,0:T(8,128)(2,1)S(1)}, u32[]{:S(2)}, u32[]{:S(2)}) async-start(bf16[16,32,384]{2,1,0:T(8,128)(2,1)} %bitcast.23), calls=%async_computation | async-start | bytes 786432 | tf_op jit(solution)/shard_map/all_to_all | solution.py:462
  10.4 1.9 %norm.1 = (bf16[144,1024]{1,0:T(8,128)(2,1)}, bf16[1,64,1024]{2,1,0:T(8,128)(2,1)}, bf16[1,64,1024]{2,1,0:T(8,128)(2,1)}) custom-call(s32[2,4]{1,0:T(2,128)} %near_any.1, bf16[128,1024]{1,0:T(8,128)(2,1)} %bitcast.24), custom_call_target="tpu_custom_call" | custom-call | flops 1048576 | bytes 1048576 | tf_op jit(solution)/shard_map/norm/pallas_call | solution.py:63
  12.3 0.9 select_bitcast_fusion.1
  13.3 1.5 %collective-permute-start.1 = (bf16[144,1024]{1,0:T(8,128)(2,1)}, bf16[144,1024]{1,0:T(8,128)(2,1)S(1)}, u32[]{:S(2)}, u32[]{:S(2)}) collective-permute-start(bf16[144,1024]{1,0:T(8,128)(2,1)} %get-tuple-element.40.refs_0_), channel_id=1, source_target_pairs={{0,4},{4,0},{8,12},{12,8},{1,5},{5,1},{9,13},{13,9},{2,6},{6,2},{1... | collective-permute-start | bytes 884744 | tf_op jit(solution)/shard_map/ppermute | solution.py:466
  14.7 1.2 %collective-permute-start.3 = (bf16[144,1024]{1,0:T(8,128)(2,1)}, bf16[144,1024]{1,0:T(8,128)(2,1)S(1)}, u32[]{:S(2)}, u32[]{:S(2)}) collective-permute-start(bf16[144,1024]{1,0:T(8,128)(2,1)} %get-tuple-element.40.refs_0_), channel_id=1, source_target_pairs={{0,12},{4,8},{8,4},{12,0},{1,13},{5,9},{9,5},{13,1},{2,14},{6,10},... | collective-permute-start | bytes 884744 | tf_op jit(solution)/shard_map/ppermute | solution.py:466
  15.9 6.0 %all-to-all-done.refs_0_ = bf16[16,32,384]{2,1,0:T(8,128)(2,1)S(1)} async-done(((bf16[16,32,384]{2,1,0:T(8,128)(2,1)}), bf16[16,32,384]{2,1,0:T(8,128)(2,1)S(1)}, u32[]{:S(2)}, u32[]{:S(2)}) %all-to-all-start) | async-done | bytes 393248 | tf_op jit(solution)/shard_map/all_to_all | solution.py:462
  21.9 1.7 %collective-permute-start.2 = (bf16[144,1024]{1,0:T(8,128)(2,1)}, bf16[144,1024]{1,0:T(8,128)(2,1)S(1)}, u32[]{:S(2)}, u32[]{:S(2)}) collective-permute-start(bf16[144,1024]{1,0:T(8,128)(2,1)} %get-tuple-element.40.refs_0_), channel_id=1, source_target_pairs={{0,8},{4,12},{8,0},{12,4},{1,9},{5,13},{9,1},{13,5},{2,10},{6,14},... | collective-permute-start | bytes 884744 | tf_op jit(solution)/shard_map/ppermute | solution.py:466
  23.6 0.9 attach_sources.1.mine_ref
  24.5 1.3 %collective-permute-start.9 = (bf16[2,32,2176]{2,1,0:T(8,128)(2,1)S(1)}, bf16[2,32,2176]{2,1,0:T(8,128)(2,1)S(1)}, u32[]{:S(2)}, u32[]{:S(2)}) collective-permute-start(bf16[2,32,2176]{2,1,0:T(8,128)(2,1)S(1)} %attach_sources.1.mine_ref), channel_id=1, source_target_pairs={{0,1},{1,0},{2,3},{3,2},{4,5},{5,4},{6,7},{7,6},{8,9},{9,8},{10,11... | collective-permute-start | bytes 835592 | tf_op jit(solution)/shard_map/ppermute | solution.py:466
  26.0 4.3 %collective-permute-done.1.refs_1_ = bf16[144,1024]{1,0:T(8,128)(2,1)S(1)} collective-permute-done((bf16[144,1024]{1,0:T(8,128)(2,1)}, bf16[144,1024]{1,0:T(8,128)(2,1)S(1)}, u32[]{:S(2)}, u32[]{:S(2)}) %collective-permute-start.1) | collective-permute-done | bytes 294944 | tf_op jit(solution)/shard_map/ppermute | solution.py:466
  30.3 1.4 %collective-permute-done.2.refs_2_ = bf16[144,1024]{1,0:T(8,128)(2,1)S(1)} collective-permute-done((bf16[144,1024]{1,0:T(8,128)(2,1)}, bf16[144,1024]{1,0:T(8,128)(2,1)S(1)}, u32[]{:S(2)}, u32[]{:S(2)}) %collective-permute-start.2) | collective-permute-done | bytes 294944 | tf_op jit(solution)/shard_map/ppermute | solution.py:466
  31.7 1.0 collective-permute-start.6
  32.7 0.5 collective-permute-start.5
  33.2 0.7 collective-permute-start.7
  34.3 1.5 %collective-permute-start.10 = (bf16[2,64,1152]{2,1,0:T(8,128)(2,1)S(1)}, bf16[2,64,1152]{2,1,0:T(8,128)(2,1)S(1)}, u32[]{:S(2)}, u32[]{:S(2)}) collective-permute-start(bf16[2,64,1152]{2,1,0:T(8,128)(2,1)S(1)} %bitcast.17), channel_id=1, source_target_pairs={{0,4},{4,0},{8,12},{12,8},{1,5},{5,1},{9,13},{13,9},{2,6},{6,2},{1... | collective-permute-start | bytes 884744 | tf_op jit(solution)/shard_map/ppermute | solution.py:466
  35.9 0.5 collective-permute-start.11
  36.4 1.3 %collective-permute-start.12 = (bf16[2,64,1152]{2,1,0:T(8,128)(2,1)S(1)}, bf16[2,64,1152]{2,1,0:T(8,128)(2,1)S(1)}, u32[]{:S(2)}, u32[]{:S(2)}) collective-permute-start(bf16[2,64,1152]{2,1,0:T(8,128)(2,1)S(1)} %bitcast.19), channel_id=1, source_target_pairs={{0,12},{4,8},{8,4},{12,0},{1,13},{5,9},{9,5},{13,1},{2,14},{6,10},... | collective-permute-start | bytes 884744 | tf_op jit(solution)/shard_map/ppermute | solution.py:466
  37.6 1.0 copy-done.1
  38.6 1.5 %collect.1 = (bf16[1024,1024]{1,0:T(8,128)(2,1)}, f32[8,16,128]{2,1,0:T(8,128)S(1)}) custom-call(bf16[144,1024]{1,0:T(8,128)(2,1)S(1)} %copy-done.1, bf16[144,1024]{1,0:T(8,128)(2,1)S(1)} %collective-permute-done.1.refs_1_, bf16[144,1024]{1,0:T(8,128)(2,1)S(1)} %collective-permute-done.2.refs_2_, bf16[144,1024]{1,0:T(8,128)(2,1)S(1)} %collective-permute-done.3.refs_3_, ...), custom_call_target="tpu_custom_call" | custom-call | bytes 4194304 | tf_op jit(solution)/shard_map/collect/pallas_call | solution.py:63
  40.1 1.3 %collective-permute-done.8.refs_1_ = bf16[16,32,384]{2,1,0:T(8,128)(2,1)S(1)} collective-permute-done((bf16[16,32,384]{2,1,0:T(8,128)(2,1)S(1)}, bf16[16,32,384]{2,1,0:T(8,128)(2,1)S(1)}, u32[]{:S(2)}, u32[]{:S(2)}) %collective-permute-start.8) | collective-permute-done | bytes 393248 | tf_op jit(solution)/shard_map/ppermute | solution.py:466
  41.4 1.3 %project_rims.1 = (bf16[16,2,32,384]{3,2,1,0:T(8,128)(2,1)S(1)}, bf16[128,256]{1,0:T(8,128)(2,1)S(1)}) custom-call(bf16[1024,1024]{1,0:T(8,128)(2,1)} %get-tuple-element.44.normed_any.normed_ref, bf16[16,32,384]{2,1,0:T(8,128)(2,1)S(1)} %all-to-all-done.refs_0_, bf16[16,32,384]{2,1,0:T(8,128)(2,1)S(1)} %collective-permute-done.8.refs_1_), custom_call_target="tpu_custom_call" | custom-call | flops 67108864 | bytes 1048576 | tf_op jit(solution)/shard_map/project_rims/pallas_call | solution.py:63
  42.7 0.9 collective-permute-start.13
  43.6 2.8 %project.1 = (bf16[1024,128]{1,0:T(8,128)(2,1)S(1)}, bf16[1024,256]{1,0:T(8,128)(2,1)S(1)}) custom-call(bf16[1024,1024]{1,0:T(8,128)(2,1)} %get-tuple-element.44.normed_any.normed_ref, bf16[16,2,32,384]{3,2,1,0:T(8,128)(2,1)S(1)} %get-tuple-element.47.w_ref), custom_call_target="tpu_custom_call" | custom-call | flops 805306368 | bytes 4194304 | tf_op jit(solution)/shard_map/project/pallas_call | solution.py:63
  46.5 1.9 %attention_interior.1.done_ref = bf16[1024,128]{1,0:T(8,128)(2,1)S(1)} custom-call(f32[8,16,128]{2,1,0:T(8,128)S(1)} %get-tuple-element.45.steps_ref, bf16[1024,128]{1,0:T(8,128)(2,1)S(1)} %get-tuple-element.48.q_ref, bf16[1024,256]{1,0:T(8,128)(2,1)S(1)} %get-tuple-element.54.kv_ref), custom_call_target="tpu_custom_call" | custom-call | flops 268435456 | bytes 2097152 | tf_op jit(solution)/shard_map/attention_interior/pallas_call | solution.py:63
  48.3 1.4 %collective-permute-done.13.low_ref.high_ref = bf16[128,256]{1,0:T(8,128)(2,1)S(1)} collective-permute-done((bf16[128,256]{1,0:T(8,128)(2,1)S(1)}, bf16[128,256]{1,0:T(8,128)(2,1)S(1)}, u32[]{:S(2)}, u32[]{:S(2)}) %collective-permute-start.13) | collective-permute-done | bytes 65568 | tf_op jit(solution)/shard_map/ppermute | solution.py:466
  49.8 1.4 %attention_edges.1 = bf16[1024,128]{1,0:T(8,128)(2,1)} custom-call(f32[8,16,128]{2,1,0:T(8,128)S(1)} %get-tuple-element.45.steps_ref, bf16[1024,128]{1,0:T(8,128)(2,1)S(1)} %get-tuple-element.48.q_ref, bf16[1024,256]{1,0:T(8,128)(2,1)S(1)} %get-tuple-element.54.kv_ref, bf16[128,256]{1,0:T(8,128)(2,1)S(1)} %collective-permute-done.13.low_ref.high_ref, ...), custom_call_target="tpu_custom_call" | custom-call | flops 67108864 | bytes 1048576 | tf_op jit(solution)/shard_map/attention_edges/pallas_call | solution.py:63
  51.2 8.1 %all-to-all-start.1 = ((bf16[16,64,128]{2,1,0:T(8,128)(2,1)}), bf16[16,64,128]{2,1,0:T(8,128)(2,1)S(1)}, u32[]{:S(2)}, u32[]{:S(2)}) async-start(bf16[16,64,128]{2,1,0:T(8,128)(2,1)} %bitcast.5), calls=%async_computation.1 | async-start | bytes 524288 | tf_op jit(solution)/shard_map/all_to_all | solution.py:462
  60.5 0.6 collective-permute-done.14.refs_4_
  61.0 0.4 collective-permute-done.15.refs_5_
  61.5 0.4 collective-permute-done.16.refs_6_
  61.9 0.4 collective-permute-done.17.refs_7_
  62.3 1.5 %assemble.1.w_any = bf16[2,4,2,64,1152]{4,3,2,1,0:T(8,128)(2,1)} custom-call(bf16[2,64,1152]{2,1,0:T(8,128)(2,1)S(1)} %bitcast.21, bf16[2,64,1152]{2,1,0:T(8,128)(2,1)S(1)} %collective-permute-done.10.refs_1_, bf16[2,64,1152]{2,1,0:T(8,128)(2,1)S(1)} %collective-permute-done.11.refs_2_, bf16[2,64,1152]{2,1,0:T(8,128)(2,1)S(1)} %collective-permute-done.12.refs_3_, ...), custom_call_target="tpu_custom_call" | custom-call | bytes 4194304 | tf_op jit(solution)/shard_map/assemble/pallas_call | solution.py:63
  63.8 2.4 %all-to-all-done.1.att_ref = bf16[16,64,128]{2,1,0:T(8,128)(2,1)S(1)} async-done(((bf16[16,64,128]{2,1,0:T(8,128)(2,1)}), bf16[16,64,128]{2,1,0:T(8,128)(2,1)S(1)}, u32[]{:S(2)}, u32[]{:S(2)}) %all-to-all-start.1) | async-done | bytes 262176 | tf_op jit(solution)/shard_map/all_to_all | solution.py:462
  66.2 3.7 %mix_loss_backward.1 = (f32[100,128]{1,0:T(8,128)S(1)}, bf16[16,64,128]{2,1,0:T(8,128)(2,1)S(1)}) custom-call(bf16[16,64,128]{2,1,0:T(8,128)(2,1)S(1)} %all-to-all-done.1.att_ref, f32[1,128]{1,0:T(1,128)S(1)} %bitcast.22, f32[100,128]{1,0:T(8,128)} %truth_any.1, bf16[2,4,2,64,1152]{4,3,2,1,0:T(8,128)(2,1)} %assemble.1.w_any, ...), custom_call_target="tpu_custom_call" | custom-call | flops 603979776 | bytes 4194304 | tf_op jit(solution)/shard_map/mix_loss_backward/pallas_call | solution.py:63
  69.9 9.9 %all_to_all.20 = bf16[16,64,128]{2,1,0:T(8,128)(2,1)S(1)} all-to-all(bf16[16,64,128]{2,1,0:T(8,128)(2,1)S(1)} %get-tuple-element.62), channel_id=1, replica_groups=mesh['half'=2,'quad'=4,'core'=2,'ens'=2] {'quad','core','ens'}, dimensions={0} | all-to-all | bytes 524288 | tf_op jit(solution)/shard_map/all_to_all | solution.py:462
  79.8 1.4 %attention_edges_back.1 = (f32[2,256,256]{2,1,0:T(8,128)S(1)}, bf16[128,256]{1,0:T(8,128)(2,1)S(1)}) custom-call(f32[8,16,128]{2,1,0:T(8,128)S(1)} %get-tuple-element.45.steps_ref, bf16[1024,128]{1,0:T(8,128)(2,1)S(1)} %get-tuple-element.48.q_ref, bf16[1024,256]{1,0:T(8,128)(2,1)S(1)} %get-tuple-element.54.kv_ref, ...), custom_call_target="tpu_custom_call" | custom-call | flops 167772160 | bytes 1048576 | tf_op jit(solution)/shard_map/attention_edges_back/pallas_call | solution.py:63
  81.3 3.8 %attention_interior_back.1.grads_ref = f32[1024,256]{1,0:T(8,128)S(1)} custom-call(f32[8,16,128]{2,1,0:T(8,128)S(1)} %get-tuple-element.45.steps_ref, bf16[1024,128]{1,0:T(8,128)(2,1)S(1)} %get-tuple-element.48.q_ref, bf16[1024,256]{1,0:T(8,128)(2,1)S(1)} %get-tuple-element.54.kv_ref, bf16[1024,128]{1,0:T(8,128)(2,1)S(1)} %bitcast.15, ...), custom_call_target="tpu_custom_call" | custom-call | flops 536870912 | bytes 4194304 | tf_op jit(solution)/shard_map/attention_interior_back/pallas_call | solution.py:63
  85.2 1.3 %product.1.total_ref = f32[1024,256]{1,0:T(8,128)S(1)} custom-call(bf16[1024,1024]{1,0:T(8,128)(2,1)S(1)} %copy-done, f32[1024,256]{1,0:T(8,128)S(1)} %attention_interior_back.1.grads_ref), custom_call_target="tpu_custom_call" | custom-call | tf_op jit(solution)/shard_map/product/pallas_call | solution.py:63
  86.5 1.0 collective-permute-done.18.refs_0_
  87.5 1.1 %product_rims.1 = bf16[1024,256]{1,0:T(8,128)(2,1)} custom-call(bf16[1024,1024]{1,0:T(8,128)(2,1)S(1)} %copy-done, f32[1024,256]{1,0:T(8,128)S(1)} %product.1.total_ref, bf16[128,256]{1,0:T(8,128)(2,1)S(1)} %collective-permute-done.18.refs_0_), custom_call_target="tpu_custom_call" | custom-call | flops 67108864 | bytes 2097152 | tf_op jit(solution)/shard_map/product_rims/pallas_call | solution.py:63
  88.6 3.0 %all-to-all-start.3 = ((bf16[32,32,256]{2,1,0:T(8,128)(2,1)}), bf16[32,32,256]{2,1,0:T(8,128)(2,1)S(1)}, u32[]{:S(2)}, u32[]{:S(2)}) async-start(bf16[32,32,256]{2,1,0:T(8,128)(2,1)} %bitcast.9), calls=%async_computation.3 | async-start | bytes 1048576 | tf_op jit(solution)/shard_map/all_to_all | solution.py:462
  91.6 1.5 %collective-permute-start.19 = (f32[100,128]{1,0:T(8,128)S(1)}, f32[100,128]{1,0:T(8,128)S(1)}, u32[]{:S(2)}, u32[]{:S(2)}) collective-permute-start(f32[100,128]{1,0:T(8,128)S(1)} %get-tuple-element.66), channel_id=1, source_target_pairs={{0,1},{1,0},{2,3},{3,2},{4,5},{5,4},{6,7},{7,6},{8,9},{9,8},{10,11... | collective-permute-start | bytes 153608 | tf_op jit(solution)/shard_map/ppermute | solution.py:466
  93.1 4.5 %collective-permute-done.19 = f32[100,128]{1,0:T(8,128)S(1)} collective-permute-done((f32[100,128]{1,0:T(8,128)S(1)}, f32[100,128]{1,0:T(8,128)S(1)}, u32[]{:S(2)}, u32[]{:S(2)}) %collective-permute-start.19) | collective-permute-done | bytes 51232 | tf_op jit(solution)/shard_map/ppermute | solution.py:466
  97.8 0.7 copy.9
  98.5 9.0 %all-to-all-done.3 = bf16[32,32,256]{2,1,0:T(8,128)(2,1)S(1)} async-done(((bf16[32,32,256]{2,1,0:T(8,128)(2,1)}), bf16[32,32,256]{2,1,0:T(8,128)(2,1)S(1)}, u32[]{:S(2)}, u32[]{:S(2)}) %all-to-all-start.3) | async-done | bytes 524320 | tf_op jit(solution)/shard_map/all_to_all | solution.py:462
  107.4 0.8 gather_sums.1
  (30 shorter events, 2.1 us)
Async XLA Ops:
  2.5 9.9 %collective-permute-start = (bf16[32,1152]{1,0:T(8,128)(2,1)}, bf16[32,1152]{1,0:T(8,128)(2,1)S(1)}, u32[]{:S(2)}, u32[]{:S(2)}) collective-permute-start(bf16[32,1152]{1,0:T(8,128)(2,1)} %get-tuple-element.35), channel_id=1, source_target_pairs={{0,16},{16,0},{1,17},{17,1},{2,18},{18,2},{3,19},{19,3},{4,20},{20... | collective-permute-start | bytes 221192 | tf_op jit(solution)/shard_map/ppermute | solution.py:466
  5.7 16.2 %all-to-all-start = ((bf16[16,32,384]{2,1,0:T(8,128)(2,1)}), bf16[16,32,384]{2,1,0:T(8,128)(2,1)S(1)}, u32[]{:S(2)}, u32[]{:S(2)}) async-start(bf16[16,32,384]{2,1,0:T(8,128)(2,1)} %bitcast.23), calls=%async_computation | async-start | bytes 786432 | tf_op jit(solution)/shard_map/all_to_all | solution.py:462
  13.3 17.0 %collective-permute-start.1 = (bf16[144,1024]{1,0:T(8,128)(2,1)}, bf16[144,1024]{1,0:T(8,128)(2,1)S(1)}, u32[]{:S(2)}, u32[]{:S(2)}) collective-permute-start(bf16[144,1024]{1,0:T(8,128)(2,1)} %get-tuple-element.40.refs_0_), channel_id=1, source_target_pairs={{0,4},{4,0},{8,12},{12,8},{1,5},{5,1},{9,13},{13,9},{2,6},{6,2},{1... | collective-permute-start | bytes 884744 | tf_op jit(solution)/shard_map/ppermute | solution.py:466
  14.7 15.6 %collective-permute-start.3 = (bf16[144,1024]{1,0:T(8,128)(2,1)}, bf16[144,1024]{1,0:T(8,128)(2,1)S(1)}, u32[]{:S(2)}, u32[]{:S(2)}) collective-permute-start(bf16[144,1024]{1,0:T(8,128)(2,1)} %get-tuple-element.40.refs_0_), channel_id=1, source_target_pairs={{0,12},{4,8},{8,4},{12,0},{1,13},{5,9},{9,5},{13,1},{2,14},{6,10},... | collective-permute-start | bytes 884744 | tf_op jit(solution)/shard_map/ppermute | solution.py:466
  21.9 9.8 %collective-permute-start.2 = (bf16[144,1024]{1,0:T(8,128)(2,1)}, bf16[144,1024]{1,0:T(8,128)(2,1)S(1)}, u32[]{:S(2)}, u32[]{:S(2)}) collective-permute-start(bf16[144,1024]{1,0:T(8,128)(2,1)} %get-tuple-element.40.refs_0_), channel_id=1, source_target_pairs={{0,8},{4,12},{8,0},{12,4},{1,9},{5,13},{9,1},{13,5},{2,10},{6,14},... | collective-permute-start | bytes 884744 | tf_op jit(solution)/shard_map/ppermute | solution.py:466
  24.5 8.7 %collective-permute-start.9 = (bf16[2,32,2176]{2,1,0:T(8,128)(2,1)S(1)}, bf16[2,32,2176]{2,1,0:T(8,128)(2,1)S(1)}, u32[]{:S(2)}, u32[]{:S(2)}) collective-permute-start(bf16[2,32,2176]{2,1,0:T(8,128)(2,1)S(1)} %attach_sources.1.mine_ref), channel_id=1, source_target_pairs={{0,1},{1,0},{2,3},{3,2},{4,5},{5,4},{6,7},{7,6},{8,9},{9,8},{10,11... | collective-permute-start | bytes 835592 | tf_op jit(solution)/shard_map/ppermute | solution.py:466
  25.8 15.6 %collective-permute-start.8 = (bf16[16,32,384]{2,1,0:T(8,128)(2,1)S(1)}, bf16[16,32,384]{2,1,0:T(8,128)(2,1)S(1)}, u32[]{:S(2)}, u32[]{:S(2)}) collective-permute-start(bf16[16,32,384]{2,1,0:T(8,128)(2,1)S(1)} %all-to-all-done.refs_0_), channel_id=1, source_target_pairs={{0,1},{1,0},{2,3},{3,2},{4,5},{5,4},{6,7},{7,6},{8,9},{9,8},{10,11... | collective-permute-start | bytes 1179656 | tf_op jit(solution)/shard_map/ppermute | solution.py:466
  31.7 2.6 %collective-permute-start.6 = (bf16[144,1024]{1,0:T(8,128)(2,1)S(1)}, bf16[144,1024]{1,0:T(8,128)(2,1)S(1)}, u32[]{:S(2)}, u32[]{:S(2)}) collective-permute-start(bf16[144,1024]{1,0:T(8,128)(2,1)S(1)} %collective-permute-done.2.refs_2_), channel_id=1, source_target_pairs={{0,2},{2,0},{1,3},{3,1},{4,6},{6,4},{5,7},{7,5},{8,10},{10,8},{9,1... | collective-permute-start | bytes 884744 | tf_op jit(solution)/shard_map/ppermute | solution.py:466
  32.7 3.1 %collective-permute-start.4 = (bf16[144,1024]{1,0:T(8,128)(2,1)}, bf16[144,1024]{1,0:T(8,128)(2,1)S(1)}, u32[]{:S(2)}, u32[]{:S(2)}) collective-permute-start(bf16[144,1024]{1,0:T(8,128)(2,1)} %get-tuple-element.40.refs_0_), channel_id=1, source_target_pairs={{0,2},{2,0},{1,3},{3,1},{4,6},{6,4},{5,7},{7,5},{8,10},{10,8},{9,1... | collective-permute-start | bytes 884744 | tf_op jit(solution)/shard_map/ppermute | solution.py:466
  32.7 3.6 %collective-permute-start.5 = (bf16[144,1024]{1,0:T(8,128)(2,1)S(1)}, bf16[144,1024]{1,0:T(8,128)(2,1)S(1)}, u32[]{:S(2)}, u32[]{:S(2)}) collective-permute-start(bf16[144,1024]{1,0:T(8,128)(2,1)S(1)} %collective-permute-done.1.refs_1_), channel_id=1, source_target_pairs={{0,2},{2,0},{1,3},{3,1},{4,6},{6,4},{5,7},{7,5},{8,10},{10,8},{9,1... | collective-permute-start | bytes 884744 | tf_op jit(solution)/shard_map/ppermute | solution.py:466
  33.2 4.4 %collective-permute-start.7 = (bf16[144,1024]{1,0:T(8,128)(2,1)S(1)}, bf16[144,1024]{1,0:T(8,128)(2,1)S(1)}, u32[]{:S(2)}, u32[]{:S(2)}) collective-permute-start(bf16[144,1024]{1,0:T(8,128)(2,1)S(1)} %collective-permute-done.3.refs_3_), channel_id=1, source_target_pairs={{0,2},{2,0},{1,3},{3,1},{4,6},{6,4},{5,7},{7,5},{8,10},{10,8},{9,1... | collective-permute-start | bytes 884744 | tf_op jit(solution)/shard_map/ppermute | solution.py:466
  34.3 25.0 %collective-permute-start.10 = (bf16[2,64,1152]{2,1,0:T(8,128)(2,1)S(1)}, bf16[2,64,1152]{2,1,0:T(8,128)(2,1)S(1)}, u32[]{:S(2)}, u32[]{:S(2)}) collective-permute-start(bf16[2,64,1152]{2,1,0:T(8,128)(2,1)S(1)} %bitcast.17), channel_id=1, source_target_pairs={{0,4},{4,0},{8,12},{12,8},{1,5},{5,1},{9,13},{13,9},{2,6},{6,2},{1... | collective-permute-start | bytes 884744 | tf_op jit(solution)/shard_map/ppermute | solution.py:466
  35.9 23.5 %collective-permute-start.11 = (bf16[2,64,1152]{2,1,0:T(8,128)(2,1)S(1)}, bf16[2,64,1152]{2,1,0:T(8,128)(2,1)S(1)}, u32[]{:S(2)}, u32[]{:S(2)}) collective-permute-start(bf16[2,64,1152]{2,1,0:T(8,128)(2,1)S(1)} %bitcast.18), channel_id=1, source_target_pairs={{0,8},{4,12},{8,0},{12,4},{1,9},{5,13},{9,1},{13,5},{2,10},{6,14},... | collective-permute-start | bytes 884744 | tf_op jit(solution)/shard_map/ppermute | solution.py:466
  36.4 23.0 %collective-permute-start.12 = (bf16[2,64,1152]{2,1,0:T(8,128)(2,1)S(1)}, bf16[2,64,1152]{2,1,0:T(8,128)(2,1)S(1)}, u32[]{:S(2)}, u32[]{:S(2)}) collective-permute-start(bf16[2,64,1152]{2,1,0:T(8,128)(2,1)S(1)} %bitcast.19), channel_id=1, source_target_pairs={{0,12},{4,8},{8,4},{12,0},{1,13},{5,9},{9,5},{13,1},{2,14},{6,10},... | collective-permute-start | bytes 884744 | tf_op jit(solution)/shard_map/ppermute | solution.py:466
  37.6 1.0 copy-start.1
  42.7 7.1 %collective-permute-start.13 = (bf16[128,256]{1,0:T(8,128)(2,1)S(1)}, bf16[128,256]{1,0:T(8,128)(2,1)S(1)}, u32[]{:S(2)}, u32[]{:S(2)}) collective-permute-start(bf16[128,256]{1,0:T(8,128)(2,1)S(1)} %get-tuple-element.55), channel_id=1, source_target_pairs={{0,16},{16,0},{1,17},{17,1},{2,18},{18,2},{3,19},{19,3},{4,20},{20... | collective-permute-start | bytes 196616 | tf_op jit(solution)/shard_map/ppermute | solution.py:466
  51.2 15.0 %all-to-all-start.1 = ((bf16[16,64,128]{2,1,0:T(8,128)(2,1)}), bf16[16,64,128]{2,1,0:T(8,128)(2,1)S(1)}, u32[]{:S(2)}, u32[]{:S(2)}) async-start(bf16[16,64,128]{2,1,0:T(8,128)(2,1)} %bitcast.5), calls=%async_computation.1 | async-start | bytes 524288 | tf_op jit(solution)/shard_map/all_to_all | solution.py:462
  59.3 6.9 %copy-start.2 = (bf16[1,64,1024]{2,1,0:T(8,128)(2,1)S(1)}, bf16[1,64,1024]{2,1,0:T(8,128)(2,1)}, u32[]{:S(2)}) copy-start(bf16[1,64,1024]{2,1,0:T(8,128)(2,1)} %get-tuple-element.60.refs_0_) | copy-start | bytes 393220
  59.3 6.9 %copy-start.3 = (f32[128]{0:T(128)S(1)}, f32[128]{0:T(128)}, u32[]{:S(2)}) copy-start(f32[128]{0:T(128)} %param.12) | copy-start | bytes 1540
  59.4 1.6 %collective-permute-start.14 = (bf16[2,64,1152]{2,1,0:T(8,128)(2,1)S(1)}, bf16[2,64,1152]{2,1,0:T(8,128)(2,1)S(1)}, u32[]{:S(2)}, u32[]{:S(2)}) collective-permute-start(bf16[2,64,1152]{2,1,0:T(8,128)(2,1)S(1)} %bitcast.20), channel_id=1, source_target_pairs={{0,2},{2,0},{1,3},{3,1},{4,6},{6,4},{5,7},{7,5},{8,10},{10,8},{9,1... | collective-permute-start | bytes 884744 | tf_op jit(solution)/shard_map/ppermute | solution.py:466
  59.6 1.9 %collective-permute-start.15 = (bf16[2,64,1152]{2,1,0:T(8,128)(2,1)S(1)}, bf16[2,64,1152]{2,1,0:T(8,128)(2,1)S(1)}, u32[]{:S(2)}, u32[]{:S(2)}) collective-permute-start(bf16[2,64,1152]{2,1,0:T(8,128)(2,1)S(1)} %collective-permute-done.10.refs_1_), channel_id=1, source_target_pairs={{0,2},{2,0},{1,3},{3,1},{4,6},{6,4},{5,7},{7,5},{8,10},{10,8},{9,1... | collective-permute-start | bytes 884744 | tf_op jit(solution)/shard_map/ppermute | solution.py:466
  60.0 1.9 %collective-permute-start.16 = (bf16[2,64,1152]{2,1,0:T(8,128)(2,1)S(1)}, bf16[2,64,1152]{2,1,0:T(8,128)(2,1)S(1)}, u32[]{:S(2)}, u32[]{:S(2)}) collective-permute-start(bf16[2,64,1152]{2,1,0:T(8,128)(2,1)S(1)} %collective-permute-done.11.refs_2_), channel_id=1, source_target_pairs={{0,2},{2,0},{1,3},{3,1},{4,6},{6,4},{5,7},{7,5},{8,10},{10,8},{9,1... | collective-permute-start | bytes 884744 | tf_op jit(solution)/shard_map/ppermute | solution.py:466
  60.1 2.2 %collective-permute-start.17 = (bf16[2,64,1152]{2,1,0:T(8,128)(2,1)S(1)}, bf16[2,64,1152]{2,1,0:T(8,128)(2,1)S(1)}, u32[]{:S(2)}, u32[]{:S(2)}) collective-permute-start(bf16[2,64,1152]{2,1,0:T(8,128)(2,1)S(1)} %collective-permute-done.12.refs_3_), channel_id=1, source_target_pairs={{0,2},{2,0},{1,3},{3,1},{4,6},{6,4},{5,7},{7,5},{8,10},{10,8},{9,1... | collective-permute-start | bytes 884744 | tf_op jit(solution)/shard_map/ppermute | solution.py:466
  69.9 15.2 %copy-start = (bf16[1024,1024]{1,0:T(8,128)(2,1)S(1)}, bf16[1024,1024]{1,0:T(8,128)(2,1)}, u32[]{:S(2)}) copy-start(bf16[1024,1024]{1,0:T(8,128)(2,1)} %get-tuple-element.44.normed_any.normed_ref) | copy-start | bytes 6291460
  81.2 6.3 %collective-permute-start.18 = (bf16[128,256]{1,0:T(8,128)(2,1)S(1)}, bf16[128,256]{1,0:T(8,128)(2,1)S(1)}, u32[]{:S(2)}, u32[]{:S(2)}) collective-permute-start(bf16[128,256]{1,0:T(8,128)(2,1)S(1)} %get-tuple-element.64), channel_id=1, source_target_pairs={{0,16},{16,0},{1,17},{17,1},{2,18},{18,2},{3,19},{19,3},{4,20},{20... | collective-permute-start | bytes 196616 | tf_op jit(solution)/shard_map/ppermute | solution.py:466
  88.6 18.8 %all-to-all-start.3 = ((bf16[32,32,256]{2,1,0:T(8,128)(2,1)}), bf16[32,32,256]{2,1,0:T(8,128)(2,1)S(1)}, u32[]{:S(2)}, u32[]{:S(2)}) async-start(bf16[32,32,256]{2,1,0:T(8,128)(2,1)} %bitcast.9), calls=%async_computation.3 | async-start | bytes 1048576 | tf_op jit(solution)/shard_map/all_to_all | solution.py:462
  91.6 6.0 %collective-permute-start.19 = (f32[100,128]{1,0:T(8,128)S(1)}, f32[100,128]{1,0:T(8,128)S(1)}, u32[]{:S(2)}, u32[]{:S(2)}) collective-permute-start(f32[100,128]{1,0:T(8,128)S(1)} %get-tuple-element.66), channel_id=1, source_target_pairs={{0,1},{1,0},{2,3},{3,2},{4,5},{5,4},{6,7},{7,6},{8,9},{9,8},{10,11... | collective-permute-start | bytes 153608 | tf_op jit(solution)/shard_map/ppermute | solution.py:466

commit v26 on v25

--- a/solution.py
+++ b/solution.py
@@ -353,19 +353,17 @@
     return spread * lax.rsqrt(spread * spread + SOFT_WIDTH)
 
 
-def mix_kernel(att_ref, factor_ref, truth_any, w_any, *refs):
-    sources, refs = refs[:-8], refs[-8:]
-    pred_ref, grad_ref, a, truth_ref, truth, source, w, sems = refs
+def mix_kernel(att_ref, factor_ref, truth_any, w, *refs):
+    sources, refs = refs[:-7], refs[-7:]
+    pred_ref, grad_ref, a, truth_ref, truth, source, sems = refs
     members_num, part, _ = source.shape
-    halves = w.shape[0]
     ens = lax.axis_index("ens")
-    copies = fetch([(w_any.at[half], w.at[half]) for half in range(halves)], sems)
     pairs = [(truth_any, truth_ref)]
     if len(sources) == 1:
         pairs.append((sources[0], source))
     else:
         pairs += [(rows.at[0], source.at[ens ^ step]) for step, rows in enumerate(sources)]
-    others = fetch(pairs, sems, halves)
+    others = fetch(pairs, sems)
     for g in range(GROUP):
         for m in range(members_num):
             a[m * part : (m + 1) * part, g * COLS : (g + 1) * COLS] = att_ref[g * members_num + m]
@@ -380,15 +378,9 @@
     truth[...] = jnp.zeros_like(truth)
     truth[:FIELD_NUM, :] = own_truth
     hidden = source[...].reshape(a.shape).astype(F32)
-    count = LATENT_DIM // halves
-    for half in range(halves):
-        copies[half].wait()
-        mix = w[half].reshape(count, LATENT_DIM + FIELD_PAD)[:, :LATENT_DIM]
-        hidden += jnp.dot(
-            a[:, half * count : (half + 1) * count], mix, preferred_element_type=F32
-        )
     both = w[...].reshape(LATENT_DIM, LATENT_DIM + FIELD_PAD)
     mix, readout = both[:, :LATENT_DIM], both[:, LATENT_DIM:]
+    hidden += jnp.dot(a[...], mix, preferred_element_type=F32)
     inverse = lax.rsqrt(jnp.mean(hidden * hidden, axis=-1, keepdims=True) + NORM_EPS)
     decoded = (hidden * inverse).astype(BF16)
     prediction = lax.dot_general(
@@ -523,10 +515,22 @@
     )(neighbours, members.reshape(node_rows, LATENT_DIM))
 
     packed, normed = lax.optimization_barrier((in_order(packed, "half", 0), normed))
+    square = paired and halves == 2 and shard % 16 == 0
     near = [normed, swap(normed, "quad", 1), None, swap(normed, "quad", 3)]
     if paired:
         columns = exchange(columns.reshape(-1, shard, 3 * COLS), nodes)
-        columns, late = lax.optimization_barrier((columns, normed))
+        if square:
+            (wide,) = call(
+                attach_kernel,
+                "attach_sources",
+                [((2, shard, width + LATENT_DIM), BF16)],
+                "vh",
+                [pltpu.SemaphoreType.DMA((2,))],
+                moved=2**19,
+            )(packed, sources[1])
+            columns, late, wide = lax.optimization_barrier((columns, normed, wide))
+        else:
+            columns, late = lax.optimization_barrier((columns, normed))
         columns = [columns, swap(columns, "ens", 1)]
     else:
         columns = [exchange(columns.reshape(-1, shard, 3 * COLS), everyone)]
@@ -545,16 +549,7 @@
         results="hv",
     )(*near, *far)
 
-    square = paired and halves == 2 and shard % 16 == 0
     if square:
-        (wide,) = call(
-            attach_kernel,
-            "attach_sources",
-            [((2, shard, width + LATENT_DIM), BF16)],
-            "vh",
-            [pltpu.SemaphoreType.DMA((2,))],
-            moved=2**19,
-        )(packed, sources[1])
         packed, arrived = call(
             merge_members_kernel,
             "merge_members",
@@ -631,21 +626,19 @@
         "a" * len(pieces),
         [pltpu.SemaphoreType.DMA((GROUP,))],
         moved=4 * 2**20,
-        results="h",
     )(*pieces)
 
     prediction, grads = call(
         mix_kernel,
         "mix_loss_backward",
         [((FIELD_NUM, node_rows), F32), ((GROUP * members_num, part, COLS), BF16)],
-        "vvhh" + "a" * len(sources),
+        "vvhv" + "a" * len(sources),
         [
             pltpu.VMEM((node_rows, LATENT_DIM), BF16),
             pltpu.VMEM(observed_truth.shape, F32),
             pltpu.VMEM((FIELD_PAD, node_rows), F32),
             pltpu.VMEM((members_num, part, LATENT_DIM), BF16),
-            pltpu.VMEM(block, BF16),
-            pltpu.SemaphoreType.DMA((halves + 1 + len(sources),)),
+            pltpu.SemaphoreType.DMA((1 + len(sources),)),
         ],
         flops=node_rows * LATENT_DIM * 4 * width,
         moved=2**22,

time: 109 us -> 113 us (1.037)
  local copies, waits for them, and re-layouts: 1.73 us -> 9.55 us
  waiting for transfers between devices: 33.5 us -> 29.7 us
  blocking collectives: 9.89 us -> 11.9 us
  Pallas kernels: 27.2 us -> 25.2 us
    unnamed x9 -> x33, local copies, waits for them, and re-layouts: 1.65 us -> 9.48 us
    all_to_all x3, waiting for transfers between devices: 17.3 us -> 14.2 us  [exchange(): return lax.all_to_all(chunks, axes, 0, 0)]
    all_to_all x1, blocking collectives: 9.89 us -> 11.9 us  [exchange(): return lax.all_to_all(chunks, axes, 0, 0)]
    pallas_call x16, Pallas kernels: 27.2 us -> 25.2 us  [run(): made(*[pltpu.with_memory_space_constraint(arg, pltpu.HBM) if space == 'h'...]
  transfers between devices with their start and end apart: 23 -> 23, of which waited for: 14 -> 10; matrix products, arithmetic and copies ran while one was open for 2% -> 2% of each run, Pallas kernels for 17% -> 15%
where the time goes in v26:
time: 113 us; the launch traced here: 112 us
  starting transfers between devices  34.1 us (30%)
  waiting for transfers between devices  29.7 us (26%)
  Pallas kernels  25.2 us (22%)
  blocking collectives  11.9 us (11%)
  local copies, waits for them, and re-layouts  9.55 us (8%)
    pallas_call x16, Pallas kernels, run(): made(*[pltpu.with_memory_space_constraint(arg, pltpu.HBM) if space == 'h'...  25.2 us
    ppermute x20, starting transfers between devices, swap(): lax.ppermute(value, axis, [(i, i ^ step) for i in range(lax.axis_size(axi...  18.3 us
    all_to_all x3, starting transfers between devices, exchange(): return lax.all_to_all(chunks, axes, 0, 0)  15.8 us
    ppermute x20, waiting for transfers between devices, swap(): lax.ppermute(value, axis, [(i, i ^ step) for i in range(lax.axis_size(axi...  15.5 us
    all_to_all x3, waiting for transfers between devices, exchange(): return lax.all_to_all(chunks, axes, 0, 0)  14.2 us
    all_to_all x1, blocking collectives, exchange(): return lax.all_to_all(chunks, axes, 0, 0)  11.9 us
    unnamed x33, local copies, waits for them, and re-layouts  9.48 us
  transfers between devices with their start and end apart: 23, of which 10 were waited for; matrix products, arithmetic and copies ran while one was open for 2% of the time, Pallas kernels for 15%

profile of v26, /device:TPU:1, one launch (start us, length us, event | category | flops | bytes accessed | tf_op | source)
XLA Modules:
  0.0 112.5 jit_solution(7040944505853325391)
XLA Ops:
  0.6 1.8 %prepare_weights.1 = (bf16[2,8,1,32,384]{4,3,2,1,0:T(8,128)(2,1)}, bf16[32,1152]{1,0:T(8,128)(2,1)}) custom-call(bf16[32,3072]{1,0:T(8,128)(2,1)} %w_any.1, bf16[32,1024]{1,0:T(8,128)(2,1)} %mix_any.1, bf16[32,100]{1,0:T(8,128)(2,1)} %readout_any.1), custom_call_target="tpu_custom_call" | custom-call | bytes 1048576 | tf_op jit(solution)/shard_map/prepare_weights/pallas_call | solution.py:63
  2.4 3.2 %collective-permute-start = (bf16[32,1152]{1,0:T(8,128)(2,1)}, bf16[32,1152]{1,0:T(8,128)(2,1)S(1)}, u32[]{:S(2)}, u32[]{:S(2)}) collective-permute-start(bf16[32,1152]{1,0:T(8,128)(2,1)} %get-tuple-element.36), channel_id=1, source_target_pairs={{0,16},{16,0},{1,17},{17,1},{2,18},{18,2},{3,19},{19,3},{4,20},{20... | collective-permute-start | bytes 221192 | tf_op jit(solution)/shard_map/ppermute | solution.py:458
  5.7 4.8 %all-to-all-start = ((bf16[16,32,384]{2,1,0:T(8,128)(2,1)}), bf16[16,32,384]{2,1,0:T(8,128)(2,1)S(1)}, u32[]{:S(2)}, u32[]{:S(2)}) async-start(bf16[16,32,384]{2,1,0:T(8,128)(2,1)} %bitcast.23), calls=%async_computation | async-start | bytes 786432 | tf_op jit(solution)/shard_map/all_to_all | solution.py:454
  10.4 1.9 %norm.1 = (bf16[144,1024]{1,0:T(8,128)(2,1)}, bf16[1,64,1024]{2,1,0:T(8,128)(2,1)}, bf16[1,64,1024]{2,1,0:T(8,128)(2,1)}) custom-call(s32[2,4]{1,0:T(2,128)} %near_any.1, bf16[128,1024]{1,0:T(8,128)(2,1)} %bitcast.24), custom_call_target="tpu_custom_call" | custom-call | flops 1048576 | bytes 1048576 | tf_op jit(solution)/shard_map/norm/pallas_call | solution.py:63
  12.3 0.9 select_bitcast_fusion.1
  13.3 1.5 %collective-permute-start.1 = (bf16[144,1024]{1,0:T(8,128)(2,1)}, bf16[144,1024]{1,0:T(8,128)(2,1)S(1)}, u32[]{:S(2)}, u32[]{:S(2)}) collective-permute-start(bf16[144,1024]{1,0:T(8,128)(2,1)} %get-tuple-element.43.refs_0_), channel_id=1, source_target_pairs={{0,4},{4,0},{8,12},{12,8},{1,5},{5,1},{9,13},{13,9},{2,6},{6,2},{1... | collective-permute-start | bytes 884744 | tf_op jit(solution)/shard_map/ppermute | solution.py:458
  14.7 1.2 %collective-permute-start.3 = (bf16[144,1024]{1,0:T(8,128)(2,1)}, bf16[144,1024]{1,0:T(8,128)(2,1)S(1)}, u32[]{:S(2)}, u32[]{:S(2)}) collective-permute-start(bf16[144,1024]{1,0:T(8,128)(2,1)} %get-tuple-element.43.refs_0_), channel_id=1, source_target_pairs={{0,12},{4,8},{8,4},{12,0},{1,13},{5,9},{9,5},{13,1},{2,14},{6,10},... | collective-permute-start | bytes 884744 | tf_op jit(solution)/shard_map/ppermute | solution.py:458
  15.9 0.9 attach_sources.1.mine_ref
  16.8 5.1 %all-to-all-done.refs_0_ = bf16[16,32,384]{2,1,0:T(8,128)(2,1)S(1)} async-done(((bf16[16,32,384]{2,1,0:T(8,128)(2,1)}), bf16[16,32,384]{2,1,0:T(8,128)(2,1)S(1)}, u32[]{:S(2)}, u32[]{:S(2)}) %all-to-all-start) | async-done | bytes 393248 | tf_op jit(solution)/shard_map/all_to_all | solution.py:454
  21.9 1.7 %collective-permute-start.2 = (bf16[144,1024]{1,0:T(8,128)(2,1)}, bf16[144,1024]{1,0:T(8,128)(2,1)S(1)}, u32[]{:S(2)}, u32[]{:S(2)}) collective-permute-start(bf16[144,1024]{1,0:T(8,128)(2,1)} %get-tuple-element.43.refs_0_), channel_id=1, source_target_pairs={{0,8},{4,12},{8,0},{12,4},{1,9},{5,13},{9,1},{13,5},{2,10},{6,14},... | collective-permute-start | bytes 884744 | tf_op jit(solution)/shard_map/ppermute | solution.py:458
  23.6 1.2 %collective-permute-start.9 = (bf16[2,32,2176]{2,1,0:T(8,128)(2,1)S(1)}, bf16[2,32,2176]{2,1,0:T(8,128)(2,1)S(1)}, u32[]{:S(2)}, u32[]{:S(2)}) collective-permute-start(bf16[2,32,2176]{2,1,0:T(8,128)(2,1)S(1)} %attach_sources.1.mine_ref), channel_id=1, source_target_pairs={{0,1},{1,0},{2,3},{3,2},{4,5},{5,4},{6,7},{7,6},{8,9},{9,8},{10,11... | collective-permute-start | bytes 835592 | tf_op jit(solution)/shard_map/ppermute | solution.py:458
  25.1 5.2 %collective-permute-done.1.refs_1_ = bf16[144,1024]{1,0:T(8,128)(2,1)S(1)} collective-permute-done((bf16[144,1024]{1,0:T(8,128)(2,1)}, bf16[144,1024]{1,0:T(8,128)(2,1)S(1)}, u32[]{:S(2)}, u32[]{:S(2)}) %collective-permute-start.1) | collective-permute-done | bytes 294944 | tf_op jit(solution)/shard_map/ppermute | solution.py:458
  30.3 1.4 %collective-permute-done.2.refs_2_ = bf16[144,1024]{1,0:T(8,128)(2,1)S(1)} collective-permute-done((bf16[144,1024]{1,0:T(8,128)(2,1)}, bf16[144,1024]{1,0:T(8,128)(2,1)S(1)}, u32[]{:S(2)}, u32[]{:S(2)}) %collective-permute-start.2) | collective-permute-done | bytes 294944 | tf_op jit(solution)/shard_map/ppermute | solution.py:458
  31.7 1.0 collective-permute-start.6
  33.3 1.0 collective-permute-done.6.refs_6_
  34.3 1.5 %collective-permute-start.10 = (bf16[2,64,1152]{2,1,0:T(8,128)(2,1)S(1)}, bf16[2,64,1152]{2,1,0:T(8,128)(2,1)S(1)}, u32[]{:S(2)}, u32[]{:S(2)}) collective-permute-start(bf16[2,64,1152]{2,1,0:T(8,128)(2,1)S(1)} %bitcast.17), channel_id=1, source_target_pairs={{0,4},{4,0},{8,12},{12,8},{1,5},{5,1},{9,13},{13,9},{2,6},{6,2},{1... | collective-permute-start | bytes 884744 | tf_op jit(solution)/shard_map/ppermute | solution.py:458
  36.3 1.3 %collective-permute-start.12 = (bf16[2,64,1152]{2,1,0:T(8,128)(2,1)S(1)}, bf16[2,64,1152]{2,1,0:T(8,128)(2,1)S(1)}, u32[]{:S(2)}, u32[]{:S(2)}) collective-permute-start(bf16[2,64,1152]{2,1,0:T(8,128)(2,1)S(1)} %bitcast.19), channel_id=1, source_target_pairs={{0,12},{4,8},{8,4},{12,0},{1,13},{5,9},{9,5},{13,1},{2,14},{6,10},... | collective-permute-start | bytes 884744 | tf_op jit(solution)/shard_map/ppermute | solution.py:458
  37.6 1.0 copy-done.3
  38.6 1.5 %collect.1 = (bf16[1024,1024]{1,0:T(8,128)(2,1)}, f32[8,16,128]{2,1,0:T(8,128)S(1)}) custom-call(bf16[144,1024]{1,0:T(8,128)(2,1)S(1)} %copy-done.3, bf16[144,1024]{1,0:T(8,128)(2,1)S(1)} %collective-permute-done.1.refs_1_, bf16[144,1024]{1,0:T(8,128)(2,1)S(1)} %collective-permute-done.2.refs_2_, bf16[144,1024]{1,0:T(8,128)(2,1)S(1)} %collective-permute-done.3.refs_3_, ...), custom_call_target="tpu_custom_call" | custom-call | bytes 4194304 | tf_op jit(solution)/shard_map/collect/pallas_call | solution.py:63
  40.4 1.3 %project_rims.1 = (bf16[16,2,32,384]{3,2,1,0:T(8,128)(2,1)S(1)}, bf16[128,256]{1,0:T(8,128)(2,1)S(1)}) custom-call(bf16[1024,1024]{1,0:T(8,128)(2,1)} %get-tuple-element.47.normed_any.normed_ref, bf16[16,32,384]{2,1,0:T(8,128)(2,1)S(1)} %all-to-all-done.refs_0_, bf16[16,32,384]{2,1,0:T(8,128)(2,1)S(1)} %collective-permute-done.8.refs_1_), custom_call_target="tpu_custom_call" | custom-call | flops 67108864 | bytes 1048576 | tf_op jit(solution)/shard_map/project_rims/pallas_call | solution.py:63
  41.7 1.8 %collective-permute-start.13 = (bf16[128,256]{1,0:T(8,128)(2,1)S(1)}, bf16[128,256]{1,0:T(8,128)(2,1)S(1)}, u32[]{:S(2)}, u32[]{:S(2)}) collective-permute-start(bf16[128,256]{1,0:T(8,128)(2,1)S(1)} %get-tuple-element.57), channel_id=1, source_target_pairs={{0,16},{16,0},{1,17},{17,1},{2,18},{18,2},{3,19},{19,3},{4,20},{20... | collective-permute-start | bytes 196616 | tf_op jit(solution)/shard_map/ppermute | solution.py:458
  43.6 2.8 %project.1 = (bf16[1024,128]{1,0:T(8,128)(2,1)S(1)}, bf16[1024,256]{1,0:T(8,128)(2,1)S(1)}) custom-call(bf16[1024,1024]{1,0:T(8,128)(2,1)} %get-tuple-element.47.normed_any.normed_ref, bf16[16,2,32,384]{3,2,1,0:T(8,128)(2,1)S(1)} %get-tuple-element.50.w_ref), custom_call_target="tpu_custom_call" | custom-call | flops 805306368 | bytes 4194304 | tf_op jit(solution)/shard_map/project/pallas_call | solution.py:63
  46.4 1.9 %attention_interior.1.done_ref = bf16[1024,128]{1,0:T(8,128)(2,1)S(1)} custom-call(f32[8,16,128]{2,1,0:T(8,128)S(1)} %get-tuple-element.48.steps_ref, bf16[1024,128]{1,0:T(8,128)(2,1)S(1)} %get-tuple-element.51.q_ref, bf16[1024,256]{1,0:T(8,128)(2,1)S(1)} %get-tuple-element.56.kv_ref), custom_call_target="tpu_custom_call" | custom-call | flops 268435456 | bytes 2097152 | tf_op jit(solution)/shard_map/attention_interior/pallas_call | solution.py:63
  48.3 1.5 %collective-permute-done.13.low_ref.high_ref = bf16[128,256]{1,0:T(8,128)(2,1)S(1)} collective-permute-done((bf16[128,256]{1,0:T(8,128)(2,1)S(1)}, bf16[128,256]{1,0:T(8,128)(2,1)S(1)}, u32[]{:S(2)}, u32[]{:S(2)}) %collective-permute-start.13) | collective-permute-done | bytes 65568 | tf_op jit(solution)/shard_map/ppermute | solution.py:458
  49.8 1.4 %attention_edges.1 = bf16[1024,128]{1,0:T(8,128)(2,1)} custom-call(f32[8,16,128]{2,1,0:T(8,128)S(1)} %get-tuple-element.48.steps_ref, bf16[1024,128]{1,0:T(8,128)(2,1)S(1)} %get-tuple-element.51.q_ref, bf16[1024,256]{1,0:T(8,128)(2,1)S(1)} %get-tuple-element.56.kv_ref, bf16[128,256]{1,0:T(8,128)(2,1)S(1)} %collective-permute-done.13.low_ref.high_ref, ...), custom_call_target="tpu_custom_call" | custom-call | flops 67108864 | bytes 1048576 | tf_op jit(solution)/shard_map/attention_edges/pallas_call | solution.py:63
  51.2 8.3 %all-to-all-start.1 = ((bf16[16,64,128]{2,1,0:T(8,128)(2,1)}), bf16[16,64,128]{2,1,0:T(8,128)(2,1)S(1)}, u32[]{:S(2)}, u32[]{:S(2)}) async-start(bf16[16,64,128]{2,1,0:T(8,128)(2,1)} %bitcast.5), calls=%async_computation.1 | async-start | bytes 524288 | tf_op jit(solution)/shard_map/all_to_all | solution.py:454
  60.1 0.7 copy-done.4
  60.9 0.7 copy-done.6
  62.0 0.7 copy-done.8
  63.2 1.0 copy-done.2
  64.2 1.0 copy-done.5
  65.2 1.0 copy-done.7
  66.1 1.0 copy-done.9
  67.5 0.9 copy-done.10
  68.4 0.9 copy-done.12
  69.3 2.8 %mix_loss_backward.1 = (f32[100,128]{1,0:T(8,128)S(1)}, bf16[16,64,128]{2,1,0:T(8,128)(2,1)S(1)}) custom-call(bf16[16,64,128]{2,1,0:T(8,128)(2,1)S(1)} %all-to-all-done.1.att_ref, f32[1,128]{1,0:T(1,128)S(1)} %bitcast.22, f32[100,128]{1,0:T(8,128)} %truth_any.1, bf16[2,4,2,64,1152]{4,3,2,1,0:T(8,128)(2,1)S(1)} %assemble.1.w, ...), custom_call_target="tpu_custom_call" | custom-call | flops 603979776 | bytes 4194304 | tf_op jit(solution)/shard_map/mix_loss_backward/pallas_call | solution.py:63
  72.2 11.9 %all_to_all.20 = bf16[16,64,128]{2,1,0:T(8,128)(2,1)S(1)} all-to-all(bf16[16,64,128]{2,1,0:T(8,128)(2,1)S(1)} %get-tuple-element.64), channel_id=1, replica_groups=mesh['half'=2,'quad'=4,'core'=2,'ens'=2] {'quad','core','ens'}, dimensions={0} | all-to-all | bytes 524288 | tf_op jit(solution)/shard_map/all_to_all | solution.py:454
  84.1 1.4 %attention_edges_back.1 = (f32[2,256,256]{2,1,0:T(8,128)S(1)}, bf16[128,256]{1,0:T(8,128)(2,1)S(1)}) custom-call(f32[8,16,128]{2,1,0:T(8,128)S(1)} %get-tuple-element.48.steps_ref, bf16[1024,128]{1,0:T(8,128)(2,1)S(1)} %get-tuple-element.51.q_ref, bf16[1024,256]{1,0:T(8,128)(2,1)S(1)} %get-tuple-element.56.kv_ref, ...), custom_call_target="tpu_custom_call" | custom-call | flops 167772160 | bytes 1048576 | tf_op jit(solution)/shard_map/attention_edges_back/pallas_call | solution.py:63
  85.6 3.9 %attention_interior_back.1.grads_ref = f32[1024,256]{1,0:T(8,128)S(1)} custom-call(f32[8,16,128]{2,1,0:T(8,128)S(1)} %get-tuple-element.48.steps_ref, bf16[1024,128]{1,0:T(8,128)(2,1)S(1)} %get-tuple-element.51.q_ref, bf16[1024,256]{1,0:T(8,128)(2,1)S(1)} %get-tuple-element.56.kv_ref, bf16[1024,128]{1,0:T(8,128)(2,1)S(1)} %bitcast.15, ...), custom_call_target="tpu_custom_call" | custom-call | flops 536870912 | bytes 4194304 | tf_op jit(solution)/shard_map/attention_interior_back/pallas_call | solution.py:63
  89.5 1.3 %product.1.total_ref = f32[1024,256]{1,0:T(8,128)S(1)} custom-call(bf16[1024,1024]{1,0:T(8,128)(2,1)S(1)} %copy-done, f32[1024,256]{1,0:T(8,128)S(1)} %attention_interior_back.1.grads_ref), custom_call_target="tpu_custom_call" | custom-call | tf_op jit(solution)/shard_map/product/pallas_call | solution.py:63
  90.8 1.0 collective-permute-done.18.refs_0_
  91.8 1.1 %product_rims.1 = bf16[1024,256]{1,0:T(8,128)(2,1)} custom-call(bf16[1024,1024]{1,0:T(8,128)(2,1)S(1)} %copy-done, f32[1024,256]{1,0:T(8,128)S(1)} %product.1.total_ref, bf16[128,256]{1,0:T(8,128)(2,1)S(1)} %collective-permute-done.18.refs_0_), custom_call_target="tpu_custom_call" | custom-call | flops 67108864 | bytes 2097152 | tf_op jit(solution)/shard_map/product_rims/pallas_call | solution.py:63
  93.0 2.8 %all-to-all-start.3 = ((bf16[32,32,256]{2,1,0:T(8,128)(2,1)}), bf16[32,32,256]{2,1,0:T(8,128)(2,1)S(1)}, u32[]{:S(2)}, u32[]{:S(2)}) async-start(bf16[32,32,256]{2,1,0:T(8,128)(2,1)} %bitcast.9), calls=%async_computation.3 | async-start | bytes 1048576 | tf_op jit(solution)/shard_map/all_to_all | solution.py:454
  95.8 1.5 %collective-permute-start.19 = (f32[100,128]{1,0:T(8,128)S(1)}, f32[100,128]{1,0:T(8,128)S(1)}, u32[]{:S(2)}, u32[]{:S(2)}) collective-permute-start(f32[100,128]{1,0:T(8,128)S(1)} %copy-done.14), channel_id=1, source_target_pairs={{0,1},{1,0},{2,3},{3,2},{4,5},{5,4},{6,7},{7,6},{8,9},{9,8},{10,11... | collective-permute-start | bytes 153608 | tf_op jit(solution)/shard_map/ppermute | solution.py:458
  97.2 4.5 %collective-permute-done.19 = f32[100,128]{1,0:T(8,128)S(1)} collective-permute-done((f32[100,128]{1,0:T(8,128)S(1)}, f32[100,128]{1,0:T(8,128)S(1)}, u32[]{:S(2)}, u32[]{:S(2)}) %collective-permute-start.19) | collective-permute-done | bytes 51232 | tf_op jit(solution)/shard_map/ppermute | solution.py:458
  101.9 0.7 copy.9
  102.6 9.1 %all-to-all-done.3 = bf16[32,32,256]{2,1,0:T(8,128)(2,1)S(1)} async-done(((bf16[32,32,256]{2,1,0:T(8,128)(2,1)}), bf16[32,32,256]{2,1,0:T(8,128)(2,1)S(1)}, u32[]{:S(2)}, u32[]{:S(2)}) %all-to-all-start.3) | async-done | bytes 524320 | tf_op jit(solution)/shard_map/all_to_all | solution.py:454
  111.7 0.8 gather_sums.1
  (54 shorter events, 4.0 us)
Async XLA Ops:
  2.4 9.9 %collective-permute-start = (bf16[32,1152]{1,0:T(8,128)(2,1)}, bf16[32,1152]{1,0:T(8,128)(2,1)S(1)}, u32[]{:S(2)}, u32[]{:S(2)}) collective-permute-start(bf16[32,1152]{1,0:T(8,128)(2,1)} %get-tuple-element.36), channel_id=1, source_target_pairs={{0,16},{16,0},{1,17},{17,1},{2,18},{18,2},{3,19},{19,3},{4,20},{20... | collective-permute-start | bytes 221192 | tf_op jit(solution)/shard_map/ppermute | solution.py:458
  5.7 16.2 %all-to-all-start = ((bf16[16,32,384]{2,1,0:T(8,128)(2,1)}), bf16[16,32,384]{2,1,0:T(8,128)(2,1)S(1)}, u32[]{:S(2)}, u32[]{:S(2)}) async-start(bf16[16,32,384]{2,1,0:T(8,128)(2,1)} %bitcast.23), calls=%async_computation | async-start | bytes 786432 | tf_op jit(solution)/shard_map/all_to_all | solution.py:454
  13.3 17.0 %collective-permute-start.1 = (bf16[144,1024]{1,0:T(8,128)(2,1)}, bf16[144,1024]{1,0:T(8,128)(2,1)S(1)}, u32[]{:S(2)}, u32[]{:S(2)}) collective-permute-start(bf16[144,1024]{1,0:T(8,128)(2,1)} %get-tuple-element.43.refs_0_), channel_id=1, source_target_pairs={{0,4},{4,0},{8,12},{12,8},{1,5},{5,1},{9,13},{13,9},{2,6},{6,2},{1... | collective-permute-start | bytes 884744 | tf_op jit(solution)/shard_map/ppermute | solution.py:458
  14.7 15.6 %collective-permute-start.3 = (bf16[144,1024]{1,0:T(8,128)(2,1)}, bf16[144,1024]{1,0:T(8,128)(2,1)S(1)}, u32[]{:S(2)}, u32[]{:S(2)}) collective-permute-start(bf16[144,1024]{1,0:T(8,128)(2,1)} %get-tuple-element.43.refs_0_), channel_id=1, source_target_pairs={{0,12},{4,8},{8,4},{12,0},{1,13},{5,9},{9,5},{13,1},{2,14},{6,10},... | collective-permute-start | bytes 884744 | tf_op jit(solution)/shard_map/ppermute | solution.py:458
  21.9 9.8 %collective-permute-start.2 = (bf16[144,1024]{1,0:T(8,128)(2,1)}, bf16[144,1024]{1,0:T(8,128)(2,1)S(1)}, u32[]{:S(2)}, u32[]{:S(2)}) collective-permute-start(bf16[144,1024]{1,0:T(8,128)(2,1)} %get-tuple-element.43.refs_0_), channel_id=1, source_target_pairs={{0,8},{4,12},{8,0},{12,4},{1,9},{5,13},{9,1},{13,5},{2,10},{6,14},... | collective-permute-start | bytes 884744 | tf_op jit(solution)/shard_map/ppermute | solution.py:458
  23.6 9.6 %collective-permute-start.9 = (bf16[2,32,2176]{2,1,0:T(8,128)(2,1)S(1)}, bf16[2,32,2176]{2,1,0:T(8,128)(2,1)S(1)}, u32[]{:S(2)}, u32[]{:S(2)}) collective-permute-start(bf16[2,32,2176]{2,1,0:T(8,128)(2,1)S(1)} %attach_sources.1.mine_ref), channel_id=1, source_target_pairs={{0,1},{1,0},{2,3},{3,2},{4,5},{5,4},{6,7},{7,6},{8,9},{9,8},{10,11... | collective-permute-start | bytes 835592 | tf_op jit(solution)/shard_map/ppermute | solution.py:458
  24.8 15.6 %collective-permute-start.8 = (bf16[16,32,384]{2,1,0:T(8,128)(2,1)S(1)}, bf16[16,32,384]{2,1,0:T(8,128)(2,1)S(1)}, u32[]{:S(2)}, u32[]{:S(2)}) collective-permute-start(bf16[16,32,384]{2,1,0:T(8,128)(2,1)S(1)} %all-to-all-done.refs_0_), channel_id=1, source_target_pairs={{0,1},{1,0},{2,3},{3,2},{4,5},{5,4},{6,7},{7,6},{8,9},{9,8},{10,11... | collective-permute-start | bytes 1179656 | tf_op jit(solution)/shard_map/ppermute | solution.py:458
  31.7 2.6 %collective-permute-start.6 = (bf16[144,1024]{1,0:T(8,128)(2,1)S(1)}, bf16[144,1024]{1,0:T(8,128)(2,1)S(1)}, u32[]{:S(2)}, u32[]{:S(2)}) collective-permute-start(bf16[144,1024]{1,0:T(8,128)(2,1)S(1)} %collective-permute-done.2.refs_2_), channel_id=1, source_target_pairs={{0,2},{2,0},{1,3},{3,1},{4,6},{6,4},{5,7},{7,5},{8,10},{10,8},{9,1... | collective-permute-start | bytes 884744 | tf_op jit(solution)/shard_map/ppermute | solution.py:458
  32.7 3.1 %collective-permute-start.4 = (bf16[144,1024]{1,0:T(8,128)(2,1)}, bf16[144,1024]{1,0:T(8,128)(2,1)S(1)}, u32[]{:S(2)}, u32[]{:S(2)}) collective-permute-start(bf16[144,1024]{1,0:T(8,128)(2,1)} %get-tuple-element.43.refs_0_), channel_id=1, source_target_pairs={{0,2},{2,0},{1,3},{3,1},{4,6},{6,4},{5,7},{7,5},{8,10},{10,8},{9,1... | collective-permute-start | bytes 884744 | tf_op jit(solution)/shard_map/ppermute | solution.py:458
  32.7 3.6 %collective-permute-start.5 = (bf16[144,1024]{1,0:T(8,128)(2,1)S(1)}, bf16[144,1024]{1,0:T(8,128)(2,1)S(1)}, u32[]{:S(2)}, u32[]{:S(2)}) collective-permute-start(bf16[144,1024]{1,0:T(8,128)(2,1)S(1)} %collective-permute-done.1.refs_1_), channel_id=1, source_target_pairs={{0,2},{2,0},{1,3},{3,1},{4,6},{6,4},{5,7},{7,5},{8,10},{10,8},{9,1... | collective-permute-start | bytes 884744 | tf_op jit(solution)/shard_map/ppermute | solution.py:458
  33.2 4.4 %collective-permute-start.7 = (bf16[144,1024]{1,0:T(8,128)(2,1)S(1)}, bf16[144,1024]{1,0:T(8,128)(2,1)S(1)}, u32[]{:S(2)}, u32[]{:S(2)}) collective-permute-start(bf16[144,1024]{1,0:T(8,128)(2,1)S(1)} %collective-permute-done.3.refs_3_), channel_id=1, source_target_pairs={{0,2},{2,0},{1,3},{3,1},{4,6},{6,4},{5,7},{7,5},{8,10},{10,8},{9,1... | collective-permute-start | bytes 884744 | tf_op jit(solution)/shard_map/ppermute | solution.py:458
  33.3 7.2 %copy-start.11 = (bf16[1,64,1024]{2,1,0:T(8,128)(2,1)}, bf16[1,64,1024]{2,1,0:T(8,128)(2,1)S(1)}, u32[]{:S(2)}) copy-start(bf16[1,64,1024]{2,1,0:T(8,128)(2,1)S(1)} %get-tuple-element.63.refs_1_) | copy-start | bytes 393220
  33.3 26.2 %copy-start.1 = (bf16[2,2,32,1152]{3,2,1,0:T(8,128)(2,1)}, bf16[2,2,32,1152]{3,2,1,0:T(8,128)(2,1)S(1)}, u32[]{:S(2)}) copy-start(bf16[2,2,32,1152]{3,2,1,0:T(8,128)(2,1)S(1)} %get-tuple-element.53) | copy-start | bytes 884740
  34.3 25.1 %collective-permute-start.10 = (bf16[2,64,1152]{2,1,0:T(8,128)(2,1)S(1)}, bf16[2,64,1152]{2,1,0:T(8,128)(2,1)S(1)}, u32[]{:S(2)}, u32[]{:S(2)}) collective-permute-start(bf16[2,64,1152]{2,1,0:T(8,128)(2,1)S(1)} %bitcast.17), channel_id=1, source_target_pairs={{0,4},{4,0},{8,12},{12,8},{1,5},{5,1},{9,13},{13,9},{2,6},{6,2},{1... | collective-permute-start | bytes 884744 | tf_op jit(solution)/shard_map/ppermute | solution.py:458
  35.9 23.6 %collective-permute-start.11 = (bf16[2,64,1152]{2,1,0:T(8,128)(2,1)S(1)}, bf16[2,64,1152]{2,1,0:T(8,128)(2,1)S(1)}, u32[]{:S(2)}, u32[]{:S(2)}) collective-permute-start(bf16[2,64,1152]{2,1,0:T(8,128)(2,1)S(1)} %bitcast.18), channel_id=1, source_target_pairs={{0,8},{4,12},{8,0},{12,4},{1,9},{5,13},{9,1},{13,5},{2,10},{6,14},... | collective-permute-start | bytes 884744 | tf_op jit(solution)/shard_map/ppermute | solution.py:458
  36.3 23.1 %collective-permute-start.12 = (bf16[2,64,1152]{2,1,0:T(8,128)(2,1)S(1)}, bf16[2,64,1152]{2,1,0:T(8,128)(2,1)S(1)}, u32[]{:S(2)}, u32[]{:S(2)}) collective-permute-start(bf16[2,64,1152]{2,1,0:T(8,128)(2,1)S(1)} %bitcast.19), channel_id=1, source_target_pairs={{0,12},{4,8},{8,4},{12,0},{1,13},{5,9},{9,5},{13,1},{2,14},{6,10},... | collective-permute-start | bytes 884744 | tf_op jit(solution)/shard_map/ppermute | solution.py:458
  37.6 1.0 copy-start.3
  41.7 8.0 %collective-permute-start.13 = (bf16[128,256]{1,0:T(8,128)(2,1)S(1)}, bf16[128,256]{1,0:T(8,128)(2,1)S(1)}, u32[]{:S(2)}, u32[]{:S(2)}) collective-permute-start(bf16[128,256]{1,0:T(8,128)(2,1)S(1)} %get-tuple-element.57), channel_id=1, source_target_pairs={{0,16},{16,0},{1,17},{17,1},{2,18},{18,2},{3,19},{19,3},{4,20},{20... | collective-permute-start | bytes 196616 | tf_op jit(solution)/shard_map/ppermute | solution.py:458
  51.2 16.3 %copy-start.15 = (f32[128]{0:T(128)S(1)}, f32[128]{0:T(128)}, u32[]{:S(2)}) copy-start(f32[128]{0:T(128)} %param.12) | copy-start | bytes 1540
  51.2 16.3 %all-to-all-start.1 = ((bf16[16,64,128]{2,1,0:T(8,128)(2,1)}), bf16[16,64,128]{2,1,0:T(8,128)(2,1)S(1)}, u32[]{:S(2)}, u32[]{:S(2)}) async-start(bf16[16,64,128]{2,1,0:T(8,128)(2,1)} %bitcast.5), calls=%async_computation.1 | async-start | bytes 524288 | tf_op jit(solution)/shard_map/all_to_all | solution.py:454
  59.5 3.3 %collective-permute-start.14 = (bf16[2,64,1152]{2,1,0:T(8,128)(2,1)S(1)}, bf16[2,64,1152]{2,1,0:T(8,128)(2,1)S(1)}, u32[]{:S(2)}, u32[]{:S(2)}) collective-permute-start(bf16[2,64,1152]{2,1,0:T(8,128)(2,1)S(1)} %bitcast.20), channel_id=1, source_target_pairs={{0,2},{2,0},{1,3},{3,1},{4,6},{6,4},{5,7},{7,5},{8,10},{10,8},{9,1... | collective-permute-start | bytes 884744 | tf_op jit(solution)/shard_map/ppermute | solution.py:458
  59.7 3.1 %collective-permute-start.15 = (bf16[2,64,1152]{2,1,0:T(8,128)(2,1)S(1)}, bf16[2,64,1152]{2,1,0:T(8,128)(2,1)S(1)}, u32[]{:S(2)}, u32[]{:S(2)}) collective-permute-start(bf16[2,64,1152]{2,1,0:T(8,128)(2,1)S(1)} %collective-permute-done.10.refs_1_), channel_id=1, source_target_pairs={{0,2},{2,0},{1,3},{3,1},{4,6},{6,4},{5,7},{7,5},{8,10},{10,8},{9,1... | collective-permute-start | bytes 884744 | tf_op jit(solution)/shard_map/ppermute | solution.py:458
  60.1 0.7 copy-start.4
  60.8 2.0 %collective-permute-start.16 = (bf16[2,64,1152]{2,1,0:T(8,128)(2,1)S(1)}, bf16[2,64,1152]{2,1,0:T(8,128)(2,1)S(1)}, u32[]{:S(2)}, u32[]{:S(2)}) collective-permute-start(bf16[2,64,1152]{2,1,0:T(8,128)(2,1)S(1)} %collective-permute-done.11.refs_2_), channel_id=1, source_target_pairs={{0,2},{2,0},{1,3},{3,1},{4,6},{6,4},{5,7},{7,5},{8,10},{10,8},{9,1... | collective-permute-start | bytes 884744 | tf_op jit(solution)/shard_map/ppermute | solution.py:458
  60.9 0.7 copy-start.6
  61.6 1.6 %collective-permute-start.17 = (bf16[2,64,1152]{2,1,0:T(8,128)(2,1)S(1)}, bf16[2,64,1152]{2,1,0:T(8,128)(2,1)S(1)}, u32[]{:S(2)}, u32[]{:S(2)}) collective-permute-start(bf16[2,64,1152]{2,1,0:T(8,128)(2,1)S(1)} %collective-permute-done.12.refs_3_), channel_id=1, source_target_pairs={{0,2},{2,0},{1,3},{3,1},{4,6},{6,4},{5,7},{7,5},{8,10},{10,8},{9,1... | collective-permute-start | bytes 884744 | tf_op jit(solution)/shard_map/ppermute | solution.py:458
  62.0 0.7 copy-start.8
  63.2 1.0 copy-start.2
  64.2 1.0 copy-start.5
  65.2 1.0 copy-start.7
  66.1 1.0 copy-start.9
  67.5 0.9 copy-start.10
  68.4 0.9 copy-start.12
  72.2 13.4 %copy-start.13 = (f32[100,128]{1,0:T(8,128)}, f32[100,128]{1,0:T(8,128)S(1)}, u32[]{:S(2)}) copy-start(f32[100,128]{1,0:T(8,128)S(1)} %get-tuple-element.68) | copy-start | bytes 153604
  72.2 17.3 %copy-start = (bf16[1024,1024]{1,0:T(8,128)(2,1)S(1)}, bf16[1024,1024]{1,0:T(8,128)(2,1)}, u32[]{:S(2)}) copy-start(bf16[1024,1024]{1,0:T(8,128)(2,1)} %get-tuple-element.47.normed_any.normed_ref) | copy-start | bytes 6291460
  85.5 6.3 %collective-permute-start.18 = (bf16[128,256]{1,0:T(8,128)(2,1)S(1)}, bf16[128,256]{1,0:T(8,128)(2,1)S(1)}, u32[]{:S(2)}, u32[]{:S(2)}) collective-permute-start(bf16[128,256]{1,0:T(8,128)(2,1)S(1)} %get-tuple-element.66), channel_id=1, source_target_pairs={{0,16},{16,0},{1,17},{17,1},{2,18},{18,2},{3,19},{19,3},{4,20},{20... | collective-permute-start | bytes 196616 | tf_op jit(solution)/shard_map/ppermute | solution.py:458
  90.8 5.0 %copy-start.14 = (f32[100,128]{1,0:T(8,128)S(1)}, f32[100,128]{1,0:T(8,128)}, u32[]{:S(2)}) copy-start(f32[100,128]{1,0:T(8,128)} %copy-done.13) | copy-start | bytes 153604
  93.0 18.7 %all-to-all-start.3 = ((bf16[32,32,256]{2,1,0:T(8,128)(2,1)}), bf16[32,32,256]{2,1,0:T(8,128)(2,1)S(1)}, u32[]{:S(2)}, u32[]{:S(2)}) async-start(bf16[32,32,256]{2,1,0:T(8,128)(2,1)} %bitcast.9), calls=%async_computation.3 | async-start | bytes 1048576 | tf_op jit(solution)/shard_map/all_to_all | solution.py:454
  95.8 6.0 %collective-permute-start.19 = (f32[100,128]{1,0:T(8,128)S(1)}, f32[100,128]{1,0:T(8,128)S(1)}, u32[]{:S(2)}, u32[]{:S(2)}) collective-permute-start(f32[100,128]{1,0:T(8,128)S(1)} %copy-done.14), channel_id=1, source_target_pairs={{0,1},{1,0},{2,3},{3,2},{4,5},{5,4},{6,7},{7,6},{8,9},{9,8},{10,11... | collective-permute-start | bytes 153608 | tf_op jit(solution)/shard_map/ppermute | solution.py:458

commit v27 on v26

--- a/solution.py
+++ b/solution.py
@@ -353,17 +353,19 @@
     return spread * lax.rsqrt(spread * spread + SOFT_WIDTH)
 
 
-def mix_kernel(att_ref, factor_ref, truth_any, w, *refs):
-    sources, refs = refs[:-7], refs[-7:]
-    pred_ref, grad_ref, a, truth_ref, truth, source, sems = refs
+def mix_kernel(att_ref, factor_ref, truth_any, w_any, *refs):
+    sources, refs = refs[:-8], refs[-8:]
+    pred_ref, grad_ref, a, truth_ref, truth, source, w, sems = refs
     members_num, part, _ = source.shape
+    halves = w.shape[0]
     ens = lax.axis_index("ens")
+    copies = fetch([(w_any.at[0], w.at[0])], sems)
     pairs = [(truth_any, truth_ref)]
     if len(sources) == 1:
         pairs.append((sources[0], source))
     else:
         pairs += [(rows.at[0], source.at[ens ^ step]) for step, rows in enumerate(sources)]
-    others = fetch(pairs, sems)
+    others = fetch(pairs, sems, halves)
     for g in range(GROUP):
         for m in range(members_num):
             a[m * part : (m + 1) * part, g * COLS : (g + 1) * COLS] = att_ref[g * members_num + m]
@@ -378,9 +380,17 @@
     truth[...] = jnp.zeros_like(truth)
     truth[:FIELD_NUM, :] = own_truth
     hidden = source[...].reshape(a.shape).astype(F32)
+    count = LATENT_DIM // halves
+    for half in range(halves):
+        copies[half].wait()
+        if half + 1 < halves:
+            copies += fetch([(w_any.at[half + 1], w.at[half + 1])], sems, half + 1)
+        mix = w[half].reshape(count, LATENT_DIM + FIELD_PAD)[:, :LATENT_DIM]
+        hidden += jnp.dot(
+            a[:, half * count : (half + 1) * count], mix, preferred_element_type=F32
+        )
     both = w[...].reshape(LATENT_DIM, LATENT_DIM + FIELD_PAD)
     mix, readout = both[:, :LATENT_DIM], both[:, LATENT_DIM:]
-    hidden += jnp.dot(a[...], mix, preferred_element_type=F32)
     inverse = lax.rsqrt(jnp.mean(hidden * hidden, axis=-1, keepdims=True) + NORM_EPS)
     decoded = (hidden * inverse).astype(BF16)
     prediction = lax.dot_general(
@@ -626,19 +636,21 @@
         "a" * len(pieces),
         [pltpu.SemaphoreType.DMA((GROUP,))],
         moved=4 * 2**20,
+        results="h",
     )(*pieces)
 
     prediction, grads = call(
         mix_kernel,
         "mix_loss_backward",
         [((FIELD_NUM, node_rows), F32), ((GROUP * members_num, part, COLS), BF16)],
-        "vvhv" + "a" * len(sources),
+        "vvhh" + "a" * len(sources),
         [
             pltpu.VMEM((node_rows, LATENT_DIM), BF16),
             pltpu.VMEM(observed_truth.shape, F32),
             pltpu.VMEM((FIELD_PAD, node_rows), F32),
             pltpu.VMEM((members_num, part, LATENT_DIM), BF16),
-            pltpu.SemaphoreType.DMA((1 + len(sources),)),
+            pltpu.VMEM(block, BF16),
+            pltpu.SemaphoreType.DMA((halves + 1 + len(sources),)),
         ],
         flops=node_rows * LATENT_DIM * 4 * width,
         moved=2**22,

time: 113 us -> 110 us (0.973)
  local copies, waits for them, and re-layouts: 9.55 us -> 1.73 us
  waiting for transfers between devices: 29.7 us -> 33.3 us
  Pallas kernels: 25.2 us -> 27.9 us
  blocking collectives: 11.9 us -> 9.88 us
    unnamed x33 -> x9, local copies, waits for them, and re-layouts: 9.48 us -> 1.65 us
    pallas_call x16, Pallas kernels: 25.2 us -> 27.9 us  [run(): made(*[pltpu.with_memory_space_constraint(arg, pltpu.HBM) if space == 'h'...]
    all_to_all x3, waiting for transfers between devices: 14.2 us -> 16.4 us  [exchange(): return lax.all_to_all(chunks, axes, 0, 0)]
    all_to_all x1, blocking collectives: 11.9 us -> 9.88 us  [exchange(): return lax.all_to_all(chunks, axes, 0, 0)]
    ppermute x20, waiting for transfers between devices: 15.5 us -> 16.8 us  [swap(): lax.ppermute(value, axis, [(i, i ^ step) for i in range(lax.axis_size(axi...]
  transfers between devices with their start and end apart: 23 -> 23, of which waited for: 10 -> 14; matrix products, arithmetic and copies ran while one was open for 2% -> 2% of each run, Pallas kernels for 15% -> 17%
where the time goes in v27:
time: 110 us; the launch traced here: 109 us
  starting transfers between devices  34.2 us (31%)
  waiting for transfers between devices  33.3 us (30%)
  Pallas kernels  27.9 us (25%)
  blocking collectives  9.88 us (9%)
  local copies, waits for them, and re-layouts  1.73 us (2%)
    pallas_call x16, Pallas kernels, run(): made(*[pltpu.with_memory_space_constraint(arg, pltpu.HBM) if space == 'h'...  27.9 us
    ppermute x20, starting transfers between devices, swap(): lax.ppermute(value, axis, [(i, i ^ step) for i in range(lax.axis_size(axi...  18.4 us
    ppermute x20, waiting for transfers between devices, swap(): lax.ppermute(value, axis, [(i, i ^ step) for i in range(lax.axis_size(axi...  16.8 us
    all_to_all x3, waiting for transfers between devices, exchange(): return lax.all_to_all(chunks, axes, 0, 0)  16.4 us
    all_to_all x3, starting transfers between devices, exchange(): return lax.all_to_all(chunks, axes, 0, 0)  15.9 us
    all_to_all x1, blocking collectives, exchange(): return lax.all_to_all(chunks, axes, 0, 0)  9.88 us
  transfers between devices with their start and end apart: 23, of which 14 were waited for; matrix products, arithmetic and copies ran while one was open for 2% of the time, Pallas kernels for 17%

profile of v27, /device:TPU:1, one launch (start us, length us, event | category | flops | bytes accessed | tf_op | source)
XLA Modules:
  0.0 108.9 jit_solution(7323350293542295686)
XLA Ops:
  0.6 1.8 %prepare_weights.1 = (bf16[2,8,1,32,384]{4,3,2,1,0:T(8,128)(2,1)}, bf16[32,1152]{1,0:T(8,128)(2,1)}) custom-call(bf16[32,3072]{1,0:T(8,128)(2,1)} %w_any.1, bf16[32,1024]{1,0:T(8,128)(2,1)} %mix_any.1, bf16[32,100]{1,0:T(8,128)(2,1)} %readout_any.1), custom_call_target="tpu_custom_call" | custom-call | bytes 1048576 | tf_op jit(solution)/shard_map/prepare_weights/pallas_call | solution.py:63
  2.5 3.2 %collective-permute-start = (bf16[32,1152]{1,0:T(8,128)(2,1)}, bf16[32,1152]{1,0:T(8,128)(2,1)S(1)}, u32[]{:S(2)}, u32[]{:S(2)}) collective-permute-start(bf16[32,1152]{1,0:T(8,128)(2,1)} %get-tuple-element.36), channel_id=1, source_target_pairs={{0,16},{16,0},{1,17},{17,1},{2,18},{18,2},{3,19},{19,3},{4,20},{20... | collective-permute-start | bytes 221192 | tf_op jit(solution)/shard_map/ppermute | solution.py:468
  5.7 4.8 %all-to-all-start = ((bf16[16,32,384]{2,1,0:T(8,128)(2,1)}), bf16[16,32,384]{2,1,0:T(8,128)(2,1)S(1)}, u32[]{:S(2)}, u32[]{:S(2)}) async-start(bf16[16,32,384]{2,1,0:T(8,128)(2,1)} %bitcast.23), calls=%async_computation | async-start | bytes 786432 | tf_op jit(solution)/shard_map/all_to_all | solution.py:464
  10.4 1.9 %norm.1 = (bf16[144,1024]{1,0:T(8,128)(2,1)}, bf16[1,64,1024]{2,1,0:T(8,128)(2,1)}, bf16[1,64,1024]{2,1,0:T(8,128)(2,1)}) custom-call(s32[2,4]{1,0:T(2,128)} %near_any.1, bf16[128,1024]{1,0:T(8,128)(2,1)} %bitcast.24), custom_call_target="tpu_custom_call" | custom-call | flops 1048576 | bytes 1048576 | tf_op jit(solution)/shard_map/norm/pallas_call | solution.py:63
  12.3 0.9 select_bitcast_fusion.1
  13.3 1.5 %collective-permute-start.1 = (bf16[144,1024]{1,0:T(8,128)(2,1)}, bf16[144,1024]{1,0:T(8,128)(2,1)S(1)}, u32[]{:S(2)}, u32[]{:S(2)}) collective-permute-start(bf16[144,1024]{1,0:T(8,128)(2,1)} %get-tuple-element.43.refs_0_), channel_id=1, source_target_pairs={{0,4},{4,0},{8,12},{12,8},{1,5},{5,1},{9,13},{13,9},{2,6},{6,2},{1... | collective-permute-start | bytes 884744 | tf_op jit(solution)/shard_map/ppermute | solution.py:468
  14.7 1.2 %collective-permute-start.3 = (bf16[144,1024]{1,0:T(8,128)(2,1)}, bf16[144,1024]{1,0:T(8,128)(2,1)S(1)}, u32[]{:S(2)}, u32[]{:S(2)}) collective-permute-start(bf16[144,1024]{1,0:T(8,128)(2,1)} %get-tuple-element.43.refs_0_), channel_id=1, source_target_pairs={{0,12},{4,8},{8,4},{12,0},{1,13},{5,9},{9,5},{13,1},{2,14},{6,10},... | collective-permute-start | bytes 884744 | tf_op jit(solution)/shard_map/ppermute | solution.py:468
  15.9 0.9 attach_sources.1.mine_ref
  16.8 5.1 %all-to-all-done.refs_0_ = bf16[16,32,384]{2,1,0:T(8,128)(2,1)S(1)} async-done(((bf16[16,32,384]{2,1,0:T(8,128)(2,1)}), bf16[16,32,384]{2,1,0:T(8,128)(2,1)S(1)}, u32[]{:S(2)}, u32[]{:S(2)}) %all-to-all-start) | async-done | bytes 393248 | tf_op jit(solution)/shard_map/all_to_all | solution.py:464
  21.9 1.7 %collective-permute-start.2 = (bf16[144,1024]{1,0:T(8,128)(2,1)}, bf16[144,1024]{1,0:T(8,128)(2,1)S(1)}, u32[]{:S(2)}, u32[]{:S(2)}) collective-permute-start(bf16[144,1024]{1,0:T(8,128)(2,1)} %get-tuple-element.43.refs_0_), channel_id=1, source_target_pairs={{0,8},{4,12},{8,0},{12,4},{1,9},{5,13},{9,1},{13,5},{2,10},{6,14},... | collective-permute-start | bytes 884744 | tf_op jit(solution)/shard_map/ppermute | solution.py:468
  23.6 1.2 %collective-permute-start.9 = (bf16[2,32,2176]{2,1,0:T(8,128)(2,1)S(1)}, bf16[2,32,2176]{2,1,0:T(8,128)(2,1)S(1)}, u32[]{:S(2)}, u32[]{:S(2)}) collective-permute-start(bf16[2,32,2176]{2,1,0:T(8,128)(2,1)S(1)} %attach_sources.1.mine_ref), channel_id=1, source_target_pairs={{0,1},{1,0},{2,3},{3,2},{4,5},{5,4},{6,7},{7,6},{8,9},{9,8},{10,11... | collective-permute-start | bytes 835592 | tf_op jit(solution)/shard_map/ppermute | solution.py:468
  25.1 5.2 %collective-permute-done.1.refs_1_ = bf16[144,1024]{1,0:T(8,128)(2,1)S(1)} collective-permute-done((bf16[144,1024]{1,0:T(8,128)(2,1)}, bf16[144,1024]{1,0:T(8,128)(2,1)S(1)}, u32[]{:S(2)}, u32[]{:S(2)}) %collective-permute-start.1) | collective-permute-done | bytes 294944 | tf_op jit(solution)/shard_map/ppermute | solution.py:468
  30.3 1.4 %collective-permute-done.2.refs_2_ = bf16[144,1024]{1,0:T(8,128)(2,1)S(1)} collective-permute-done((bf16[144,1024]{1,0:T(8,128)(2,1)}, bf16[144,1024]{1,0:T(8,128)(2,1)S(1)}, u32[]{:S(2)}, u32[]{:S(2)}) %collective-permute-start.2) | collective-permute-done | bytes 294944 | tf_op jit(solution)/shard_map/ppermute | solution.py:468
  31.7 1.0 collective-permute-start.6
  32.7 0.5 collective-permute-start.5
  33.3 1.0 collective-permute-done.6.refs_6_
  34.3 1.5 %collective-permute-start.10 = (bf16[2,64,1152]{2,1,0:T(8,128)(2,1)S(1)}, bf16[2,64,1152]{2,1,0:T(8,128)(2,1)S(1)}, u32[]{:S(2)}, u32[]{:S(2)}) collective-permute-start(bf16[2,64,1152]{2,1,0:T(8,128)(2,1)S(1)} %bitcast.17), channel_id=1, source_target_pairs={{0,4},{4,0},{8,12},{12,8},{1,5},{5,1},{9,13},{13,9},{2,6},{6,2},{1... | collective-permute-start | bytes 884744 | tf_op jit(solution)/shard_map/ppermute | solution.py:468
  35.9 0.5 collective-permute-start.11
  36.4 1.3 %collective-permute-start.12 = (bf16[2,64,1152]{2,1,0:T(8,128)(2,1)S(1)}, bf16[2,64,1152]{2,1,0:T(8,128)(2,1)S(1)}, u32[]{:S(2)}, u32[]{:S(2)}) collective-permute-start(bf16[2,64,1152]{2,1,0:T(8,128)(2,1)S(1)} %bitcast.19), channel_id=1, source_target_pairs={{0,12},{4,8},{8,4},{12,0},{1,13},{5,9},{9,5},{13,1},{2,14},{6,10},... | collective-permute-start | bytes 884744 | tf_op jit(solution)/shard_map/ppermute | solution.py:468
  37.6 1.0 copy-done.1
  38.6 1.5 %collect.1 = (bf16[1024,1024]{1,0:T(8,128)(2,1)}, f32[8,16,128]{2,1,0:T(8,128)S(1)}) custom-call(bf16[144,1024]{1,0:T(8,128)(2,1)S(1)} %copy-done.1, bf16[144,1024]{1,0:T(8,128)(2,1)S(1)} %collective-permute-done.1.refs_1_, bf16[144,1024]{1,0:T(8,128)(2,1)S(1)} %collective-permute-done.2.refs_2_, bf16[144,1024]{1,0:T(8,128)(2,1)S(1)} %collective-permute-done.3.refs_3_, ...), custom_call_target="tpu_custom_call" | custom-call | bytes 4194304 | tf_op jit(solution)/shard_map/collect/pallas_call | solution.py:63
  40.5 1.3 %project_rims.1 = (bf16[16,2,32,384]{3,2,1,0:T(8,128)(2,1)S(1)}, bf16[128,256]{1,0:T(8,128)(2,1)S(1)}) custom-call(bf16[1024,1024]{1,0:T(8,128)(2,1)} %get-tuple-element.47.normed_any.normed_ref, bf16[16,32,384]{2,1,0:T(8,128)(2,1)S(1)} %all-to-all-done.refs_0_, bf16[16,32,384]{2,1,0:T(8,128)(2,1)S(1)} %collective-permute-done.8.refs_1_), custom_call_target="tpu_custom_call" | custom-call | flops 67108864 | bytes 1048576 | tf_op jit(solution)/shard_map/project_rims/pallas_call | solution.py:63
  41.8 1.8 %collective-permute-start.13 = (bf16[128,256]{1,0:T(8,128)(2,1)S(1)}, bf16[128,256]{1,0:T(8,128)(2,1)S(1)}, u32[]{:S(2)}, u32[]{:S(2)}) collective-permute-start(bf16[128,256]{1,0:T(8,128)(2,1)S(1)} %get-tuple-element.57), channel_id=1, source_target_pairs={{0,16},{16,0},{1,17},{17,1},{2,18},{18,2},{3,19},{19,3},{4,20},{20... | collective-permute-start | bytes 196616 | tf_op jit(solution)/shard_map/ppermute | solution.py:468
  43.6 2.8 %project.1 = (bf16[1024,128]{1,0:T(8,128)(2,1)S(1)}, bf16[1024,256]{1,0:T(8,128)(2,1)S(1)}) custom-call(bf16[1024,1024]{1,0:T(8,128)(2,1)} %get-tuple-element.47.normed_any.normed_ref, bf16[16,2,32,384]{3,2,1,0:T(8,128)(2,1)S(1)} %get-tuple-element.50.w_ref), custom_call_target="tpu_custom_call" | custom-call | flops 805306368 | bytes 4194304 | tf_op jit(solution)/shard_map/project/pallas_call | solution.py:63
  46.5 1.9 %attention_interior.1.done_ref = bf16[1024,128]{1,0:T(8,128)(2,1)S(1)} custom-call(f32[8,16,128]{2,1,0:T(8,128)S(1)} %get-tuple-element.48.steps_ref, bf16[1024,128]{1,0:T(8,128)(2,1)S(1)} %get-tuple-element.51.q_ref, bf16[1024,256]{1,0:T(8,128)(2,1)S(1)} %get-tuple-element.56.kv_ref), custom_call_target="tpu_custom_call" | custom-call | flops 268435456 | bytes 2097152 | tf_op jit(solution)/shard_map/attention_interior/pallas_call | solution.py:63
  48.3 1.4 %collective-permute-done.13.low_ref.high_ref = bf16[128,256]{1,0:T(8,128)(2,1)S(1)} collective-permute-done((bf16[128,256]{1,0:T(8,128)(2,1)S(1)}, bf16[128,256]{1,0:T(8,128)(2,1)S(1)}, u32[]{:S(2)}, u32[]{:S(2)}) %collective-permute-start.13) | collective-permute-done | bytes 65568 | tf_op jit(solution)/shard_map/ppermute | solution.py:468
  49.8 1.4 %attention_edges.1 = bf16[1024,128]{1,0:T(8,128)(2,1)} custom-call(f32[8,16,128]{2,1,0:T(8,128)S(1)} %get-tuple-element.48.steps_ref, bf16[1024,128]{1,0:T(8,128)(2,1)S(1)} %get-tuple-element.51.q_ref, bf16[1024,256]{1,0:T(8,128)(2,1)S(1)} %get-tuple-element.56.kv_ref, bf16[128,256]{1,0:T(8,128)(2,1)S(1)} %collective-permute-done.13.low_ref.high_ref, ...), custom_call_target="tpu_custom_call" | custom-call | flops 67108864 | bytes 1048576 | tf_op jit(solution)/shard_map/attention_edges/pallas_call | solution.py:63
  51.2 8.1 %all-to-all-start.1 = ((bf16[16,64,128]{2,1,0:T(8,128)(2,1)}), bf16[16,64,128]{2,1,0:T(8,128)(2,1)S(1)}, u32[]{:S(2)}, u32[]{:S(2)}) async-start(bf16[16,64,128]{2,1,0:T(8,128)(2,1)} %bitcast.5), calls=%async_computation.1 | async-start | bytes 524288 | tf_op jit(solution)/shard_map/all_to_all | solution.py:464
  59.6 0.4 collective-permute-start.15
  60.5 0.6 collective-permute-done.14.refs_4_
  61.0 0.4 collective-permute-done.15.refs_5_
  61.5 0.4 collective-permute-done.16.refs_6_
  61.9 0.4 collective-permute-done.17.refs_7_
  62.3 1.5 %assemble.1.w_any = bf16[2,4,2,64,1152]{4,3,2,1,0:T(8,128)(2,1)} custom-call(bf16[2,64,1152]{2,1,0:T(8,128)(2,1)S(1)} %bitcast.21, bf16[2,64,1152]{2,1,0:T(8,128)(2,1)S(1)} %collective-permute-done.10.refs_1_, bf16[2,64,1152]{2,1,0:T(8,128)(2,1)S(1)} %collective-permute-done.11.refs_2_, bf16[2,64,1152]{2,1,0:T(8,128)(2,1)S(1)} %collective-permute-done.12.refs_3_, ...), custom_call_target="tpu_custom_call" | custom-call | bytes 4194304 | tf_op jit(solution)/shard_map/assemble/pallas_call | solution.py:63
  63.8 2.4 %all-to-all-done.1.att_ref = bf16[16,64,128]{2,1,0:T(8,128)(2,1)S(1)} async-done(((bf16[16,64,128]{2,1,0:T(8,128)(2,1)}), bf16[16,64,128]{2,1,0:T(8,128)(2,1)S(1)}, u32[]{:S(2)}, u32[]{:S(2)}) %all-to-all-start.1) | async-done | bytes 262176 | tf_op jit(solution)/shard_map/all_to_all | solution.py:464
  66.2 4.4 %mix_loss_backward.1 = (f32[100,128]{1,0:T(8,128)S(1)}, bf16[16,64,128]{2,1,0:T(8,128)(2,1)S(1)}) custom-call(bf16[16,64,128]{2,1,0:T(8,128)(2,1)S(1)} %all-to-all-done.1.att_ref, f32[1,128]{1,0:T(1,128)S(1)} %bitcast.22, f32[100,128]{1,0:T(8,128)} %truth_any.1, bf16[2,4,2,64,1152]{4,3,2,1,0:T(8,128)(2,1)} %assemble.1.w_any, ...), custom_call_target="tpu_custom_call" | custom-call | flops 603979776 | bytes 4194304 | tf_op jit(solution)/shard_map/mix_loss_backward/pallas_call | solution.py:63
  70.7 9.9 %all_to_all.20 = bf16[16,64,128]{2,1,0:T(8,128)(2,1)S(1)} all-to-all(bf16[16,64,128]{2,1,0:T(8,128)(2,1)S(1)} %get-tuple-element.64), channel_id=1, replica_groups=mesh['half'=2,'quad'=4,'core'=2,'ens'=2] {'quad','core','ens'}, dimensions={0} | all-to-all | bytes 524288 | tf_op jit(solution)/shard_map/all_to_all | solution.py:464
  80.5 1.4 %attention_edges_back.1 = (f32[2,256,256]{2,1,0:T(8,128)S(1)}, bf16[128,256]{1,0:T(8,128)(2,1)S(1)}) custom-call(f32[8,16,128]{2,1,0:T(8,128)S(1)} %get-tuple-element.48.steps_ref, bf16[1024,128]{1,0:T(8,128)(2,1)S(1)} %get-tuple-element.51.q_ref, bf16[1024,256]{1,0:T(8,128)(2,1)S(1)} %get-tuple-element.56.kv_ref, ...), custom_call_target="tpu_custom_call" | custom-call | flops 167772160 | bytes 1048576 | tf_op jit(solution)/shard_map/attention_edges_back/pallas_call | solution.py:63
  82.0 3.8 %attention_interior_back.1.grads_ref = f32[1024,256]{1,0:T(8,128)S(1)} custom-call(f32[8,16,128]{2,1,0:T(8,128)S(1)} %get-tuple-element.48.steps_ref, bf16[1024,128]{1,0:T(8,128)(2,1)S(1)} %get-tuple-element.51.q_ref, bf16[1024,256]{1,0:T(8,128)(2,1)S(1)} %get-tuple-element.56.kv_ref, bf16[1024,128]{1,0:T(8,128)(2,1)S(1)} %bitcast.15, ...), custom_call_target="tpu_custom_call" | custom-call | flops 536870912 | bytes 4194304 | tf_op jit(solution)/shard_map/attention_interior_back/pallas_call | solution.py:63
  85.9 1.3 %product.1.total_ref = f32[1024,256]{1,0:T(8,128)S(1)} custom-call(bf16[1024,1024]{1,0:T(8,128)(2,1)S(1)} %copy-done, f32[1024,256]{1,0:T(8,128)S(1)} %attention_interior_back.1.grads_ref), custom_call_target="tpu_custom_call" | custom-call | tf_op jit(solution)/shard_map/product/pallas_call | solution.py:63
  87.2 1.0 collective-permute-done.18.refs_0_
  88.2 1.1 %product_rims.1 = bf16[1024,256]{1,0:T(8,128)(2,1)} custom-call(bf16[1024,1024]{1,0:T(8,128)(2,1)S(1)} %copy-done, f32[1024,256]{1,0:T(8,128)S(1)} %product.1.total_ref, bf16[128,256]{1,0:T(8,128)(2,1)S(1)} %collective-permute-done.18.refs_0_), custom_call_target="tpu_custom_call" | custom-call | flops 67108864 | bytes 2097152 | tf_op jit(solution)/shard_map/product_rims/pallas_call | solution.py:63
  89.3 3.0 %all-to-all-start.3 = ((bf16[32,32,256]{2,1,0:T(8,128)(2,1)}), bf16[32,32,256]{2,1,0:T(8,128)(2,1)S(1)}, u32[]{:S(2)}, u32[]{:S(2)}) async-start(bf16[32,32,256]{2,1,0:T(8,128)(2,1)} %bitcast.9), calls=%async_computation.3 | async-start | bytes 1048576 | tf_op jit(solution)/shard_map/all_to_all | solution.py:464
  92.3 1.5 %collective-permute-start.19 = (f32[100,128]{1,0:T(8,128)S(1)}, f32[100,128]{1,0:T(8,128)S(1)}, u32[]{:S(2)}, u32[]{:S(2)}) collective-permute-start(f32[100,128]{1,0:T(8,128)S(1)} %get-tuple-element.68), channel_id=1, source_target_pairs={{0,1},{1,0},{2,3},{3,2},{4,5},{5,4},{6,7},{7,6},{8,9},{9,8},{10,11... | collective-permute-start | bytes 153608 | tf_op jit(solution)/shard_map/ppermute | solution.py:468
  93.8 4.5 %collective-permute-done.19 = f32[100,128]{1,0:T(8,128)S(1)} collective-permute-done((f32[100,128]{1,0:T(8,128)S(1)}, f32[100,128]{1,0:T(8,128)S(1)}, u32[]{:S(2)}, u32[]{:S(2)}) %collective-permute-start.19) | collective-permute-done | bytes 51232 | tf_op jit(solution)/shard_map/ppermute | solution.py:468
  98.5 0.7 copy.9
  99.2 9.0 %all-to-all-done.3 = bf16[32,32,256]{2,1,0:T(8,128)(2,1)S(1)} async-done(((bf16[32,32,256]{2,1,0:T(8,128)(2,1)}), bf16[32,32,256]{2,1,0:T(8,128)(2,1)S(1)}, u32[]{:S(2)}, u32[]{:S(2)}) %all-to-all-start.3) | async-done | bytes 524320 | tf_op jit(solution)/shard_map/all_to_all | solution.py:464
  108.1 0.8 gather_sums.1
  (30 shorter events, 1.6 us)
Async XLA Ops:
  2.5 9.9 %collective-permute-start = (bf16[32,1152]{1,0:T(8,128)(2,1)}, bf16[32,1152]{1,0:T(8,128)(2,1)S(1)}, u32[]{:S(2)}, u32[]{:S(2)}) collective-permute-start(bf16[32,1152]{1,0:T(8,128)(2,1)} %get-tuple-element.36), channel_id=1, source_target_pairs={{0,16},{16,0},{1,17},{17,1},{2,18},{18,2},{3,19},{19,3},{4,20},{20... | collective-permute-start | bytes 221192 | tf_op jit(solution)/shard_map/ppermute | solution.py:468
  5.7 16.2 %all-to-all-start = ((bf16[16,32,384]{2,1,0:T(8,128)(2,1)}), bf16[16,32,384]{2,1,0:T(8,128)(2,1)S(1)}, u32[]{:S(2)}, u32[]{:S(2)}) async-start(bf16[16,32,384]{2,1,0:T(8,128)(2,1)} %bitcast.23), calls=%async_computation | async-start | bytes 786432 | tf_op jit(solution)/shard_map/all_to_all | solution.py:464
  13.3 17.0 %collective-permute-start.1 = (bf16[144,1024]{1,0:T(8,128)(2,1)}, bf16[144,1024]{1,0:T(8,128)(2,1)S(1)}, u32[]{:S(2)}, u32[]{:S(2)}) collective-permute-start(bf16[144,1024]{1,0:T(8,128)(2,1)} %get-tuple-element.43.refs_0_), channel_id=1, source_target_pairs={{0,4},{4,0},{8,12},{12,8},{1,5},{5,1},{9,13},{13,9},{2,6},{6,2},{1... | collective-permute-start | bytes 884744 | tf_op jit(solution)/shard_map/ppermute | solution.py:468
  14.7 15.6 %collective-permute-start.3 = (bf16[144,1024]{1,0:T(8,128)(2,1)}, bf16[144,1024]{1,0:T(8,128)(2,1)S(1)}, u32[]{:S(2)}, u32[]{:S(2)}) collective-permute-start(bf16[144,1024]{1,0:T(8,128)(2,1)} %get-tuple-element.43.refs_0_), channel_id=1, source_target_pairs={{0,12},{4,8},{8,4},{12,0},{1,13},{5,9},{9,5},{13,1},{2,14},{6,10},... | collective-permute-start | bytes 884744 | tf_op jit(solution)/shard_map/ppermute | solution.py:468
  21.9 9.8 %collective-permute-start.2 = (bf16[144,1024]{1,0:T(8,128)(2,1)}, bf16[144,1024]{1,0:T(8,128)(2,1)S(1)}, u32[]{:S(2)}, u32[]{:S(2)}) collective-permute-start(bf16[144,1024]{1,0:T(8,128)(2,1)} %get-tuple-element.43.refs_0_), channel_id=1, source_target_pairs={{0,8},{4,12},{8,0},{12,4},{1,9},{5,13},{9,1},{13,5},{2,10},{6,14},... | collective-permute-start | bytes 884744 | tf_op jit(solution)/shard_map/ppermute | solution.py:468
  23.6 9.6 %collective-permute-start.9 = (bf16[2,32,2176]{2,1,0:T(8,128)(2,1)S(1)}, bf16[2,32,2176]{2,1,0:T(8,128)(2,1)S(1)}, u32[]{:S(2)}, u32[]{:S(2)}) collective-permute-start(bf16[2,32,2176]{2,1,0:T(8,128)(2,1)S(1)} %attach_sources.1.mine_ref), channel_id=1, source_target_pairs={{0,1},{1,0},{2,3},{3,2},{4,5},{5,4},{6,7},{7,6},{8,9},{9,8},{10,11... | collective-permute-start | bytes 835592 | tf_op jit(solution)/shard_map/ppermute | solution.py:468
  24.8 15.6 %collective-permute-start.8 = (bf16[16,32,384]{2,1,0:T(8,128)(2,1)S(1)}, bf16[16,32,384]{2,1,0:T(8,128)(2,1)S(1)}, u32[]{:S(2)}, u32[]{:S(2)}) collective-permute-start(bf16[16,32,384]{2,1,0:T(8,128)(2,1)S(1)} %all-to-all-done.refs_0_), channel_id=1, source_target_pairs={{0,1},{1,0},{2,3},{3,2},{4,5},{5,4},{6,7},{7,6},{8,9},{9,8},{10,11... | collective-permute-start | bytes 1179656 | tf_op jit(solution)/shard_map/ppermute | solution.py:468
  31.7 2.6 %collective-permute-start.6 = (bf16[144,1024]{1,0:T(8,128)(2,1)S(1)}, bf16[144,1024]{1,0:T(8,128)(2,1)S(1)}, u32[]{:S(2)}, u32[]{:S(2)}) collective-permute-start(bf16[144,1024]{1,0:T(8,128)(2,1)S(1)} %collective-permute-done.2.refs_2_), channel_id=1, source_target_pairs={{0,2},{2,0},{1,3},{3,1},{4,6},{6,4},{5,7},{7,5},{8,10},{10,8},{9,1... | collective-permute-start | bytes 884744 | tf_op jit(solution)/shard_map/ppermute | solution.py:468
  32.7 3.1 %collective-permute-start.4 = (bf16[144,1024]{1,0:T(8,128)(2,1)}, bf16[144,1024]{1,0:T(8,128)(2,1)S(1)}, u32[]{:S(2)}, u32[]{:S(2)}) collective-permute-start(bf16[144,1024]{1,0:T(8,128)(2,1)} %get-tuple-element.43.refs_0_), channel_id=1, source_target_pairs={{0,2},{2,0},{1,3},{3,1},{4,6},{6,4},{5,7},{7,5},{8,10},{10,8},{9,1... | collective-permute-start | bytes 884744 | tf_op jit(solution)/shard_map/ppermute | solution.py:468
  32.7 3.6 %collective-permute-start.5 = (bf16[144,1024]{1,0:T(8,128)(2,1)S(1)}, bf16[144,1024]{1,0:T(8,128)(2,1)S(1)}, u32[]{:S(2)}, u32[]{:S(2)}) collective-permute-start(bf16[144,1024]{1,0:T(8,128)(2,1)S(1)} %collective-permute-done.1.refs_1_), channel_id=1, source_target_pairs={{0,2},{2,0},{1,3},{3,1},{4,6},{6,4},{5,7},{7,5},{8,10},{10,8},{9,1... | collective-permute-start | bytes 884744 | tf_op jit(solution)/shard_map/ppermute | solution.py:468
  33.2 4.4 %collective-permute-start.7 = (bf16[144,1024]{1,0:T(8,128)(2,1)S(1)}, bf16[144,1024]{1,0:T(8,128)(2,1)S(1)}, u32[]{:S(2)}, u32[]{:S(2)}) collective-permute-start(bf16[144,1024]{1,0:T(8,128)(2,1)S(1)} %collective-permute-done.3.refs_3_), channel_id=1, source_target_pairs={{0,2},{2,0},{1,3},{3,1},{4,6},{6,4},{5,7},{7,5},{8,10},{10,8},{9,1... | collective-permute-start | bytes 884744 | tf_op jit(solution)/shard_map/ppermute | solution.py:468
  34.3 25.0 %collective-permute-start.10 = (bf16[2,64,1152]{2,1,0:T(8,128)(2,1)S(1)}, bf16[2,64,1152]{2,1,0:T(8,128)(2,1)S(1)}, u32[]{:S(2)}, u32[]{:S(2)}) collective-permute-start(bf16[2,64,1152]{2,1,0:T(8,128)(2,1)S(1)} %bitcast.17), channel_id=1, source_target_pairs={{0,4},{4,0},{8,12},{12,8},{1,5},{5,1},{9,13},{13,9},{2,6},{6,2},{1... | collective-permute-start | bytes 884744 | tf_op jit(solution)/shard_map/ppermute | solution.py:468
  35.9 23.5 %collective-permute-start.11 = (bf16[2,64,1152]{2,1,0:T(8,128)(2,1)S(1)}, bf16[2,64,1152]{2,1,0:T(8,128)(2,1)S(1)}, u32[]{:S(2)}, u32[]{:S(2)}) collective-permute-start(bf16[2,64,1152]{2,1,0:T(8,128)(2,1)S(1)} %bitcast.18), channel_id=1, source_target_pairs={{0,8},{4,12},{8,0},{12,4},{1,9},{5,13},{9,1},{13,5},{2,10},{6,14},... | collective-permute-start | bytes 884744 | tf_op jit(solution)/shard_map/ppermute | solution.py:468
  36.4 23.0 %collective-permute-start.12 = (bf16[2,64,1152]{2,1,0:T(8,128)(2,1)S(1)}, bf16[2,64,1152]{2,1,0:T(8,128)(2,1)S(1)}, u32[]{:S(2)}, u32[]{:S(2)}) collective-permute-start(bf16[2,64,1152]{2,1,0:T(8,128)(2,1)S(1)} %bitcast.19), channel_id=1, source_target_pairs={{0,12},{4,8},{8,4},{12,0},{1,13},{5,9},{9,5},{13,1},{2,14},{6,10},... | collective-permute-start | bytes 884744 | tf_op jit(solution)/shard_map/ppermute | solution.py:468
  37.6 1.0 copy-start.1
  41.8 8.0 %collective-permute-start.13 = (bf16[128,256]{1,0:T(8,128)(2,1)S(1)}, bf16[128,256]{1,0:T(8,128)(2,1)S(1)}, u32[]{:S(2)}, u32[]{:S(2)}) collective-permute-start(bf16[128,256]{1,0:T(8,128)(2,1)S(1)} %get-tuple-element.57), channel_id=1, source_target_pairs={{0,16},{16,0},{1,17},{17,1},{2,18},{18,2},{3,19},{19,3},{4,20},{20... | collective-permute-start | bytes 196616 | tf_op jit(solution)/shard_map/ppermute | solution.py:468
  51.2 15.0 %all-to-all-start.1 = ((bf16[16,64,128]{2,1,0:T(8,128)(2,1)}), bf16[16,64,128]{2,1,0:T(8,128)(2,1)S(1)}, u32[]{:S(2)}, u32[]{:S(2)}) async-start(bf16[16,64,128]{2,1,0:T(8,128)(2,1)} %bitcast.5), calls=%async_computation.1 | async-start | bytes 524288 | tf_op jit(solution)/shard_map/all_to_all | solution.py:464
  59.3 6.9 %copy-start.2 = (bf16[1,64,1024]{2,1,0:T(8,128)(2,1)S(1)}, bf16[1,64,1024]{2,1,0:T(8,128)(2,1)}, u32[]{:S(2)}) copy-start(bf16[1,64,1024]{2,1,0:T(8,128)(2,1)} %get-tuple-element.62.refs_0_) | copy-start | bytes 393220
  59.3 6.9 %copy-start.3 = (f32[128]{0:T(128)S(1)}, f32[128]{0:T(128)}, u32[]{:S(2)}) copy-start(f32[128]{0:T(128)} %param.12) | copy-start | bytes 1540
  59.4 1.6 %collective-permute-start.14 = (bf16[2,64,1152]{2,1,0:T(8,128)(2,1)S(1)}, bf16[2,64,1152]{2,1,0:T(8,128)(2,1)S(1)}, u32[]{:S(2)}, u32[]{:S(2)}) collective-permute-start(bf16[2,64,1152]{2,1,0:T(8,128)(2,1)S(1)} %bitcast.20), channel_id=1, source_target_pairs={{0,2},{2,0},{1,3},{3,1},{4,6},{6,4},{5,7},{7,5},{8,10},{10,8},{9,1... | collective-permute-start | bytes 884744 | tf_op jit(solution)/shard_map/ppermute | solution.py:468
  59.6 1.9 %collective-permute-start.15 = (bf16[2,64,1152]{2,1,0:T(8,128)(2,1)S(1)}, bf16[2,64,1152]{2,1,0:T(8,128)(2,1)S(1)}, u32[]{:S(2)}, u32[]{:S(2)}) collective-permute-start(bf16[2,64,1152]{2,1,0:T(8,128)(2,1)S(1)} %collective-permute-done.10.refs_1_), channel_id=1, source_target_pairs={{0,2},{2,0},{1,3},{3,1},{4,6},{6,4},{5,7},{7,5},{8,10},{10,8},{9,1... | collective-permute-start | bytes 884744 | tf_op jit(solution)/shard_map/ppermute | solution.py:468
  60.0 1.9 %collective-permute-start.16 = (bf16[2,64,1152]{2,1,0:T(8,128)(2,1)S(1)}, bf16[2,64,1152]{2,1,0:T(8,128)(2,1)S(1)}, u32[]{:S(2)}, u32[]{:S(2)}) collective-permute-start(bf16[2,64,1152]{2,1,0:T(8,128)(2,1)S(1)} %collective-permute-done.11.refs_2_), channel_id=1, source_target_pairs={{0,2},{2,0},{1,3},{3,1},{4,6},{6,4},{5,7},{7,5},{8,10},{10,8},{9,1... | collective-permute-start | bytes 884744 | tf_op jit(solution)/shard_map/ppermute | solution.py:468
  60.1 2.2 %collective-permute-start.17 = (bf16[2,64,1152]{2,1,0:T(8,128)(2,1)S(1)}, bf16[2,64,1152]{2,1,0:T(8,128)(2,1)S(1)}, u32[]{:S(2)}, u32[]{:S(2)}) collective-permute-start(bf16[2,64,1152]{2,1,0:T(8,128)(2,1)S(1)} %collective-permute-done.12.refs_3_), channel_id=1, source_target_pairs={{0,2},{2,0},{1,3},{3,1},{4,6},{6,4},{5,7},{7,5},{8,10},{10,8},{9,1... | collective-permute-start | bytes 884744 | tf_op jit(solution)/shard_map/ppermute | solution.py:468
  70.6 15.2 %copy-start = (bf16[1024,1024]{1,0:T(8,128)(2,1)S(1)}, bf16[1024,1024]{1,0:T(8,128)(2,1)}, u32[]{:S(2)}) copy-start(bf16[1024,1024]{1,0:T(8,128)(2,1)} %get-tuple-element.47.normed_any.normed_ref) | copy-start | bytes 6291460
  81.9 6.3 %collective-permute-start.18 = (bf16[128,256]{1,0:T(8,128)(2,1)S(1)}, bf16[128,256]{1,0:T(8,128)(2,1)S(1)}, u32[]{:S(2)}, u32[]{:S(2)}) collective-permute-start(bf16[128,256]{1,0:T(8,128)(2,1)S(1)} %get-tuple-element.66), channel_id=1, source_target_pairs={{0,16},{16,0},{1,17},{17,1},{2,18},{18,2},{3,19},{19,3},{4,20},{20... | collective-permute-start | bytes 196616 | tf_op jit(solution)/shard_map/ppermute | solution.py:468
  89.3 18.8 %all-to-all-start.3 = ((bf16[32,32,256]{2,1,0:T(8,128)(2,1)}), bf16[32,32,256]{2,1,0:T(8,128)(2,1)S(1)}, u32[]{:S(2)}, u32[]{:S(2)}) async-start(bf16[32,32,256]{2,1,0:T(8,128)(2,1)} %bitcast.9), calls=%async_computation.3 | async-start | bytes 1048576 | tf_op jit(solution)/shard_map/all_to_all | solution.py:464
  92.3 6.0 %collective-permute-start.19 = (f32[100,128]{1,0:T(8,128)S(1)}, f32[100,128]{1,0:T(8,128)S(1)}, u32[]{:S(2)}, u32[]{:S(2)}) collective-permute-start(f32[100,128]{1,0:T(8,128)S(1)} %get-tuple-element.68), channel_id=1, source_target_pairs={{0,1},{1,0},{2,3},{3,2},{4,5},{5,4},{6,7},{7,6},{8,9},{9,8},{10,11... | collective-permute-start | bytes 153608 | tf_op jit(solution)/shard_map/ppermute | solution.py:468

commit v28 on v27

--- a/solution.py
+++ b/solution.py
@@ -359,7 +359,7 @@
     members_num, part, _ = source.shape
     halves = w.shape[0]
     ens = lax.axis_index("ens")
-    copies = fetch([(w_any.at[0], w.at[0])], sems)
+    copies = fetch([(w_any.at[half], w.at[half]) for half in range(halves)], sems)
     pairs = [(truth_any, truth_ref)]
     if len(sources) == 1:
         pairs.append((sources[0], source))
@@ -383,8 +383,6 @@
     count = LATENT_DIM // halves
     for half in range(halves):
         copies[half].wait()
-        if half + 1 < halves:
-            copies += fetch([(w_any.at[half + 1], w.at[half + 1])], sems, half + 1)
         mix = w[half].reshape(count, LATENT_DIM + FIELD_PAD)[:, :LATENT_DIM]
         hidden += jnp.dot(
             a[:, half * count : (half + 1) * count], mix, preferred_element_type=F32
@@ -572,7 +570,7 @@
     else:
         packed = in_order(packed, "ens", 1).reshape(halves, members_num * shard, width)
     packed, near[2] = lax.optimization_barrier((packed, near[2]))
-    pieces = [packed] + [swap(packed, "quad", step) for step in range(1, QUAD)]
+    pieces = [packed] + [swap(packed, "quad", step) for step in range(1, QUAD - 1)]
 
     rim = ((RIM, 2 * COLS), BF16)
     rims = [rim] if halves == 2 else [rim, rim]
@@ -626,6 +624,8 @@
         exps=rows * 128,
     )(steps, queries, own, low, high, outcome)
     *pieces, own = lax.optimization_barrier((*pieces, own))
+    packed, low = lax.optimization_barrier((packed, low))
+    pieces.append(swap(packed, "quad", QUAD - 1))
     pieces = pieces + [swap(piece, "core", 1) for piece in pieces]
     attended = exchange(outcome.reshape(GROUP * members_num, part, COLS), ("quad", "core", "ens"))
     block = (halves, QUAD, CORES, members_num * shard, width)

time: 110 us -> 115 us (1.045)
  waiting for transfers between devices: 33.3 us -> 38 us
  starting transfers between devices: 34.2 us -> 35.5 us
    ppermute x20, waiting for transfers between devices: 16.8 us -> 22 us  [swap(): lax.ppermute(value, axis, [(i, i ^ step) for i in range(lax.axis_size(axi...]
    ppermute x20, starting transfers between devices: 18.4 us -> 22.2 us  [swap(): lax.ppermute(value, axis, [(i, i ^ step) for i in range(lax.axis_size(axi...]
    all_to_all x3, starting transfers between devices: 15.9 us -> 13.4 us  [exchange(): return lax.all_to_all(chunks, axes, 0, 0)]
  transfers between devices with their start and end apart: 23 -> 23, of which waited for: 14 -> 13; matrix products, arithmetic and copies ran while one was open for 2% -> 2% of each run, Pallas kernels for 17% -> 16%
where the time goes in v28:
time: 115 us; the launch traced here: 114 us
  waiting for transfers between devices  38 us (33%)
  starting transfers between devices  35.5 us (31%)
  Pallas kernels  27.2 us (24%)
  blocking collectives  9.9 us (9%)
  local copies, waits for them, and re-layouts  1.73 us (2%)
    pallas_call x16, Pallas kernels, run(): made(*[pltpu.with_memory_space_constraint(arg, pltpu.HBM) if space == 'h'...  27.2 us
    ppermute x20, starting transfers between devices, swap(): lax.ppermute(value, axis, [(i, i ^ step) for i in range(lax.axis_size(axi...  22.2 us
    ppermute x20, waiting for transfers between devices, swap(): lax.ppermute(value, axis, [(i, i ^ step) for i in range(lax.axis_size(axi...  22 us
    all_to_all x3, waiting for transfers between devices, exchange(): return lax.all_to_all(chunks, axes, 0, 0)  15.9 us
    all_to_all x3, starting transfers between devices, exchange(): return lax.all_to_all(chunks, axes, 0, 0)  13.4 us
    all_to_all x1, blocking collectives, exchange(): return lax.all_to_all(chunks, axes, 0, 0)  9.9 us
  transfers between devices with their start and end apart: 23, of which 13 were waited for; matrix products, arithmetic and copies ran while one was open for 2% of the time, Pallas kernels for 16%

profile of v28, /device:TPU:1, one launch (start us, length us, event | category | flops | bytes accessed | tf_op | source)
XLA Modules:
  0.0 114.2 jit_solution(12989347906255442466)
XLA Ops:
  0.6 1.8 %prepare_weights.1 = (bf16[2,8,1,32,384]{4,3,2,1,0:T(8,128)(2,1)}, bf16[32,1152]{1,0:T(8,128)(2,1)}) custom-call(bf16[32,3072]{1,0:T(8,128)(2,1)} %w_any.1, bf16[32,1024]{1,0:T(8,128)(2,1)} %mix_any.1, bf16[32,100]{1,0:T(8,128)(2,1)} %readout_any.1), custom_call_target="tpu_custom_call" | custom-call | bytes 1048576 | tf_op jit(solution)/shard_map/prepare_weights/pallas_call | solution.py:63
  2.5 3.2 %collective-permute-start = (bf16[32,1152]{1,0:T(8,128)(2,1)}, bf16[32,1152]{1,0:T(8,128)(2,1)S(1)}, u32[]{:S(2)}, u32[]{:S(2)}) collective-permute-start(bf16[32,1152]{1,0:T(8,128)(2,1)} %get-tuple-element.37), channel_id=1, source_target_pairs={{0,16},{16,0},{1,17},{17,1},{2,18},{18,2},{3,19},{19,3},{4,20},{20... | collective-permute-start | bytes 221192 | tf_op jit(solution)/shard_map/ppermute | solution.py:466
  5.7 4.8 %all-to-all-start = ((bf16[16,32,384]{2,1,0:T(8,128)(2,1)}), bf16[16,32,384]{2,1,0:T(8,128)(2,1)S(1)}, u32[]{:S(2)}, u32[]{:S(2)}) async-start(bf16[16,32,384]{2,1,0:T(8,128)(2,1)} %bitcast.23), calls=%async_computation | async-start | bytes 786432 | tf_op jit(solution)/shard_map/all_to_all | solution.py:462
  10.4 1.9 %norm.1 = (bf16[144,1024]{1,0:T(8,128)(2,1)}, bf16[1,64,1024]{2,1,0:T(8,128)(2,1)}, bf16[1,64,1024]{2,1,0:T(8,128)(2,1)}) custom-call(s32[2,4]{1,0:T(2,128)} %near_any.1, bf16[128,1024]{1,0:T(8,128)(2,1)} %bitcast.24), custom_call_target="tpu_custom_call" | custom-call | flops 1048576 | bytes 1048576 | tf_op jit(solution)/shard_map/norm/pallas_call | solution.py:63
  12.3 0.9 select_bitcast_fusion.1
  13.3 1.5 %collective-permute-start.1 = (bf16[144,1024]{1,0:T(8,128)(2,1)}, bf16[144,1024]{1,0:T(8,128)(2,1)S(1)}, u32[]{:S(2)}, u32[]{:S(2)}) collective-permute-start(bf16[144,1024]{1,0:T(8,128)(2,1)} %get-tuple-element.44.refs_0_), channel_id=1, source_target_pairs={{0,4},{4,0},{8,12},{12,8},{1,5},{5,1},{9,13},{13,9},{2,6},{6,2},{1... | collective-permute-start | bytes 884744 | tf_op jit(solution)/shard_map/ppermute | solution.py:466
  14.7 1.2 %collective-permute-start.3 = (bf16[144,1024]{1,0:T(8,128)(2,1)}, bf16[144,1024]{1,0:T(8,128)(2,1)S(1)}, u32[]{:S(2)}, u32[]{:S(2)}) collective-permute-start(bf16[144,1024]{1,0:T(8,128)(2,1)} %get-tuple-element.44.refs_0_), channel_id=1, source_target_pairs={{0,12},{4,8},{8,4},{12,0},{1,13},{5,9},{9,5},{13,1},{2,14},{6,10},... | collective-permute-start | bytes 884744 | tf_op jit(solution)/shard_map/ppermute | solution.py:466
  15.9 0.9 attach_sources.1.mine_ref
  16.8 5.1 %all-to-all-done.refs_0_ = bf16[16,32,384]{2,1,0:T(8,128)(2,1)S(1)} async-done(((bf16[16,32,384]{2,1,0:T(8,128)(2,1)}), bf16[16,32,384]{2,1,0:T(8,128)(2,1)S(1)}, u32[]{:S(2)}, u32[]{:S(2)}) %all-to-all-start) | async-done | bytes 393248 | tf_op jit(solution)/shard_map/all_to_all | solution.py:462
  21.9 1.7 %collective-permute-start.2 = (bf16[144,1024]{1,0:T(8,128)(2,1)}, bf16[144,1024]{1,0:T(8,128)(2,1)S(1)}, u32[]{:S(2)}, u32[]{:S(2)}) collective-permute-start(bf16[144,1024]{1,0:T(8,128)(2,1)} %get-tuple-element.44.refs_0_), channel_id=1, source_target_pairs={{0,8},{4,12},{8,0},{12,4},{1,9},{5,13},{9,1},{13,5},{2,10},{6,14},... | collective-permute-start | bytes 884744 | tf_op jit(solution)/shard_map/ppermute | solution.py:466
  23.6 6.7 %collective-permute-done.1.refs_1_ = bf16[144,1024]{1,0:T(8,128)(2,1)S(1)} collective-permute-done((bf16[144,1024]{1,0:T(8,128)(2,1)}, bf16[144,1024]{1,0:T(8,128)(2,1)S(1)}, u32[]{:S(2)}, u32[]{:S(2)}) %collective-permute-start.1) | collective-permute-done | bytes 294944 | tf_op jit(solution)/shard_map/ppermute | solution.py:466
  30.3 1.4 %collective-permute-done.2.refs_2_ = bf16[144,1024]{1,0:T(8,128)(2,1)S(1)} collective-permute-done((bf16[144,1024]{1,0:T(8,128)(2,1)}, bf16[144,1024]{1,0:T(8,128)(2,1)S(1)}, u32[]{:S(2)}, u32[]{:S(2)}) %collective-permute-start.2) | collective-permute-done | bytes 294944 | tf_op jit(solution)/shard_map/ppermute | solution.py:466
  31.7 1.0 collective-permute-start.6
  32.7 1.2 %collective-permute-start.8 = (bf16[16,32,384]{2,1,0:T(8,128)(2,1)S(1)}, bf16[16,32,384]{2,1,0:T(8,128)(2,1)S(1)}, u32[]{:S(2)}, u32[]{:S(2)}) collective-permute-start(bf16[16,32,384]{2,1,0:T(8,128)(2,1)S(1)} %all-to-all-done.refs_0_), channel_id=1, source_target_pairs={{0,1},{1,0},{2,3},{3,2},{4,5},{5,4},{6,7},{7,6},{8,9},{9,8},{10,11... | collective-permute-start | bytes 1179656 | tf_op jit(solution)/shard_map/ppermute | solution.py:466
  34.7 0.4 collective-permute-start.9
  35.2 0.6 collective-permute-done.4.refs_4_
  35.9 0.4 collective-permute-done.7.refs_7_
  36.4 1.0 copy-done.1
  37.3 1.5 %collect.1 = (bf16[1024,1024]{1,0:T(8,128)(2,1)}, f32[8,16,128]{2,1,0:T(8,128)S(1)}) custom-call(bf16[144,1024]{1,0:T(8,128)(2,1)S(1)} %copy-done.1, bf16[144,1024]{1,0:T(8,128)(2,1)S(1)} %collective-permute-done.1.refs_1_, bf16[144,1024]{1,0:T(8,128)(2,1)S(1)} %collective-permute-done.2.refs_2_, bf16[144,1024]{1,0:T(8,128)(2,1)S(1)} %collective-permute-done.3.refs_3_, ...), custom_call_target="tpu_custom_call" | custom-call | bytes 4194304 | tf_op jit(solution)/shard_map/collect/pallas_call | solution.py:63
  38.8 4.6 %collective-permute-done.8.refs_1_ = bf16[16,32,384]{2,1,0:T(8,128)(2,1)S(1)} collective-permute-done((bf16[16,32,384]{2,1,0:T(8,128)(2,1)S(1)}, bf16[16,32,384]{2,1,0:T(8,128)(2,1)S(1)}, u32[]{:S(2)}, u32[]{:S(2)}) %collective-permute-start.8) | collective-permute-done | bytes 393248 | tf_op jit(solution)/shard_map/ppermute | solution.py:466
  43.5 1.3 %project_rims.1 = (bf16[16,2,32,384]{3,2,1,0:T(8,128)(2,1)S(1)}, bf16[128,256]{1,0:T(8,128)(2,1)S(1)}) custom-call(bf16[1024,1024]{1,0:T(8,128)(2,1)} %get-tuple-element.48.normed_any.normed_ref, bf16[16,32,384]{2,1,0:T(8,128)(2,1)S(1)} %all-to-all-done.refs_0_, bf16[16,32,384]{2,1,0:T(8,128)(2,1)S(1)} %collective-permute-done.8.refs_1_), custom_call_target="tpu_custom_call" | custom-call | flops 67108864 | bytes 1048576 | tf_op jit(solution)/shard_map/project_rims/pallas_call | solution.py:63
  44.8 2.3 %collective-permute-start.12 = (bf16[128,256]{1,0:T(8,128)(2,1)S(1)}, bf16[128,256]{1,0:T(8,128)(2,1)S(1)}, u32[]{:S(2)}, u32[]{:S(2)}) collective-permute-start(bf16[128,256]{1,0:T(8,128)(2,1)S(1)} %get-tuple-element.58), channel_id=1, source_target_pairs={{0,16},{16,0},{1,17},{17,1},{2,18},{18,2},{3,19},{19,3},{4,20},{20... | collective-permute-start | bytes 196616 | tf_op jit(solution)/shard_map/ppermute | solution.py:466
  47.1 2.4 %collective-permute-done.9.other_ref = bf16[2,32,2176]{2,1,0:T(8,128)(2,1)S(1)} collective-permute-done((bf16[2,32,2176]{2,1,0:T(8,128)(2,1)S(1)}, bf16[2,32,2176]{2,1,0:T(8,128)(2,1)S(1)}, u32[]{:S(2)}, u32[]{:S(2)}) %collective-permute-start.9) | collective-permute-done | bytes 278560 | tf_op jit(solution)/shard_map/ppermute | solution.py:466
  49.5 1.6 %collective-permute-start.10 = (bf16[2,64,1152]{2,1,0:T(8,128)(2,1)S(1)}, bf16[2,64,1152]{2,1,0:T(8,128)(2,1)S(1)}, u32[]{:S(2)}, u32[]{:S(2)}) collective-permute-start(bf16[2,64,1152]{2,1,0:T(8,128)(2,1)S(1)} %bitcast.17), channel_id=1, source_target_pairs={{0,4},{4,0},{8,12},{12,8},{1,5},{5,1},{9,13},{13,9},{2,6},{6,2},{1... | collective-permute-start | bytes 884744 | tf_op jit(solution)/shard_map/ppermute | solution.py:466
  51.1 0.5 collective-permute-start.11
  51.6 0.8 collective-permute-start.13
  52.4 2.8 %project.1 = (bf16[1024,128]{1,0:T(8,128)(2,1)S(1)}, bf16[1024,256]{1,0:T(8,128)(2,1)S(1)}) custom-call(bf16[1024,1024]{1,0:T(8,128)(2,1)} %get-tuple-element.48.normed_any.normed_ref, bf16[16,2,32,384]{3,2,1,0:T(8,128)(2,1)S(1)} %get-tuple-element.51.w_ref), custom_call_target="tpu_custom_call" | custom-call | flops 805306368 | bytes 4194304 | tf_op jit(solution)/shard_map/project/pallas_call | solution.py:63
  55.2 1.9 %attention_interior.1.done_ref = bf16[1024,128]{1,0:T(8,128)(2,1)S(1)} custom-call(f32[8,16,128]{2,1,0:T(8,128)S(1)} %get-tuple-element.49.steps_ref, bf16[1024,128]{1,0:T(8,128)(2,1)S(1)} %get-tuple-element.52.q_ref, bf16[1024,256]{1,0:T(8,128)(2,1)S(1)} %get-tuple-element.57.kv_ref), custom_call_target="tpu_custom_call" | custom-call | flops 268435456 | bytes 2097152 | tf_op jit(solution)/shard_map/attention_interior/pallas_call | solution.py:63
  57.1 1.4 %attention_edges.1 = bf16[1024,128]{1,0:T(8,128)(2,1)} custom-call(f32[8,16,128]{2,1,0:T(8,128)S(1)} %get-tuple-element.49.steps_ref, bf16[1024,128]{1,0:T(8,128)(2,1)S(1)} %get-tuple-element.52.q_ref, bf16[1024,256]{1,0:T(8,128)(2,1)S(1)} %get-tuple-element.57.kv_ref, bf16[128,256]{1,0:T(8,128)(2,1)S(1)} %collective-permute-done.12.low_ref.high_ref, ...), custom_call_target="tpu_custom_call" | custom-call | flops 67108864 | bytes 1048576 | tf_op jit(solution)/shard_map/attention_edges/pallas_call | solution.py:63
  58.5 5.7 %all-to-all-start.1 = ((bf16[16,64,128]{2,1,0:T(8,128)(2,1)}), bf16[16,64,128]{2,1,0:T(8,128)(2,1)S(1)}, u32[]{:S(2)}, u32[]{:S(2)}) async-start(bf16[16,64,128]{2,1,0:T(8,128)(2,1)} %bitcast.5), calls=%async_computation.1 | async-start | bytes 524288 | tf_op jit(solution)/shard_map/all_to_all | solution.py:462
  64.5 0.4 collective-permute-start.15
  65.0 1.7 %collective-permute-start.17 = (bf16[2,64,1152]{2,1,0:T(8,128)(2,1)S(1)}, bf16[2,64,1152]{2,1,0:T(8,128)(2,1)S(1)}, u32[]{:S(2)}, u32[]{:S(2)}) collective-permute-start(bf16[2,64,1152]{2,1,0:T(8,128)(2,1)S(1)} %collective-permute-done.13.refs_3_), channel_id=1, source_target_pairs={{0,2},{2,0},{1,3},{3,1},{4,6},{6,4},{5,7},{7,5},{8,10},{10,8},{9,1... | collective-permute-start | bytes 884744 | tf_op jit(solution)/shard_map/ppermute | solution.py:466
  66.8 1.1 collective-permute-done.17.refs_7_
  67.8 1.5 %assemble.1.w_any = bf16[2,4,2,64,1152]{4,3,2,1,0:T(8,128)(2,1)} custom-call(bf16[2,64,1152]{2,1,0:T(8,128)(2,1)S(1)} %bitcast.21, bf16[2,64,1152]{2,1,0:T(8,128)(2,1)S(1)} %collective-permute-done.10.refs_1_, bf16[2,64,1152]{2,1,0:T(8,128)(2,1)S(1)} %collective-permute-done.11.refs_2_, bf16[2,64,1152]{2,1,0:T(8,128)(2,1)S(1)} %collective-permute-done.13.refs_3_, ...), custom_call_target="tpu_custom_call" | custom-call | bytes 4194304 | tf_op jit(solution)/shard_map/assemble/pallas_call | solution.py:63
  69.3 1.8 %all-to-all-done.1.att_ref = bf16[16,64,128]{2,1,0:T(8,128)(2,1)S(1)} async-done(((bf16[16,64,128]{2,1,0:T(8,128)(2,1)}), bf16[16,64,128]{2,1,0:T(8,128)(2,1)S(1)}, u32[]{:S(2)}, u32[]{:S(2)}) %all-to-all-start.1) | async-done | bytes 262176 | tf_op jit(solution)/shard_map/all_to_all | solution.py:462
  71.1 3.7 %mix_loss_backward.1 = (f32[100,128]{1,0:T(8,128)S(1)}, bf16[16,64,128]{2,1,0:T(8,128)(2,1)S(1)}) custom-call(bf16[16,64,128]{2,1,0:T(8,128)(2,1)S(1)} %all-to-all-done.1.att_ref, f32[1,128]{1,0:T(1,128)S(1)} %bitcast.22, f32[100,128]{1,0:T(8,128)} %truth_any.1, bf16[2,4,2,64,1152]{4,3,2,1,0:T(8,128)(2,1)} %assemble.1.w_any, ...), custom_call_target="tpu_custom_call" | custom-call | flops 603979776 | bytes 4194304 | tf_op jit(solution)/shard_map/mix_loss_backward/pallas_call | solution.py:63
  74.8 9.9 %all_to_all.20 = bf16[16,64,128]{2,1,0:T(8,128)(2,1)S(1)} all-to-all(bf16[16,64,128]{2,1,0:T(8,128)(2,1)S(1)} %get-tuple-element.65), channel_id=1, replica_groups=mesh['half'=2,'quad'=4,'core'=2,'ens'=2] {'quad','core','ens'}, dimensions={0} | all-to-all | bytes 524288 | tf_op jit(solution)/shard_map/all_to_all | solution.py:462
  84.7 1.4 %attention_edges_back.1 = (f32[2,256,256]{2,1,0:T(8,128)S(1)}, bf16[128,256]{1,0:T(8,128)(2,1)S(1)}) custom-call(f32[8,16,128]{2,1,0:T(8,128)S(1)} %get-tuple-element.49.steps_ref, bf16[1024,128]{1,0:T(8,128)(2,1)S(1)} %get-tuple-element.52.q_ref, bf16[1024,256]{1,0:T(8,128)(2,1)S(1)} %get-tuple-element.57.kv_ref, ...), custom_call_target="tpu_custom_call" | custom-call | flops 167772160 | bytes 1048576 | tf_op jit(solution)/shard_map/attention_edges_back/pallas_call | solution.py:63
  86.1 2.2 %collective-permute-start.18 = (bf16[128,256]{1,0:T(8,128)(2,1)S(1)}, bf16[128,256]{1,0:T(8,128)(2,1)S(1)}, u32[]{:S(2)}, u32[]{:S(2)}) collective-permute-start(bf16[128,256]{1,0:T(8,128)(2,1)S(1)} %get-tuple-element.68), channel_id=1, source_target_pairs={{0,16},{16,0},{1,17},{17,1},{2,18},{18,2},{3,19},{19,3},{4,20},{20... | collective-permute-start | bytes 196616 | tf_op jit(solution)/shard_map/ppermute | solution.py:466
  88.3 3.8 %attention_interior_back.1.grads_ref = f32[1024,256]{1,0:T(8,128)S(1)} custom-call(f32[8,16,128]{2,1,0:T(8,128)S(1)} %get-tuple-element.49.steps_ref, bf16[1024,128]{1,0:T(8,128)(2,1)S(1)} %get-tuple-element.52.q_ref, bf16[1024,256]{1,0:T(8,128)(2,1)S(1)} %get-tuple-element.57.kv_ref, bf16[1024,128]{1,0:T(8,128)(2,1)S(1)} %bitcast.15, ...), custom_call_target="tpu_custom_call" | custom-call | flops 536870912 | bytes 4194304 | tf_op jit(solution)/shard_map/attention_interior_back/pallas_call | solution.py:63
  92.1 1.3 %product.1.total_ref = f32[1024,256]{1,0:T(8,128)S(1)} custom-call(bf16[1024,1024]{1,0:T(8,128)(2,1)S(1)} %copy-done, f32[1024,256]{1,0:T(8,128)S(1)} %attention_interior_back.1.grads_ref), custom_call_target="tpu_custom_call" | custom-call | tf_op jit(solution)/shard_map/product/pallas_call | solution.py:63
  93.4 1.1 product_rims.1
  94.6 2.9 %all-to-all-start.3 = ((bf16[32,32,256]{2,1,0:T(8,128)(2,1)}), bf16[32,32,256]{2,1,0:T(8,128)(2,1)S(1)}, u32[]{:S(2)}, u32[]{:S(2)}) async-start(bf16[32,32,256]{2,1,0:T(8,128)(2,1)} %bitcast.9), calls=%async_computation.3 | async-start | bytes 1048576 | tf_op jit(solution)/shard_map/all_to_all | solution.py:462
  97.5 1.5 %collective-permute-start.19 = (f32[100,128]{1,0:T(8,128)S(1)}, f32[100,128]{1,0:T(8,128)S(1)}, u32[]{:S(2)}, u32[]{:S(2)}) collective-permute-start(f32[100,128]{1,0:T(8,128)S(1)} %get-tuple-element.70), channel_id=1, source_target_pairs={{0,1},{1,0},{2,3},{3,2},{4,5},{5,4},{6,7},{7,6},{8,9},{9,8},{10,11... | collective-permute-start | bytes 153608 | tf_op jit(solution)/shard_map/ppermute | solution.py:466
  99.0 4.5 %collective-permute-done.19 = f32[100,128]{1,0:T(8,128)S(1)} collective-permute-done((f32[100,128]{1,0:T(8,128)S(1)}, f32[100,128]{1,0:T(8,128)S(1)}, u32[]{:S(2)}, u32[]{:S(2)}) %collective-permute-start.19) | collective-permute-done | bytes 51232 | tf_op jit(solution)/shard_map/ppermute | solution.py:466
  103.7 0.7 copy.9
  104.4 9.1 %all-to-all-done.3 = bf16[32,32,256]{2,1,0:T(8,128)(2,1)S(1)} async-done(((bf16[32,32,256]{2,1,0:T(8,128)(2,1)}), bf16[32,32,256]{2,1,0:T(8,128)(2,1)S(1)}, u32[]{:S(2)}, u32[]{:S(2)}) %all-to-all-start.3) | async-done | bytes 524320 | tf_op jit(solution)/shard_map/all_to_all | solution.py:462
  113.4 0.8 gather_sums.1
  (30 shorter events, 1.7 us)
Async XLA Ops:
  2.5 9.9 %collective-permute-start = (bf16[32,1152]{1,0:T(8,128)(2,1)}, bf16[32,1152]{1,0:T(8,128)(2,1)S(1)}, u32[]{:S(2)}, u32[]{:S(2)}) collective-permute-start(bf16[32,1152]{1,0:T(8,128)(2,1)} %get-tuple-element.37), channel_id=1, source_target_pairs={{0,16},{16,0},{1,17},{17,1},{2,18},{18,2},{3,19},{19,3},{4,20},{20... | collective-permute-start | bytes 221192 | tf_op jit(solution)/shard_map/ppermute | solution.py:466
  5.7 16.2 %all-to-all-start = ((bf16[16,32,384]{2,1,0:T(8,128)(2,1)}), bf16[16,32,384]{2,1,0:T(8,128)(2,1)S(1)}, u32[]{:S(2)}, u32[]{:S(2)}) async-start(bf16[16,32,384]{2,1,0:T(8,128)(2,1)} %bitcast.23), calls=%async_computation | async-start | bytes 786432 | tf_op jit(solution)/shard_map/all_to_all | solution.py:462
  13.3 17.0 %collective-permute-start.1 = (bf16[144,1024]{1,0:T(8,128)(2,1)}, bf16[144,1024]{1,0:T(8,128)(2,1)S(1)}, u32[]{:S(2)}, u32[]{:S(2)}) collective-permute-start(bf16[144,1024]{1,0:T(8,128)(2,1)} %get-tuple-element.44.refs_0_), channel_id=1, source_target_pairs={{0,4},{4,0},{8,12},{12,8},{1,5},{5,1},{9,13},{13,9},{2,6},{6,2},{1... | collective-permute-start | bytes 884744 | tf_op jit(solution)/shard_map/ppermute | solution.py:466
  14.7 15.6 %collective-permute-start.3 = (bf16[144,1024]{1,0:T(8,128)(2,1)}, bf16[144,1024]{1,0:T(8,128)(2,1)S(1)}, u32[]{:S(2)}, u32[]{:S(2)}) collective-permute-start(bf16[144,1024]{1,0:T(8,128)(2,1)} %get-tuple-element.44.refs_0_), channel_id=1, source_target_pairs={{0,12},{4,8},{8,4},{12,0},{1,13},{5,9},{9,5},{13,1},{2,14},{6,10},... | collective-permute-start | bytes 884744 | tf_op jit(solution)/shard_map/ppermute | solution.py:466
  21.9 9.8 %collective-permute-start.2 = (bf16[144,1024]{1,0:T(8,128)(2,1)}, bf16[144,1024]{1,0:T(8,128)(2,1)S(1)}, u32[]{:S(2)}, u32[]{:S(2)}) collective-permute-start(bf16[144,1024]{1,0:T(8,128)(2,1)} %get-tuple-element.44.refs_0_), channel_id=1, source_target_pairs={{0,8},{4,12},{8,0},{12,4},{1,9},{5,13},{9,1},{13,5},{2,10},{6,14},... | collective-permute-start | bytes 884744 | tf_op jit(solution)/shard_map/ppermute | solution.py:466
  31.7 3.1 %collective-permute-start.6 = (bf16[144,1024]{1,0:T(8,128)(2,1)S(1)}, bf16[144,1024]{1,0:T(8,128)(2,1)S(1)}, u32[]{:S(2)}, u32[]{:S(2)}) collective-permute-start(bf16[144,1024]{1,0:T(8,128)(2,1)S(1)} %collective-permute-done.2.refs_2_), channel_id=1, source_target_pairs={{0,2},{2,0},{1,3},{3,1},{4,6},{6,4},{5,7},{7,5},{8,10},{10,8},{9,1... | collective-permute-start | bytes 884744 | tf_op jit(solution)/shard_map/ppermute | solution.py:466
  32.7 10.7 %collective-permute-start.8 = (bf16[16,32,384]{2,1,0:T(8,128)(2,1)S(1)}, bf16[16,32,384]{2,1,0:T(8,128)(2,1)S(1)}, u32[]{:S(2)}, u32[]{:S(2)}) collective-permute-start(bf16[16,32,384]{2,1,0:T(8,128)(2,1)S(1)} %all-to-all-done.refs_0_), channel_id=1, source_target_pairs={{0,1},{1,0},{2,3},{3,2},{4,5},{5,4},{6,7},{7,6},{8,9},{9,8},{10,11... | collective-permute-start | bytes 1179656 | tf_op jit(solution)/shard_map/ppermute | solution.py:466
  33.9 1.8 %collective-permute-start.4 = (bf16[144,1024]{1,0:T(8,128)(2,1)}, bf16[144,1024]{1,0:T(8,128)(2,1)S(1)}, u32[]{:S(2)}, u32[]{:S(2)}) collective-permute-start(bf16[144,1024]{1,0:T(8,128)(2,1)} %get-tuple-element.44.refs_0_), channel_id=1, source_target_pairs={{0,2},{2,0},{1,3},{3,1},{4,6},{6,4},{5,7},{7,5},{8,10},{10,8},{9,1... | collective-permute-start | bytes 884744 | tf_op jit(solution)/shard_map/ppermute | solution.py:466
  34.2 1.7 %collective-permute-start.5 = (bf16[144,1024]{1,0:T(8,128)(2,1)S(1)}, bf16[144,1024]{1,0:T(8,128)(2,1)S(1)}, u32[]{:S(2)}, u32[]{:S(2)}) collective-permute-start(bf16[144,1024]{1,0:T(8,128)(2,1)S(1)} %collective-permute-done.1.refs_1_), channel_id=1, source_target_pairs={{0,2},{2,0},{1,3},{3,1},{4,6},{6,4},{5,7},{7,5},{8,10},{10,8},{9,1... | collective-permute-start | bytes 884744 | tf_op jit(solution)/shard_map/ppermute | solution.py:466
  34.5 1.9 %collective-permute-start.7 = (bf16[144,1024]{1,0:T(8,128)(2,1)S(1)}, bf16[144,1024]{1,0:T(8,128)(2,1)S(1)}, u32[]{:S(2)}, u32[]{:S(2)}) collective-permute-start(bf16[144,1024]{1,0:T(8,128)(2,1)S(1)} %collective-permute-done.3.refs_3_), channel_id=1, source_target_pairs={{0,2},{2,0},{1,3},{3,1},{4,6},{6,4},{5,7},{7,5},{8,10},{10,8},{9,1... | collective-permute-start | bytes 884744 | tf_op jit(solution)/shard_map/ppermute | solution.py:466
  34.7 14.7 %collective-permute-start.9 = (bf16[2,32,2176]{2,1,0:T(8,128)(2,1)S(1)}, bf16[2,32,2176]{2,1,0:T(8,128)(2,1)S(1)}, u32[]{:S(2)}, u32[]{:S(2)}) collective-permute-start(bf16[2,32,2176]{2,1,0:T(8,128)(2,1)S(1)} %attach_sources.1.mine_ref), channel_id=1, source_target_pairs={{0,1},{1,0},{2,3},{3,2},{4,5},{5,4},{6,7},{7,6},{8,9},{9,8},{10,11... | collective-permute-start | bytes 835592 | tf_op jit(solution)/shard_map/ppermute | solution.py:466
  36.4 1.0 copy-start.1
  44.8 6.8 %collective-permute-start.12 = (bf16[128,256]{1,0:T(8,128)(2,1)S(1)}, bf16[128,256]{1,0:T(8,128)(2,1)S(1)}, u32[]{:S(2)}, u32[]{:S(2)}) collective-permute-start(bf16[128,256]{1,0:T(8,128)(2,1)S(1)} %get-tuple-element.58), channel_id=1, source_target_pairs={{0,16},{16,0},{1,17},{17,1},{2,18},{18,2},{3,19},{19,3},{4,20},{20... | collective-permute-start | bytes 196616 | tf_op jit(solution)/shard_map/ppermute | solution.py:466
  49.5 14.8 %collective-permute-start.10 = (bf16[2,64,1152]{2,1,0:T(8,128)(2,1)S(1)}, bf16[2,64,1152]{2,1,0:T(8,128)(2,1)S(1)}, u32[]{:S(2)}, u32[]{:S(2)}) collective-permute-start(bf16[2,64,1152]{2,1,0:T(8,128)(2,1)S(1)} %bitcast.17), channel_id=1, source_target_pairs={{0,4},{4,0},{8,12},{12,8},{1,5},{5,1},{9,13},{13,9},{2,6},{6,2},{1... | collective-permute-start | bytes 884744 | tf_op jit(solution)/shard_map/ppermute | solution.py:466
  51.1 13.2 %collective-permute-start.11 = (bf16[2,64,1152]{2,1,0:T(8,128)(2,1)S(1)}, bf16[2,64,1152]{2,1,0:T(8,128)(2,1)S(1)}, u32[]{:S(2)}, u32[]{:S(2)}) collective-permute-start(bf16[2,64,1152]{2,1,0:T(8,128)(2,1)S(1)} %bitcast.18), channel_id=1, source_target_pairs={{0,8},{4,12},{8,0},{12,4},{1,9},{5,13},{9,1},{13,5},{2,10},{6,14},... | collective-permute-start | bytes 884744 | tf_op jit(solution)/shard_map/ppermute | solution.py:466
  51.6 13.4 %collective-permute-start.13 = (bf16[2,64,1152]{2,1,0:T(8,128)(2,1)S(1)}, bf16[2,64,1152]{2,1,0:T(8,128)(2,1)S(1)}, u32[]{:S(2)}, u32[]{:S(2)}) collective-permute-start(bf16[2,64,1152]{2,1,0:T(8,128)(2,1)S(1)} %bitcast.19), channel_id=1, source_target_pairs={{0,12},{4,8},{8,4},{12,0},{1,13},{5,9},{9,5},{13,1},{2,14},{6,10},... | collective-permute-start | bytes 884744 | tf_op jit(solution)/shard_map/ppermute | solution.py:466
  58.5 12.6 %all-to-all-start.1 = ((bf16[16,64,128]{2,1,0:T(8,128)(2,1)}), bf16[16,64,128]{2,1,0:T(8,128)(2,1)S(1)}, u32[]{:S(2)}, u32[]{:S(2)}) async-start(bf16[16,64,128]{2,1,0:T(8,128)(2,1)} %bitcast.5), calls=%async_computation.1 | async-start | bytes 524288 | tf_op jit(solution)/shard_map/all_to_all | solution.py:462
  64.2 6.9 %copy-start.2 = (bf16[1,64,1024]{2,1,0:T(8,128)(2,1)S(1)}, bf16[1,64,1024]{2,1,0:T(8,128)(2,1)}, u32[]{:S(2)}) copy-start(bf16[1,64,1024]{2,1,0:T(8,128)(2,1)} %get-tuple-element.63.refs_0_) | copy-start | bytes 393220
  64.3 6.9 %copy-start.3 = (f32[128]{0:T(128)S(1)}, f32[128]{0:T(128)}, u32[]{:S(2)}) copy-start(f32[128]{0:T(128)} %param.12) | copy-start | bytes 1540
  64.3 2.4 %collective-permute-start.14 = (bf16[2,64,1152]{2,1,0:T(8,128)(2,1)S(1)}, bf16[2,64,1152]{2,1,0:T(8,128)(2,1)S(1)}, u32[]{:S(2)}, u32[]{:S(2)}) collective-permute-start(bf16[2,64,1152]{2,1,0:T(8,128)(2,1)S(1)} %bitcast.20), channel_id=1, source_target_pairs={{0,2},{2,0},{1,3},{3,1},{4,6},{6,4},{5,7},{7,5},{8,10},{10,8},{9,1... | collective-permute-start | bytes 884744 | tf_op jit(solution)/shard_map/ppermute | solution.py:466
  64.5 2.2 %collective-permute-start.15 = (bf16[2,64,1152]{2,1,0:T(8,128)(2,1)S(1)}, bf16[2,64,1152]{2,1,0:T(8,128)(2,1)S(1)}, u32[]{:S(2)}, u32[]{:S(2)}) collective-permute-start(bf16[2,64,1152]{2,1,0:T(8,128)(2,1)S(1)} %collective-permute-done.10.refs_1_), channel_id=1, source_target_pairs={{0,2},{2,0},{1,3},{3,1},{4,6},{6,4},{5,7},{7,5},{8,10},{10,8},{9,1... | collective-permute-start | bytes 884744 | tf_op jit(solution)/shard_map/ppermute | solution.py:466
  64.9 1.9 %collective-permute-start.16 = (bf16[2,64,1152]{2,1,0:T(8,128)(2,1)S(1)}, bf16[2,64,1152]{2,1,0:T(8,128)(2,1)S(1)}, u32[]{:S(2)}, u32[]{:S(2)}) collective-permute-start(bf16[2,64,1152]{2,1,0:T(8,128)(2,1)S(1)} %collective-permute-done.11.refs_2_), channel_id=1, source_target_pairs={{0,2},{2,0},{1,3},{3,1},{4,6},{6,4},{5,7},{7,5},{8,10},{10,8},{9,1... | collective-permute-start | bytes 884744 | tf_op jit(solution)/shard_map/ppermute | solution.py:466
  65.0 2.9 %collective-permute-start.17 = (bf16[2,64,1152]{2,1,0:T(8,128)(2,1)S(1)}, bf16[2,64,1152]{2,1,0:T(8,128)(2,1)S(1)}, u32[]{:S(2)}, u32[]{:S(2)}) collective-permute-start(bf16[2,64,1152]{2,1,0:T(8,128)(2,1)S(1)} %collective-permute-done.13.refs_3_), channel_id=1, source_target_pairs={{0,2},{2,0},{1,3},{3,1},{4,6},{6,4},{5,7},{7,5},{8,10},{10,8},{9,1... | collective-permute-start | bytes 884744 | tf_op jit(solution)/shard_map/ppermute | solution.py:466
  74.8 17.3 %copy-start = (bf16[1024,1024]{1,0:T(8,128)(2,1)S(1)}, bf16[1024,1024]{1,0:T(8,128)(2,1)}, u32[]{:S(2)}) copy-start(bf16[1024,1024]{1,0:T(8,128)(2,1)} %get-tuple-element.48.normed_any.normed_ref) | copy-start | bytes 6291460
  86.1 7.3 %collective-permute-start.18 = (bf16[128,256]{1,0:T(8,128)(2,1)S(1)}, bf16[128,256]{1,0:T(8,128)(2,1)S(1)}, u32[]{:S(2)}, u32[]{:S(2)}) collective-permute-start(bf16[128,256]{1,0:T(8,128)(2,1)S(1)} %get-tuple-element.68), channel_id=1, source_target_pairs={{0,16},{16,0},{1,17},{17,1},{2,18},{18,2},{3,19},{19,3},{4,20},{20... | collective-permute-start | bytes 196616 | tf_op jit(solution)/shard_map/ppermute | solution.py:466
  94.6 18.9 %all-to-all-start.3 = ((bf16[32,32,256]{2,1,0:T(8,128)(2,1)}), bf16[32,32,256]{2,1,0:T(8,128)(2,1)S(1)}, u32[]{:S(2)}, u32[]{:S(2)}) async-start(bf16[32,32,256]{2,1,0:T(8,128)(2,1)} %bitcast.9), calls=%async_computation.3 | async-start | bytes 1048576 | tf_op jit(solution)/shard_map/all_to_all | solution.py:462
  97.5 6.0 %collective-permute-start.19 = (f32[100,128]{1,0:T(8,128)S(1)}, f32[100,128]{1,0:T(8,128)S(1)}, u32[]{:S(2)}, u32[]{:S(2)}) collective-permute-start(f32[100,128]{1,0:T(8,128)S(1)} %get-tuple-element.70), channel_id=1, source_target_pairs={{0,1},{1,0},{2,3},{3,2},{4,5},{5,4},{6,7},{7,6},{8,9},{9,8},{10,11... | collective-permute-start | bytes 153608 | tf_op jit(solution)/shard_map/ppermute | solution.py:466

commit v29 on v28

--- a/solution.py
+++ b/solution.py
@@ -570,7 +570,7 @@
     else:
         packed = in_order(packed, "ens", 1).reshape(halves, members_num * shard, width)
     packed, near[2] = lax.optimization_barrier((packed, near[2]))
-    pieces = [packed] + [swap(packed, "quad", step) for step in range(1, QUAD - 1)]
+    pieces = [packed] + [swap(packed, "quad", step) for step in range(1, QUAD)]
 
     rim = ((RIM, 2 * COLS), BF16)
     rims = [rim] if halves == 2 else [rim, rim]
@@ -624,8 +624,6 @@
         exps=rows * 128,
     )(steps, queries, own, low, high, outcome)
     *pieces, own = lax.optimization_barrier((*pieces, own))
-    packed, low = lax.optimization_barrier((packed, low))
-    pieces.append(swap(packed, "quad", QUAD - 1))
     pieces = pieces + [swap(piece, "core", 1) for piece in pieces]
     attended = exchange(outcome.reshape(GROUP * members_num, part, COLS), ("quad", "core", "ens"))
     block = (halves, QUAD, CORES, members_num * shard, width)

time: 115 us -> 109 us (0.948)
  waiting for transfers between devices: 38 us -> 33.3 us
  starting transfers between devices: 35.5 us -> 34.2 us
    ppermute x20, waiting for transfers between devices: 22 us -> 16.8 us  [swap(): lax.ppermute(value, axis, [(i, i ^ step) for i in range(lax.axis_size(axi...]
    ppermute x20, starting transfers between devices: 22.2 us -> 18.4 us  [swap(): lax.ppermute(value, axis, [(i, i ^ step) for i in range(lax.axis_size(axi...]
    all_to_all x3, starting transfers between devices: 13.4 us -> 15.9 us  [exchange(): return lax.all_to_all(chunks, axes, 0, 0)]
  transfers between devices with their start and end apart: 23 -> 23, of which waited for: 13 -> 14; matrix products, arithmetic and copies ran while one was open for 2% -> 2% of each run, Pallas kernels for 16% -> 17%
where the time goes in v29:
time: 109 us; the launch traced here: 108 us
  starting transfers between devices  34.2 us (31%)
  waiting for transfers between devices  33.3 us (31%)
  Pallas kernels  27.2 us (25%)
  blocking collectives  9.89 us (9%)
  local copies, waits for them, and re-layouts  1.73 us (2%)
    pallas_call x16, Pallas kernels, run(): made(*[pltpu.with_memory_space_constraint(arg, pltpu.HBM) if space == 'h'...  27.2 us
    ppermute x20, starting transfers between devices, swap(): lax.ppermute(value, axis, [(i, i ^ step) for i in range(lax.axis_size(axi...  18.4 us
    ppermute x20, waiting for transfers between devices, swap(): lax.ppermute(value, axis, [(i, i ^ step) for i in range(lax.axis_size(axi...  16.8 us
    all_to_all x3, waiting for transfers between devices, exchange(): return lax.all_to_all(chunks, axes, 0, 0)  16.4 us
    all_to_all x3, starting transfers between devices, exchange(): return lax.all_to_all(chunks, axes, 0, 0)  15.9 us
    all_to_all x1, blocking collectives, exchange(): return lax.all_to_all(chunks, axes, 0, 0)  9.89 us
  transfers between devices with their start and end apart: 23, of which 14 were waited for; matrix products, arithmetic and copies ran while one was open for 2% of the time, Pallas kernels for 17%

profile of v29, /device:TPU:1, one launch (start us, length us, event | category | flops | bytes accessed | tf_op | source)
XLA Modules:
  0.0 108.2 jit_solution(703214876262048359)
XLA Ops:
  0.6 1.8 %prepare_weights.1 = (bf16[2,8,1,32,384]{4,3,2,1,0:T(8,128)(2,1)}, bf16[32,1152]{1,0:T(8,128)(2,1)}) custom-call(bf16[32,3072]{1,0:T(8,128)(2,1)} %w_any.1, bf16[32,1024]{1,0:T(8,128)(2,1)} %mix_any.1, bf16[32,100]{1,0:T(8,128)(2,1)} %readout_any.1), custom_call_target="tpu_custom_call" | custom-call | bytes 1048576 | tf_op jit(solution)/shard_map/prepare_weights/pallas_call | solution.py:63
  2.5 3.2 %collective-permute-start = (bf16[32,1152]{1,0:T(8,128)(2,1)}, bf16[32,1152]{1,0:T(8,128)(2,1)S(1)}, u32[]{:S(2)}, u32[]{:S(2)}) collective-permute-start(bf16[32,1152]{1,0:T(8,128)(2,1)} %get-tuple-element.36), channel_id=1, source_target_pairs={{0,16},{16,0},{1,17},{17,1},{2,18},{18,2},{3,19},{19,3},{4,20},{20... | collective-permute-start | bytes 221192 | tf_op jit(solution)/shard_map/ppermute | solution.py:466
  5.7 4.8 %all-to-all-start = ((bf16[16,32,384]{2,1,0:T(8,128)(2,1)}), bf16[16,32,384]{2,1,0:T(8,128)(2,1)S(1)}, u32[]{:S(2)}, u32[]{:S(2)}) async-start(bf16[16,32,384]{2,1,0:T(8,128)(2,1)} %bitcast.23), calls=%async_computation | async-start | bytes 786432 | tf_op jit(solution)/shard_map/all_to_all | solution.py:462
  10.4 1.9 %norm.1 = (bf16[144,1024]{1,0:T(8,128)(2,1)}, bf16[1,64,1024]{2,1,0:T(8,128)(2,1)}, bf16[1,64,1024]{2,1,0:T(8,128)(2,1)}) custom-call(s32[2,4]{1,0:T(2,128)} %near_any.1, bf16[128,1024]{1,0:T(8,128)(2,1)} %bitcast.24), custom_call_target="tpu_custom_call" | custom-call | flops 1048576 | bytes 1048576 | tf_op jit(solution)/shard_map/norm/pallas_call | solution.py:63
  12.3 0.9 select_bitcast_fusion.1
  13.3 1.5 %collective-permute-start.1 = (bf16[144,1024]{1,0:T(8,128)(2,1)}, bf16[144,1024]{1,0:T(8,128)(2,1)S(1)}, u32[]{:S(2)}, u32[]{:S(2)}) collective-permute-start(bf16[144,1024]{1,0:T(8,128)(2,1)} %get-tuple-element.43.refs_0_), channel_id=1, source_target_pairs={{0,4},{4,0},{8,12},{12,8},{1,5},{5,1},{9,13},{13,9},{2,6},{6,2},{1... | collective-permute-start | bytes 884744 | tf_op jit(solution)/shard_map/ppermute | solution.py:466
  14.7 1.2 %collective-permute-start.3 = (bf16[144,1024]{1,0:T(8,128)(2,1)}, bf16[144,1024]{1,0:T(8,128)(2,1)S(1)}, u32[]{:S(2)}, u32[]{:S(2)}) collective-permute-start(bf16[144,1024]{1,0:T(8,128)(2,1)} %get-tuple-element.43.refs_0_), channel_id=1, source_target_pairs={{0,12},{4,8},{8,4},{12,0},{1,13},{5,9},{9,5},{13,1},{2,14},{6,10},... | collective-permute-start | bytes 884744 | tf_op jit(solution)/shard_map/ppermute | solution.py:466
  15.9 0.9 attach_sources.1.mine_ref
  16.8 5.1 %all-to-all-done.refs_0_ = bf16[16,32,384]{2,1,0:T(8,128)(2,1)S(1)} async-done(((bf16[16,32,384]{2,1,0:T(8,128)(2,1)}), bf16[16,32,384]{2,1,0:T(8,128)(2,1)S(1)}, u32[]{:S(2)}, u32[]{:S(2)}) %all-to-all-start) | async-done | bytes 393248 | tf_op jit(solution)/shard_map/all_to_all | solution.py:462
  21.9 1.7 %collective-permute-start.2 = (bf16[144,1024]{1,0:T(8,128)(2,1)}, bf16[144,1024]{1,0:T(8,128)(2,1)S(1)}, u32[]{:S(2)}, u32[]{:S(2)}) collective-permute-start(bf16[144,1024]{1,0:T(8,128)(2,1)} %get-tuple-element.43.refs_0_), channel_id=1, source_target_pairs={{0,8},{4,12},{8,0},{12,4},{1,9},{5,13},{9,1},{13,5},{2,10},{6,14},... | collective-permute-start | bytes 884744 | tf_op jit(solution)/shard_map/ppermute | solution.py:466
  23.6 1.2 %collective-permute-start.9 = (bf16[2,32,2176]{2,1,0:T(8,128)(2,1)S(1)}, bf16[2,32,2176]{2,1,0:T(8,128)(2,1)S(1)}, u32[]{:S(2)}, u32[]{:S(2)}) collective-permute-start(bf16[2,32,2176]{2,1,0:T(8,128)(2,1)S(1)} %attach_sources.1.mine_ref), channel_id=1, source_target_pairs={{0,1},{1,0},{2,3},{3,2},{4,5},{5,4},{6,7},{7,6},{8,9},{9,8},{10,11... | collective-permute-start | bytes 835592 | tf_op jit(solution)/shard_map/ppermute | solution.py:466
  25.1 5.2 %collective-permute-done.1.refs_1_ = bf16[144,1024]{1,0:T(8,128)(2,1)S(1)} collective-permute-done((bf16[144,1024]{1,0:T(8,128)(2,1)}, bf16[144,1024]{1,0:T(8,128)(2,1)S(1)}, u32[]{:S(2)}, u32[]{:S(2)}) %collective-permute-start.1) | collective-permute-done | bytes 294944 | tf_op jit(solution)/shard_map/ppermute | solution.py:466
  30.3 1.4 %collective-permute-done.2.refs_2_ = bf16[144,1024]{1,0:T(8,128)(2,1)S(1)} collective-permute-done((bf16[144,1024]{1,0:T(8,128)(2,1)}, bf16[144,1024]{1,0:T(8,128)(2,1)S(1)}, u32[]{:S(2)}, u32[]{:S(2)}) %collective-permute-start.2) | collective-permute-done | bytes 294944 | tf_op jit(solution)/shard_map/ppermute | solution.py:466
  31.7 1.0 collective-permute-start.6
  32.7 0.5 collective-permute-start.5
  33.3 1.0 collective-permute-done.6.refs_6_
  34.3 1.5 %collective-permute-start.10 = (bf16[2,64,1152]{2,1,0:T(8,128)(2,1)S(1)}, bf16[2,64,1152]{2,1,0:T(8,128)(2,1)S(1)}, u32[]{:S(2)}, u32[]{:S(2)}) collective-permute-start(bf16[2,64,1152]{2,1,0:T(8,128)(2,1)S(1)} %bitcast.17), channel_id=1, source_target_pairs={{0,4},{4,0},{8,12},{12,8},{1,5},{5,1},{9,13},{13,9},{2,6},{6,2},{1... | collective-permute-start | bytes 884744 | tf_op jit(solution)/shard_map/ppermute | solution.py:466
  35.9 0.5 collective-permute-start.11
  36.4 1.3 %collective-permute-start.12 = (bf16[2,64,1152]{2,1,0:T(8,128)(2,1)S(1)}, bf16[2,64,1152]{2,1,0:T(8,128)(2,1)S(1)}, u32[]{:S(2)}, u32[]{:S(2)}) collective-permute-start(bf16[2,64,1152]{2,1,0:T(8,128)(2,1)S(1)} %bitcast.19), channel_id=1, source_target_pairs={{0,12},{4,8},{8,4},{12,0},{1,13},{5,9},{9,5},{13,1},{2,14},{6,10},... | collective-permute-start | bytes 884744 | tf_op jit(solution)/shard_map/ppermute | solution.py:466
  37.6 1.0 copy-done.1
  38.6 1.5 %collect.1 = (bf16[1024,1024]{1,0:T(8,128)(2,1)}, f32[8,16,128]{2,1,0:T(8,128)S(1)}) custom-call(bf16[144,1024]{1,0:T(8,128)(2,1)S(1)} %copy-done.1, bf16[144,1024]{1,0:T(8,128)(2,1)S(1)} %collective-permute-done.1.refs_1_, bf16[144,1024]{1,0:T(8,128)(2,1)S(1)} %collective-permute-done.2.refs_2_, bf16[144,1024]{1,0:T(8,128)(2,1)S(1)} %collective-permute-done.3.refs_3_, ...), custom_call_target="tpu_custom_call" | custom-call | bytes 4194304 | tf_op jit(solution)/shard_map/collect/pallas_call | solution.py:63
  40.5 1.3 %project_rims.1 = (bf16[16,2,32,384]{3,2,1,0:T(8,128)(2,1)S(1)}, bf16[128,256]{1,0:T(8,128)(2,1)S(1)}) custom-call(bf16[1024,1024]{1,0:T(8,128)(2,1)} %get-tuple-element.47.normed_any.normed_ref, bf16[16,32,384]{2,1,0:T(8,128)(2,1)S(1)} %all-to-all-done.refs_0_, bf16[16,32,384]{2,1,0:T(8,128)(2,1)S(1)} %collective-permute-done.8.refs_1_), custom_call_target="tpu_custom_call" | custom-call | flops 67108864 | bytes 1048576 | tf_op jit(solution)/shard_map/project_rims/pallas_call | solution.py:63
  41.8 1.8 %collective-permute-start.13 = (bf16[128,256]{1,0:T(8,128)(2,1)S(1)}, bf16[128,256]{1,0:T(8,128)(2,1)S(1)}, u32[]{:S(2)}, u32[]{:S(2)}) collective-permute-start(bf16[128,256]{1,0:T(8,128)(2,1)S(1)} %get-tuple-element.57), channel_id=1, source_target_pairs={{0,16},{16,0},{1,17},{17,1},{2,18},{18,2},{3,19},{19,3},{4,20},{20... | collective-permute-start | bytes 196616 | tf_op jit(solution)/shard_map/ppermute | solution.py:466
  43.6 2.8 %project.1 = (bf16[1024,128]{1,0:T(8,128)(2,1)S(1)}, bf16[1024,256]{1,0:T(8,128)(2,1)S(1)}) custom-call(bf16[1024,1024]{1,0:T(8,128)(2,1)} %get-tuple-element.47.normed_any.normed_ref, bf16[16,2,32,384]{3,2,1,0:T(8,128)(2,1)S(1)} %get-tuple-element.50.w_ref), custom_call_target="tpu_custom_call" | custom-call | flops 805306368 | bytes 4194304 | tf_op jit(solution)/shard_map/project/pallas_call | solution.py:63
  46.5 1.9 %attention_interior.1.done_ref = bf16[1024,128]{1,0:T(8,128)(2,1)S(1)} custom-call(f32[8,16,128]{2,1,0:T(8,128)S(1)} %get-tuple-element.48.steps_ref, bf16[1024,128]{1,0:T(8,128)(2,1)S(1)} %get-tuple-element.51.q_ref, bf16[1024,256]{1,0:T(8,128)(2,1)S(1)} %get-tuple-element.56.kv_ref), custom_call_target="tpu_custom_call" | custom-call | flops 268435456 | bytes 2097152 | tf_op jit(solution)/shard_map/attention_interior/pallas_call | solution.py:63
  48.3 1.4 %collective-permute-done.13.low_ref.high_ref = bf16[128,256]{1,0:T(8,128)(2,1)S(1)} collective-permute-done((bf16[128,256]{1,0:T(8,128)(2,1)S(1)}, bf16[128,256]{1,0:T(8,128)(2,1)S(1)}, u32[]{:S(2)}, u32[]{:S(2)}) %collective-permute-start.13) | collective-permute-done | bytes 65568 | tf_op jit(solution)/shard_map/ppermute | solution.py:466
  49.8 1.4 %attention_edges.1 = bf16[1024,128]{1,0:T(8,128)(2,1)} custom-call(f32[8,16,128]{2,1,0:T(8,128)S(1)} %get-tuple-element.48.steps_ref, bf16[1024,128]{1,0:T(8,128)(2,1)S(1)} %get-tuple-element.51.q_ref, bf16[1024,256]{1,0:T(8,128)(2,1)S(1)} %get-tuple-element.56.kv_ref, bf16[128,256]{1,0:T(8,128)(2,1)S(1)} %collective-permute-done.13.low_ref.high_ref, ...), custom_call_target="tpu_custom_call" | custom-call | flops 67108864 | bytes 1048576 | tf_op jit(solution)/shard_map/attention_edges/pallas_call | solution.py:63
  51.2 8.1 %all-to-all-start.1 = ((bf16[16,64,128]{2,1,0:T(8,128)(2,1)}), bf16[16,64,128]{2,1,0:T(8,128)(2,1)S(1)}, u32[]{:S(2)}, u32[]{:S(2)}) async-start(bf16[16,64,128]{2,1,0:T(8,128)(2,1)} %bitcast.5), calls=%async_computation.1 | async-start | bytes 524288 | tf_op jit(solution)/shard_map/all_to_all | solution.py:462
  59.6 0.4 collective-permute-start.15
  60.5 0.6 collective-permute-done.14.refs_4_
  61.0 0.4 collective-permute-done.15.refs_5_
  61.5 0.4 collective-permute-done.16.refs_6_
  61.9 0.4 collective-permute-done.17.refs_7_
  62.3 1.5 %assemble.1.w_any = bf16[2,4,2,64,1152]{4,3,2,1,0:T(8,128)(2,1)} custom-call(bf16[2,64,1152]{2,1,0:T(8,128)(2,1)S(1)} %bitcast.21, bf16[2,64,1152]{2,1,0:T(8,128)(2,1)S(1)} %collective-permute-done.10.refs_1_, bf16[2,64,1152]{2,1,0:T(8,128)(2,1)S(1)} %collective-permute-done.11.refs_2_, bf16[2,64,1152]{2,1,0:T(8,128)(2,1)S(1)} %collective-permute-done.12.refs_3_, ...), custom_call_target="tpu_custom_call" | custom-call | bytes 4194304 | tf_op jit(solution)/shard_map/assemble/pallas_call | solution.py:63
  63.8 2.4 %all-to-all-done.1.att_ref = bf16[16,64,128]{2,1,0:T(8,128)(2,1)S(1)} async-done(((bf16[16,64,128]{2,1,0:T(8,128)(2,1)}), bf16[16,64,128]{2,1,0:T(8,128)(2,1)S(1)}, u32[]{:S(2)}, u32[]{:S(2)}) %all-to-all-start.1) | async-done | bytes 262176 | tf_op jit(solution)/shard_map/all_to_all | solution.py:462
  66.2 3.7 %mix_loss_backward.1 = (f32[100,128]{1,0:T(8,128)S(1)}, bf16[16,64,128]{2,1,0:T(8,128)(2,1)S(1)}) custom-call(bf16[16,64,128]{2,1,0:T(8,128)(2,1)S(1)} %all-to-all-done.1.att_ref, f32[1,128]{1,0:T(1,128)S(1)} %bitcast.22, f32[100,128]{1,0:T(8,128)} %truth_any.1, bf16[2,4,2,64,1152]{4,3,2,1,0:T(8,128)(2,1)} %assemble.1.w_any, ...), custom_call_target="tpu_custom_call" | custom-call | flops 603979776 | bytes 4194304 | tf_op jit(solution)/shard_map/mix_loss_backward/pallas_call | solution.py:63
  69.9 9.9 %all_to_all.20 = bf16[16,64,128]{2,1,0:T(8,128)(2,1)S(1)} all-to-all(bf16[16,64,128]{2,1,0:T(8,128)(2,1)S(1)} %get-tuple-element.64), channel_id=1, replica_groups=mesh['half'=2,'quad'=4,'core'=2,'ens'=2] {'quad','core','ens'}, dimensions={0} | all-to-all | bytes 524288 | tf_op jit(solution)/shard_map/all_to_all | solution.py:462
  79.8 1.4 %attention_edges_back.1 = (f32[2,256,256]{2,1,0:T(8,128)S(1)}, bf16[128,256]{1,0:T(8,128)(2,1)S(1)}) custom-call(f32[8,16,128]{2,1,0:T(8,128)S(1)} %get-tuple-element.48.steps_ref, bf16[1024,128]{1,0:T(8,128)(2,1)S(1)} %get-tuple-element.51.q_ref, bf16[1024,256]{1,0:T(8,128)(2,1)S(1)} %get-tuple-element.56.kv_ref, ...), custom_call_target="tpu_custom_call" | custom-call | flops 167772160 | bytes 1048576 | tf_op jit(solution)/shard_map/attention_edges_back/pallas_call | solution.py:63
  81.3 3.8 %attention_interior_back.1.grads_ref = f32[1024,256]{1,0:T(8,128)S(1)} custom-call(f32[8,16,128]{2,1,0:T(8,128)S(1)} %get-tuple-element.48.steps_ref, bf16[1024,128]{1,0:T(8,128)(2,1)S(1)} %get-tuple-element.51.q_ref, bf16[1024,256]{1,0:T(8,128)(2,1)S(1)} %get-tuple-element.56.kv_ref, bf16[1024,128]{1,0:T(8,128)(2,1)S(1)} %bitcast.15, ...), custom_call_target="tpu_custom_call" | custom-call | flops 536870912 | bytes 4194304 | tf_op jit(solution)/shard_map/attention_interior_back/pallas_call | solution.py:63
  85.2 1.3 %product.1.total_ref = f32[1024,256]{1,0:T(8,128)S(1)} custom-call(bf16[1024,1024]{1,0:T(8,128)(2,1)S(1)} %copy-done, f32[1024,256]{1,0:T(8,128)S(1)} %attention_interior_back.1.grads_ref), custom_call_target="tpu_custom_call" | custom-call | tf_op jit(solution)/shard_map/product/pallas_call | solution.py:63
  86.5 1.0 collective-permute-done.18.refs_0_
  87.5 1.1 %product_rims.1 = bf16[1024,256]{1,0:T(8,128)(2,1)} custom-call(bf16[1024,1024]{1,0:T(8,128)(2,1)S(1)} %copy-done, f32[1024,256]{1,0:T(8,128)S(1)} %product.1.total_ref, bf16[128,256]{1,0:T(8,128)(2,1)S(1)} %collective-permute-done.18.refs_0_), custom_call_target="tpu_custom_call" | custom-call | flops 67108864 | bytes 2097152 | tf_op jit(solution)/shard_map/product_rims/pallas_call | solution.py:63
  88.6 3.0 %all-to-all-start.3 = ((bf16[32,32,256]{2,1,0:T(8,128)(2,1)}), bf16[32,32,256]{2,1,0:T(8,128)(2,1)S(1)}, u32[]{:S(2)}, u32[]{:S(2)}) async-start(bf16[32,32,256]{2,1,0:T(8,128)(2,1)} %bitcast.9), calls=%async_computation.3 | async-start | bytes 1048576 | tf_op jit(solution)/shard_map/all_to_all | solution.py:462
  91.6 1.5 %collective-permute-start.19 = (f32[100,128]{1,0:T(8,128)S(1)}, f32[100,128]{1,0:T(8,128)S(1)}, u32[]{:S(2)}, u32[]{:S(2)}) collective-permute-start(f32[100,128]{1,0:T(8,128)S(1)} %get-tuple-element.68), channel_id=1, source_target_pairs={{0,1},{1,0},{2,3},{3,2},{4,5},{5,4},{6,7},{7,6},{8,9},{9,8},{10,11... | collective-permute-start | bytes 153608 | tf_op jit(solution)/shard_map/ppermute | solution.py:466
  93.1 4.5 %collective-permute-done.19 = f32[100,128]{1,0:T(8,128)S(1)} collective-permute-done((f32[100,128]{1,0:T(8,128)S(1)}, f32[100,128]{1,0:T(8,128)S(1)}, u32[]{:S(2)}, u32[]{:S(2)}) %collective-permute-start.19) | collective-permute-done | bytes 51232 | tf_op jit(solution)/shard_map/ppermute | solution.py:466
  97.8 0.7 copy.9
  98.5 9.0 %all-to-all-done.3 = bf16[32,32,256]{2,1,0:T(8,128)(2,1)S(1)} async-done(((bf16[32,32,256]{2,1,0:T(8,128)(2,1)}), bf16[32,32,256]{2,1,0:T(8,128)(2,1)S(1)}, u32[]{:S(2)}, u32[]{:S(2)}) %all-to-all-start.3) | async-done | bytes 524320 | tf_op jit(solution)/shard_map/all_to_all | solution.py:462
  107.4 0.8 gather_sums.1
  (30 shorter events, 1.6 us)
Async XLA Ops:
  2.5 9.9 %collective-permute-start = (bf16[32,1152]{1,0:T(8,128)(2,1)}, bf16[32,1152]{1,0:T(8,128)(2,1)S(1)}, u32[]{:S(2)}, u32[]{:S(2)}) collective-permute-start(bf16[32,1152]{1,0:T(8,128)(2,1)} %get-tuple-element.36), channel_id=1, source_target_pairs={{0,16},{16,0},{1,17},{17,1},{2,18},{18,2},{3,19},{19,3},{4,20},{20... | collective-permute-start | bytes 221192 | tf_op jit(solution)/shard_map/ppermute | solution.py:466
  5.7 16.2 %all-to-all-start = ((bf16[16,32,384]{2,1,0:T(8,128)(2,1)}), bf16[16,32,384]{2,1,0:T(8,128)(2,1)S(1)}, u32[]{:S(2)}, u32[]{:S(2)}) async-start(bf16[16,32,384]{2,1,0:T(8,128)(2,1)} %bitcast.23), calls=%async_computation | async-start | bytes 786432 | tf_op jit(solution)/shard_map/all_to_all | solution.py:462
  13.3 17.0 %collective-permute-start.1 = (bf16[144,1024]{1,0:T(8,128)(2,1)}, bf16[144,1024]{1,0:T(8,128)(2,1)S(1)}, u32[]{:S(2)}, u32[]{:S(2)}) collective-permute-start(bf16[144,1024]{1,0:T(8,128)(2,1)} %get-tuple-element.43.refs_0_), channel_id=1, source_target_pairs={{0,4},{4,0},{8,12},{12,8},{1,5},{5,1},{9,13},{13,9},{2,6},{6,2},{1... | collective-permute-start | bytes 884744 | tf_op jit(solution)/shard_map/ppermute | solution.py:466
  14.7 15.6 %collective-permute-start.3 = (bf16[144,1024]{1,0:T(8,128)(2,1)}, bf16[144,1024]{1,0:T(8,128)(2,1)S(1)}, u32[]{:S(2)}, u32[]{:S(2)}) collective-permute-start(bf16[144,1024]{1,0:T(8,128)(2,1)} %get-tuple-element.43.refs_0_), channel_id=1, source_target_pairs={{0,12},{4,8},{8,4},{12,0},{1,13},{5,9},{9,5},{13,1},{2,14},{6,10},... | collective-permute-start | bytes 884744 | tf_op jit(solution)/shard_map/ppermute | solution.py:466
  21.9 9.8 %collective-permute-start.2 = (bf16[144,1024]{1,0:T(8,128)(2,1)}, bf16[144,1024]{1,0:T(8,128)(2,1)S(1)}, u32[]{:S(2)}, u32[]{:S(2)}) collective-permute-start(bf16[144,1024]{1,0:T(8,128)(2,1)} %get-tuple-element.43.refs_0_), channel_id=1, source_target_pairs={{0,8},{4,12},{8,0},{12,4},{1,9},{5,13},{9,1},{13,5},{2,10},{6,14},... | collective-permute-start | bytes 884744 | tf_op jit(solution)/shard_map/ppermute | solution.py:466
  23.6 9.6 %collective-permute-start.9 = (bf16[2,32,2176]{2,1,0:T(8,128)(2,1)S(1)}, bf16[2,32,2176]{2,1,0:T(8,128)(2,1)S(1)}, u32[]{:S(2)}, u32[]{:S(2)}) collective-permute-start(bf16[2,32,2176]{2,1,0:T(8,128)(2,1)S(1)} %attach_sources.1.mine_ref), channel_id=1, source_target_pairs={{0,1},{1,0},{2,3},{3,2},{4,5},{5,4},{6,7},{7,6},{8,9},{9,8},{10,11... | collective-permute-start | bytes 835592 | tf_op jit(solution)/shard_map/ppermute | solution.py:466
  24.8 15.6 %collective-permute-start.8 = (bf16[16,32,384]{2,1,0:T(8,128)(2,1)S(1)}, bf16[16,32,384]{2,1,0:T(8,128)(2,1)S(1)}, u32[]{:S(2)}, u32[]{:S(2)}) collective-permute-start(bf16[16,32,384]{2,1,0:T(8,128)(2,1)S(1)} %all-to-all-done.refs_0_), channel_id=1, source_target_pairs={{0,1},{1,0},{2,3},{3,2},{4,5},{5,4},{6,7},{7,6},{8,9},{9,8},{10,11... | collective-permute-start | bytes 1179656 | tf_op jit(solution)/shard_map/ppermute | solution.py:466
  31.7 2.6 %collective-permute-start.6 = (bf16[144,1024]{1,0:T(8,128)(2,1)S(1)}, bf16[144,1024]{1,0:T(8,128)(2,1)S(1)}, u32[]{:S(2)}, u32[]{:S(2)}) collective-permute-start(bf16[144,1024]{1,0:T(8,128)(2,1)S(1)} %collective-permute-done.2.refs_2_), channel_id=1, source_target_pairs={{0,2},{2,0},{1,3},{3,1},{4,6},{6,4},{5,7},{7,5},{8,10},{10,8},{9,1... | collective-permute-start | bytes 884744 | tf_op jit(solution)/shard_map/ppermute | solution.py:466
  32.7 3.1 %collective-permute-start.4 = (bf16[144,1024]{1,0:T(8,128)(2,1)}, bf16[144,1024]{1,0:T(8,128)(2,1)S(1)}, u32[]{:S(2)}, u32[]{:S(2)}) collective-permute-start(bf16[144,1024]{1,0:T(8,128)(2,1)} %get-tuple-element.43.refs_0_), channel_id=1, source_target_pairs={{0,2},{2,0},{1,3},{3,1},{4,6},{6,4},{5,7},{7,5},{8,10},{10,8},{9,1... | collective-permute-start | bytes 884744 | tf_op jit(solution)/shard_map/ppermute | solution.py:466
  32.7 3.6 %collective-permute-start.5 = (bf16[144,1024]{1,0:T(8,128)(2,1)S(1)}, bf16[144,1024]{1,0:T(8,128)(2,1)S(1)}, u32[]{:S(2)}, u32[]{:S(2)}) collective-permute-start(bf16[144,1024]{1,0:T(8,128)(2,1)S(1)} %collective-permute-done.1.refs_1_), channel_id=1, source_target_pairs={{0,2},{2,0},{1,3},{3,1},{4,6},{6,4},{5,7},{7,5},{8,10},{10,8},{9,1... | collective-permute-start | bytes 884744 | tf_op jit(solution)/shard_map/ppermute | solution.py:466
  33.2 4.4 %collective-permute-start.7 = (bf16[144,1024]{1,0:T(8,128)(2,1)S(1)}, bf16[144,1024]{1,0:T(8,128)(2,1)S(1)}, u32[]{:S(2)}, u32[]{:S(2)}) collective-permute-start(bf16[144,1024]{1,0:T(8,128)(2,1)S(1)} %collective-permute-done.3.refs_3_), channel_id=1, source_target_pairs={{0,2},{2,0},{1,3},{3,1},{4,6},{6,4},{5,7},{7,5},{8,10},{10,8},{9,1... | collective-permute-start | bytes 884744 | tf_op jit(solution)/shard_map/ppermute | solution.py:466
  34.3 25.0 %collective-permute-start.10 = (bf16[2,64,1152]{2,1,0:T(8,128)(2,1)S(1)}, bf16[2,64,1152]{2,1,0:T(8,128)(2,1)S(1)}, u32[]{:S(2)}, u32[]{:S(2)}) collective-permute-start(bf16[2,64,1152]{2,1,0:T(8,128)(2,1)S(1)} %bitcast.17), channel_id=1, source_target_pairs={{0,4},{4,0},{8,12},{12,8},{1,5},{5,1},{9,13},{13,9},{2,6},{6,2},{1... | collective-permute-start | bytes 884744 | tf_op jit(solution)/shard_map/ppermute | solution.py:466
  35.9 23.5 %collective-permute-start.11 = (bf16[2,64,1152]{2,1,0:T(8,128)(2,1)S(1)}, bf16[2,64,1152]{2,1,0:T(8,128)(2,1)S(1)}, u32[]{:S(2)}, u32[]{:S(2)}) collective-permute-start(bf16[2,64,1152]{2,1,0:T(8,128)(2,1)S(1)} %bitcast.18), channel_id=1, source_target_pairs={{0,8},{4,12},{8,0},{12,4},{1,9},{5,13},{9,1},{13,5},{2,10},{6,14},... | collective-permute-start | bytes 884744 | tf_op jit(solution)/shard_map/ppermute | solution.py:466
  36.4 23.0 %collective-permute-start.12 = (bf16[2,64,1152]{2,1,0:T(8,128)(2,1)S(1)}, bf16[2,64,1152]{2,1,0:T(8,128)(2,1)S(1)}, u32[]{:S(2)}, u32[]{:S(2)}) collective-permute-start(bf16[2,64,1152]{2,1,0:T(8,128)(2,1)S(1)} %bitcast.19), channel_id=1, source_target_pairs={{0,12},{4,8},{8,4},{12,0},{1,13},{5,9},{9,5},{13,1},{2,14},{6,10},... | collective-permute-start | bytes 884744 | tf_op jit(solution)/shard_map/ppermute | solution.py:466
  37.6 1.0 copy-start.1
  41.8 8.0 %collective-permute-start.13 = (bf16[128,256]{1,0:T(8,128)(2,1)S(1)}, bf16[128,256]{1,0:T(8,128)(2,1)S(1)}, u32[]{:S(2)}, u32[]{:S(2)}) collective-permute-start(bf16[128,256]{1,0:T(8,128)(2,1)S(1)} %get-tuple-element.57), channel_id=1, source_target_pairs={{0,16},{16,0},{1,17},{17,1},{2,18},{18,2},{3,19},{19,3},{4,20},{20... | collective-permute-start | bytes 196616 | tf_op jit(solution)/shard_map/ppermute | solution.py:466
  51.2 15.0 %all-to-all-start.1 = ((bf16[16,64,128]{2,1,0:T(8,128)(2,1)}), bf16[16,64,128]{2,1,0:T(8,128)(2,1)S(1)}, u32[]{:S(2)}, u32[]{:S(2)}) async-start(bf16[16,64,128]{2,1,0:T(8,128)(2,1)} %bitcast.5), calls=%async_computation.1 | async-start | bytes 524288 | tf_op jit(solution)/shard_map/all_to_all | solution.py:462
  59.3 6.9 %copy-start.2 = (bf16[1,64,1024]{2,1,0:T(8,128)(2,1)S(1)}, bf16[1,64,1024]{2,1,0:T(8,128)(2,1)}, u32[]{:S(2)}) copy-start(bf16[1,64,1024]{2,1,0:T(8,128)(2,1)} %get-tuple-element.62.refs_0_) | copy-start | bytes 393220
  59.3 6.9 %copy-start.3 = (f32[128]{0:T(128)S(1)}, f32[128]{0:T(128)}, u32[]{:S(2)}) copy-start(f32[128]{0:T(128)} %param.12) | copy-start | bytes 1540
  59.4 1.6 %collective-permute-start.14 = (bf16[2,64,1152]{2,1,0:T(8,128)(2,1)S(1)}, bf16[2,64,1152]{2,1,0:T(8,128)(2,1)S(1)}, u32[]{:S(2)}, u32[]{:S(2)}) collective-permute-start(bf16[2,64,1152]{2,1,0:T(8,128)(2,1)S(1)} %bitcast.20), channel_id=1, source_target_pairs={{0,2},{2,0},{1,3},{3,1},{4,6},{6,4},{5,7},{7,5},{8,10},{10,8},{9,1... | collective-permute-start | bytes 884744 | tf_op jit(solution)/shard_map/ppermute | solution.py:466
  59.6 1.9 %collective-permute-start.15 = (bf16[2,64,1152]{2,1,0:T(8,128)(2,1)S(1)}, bf16[2,64,1152]{2,1,0:T(8,128)(2,1)S(1)}, u32[]{:S(2)}, u32[]{:S(2)}) collective-permute-start(bf16[2,64,1152]{2,1,0:T(8,128)(2,1)S(1)} %collective-permute-done.10.refs_1_), channel_id=1, source_target_pairs={{0,2},{2,0},{1,3},{3,1},{4,6},{6,4},{5,7},{7,5},{8,10},{10,8},{9,1... | collective-permute-start | bytes 884744 | tf_op jit(solution)/shard_map/ppermute | solution.py:466
  60.0 1.9 %collective-permute-start.16 = (bf16[2,64,1152]{2,1,0:T(8,128)(2,1)S(1)}, bf16[2,64,1152]{2,1,0:T(8,128)(2,1)S(1)}, u32[]{:S(2)}, u32[]{:S(2)}) collective-permute-start(bf16[2,64,1152]{2,1,0:T(8,128)(2,1)S(1)} %collective-permute-done.11.refs_2_), channel_id=1, source_target_pairs={{0,2},{2,0},{1,3},{3,1},{4,6},{6,4},{5,7},{7,5},{8,10},{10,8},{9,1... | collective-permute-start | bytes 884744 | tf_op jit(solution)/shard_map/ppermute | solution.py:466
  60.1 2.2 %collective-permute-start.17 = (bf16[2,64,1152]{2,1,0:T(8,128)(2,1)S(1)}, bf16[2,64,1152]{2,1,0:T(8,128)(2,1)S(1)}, u32[]{:S(2)}, u32[]{:S(2)}) collective-permute-start(bf16[2,64,1152]{2,1,0:T(8,128)(2,1)S(1)} %collective-permute-done.12.refs_3_), channel_id=1, source_target_pairs={{0,2},{2,0},{1,3},{3,1},{4,6},{6,4},{5,7},{7,5},{8,10},{10,8},{9,1... | collective-permute-start | bytes 884744 | tf_op jit(solution)/shard_map/ppermute | solution.py:466
  69.9 15.2 %copy-start = (bf16[1024,1024]{1,0:T(8,128)(2,1)S(1)}, bf16[1024,1024]{1,0:T(8,128)(2,1)}, u32[]{:S(2)}) copy-start(bf16[1024,1024]{1,0:T(8,128)(2,1)} %get-tuple-element.47.normed_any.normed_ref) | copy-start | bytes 6291460
  81.2 6.3 %collective-permute-start.18 = (bf16[128,256]{1,0:T(8,128)(2,1)S(1)}, bf16[128,256]{1,0:T(8,128)(2,1)S(1)}, u32[]{:S(2)}, u32[]{:S(2)}) collective-permute-start(bf16[128,256]{1,0:T(8,128)(2,1)S(1)} %get-tuple-element.66), channel_id=1, source_target_pairs={{0,16},{16,0},{1,17},{17,1},{2,18},{18,2},{3,19},{19,3},{4,20},{20... | collective-permute-start | bytes 196616 | tf_op jit(solution)/shard_map/ppermute | solution.py:466
  88.6 18.8 %all-to-all-start.3 = ((bf16[32,32,256]{2,1,0:T(8,128)(2,1)}), bf16[32,32,256]{2,1,0:T(8,128)(2,1)S(1)}, u32[]{:S(2)}, u32[]{:S(2)}) async-start(bf16[32,32,256]{2,1,0:T(8,128)(2,1)} %bitcast.9), calls=%async_computation.3 | async-start | bytes 1048576 | tf_op jit(solution)/shard_map/all_to_all | solution.py:462
  91.6 6.0 %collective-permute-start.19 = (f32[100,128]{1,0:T(8,128)S(1)}, f32[100,128]{1,0:T(8,128)S(1)}, u32[]{:S(2)}, u32[]{:S(2)}) collective-permute-start(f32[100,128]{1,0:T(8,128)S(1)} %get-tuple-element.68), channel_id=1, source_target_pairs={{0,1},{1,0},{2,3},{3,2},{4,5},{5,4},{6,7},{7,6},{8,9},{9,8},{10,11... | collective-permute-start | bytes 153608 | tf_op jit(solution)/shard_map/ppermute | solution.py:466

commit v30 on v29

--- a/solution.py
+++ b/solution.py
@@ -570,7 +570,8 @@
     else:
         packed = in_order(packed, "ens", 1).reshape(halves, members_num * shard, width)
     packed, near[2] = lax.optimization_barrier((packed, near[2]))
-    pieces = [packed] + [swap(packed, "quad", step) for step in range(1, QUAD)]
+    pieces = {step: swap(packed, "quad", step) for step in (2, 3, 1)}
+    pieces = [packed] + [pieces[step] for step in range(1, QUAD)]
 
     rim = ((RIM, 2 * COLS), BF16)
     rims = [rim] if halves == 2 else [rim, rim]

time: 109 us -> 109 us (level)
  no operation moved by 1% of the time
where the time goes in v30:
time: 109 us; the launch traced here: 108 us
  starting transfers between devices  34.2 us (31%)
  waiting for transfers between devices  33.3 us (31%)
  Pallas kernels  27.2 us (25%)
  blocking collectives  9.89 us (9%)
  local copies, waits for them, and re-layouts  1.73 us (2%)
    pallas_call x16, Pallas kernels, run(): made(*[pltpu.with_memory_space_constraint(arg, pltpu.HBM) if space == 'h'...  27.2 us
    ppermute x20, starting transfers between devices, swap(): lax.ppermute(value, axis, [(i, i ^ step) for i in range(lax.axis_size(axi...  18.4 us
    ppermute x20, waiting for transfers between devices, swap(): lax.ppermute(value, axis, [(i, i ^ step) for i in range(lax.axis_size(axi...  16.8 us
    all_to_all x3, waiting for transfers between devices, exchange(): return lax.all_to_all(chunks, axes, 0, 0)  16.4 us
    all_to_all x3, starting transfers between devices, exchange(): return lax.all_to_all(chunks, axes, 0, 0)  15.9 us
    all_to_all x1, blocking collectives, exchange(): return lax.all_to_all(chunks, axes, 0, 0)  9.89 us
  transfers between devices with their start and end apart: 23, of which 14 were waited for; matrix products, arithmetic and copies ran while one was open for 2% of the time, Pallas kernels for 17%

profile of v30, /device:TPU:1, one launch (start us, length us, event | category | flops | bytes accessed | tf_op | source)
XLA Modules:
  0.0 108.2 jit_solution(703214876262048359)
XLA Ops:
  0.6 1.8 %prepare_weights.1 = (bf16[2,8,1,32,384]{4,3,2,1,0:T(8,128)(2,1)}, bf16[32,1152]{1,0:T(8,128)(2,1)}) custom-call(bf16[32,3072]{1,0:T(8,128)(2,1)} %w_any.1, bf16[32,1024]{1,0:T(8,128)(2,1)} %mix_any.1, bf16[32,100]{1,0:T(8,128)(2,1)} %readout_any.1), custom_call_target="tpu_custom_call" | custom-call | bytes 1048576 | tf_op jit(solution)/shard_map/prepare_weights/pallas_call | solution.py:63
  2.5 3.2 %collective-permute-start = (bf16[32,1152]{1,0:T(8,128)(2,1)}, bf16[32,1152]{1,0:T(8,128)(2,1)S(1)}, u32[]{:S(2)}, u32[]{:S(2)}) collective-permute-start(bf16[32,1152]{1,0:T(8,128)(2,1)} %get-tuple-element.36), channel_id=1, source_target_pairs={{0,16},{16,0},{1,17},{17,1},{2,18},{18,2},{3,19},{19,3},{4,20},{20... | collective-permute-start | bytes 221192 | tf_op jit(solution)/shard_map/ppermute | solution.py:466
  5.7 4.8 %all-to-all-start = ((bf16[16,32,384]{2,1,0:T(8,128)(2,1)}), bf16[16,32,384]{2,1,0:T(8,128)(2,1)S(1)}, u32[]{:S(2)}, u32[]{:S(2)}) async-start(bf16[16,32,384]{2,1,0:T(8,128)(2,1)} %bitcast.23), calls=%async_computation | async-start | bytes 786432 | tf_op jit(solution)/shard_map/all_to_all | solution.py:462
  10.4 1.9 %norm.1 = (bf16[144,1024]{1,0:T(8,128)(2,1)}, bf16[1,64,1024]{2,1,0:T(8,128)(2,1)}, bf16[1,64,1024]{2,1,0:T(8,128)(2,1)}) custom-call(s32[2,4]{1,0:T(2,128)} %near_any.1, bf16[128,1024]{1,0:T(8,128)(2,1)} %bitcast.24), custom_call_target="tpu_custom_call" | custom-call | flops 1048576 | bytes 1048576 | tf_op jit(solution)/shard_map/norm/pallas_call | solution.py:63
  12.3 0.9 select_bitcast_fusion.1
  13.3 1.5 %collective-permute-start.1 = (bf16[144,1024]{1,0:T(8,128)(2,1)}, bf16[144,1024]{1,0:T(8,128)(2,1)S(1)}, u32[]{:S(2)}, u32[]{:S(2)}) collective-permute-start(bf16[144,1024]{1,0:T(8,128)(2,1)} %get-tuple-element.43.refs_0_), channel_id=1, source_target_pairs={{0,4},{4,0},{8,12},{12,8},{1,5},{5,1},{9,13},{13,9},{2,6},{6,2},{1... | collective-permute-start | bytes 884744 | tf_op jit(solution)/shard_map/ppermute | solution.py:466
  14.7 1.2 %collective-permute-start.3 = (bf16[144,1024]{1,0:T(8,128)(2,1)}, bf16[144,1024]{1,0:T(8,128)(2,1)S(1)}, u32[]{:S(2)}, u32[]{:S(2)}) collective-permute-start(bf16[144,1024]{1,0:T(8,128)(2,1)} %get-tuple-element.43.refs_0_), channel_id=1, source_target_pairs={{0,12},{4,8},{8,4},{12,0},{1,13},{5,9},{9,5},{13,1},{2,14},{6,10},... | collective-permute-start | bytes 884744 | tf_op jit(solution)/shard_map/ppermute | solution.py:466
  15.9 0.9 attach_sources.1.mine_ref
  16.8 5.1 %all-to-all-done.refs_0_ = bf16[16,32,384]{2,1,0:T(8,128)(2,1)S(1)} async-done(((bf16[16,32,384]{2,1,0:T(8,128)(2,1)}), bf16[16,32,384]{2,1,0:T(8,128)(2,1)S(1)}, u32[]{:S(2)}, u32[]{:S(2)}) %all-to-all-start) | async-done | bytes 393248 | tf_op jit(solution)/shard_map/all_to_all | solution.py:462
  21.9 1.7 %collective-permute-start.2 = (bf16[144,1024]{1,0:T(8,128)(2,1)}, bf16[144,1024]{1,0:T(8,128)(2,1)S(1)}, u32[]{:S(2)}, u32[]{:S(2)}) collective-permute-start(bf16[144,1024]{1,0:T(8,128)(2,1)} %get-tuple-element.43.refs_0_), channel_id=1, source_target_pairs={{0,8},{4,12},{8,0},{12,4},{1,9},{5,13},{9,1},{13,5},{2,10},{6,14},... | collective-permute-start | bytes 884744 | tf_op jit(solution)/shard_map/ppermute | solution.py:466
  23.6 1.2 %collective-permute-start.9 = (bf16[2,32,2176]{2,1,0:T(8,128)(2,1)S(1)}, bf16[2,32,2176]{2,1,0:T(8,128)(2,1)S(1)}, u32[]{:S(2)}, u32[]{:S(2)}) collective-permute-start(bf16[2,32,2176]{2,1,0:T(8,128)(2,1)S(1)} %attach_sources.1.mine_ref), channel_id=1, source_target_pairs={{0,1},{1,0},{2,3},{3,2},{4,5},{5,4},{6,7},{7,6},{8,9},{9,8},{10,11... | collective-permute-start | bytes 835592 | tf_op jit(solution)/shard_map/ppermute | solution.py:466
  25.1 5.2 %collective-permute-done.1.refs_1_ = bf16[144,1024]{1,0:T(8,128)(2,1)S(1)} collective-permute-done((bf16[144,1024]{1,0:T(8,128)(2,1)}, bf16[144,1024]{1,0:T(8,128)(2,1)S(1)}, u32[]{:S(2)}, u32[]{:S(2)}) %collective-permute-start.1) | collective-permute-done | bytes 294944 | tf_op jit(solution)/shard_map/ppermute | solution.py:466
  30.3 1.4 %collective-permute-done.2.refs_2_ = bf16[144,1024]{1,0:T(8,128)(2,1)S(1)} collective-permute-done((bf16[144,1024]{1,0:T(8,128)(2,1)}, bf16[144,1024]{1,0:T(8,128)(2,1)S(1)}, u32[]{:S(2)}, u32[]{:S(2)}) %collective-permute-start.2) | collective-permute-done | bytes 294944 | tf_op jit(solution)/shard_map/ppermute | solution.py:466
  31.7 1.0 collective-permute-start.6
  32.7 0.5 collective-permute-start.5
  33.3 1.0 collective-permute-done.6.refs_6_
  34.3 1.5 %collective-permute-start.10 = (bf16[2,64,1152]{2,1,0:T(8,128)(2,1)S(1)}, bf16[2,64,1152]{2,1,0:T(8,128)(2,1)S(1)}, u32[]{:S(2)}, u32[]{:S(2)}) collective-permute-start(bf16[2,64,1152]{2,1,0:T(8,128)(2,1)S(1)} %bitcast.17), channel_id=1, source_target_pairs={{0,4},{4,0},{8,12},{12,8},{1,5},{5,1},{9,13},{13,9},{2,6},{6,2},{1... | collective-permute-start | bytes 884744 | tf_op jit(solution)/shard_map/ppermute | solution.py:466
  35.9 0.5 collective-permute-start.11
  36.4 1.3 %collective-permute-start.12 = (bf16[2,64,1152]{2,1,0:T(8,128)(2,1)S(1)}, bf16[2,64,1152]{2,1,0:T(8,128)(2,1)S(1)}, u32[]{:S(2)}, u32[]{:S(2)}) collective-permute-start(bf16[2,64,1152]{2,1,0:T(8,128)(2,1)S(1)} %bitcast.19), channel_id=1, source_target_pairs={{0,12},{4,8},{8,4},{12,0},{1,13},{5,9},{9,5},{13,1},{2,14},{6,10},... | collective-permute-start | bytes 884744 | tf_op jit(solution)/shard_map/ppermute | solution.py:466
  37.6 1.0 copy-done.1
  38.6 1.5 %collect.1 = (bf16[1024,1024]{1,0:T(8,128)(2,1)}, f32[8,16,128]{2,1,0:T(8,128)S(1)}) custom-call(bf16[144,1024]{1,0:T(8,128)(2,1)S(1)} %copy-done.1, bf16[144,1024]{1,0:T(8,128)(2,1)S(1)} %collective-permute-done.1.refs_1_, bf16[144,1024]{1,0:T(8,128)(2,1)S(1)} %collective-permute-done.2.refs_2_, bf16[144,1024]{1,0:T(8,128)(2,1)S(1)} %collective-permute-done.3.refs_3_, ...), custom_call_target="tpu_custom_call" | custom-call | bytes 4194304 | tf_op jit(solution)/shard_map/collect/pallas_call | solution.py:63
  40.5 1.3 %project_rims.1 = (bf16[16,2,32,384]{3,2,1,0:T(8,128)(2,1)S(1)}, bf16[128,256]{1,0:T(8,128)(2,1)S(1)}) custom-call(bf16[1024,1024]{1,0:T(8,128)(2,1)} %get-tuple-element.47.normed_any.normed_ref, bf16[16,32,384]{2,1,0:T(8,128)(2,1)S(1)} %all-to-all-done.refs_0_, bf16[16,32,384]{2,1,0:T(8,128)(2,1)S(1)} %collective-permute-done.8.refs_1_), custom_call_target="tpu_custom_call" | custom-call | flops 67108864 | bytes 1048576 | tf_op jit(solution)/shard_map/project_rims/pallas_call | solution.py:63
  41.8 1.8 %collective-permute-start.13 = (bf16[128,256]{1,0:T(8,128)(2,1)S(1)}, bf16[128,256]{1,0:T(8,128)(2,1)S(1)}, u32[]{:S(2)}, u32[]{:S(2)}) collective-permute-start(bf16[128,256]{1,0:T(8,128)(2,1)S(1)} %get-tuple-element.57), channel_id=1, source_target_pairs={{0,16},{16,0},{1,17},{17,1},{2,18},{18,2},{3,19},{19,3},{4,20},{20... | collective-permute-start | bytes 196616 | tf_op jit(solution)/shard_map/ppermute | solution.py:466
  43.6 2.8 %project.1 = (bf16[1024,128]{1,0:T(8,128)(2,1)S(1)}, bf16[1024,256]{1,0:T(8,128)(2,1)S(1)}) custom-call(bf16[1024,1024]{1,0:T(8,128)(2,1)} %get-tuple-element.47.normed_any.normed_ref, bf16[16,2,32,384]{3,2,1,0:T(8,128)(2,1)S(1)} %get-tuple-element.50.w_ref), custom_call_target="tpu_custom_call" | custom-call | flops 805306368 | bytes 4194304 | tf_op jit(solution)/shard_map/project/pallas_call | solution.py:63
  46.5 1.9 %attention_interior.1.done_ref = bf16[1024,128]{1,0:T(8,128)(2,1)S(1)} custom-call(f32[8,16,128]{2,1,0:T(8,128)S(1)} %get-tuple-element.48.steps_ref, bf16[1024,128]{1,0:T(8,128)(2,1)S(1)} %get-tuple-element.51.q_ref, bf16[1024,256]{1,0:T(8,128)(2,1)S(1)} %get-tuple-element.56.kv_ref), custom_call_target="tpu_custom_call" | custom-call | flops 268435456 | bytes 2097152 | tf_op jit(solution)/shard_map/attention_interior/pallas_call | solution.py:63
  48.3 1.4 %collective-permute-done.13.low_ref.high_ref = bf16[128,256]{1,0:T(8,128)(2,1)S(1)} collective-permute-done((bf16[128,256]{1,0:T(8,128)(2,1)S(1)}, bf16[128,256]{1,0:T(8,128)(2,1)S(1)}, u32[]{:S(2)}, u32[]{:S(2)}) %collective-permute-start.13) | collective-permute-done | bytes 65568 | tf_op jit(solution)/shard_map/ppermute | solution.py:466
  49.8 1.4 %attention_edges.1 = bf16[1024,128]{1,0:T(8,128)(2,1)} custom-call(f32[8,16,128]{2,1,0:T(8,128)S(1)} %get-tuple-element.48.steps_ref, bf16[1024,128]{1,0:T(8,128)(2,1)S(1)} %get-tuple-element.51.q_ref, bf16[1024,256]{1,0:T(8,128)(2,1)S(1)} %get-tuple-element.56.kv_ref, bf16[128,256]{1,0:T(8,128)(2,1)S(1)} %collective-permute-done.13.low_ref.high_ref, ...), custom_call_target="tpu_custom_call" | custom-call | flops 67108864 | bytes 1048576 | tf_op jit(solution)/shard_map/attention_edges/pallas_call | solution.py:63
  51.2 8.1 %all-to-all-start.1 = ((bf16[16,64,128]{2,1,0:T(8,128)(2,1)}), bf16[16,64,128]{2,1,0:T(8,128)(2,1)S(1)}, u32[]{:S(2)}, u32[]{:S(2)}) async-start(bf16[16,64,128]{2,1,0:T(8,128)(2,1)} %bitcast.5), calls=%async_computation.1 | async-start | bytes 524288 | tf_op jit(solution)/shard_map/all_to_all | solution.py:462
  59.6 0.4 collective-permute-start.15
  60.5 0.6 collective-permute-done.14.refs_4_
  61.0 0.4 collective-permute-done.15.refs_5_
  61.5 0.4 collective-permute-done.16.refs_6_
  61.9 0.4 collective-permute-done.17.refs_7_
  62.3 1.5 %assemble.1.w_any = bf16[2,4,2,64,1152]{4,3,2,1,0:T(8,128)(2,1)} custom-call(bf16[2,64,1152]{2,1,0:T(8,128)(2,1)S(1)} %bitcast.21, bf16[2,64,1152]{2,1,0:T(8,128)(2,1)S(1)} %collective-permute-done.10.refs_1_, bf16[2,64,1152]{2,1,0:T(8,128)(2,1)S(1)} %collective-permute-done.11.refs_2_, bf16[2,64,1152]{2,1,0:T(8,128)(2,1)S(1)} %collective-permute-done.12.refs_3_, ...), custom_call_target="tpu_custom_call" | custom-call | bytes 4194304 | tf_op jit(solution)/shard_map/assemble/pallas_call | solution.py:63
  63.8 2.4 %all-to-all-done.1.att_ref = bf16[16,64,128]{2,1,0:T(8,128)(2,1)S(1)} async-done(((bf16[16,64,128]{2,1,0:T(8,128)(2,1)}), bf16[16,64,128]{2,1,0:T(8,128)(2,1)S(1)}, u32[]{:S(2)}, u32[]{:S(2)}) %all-to-all-start.1) | async-done | bytes 262176 | tf_op jit(solution)/shard_map/all_to_all | solution.py:462
  66.2 3.7 %mix_loss_backward.1 = (f32[100,128]{1,0:T(8,128)S(1)}, bf16[16,64,128]{2,1,0:T(8,128)(2,1)S(1)}) custom-call(bf16[16,64,128]{2,1,0:T(8,128)(2,1)S(1)} %all-to-all-done.1.att_ref, f32[1,128]{1,0:T(1,128)S(1)} %bitcast.22, f32[100,128]{1,0:T(8,128)} %truth_any.1, bf16[2,4,2,64,1152]{4,3,2,1,0:T(8,128)(2,1)} %assemble.1.w_any, ...), custom_call_target="tpu_custom_call" | custom-call | flops 603979776 | bytes 4194304 | tf_op jit(solution)/shard_map/mix_loss_backward/pallas_call | solution.py:63
  69.9 9.9 %all_to_all.20 = bf16[16,64,128]{2,1,0:T(8,128)(2,1)S(1)} all-to-all(bf16[16,64,128]{2,1,0:T(8,128)(2,1)S(1)} %get-tuple-element.64), channel_id=1, replica_groups=mesh['half'=2,'quad'=4,'core'=2,'ens'=2] {'quad','core','ens'}, dimensions={0} | all-to-all | bytes 524288 | tf_op jit(solution)/shard_map/all_to_all | solution.py:462
  79.8 1.4 %attention_edges_back.1 = (f32[2,256,256]{2,1,0:T(8,128)S(1)}, bf16[128,256]{1,0:T(8,128)(2,1)S(1)}) custom-call(f32[8,16,128]{2,1,0:T(8,128)S(1)} %get-tuple-element.48.steps_ref, bf16[1024,128]{1,0:T(8,128)(2,1)S(1)} %get-tuple-element.51.q_ref, bf16[1024,256]{1,0:T(8,128)(2,1)S(1)} %get-tuple-element.56.kv_ref, ...), custom_call_target="tpu_custom_call" | custom-call | flops 167772160 | bytes 1048576 | tf_op jit(solution)/shard_map/attention_edges_back/pallas_call | solution.py:63
  81.3 3.8 %attention_interior_back.1.grads_ref = f32[1024,256]{1,0:T(8,128)S(1)} custom-call(f32[8,16,128]{2,1,0:T(8,128)S(1)} %get-tuple-element.48.steps_ref, bf16[1024,128]{1,0:T(8,128)(2,1)S(1)} %get-tuple-element.51.q_ref, bf16[1024,256]{1,0:T(8,128)(2,1)S(1)} %get-tuple-element.56.kv_ref, bf16[1024,128]{1,0:T(8,128)(2,1)S(1)} %bitcast.15, ...), custom_call_target="tpu_custom_call" | custom-call | flops 536870912 | bytes 4194304 | tf_op jit(solution)/shard_map/attention_interior_back/pallas_call | solution.py:63
  85.2 1.3 %product.1.total_ref = f32[1024,256]{1,0:T(8,128)S(1)} custom-call(bf16[1024,1024]{1,0:T(8,128)(2,1)S(1)} %copy-done, f32[1024,256]{1,0:T(8,128)S(1)} %attention_interior_back.1.grads_ref), custom_call_target="tpu_custom_call" | custom-call | tf_op jit(solution)/shard_map/product/pallas_call | solution.py:63
  86.5 1.0 collective-permute-done.18.refs_0_
  87.5 1.1 %product_rims.1 = bf16[1024,256]{1,0:T(8,128)(2,1)} custom-call(bf16[1024,1024]{1,0:T(8,128)(2,1)S(1)} %copy-done, f32[1024,256]{1,0:T(8,128)S(1)} %product.1.total_ref, bf16[128,256]{1,0:T(8,128)(2,1)S(1)} %collective-permute-done.18.refs_0_), custom_call_target="tpu_custom_call" | custom-call | flops 67108864 | bytes 2097152 | tf_op jit(solution)/shard_map/product_rims/pallas_call | solution.py:63
  88.6 3.0 %all-to-all-start.3 = ((bf16[32,32,256]{2,1,0:T(8,128)(2,1)}), bf16[32,32,256]{2,1,0:T(8,128)(2,1)S(1)}, u32[]{:S(2)}, u32[]{:S(2)}) async-start(bf16[32,32,256]{2,1,0:T(8,128)(2,1)} %bitcast.9), calls=%async_computation.3 | async-start | bytes 1048576 | tf_op jit(solution)/shard_map/all_to_all | solution.py:462
  91.6 1.5 %collective-permute-start.19 = (f32[100,128]{1,0:T(8,128)S(1)}, f32[100,128]{1,0:T(8,128)S(1)}, u32[]{:S(2)}, u32[]{:S(2)}) collective-permute-start(f32[100,128]{1,0:T(8,128)S(1)} %get-tuple-element.68), channel_id=1, source_target_pairs={{0,1},{1,0},{2,3},{3,2},{4,5},{5,4},{6,7},{7,6},{8,9},{9,8},{10,11... | collective-permute-start | bytes 153608 | tf_op jit(solution)/shard_map/ppermute | solution.py:466
  93.1 4.5 %collective-permute-done.19 = f32[100,128]{1,0:T(8,128)S(1)} collective-permute-done((f32[100,128]{1,0:T(8,128)S(1)}, f32[100,128]{1,0:T(8,128)S(1)}, u32[]{:S(2)}, u32[]{:S(2)}) %collective-permute-start.19) | collective-permute-done | bytes 51232 | tf_op jit(solution)/shard_map/ppermute | solution.py:466
  97.8 0.7 copy.9
  98.5 9.0 %all-to-all-done.3 = bf16[32,32,256]{2,1,0:T(8,128)(2,1)S(1)} async-done(((bf16[32,32,256]{2,1,0:T(8,128)(2,1)}), bf16[32,32,256]{2,1,0:T(8,128)(2,1)S(1)}, u32[]{:S(2)}, u32[]{:S(2)}) %all-to-all-start.3) | async-done | bytes 524320 | tf_op jit(solution)/shard_map/all_to_all | solution.py:462
  107.4 0.8 gather_sums.1
  (30 shorter events, 1.6 us)
Async XLA Ops:
  2.5 9.9 %collective-permute-start = (bf16[32,1152]{1,0:T(8,128)(2,1)}, bf16[32,1152]{1,0:T(8,128)(2,1)S(1)}, u32[]{:S(2)}, u32[]{:S(2)}) collective-permute-start(bf16[32,1152]{1,0:T(8,128)(2,1)} %get-tuple-element.36), channel_id=1, source_target_pairs={{0,16},{16,0},{1,17},{17,1},{2,18},{18,2},{3,19},{19,3},{4,20},{20... | collective-permute-start | bytes 221192 | tf_op jit(solution)/shard_map/ppermute | solution.py:466
  5.7 16.2 %all-to-all-start = ((bf16[16,32,384]{2,1,0:T(8,128)(2,1)}), bf16[16,32,384]{2,1,0:T(8,128)(2,1)S(1)}, u32[]{:S(2)}, u32[]{:S(2)}) async-start(bf16[16,32,384]{2,1,0:T(8,128)(2,1)} %bitcast.23), calls=%async_computation | async-start | bytes 786432 | tf_op jit(solution)/shard_map/all_to_all | solution.py:462
  13.3 17.0 %collective-permute-start.1 = (bf16[144,1024]{1,0:T(8,128)(2,1)}, bf16[144,1024]{1,0:T(8,128)(2,1)S(1)}, u32[]{:S(2)}, u32[]{:S(2)}) collective-permute-start(bf16[144,1024]{1,0:T(8,128)(2,1)} %get-tuple-element.43.refs_0_), channel_id=1, source_target_pairs={{0,4},{4,0},{8,12},{12,8},{1,5},{5,1},{9,13},{13,9},{2,6},{6,2},{1... | collective-permute-start | bytes 884744 | tf_op jit(solution)/shard_map/ppermute | solution.py:466
  14.7 15.6 %collective-permute-start.3 = (bf16[144,1024]{1,0:T(8,128)(2,1)}, bf16[144,1024]{1,0:T(8,128)(2,1)S(1)}, u32[]{:S(2)}, u32[]{:S(2)}) collective-permute-start(bf16[144,1024]{1,0:T(8,128)(2,1)} %get-tuple-element.43.refs_0_), channel_id=1, source_target_pairs={{0,12},{4,8},{8,4},{12,0},{1,13},{5,9},{9,5},{13,1},{2,14},{6,10},... | collective-permute-start | bytes 884744 | tf_op jit(solution)/shard_map/ppermute | solution.py:466
  21.9 9.8 %collective-permute-start.2 = (bf16[144,1024]{1,0:T(8,128)(2,1)}, bf16[144,1024]{1,0:T(8,128)(2,1)S(1)}, u32[]{:S(2)}, u32[]{:S(2)}) collective-permute-start(bf16[144,1024]{1,0:T(8,128)(2,1)} %get-tuple-element.43.refs_0_), channel_id=1, source_target_pairs={{0,8},{4,12},{8,0},{12,4},{1,9},{5,13},{9,1},{13,5},{2,10},{6,14},... | collective-permute-start | bytes 884744 | tf_op jit(solution)/shard_map/ppermute | solution.py:466
  23.6 9.6 %collective-permute-start.9 = (bf16[2,32,2176]{2,1,0:T(8,128)(2,1)S(1)}, bf16[2,32,2176]{2,1,0:T(8,128)(2,1)S(1)}, u32[]{:S(2)}, u32[]{:S(2)}) collective-permute-start(bf16[2,32,2176]{2,1,0:T(8,128)(2,1)S(1)} %attach_sources.1.mine_ref), channel_id=1, source_target_pairs={{0,1},{1,0},{2,3},{3,2},{4,5},{5,4},{6,7},{7,6},{8,9},{9,8},{10,11... | collective-permute-start | bytes 835592 | tf_op jit(solution)/shard_map/ppermute | solution.py:466
  24.8 15.6 %collective-permute-start.8 = (bf16[16,32,384]{2,1,0:T(8,128)(2,1)S(1)}, bf16[16,32,384]{2,1,0:T(8,128)(2,1)S(1)}, u32[]{:S(2)}, u32[]{:S(2)}) collective-permute-start(bf16[16,32,384]{2,1,0:T(8,128)(2,1)S(1)} %all-to-all-done.refs_0_), channel_id=1, source_target_pairs={{0,1},{1,0},{2,3},{3,2},{4,5},{5,4},{6,7},{7,6},{8,9},{9,8},{10,11... | collective-permute-start | bytes 1179656 | tf_op jit(solution)/shard_map/ppermute | solution.py:466
  31.7 2.6 %collective-permute-start.6 = (bf16[144,1024]{1,0:T(8,128)(2,1)S(1)}, bf16[144,1024]{1,0:T(8,128)(2,1)S(1)}, u32[]{:S(2)}, u32[]{:S(2)}) collective-permute-start(bf16[144,1024]{1,0:T(8,128)(2,1)S(1)} %collective-permute-done.2.refs_2_), channel_id=1, source_target_pairs={{0,2},{2,0},{1,3},{3,1},{4,6},{6,4},{5,7},{7,5},{8,10},{10,8},{9,1... | collective-permute-start | bytes 884744 | tf_op jit(solution)/shard_map/ppermute | solution.py:466
  32.7 3.1 %collective-permute-start.4 = (bf16[144,1024]{1,0:T(8,128)(2,1)}, bf16[144,1024]{1,0:T(8,128)(2,1)S(1)}, u32[]{:S(2)}, u32[]{:S(2)}) collective-permute-start(bf16[144,1024]{1,0:T(8,128)(2,1)} %get-tuple-element.43.refs_0_), channel_id=1, source_target_pairs={{0,2},{2,0},{1,3},{3,1},{4,6},{6,4},{5,7},{7,5},{8,10},{10,8},{9,1... | collective-permute-start | bytes 884744 | tf_op jit(solution)/shard_map/ppermute | solution.py:466
  32.7 3.6 %collective-permute-start.5 = (bf16[144,1024]{1,0:T(8,128)(2,1)S(1)}, bf16[144,1024]{1,0:T(8,128)(2,1)S(1)}, u32[]{:S(2)}, u32[]{:S(2)}) collective-permute-start(bf16[144,1024]{1,0:T(8,128)(2,1)S(1)} %collective-permute-done.1.refs_1_), channel_id=1, source_target_pairs={{0,2},{2,0},{1,3},{3,1},{4,6},{6,4},{5,7},{7,5},{8,10},{10,8},{9,1... | collective-permute-start | bytes 884744 | tf_op jit(solution)/shard_map/ppermute | solution.py:466
  33.2 4.4 %collective-permute-start.7 = (bf16[144,1024]{1,0:T(8,128)(2,1)S(1)}, bf16[144,1024]{1,0:T(8,128)(2,1)S(1)}, u32[]{:S(2)}, u32[]{:S(2)}) collective-permute-start(bf16[144,1024]{1,0:T(8,128)(2,1)S(1)} %collective-permute-done.3.refs_3_), channel_id=1, source_target_pairs={{0,2},{2,0},{1,3},{3,1},{4,6},{6,4},{5,7},{7,5},{8,10},{10,8},{9,1... | collective-permute-start | bytes 884744 | tf_op jit(solution)/shard_map/ppermute | solution.py:466
  34.3 25.0 %collective-permute-start.10 = (bf16[2,64,1152]{2,1,0:T(8,128)(2,1)S(1)}, bf16[2,64,1152]{2,1,0:T(8,128)(2,1)S(1)}, u32[]{:S(2)}, u32[]{:S(2)}) collective-permute-start(bf16[2,64,1152]{2,1,0:T(8,128)(2,1)S(1)} %bitcast.17), channel_id=1, source_target_pairs={{0,4},{4,0},{8,12},{12,8},{1,5},{5,1},{9,13},{13,9},{2,6},{6,2},{1... | collective-permute-start | bytes 884744 | tf_op jit(solution)/shard_map/ppermute | solution.py:466
  35.9 23.5 %collective-permute-start.11 = (bf16[2,64,1152]{2,1,0:T(8,128)(2,1)S(1)}, bf16[2,64,1152]{2,1,0:T(8,128)(2,1)S(1)}, u32[]{:S(2)}, u32[]{:S(2)}) collective-permute-start(bf16[2,64,1152]{2,1,0:T(8,128)(2,1)S(1)} %bitcast.18), channel_id=1, source_target_pairs={{0,8},{4,12},{8,0},{12,4},{1,9},{5,13},{9,1},{13,5},{2,10},{6,14},... | collective-permute-start | bytes 884744 | tf_op jit(solution)/shard_map/ppermute | solution.py:466
  36.4 23.0 %collective-permute-start.12 = (bf16[2,64,1152]{2,1,0:T(8,128)(2,1)S(1)}, bf16[2,64,1152]{2,1,0:T(8,128)(2,1)S(1)}, u32[]{:S(2)}, u32[]{:S(2)}) collective-permute-start(bf16[2,64,1152]{2,1,0:T(8,128)(2,1)S(1)} %bitcast.19), channel_id=1, source_target_pairs={{0,12},{4,8},{8,4},{12,0},{1,13},{5,9},{9,5},{13,1},{2,14},{6,10},... | collective-permute-start | bytes 884744 | tf_op jit(solution)/shard_map/ppermute | solution.py:466
  37.6 1.0 copy-start.1
  41.8 8.0 %collective-permute-start.13 = (bf16[128,256]{1,0:T(8,128)(2,1)S(1)}, bf16[128,256]{1,0:T(8,128)(2,1)S(1)}, u32[]{:S(2)}, u32[]{:S(2)}) collective-permute-start(bf16[128,256]{1,0:T(8,128)(2,1)S(1)} %get-tuple-element.57), channel_id=1, source_target_pairs={{0,16},{16,0},{1,17},{17,1},{2,18},{18,2},{3,19},{19,3},{4,20},{20... | collective-permute-start | bytes 196616 | tf_op jit(solution)/shard_map/ppermute | solution.py:466
  51.2 15.0 %all-to-all-start.1 = ((bf16[16,64,128]{2,1,0:T(8,128)(2,1)}), bf16[16,64,128]{2,1,0:T(8,128)(2,1)S(1)}, u32[]{:S(2)}, u32[]{:S(2)}) async-start(bf16[16,64,128]{2,1,0:T(8,128)(2,1)} %bitcast.5), calls=%async_computation.1 | async-start | bytes 524288 | tf_op jit(solution)/shard_map/all_to_all | solution.py:462
  59.3 6.9 %copy-start.2 = (bf16[1,64,1024]{2,1,0:T(8,128)(2,1)S(1)}, bf16[1,64,1024]{2,1,0:T(8,128)(2,1)}, u32[]{:S(2)}) copy-start(bf16[1,64,1024]{2,1,0:T(8,128)(2,1)} %get-tuple-element.62.refs_0_) | copy-start | bytes 393220
  59.3 6.9 %copy-start.3 = (f32[128]{0:T(128)S(1)}, f32[128]{0:T(128)}, u32[]{:S(2)}) copy-start(f32[128]{0:T(128)} %param.12) | copy-start | bytes 1540
  59.4 1.6 %collective-permute-start.14 = (bf16[2,64,1152]{2,1,0:T(8,128)(2,1)S(1)}, bf16[2,64,1152]{2,1,0:T(8,128)(2,1)S(1)}, u32[]{:S(2)}, u32[]{:S(2)}) collective-permute-start(bf16[2,64,1152]{2,1,0:T(8,128)(2,1)S(1)} %bitcast.20), channel_id=1, source_target_pairs={{0,2},{2,0},{1,3},{3,1},{4,6},{6,4},{5,7},{7,5},{8,10},{10,8},{9,1... | collective-permute-start | bytes 884744 | tf_op jit(solution)/shard_map/ppermute | solution.py:466
  59.6 1.9 %collective-permute-start.15 = (bf16[2,64,1152]{2,1,0:T(8,128)(2,1)S(1)}, bf16[2,64,1152]{2,1,0:T(8,128)(2,1)S(1)}, u32[]{:S(2)}, u32[]{:S(2)}) collective-permute-start(bf16[2,64,1152]{2,1,0:T(8,128)(2,1)S(1)} %collective-permute-done.10.refs_1_), channel_id=1, source_target_pairs={{0,2},{2,0},{1,3},{3,1},{4,6},{6,4},{5,7},{7,5},{8,10},{10,8},{9,1... | collective-permute-start | bytes 884744 | tf_op jit(solution)/shard_map/ppermute | solution.py:466
  60.0 1.9 %collective-permute-start.16 = (bf16[2,64,1152]{2,1,0:T(8,128)(2,1)S(1)}, bf16[2,64,1152]{2,1,0:T(8,128)(2,1)S(1)}, u32[]{:S(2)}, u32[]{:S(2)}) collective-permute-start(bf16[2,64,1152]{2,1,0:T(8,128)(2,1)S(1)} %collective-permute-done.11.refs_2_), channel_id=1, source_target_pairs={{0,2},{2,0},{1,3},{3,1},{4,6},{6,4},{5,7},{7,5},{8,10},{10,8},{9,1... | collective-permute-start | bytes 884744 | tf_op jit(solution)/shard_map/ppermute | solution.py:466
  60.1 2.2 %collective-permute-start.17 = (bf16[2,64,1152]{2,1,0:T(8,128)(2,1)S(1)}, bf16[2,64,1152]{2,1,0:T(8,128)(2,1)S(1)}, u32[]{:S(2)}, u32[]{:S(2)}) collective-permute-start(bf16[2,64,1152]{2,1,0:T(8,128)(2,1)S(1)} %collective-permute-done.12.refs_3_), channel_id=1, source_target_pairs={{0,2},{2,0},{1,3},{3,1},{4,6},{6,4},{5,7},{7,5},{8,10},{10,8},{9,1... | collective-permute-start | bytes 884744 | tf_op jit(solution)/shard_map/ppermute | solution.py:466
  69.9 15.2 %copy-start = (bf16[1024,1024]{1,0:T(8,128)(2,1)S(1)}, bf16[1024,1024]{1,0:T(8,128)(2,1)}, u32[]{:S(2)}) copy-start(bf16[1024,1024]{1,0:T(8,128)(2,1)} %get-tuple-element.47.normed_any.normed_ref) | copy-start | bytes 6291460
  81.2 6.3 %collective-permute-start.18 = (bf16[128,256]{1,0:T(8,128)(2,1)S(1)}, bf16[128,256]{1,0:T(8,128)(2,1)S(1)}, u32[]{:S(2)}, u32[]{:S(2)}) collective-permute-start(bf16[128,256]{1,0:T(8,128)(2,1)S(1)} %get-tuple-element.66), channel_id=1, source_target_pairs={{0,16},{16,0},{1,17},{17,1},{2,18},{18,2},{3,19},{19,3},{4,20},{20... | collective-permute-start | bytes 196616 | tf_op jit(solution)/shard_map/ppermute | solution.py:466
  88.6 18.8 %all-to-all-start.3 = ((bf16[32,32,256]{2,1,0:T(8,128)(2,1)}), bf16[32,32,256]{2,1,0:T(8,128)(2,1)S(1)}, u32[]{:S(2)}, u32[]{:S(2)}) async-start(bf16[32,32,256]{2,1,0:T(8,128)(2,1)} %bitcast.9), calls=%async_computation.3 | async-start | bytes 1048576 | tf_op jit(solution)/shard_map/all_to_all | solution.py:462
  91.6 6.0 %collective-permute-start.19 = (f32[100,128]{1,0:T(8,128)S(1)}, f32[100,128]{1,0:T(8,128)S(1)}, u32[]{:S(2)}, u32[]{:S(2)}) collective-permute-start(f32[100,128]{1,0:T(8,128)S(1)} %get-tuple-element.68), channel_id=1, source_target_pairs={{0,1},{1,0},{2,3},{3,2},{4,5},{5,4},{6,7},{7,6},{8,9},{9,8},{10,11... | collective-permute-start | bytes 153608 | tf_op jit(solution)/shard_map/ppermute | solution.py:466

commit v31 on v30

--- a/solution.py
+++ b/solution.py
@@ -112,7 +112,7 @@
 
 
 def norm_kernel(near_any, source_any, normed_any, *refs):
-    parts, (near, source, normed, sems) = refs[:-4], refs[-4:]
+    parts, (normed, near, source, sems) = refs[:-4], refs[-4:]
     ens = lax.axis_index("ens")
     copies = fetch([(source_any, source), (near_any, near)], sems)
     rows = source.shape[0]
@@ -505,21 +505,21 @@
         moved=2**20,
         results="hh",
     )(w_attn, w_mix, readout_matrix)
-    normed, *sources = call(
+    normed, *sources, own_block = call(
         norm_kernel,
         "norm",
         [((node_rows + NOTE_ROWS, LATENT_DIM), BF16)]
-        + [((1 if paired else members_num, part, LATENT_DIM), BF16)] * source_parts,
+        + [((1 if paired else members_num, part, LATENT_DIM), BF16)] * source_parts
+        + [((node_rows + NOTE_ROWS, LATENT_DIM), BF16)],
         "hh",
         [
             pltpu.SMEM(neighbours.shape, jnp.int32),
             pltpu.VMEM((node_rows, LATENT_DIM), BF16),
-            pltpu.VMEM((node_rows + NOTE_ROWS, LATENT_DIM), BF16),
             pltpu.SemaphoreType.DMA((3 + max(2, members_num),)),
         ],
         flops=2**20,
         moved=2**20,
-        results="h" + "h" * source_parts,
+        results="h" + "h" * source_parts + "v",
     )(neighbours, members.reshape(node_rows, LATENT_DIM))
 
     packed, normed = lax.optimization_barrier((in_order(packed, "half", 0), normed))
@@ -555,7 +555,7 @@
         [pltpu.VMEM((GROUP, NOTE_ROWS, 128), BF16), pltpu.SemaphoreType.DMA((2 * GROUP,))],
         moved=4 * 2**20,
         results="hv",
-    )(*near, *far)
+    )(own_block, *near[1:], *far)
 
     if square:
         packed, arrived = call(

time: 109 us -> 108 us (level)
  waiting for transfers between devices: 33.3 us -> 35.5 us
  starting transfers between devices: 34.2 us -> 32.4 us
    ppermute x20, waiting for transfers between devices: 16.8 us -> 19.1 us  [swap(): lax.ppermute(value, axis, [(i, i ^ step) for i in range(lax.axis_size(axi...]
    ppermute x20, starting transfers between devices: 18.4 us -> 16.7 us  [swap(): lax.ppermute(value, axis, [(i, i ^ step) for i in range(lax.axis_size(axi...]
where the time goes in v31:
time: 108 us
  waiting for transfers between devices  35.5 us (33%)
  starting transfers between devices  32.4 us (30%)
  Pallas kernels  27.2 us (25%)
  blocking collectives  9.88 us (9%)
    pallas_call x16, Pallas kernels, run(): made(*[pltpu.with_memory_space_constraint(arg, pltpu.HBM) if space == 'h'...  27.2 us
    ppermute x20, waiting for transfers between devices, swap(): lax.ppermute(value, axis, [(i, i ^ step) for i in range(lax.axis_size(axi...  19.1 us
    ppermute x20, starting transfers between devices, swap(): lax.ppermute(value, axis, [(i, i ^ step) for i in range(lax.axis_size(axi...  16.7 us
    all_to_all x3, waiting for transfers between devices, exchange(): return lax.all_to_all(chunks, axes, 0, 0)  16.4 us
    all_to_all x3, starting transfers between devices, exchange(): return lax.all_to_all(chunks, axes, 0, 0)  15.7 us
    all_to_all x1, blocking collectives, exchange(): return lax.all_to_all(chunks, axes, 0, 0)  9.88 us
  transfers between devices with their start and end apart: 23, of which 14 were waited for; matrix products, arithmetic and copies ran while one was open for 2% of the time, Pallas kernels for 17%

profile of v31, /device:TPU:1, one launch (start us, length us, event | category | flops | bytes accessed | tf_op | source)
XLA Modules:
  0.0 107.6 jit_solution(11555321554203269129)
XLA Ops:
  0.6 1.8 %prepare_weights.1 = (bf16[2,8,1,32,384]{4,3,2,1,0:T(8,128)(2,1)}, bf16[32,1152]{1,0:T(8,128)(2,1)}) custom-call(bf16[32,3072]{1,0:T(8,128)(2,1)} %w_any.1, bf16[32,1024]{1,0:T(8,128)(2,1)} %mix_any.1, bf16[32,100]{1,0:T(8,128)(2,1)} %readout_any.1), custom_call_target="tpu_custom_call" | custom-call | bytes 1048576 | tf_op jit(solution)/shard_map/prepare_weights/pallas_call | solution.py:63
  2.4 3.2 %collective-permute-start = (bf16[32,1152]{1,0:T(8,128)(2,1)}, bf16[32,1152]{1,0:T(8,128)(2,1)S(1)}, u32[]{:S(2)}, u32[]{:S(2)}) collective-permute-start(bf16[32,1152]{1,0:T(8,128)(2,1)} %get-tuple-element.38), channel_id=1, source_target_pairs={{0,16},{16,0},{1,17},{17,1},{2,18},{18,2},{3,19},{19,3},{4,20},{20... | collective-permute-start | bytes 221192 | tf_op jit(solution)/shard_map/ppermute | solution.py:466
  5.7 4.8 %all-to-all-start = ((bf16[16,32,384]{2,1,0:T(8,128)(2,1)}), bf16[16,32,384]{2,1,0:T(8,128)(2,1)S(1)}, u32[]{:S(2)}, u32[]{:S(2)}) async-start(bf16[16,32,384]{2,1,0:T(8,128)(2,1)} %bitcast.23), calls=%async_computation | async-start | bytes 786432 | tf_op jit(solution)/shard_map/all_to_all | solution.py:462
  10.4 1.9 %norm.1 = (bf16[144,1024]{1,0:T(8,128)(2,1)}, bf16[1,64,1024]{2,1,0:T(8,128)(2,1)}, bf16[1,64,1024]{2,1,0:T(8,128)(2,1)}, bf16[144,1024]{1,0:T(8,128)(2,1)S(1)}) custom-call(s32[2,4]{1,0:T(2,128)} %near_any.1, bf16[128,1024]{1,0:T(8,128)(2,1)} %bitcast.24), custom_call_target="tpu_custom_call" | custom-call | flops 1048576 | bytes 1048576 | tf_op jit(solution)/shard_map/norm/pallas_call | solution.py:63
  12.3 0.9 select_bitcast_fusion.1
  13.3 1.5 %collective-permute-start.1 = (bf16[144,1024]{1,0:T(8,128)(2,1)}, bf16[144,1024]{1,0:T(8,128)(2,1)S(1)}, u32[]{:S(2)}, u32[]{:S(2)}) collective-permute-start(bf16[144,1024]{1,0:T(8,128)(2,1)} %get-tuple-element.48), channel_id=1, source_target_pairs={{0,4},{4,0},{8,12},{12,8},{1,5},{5,1},{9,13},{13,9},{2,6},{6,2},{1... | collective-permute-start | bytes 884744 | tf_op jit(solution)/shard_map/ppermute | solution.py:466
  14.7 1.2 %collective-permute-start.3 = (bf16[144,1024]{1,0:T(8,128)(2,1)}, bf16[144,1024]{1,0:T(8,128)(2,1)S(1)}, u32[]{:S(2)}, u32[]{:S(2)}) collective-permute-start(bf16[144,1024]{1,0:T(8,128)(2,1)} %get-tuple-element.48), channel_id=1, source_target_pairs={{0,12},{4,8},{8,4},{12,0},{1,13},{5,9},{9,5},{13,1},{2,14},{6,10},... | collective-permute-start | bytes 884744 | tf_op jit(solution)/shard_map/ppermute | solution.py:466
  15.9 0.9 attach_sources.1.mine_ref
  16.8 5.1 %all-to-all-done.refs_0_ = bf16[16,32,384]{2,1,0:T(8,128)(2,1)S(1)} async-done(((bf16[16,32,384]{2,1,0:T(8,128)(2,1)}), bf16[16,32,384]{2,1,0:T(8,128)(2,1)S(1)}, u32[]{:S(2)}, u32[]{:S(2)}) %all-to-all-start) | async-done | bytes 393248 | tf_op jit(solution)/shard_map/all_to_all | solution.py:462
  21.9 1.7 %collective-permute-start.2 = (bf16[144,1024]{1,0:T(8,128)(2,1)}, bf16[144,1024]{1,0:T(8,128)(2,1)S(1)}, u32[]{:S(2)}, u32[]{:S(2)}) collective-permute-start(bf16[144,1024]{1,0:T(8,128)(2,1)} %get-tuple-element.48), channel_id=1, source_target_pairs={{0,8},{4,12},{8,0},{12,4},{1,9},{5,13},{9,1},{13,5},{2,10},{6,14},... | collective-permute-start | bytes 884744 | tf_op jit(solution)/shard_map/ppermute | solution.py:466
  23.6 1.2 %collective-permute-start.9 = (bf16[2,32,2176]{2,1,0:T(8,128)(2,1)S(1)}, bf16[2,32,2176]{2,1,0:T(8,128)(2,1)S(1)}, u32[]{:S(2)}, u32[]{:S(2)}) collective-permute-start(bf16[2,32,2176]{2,1,0:T(8,128)(2,1)S(1)} %attach_sources.1.mine_ref), channel_id=1, source_target_pairs={{0,1},{1,0},{2,3},{3,2},{4,5},{5,4},{6,7},{7,6},{8,9},{9,8},{10,11... | collective-permute-start | bytes 835592 | tf_op jit(solution)/shard_map/ppermute | solution.py:466
  25.1 5.2 %collective-permute-done.1.refs_1_ = bf16[144,1024]{1,0:T(8,128)(2,1)S(1)} collective-permute-done((bf16[144,1024]{1,0:T(8,128)(2,1)}, bf16[144,1024]{1,0:T(8,128)(2,1)S(1)}, u32[]{:S(2)}, u32[]{:S(2)}) %collective-permute-start.1) | collective-permute-done | bytes 294944 | tf_op jit(solution)/shard_map/ppermute | solution.py:466
  30.3 1.4 %collective-permute-done.2.refs_2_ = bf16[144,1024]{1,0:T(8,128)(2,1)S(1)} collective-permute-done((bf16[144,1024]{1,0:T(8,128)(2,1)}, bf16[144,1024]{1,0:T(8,128)(2,1)S(1)}, u32[]{:S(2)}, u32[]{:S(2)}) %collective-permute-start.2) | collective-permute-done | bytes 294944 | tf_op jit(solution)/shard_map/ppermute | solution.py:466
  31.7 1.0 collective-permute-start.6
  32.7 0.5 collective-permute-start.7
  33.3 0.6 collective-permute-done.6.refs_6_
  33.9 1.5 %collective-permute-start.10 = (bf16[2,64,1152]{2,1,0:T(8,128)(2,1)S(1)}, bf16[2,64,1152]{2,1,0:T(8,128)(2,1)S(1)}, u32[]{:S(2)}, u32[]{:S(2)}) collective-permute-start(bf16[2,64,1152]{2,1,0:T(8,128)(2,1)S(1)} %bitcast.17), channel_id=1, source_target_pairs={{0,4},{4,0},{8,12},{12,8},{1,5},{5,1},{9,13},{13,9},{2,6},{6,2},{1... | collective-permute-start | bytes 884744 | tf_op jit(solution)/shard_map/ppermute | solution.py:466
  35.5 0.5 collective-permute-start.11
  36.0 1.1 %collective-permute-start.12 = (bf16[2,64,1152]{2,1,0:T(8,128)(2,1)S(1)}, bf16[2,64,1152]{2,1,0:T(8,128)(2,1)S(1)}, u32[]{:S(2)}, u32[]{:S(2)}) collective-permute-start(bf16[2,64,1152]{2,1,0:T(8,128)(2,1)S(1)} %bitcast.19), channel_id=1, source_target_pairs={{0,12},{4,8},{8,4},{12,0},{1,13},{5,9},{9,5},{13,1},{2,14},{6,10},... | collective-permute-start | bytes 884744 | tf_op jit(solution)/shard_map/ppermute | solution.py:466
  37.1 1.5 %collect.1 = (bf16[1024,1024]{1,0:T(8,128)(2,1)}, f32[8,16,128]{2,1,0:T(8,128)S(1)}) custom-call(bf16[144,1024]{1,0:T(8,128)(2,1)S(1)} %get-tuple-element.37.refs_0_, bf16[144,1024]{1,0:T(8,128)(2,1)S(1)} %collective-permute-done.1.refs_1_, bf16[144,1024]{1,0:T(8,128)(2,1)S(1)} %collective-permute-done.2.refs_2_, ...), custom_call_target="tpu_custom_call" | custom-call | bytes 4194304 | tf_op jit(solution)/shard_map/collect/pallas_call | solution.py:63
  38.6 1.8 %collective-permute-done.8.refs_1_ = bf16[16,32,384]{2,1,0:T(8,128)(2,1)S(1)} collective-permute-done((bf16[16,32,384]{2,1,0:T(8,128)(2,1)S(1)}, bf16[16,32,384]{2,1,0:T(8,128)(2,1)S(1)}, u32[]{:S(2)}, u32[]{:S(2)}) %collective-permute-start.8) | collective-permute-done | bytes 393248 | tf_op jit(solution)/shard_map/ppermute | solution.py:466
  40.4 1.3 %project_rims.1 = (bf16[16,2,32,384]{3,2,1,0:T(8,128)(2,1)S(1)}, bf16[128,256]{1,0:T(8,128)(2,1)S(1)}) custom-call(bf16[1024,1024]{1,0:T(8,128)(2,1)} %get-tuple-element.49.normed_any.normed_ref, bf16[16,32,384]{2,1,0:T(8,128)(2,1)S(1)} %all-to-all-done.refs_0_, bf16[16,32,384]{2,1,0:T(8,128)(2,1)S(1)} %collective-permute-done.8.refs_1_), custom_call_target="tpu_custom_call" | custom-call | flops 67108864 | bytes 1048576 | tf_op jit(solution)/shard_map/project_rims/pallas_call | solution.py:63
  42.1 2.8 %project.1 = (bf16[1024,128]{1,0:T(8,128)(2,1)S(1)}, bf16[1024,256]{1,0:T(8,128)(2,1)S(1)}) custom-call(bf16[1024,1024]{1,0:T(8,128)(2,1)} %get-tuple-element.49.normed_any.normed_ref, bf16[16,2,32,384]{3,2,1,0:T(8,128)(2,1)S(1)} %get-tuple-element.52.w_ref), custom_call_target="tpu_custom_call" | custom-call | flops 805306368 | bytes 4194304 | tf_op jit(solution)/shard_map/project/pallas_call | solution.py:63
  44.9 1.9 %attention_interior.1.done_ref = bf16[1024,128]{1,0:T(8,128)(2,1)S(1)} custom-call(f32[8,16,128]{2,1,0:T(8,128)S(1)} %get-tuple-element.50.steps_ref, bf16[1024,128]{1,0:T(8,128)(2,1)S(1)} %get-tuple-element.53.q_ref, bf16[1024,256]{1,0:T(8,128)(2,1)S(1)} %get-tuple-element.58.kv_ref), custom_call_target="tpu_custom_call" | custom-call | flops 268435456 | bytes 2097152 | tf_op jit(solution)/shard_map/attention_interior/pallas_call | solution.py:63
  46.8 2.6 %collective-permute-done.13.low_ref.high_ref = bf16[128,256]{1,0:T(8,128)(2,1)S(1)} collective-permute-done((bf16[128,256]{1,0:T(8,128)(2,1)S(1)}, bf16[128,256]{1,0:T(8,128)(2,1)S(1)}, u32[]{:S(2)}, u32[]{:S(2)}) %collective-permute-start.13) | collective-permute-done | bytes 65568 | tf_op jit(solution)/shard_map/ppermute | solution.py:466
  49.4 1.4 %attention_edges.1 = bf16[1024,128]{1,0:T(8,128)(2,1)} custom-call(f32[8,16,128]{2,1,0:T(8,128)S(1)} %get-tuple-element.50.steps_ref, bf16[1024,128]{1,0:T(8,128)(2,1)S(1)} %get-tuple-element.53.q_ref, bf16[1024,256]{1,0:T(8,128)(2,1)S(1)} %get-tuple-element.58.kv_ref, bf16[128,256]{1,0:T(8,128)(2,1)S(1)} %collective-permute-done.13.low_ref.high_ref, ...), custom_call_target="tpu_custom_call" | custom-call | flops 67108864 | bytes 1048576 | tf_op jit(solution)/shard_map/attention_edges/pallas_call | solution.py:63
  50.8 8.0 %all-to-all-start.1 = ((bf16[16,64,128]{2,1,0:T(8,128)(2,1)}), bf16[16,64,128]{2,1,0:T(8,128)(2,1)S(1)}, u32[]{:S(2)}, u32[]{:S(2)}) async-start(bf16[16,64,128]{2,1,0:T(8,128)(2,1)} %bitcast.5), calls=%async_computation.1 | async-start | bytes 524288 | tf_op jit(solution)/shard_map/all_to_all | solution.py:462
  59.0 0.4 collective-permute-start.15
  59.5 0.4 collective-permute-start.17
  59.9 0.6 collective-permute-done.14.refs_4_
  60.5 0.4 collective-permute-done.15.refs_5_
  60.9 0.4 collective-permute-done.16.refs_6_
  61.3 0.4 collective-permute-done.17.refs_7_
  61.7 1.5 %assemble.1.w_any = bf16[2,4,2,64,1152]{4,3,2,1,0:T(8,128)(2,1)} custom-call(bf16[2,64,1152]{2,1,0:T(8,128)(2,1)S(1)} %bitcast.21, bf16[2,64,1152]{2,1,0:T(8,128)(2,1)S(1)} %collective-permute-done.10.refs_1_, bf16[2,64,1152]{2,1,0:T(8,128)(2,1)S(1)} %collective-permute-done.11.refs_2_, bf16[2,64,1152]{2,1,0:T(8,128)(2,1)S(1)} %collective-permute-done.12.refs_3_, ...), custom_call_target="tpu_custom_call" | custom-call | bytes 4194304 | tf_op jit(solution)/shard_map/assemble/pallas_call | solution.py:63
  63.2 2.4 %all-to-all-done.1.att_ref = bf16[16,64,128]{2,1,0:T(8,128)(2,1)S(1)} async-done(((bf16[16,64,128]{2,1,0:T(8,128)(2,1)}), bf16[16,64,128]{2,1,0:T(8,128)(2,1)S(1)}, u32[]{:S(2)}, u32[]{:S(2)}) %all-to-all-start.1) | async-done | bytes 262176 | tf_op jit(solution)/shard_map/all_to_all | solution.py:462
  65.6 3.7 %mix_loss_backward.1 = (f32[100,128]{1,0:T(8,128)S(1)}, bf16[16,64,128]{2,1,0:T(8,128)(2,1)S(1)}) custom-call(bf16[16,64,128]{2,1,0:T(8,128)(2,1)S(1)} %all-to-all-done.1.att_ref, f32[1,128]{1,0:T(1,128)S(1)} %bitcast.22, f32[100,128]{1,0:T(8,128)} %truth_any.1, bf16[2,4,2,64,1152]{4,3,2,1,0:T(8,128)(2,1)} %assemble.1.w_any, ...), custom_call_target="tpu_custom_call" | custom-call | flops 603979776 | bytes 4194304 | tf_op jit(solution)/shard_map/mix_loss_backward/pallas_call | solution.py:63
  69.4 9.9 %all_to_all.20 = bf16[16,64,128]{2,1,0:T(8,128)(2,1)S(1)} all-to-all(bf16[16,64,128]{2,1,0:T(8,128)(2,1)S(1)} %get-tuple-element.66), channel_id=1, replica_groups=mesh['half'=2,'quad'=4,'core'=2,'ens'=2] {'quad','core','ens'}, dimensions={0} | all-to-all | bytes 524288 | tf_op jit(solution)/shard_map/all_to_all | solution.py:462
  79.2 1.4 %attention_edges_back.1 = (f32[2,256,256]{2,1,0:T(8,128)S(1)}, bf16[128,256]{1,0:T(8,128)(2,1)S(1)}) custom-call(f32[8,16,128]{2,1,0:T(8,128)S(1)} %get-tuple-element.50.steps_ref, bf16[1024,128]{1,0:T(8,128)(2,1)S(1)} %get-tuple-element.53.q_ref, bf16[1024,256]{1,0:T(8,128)(2,1)S(1)} %get-tuple-element.58.kv_ref, ...), custom_call_target="tpu_custom_call" | custom-call | flops 167772160 | bytes 1048576 | tf_op jit(solution)/shard_map/attention_edges_back/pallas_call | solution.py:63
  80.8 3.8 %attention_interior_back.1.grads_ref = f32[1024,256]{1,0:T(8,128)S(1)} custom-call(f32[8,16,128]{2,1,0:T(8,128)S(1)} %get-tuple-element.50.steps_ref, bf16[1024,128]{1,0:T(8,128)(2,1)S(1)} %get-tuple-element.53.q_ref, bf16[1024,256]{1,0:T(8,128)(2,1)S(1)} %get-tuple-element.58.kv_ref, bf16[1024,128]{1,0:T(8,128)(2,1)S(1)} %bitcast.15, ...), custom_call_target="tpu_custom_call" | custom-call | flops 536870912 | bytes 4194304 | tf_op jit(solution)/shard_map/attention_interior_back/pallas_call | solution.py:63
  84.6 1.3 %product.1.total_ref = f32[1024,256]{1,0:T(8,128)S(1)} custom-call(bf16[1024,1024]{1,0:T(8,128)(2,1)S(1)} %copy-done, f32[1024,256]{1,0:T(8,128)S(1)} %attention_interior_back.1.grads_ref), custom_call_target="tpu_custom_call" | custom-call | tf_op jit(solution)/shard_map/product/pallas_call | solution.py:63
  85.9 1.0 collective-permute-done.18.refs_0_
  86.9 1.1 %product_rims.1 = bf16[1024,256]{1,0:T(8,128)(2,1)} custom-call(bf16[1024,1024]{1,0:T(8,128)(2,1)S(1)} %copy-done, f32[1024,256]{1,0:T(8,128)S(1)} %product.1.total_ref, bf16[128,256]{1,0:T(8,128)(2,1)S(1)} %collective-permute-done.18.refs_0_), custom_call_target="tpu_custom_call" | custom-call | flops 67108864 | bytes 2097152 | tf_op jit(solution)/shard_map/product_rims/pallas_call | solution.py:63
  88.0 3.0 %all-to-all-start.3 = ((bf16[32,32,256]{2,1,0:T(8,128)(2,1)}), bf16[32,32,256]{2,1,0:T(8,128)(2,1)S(1)}, u32[]{:S(2)}, u32[]{:S(2)}) async-start(bf16[32,32,256]{2,1,0:T(8,128)(2,1)} %bitcast.9), calls=%async_computation.3 | async-start | bytes 1048576 | tf_op jit(solution)/shard_map/all_to_all | solution.py:462
  91.0 1.5 %collective-permute-start.19 = (f32[100,128]{1,0:T(8,128)S(1)}, f32[100,128]{1,0:T(8,128)S(1)}, u32[]{:S(2)}, u32[]{:S(2)}) collective-permute-start(f32[100,128]{1,0:T(8,128)S(1)} %get-tuple-element.70), channel_id=1, source_target_pairs={{0,1},{1,0},{2,3},{3,2},{4,5},{5,4},{6,7},{7,6},{8,9},{9,8},{10,11... | collective-permute-start | bytes 153608 | tf_op jit(solution)/shard_map/ppermute | solution.py:466
  92.5 4.5 %collective-permute-done.19 = f32[100,128]{1,0:T(8,128)S(1)} collective-permute-done((f32[100,128]{1,0:T(8,128)S(1)}, f32[100,128]{1,0:T(8,128)S(1)}, u32[]{:S(2)}, u32[]{:S(2)}) %collective-permute-start.19) | collective-permute-done | bytes 51232 | tf_op jit(solution)/shard_map/ppermute | solution.py:466
  97.2 0.7 copy.9
  97.9 9.0 %all-to-all-done.3 = bf16[32,32,256]{2,1,0:T(8,128)(2,1)S(1)} async-done(((bf16[32,32,256]{2,1,0:T(8,128)(2,1)}), bf16[32,32,256]{2,1,0:T(8,128)(2,1)S(1)}, u32[]{:S(2)}, u32[]{:S(2)}) %all-to-all-start.3) | async-done | bytes 524320 | tf_op jit(solution)/shard_map/all_to_all | solution.py:462
  106.8 0.8 gather_sums.1
  (28 shorter events, 1.3 us)
Async XLA Ops:
  2.4 9.9 %collective-permute-start = (bf16[32,1152]{1,0:T(8,128)(2,1)}, bf16[32,1152]{1,0:T(8,128)(2,1)S(1)}, u32[]{:S(2)}, u32[]{:S(2)}) collective-permute-start(bf16[32,1152]{1,0:T(8,128)(2,1)} %get-tuple-element.38), channel_id=1, source_target_pairs={{0,16},{16,0},{1,17},{17,1},{2,18},{18,2},{3,19},{19,3},{4,20},{20... | collective-permute-start | bytes 221192 | tf_op jit(solution)/shard_map/ppermute | solution.py:466
  5.7 16.2 %all-to-all-start = ((bf16[16,32,384]{2,1,0:T(8,128)(2,1)}), bf16[16,32,384]{2,1,0:T(8,128)(2,1)S(1)}, u32[]{:S(2)}, u32[]{:S(2)}) async-start(bf16[16,32,384]{2,1,0:T(8,128)(2,1)} %bitcast.23), calls=%async_computation | async-start | bytes 786432 | tf_op jit(solution)/shard_map/all_to_all | solution.py:462
  13.3 17.0 %collective-permute-start.1 = (bf16[144,1024]{1,0:T(8,128)(2,1)}, bf16[144,1024]{1,0:T(8,128)(2,1)S(1)}, u32[]{:S(2)}, u32[]{:S(2)}) collective-permute-start(bf16[144,1024]{1,0:T(8,128)(2,1)} %get-tuple-element.48), channel_id=1, source_target_pairs={{0,4},{4,0},{8,12},{12,8},{1,5},{5,1},{9,13},{13,9},{2,6},{6,2},{1... | collective-permute-start | bytes 884744 | tf_op jit(solution)/shard_map/ppermute | solution.py:466
  14.7 15.6 %collective-permute-start.3 = (bf16[144,1024]{1,0:T(8,128)(2,1)}, bf16[144,1024]{1,0:T(8,128)(2,1)S(1)}, u32[]{:S(2)}, u32[]{:S(2)}) collective-permute-start(bf16[144,1024]{1,0:T(8,128)(2,1)} %get-tuple-element.48), channel_id=1, source_target_pairs={{0,12},{4,8},{8,4},{12,0},{1,13},{5,9},{9,5},{13,1},{2,14},{6,10},... | collective-permute-start | bytes 884744 | tf_op jit(solution)/shard_map/ppermute | solution.py:466
  21.9 9.8 %collective-permute-start.2 = (bf16[144,1024]{1,0:T(8,128)(2,1)}, bf16[144,1024]{1,0:T(8,128)(2,1)S(1)}, u32[]{:S(2)}, u32[]{:S(2)}) collective-permute-start(bf16[144,1024]{1,0:T(8,128)(2,1)} %get-tuple-element.48), channel_id=1, source_target_pairs={{0,8},{4,12},{8,0},{12,4},{1,9},{5,13},{9,1},{13,5},{2,10},{6,14},... | collective-permute-start | bytes 884744 | tf_op jit(solution)/shard_map/ppermute | solution.py:466
  23.6 9.6 %collective-permute-start.9 = (bf16[2,32,2176]{2,1,0:T(8,128)(2,1)S(1)}, bf16[2,32,2176]{2,1,0:T(8,128)(2,1)S(1)}, u32[]{:S(2)}, u32[]{:S(2)}) collective-permute-start(bf16[2,32,2176]{2,1,0:T(8,128)(2,1)S(1)} %attach_sources.1.mine_ref), channel_id=1, source_target_pairs={{0,1},{1,0},{2,3},{3,2},{4,5},{5,4},{6,7},{7,6},{8,9},{9,8},{10,11... | collective-permute-start | bytes 835592 | tf_op jit(solution)/shard_map/ppermute | solution.py:466
  24.8 15.6 %collective-permute-start.8 = (bf16[16,32,384]{2,1,0:T(8,128)(2,1)S(1)}, bf16[16,32,384]{2,1,0:T(8,128)(2,1)S(1)}, u32[]{:S(2)}, u32[]{:S(2)}) collective-permute-start(bf16[16,32,384]{2,1,0:T(8,128)(2,1)S(1)} %all-to-all-done.refs_0_), channel_id=1, source_target_pairs={{0,1},{1,0},{2,3},{3,2},{4,5},{5,4},{6,7},{7,6},{8,9},{9,8},{10,11... | collective-permute-start | bytes 1179656 | tf_op jit(solution)/shard_map/ppermute | solution.py:466
  31.7 2.2 %collective-permute-start.6 = (bf16[144,1024]{1,0:T(8,128)(2,1)S(1)}, bf16[144,1024]{1,0:T(8,128)(2,1)S(1)}, u32[]{:S(2)}, u32[]{:S(2)}) collective-permute-start(bf16[144,1024]{1,0:T(8,128)(2,1)S(1)} %collective-permute-done.2.refs_2_), channel_id=1, source_target_pairs={{0,2},{2,0},{1,3},{3,1},{4,6},{6,4},{5,7},{7,5},{8,10},{10,8},{9,1... | collective-permute-start | bytes 884744 | tf_op jit(solution)/shard_map/ppermute | solution.py:466
  32.7 2.8 %collective-permute-start.5 = (bf16[144,1024]{1,0:T(8,128)(2,1)S(1)}, bf16[144,1024]{1,0:T(8,128)(2,1)S(1)}, u32[]{:S(2)}, u32[]{:S(2)}) collective-permute-start(bf16[144,1024]{1,0:T(8,128)(2,1)S(1)} %collective-permute-done.1.refs_1_), channel_id=1, source_target_pairs={{0,2},{2,0},{1,3},{3,1},{4,6},{6,4},{5,7},{7,5},{8,10},{10,8},{9,1... | collective-permute-start | bytes 884744 | tf_op jit(solution)/shard_map/ppermute | solution.py:466
  32.7 3.2 %collective-permute-start.7 = (bf16[144,1024]{1,0:T(8,128)(2,1)S(1)}, bf16[144,1024]{1,0:T(8,128)(2,1)S(1)}, u32[]{:S(2)}, u32[]{:S(2)}) collective-permute-start(bf16[144,1024]{1,0:T(8,128)(2,1)S(1)} %collective-permute-done.3.refs_3_), channel_id=1, source_target_pairs={{0,2},{2,0},{1,3},{3,1},{4,6},{6,4},{5,7},{7,5},{8,10},{10,8},{9,1... | collective-permute-start | bytes 884744 | tf_op jit(solution)/shard_map/ppermute | solution.py:466
  33.2 3.8 %collective-permute-start.4 = (bf16[144,1024]{1,0:T(8,128)(2,1)}, bf16[144,1024]{1,0:T(8,128)(2,1)S(1)}, u32[]{:S(2)}, u32[]{:S(2)}) collective-permute-start(bf16[144,1024]{1,0:T(8,128)(2,1)} %get-tuple-element.48), channel_id=1, source_target_pairs={{0,2},{2,0},{1,3},{3,1},{4,6},{6,4},{5,7},{7,5},{8,10},{10,8},{9,1... | collective-permute-start | bytes 884744 | tf_op jit(solution)/shard_map/ppermute | solution.py:466
  33.9 24.9 %collective-permute-start.10 = (bf16[2,64,1152]{2,1,0:T(8,128)(2,1)S(1)}, bf16[2,64,1152]{2,1,0:T(8,128)(2,1)S(1)}, u32[]{:S(2)}, u32[]{:S(2)}) collective-permute-start(bf16[2,64,1152]{2,1,0:T(8,128)(2,1)S(1)} %bitcast.17), channel_id=1, source_target_pairs={{0,4},{4,0},{8,12},{12,8},{1,5},{5,1},{9,13},{13,9},{2,6},{6,2},{1... | collective-permute-start | bytes 884744 | tf_op jit(solution)/shard_map/ppermute | solution.py:466
  35.5 23.3 %collective-permute-start.11 = (bf16[2,64,1152]{2,1,0:T(8,128)(2,1)S(1)}, bf16[2,64,1152]{2,1,0:T(8,128)(2,1)S(1)}, u32[]{:S(2)}, u32[]{:S(2)}) collective-permute-start(bf16[2,64,1152]{2,1,0:T(8,128)(2,1)S(1)} %bitcast.18), channel_id=1, source_target_pairs={{0,8},{4,12},{8,0},{12,4},{1,9},{5,13},{9,1},{13,5},{2,10},{6,14},... | collective-permute-start | bytes 884744 | tf_op jit(solution)/shard_map/ppermute | solution.py:466
  36.0 22.9 %collective-permute-start.12 = (bf16[2,64,1152]{2,1,0:T(8,128)(2,1)S(1)}, bf16[2,64,1152]{2,1,0:T(8,128)(2,1)S(1)}, u32[]{:S(2)}, u32[]{:S(2)}) collective-permute-start(bf16[2,64,1152]{2,1,0:T(8,128)(2,1)S(1)} %bitcast.19), channel_id=1, source_target_pairs={{0,12},{4,8},{8,4},{12,0},{1,13},{5,9},{9,5},{13,1},{2,14},{6,10},... | collective-permute-start | bytes 884744 | tf_op jit(solution)/shard_map/ppermute | solution.py:466
  41.7 7.6 %collective-permute-start.13 = (bf16[128,256]{1,0:T(8,128)(2,1)S(1)}, bf16[128,256]{1,0:T(8,128)(2,1)S(1)}, u32[]{:S(2)}, u32[]{:S(2)}) collective-permute-start(bf16[128,256]{1,0:T(8,128)(2,1)S(1)} %get-tuple-element.59), channel_id=1, source_target_pairs={{0,16},{16,0},{1,17},{17,1},{2,18},{18,2},{3,19},{19,3},{4,20},{20... | collective-permute-start | bytes 196616 | tf_op jit(solution)/shard_map/ppermute | solution.py:466
  50.8 14.8 %all-to-all-start.1 = ((bf16[16,64,128]{2,1,0:T(8,128)(2,1)}), bf16[16,64,128]{2,1,0:T(8,128)(2,1)S(1)}, u32[]{:S(2)}, u32[]{:S(2)}) async-start(bf16[16,64,128]{2,1,0:T(8,128)(2,1)} %bitcast.5), calls=%async_computation.1 | async-start | bytes 524288 | tf_op jit(solution)/shard_map/all_to_all | solution.py:462
  58.8 6.9 %copy-start.1 = (bf16[1,64,1024]{2,1,0:T(8,128)(2,1)S(1)}, bf16[1,64,1024]{2,1,0:T(8,128)(2,1)}, u32[]{:S(2)}) copy-start(bf16[1,64,1024]{2,1,0:T(8,128)(2,1)} %get-tuple-element.64.refs_0_) | copy-start | bytes 393220
  58.8 6.9 %copy-start.2 = (f32[128]{0:T(128)S(1)}, f32[128]{0:T(128)}, u32[]{:S(2)}) copy-start(f32[128]{0:T(128)} %param.12) | copy-start | bytes 1540
  58.8 1.6 %collective-permute-start.14 = (bf16[2,64,1152]{2,1,0:T(8,128)(2,1)S(1)}, bf16[2,64,1152]{2,1,0:T(8,128)(2,1)S(1)}, u32[]{:S(2)}, u32[]{:S(2)}) collective-permute-start(bf16[2,64,1152]{2,1,0:T(8,128)(2,1)S(1)} %bitcast.20), channel_id=1, source_target_pairs={{0,2},{2,0},{1,3},{3,1},{4,6},{6,4},{5,7},{7,5},{8,10},{10,8},{9,1... | collective-permute-start | bytes 884744 | tf_op jit(solution)/shard_map/ppermute | solution.py:466
  59.0 1.9 %collective-permute-start.15 = (bf16[2,64,1152]{2,1,0:T(8,128)(2,1)S(1)}, bf16[2,64,1152]{2,1,0:T(8,128)(2,1)S(1)}, u32[]{:S(2)}, u32[]{:S(2)}) collective-permute-start(bf16[2,64,1152]{2,1,0:T(8,128)(2,1)S(1)} %collective-permute-done.10.refs_1_), channel_id=1, source_target_pairs={{0,2},{2,0},{1,3},{3,1},{4,6},{6,4},{5,7},{7,5},{8,10},{10,8},{9,1... | collective-permute-start | bytes 884744 | tf_op jit(solution)/shard_map/ppermute | solution.py:466
  59.4 1.9 %collective-permute-start.16 = (bf16[2,64,1152]{2,1,0:T(8,128)(2,1)S(1)}, bf16[2,64,1152]{2,1,0:T(8,128)(2,1)S(1)}, u32[]{:S(2)}, u32[]{:S(2)}) collective-permute-start(bf16[2,64,1152]{2,1,0:T(8,128)(2,1)S(1)} %collective-permute-done.11.refs_2_), channel_id=1, source_target_pairs={{0,2},{2,0},{1,3},{3,1},{4,6},{6,4},{5,7},{7,5},{8,10},{10,8},{9,1... | collective-permute-start | bytes 884744 | tf_op jit(solution)/shard_map/ppermute | solution.py:466
  59.5 2.2 %collective-permute-start.17 = (bf16[2,64,1152]{2,1,0:T(8,128)(2,1)S(1)}, bf16[2,64,1152]{2,1,0:T(8,128)(2,1)S(1)}, u32[]{:S(2)}, u32[]{:S(2)}) collective-permute-start(bf16[2,64,1152]{2,1,0:T(8,128)(2,1)S(1)} %collective-permute-done.12.refs_3_), channel_id=1, source_target_pairs={{0,2},{2,0},{1,3},{3,1},{4,6},{6,4},{5,7},{7,5},{8,10},{10,8},{9,1... | collective-permute-start | bytes 884744 | tf_op jit(solution)/shard_map/ppermute | solution.py:466
  69.4 15.3 %copy-start = (bf16[1024,1024]{1,0:T(8,128)(2,1)S(1)}, bf16[1024,1024]{1,0:T(8,128)(2,1)}, u32[]{:S(2)}) copy-start(bf16[1024,1024]{1,0:T(8,128)(2,1)} %get-tuple-element.49.normed_any.normed_ref) | copy-start | bytes 6291460
  80.7 6.3 %collective-permute-start.18 = (bf16[128,256]{1,0:T(8,128)(2,1)S(1)}, bf16[128,256]{1,0:T(8,128)(2,1)S(1)}, u32[]{:S(2)}, u32[]{:S(2)}) collective-permute-start(bf16[128,256]{1,0:T(8,128)(2,1)S(1)} %get-tuple-element.68), channel_id=1, source_target_pairs={{0,16},{16,0},{1,17},{17,1},{2,18},{18,2},{3,19},{19,3},{4,20},{20... | collective-permute-start | bytes 196616 | tf_op jit(solution)/shard_map/ppermute | solution.py:466
  88.0 18.8 %all-to-all-start.3 = ((bf16[32,32,256]{2,1,0:T(8,128)(2,1)}), bf16[32,32,256]{2,1,0:T(8,128)(2,1)S(1)}, u32[]{:S(2)}, u32[]{:S(2)}) async-start(bf16[32,32,256]{2,1,0:T(8,128)(2,1)} %bitcast.9), calls=%async_computation.3 | async-start | bytes 1048576 | tf_op jit(solution)/shard_map/all_to_all | solution.py:462
  91.0 6.0 %collective-permute-start.19 = (f32[100,128]{1,0:T(8,128)S(1)}, f32[100,128]{1,0:T(8,128)S(1)}, u32[]{:S(2)}, u32[]{:S(2)}) collective-permute-start(f32[100,128]{1,0:T(8,128)S(1)} %get-tuple-element.70), channel_id=1, source_target_pairs={{0,1},{1,0},{2,3},{3,2},{4,5},{5,4},{6,7},{7,6},{8,9},{9,8},{10,11... | collective-permute-start | bytes 153608 | tf_op jit(solution)/shard_map/ppermute | solution.py:466
